TPU v7x, 32 devices: a whole 2x2x4 slice. The times are simulated.
32 devices in a mesh: groups: 2 (over y), blk: 4 (over z), tile: 2 (over x), pair: 2 (over core).
Axes of the slice: x: 2, y: 2, z: 4, core: 2. Of those that a mesh axis runs over, the one named last changes fastest.
Arguments:
- left_tokens: bfloat16 [4, 1536, 768], P(('groups', 'pair'), 'blk', 'tile'), parts along dimension 0, may hold values from -32 to 32
- right_tokens: bfloat16 [4, 1536, 768], P(('groups', 'pair'), 'blk', 'tile'), parts along dimension 0, may hold values from -32 to 32
- self_qkv: bfloat16 [3, 768, 512], P(None, None, 'tile'), may hold values from -1 to 1
- self_out: bfloat16 [512, 768], P('tile'), may hold values from -0.25 to 0.25
- cross_qkv: bfloat16 [3, 768, 512], P(None, None, 'tile'), may hold values from -1 to 1
- cross_out: bfloat16 [512, 768], P('tile'), may hold values from -0.25 to 0.25
- reassemble: bfloat16 [768, 256], P('tile'), may hold values from -0.21875 to 0.21875
- conv_weight: bfloat16 [3, 3, 256, 256], replicated, may hold values from -0.125 to 0.125
Outputs:
- joined: bfloat16 [4, 12, 128, 256], P(('groups', 'pair'), 'blk', 'tile'), parts along dimension 0
There are 2 independent parts, one for each index of `groups`. A program takes and returns all parts, laid end to end along the dimension named above; an argument that names none is the same for every part. Nothing has to cross between parts.
All inputs are finite; a program needn't handle non-finite values.
Results may differ from a plain program's by a relative error of at most 0.018.
Values may be sent and summed in bfloat16 or wider, within the bound.
No kernel may reach another device: no remote copies, remote signals or barrier semaphores. Data moves between devices by JAX's collectives and lax.ppermute only.
A program may use at most 64 MiB of HBM per device.

v0:
```python
import jax
import jax.numpy as jnp
from jax import lax
from jax.sharding import PartitionSpec as P

HD = 64
CH = 256
GRID_W = 128


def padded_2(cells, sides, width):
    for axis, dim in sides:
        count = lax.axis_size(axis)
        ends = count - 1
        head = lax.slice_in_dim(cells, 0, width, axis=dim)
        tail = lax.slice_in_dim(cells, cells.shape[dim] - width, cells.shape[dim], axis=dim)
        cells = jnp.concatenate(
            [
                lax.ppermute(tail, axis, [(i, (i + 1) % count) for i in range(ends)]),
                cells,
                lax.ppermute(head, axis, [((i + 1) % count, i) for i in range(ends)]),
            ],
            axis=dim,
        )
    return cells


def layer_norm(values):
    widened = values.astype(jnp.float32)
    centred = widened - jnp.mean(widened, axis=-1, keepdims=True)
    variance = jnp.mean(centred * centred, axis=-1, keepdims=True)
    return (centred * lax.rsqrt(variance + 1e-06)).astype(jnp.bfloat16)


def project_rows(normed, weight):
    return jnp.dot(normed, weight, preferred_element_type=jnp.float32).astype(jnp.bfloat16)


def initial_state(queries):
    query_count = queries.shape[0]
    head_count = queries.shape[1] // HD
    return (
        jnp.full((head_count, query_count), -1e30, jnp.float32),
        jnp.zeros((head_count, query_count), jnp.float32),
        jnp.zeros(queries.shape, jnp.float32),
    )


def attend_keys(running, queries, keys_rows, values_rows):
    maxima, totals, accumulated = running
    query_count = queries.shape[0]
    head_count = queries.shape[1] // HD
    key_count = keys_rows.shape[0]
    scores = jnp.einsum(
        "qhd,khd->hqk",
        queries.reshape(query_count, head_count, HD),
        keys_rows.reshape(key_count, head_count, HD),
        preferred_element_type=jnp.float32,
    ) * HD ** (-0.5)
    new_maxima = jnp.maximum(maxima, jnp.max(scores, axis=2))
    correction = jnp.exp(maxima - new_maxima)
    expanded = jnp.exp(scores - new_maxima[:, :, None])
    totals = totals * correction + jnp.sum(expanded, axis=2)
    mixed = jnp.einsum(
        "hqk,khd->qhd",
        expanded.astype(jnp.bfloat16),
        values_rows.reshape(key_count, head_count, HD),
        preferred_element_type=jnp.float32,
    )
    accumulated = (
        accumulated.reshape(query_count, head_count, HD) * correction.T[:, :, None] + mixed
    )
    return (new_maxima, totals, accumulated.reshape(query_count, head_count * HD))


def fold_keys(running, queries, keys_rows, values_rows):
    key_count = keys_rows.shape[0]
    block_rows = max((divisor for divisor in range(1, 1025) if key_count % divisor == 0))
    if block_rows == key_count:
        return attend_keys(running, queries, keys_rows, values_rows)
    stacked_keys = keys_rows.reshape(key_count // block_rows, block_rows, keys_rows.shape[1])
    stacked_values = values_rows.reshape(key_count // block_rows, block_rows, values_rows.shape[1])

    def step_block(current, blocks):
        return (attend_keys(current, queries, blocks[0], blocks[1]), None)

    result, unused = lax.scan(step_block, running, (stacked_keys, stacked_values))
    return result


def finish_state(running):
    maxima, totals, accumulated = running
    query_count = accumulated.shape[0]
    head_count = accumulated.shape[1] // HD
    normalized = accumulated.reshape(query_count, head_count, HD) / totals.T[:, :, None]
    return normalized.reshape(query_count, head_count * HD).astype(jnp.bfloat16)


def body(
    left_tokens, right_tokens, self_qkv, self_out, cross_qkv, cross_out, reassemble, conv_weight
):
    left_full, right_full = (
        lax.all_gather(left_tokens, "tile", axis=2, tiled=True),
        lax.all_gather(right_tokens, "tile", axis=2, tiled=True),
    )
    left_rows = left_full[0]
    left_normed = layer_norm(left_rows)
    right_normed = layer_norm(right_full[0])
    self_query = project_rows(left_normed, self_qkv[0])
    self_key = project_rows(left_normed, self_qkv[1])
    self_value = project_rows(left_normed, self_qkv[2])
    cross_key = project_rows(right_normed, cross_qkv[1])
    cross_value = project_rows(right_normed, cross_qkv[2])
    pieces = (
        lax.all_gather(self_key, "blk", axis=0, tiled=True),
        lax.all_gather(self_value, "blk", axis=0, tiled=True),
    )
    self_state = fold_keys(initial_state(self_query), self_query, pieces[0], pieces[1])
    self_mixed = finish_state(self_state)
    self_term = jnp.dot(self_mixed, self_out, preferred_element_type=jnp.float32)
    self_share = lax.psum_scatter(
        self_term.astype(jnp.bfloat16), "tile", scatter_dimension=1, tiled=True
    ).astype(jnp.float32)
    updated = (left_tokens[0].astype(jnp.float32) + self_share).astype(jnp.bfloat16)
    updated_full = lax.all_gather(updated, "tile", axis=1, tiled=True)
    updated_normed = layer_norm(updated_full)
    cross_query = project_rows(updated_normed, cross_qkv[0])
    pieces = (
        lax.all_gather(cross_key, "blk", axis=0, tiled=True),
        lax.all_gather(cross_value, "blk", axis=0, tiled=True),
    )
    cross_state = fold_keys(initial_state(cross_query), cross_query, pieces[0], pieces[1])
    cross_mixed = finish_state(cross_state)
    cross_share = lax.psum_scatter(
        jnp.dot(cross_mixed, cross_out, preferred_element_type=jnp.float32).astype(jnp.bfloat16),
        "tile",
        scatter_dimension=1,
        tiled=True,
    ).astype(jnp.float32)
    final_tokens = (updated.astype(jnp.float32) + cross_share).astype(jnp.bfloat16)
    band_rows = final_tokens.shape[0] // GRID_W
    partial_map = jnp.dot(final_tokens, reassemble, preferred_element_type=jnp.float32).reshape(
        band_rows, GRID_W, CH
    )
    feature_map = lax.psum_scatter(
        partial_map.astype(jnp.bfloat16), "tile", scatter_dimension=1, tiled=True
    )
    column_count = feature_map.shape[1]
    activated = jnp.maximum(feature_map, jnp.zeros((), jnp.bfloat16))
    padded = padded_2(activated, (("blk", 0), ("tile", 1)), 1)
    stacked = jnp.concatenate(
        [
            padded[row_shift : row_shift + band_rows, col_shift : col_shift + column_count]
            for row_shift in range(3)
            for col_shift in range(3)
        ],
        axis=-1,
    )
    convolved = jnp.dot(
        stacked.reshape(band_rows * column_count, 9 * CH),
        conv_weight.reshape(9 * CH, CH),
        preferred_element_type=jnp.float32,
    )
    joined = (
        feature_map.astype(jnp.float32) + convolved.reshape(band_rows, column_count, CH)
    ).astype(jnp.bfloat16)
    return joined[None]


def solution(mesh):
    placed = (
        P(("groups", "pair"), "blk", "tile"),
        P(("groups", "pair"), "blk", "tile"),
        P(None, None, "tile"),
        P("tile", None),
        P(None, None, "tile"),
        P("tile", None),
        P("tile", None),
        P(),
    )
    return jax.shard_map(
        body,
        mesh=mesh,
        in_specs=placed,
        out_specs=P(("groups", "pair"), "blk", "tile", None),
        check_vma=False,
    )
```

profile of v0, /device:TPU:1, one launch (start us, length us, event | category | flops | bytes accessed | tf_op | source)
XLA Modules:
  0.0 214.9 jit_solution(9744858873867985740)
XLA Ops:
  6.5 9.8 %all_gather.21 = bf16[1,384,768]{2,1,0:T(8,128)(2,1)S(1)} all-gather(bf16[1,384,384]{2,1,0:T(8,128)(2,1)} %param.12), channel_id=1, replica_groups=mesh['groups'=2,'blk'=4,'tile'=2,'pair'=2] {'tile'}, dimensions={2}, use_global_device_ids=true | all-gather | bytes 884736 | tf_op jit(solution)/shard_map/all_gather | solution.py:103
  16.9 1.4 convolution_convert_fusion.8
  19.1 16.1 %all_gather.22 = bf16[1536,256]{1,0:T(8,128)(2,1)S(1)} all-gather(bf16[384,256]{1,0:T(8,128)(2,1)S(1)} %convolution_convert_fusion.8), channel_id=1, replica_groups=mesh['groups'=2,'blk'=4,'tile'=2,'pair'=2] {'blk'}, dimensions={0}, use_global_device_ids=true | all-gather | bytes 983040 | tf_op jit(solution)/shard_map/all_gather | solution.py:115
  35.1 16.1 %all_gather.23 = bf16[1536,256]{1,0:T(8,128)(2,1)} all-gather(bf16[384,256]{1,0:T(8,128)(2,1)S(1)} %convolution_convert_fusion.6), channel_id=1, replica_groups=mesh['groups'=2,'blk'=4,'tile'=2,'pair'=2] {'blk'}, dimensions={0}, use_global_device_ids=true | all-gather | bytes 983040 | tf_op jit(solution)/shard_map/all_gather | solution.py:116
  52.1 19.8 %while.30 = (s32[]{:T(128)}, f32[4,384]{1,0:T(4,128)S(1)}, f32[4,384]{1,0:T(4,128)S(1)}, f32[384,256]{0,1:T(8,128)S(1)}, bf16[2,768,256]{2,1,0:T(8,128)(2,1)S(1)...) while((s32[]{:T(128)}, f32[4,384]{1,0:T(4,128)S(1)}, ...), condition=%wide.region_5.0_spmd.clone, body=%wide.region_2.5_spmd.clone.sunk | while | flops 311632896 | bytes 38043784 | solution.py:87
  53.4 3.9 %bitcast_reduce_fusion.4 = (f32[4,384]{1,0:T(4,128)S(1)}, f32[4,768,384]{2,1,0:T(8,128)}) fusion(bf16[768,4,64]{0,2,1:T(8,128)(2,1)S(1)} %bitcast.186, bf16[384,4,64]{0,2,1:T(8,128)(2,1)} %bitcast.199), kind=kOutput, calls=%fused_computation.1.clone.1 | convolution fusion | flops 153352704 | bytes 5314560 | tf_op jit(solution)/shard_map/while/body/eval_jaxpr/qhd,khd->hqk/dot_general | solution.py:54
  57.5 3.5 %fusion.112 = f32[384,4,64]{0,2,1:T(8,128)S(1)} fusion(bf16[768,4,64]{0,2,1:T(8,128)(2,1)S(1)} %bitcast.187, f32[4,768,384]{2,1,0:T(8,128)} %get-tuple-element.301, f32[4,384]{1,0:T(4,128)S(1)} %get-tuple-element.336, f32[384,4,64]{0,2,1:T(8,128)S(1)} %bitcast.192, f32[384,4]{0,1:T(4,128)S(1)} %get-tuple-element.303), kind=kOutput, calls=%fused_computation.9.clone.1 | convolution fusion | flops 154730496 | bytes 5910528 | tf_op jit(solution)/shard_map/while/body/eval_jaxpr/hqk,khd->qhd/dot_general | solution.py:64
  63.3 3.9 %bitcast_reduce_fusion.4 = (f32[4,384]{1,0:T(4,128)S(1)}, f32[4,768,384]{2,1,0:T(8,128)}) fusion(bf16[768,4,64]{0,2,1:T(8,128)(2,1)S(1)} %bitcast.186, bf16[384,4,64]{0,2,1:T(8,128)(2,1)} %bitcast.199), kind=kOutput, calls=%fused_computation.1.clone.1 | convolution fusion | flops 153352704 | bytes 5314560 | tf_op jit(solution)/shard_map/while/body/eval_jaxpr/qhd,khd->hqk/dot_general | solution.py:54
  67.4 3.5 %fusion.112 = f32[384,4,64]{0,2,1:T(8,128)S(1)} fusion(bf16[768,4,64]{0,2,1:T(8,128)(2,1)S(1)} %bitcast.187, f32[4,768,384]{2,1,0:T(8,128)} %get-tuple-element.301, f32[4,384]{1,0:T(4,128)S(1)} %get-tuple-element.336, f32[384,4,64]{0,2,1:T(8,128)S(1)} %bitcast.192, f32[384,4]{0,1:T(4,128)S(1)} %get-tuple-element.303), kind=kOutput, calls=%fused_computation.9.clone.1 | convolution fusion | flops 154730496 | bytes 5910528 | tf_op jit(solution)/shard_map/while/body/eval_jaxpr/hqk,khd->qhd/dot_general | solution.py:64
  74.5 6.3 %all_gather.24 = bf16[1,384,768]{2,1,0:T(8,128)(2,1)S(1)} all-gather(bf16[1,384,384]{2,1,0:T(8,128)(2,1)S(1)} %copy-done.7), channel_id=1, replica_groups=mesh['groups'=2,'blk'=4,'tile'=2,'pair'=2] {'tile'}, dimensions={2}, use_global_device_ids=true | all-gather | bytes 884736 | tf_op jit(solution)/shard_map/all_gather | solution.py:104
  84.0 12.9 %all_gather.27 = bf16[1536,256]{1,0:T(8,128)(2,1)S(1)} all-gather(bf16[384,256]{1,0:T(8,128)(2,1)S(1)} %convolution_convert_fusion.3), channel_id=1, replica_groups=mesh['groups'=2,'blk'=4,'tile'=2,'pair'=2] {'blk'}, dimensions={0}, use_global_device_ids=true | all-gather | bytes 983040 | tf_op jit(solution)/shard_map/all_gather | solution.py:130
  96.9 15.9 %all_gather.25 = bf16[1536,256]{1,0:T(8,128)(2,1)} all-gather(bf16[384,256]{1,0:T(8,128)(2,1)S(1)} %convolution_convert_fusion.5), channel_id=1, replica_groups=mesh['groups'=2,'blk'=4,'tile'=2,'pair'=2] {'blk'}, dimensions={0}, use_global_device_ids=true | all-gather | bytes 983040 | tf_op jit(solution)/shard_map/all_gather | solution.py:129
  114.9 7.1 %all_gather.26 = bf16[384,768]{1,0:T(8,128)(2,1)S(1)} all-gather(bf16[384,384]{1,0:T(8,128)(2,1)S(1)} %fusion.51), channel_id=1, replica_groups=mesh['groups'=2,'blk'=4,'tile'=2,'pair'=2] {'tile'}, dimensions={1}, use_global_device_ids=true | all-gather | bytes 884736 | tf_op jit(solution)/shard_map/all_gather | solution.py:125
  124.7 19.8 %while.31 = (s32[]{:T(128)}, f32[4,384]{1,0:T(4,128)S(1)}, f32[4,384]{1,0:T(4,128)S(1)}, f32[384,256]{0,1:T(8,128)S(1)}, bf16[2,768,256]{2,1,0:T(8,128)(2,1)}, /...) while((s32[]{:T(128)}, f32[4,384]{1,0:T(4,128)S(1)}, ...), condition=%wide.region_14.15_spmd.clone, body=%wide.region_11.14_spmd.clone.sunk | while | flops 311632896 | bytes 38043784 | solution.py:87
  126.0 3.9 %bitcast_reduce_fusion.5 = (f32[4,384]{1,0:T(4,128)S(1)}, f32[4,768,384]{2,1,0:T(8,128)}) fusion(bf16[768,4,64]{0,2,1:T(8,128)(2,1)S(1)} %bitcast.188, bf16[384,4,64]{0,2,1:T(8,128)(2,1)} %bitcast.198), kind=kOutput, calls=%fused_computation.19.clone.1 | convolution fusion | flops 153352704 | bytes 5314560 | tf_op jit(solution)/shard_map/while/body/eval_jaxpr/qhd,khd->hqk/dot_general | solution.py:54
  130.1 3.5 %fusion.120 = f32[384,4,64]{0,2,1:T(8,128)S(1)} fusion(bf16[768,4,64]{0,2,1:T(8,128)(2,1)S(1)} %bitcast.189, f32[4,768,384]{2,1,0:T(8,128)} %get-tuple-element.314, f32[4,384]{1,0:T(4,128)S(1)} %get-tuple-element.363, f32[384,4,64]{0,2,1:T(8,128)S(1)} %bitcast.190, f32[384,4]{0,1:T(4,128)S(1)} %get-tuple-element.316), kind=kOutput, calls=%fused_computation.27.clone.1 | convolution fusion | flops 154730496 | bytes 5910528 | tf_op jit(solution)/shard_map/while/body/eval_jaxpr/hqk,khd->qhd/dot_general | solution.py:64
  135.9 3.9 %bitcast_reduce_fusion.5 = (f32[4,384]{1,0:T(4,128)S(1)}, f32[4,768,384]{2,1,0:T(8,128)}) fusion(bf16[768,4,64]{0,2,1:T(8,128)(2,1)S(1)} %bitcast.188, bf16[384,4,64]{0,2,1:T(8,128)(2,1)} %bitcast.198), kind=kOutput, calls=%fused_computation.19.clone.1 | convolution fusion | flops 153352704 | bytes 5314560 | tf_op jit(solution)/shard_map/while/body/eval_jaxpr/qhd,khd->hqk/dot_general | solution.py:54
  140.0 3.5 %fusion.120 = f32[384,4,64]{0,2,1:T(8,128)S(1)} fusion(bf16[768,4,64]{0,2,1:T(8,128)(2,1)S(1)} %bitcast.189, f32[4,768,384]{2,1,0:T(8,128)} %get-tuple-element.314, f32[4,384]{1,0:T(4,128)S(1)} %get-tuple-element.363, f32[384,4,64]{0,2,1:T(8,128)S(1)} %bitcast.190, f32[384,4]{0,1:T(4,128)S(1)} %get-tuple-element.316), kind=kOutput, calls=%fused_computation.27.clone.1 | convolution fusion | flops 154730496 | bytes 5910528 | tf_op jit(solution)/shard_map/while/body/eval_jaxpr/hqk,khd->qhd/dot_general | solution.py:64
  147.1 31.4 %reduce-scatter.12.cloned.1.call-done = bf16[384,384]{1,0:T(8,128)(2,1)} async-done(((bf16[768,384]{1,0:T(8,128)(2,1)}), bf16[384,384]{1,0:T(8,128)(2,1)}) %reduce-scatter.12.cloned.1.call-update) | async-done | bytes 294928
  180.6 11.1 %reduce-scatter.8.cloned.1.call-done = bf16[3,64,256]{2,1,0:T(8,128)(2,1)} async-done(((bf16[3,128,256]{2,1,0:T(8,128)(2,1)}), bf16[3,64,256]{2,1,0:T(8,128)(2,1)}) %reduce-scatter.8.cloned.1.call-update) | async-done | bytes 98320 | tf_op jit(solution)/shard_map/reduce_scatter | solution.py:145
  192.7 3.1 %collective-permute-start = (bf16[1,64,256]{2,1,0:T(8,128)(2,1)S(1)}, bf16[1,64,256]{2,1,0:T(8,128)(2,1)S(1)}, u32[]{:S(2)}, u32[]{:S(2)}) collective-permute-start(bf16[1,64,256]{2,1,0:T(8,128)(2,1)S(1)} %get-tuple-element.205), channel_id=1, source_target_pairs={{0,4},{4,8},{8,12},{1,5},{5,9},{9,13},{2,6},{6,10},{10,14},{3,7},{... | collective-permute-start | bytes 98312 | tf_op jit(solution)/shard_map/ppermute | solution.py:19
  197.1 3.3 %collective-permute-done.1 = bf16[1,64,256]{2,1,0:T(8,128)(2,1)S(1)} collective-permute-done((bf16[1,64,256]{2,1,0:T(8,128)(2,1)S(1)}, bf16[1,64,256]{2,1,0:T(8,128)(2,1)S(1)}, u32[]{:S(2)}, u32[]{:S(2)}) %collective-permute-start.1) | collective-permute-done | bytes 32800 | tf_op jit(solution)/shard_map/ppermute | solution.py:21
  200.5 2.2 %collective-permute-start.2 = (bf16[5,1,256]{2,1,0:T(2,128)(2,1)S(1)}, bf16[5,1,256]{2,1,0:T(2,128)(2,1)S(1)}, u32[]{:S(2)}, u32[]{:S(2)}) collective-permute-start(bf16[5,1,256]{2,1,0:T(2,128)(2,1)S(1)} %get-tuple-element.204), channel_id=1, source_target_pairs={{0,2},{1,3},{4,6},{5,7},{8,10},{9,11},{12,14},{13,15},{16,18},{17,... | collective-permute-start | bytes 7688 | tf_op jit(solution)/shard_map/ppermute | solution.py:19
  203.9 3.1 %collective-permute-done.3 = bf16[5,1,256]{2,1,0:T(2,128)(2,1)S(1)} collective-permute-done((bf16[5,1,256]{2,1,0:T(2,128)(2,1)S(1)}, bf16[5,1,256]{2,1,0:T(2,128)(2,1)S(1)}, u32[]{:S(2)}, u32[]{:S(2)}) %collective-permute-start.3) | collective-permute-done | bytes 2592 | tf_op jit(solution)/shard_map/ppermute | solution.py:21
  (112 shorter events, 31.9 us)
Async XLA Ops:
  6.5 200.8 %copy-start = (bf16[3,3,256,256]{3,2,1,0:T(8,128)(2,1)S(1)}, bf16[3,3,256,256]{3,2,1,0:T(8,128)(2,1)}, u32[]{:S(2)}) copy-start(bf16[3,3,256,256]{3,2,1,0:T(8,128)(2,1)} %param.19) | copy-start | bytes 3538948
  6.5 106.3 %reduce-scatter.10.cloned.1.call-start = ((), (), s32[]{:S(2)}) async-start(), calls=%async_computation.4 | async-start | bytes 884736
  16.5 1.8 copy-start.9
  57.5 3.8 %copy-start.1 = (f32[4,768,384]{2,1,0:T(8,128)S(1)}, f32[4,768,384]{2,1,0:T(8,128)}, u32[]{:S(2)}) copy-start(f32[4,768,384]{2,1,0:T(8,128)} %get-tuple-element.301) | copy-start | bytes 14155780 | tf_op jit(solution)/shard_map/while
  67.4 3.8 %copy-start.1 = (f32[4,768,384]{2,1,0:T(8,128)S(1)}, f32[4,768,384]{2,1,0:T(8,128)}, u32[]{:S(2)}) copy-start(f32[4,768,384]{2,1,0:T(8,128)} %get-tuple-element.301) | copy-start | bytes 14155780 | tf_op jit(solution)/shard_map/while
  73.3 1.1 copy-start.7
  74.4 104.0 %reduce-scatter.12.cloned.1.call-start = ((), (), s32[]{:S(2)}) async-start(), calls=%async_computation.5 | async-start | bytes 884736
  84.0 30.1 %copy-start.5 = (bf16[1,384,384]{2,1,0:T(8,128)(2,1)S(1)}, bf16[1,384,384]{2,1,0:T(8,128)(2,1)}, u32[]{:S(2)}) copy-start(bf16[1,384,384]{2,1,0:T(8,128)(2,1)} %param.12) | copy-start | bytes 884740
  114.1 0.7 copy-start.3
  130.1 3.8 %copy-start.2 = (f32[4,768,384]{2,1,0:T(8,128)S(1)}, f32[4,768,384]{2,1,0:T(8,128)}, u32[]{:S(2)}) copy-start(f32[4,768,384]{2,1,0:T(8,128)} %get-tuple-element.314) | copy-start | bytes 14155780 | tf_op jit(solution)/shard_map/while
  140.0 3.8 %copy-start.2 = (f32[4,768,384]{2,1,0:T(8,128)S(1)}, f32[4,768,384]{2,1,0:T(8,128)}, u32[]{:S(2)}) copy-start(f32[4,768,384]{2,1,0:T(8,128)} %get-tuple-element.314) | copy-start | bytes 14155780 | tf_op jit(solution)/shard_map/while
  145.9 33.7 %copy-start.4 = (bf16[384,384]{1,0:T(8,128)(2,1)S(1)}, bf16[384,384]{1,0:T(8,128)(2,1)}, u32[]{:S(2)}) copy-start(bf16[384,384]{1,0:T(8,128)(2,1)} %copy-done.3) | copy-start | bytes 884740
  146.0 33.7 %copy-start.8 = (bf16[384,256]{1,0:T(8,128)(2,1)S(1)}, bf16[384,256]{1,0:T(8,128)(2,1)}, u32[]{:S(2)}) copy-start(bf16[384,256]{1,0:T(8,128)(2,1)} %param.18) | copy-start | bytes 589828
  147.0 44.6 %reduce-scatter.8.cloned.1.call-start = ((), (), s32[]{:S(2)}) async-start(), calls=%async_computation.3 | async-start | bytes 294912 | tf_op jit(solution)/shard_map/reduce_scatter | solution.py:145
  191.7 15.5 %copy-start.6 = (bf16[3,64,256]{2,1,0:T(8,128)(2,1)S(1)}, bf16[3,64,256]{2,1,0:T(8,128)(2,1)}, u32[]{:S(2)}) copy-start(bf16[3,64,256]{2,1,0:T(8,128)(2,1)} %reduce-scatter.8.cloned.1.call-done) | copy-start | bytes 294916
  192.7 4.4 %collective-permute-start = (bf16[1,64,256]{2,1,0:T(8,128)(2,1)S(1)}, bf16[1,64,256]{2,1,0:T(8,128)(2,1)S(1)}, u32[]{:S(2)}, u32[]{:S(2)}) collective-permute-start(bf16[1,64,256]{2,1,0:T(8,128)(2,1)S(1)} %get-tuple-element.205), channel_id=1, source_target_pairs={{0,4},{4,8},{8,12},{1,5},{5,9},{9,13},{2,6},{6,10},{10,14},{3,7},{... | collective-permute-start | bytes 98312 | tf_op jit(solution)/shard_map/ppermute | solution.py:19
  195.8 4.7 %collective-permute-start.1 = (bf16[1,64,256]{2,1,0:T(8,128)(2,1)S(1)}, bf16[1,64,256]{2,1,0:T(8,128)(2,1)S(1)}, u32[]{:S(2)}, u32[]{:S(2)}) collective-permute-start(bf16[1,64,256]{2,1,0:T(8,128)(2,1)S(1)} %get-tuple-element.206), channel_id=1, source_target_pairs={{4,0},{8,4},{12,8},{5,1},{9,5},{13,9},{6,2},{10,6},{14,10},{7,3},{... | collective-permute-start | bytes 98312 | tf_op jit(solution)/shard_map/ppermute | solution.py:21
  200.5 3.5 %collective-permute-start.2 = (bf16[5,1,256]{2,1,0:T(2,128)(2,1)S(1)}, bf16[5,1,256]{2,1,0:T(2,128)(2,1)S(1)}, u32[]{:S(2)}, u32[]{:S(2)}) collective-permute-start(bf16[5,1,256]{2,1,0:T(2,128)(2,1)S(1)} %get-tuple-element.204), channel_id=1, source_target_pairs={{0,2},{1,3},{4,6},{5,7},{8,10},{9,11},{12,14},{13,15},{16,18},{17,... | collective-permute-start | bytes 7688 | tf_op jit(solution)/shard_map/ppermute | solution.py:19
  202.6 4.4 %collective-permute-start.3 = (bf16[5,1,256]{2,1,0:T(2,128)(2,1)S(1)}, bf16[5,1,256]{2,1,0:T(2,128)(2,1)S(1)}, u32[]{:S(2)}, u32[]{:S(2)}) collective-permute-start(bf16[5,1,256]{2,1,0:T(2,128)(2,1)S(1)} %get-tuple-element.203), channel_id=1, source_target_pairs={{2,0},{3,1},{6,4},{7,5},{10,8},{11,9},{14,12},{15,13},{18,16},{19,... | collective-permute-start | bytes 7688 | tf_op jit(solution)/shard_map/ppermute | solution.py:21
Sparse Core Ops, SparseCore 0:
  74.6 21.4 reduce-scatter.9
  147.2 31.2 reduce-scatter.11
  180.7 10.9 reduce-scatter.7
where the time goes:
time: 219 us; the launch traced here: 215 us
  blocking collectives  84.3 us (38%)
  waiting for transfers between devices  48.9 us (22%)
  matrix products  40.5 us (18%)
  local copies, waits for them, and re-layouts  13.6 us (6%)
  between operations  13.5 us (6%)
  starting transfers between devices  7.96 us (4%)
  other arithmetic  5.96 us (3%)
    unnamed x5, waiting for transfers between devices  31.4 us
    all_gather x1, blocking collectives, body(): lax.all_gather(self_value, 'blk', axis=0, tiled=True)  16.1 us
    all_gather x1, blocking collectives, body(): lax.all_gather(self_key, 'blk', axis=0, tiled=True)  16.1 us
    all_gather x1, blocking collectives, body(): lax.all_gather(cross_key, 'blk', axis=0, tiled=True)  15.9 us
    dot_general x4, matrix products, attend_keys(): jnp.einsum('qhd,khd->hqk', queries.reshape(query_count, head_count, HD),...  15.5 us
    dot_general x4, matrix products, attend_keys(): jnp.einsum('hqk,khd->qhd', expanded.astype(jnp.bfloat16), values_rows.res...  14 us
    all_gather x1, blocking collectives, body(): lax.all_gather(cross_value, 'blk', axis=0, tiled=True)  12.9 us
    reduce_scatter x1, waiting for transfers between devices, body(): lax.psum_scatter(partial_map.astype(jnp.bfloat16), 'tile', scatter_dimens...  11.1 us
  transfers between devices with their start and end apart: 7, of which 4 were waited for; matrix products, arithmetic and copies ran while one was open for 2% of the time, Pallas kernels for 0%

commit v1 on v0

v1 whole, which is shorter than its diff:
```python
import functools
import math

import jax
import jax.numpy as jnp
from jax import lax
from jax.experimental import pallas as pl
from jax.experimental.pallas import tpu as pltpu
from jax.sharding import PartitionSpec as P

HD = 64
GRID_W = 128
EDGE = 16
F32 = jnp.float32
BF16 = jnp.bfloat16
QUERY_SCALE = math.log2(math.e) * HD**-0.5
VMEM = pl.BlockSpec(memory_space=pltpu.VMEM)
SMEM = pl.BlockSpec(memory_space=pltpu.SMEM)


def run_kernel(kernel, name, shapes, operands, flops, place=None):
    leading = () if place is None else (place,)
    moved = sum(v.size * 2 for v in operands) + sum(2 * math.prod(s) for s in shapes)
    return pl.pallas_call(
        kernel,
        out_shape=[jax.ShapeDtypeStruct(s, BF16) for s in shapes],
        in_specs=[SMEM] * len(leading) + [VMEM] * len(operands),
        out_specs=[VMEM] * len(shapes),
        compiler_params=pltpu.CompilerParams(vmem_limit_bytes=48 << 20),
        cost_estimate=pl.CostEstimate(flops=flops, bytes_accessed=moved, transcendentals=0),
        name=name,
    )(*leading, *operands)


def normalized(pieces):
    widened = [piece.astype(F32) for piece in pieces]
    width = sum(piece.shape[1] for piece in widened)
    mean = sum(jnp.sum(piece, axis=1, keepdims=True) for piece in widened) / width
    centred = [piece - mean for piece in widened]
    variance = sum(jnp.sum(piece * piece, axis=1, keepdims=True) for piece in centred) / width
    scale = lax.rsqrt(variance + 1e-06)
    return [(piece * scale).astype(BF16) for piece in centred]


def dot(left, right):
    return jnp.dot(left, right, preferred_element_type=F32)


def project_kernel(place, *refs, count, scaled):
    pieces, weight, outs = refs[:count], refs[count], refs[count + 1 :]
    normed = normalized([piece[...] for piece in pieces])
    products = []
    for which in range(weight.shape[0]):
        products.append(
            sum(
                dot(normed[step], weight[which, lax.rem(place[0] + step, count)])
                for step in range(count)
            )
        )
    if scaled:
        outs[0][...] = (products.pop(0) * QUERY_SCALE).astype(BF16)
    columns = weight.shape[3]
    for which, product in enumerate(products):
        outs[-1][:, which * columns : (which + 1) * columns] = product.astype(BF16)


def attend_kernel(query, *refs):
    packs, out = refs[:-1], refs[-1]
    columns = query.shape[1]
    heads = []
    for start in range(0, columns, HD):
        head = slice(start, start + HD)
        values = slice(columns + start, columns + start + HD)
        asked = query[:, head]
        scores = [
            lax.dot_general(
                asked, pack[:, head], (((1,), (1,)), ((), ())), preferred_element_type=F32
            )
            for pack in packs
        ]
        maxima = functools.reduce(
            jnp.maximum, [jnp.max(score, axis=1, keepdims=True) for score in scores]
        )
        total, mixed = 0.0, 0.0
        for score, pack in zip(scores, packs):
            expanded = jnp.exp2(score - maxima)
            total = total + jnp.sum(expanded, axis=1, keepdims=True)
            mixed = mixed + dot(expanded.astype(BF16), pack[:, values])
        heads.append(mixed / total)
    out[...] = jnp.concatenate(heads, axis=1).astype(BF16)


def update_kernel(place, *refs, count):
    mixed, weights = refs[:count], refs[count : 2 * count]
    tokens, query_weight = refs[2 * count : 3 * count], refs[3 * count]
    updated, query = refs[3 * count + 1 :]
    pieces = []
    for step in range(count):
        slot = lax.rem(place[0] + step, count)
        term = sum(dot(mixed[t][...], weights[t][slot]) for t in range(count))
        piece = (tokens[step][...].astype(F32) + term).astype(BF16)
        updated[step] = piece
        pieces.append(piece)
    normed = normalized(pieces)
    product = sum(
        dot(normed[step], query_weight[lax.rem(place[0] + step, count)]) for step in range(count)
    )
    query[...] = (product * QUERY_SCALE).astype(BF16)


def finish_kernel(place, *refs, count, width):
    mixed, weights = refs[:count], refs[count : 2 * count]
    updated, reassemble = refs[2 * count], refs[2 * count + 1 : 3 * count + 1]
    window, board = refs[3 * count + 1], refs[3 * count + 2]
    features = 0.0
    for step in range(count):
        slot = lax.rem(place[0] + step, count)
        term = sum(dot(mixed[t][...], weights[t][slot]) for t in range(count))
        final = (updated[step].astype(F32) + term).astype(BF16)
        features = features + dot(final, reassemble[step][...])
    features = features.astype(BF16)
    band_rows = board.shape[0]
    edge = jnp.zeros((band_rows, EDGE, board.shape[2]), BF16)
    board[:, :EDGE, :] = edge
    board[:, EDGE + GRID_W :, :] = edge
    board[:, EDGE : EDGE + GRID_W, :] = features.reshape(band_rows, GRID_W, board.shape[2])
    start = pl.multiple_of(place[0] * width, EDGE)
    window[...] = board[:, pl.ds(start, width + 2 * EDGE), :]


def conv_kernel(window, above, below, weight, out):
    width = out.shape[1]
    band_rows, channels = out.shape[0], out.shape[2]
    grid = jnp.concatenate([above[...], window[...], below[...]], axis=0).astype(F32)
    active = jnp.maximum(grid, 0.0)
    total = grid[1 : 1 + band_rows, EDGE : EDGE + width, :].reshape(band_rows * width, channels)
    for column in range(3):
        first = EDGE - 1 + column
        shifted = active[:, first : first + width, :].astype(BF16)
        for row in range(3):
            rows = shifted[row : row + band_rows].reshape(band_rows * width, channels)
            total = total + dot(rows, weight[row, column])
    out[...] = total.reshape(out.shape).astype(BF16)


def body(
    left_tokens, right_tokens, self_qkv, self_out, cross_qkv, cross_out, reassemble, conv_weight
):
    bands, tiles, cores = (lax.axis_size(axis) for axis in ("blk", "tile", "pair"))
    half = bands // cores
    both = ("blk", "pair")
    place = lax.axis_index("tile").astype(jnp.int32).reshape(1)
    rows, share = left_tokens.shape[1:]
    columns = self_qkv.shape[2]
    channels = reassemble.shape[1]
    width = GRID_W // tiles
    band_rows = rows // GRID_W

    def home(band, pair):
        return band * cores + pair

    def worker(band, pair):
        shift = (pair - band // half) % cores
        return ((band + shift * half) % bands) * cores + (pair - shift) % cores

    places = [(band, pair) for band in range(bands) for pair in range(cores)]

    def tile_pieces(own):
        others = [
            lax.ppermute(own, "tile", [((i + s) % tiles, i) for i in range(tiles)])
            for s in range(1, tiles)
        ]
        return [own, *others]

    def gathered(pack):
        near = [pack] + [
            lax.ppermute(
                pack,
                "blk",
                [(g * half + (i + s) % half, g * half + i) for g in range(cores) for i in range(half)],
            )
            for s in range(1, half)
        ]
        packs = list(near)
        for s in range(1, cores):
            packs += [
                lax.ppermute(p, "pair", [((i + s) % cores, i) for i in range(cores)]) for p in near
            ]
        if len(packs) > 4:
            size = -(-len(packs) // 4)
            packs = [jnp.concatenate(packs[i : i + size]) for i in range(0, len(packs), size)]
        return packs

    def moved(tokens):
        return lax.ppermute(tokens[0], both, [(home(*p), worker(*p)) for p in places])

    def project(pieces, weights, scaled):
        shapes = [(rows, columns)] * scaled + [(rows, 2 * columns)]
        stacked = weights.reshape(weights.shape[0], tiles, share, columns)
        return run_kernel(
            functools.partial(project_kernel, count=tiles, scaled=scaled),
            "project",
            shapes,
            [*pieces, stacked],
            2 * rows * share * tiles * columns * weights.shape[0],
            place,
        )

    def attend(query, packs):
        keys = sum(p.shape[0] for p in packs)
        return run_kernel(
            attend_kernel, "attend", [(rows, columns)], [query, *packs], 16 * rows * keys * columns
        )[0]

    def feature_blocks(weight):
        return weight.reshape(columns, tiles, share).transpose(1, 0, 2)

    left = tile_pieces(moved(left_tokens))
    self_out_pieces = tile_pieces(feature_blocks(self_out))
    cross_out_pieces = tile_pieces(feature_blocks(cross_out))
    reassemble_pieces = tile_pieces(reassemble)
    query, pack = project(left, self_qkv, True)
    self_packs = gathered(pack)
    right = tile_pieces(moved(right_tokens))
    (pack,) = project(right, cross_qkv[1:], False)
    cross_packs = gathered(pack)

    mixed = tile_pieces(attend(query, self_packs))
    updated, cross_query = run_kernel(
        functools.partial(update_kernel, count=tiles),
        "update",
        [(tiles, rows, share), (rows, columns)],
        [*mixed, *self_out_pieces, *left, cross_qkv[0].reshape(tiles, share, columns)],
        4 * rows * share * tiles * columns * tiles,
        place,
    )
    mixed = tile_pieces(attend(cross_query, cross_packs))
    board = (band_rows, GRID_W + 2 * EDGE, channels)
    operands = [*mixed, *cross_out_pieces, updated, *reassemble_pieces]
    window = pl.pallas_call(
        functools.partial(finish_kernel, count=tiles, width=width),
        out_shape=jax.ShapeDtypeStruct((band_rows, width + 2 * EDGE, channels), BF16),
        in_specs=[SMEM] + [VMEM] * len(operands),
        out_specs=VMEM,
        scratch_shapes=[pltpu.VMEM(board, BF16)],
        compiler_params=pltpu.CompilerParams(vmem_limit_bytes=48 << 20),
        name="finish",
    )(place, *operands)
    back = lax.ppermute(window, both, [(worker(*p), home(*p)) for p in places])
    above = lax.ppermute(
        window[-1:], both, [(worker(b, p), home(b + 1, p)) for b, p in places if b + 1 < bands]
    )
    below = lax.ppermute(
        window[:1], both, [(worker(b, p), home(b - 1, p)) for b, p in places if b > 0]
    )
    (joined,) = run_kernel(
        conv_kernel,
        "join",
        [(band_rows, width, channels)],
        [back, above, below, conv_weight],
        18 * band_rows * width * channels * channels,
    )
    return joined[None]


def solution(mesh):
    placed = (
        P(("groups", "pair"), "blk", "tile"),
        P(("groups", "pair"), "blk", "tile"),
        P(None, None, "tile"),
        P("tile", None),
        P(None, None, "tile"),
        P("tile", None),
        P("tile", None),
        P(),
    )
    return jax.shard_map(
        body,
        mesh=mesh,
        in_specs=placed,
        out_specs=P(("groups", "pair"), "blk", "tile", None),
        check_vma=False,
    )
```

time: 219 us -> 88.2 us (0.40); the launches traced: 215 us -> 87.8 us
  blocking collectives: 84.3 us -> 0 us
  matrix products: 40.5 us -> 0 us
  starting transfers between devices: 7.96 us -> 25.1 us
  Pallas kernels: 0 us -> 16.6 us
  between operations: 13.5 us -> 0.2 us
  local copies, waits for them, and re-layouts: 13.6 us -> 4.12 us
  waiting for transfers between devices: 48.9 us -> 41.8 us
  other arithmetic: 5.96 us -> 0 us
    all_gather x7 -> x0, blocking collectives: 84.3 us -> none  [the longest x1 16.1 us: body(): lax.all_gather(self_value, 'blk', axis=0, tiled=True)]
    dot_general x18 -> x0, matrix products: 40.5 us -> none  [the longest x4 15.5 us: attend_keys(): jnp.einsum('qhd,khd->hqk', queries.reshape(query_count, head_count, HD),...]
    ppermute x4 -> x18, waiting for transfers between devices: 6.41 us -> 41.8 us  [the longest x7 21.7 us: tile_pieces(): lax.ppermute(own, 'tile', [((i + s) % tiles, i) for i in range(tiles)])]
    unnamed x5 -> x0, waiting for transfers between devices: 31.4 us -> none
    ppermute x4 -> x18, starting transfers between devices: 7.87 us -> 25.1 us  [the longest x2 7.72 us: moved(): lax.ppermute(tokens[0], both, [(home(*p), worker(*p)) for p in places])]
    pallas_call x0 -> x7, Pallas kernels: none -> 16.6 us  [the longest x6 15.5 us: run_kernel(): pl.pallas_call(kernel, out_shape=[jax.ShapeDtypeStruct(s, BF16) for s in...]
    reduce_scatter x1 -> x0, waiting for transfers between devices: 11.1 us -> none  [body(): lax.psum_scatter(partial_map.astype(jnp.bfloat16), 'tile', scatter_dimens...]
    dynamic_slice x12 -> x0, local copies, waits for them, and re-layouts: 5.59 us -> none  [fold_keys(): lax.scan(step_block, running, (stacked_keys, stacked_values))]
  transfers between devices with their start and end apart: 7 -> 18, of which waited for: 4 -> 10; matrix products, arithmetic and copies ran while one was open for 2% -> 3% of each run, Pallas kernels for 0% -> 16%
where the time goes in v1:
time: 88.2 us; the launch traced here: 87.8 us
  waiting for transfers between devices  41.8 us (47%)
  starting transfers between devices  25.1 us (28%)
  Pallas kernels  16.6 us (19%)
  local copies, waits for them, and re-layouts  4.12 us (5%)
    ppermute x7, waiting for transfers between devices, tile_pieces(): lax.ppermute(own, 'tile', [((i + s) % tiles, i) for i in range(tiles)])  21.7 us
    pallas_call x6, Pallas kernels, run_kernel(): pl.pallas_call(kernel, out_shape=[jax.ShapeDtypeStruct(s, BF16) for s in...  15.5 us
    ppermute x2, waiting for transfers between devices, moved(): lax.ppermute(tokens[0], both, [(home(*p), worker(*p)) for p in places])  9.54 us
    ppermute x2, starting transfers between devices, moved(): lax.ppermute(tokens[0], both, [(home(*p), worker(*p)) for p in places])  7.72 us
    ppermute x1, starting transfers between devices, body(): back = lax.ppermute(window, both, [(worker(*p), home(*p)) for p in places])  5.9 us
    ppermute x2, waiting for transfers between devices, gathered(): lax.ppermute(pack, 'blk', [(g * half + (i + s) % half, g * half + i) for...  5.3 us
    ppermute x1, waiting for transfers between devices, body(): lax.ppermute(window[:1], both, [(worker(b, p), home(b - 1, p)) for b, p i...  5.27 us
    ppermute x7, starting transfers between devices, tile_pieces(): lax.ppermute(own, 'tile', [((i + s) % tiles, i) for i in range(tiles)])  3.91 us
  transfers between devices with their start and end apart: 18, of which 10 were waited for; matrix products, arithmetic and copies ran while one was open for 3% of the time, Pallas kernels for 16%

profile of v1, /device:TPU:1, one launch (start us, length us, event | category | flops | bytes accessed | tf_op | source)
XLA Modules:
  0.0 87.8 jit_solution(8832501949630553465)
XLA Ops:
  0.0 5.6 %collective-permute-start = (bf16[384,384]{1,0:T(8,128)(2,1)}, bf16[384,384]{1,0:T(8,128)(2,1)S(1)}, u32[]{:S(2)}, u32[]{:S(2)}) collective-permute-start(bf16[384,384]{1,0:T(8,128)(2,1)} %bitcast.20), channel_id=1, source_target_pairs={{0,0},{1,8},{4,4},{5,12},{8,1},{9,9},{12,5},{13,13},{2,2},{3,10},{... | collective-permute-start | bytes 884744 | tf_op jit(solution)/shard_map/ppermute | solution.py:195
  5.6 7.8 %collective-permute-done.refs_0_.refs_4_ = bf16[384,384]{1,0:T(8,128)(2,1)S(1)} collective-permute-done((bf16[384,384]{1,0:T(8,128)(2,1)}, bf16[384,384]{1,0:T(8,128)(2,1)S(1)}, u32[]{:S(2)}, u32[]{:S(2)}) %collective-permute-start) | collective-permute-done | bytes 294944 | tf_op jit(solution)/shard_map/ppermute | solution.py:195
  13.4 1.2 %collective-permute-start.1 = (bf16[384,384]{1,0:T(8,128)(2,1)S(1)}, bf16[384,384]{1,0:T(8,128)(2,1)S(1)}, u32[]{:S(2)}, u32[]{:S(2)}) collective-permute-start(bf16[384,384]{1,0:T(8,128)(2,1)S(1)} %collective-permute-done.refs_0_.refs_4_), channel_id=1, source_target_pairs={{2,0},{0,2},{3,1},{1,3},{6,4},{4,6},{7,5},{5,7},{10,8},{8,10},{11,... | collective-permute-start | bytes 884744 | tf_op jit(solution)/shard_map/ppermute | solution.py:170
  14.6 2.1 %collective-permute-start.7 = (bf16[384,384]{1,0:T(8,128)(2,1)}, bf16[384,384]{1,0:T(8,128)(2,1)S(1)}, u32[]{:S(2)}, u32[]{:S(2)}) collective-permute-start(bf16[384,384]{1,0:T(8,128)(2,1)} %bitcast.21), channel_id=1, source_target_pairs={{0,0},{1,8},{4,4},{5,12},{8,1},{9,9},{12,5},{13,13},{2,2},{3,10},{... | collective-permute-start | bytes 884744 | tf_op jit(solution)/shard_map/ppermute | solution.py:195
  16.7 4.8 %collective-permute-done.1.refs_1_.refs_5_ = bf16[384,384]{1,0:T(8,128)(2,1)S(1)} collective-permute-done((bf16[384,384]{1,0:T(8,128)(2,1)S(1)}, bf16[384,384]{1,0:T(8,128)(2,1)S(1)}, u32[]{:S(2)}, u32[]{:S(2)}) %collective-permute-start.1) | collective-permute-done | bytes 294944 | tf_op jit(solution)/shard_map/ppermute | solution.py:170
  21.5 1.3 %copy-done = bf16[3,768,256]{2,1,0:T(8,128)(2,1)S(1)} copy-done((bf16[3,768,256]{2,1,0:T(8,128)(2,1)S(1)}, bf16[3,768,256]{2,1,0:T(8,128)(2,1)}, u32[]{:S(2)}) %copy-start) | copy-done | bytes 1179672
  23.8 1.3 %collective-permute-start.2 = (bf16[384,512]{1,0:T(8,128)(2,1)S(1)}, bf16[384,512]{1,0:T(8,128)(2,1)S(1)}, u32[]{:S(2)}, u32[]{:S(2)}) collective-permute-start(bf16[384,512]{1,0:T(8,128)(2,1)S(1)} %get-tuple-element.10.refs_0_), channel_id=1, source_target_pairs={{4,0},{0,4},{12,8},{8,12},{5,1},{1,5},{13,9},{9,13},{6,2},{2,6},{1... | collective-permute-start | bytes 1179656 | tf_op jit(solution)/shard_map/ppermute | solution.py:177
  25.2 1.8 %collective-permute-done.7.refs_0_ = bf16[384,384]{1,0:T(8,128)(2,1)S(1)} collective-permute-done((bf16[384,384]{1,0:T(8,128)(2,1)}, bf16[384,384]{1,0:T(8,128)(2,1)S(1)}, u32[]{:S(2)}, u32[]{:S(2)}) %collective-permute-start.7) | collective-permute-done | bytes 294944 | tf_op jit(solution)/shard_map/ppermute | solution.py:195
  27.2 5.6 %collective-permute-done.8.refs_1_ = bf16[384,384]{1,0:T(8,128)(2,1)S(1)} collective-permute-done((bf16[384,384]{1,0:T(8,128)(2,1)S(1)}, bf16[384,384]{1,0:T(8,128)(2,1)S(1)}, u32[]{:S(2)}, u32[]{:S(2)}) %collective-permute-start.8) | collective-permute-done | bytes 294944 | tf_op jit(solution)/shard_map/ppermute | solution.py:170
  33.8 1.8 %collective-permute-done.2.refs_1_ = bf16[384,512]{1,0:T(8,128)(2,1)S(1)} collective-permute-done((bf16[384,512]{1,0:T(8,128)(2,1)S(1)}, bf16[384,512]{1,0:T(8,128)(2,1)S(1)}, u32[]{:S(2)}, u32[]{:S(2)}) %collective-permute-start.2) | collective-permute-done | bytes 393248 | tf_op jit(solution)/shard_map/ppermute | solution.py:177
  37.2 3.5 %collective-permute-done.9.refs_1_ = bf16[384,512]{1,0:T(8,128)(2,1)S(1)} collective-permute-done((bf16[384,512]{1,0:T(8,128)(2,1)S(1)}, bf16[384,512]{1,0:T(8,128)(2,1)S(1)}, u32[]{:S(2)}, u32[]{:S(2)}) %collective-permute-start.9) | collective-permute-done | bytes 393248 | tf_op jit(solution)/shard_map/ppermute | solution.py:177
  40.8 5.3 %attend.2.refs_0_ = bf16[384,256]{1,0:T(8,128)(2,1)} custom-call(bf16[384,256]{1,0:T(8,128)(2,1)S(1)} %get-tuple-element.9.query, bf16[384,512]{1,0:T(8,128)(2,1)S(1)} %get-tuple-element.10.refs_0_, bf16[384,512]{1,0:T(8,128)(2,1)S(1)} %collective-permute-done.2.refs_1_, bf16[384,512]{1,0:T(8,128)(2,1)S(1)} %collective-permute-done.3.refs_2_, ...), custom_call_target="tpu_custom_call" | custom-call | flops 2415919104 | bytes 1966080 | tf_op jit(solution)/shard_map/attend/pallas_call | solution.py:24
  46.3 1.2 %copy.11 = bf16[256,768]{0,1:T(8,128)(2,1)S(1)} copy(bf16[256,768]{1,0:T(8,128)(2,1)} %param.13) | data formatting | bytes 786432 | tf_op args[5]
  47.7 1.3 %collective-permute-start.13 = (bf16[2,256,384]{2,1,0:T(8,128)(2,1)S(1)}, bf16[2,256,384]{2,1,0:T(8,128)(2,1)S(1)}, u32[]{:S(2)}, u32[]{:S(2)}) collective-permute-start(bf16[2,256,384]{2,1,0:T(8,128)(2,1)S(1)} %bitcast.12), channel_id=1, source_target_pairs={{2,0},{0,2},{3,1},{1,3},{6,4},{4,6},{7,5},{5,7},{10,8},{8,10},{11,... | collective-permute-start | bytes 1179656 | tf_op jit(solution)/shard_map/ppermute | solution.py:170
  50.3 1.9 %collective-permute-done.5.refs_1_ = bf16[384,256]{1,0:T(8,128)(2,1)S(1)} collective-permute-done((bf16[384,256]{1,0:T(8,128)(2,1)}, bf16[384,256]{1,0:T(8,128)(2,1)S(1)}, u32[]{:S(2)}, u32[]{:S(2)}) %collective-permute-start.5) | collective-permute-done | bytes 196640 | tf_op jit(solution)/shard_map/ppermute | solution.py:170
  52.3 2.6 %update.1 = (bf16[2,384,384]{2,1,0:T(8,128)(2,1)S(1)}, bf16[384,256]{1,0:T(8,128)(2,1)S(1)}) custom-call(s32[1]{0:T(128)} %bitcast.place, bf16[384,256]{1,0:T(8,128)(2,1)} %attend.2.refs_0_, bf16[384,256]{1,0:T(8,128)(2,1)S(1)} %collective-permute-done.5.refs_1_, bf16[2,256,384]{2,1,0:T(8,128)(2,1)S(1)} %bitcast.16, ...), custom_call_target="tpu_custom_call" | custom-call | flops 603979776 | bytes 2949120 | tf_op jit(solution)/shard_map/update/pallas_call | solution.py:24
  54.8 4.7 %attend.3.refs_0_ = bf16[384,256]{1,0:T(8,128)(2,1)S(1)} custom-call(bf16[384,256]{1,0:T(8,128)(2,1)S(1)} %get-tuple-element.11.query, bf16[384,512]{1,0:T(8,128)(2,1)S(1)} %project.3.refs_0_, bf16[384,512]{1,0:T(8,128)(2,1)S(1)} %collective-permute-done.9.refs_1_, bf16[384,512]{1,0:T(8,128)(2,1)S(1)} %collective-permute-done.10.refs_2_, ...), custom_call_target="tpu_custom_call" | custom-call | flops 2415919104 | bytes 1966080 | tf_op jit(solution)/shard_map/attend/pallas_call | solution.py:24
  59.8 5.1 %collective-permute-done.14.refs_6_ = bf16[384,256]{1,0:T(8,128)(2,1)S(1)} collective-permute-done((bf16[384,256]{1,0:T(8,128)(2,1)S(1)}, bf16[384,256]{1,0:T(8,128)(2,1)S(1)}, u32[]{:S(2)}, u32[]{:S(2)}) %collective-permute-start.14) | collective-permute-done | bytes 196640 | tf_op jit(solution)/shard_map/ppermute | solution.py:170
  64.9 4.2 %collective-permute-done.12.refs_1_ = bf16[384,256]{1,0:T(8,128)(2,1)S(1)} collective-permute-done((bf16[384,256]{1,0:T(8,128)(2,1)S(1)}, bf16[384,256]{1,0:T(8,128)(2,1)S(1)}, u32[]{:S(2)}, u32[]{:S(2)}) %collective-permute-start.12) | collective-permute-done | bytes 196640 | tf_op jit(solution)/shard_map/ppermute | solution.py:170
  69.1 1.1 %finish.1 = bf16[3,96,256]{2,1,0:T(8,128)(2,1)S(1)} custom-call(s32[1]{0:T(128)} %bitcast.place, bf16[384,256]{1,0:T(8,128)(2,1)S(1)} %attend.3.refs_0_, bf16[384,256]{1,0:T(8,128)(2,1)S(1)} %collective-permute-done.12.refs_1_, bf16[2,256,384]{2,1,0:T(8,128)(2,1)S(1)} %bitcast.13, bf16[2,256,384]{2,1,0:T(8,128)(2,1)S(1)} %collective-permute-done.13.refs_3_, ...), custom_call_target="tpu_custom_call" | custom-call | tf_op jit(solution)/shard_map/finish/pallas_call | solution.py:240
  70.2 5.9 %collective-permute-start.15 = (bf16[3,96,256]{2,1,0:T(8,128)(2,1)S(1)}, bf16[3,96,256]{2,1,0:T(8,128)(2,1)S(1)}, u32[]{:S(2)}, u32[]{:S(2)}) collective-permute-start(bf16[3,96,256]{2,1,0:T(8,128)(2,1)S(1)} %finish.1), channel_id=1, source_target_pairs={{0,0},{8,1},{4,4},{12,5},{1,8},{9,9},{5,12},{13,13},{2,2},{10,3},{... | collective-permute-start | bytes 442376 | tf_op jit(solution)/shard_map/ppermute | solution.py:249
  76.1 3.4 %collective-permute-start.16 = (bf16[1,96,256]{2,1,0:T(8,128)(2,1)S(1)}, bf16[1,96,256]{2,1,0:T(8,128)(2,1)S(1)}, u32[]{:S(2)}, u32[]{:S(2)}) collective-permute-start(bf16[1,96,256]{2,1,0:T(8,128)(2,1)S(1)} %get-tuple-element.14), channel_id=1, source_target_pairs={{0,4},{8,5},{4,8},{12,9},{1,12},{9,13},{2,6},{10,7},{6,10},{14,11}... | collective-permute-start | bytes 147464 | tf_op jit(solution)/shard_map/ppermute | solution.py:250
  79.5 1.9 %collective-permute-start.17 = (bf16[1,96,256]{2,1,0:T(8,128)(2,1)S(1)}, bf16[1,96,256]{2,1,0:T(8,128)(2,1)S(1)}, u32[]{:S(2)}, u32[]{:S(2)}) collective-permute-start(bf16[1,96,256]{2,1,0:T(8,128)(2,1)S(1)} %get-tuple-element.13), channel_id=1, source_target_pairs={{4,0},{12,1},{1,4},{9,5},{5,8},{13,9},{6,2},{14,3},{3,6},{11,7},{7... | collective-permute-start | bytes 147464 | tf_op jit(solution)/shard_map/ppermute | solution.py:253
  81.5 5.3 %collective-permute-done.17.below = bf16[1,96,256]{2,1,0:T(8,128)(2,1)S(1)} collective-permute-done((bf16[1,96,256]{2,1,0:T(8,128)(2,1)S(1)}, bf16[1,96,256]{2,1,0:T(8,128)(2,1)S(1)}, u32[]{:S(2)}, u32[]{:S(2)}) %collective-permute-start.17) | collective-permute-done | bytes 49184 | tf_op jit(solution)/shard_map/ppermute | solution.py:253
  (36 shorter events, 7.0 us)
Async XLA Ops:
  0.0 13.4 %collective-permute-start = (bf16[384,384]{1,0:T(8,128)(2,1)}, bf16[384,384]{1,0:T(8,128)(2,1)S(1)}, u32[]{:S(2)}, u32[]{:S(2)}) collective-permute-start(bf16[384,384]{1,0:T(8,128)(2,1)} %bitcast.20), channel_id=1, source_target_pairs={{0,0},{1,8},{4,4},{5,12},{8,1},{9,9},{12,5},{13,13},{2,2},{3,10},{... | collective-permute-start | bytes 884744 | tf_op jit(solution)/shard_map/ppermute | solution.py:195
  13.4 8.1 %collective-permute-start.1 = (bf16[384,384]{1,0:T(8,128)(2,1)S(1)}, bf16[384,384]{1,0:T(8,128)(2,1)S(1)}, u32[]{:S(2)}, u32[]{:S(2)}) collective-permute-start(bf16[384,384]{1,0:T(8,128)(2,1)S(1)} %collective-permute-done.refs_0_.refs_4_), channel_id=1, source_target_pairs={{2,0},{0,2},{3,1},{1,3},{6,4},{4,6},{7,5},{5,7},{10,8},{8,10},{11,... | collective-permute-start | bytes 884744 | tf_op jit(solution)/shard_map/ppermute | solution.py:170
  14.6 12.4 %collective-permute-start.7 = (bf16[384,384]{1,0:T(8,128)(2,1)}, bf16[384,384]{1,0:T(8,128)(2,1)S(1)}, u32[]{:S(2)}, u32[]{:S(2)}) collective-permute-start(bf16[384,384]{1,0:T(8,128)(2,1)} %bitcast.21), channel_id=1, source_target_pairs={{0,0},{1,8},{4,4},{5,12},{8,1},{9,9},{12,5},{13,13},{2,2},{3,10},{... | collective-permute-start | bytes 884744 | tf_op jit(solution)/shard_map/ppermute | solution.py:195
  21.5 1.3 %copy-start = (bf16[3,768,256]{2,1,0:T(8,128)(2,1)S(1)}, bf16[3,768,256]{2,1,0:T(8,128)(2,1)}, u32[]{:S(2)}) copy-start(bf16[3,768,256]{2,1,0:T(8,128)(2,1)} %param.10) | copy-start | bytes 3538948
  22.8 4.4 %copy-start.3 = (bf16[3,768,256]{2,1,0:T(8,128)(2,1)S(1)}, bf16[3,768,256]{2,1,0:T(8,128)(2,1)}, u32[]{:S(2)}) copy-start(bf16[3,768,256]{2,1,0:T(8,128)(2,1)} %param.12) | copy-start | bytes 3538948
  23.8 11.7 %collective-permute-start.2 = (bf16[384,512]{1,0:T(8,128)(2,1)S(1)}, bf16[384,512]{1,0:T(8,128)(2,1)S(1)}, u32[]{:S(2)}, u32[]{:S(2)}) collective-permute-start(bf16[384,512]{1,0:T(8,128)(2,1)S(1)} %get-tuple-element.10.refs_0_), channel_id=1, source_target_pairs={{4,0},{0,4},{12,8},{8,12},{5,1},{1,5},{13,9},{9,13},{6,2},{2,6},{1... | collective-permute-start | bytes 1179656 | tf_op jit(solution)/shard_map/ppermute | solution.py:177
  26.9 5.9 %collective-permute-start.8 = (bf16[384,384]{1,0:T(8,128)(2,1)S(1)}, bf16[384,384]{1,0:T(8,128)(2,1)S(1)}, u32[]{:S(2)}, u32[]{:S(2)}) collective-permute-start(bf16[384,384]{1,0:T(8,128)(2,1)S(1)} %collective-permute-done.7.refs_0_), channel_id=1, source_target_pairs={{2,0},{0,2},{3,1},{1,3},{6,4},{4,6},{7,5},{5,7},{10,8},{8,10},{11,... | collective-permute-start | bytes 884744 | tf_op jit(solution)/shard_map/ppermute | solution.py:170
  27.2 8.4 %copy-start.4 = (bf16[256,768]{1,0:T(8,128)(2,1)S(1)}, bf16[256,768]{1,0:T(8,128)(2,1)}, u32[]{:S(2)}) copy-start(bf16[256,768]{1,0:T(8,128)(2,1)} %param.11) | copy-start | bytes 1179652
  33.7 7.1 %collective-permute-start.9 = (bf16[384,512]{1,0:T(8,128)(2,1)S(1)}, bf16[384,512]{1,0:T(8,128)(2,1)S(1)}, u32[]{:S(2)}, u32[]{:S(2)}) collective-permute-start(bf16[384,512]{1,0:T(8,128)(2,1)S(1)} %project.3.refs_0_), channel_id=1, source_target_pairs={{4,0},{0,4},{12,8},{8,12},{5,1},{1,5},{13,9},{9,13},{6,2},{2,6},{1... | collective-permute-start | bytes 1179656 | tf_op jit(solution)/shard_map/ppermute | solution.py:177
  33.7 7.0 %collective-permute-start.3 = (bf16[384,512]{1,0:T(8,128)(2,1)S(1)}, bf16[384,512]{1,0:T(8,128)(2,1)S(1)}, u32[]{:S(2)}, u32[]{:S(2)}) collective-permute-start(bf16[384,512]{1,0:T(8,128)(2,1)S(1)} %get-tuple-element.10.refs_0_), channel_id=1, source_target_pairs={{1,0},{0,1},{3,2},{2,3},{5,4},{4,5},{7,6},{6,7},{9,8},{8,9},{11,10... | collective-permute-start | bytes 1179656 | tf_op jit(solution)/shard_map/ppermute | solution.py:187
  35.6 5.2 %collective-permute-start.4 = (bf16[384,512]{1,0:T(8,128)(2,1)S(1)}, bf16[384,512]{1,0:T(8,128)(2,1)}, u32[]{:S(2)}, u32[]{:S(2)}) collective-permute-start(bf16[384,512]{1,0:T(8,128)(2,1)S(1)} %collective-permute-done.2.refs_1_), channel_id=1, source_target_pairs={{1,0},{0,1},{3,2},{2,3},{5,4},{4,5},{7,6},{6,7},{9,8},{8,9},{11,10... | collective-permute-start | bytes 1179656 | tf_op jit(solution)/shard_map/ppermute | solution.py:187
  36.0 14.1 %collective-permute-start.6 = (bf16[2,256,384]{2,1,0:T(8,128)(2,1)S(1)}, bf16[2,256,384]{2,1,0:T(8,128)(2,1)}, u32[]{:S(2)}, u32[]{:S(2)}) collective-permute-start(bf16[2,256,384]{2,1,0:T(8,128)(2,1)S(1)} %bitcast.15), channel_id=1, source_target_pairs={{2,0},{0,2},{3,1},{1,3},{6,4},{4,6},{7,5},{5,7},{10,8},{8,10},{11,... | collective-permute-start | bytes 1179656 | tf_op jit(solution)/shard_map/ppermute | solution.py:170
  36.4 18.4 %collective-permute-start.10 = (bf16[384,512]{1,0:T(8,128)(2,1)S(1)}, bf16[384,512]{1,0:T(8,128)(2,1)S(1)}, u32[]{:S(2)}, u32[]{:S(2)}) collective-permute-start(bf16[384,512]{1,0:T(8,128)(2,1)S(1)} %project.3.refs_0_), channel_id=1, source_target_pairs={{1,0},{0,1},{3,2},{2,3},{5,4},{4,5},{7,6},{6,7},{9,8},{8,9},{11,10... | collective-permute-start | bytes 1179656 | tf_op jit(solution)/shard_map/ppermute | solution.py:187
  40.8 14.1 %collective-permute-start.11 = (bf16[384,512]{1,0:T(8,128)(2,1)S(1)}, bf16[384,512]{1,0:T(8,128)(2,1)}, u32[]{:S(2)}, u32[]{:S(2)}) collective-permute-start(bf16[384,512]{1,0:T(8,128)(2,1)S(1)} %collective-permute-done.9.refs_1_), channel_id=1, source_target_pairs={{1,0},{0,1},{3,2},{2,3},{5,4},{4,5},{7,6},{6,7},{9,8},{8,9},{11,10... | collective-permute-start | bytes 1179656 | tf_op jit(solution)/shard_map/ppermute | solution.py:187
  46.1 4.0 %copy-start.2 = (bf16[384,256]{1,0:T(8,128)(2,1)S(1)}, bf16[384,256]{1,0:T(8,128)(2,1)}, u32[]{:S(2)}) copy-start(bf16[384,256]{1,0:T(8,128)(2,1)} %refs_5_.1) | copy-start | bytes 589828
  46.1 6.2 %collective-permute-start.5 = (bf16[384,256]{1,0:T(8,128)(2,1)}, bf16[384,256]{1,0:T(8,128)(2,1)S(1)}, u32[]{:S(2)}, u32[]{:S(2)}) collective-permute-start(bf16[384,256]{1,0:T(8,128)(2,1)} %attend.2.refs_0_), channel_id=1, source_target_pairs={{2,0},{0,2},{3,1},{1,3},{6,4},{4,6},{7,5},{5,7},{10,8},{8,10},{11,... | collective-permute-start | bytes 589832 | tf_op jit(solution)/shard_map/ppermute | solution.py:170
  47.7 17.2 %collective-permute-start.13 = (bf16[2,256,384]{2,1,0:T(8,128)(2,1)S(1)}, bf16[2,256,384]{2,1,0:T(8,128)(2,1)S(1)}, u32[]{:S(2)}, u32[]{:S(2)}) collective-permute-start(bf16[2,256,384]{2,1,0:T(8,128)(2,1)S(1)} %bitcast.12), channel_id=1, source_target_pairs={{2,0},{0,2},{3,1},{1,3},{6,4},{4,6},{7,5},{5,7},{10,8},{8,10},{11,... | collective-permute-start | bytes 1179656 | tf_op jit(solution)/shard_map/ppermute | solution.py:170
  50.1 14.8 %collective-permute-start.14 = (bf16[384,256]{1,0:T(8,128)(2,1)S(1)}, bf16[384,256]{1,0:T(8,128)(2,1)S(1)}, u32[]{:S(2)}, u32[]{:S(2)}) collective-permute-start(bf16[384,256]{1,0:T(8,128)(2,1)S(1)} %copy-done.2), channel_id=1, source_target_pairs={{2,0},{0,2},{3,1},{1,3},{6,4},{4,6},{7,5},{5,7},{10,8},{8,10},{11,... | collective-permute-start | bytes 589832 | tf_op jit(solution)/shard_map/ppermute | solution.py:170
  59.5 9.6 %collective-permute-start.12 = (bf16[384,256]{1,0:T(8,128)(2,1)S(1)}, bf16[384,256]{1,0:T(8,128)(2,1)S(1)}, u32[]{:S(2)}, u32[]{:S(2)}) collective-permute-start(bf16[384,256]{1,0:T(8,128)(2,1)S(1)} %attend.3.refs_0_), channel_id=1, source_target_pairs={{2,0},{0,2},{3,1},{1,3},{6,4},{4,6},{7,5},{5,7},{10,8},{8,10},{11,... | collective-permute-start | bytes 589832 | tf_op jit(solution)/shard_map/ppermute | solution.py:170
  69.1 17.6 %copy-start.1 = (bf16[3,3,256,256]{3,2,1,0:T(8,128)(2,1)S(1)}, bf16[3,3,256,256]{3,2,1,0:T(8,128)(2,1)}, u32[]{:S(2)}) copy-start(bf16[3,3,256,256]{3,2,1,0:T(8,128)(2,1)} %weight.1) | copy-start | bytes 3538948
  70.2 16.5 %collective-permute-start.15 = (bf16[3,96,256]{2,1,0:T(8,128)(2,1)S(1)}, bf16[3,96,256]{2,1,0:T(8,128)(2,1)S(1)}, u32[]{:S(2)}, u32[]{:S(2)}) collective-permute-start(bf16[3,96,256]{2,1,0:T(8,128)(2,1)S(1)} %finish.1), channel_id=1, source_target_pairs={{0,0},{8,1},{4,4},{12,5},{1,8},{9,9},{5,12},{13,13},{2,2},{10,3},{... | collective-permute-start | bytes 442376 | tf_op jit(solution)/shard_map/ppermute | solution.py:249
  76.1 5.3 %collective-permute-start.16 = (bf16[1,96,256]{2,1,0:T(8,128)(2,1)S(1)}, bf16[1,96,256]{2,1,0:T(8,128)(2,1)S(1)}, u32[]{:S(2)}, u32[]{:S(2)}) collective-permute-start(bf16[1,96,256]{2,1,0:T(8,128)(2,1)S(1)} %get-tuple-element.14), channel_id=1, source_target_pairs={{0,4},{8,5},{4,8},{12,9},{1,12},{9,13},{2,6},{10,7},{6,10},{14,11}... | collective-permute-start | bytes 147464 | tf_op jit(solution)/shard_map/ppermute | solution.py:250
  79.5 7.2 %collective-permute-start.17 = (bf16[1,96,256]{2,1,0:T(8,128)(2,1)S(1)}, bf16[1,96,256]{2,1,0:T(8,128)(2,1)S(1)}, u32[]{:S(2)}, u32[]{:S(2)}) collective-permute-start(bf16[1,96,256]{2,1,0:T(8,128)(2,1)S(1)} %get-tuple-element.13), channel_id=1, source_target_pairs={{4,0},{12,1},{1,4},{9,5},{5,8},{13,9},{6,2},{14,3},{3,6},{11,7},{7... | collective-permute-start | bytes 147464 | tf_op jit(solution)/shard_map/ppermute | solution.py:253

commit v2 on v1

--- a/solution.py
+++ b/solution.py
@@ -18,16 +18,16 @@
 SMEM = pl.BlockSpec(memory_space=pltpu.SMEM)
 
 
-def run_kernel(kernel, name, shapes, operands, flops, place=None):
+def run_kernel(kernel, name, shapes, operands, flops=0, place=None, scratch=()):
     leading = () if place is None else (place,)
-    moved = sum(v.size * 2 for v in operands) + sum(2 * math.prod(s) for s in shapes)
     return pl.pallas_call(
         kernel,
-        out_shape=[jax.ShapeDtypeStruct(s, BF16) for s in shapes],
+        out_shape=[jax.ShapeDtypeStruct(*s) for s in shapes],
         in_specs=[SMEM] * len(leading) + [VMEM] * len(operands),
         out_specs=[VMEM] * len(shapes),
-        compiler_params=pltpu.CompilerParams(vmem_limit_bytes=48 << 20),
-        cost_estimate=pl.CostEstimate(flops=flops, bytes_accessed=moved, transcendentals=0),
+        scratch_shapes=scratch,
+        compiler_params=pltpu.CompilerParams(vmem_limit_bytes=24 << 20),
+        cost_estimate=pl.CostEstimate(flops=flops, bytes_accessed=0, transcendentals=0),
         name=name,
     )(*leading, *operands)
 
@@ -64,11 +64,13 @@
         outs[-1][:, which * columns : (which + 1) * columns] = product.astype(BF16)
 
 
-def attend_kernel(query, *refs):
-    packs, out = refs[:-1], refs[-1]
+def attend_kernel(query, *refs, packed, resumed, final):
+    packs = refs[:packed]
+    before = refs[packed : packed + 2] if resumed else ()
+    outs = refs[packed + len(before) :]
     columns = query.shape[1]
     heads = []
-    for start in range(0, columns, HD):
+    for index, start in enumerate(range(0, columns, HD)):
         head = slice(start, start + HD)
         values = slice(columns + start, columns + start + HD)
         asked = query[:, head]
@@ -78,16 +80,42 @@
             )
             for pack in packs
         ]
-        maxima = functools.reduce(
-            jnp.maximum, [jnp.max(score, axis=1, keepdims=True) for score in scores]
-        )
+        tops = [jnp.max(score, axis=1, keepdims=True) for score in scores]
         total, mixed = 0.0, 0.0
+        if resumed:
+            stats = before[1][index]
+            tops.append(stats[:, :1])
+        maxima = functools.reduce(jnp.maximum, tops)
+        if resumed:
+            correction = jnp.exp2(stats[:, :1] - maxima)
+            total = stats[:, 1:2] * correction
+            mixed = before[0][index] * correction
         for score, pack in zip(scores, packs):
             expanded = jnp.exp2(score - maxima)
             total = total + jnp.sum(expanded, axis=1, keepdims=True)
             mixed = mixed + dot(expanded.astype(BF16), pack[:, values])
-        heads.append(mixed / total)
-    out[...] = jnp.concatenate(heads, axis=1).astype(BF16)
+        if final:
+            heads.append(mixed / total)
+        else:
+            outs[0][index] = mixed
+            outs[1][index] = jnp.concatenate([maxima, total], axis=1)
+    if final:
+        outs[0][...] = jnp.concatenate(heads, axis=1).astype(BF16)
+
+
+def pick(options, slot):
+    chosen = options[0]
+    for index in range(1, len(options)):
+        chosen = jnp.where(slot == index, options[index], chosen)
+    return chosen
+
+
+def shares(mixed, weights, place):
+    count = len(mixed)
+    whole = sum(dot(m[...], w[...]) for m, w in zip(mixed, weights))
+    share = whole.shape[1] // count
+    options = [whole[:, i * share : (i + 1) * share] for i in range(count)]
+    return [pick(options, lax.rem(place[0] + step, count)) for step in range(count)]
 
 
 def update_kernel(place, *refs, count):
@@ -95,9 +123,7 @@
     tokens, query_weight = refs[2 * count : 3 * count], refs[3 * count]
     updated, query = refs[3 * count + 1 :]
     pieces = []
-    for step in range(count):
-        slot = lax.rem(place[0] + step, count)
-        term = sum(dot(mixed[t][...], weights[t][slot]) for t in range(count))
+    for step, term in enumerate(shares(mixed, weights, place)):
         piece = (tokens[step][...].astype(F32) + term).astype(BF16)
         updated[step] = piece
         pieces.append(piece)
@@ -113,9 +139,7 @@
     updated, reassemble = refs[2 * count], refs[2 * count + 1 : 3 * count + 1]
     window, board = refs[3 * count + 1], refs[3 * count + 2]
     features = 0.0
-    for step in range(count):
-        slot = lax.rem(place[0] + step, count)
-        term = sum(dot(mixed[t][...], weights[t][slot]) for t in range(count))
+    for step, term in enumerate(shares(mixed, weights, place)):
         final = (updated[step].astype(F32) + term).astype(BF16)
         features = features + dot(final, reassemble[step][...])
     features = features.astype(BF16)
@@ -165,6 +189,9 @@
 
     places = [(band, pair) for band in range(bands) for pair in range(cores)]
 
+    def tied(values, *others):
+        return lax.optimization_barrier((values, others))[0]
+
     def tile_pieces(own):
         others = [
             lax.ppermute(own, "tile", [((i + s) % tiles, i) for i in range(tiles)])
@@ -172,80 +199,94 @@
         ]
         return [own, *others]
 
-    def gathered(pack):
-        near = [pack] + [
-            lax.ppermute(
-                pack,
-                "blk",
-                [(g * half + (i + s) % half, g * half + i) for g in range(cores) for i in range(half)],
-            )
+    def neighbours(pack):
+        ring = [(g * half, i) for g in range(cores) for i in range(half)]
+        return [
+            lax.ppermute(pack, "blk", [(g + (i + s) % half, g + i) for g, i in ring])
             for s in range(1, half)
         ]
-        packs = list(near)
-        for s in range(1, cores):
-            packs += [
-                lax.ppermute(p, "pair", [((i + s) % cores, i) for i in range(cores)]) for p in near
-            ]
-        if len(packs) > 4:
-            size = -(-len(packs) // 4)
-            packs = [jnp.concatenate(packs[i : i + size]) for i in range(0, len(packs), size)]
-        return packs
+
+    def across(pack):
+        return [
+            lax.ppermute(pack, "pair", [((i + s) % cores, i) for i in range(cores)])
+            for s in range(1, cores)
+        ]
+
+    def joined_packs(packs):
+        return [packs[0] if len(packs) == 1 else jnp.concatenate(packs)]
 
     def moved(tokens):
-        return lax.ppermute(tokens[0], both, [(home(*p), worker(*p)) for p in places])
+        return lax.ppermute(tokens, both, [(home(*p), worker(*p)) for p in places])
 
     def project(pieces, weights, scaled):
-        shapes = [(rows, columns)] * scaled + [(rows, 2 * columns)]
+        shapes = [((rows, columns), BF16)] * scaled + [((rows, 2 * columns), BF16)]
         stacked = weights.reshape(weights.shape[0], tiles, share, columns)
         return run_kernel(
             functools.partial(project_kernel, count=tiles, scaled=scaled),
             "project",
             shapes,
             [*pieces, stacked],
-            2 * rows * share * tiles * columns * weights.shape[0],
+            0,
             place,
         )
 
-    def attend(query, packs):
-        keys = sum(p.shape[0] for p in packs)
+    def attend(query, packs, state=(), final=False):
+        heads = columns // HD
+        shapes = [((heads, rows, HD), F32), ((heads, rows, 2), F32)]
+        if final:
+            shapes = [((rows, columns), BF16)]
         return run_kernel(
-            attend_kernel, "attend", [(rows, columns)], [query, *packs], 16 * rows * keys * columns
-        )[0]
-
-    def feature_blocks(weight):
-        return weight.reshape(columns, tiles, share).transpose(1, 0, 2)
-
-    left = tile_pieces(moved(left_tokens))
-    self_out_pieces = tile_pieces(feature_blocks(self_out))
-    cross_out_pieces = tile_pieces(feature_blocks(cross_out))
-    reassemble_pieces = tile_pieces(reassemble)
+            functools.partial(
+                attend_kernel, packed=len(packs), resumed=len(state) > 0, final=final
+            ),
+            "attend",
+            shapes,
+            [query, *packs, *state],
+        )
+
+    left_here = moved(left_tokens[0])
+    right = tile_pieces(right_tokens[0])
+    (right_pack,) = project(right, cross_qkv[1:], False)
+    left_here, right_pack = lax.optimization_barrier((left_here, right_pack))
+    right_pack = moved(right_pack)
+    left = tile_pieces(left_here)
     query, pack = project(left, self_qkv, True)
-    self_packs = gathered(pack)
-    right = tile_pieces(moved(right_tokens))
-    (pack,) = project(right, cross_qkv[1:], False)
-    cross_packs = gathered(pack)
-
-    mixed = tile_pieces(attend(query, self_packs))
+    self_out_pieces = tile_pieces(tied(self_out, left))
+    beside = neighbours(pack)
+    state = attend(query, [pack, *across(pack)])
+    beside = tied(beside, state)
+    far = [*beside, *[p for b in beside for p in across(b)]]
+    far, self_out_pieces = lax.optimization_barrier((far, self_out_pieces))
+    (own_mixed,) = attend(query, far if len(far) < 3 else joined_packs(far), state, True)
+
+    mixed = tile_pieces(own_mixed)
+    right_pack = tied(right_pack, own_mixed)
+    right_beside = neighbours(right_pack)
+    near = [right_pack, *across(right_pack)]
+    far = [*right_beside, *[p for b in right_beside for p in across(b)]]
+    reassemble_pieces = tile_pieces(tied(reassemble, mixed))
+    cross_out_pieces = tile_pieces(tied(cross_out, mixed))
     updated, cross_query = run_kernel(
         functools.partial(update_kernel, count=tiles),
         "update",
-        [(tiles, rows, share), (rows, columns)],
+        [((tiles, rows, share), BF16), ((rows, columns), BF16)],
         [*mixed, *self_out_pieces, *left, cross_qkv[0].reshape(tiles, share, columns)],
-        4 * rows * share * tiles * columns * tiles,
+        0,
         place,
     )
-    mixed = tile_pieces(attend(cross_query, cross_packs))
-    board = (band_rows, GRID_W + 2 * EDGE, channels)
-    operands = [*mixed, *cross_out_pieces, updated, *reassemble_pieces]
-    window = pl.pallas_call(
+    state = attend(cross_query, near)
+    far = tied(far, state)
+    (mixed,) = attend(cross_query, far if len(far) < 3 else joined_packs(far), state, True)
+    mixed = tile_pieces(mixed)
+    (window,) = run_kernel(
         functools.partial(finish_kernel, count=tiles, width=width),
-        out_shape=jax.ShapeDtypeStruct((band_rows, width + 2 * EDGE, channels), BF16),
-        in_specs=[SMEM] + [VMEM] * len(operands),
-        out_specs=VMEM,
-        scratch_shapes=[pltpu.VMEM(board, BF16)],
-        compiler_params=pltpu.CompilerParams(vmem_limit_bytes=48 << 20),
-        name="finish",
-    )(place, *operands)
+        "finish",
+        [((band_rows, width + 2 * EDGE, channels), BF16)],
+        [*mixed, *cross_out_pieces, updated, *reassemble_pieces],
+        0,
+        place,
+        [pltpu.VMEM((band_rows, GRID_W + 2 * EDGE, channels), BF16)],
+    )
     back = lax.ppermute(window, both, [(worker(*p), home(*p)) for p in places])
     above = lax.ppermute(
         window[-1:], both, [(worker(b, p), home(b + 1, p)) for b, p in places if b + 1 < bands]
@@ -256,9 +297,8 @@
     (joined,) = run_kernel(
         conv_kernel,
         "join",
-        [(band_rows, width, channels)],
+        [((band_rows, width, channels), BF16)],
         [back, above, below, conv_weight],
-        18 * band_rows * width * channels * channels,
     )
     return joined[None]
 

time: 88.2 us -> 99.8 us (1.13)
  starting transfers between devices: 25.1 us -> 33.6 us
  waiting for transfers between devices: 41.8 us -> 47 us
  local copies, waits for them, and re-layouts: 4.12 us -> 2.25 us
    ppermute x8, waiting for transfers between devices: 14.9 us -> 22.7 us  [the longest x2 11.4 us: neighbours(): lax.ppermute(pack, 'blk', [(g + (i + s) % half, g + i) for g, i in ring])]
    ppermute x8, starting transfers between devices: 9.97 us -> 14 us  [the longest x2 10.7 us: moved(): return lax.ppermute(tokens, both, [(home(*p), worker(*p)) for p in places])]
    ppermute x7, waiting for transfers between devices: 21.7 us -> 19 us  [tile_pieces(): lax.ppermute(own, 'tile', [((i + s) % tiles, i) for i in range(tiles)])]
    unnamed x12, local copies, waits for them, and re-layouts: 2.62 us -> 0.03 us
    ppermute x7, starting transfers between devices: 3.91 us -> 6.22 us  [tile_pieces(): lax.ppermute(own, 'tile', [((i + s) % tiles, i) for i in range(tiles)])]
    ppermute x1, starting transfers between devices: 5.9 us -> 8.09 us  [body(): back = lax.ppermute(window, both, [(worker(*p), home(*p)) for p in places])]
    slice x1, local copies, waits for them, and re-layouts: 0.05 us -> 1.19 us  [body(): right_pack, = project(right, cross_qkv[1:], False)]
    pallas_call x7 -> x9, Pallas kernels: 16.6 us -> 16.4 us  [run_kernel(): pl.pallas_call(kernel, out_shape=[jax.ShapeDtypeStruct(*s) for s in shape...]
  transfers between devices with their start and end apart: 18 -> 18, of which waited for: 10 -> 10; matrix products, arithmetic and copies ran while one was open for 3% -> 2% of each run, Pallas kernels for 16% -> 13%
where the time goes in v2:
time: 99.8 us; the launch traced here: 99.5 us
  waiting for transfers between devices  47 us (47%)
  starting transfers between devices  33.6 us (34%)
  Pallas kernels  16.4 us (16%)
  local copies, waits for them, and re-layouts  2.25 us (2%)
    ppermute x7, waiting for transfers between devices, tile_pieces(): lax.ppermute(own, 'tile', [((i + s) % tiles, i) for i in range(tiles)])  19 us
    pallas_call x9, Pallas kernels, run_kernel(): pl.pallas_call(kernel, out_shape=[jax.ShapeDtypeStruct(*s) for s in shape...  16.4 us
    ppermute x2, waiting for transfers between devices, neighbours(): lax.ppermute(pack, 'blk', [(g + (i + s) % half, g + i) for g, i in ring])  11.4 us
    ppermute x2, waiting for transfers between devices, moved(): return lax.ppermute(tokens, both, [(home(*p), worker(*p)) for p in places])  11.3 us
    ppermute x2, starting transfers between devices, moved(): return lax.ppermute(tokens, both, [(home(*p), worker(*p)) for p in places])  10.7 us
    ppermute x1, starting transfers between devices, body(): back = lax.ppermute(window, both, [(worker(*p), home(*p)) for p in places])  8.09 us
    ppermute x7, starting transfers between devices, tile_pieces(): lax.ppermute(own, 'tile', [((i + s) % tiles, i) for i in range(tiles)])  6.22 us
    ppermute x1, waiting for transfers between devices, body(): lax.ppermute(window[:1], both, [(worker(b, p), home(b - 1, p)) for b, p i...  5.27 us
  transfers between devices with their start and end apart: 18, of which 10 were waited for; matrix products, arithmetic and copies ran while one was open for 2% of the time, Pallas kernels for 13%

profile of v2, /device:TPU:1, one launch (start us, length us, event | category | flops | bytes accessed | tf_op | source)
XLA Modules:
  0.0 99.5 jit_solution(16431253428060029153)
XLA Ops:
  0.0 2.0 %collective-permute-start.1 = (bf16[384,384]{1,0:T(8,128)(2,1)}, bf16[384,384]{1,0:T(8,128)(2,1)S(1)}, u32[]{:S(2)}, u32[]{:S(2)}) collective-permute-start(bf16[384,384]{1,0:T(8,128)(2,1)} %bitcast.10), channel_id=1, source_target_pairs={{2,0},{0,2},{3,1},{1,3},{6,4},{4,6},{7,5},{5,7},{10,8},{8,10},{11,... | collective-permute-start | bytes 884744 | tf_op jit(solution)/shard_map/ppermute | solution.py:197
  2.0 5.0 %collective-permute-start = (bf16[384,384]{1,0:T(8,128)(2,1)}, bf16[384,384]{1,0:T(8,128)(2,1)S(1)}, u32[]{:S(2)}, u32[]{:S(2)}) collective-permute-start(bf16[384,384]{1,0:T(8,128)(2,1)} %bitcast.12), channel_id=1, source_target_pairs={{0,0},{1,8},{4,4},{5,12},{8,1},{9,9},{12,5},{13,13},{2,2},{3,10},{... | collective-permute-start | bytes 884744 | tf_op jit(solution)/shard_map/ppermute | solution.py:219
  7.1 1.2 %slice.12 = bf16[2,768,256]{2,1,0:T(8,128)(2,1)S(1)} slice(bf16[3,768,256]{2,1,0:T(8,128)(2,1)} %param.12), slice={[1:3], [0:768], [0:256]} | slice | bytes 1572864 | tf_op jit(solution)/shard_map/slice | solution.py:249
  9.9 4.9 %collective-permute-done.refs_0_.refs_4_ = bf16[384,384]{1,0:T(8,128)(2,1)S(1)} collective-permute-done((bf16[384,384]{1,0:T(8,128)(2,1)}, bf16[384,384]{1,0:T(8,128)(2,1)S(1)}, u32[]{:S(2)}, u32[]{:S(2)}) %collective-permute-start) | collective-permute-done | bytes 294944 | tf_op jit(solution)/shard_map/ppermute | solution.py:219
  15.1 5.3 %collective-permute-done.2.refs_1_.refs_5_ = bf16[384,384]{1,0:T(8,128)(2,1)S(1)} collective-permute-done((bf16[384,384]{1,0:T(8,128)(2,1)S(1)}, bf16[384,384]{1,0:T(8,128)(2,1)S(1)}, u32[]{:S(2)}, u32[]{:S(2)}) %collective-permute-start.2) | collective-permute-done | bytes 294944 | tf_op jit(solution)/shard_map/ppermute | solution.py:197
  21.6 1.5 %collective-permute-start.3 = (bf16[384,512]{1,0:T(8,128)(2,1)S(1)}, bf16[384,512]{1,0:T(8,128)(2,1)S(1)}, u32[]{:S(2)}, u32[]{:S(2)}) collective-permute-start(bf16[384,512]{1,0:T(8,128)(2,1)S(1)} %get-tuple-element.28.refs_0_), channel_id=1, source_target_pairs={{4,0},{0,4},{12,8},{8,12},{5,1},{1,5},{13,9},{9,13},{6,2},{2,6},{1... | collective-permute-start | bytes 1179656 | tf_op jit(solution)/shard_map/ppermute | solution.py:205
  23.1 1.2 %collective-permute-start.6 = (bf16[256,768]{1,0:T(8,128)(2,1)S(1)}, bf16[256,768]{1,0:T(8,128)(2,1)S(1)}, u32[]{:S(2)}, u32[]{:S(2)}) collective-permute-start(bf16[256,768]{1,0:T(8,128)(2,1)S(1)} %copy-done.2), channel_id=1, source_target_pairs={{2,0},{0,2},{3,1},{1,3},{6,4},{4,6},{7,5},{5,7},{10,8},{8,10},{11,... | collective-permute-start | bytes 1179656 | tf_op jit(solution)/shard_map/ppermute | solution.py:197
  24.4 2.3 %attend.4 = (f32[4,384,64]{2,1,0:T(8,128)S(1)}, f32[4,384,2]{2,1,0:T(8,128)S(1)}) custom-call(bf16[384,256]{1,0:T(8,128)(2,1)S(1)} %get-tuple-element.27.query, bf16[384,512]{1,0:T(8,128)(2,1)S(1)} %get-tuple-element.28.refs_0_, bf16[384,512]{1,0:T(8,128)(2,1)S(1)} %collective-permute-done.4.refs_1_), custom_call_target="tpu_custom_call" | custom-call | tf_op jit(solution)/shard_map/attend/pallas_call | solution.py:23
  26.6 5.3 %collective-permute-done.3.refs_0_ = bf16[384,512]{1,0:T(8,128)(2,1)S(1)} collective-permute-done((bf16[384,512]{1,0:T(8,128)(2,1)S(1)}, bf16[384,512]{1,0:T(8,128)(2,1)S(1)}, u32[]{:S(2)}, u32[]{:S(2)}) %collective-permute-start.3) | collective-permute-done | bytes 393248 | tf_op jit(solution)/shard_map/ppermute | solution.py:205
  31.9 1.3 %collective-permute-start.5 = (bf16[384,512]{1,0:T(8,128)(2,1)S(1)}, bf16[384,512]{1,0:T(8,128)(2,1)S(1)}, u32[]{:S(2)}, u32[]{:S(2)}) collective-permute-start(bf16[384,512]{1,0:T(8,128)(2,1)S(1)} %collective-permute-done.3.refs_0_), channel_id=1, source_target_pairs={{1,0},{0,1},{3,2},{2,3},{5,4},{4,5},{7,6},{6,7},{9,8},{8,9},{11,10... | collective-permute-start | bytes 1179656 | tf_op jit(solution)/shard_map/ppermute | solution.py:211
  33.2 5.6 %collective-permute-start.8 = (bf16[384,512]{1,0:T(8,128)(2,1)S(1)}, bf16[384,512]{1,0:T(8,128)(2,1)S(1)}, u32[]{:S(2)}, u32[]{:S(2)}) collective-permute-start(bf16[384,512]{1,0:T(8,128)(2,1)S(1)} %project.2), channel_id=1, source_target_pairs={{0,0},{1,8},{4,4},{5,12},{8,1},{9,9},{12,5},{13,13},{2,2},{3,10},{... | collective-permute-start | bytes 1179656 | tf_op jit(solution)/shard_map/ppermute | solution.py:219
  38.9 3.1 %attend.5.refs_0_ = bf16[384,256]{1,0:T(8,128)(2,1)S(1)} custom-call(bf16[384,256]{1,0:T(8,128)(2,1)S(1)} %get-tuple-element.27.query, bf16[384,512]{1,0:T(8,128)(2,1)S(1)} %collective-permute-done.3.refs_0_, bf16[384,512]{1,0:T(8,128)(2,1)S(1)} %collective-permute-done.5.refs_1_, f32[4,384,64]{2,1,0:T(8,128)S(1)} %get-tuple-element.29.refs_2_, ...), custom_call_target="tpu_custom_call" | custom-call | tf_op jit(solution)/shard_map/attend/pallas_call | solution.py:23
  42.0 6.3 %collective-permute-done.8.refs_0_ = bf16[384,512]{1,0:T(8,128)(2,1)S(1)} collective-permute-done((bf16[384,512]{1,0:T(8,128)(2,1)S(1)}, bf16[384,512]{1,0:T(8,128)(2,1)S(1)}, u32[]{:S(2)}, u32[]{:S(2)}) %collective-permute-start.8) | collective-permute-done | bytes 393248 | tf_op jit(solution)/shard_map/ppermute | solution.py:219
  48.8 6.1 %collective-permute-done.9.refs_0_ = bf16[384,512]{1,0:T(8,128)(2,1)S(1)} collective-permute-done((bf16[384,512]{1,0:T(8,128)(2,1)S(1)}, bf16[384,512]{1,0:T(8,128)(2,1)S(1)}, u32[]{:S(2)}, u32[]{:S(2)}) %collective-permute-start.9) | collective-permute-done | bytes 393248 | tf_op jit(solution)/shard_map/ppermute | solution.py:205
  55.5 5.4 %collective-permute-done.7.refs_1_ = bf16[384,256]{1,0:T(8,128)(2,1)S(1)} collective-permute-done((bf16[384,256]{1,0:T(8,128)(2,1)S(1)}, bf16[384,256]{1,0:T(8,128)(2,1)S(1)}, u32[]{:S(2)}, u32[]{:S(2)}) %collective-permute-start.7) | collective-permute-done | bytes 196640 | tf_op jit(solution)/shard_map/ppermute | solution.py:197
  63.5 1.5 %update.1 = (bf16[2,384,384]{2,1,0:T(8,128)(2,1)S(1)}, bf16[384,256]{1,0:T(8,128)(2,1)S(1)}) custom-call(s32[1]{0:T(128)} %bitcast.place, bf16[384,256]{1,0:T(8,128)(2,1)S(1)} %attend.5.refs_0_, bf16[384,256]{1,0:T(8,128)(2,1)S(1)} %collective-permute-done.7.refs_1_, bf16[256,768]{1,0:T(8,128)(2,1)S(1)} %copy-done.2, ...), custom_call_target="tpu_custom_call" | custom-call | tf_op jit(solution)/shard_map/update/pallas_call | solution.py:23
  65.0 2.3 %attend.6 = (f32[4,384,64]{2,1,0:T(8,128)S(1)}, f32[4,384,2]{2,1,0:T(8,128)S(1)}) custom-call(bf16[384,256]{1,0:T(8,128)(2,1)S(1)} %get-tuple-element.37.query, bf16[384,512]{1,0:T(8,128)(2,1)S(1)} %collective-permute-done.8.refs_0_, bf16[384,512]{1,0:T(8,128)(2,1)S(1)} %collective-permute-done.11.refs_1_), custom_call_target="tpu_custom_call" | custom-call | tf_op jit(solution)/shard_map/attend/pallas_call | solution.py:23
  67.3 3.1 %attend.7.refs_0_ = bf16[384,256]{1,0:T(8,128)(2,1)S(1)} custom-call(bf16[384,256]{1,0:T(8,128)(2,1)S(1)} %get-tuple-element.37.query, bf16[384,512]{1,0:T(8,128)(2,1)S(1)} %collective-permute-done.9.refs_0_, bf16[384,512]{1,0:T(8,128)(2,1)S(1)} %collective-permute-done.10.refs_1_, f32[4,384,64]{2,1,0:T(8,128)S(1)} %get-tuple-element.40.refs_2_, ...), custom_call_target="tpu_custom_call" | custom-call | tf_op jit(solution)/shard_map/attend/pallas_call | solution.py:23
  71.0 3.4 %collective-permute-done.14.refs_6_ = bf16[384,256]{1,0:T(8,128)(2,1)S(1)} collective-permute-done((bf16[384,256]{1,0:T(8,128)(2,1)S(1)}, bf16[384,256]{1,0:T(8,128)(2,1)S(1)}, u32[]{:S(2)}, u32[]{:S(2)}) %collective-permute-start.14) | collective-permute-done | bytes 196640 | tf_op jit(solution)/shard_map/ppermute | solution.py:197
  74.4 4.2 %collective-permute-done.12.refs_1_ = bf16[384,256]{1,0:T(8,128)(2,1)S(1)} collective-permute-done((bf16[384,256]{1,0:T(8,128)(2,1)S(1)}, bf16[384,256]{1,0:T(8,128)(2,1)S(1)}, u32[]{:S(2)}, u32[]{:S(2)}) %collective-permute-start.12) | collective-permute-done | bytes 196640 | tf_op jit(solution)/shard_map/ppermute | solution.py:197
  79.7 8.1 %collective-permute-start.15 = (bf16[3,96,256]{2,1,0:T(8,128)(2,1)S(1)}, bf16[3,96,256]{2,1,0:T(8,128)(2,1)S(1)}, u32[]{:S(2)}, u32[]{:S(2)}) collective-permute-start(bf16[3,96,256]{2,1,0:T(8,128)(2,1)S(1)} %finish.1), channel_id=1, source_target_pairs={{0,0},{8,1},{4,4},{12,5},{1,8},{9,9},{5,12},{13,13},{2,2},{10,3},{... | collective-permute-start | bytes 442376 | tf_op jit(solution)/shard_map/ppermute | solution.py:290
  87.8 3.4 %collective-permute-start.16 = (bf16[1,96,256]{2,1,0:T(8,128)(2,1)S(1)}, bf16[1,96,256]{2,1,0:T(8,128)(2,1)S(1)}, u32[]{:S(2)}, u32[]{:S(2)}) collective-permute-start(bf16[1,96,256]{2,1,0:T(8,128)(2,1)S(1)} %get-tuple-element.48), channel_id=1, source_target_pairs={{0,4},{8,5},{4,8},{12,9},{1,12},{9,13},{2,6},{10,7},{6,10},{14,11}... | collective-permute-start | bytes 147464 | tf_op jit(solution)/shard_map/ppermute | solution.py:291
  91.2 1.9 %collective-permute-start.17 = (bf16[1,96,256]{2,1,0:T(8,128)(2,1)S(1)}, bf16[1,96,256]{2,1,0:T(8,128)(2,1)S(1)}, u32[]{:S(2)}, u32[]{:S(2)}) collective-permute-start(bf16[1,96,256]{2,1,0:T(8,128)(2,1)S(1)} %get-tuple-element.47), channel_id=1, source_target_pairs={{4,0},{12,1},{1,4},{9,5},{5,8},{13,9},{6,2},{14,3},{3,6},{11,7},{7... | collective-permute-start | bytes 147464 | tf_op jit(solution)/shard_map/ppermute | solution.py:294
  93.1 5.3 %collective-permute-done.17.below = bf16[1,96,256]{2,1,0:T(8,128)(2,1)S(1)} collective-permute-done((bf16[1,96,256]{2,1,0:T(8,128)(2,1)S(1)}, bf16[1,96,256]{2,1,0:T(8,128)(2,1)S(1)}, u32[]{:S(2)}, u32[]{:S(2)}) %collective-permute-start.17) | collective-permute-done | bytes 49184 | tf_op jit(solution)/shard_map/ppermute | solution.py:294
  (36 shorter events, 9.4 us)
Async XLA Ops:
  0.0 9.1 %copy-start.4 = (bf16[1,384,384]{2,1,0:T(8,128)(2,1)S(1)}, bf16[1,384,384]{2,1,0:T(8,128)(2,1)}, u32[]{:S(2)}) copy-start(bf16[1,384,384]{2,1,0:T(8,128)(2,1)} %param.9) | copy-start | bytes 884740
  0.0 9.1 %collective-permute-start.1 = (bf16[384,384]{1,0:T(8,128)(2,1)}, bf16[384,384]{1,0:T(8,128)(2,1)S(1)}, u32[]{:S(2)}, u32[]{:S(2)}) collective-permute-start(bf16[384,384]{1,0:T(8,128)(2,1)} %bitcast.10), channel_id=1, source_target_pairs={{2,0},{0,2},{3,1},{1,3},{6,4},{4,6},{7,5},{5,7},{10,8},{8,10},{11,... | collective-permute-start | bytes 884744 | tf_op jit(solution)/shard_map/ppermute | solution.py:197
  2.0 12.8 %collective-permute-start = (bf16[384,384]{1,0:T(8,128)(2,1)}, bf16[384,384]{1,0:T(8,128)(2,1)S(1)}, u32[]{:S(2)}, u32[]{:S(2)}) collective-permute-start(bf16[384,384]{1,0:T(8,128)(2,1)} %bitcast.12), channel_id=1, source_target_pairs={{0,0},{1,8},{4,4},{5,12},{8,1},{9,9},{12,5},{13,13},{2,2},{3,10},{... | collective-permute-start | bytes 884744 | tf_op jit(solution)/shard_map/ppermute | solution.py:219
  8.3 12.1 %copy-start = (bf16[3,768,256]{2,1,0:T(8,128)(2,1)S(1)}, bf16[3,768,256]{2,1,0:T(8,128)(2,1)}, u32[]{:S(2)}) copy-start(bf16[3,768,256]{2,1,0:T(8,128)(2,1)} %param.10) | copy-start | bytes 3538948
  9.9 13.2 %copy-start.2 = (bf16[256,768]{1,0:T(8,128)(2,1)S(1)}, bf16[256,768]{1,0:T(8,128)(2,1)}, u32[]{:S(2)}) copy-start(bf16[256,768]{1,0:T(8,128)(2,1)} %refs_2_) | copy-start | bytes 1179652
  14.9 5.6 %collective-permute-start.2 = (bf16[384,384]{1,0:T(8,128)(2,1)S(1)}, bf16[384,384]{1,0:T(8,128)(2,1)S(1)}, u32[]{:S(2)}, u32[]{:S(2)}) collective-permute-start(bf16[384,384]{1,0:T(8,128)(2,1)S(1)} %collective-permute-done.refs_0_.refs_4_), channel_id=1, source_target_pairs={{2,0},{0,2},{3,1},{1,3},{6,4},{4,6},{7,5},{5,7},{10,8},{8,10},{11,... | collective-permute-start | bytes 884744 | tf_op jit(solution)/shard_map/ppermute | solution.py:197
  21.5 2.8 %collective-permute-start.4 = (bf16[384,512]{1,0:T(8,128)(2,1)S(1)}, bf16[384,512]{1,0:T(8,128)(2,1)S(1)}, u32[]{:S(2)}, u32[]{:S(2)}) collective-permute-start(bf16[384,512]{1,0:T(8,128)(2,1)S(1)} %get-tuple-element.28.refs_0_), channel_id=1, source_target_pairs={{1,0},{0,1},{3,2},{2,3},{5,4},{4,5},{7,6},{6,7},{9,8},{8,9},{11,10... | collective-permute-start | bytes 1179656 | tf_op jit(solution)/shard_map/ppermute | solution.py:211
  21.6 10.3 %collective-permute-start.3 = (bf16[384,512]{1,0:T(8,128)(2,1)S(1)}, bf16[384,512]{1,0:T(8,128)(2,1)S(1)}, u32[]{:S(2)}, u32[]{:S(2)}) collective-permute-start(bf16[384,512]{1,0:T(8,128)(2,1)S(1)} %get-tuple-element.28.refs_0_), channel_id=1, source_target_pairs={{4,0},{0,4},{12,8},{8,12},{5,1},{1,5},{13,9},{9,13},{6,2},{2,6},{1... | collective-permute-start | bytes 1179656 | tf_op jit(solution)/shard_map/ppermute | solution.py:205
  23.1 15.7 %collective-permute-start.6 = (bf16[256,768]{1,0:T(8,128)(2,1)S(1)}, bf16[256,768]{1,0:T(8,128)(2,1)S(1)}, u32[]{:S(2)}, u32[]{:S(2)}) collective-permute-start(bf16[256,768]{1,0:T(8,128)(2,1)S(1)} %copy-done.2), channel_id=1, source_target_pairs={{2,0},{0,2},{3,1},{1,3},{6,4},{4,6},{7,5},{5,7},{10,8},{8,10},{11,... | collective-permute-start | bytes 1179656 | tf_op jit(solution)/shard_map/ppermute | solution.py:197
  31.9 29.0 %copy-start.3 = (bf16[256,768]{1,0:T(8,128)(2,1)S(1)}, bf16[256,768]{1,0:T(8,128)(2,1)}, u32[]{:S(2)}) copy-start(bf16[256,768]{1,0:T(8,128)(2,1)} %refs_2_.1) | copy-start | bytes 1179652
  31.9 30.6 %copy-start.5 = (bf16[384,256]{1,0:T(8,128)(2,1)S(1)}, bf16[384,256]{1,0:T(8,128)(2,1)}, u32[]{:S(2)}) copy-start(bf16[384,256]{1,0:T(8,128)(2,1)} %refs_5_) | copy-start | bytes 589828
  31.9 6.9 %collective-permute-start.5 = (bf16[384,512]{1,0:T(8,128)(2,1)S(1)}, bf16[384,512]{1,0:T(8,128)(2,1)S(1)}, u32[]{:S(2)}, u32[]{:S(2)}) collective-permute-start(bf16[384,512]{1,0:T(8,128)(2,1)S(1)} %collective-permute-done.3.refs_0_), channel_id=1, source_target_pairs={{1,0},{0,1},{3,2},{2,3},{5,4},{4,5},{7,6},{6,7},{9,8},{8,9},{11,10... | collective-permute-start | bytes 1179656 | tf_op jit(solution)/shard_map/ppermute | solution.py:211
  33.2 15.1 %collective-permute-start.8 = (bf16[384,512]{1,0:T(8,128)(2,1)S(1)}, bf16[384,512]{1,0:T(8,128)(2,1)S(1)}, u32[]{:S(2)}, u32[]{:S(2)}) collective-permute-start(bf16[384,512]{1,0:T(8,128)(2,1)S(1)} %project.2), channel_id=1, source_target_pairs={{0,0},{1,8},{4,4},{5,12},{8,1},{9,9},{12,5},{13,13},{2,2},{3,10},{... | collective-permute-start | bytes 1179656 | tf_op jit(solution)/shard_map/ppermute | solution.py:219
  48.3 6.6 %collective-permute-start.9 = (bf16[384,512]{1,0:T(8,128)(2,1)S(1)}, bf16[384,512]{1,0:T(8,128)(2,1)S(1)}, u32[]{:S(2)}, u32[]{:S(2)}) collective-permute-start(bf16[384,512]{1,0:T(8,128)(2,1)S(1)} %collective-permute-done.8.refs_0_), channel_id=1, source_target_pairs={{4,0},{0,4},{12,8},{8,12},{5,1},{1,5},{13,9},{9,13},{6,2},{2,6},{1... | collective-permute-start | bytes 1179656 | tf_op jit(solution)/shard_map/ppermute | solution.py:205
  48.8 16.2 %collective-permute-start.11 = (bf16[384,512]{1,0:T(8,128)(2,1)S(1)}, bf16[384,512]{1,0:T(8,128)(2,1)S(1)}, u32[]{:S(2)}, u32[]{:S(2)}) collective-permute-start(bf16[384,512]{1,0:T(8,128)(2,1)S(1)} %collective-permute-done.8.refs_0_), channel_id=1, source_target_pairs={{1,0},{0,1},{3,2},{2,3},{5,4},{4,5},{7,6},{6,7},{9,8},{8,9},{11,10... | collective-permute-start | bytes 1179656 | tf_op jit(solution)/shard_map/ppermute | solution.py:211
  55.0 12.3 %collective-permute-start.10 = (bf16[384,512]{1,0:T(8,128)(2,1)S(1)}, bf16[384,512]{1,0:T(8,128)(2,1)S(1)}, u32[]{:S(2)}, u32[]{:S(2)}) collective-permute-start(bf16[384,512]{1,0:T(8,128)(2,1)S(1)} %collective-permute-done.9.refs_0_), channel_id=1, source_target_pairs={{1,0},{0,1},{3,2},{2,3},{5,4},{4,5},{7,6},{6,7},{9,8},{8,9},{11,10... | collective-permute-start | bytes 1179656 | tf_op jit(solution)/shard_map/ppermute | solution.py:211
  55.0 6.0 %collective-permute-start.7 = (bf16[384,256]{1,0:T(8,128)(2,1)S(1)}, bf16[384,256]{1,0:T(8,128)(2,1)S(1)}, u32[]{:S(2)}, u32[]{:S(2)}) collective-permute-start(bf16[384,256]{1,0:T(8,128)(2,1)S(1)} %attend.5.refs_0_), channel_id=1, source_target_pairs={{2,0},{0,2},{3,1},{1,3},{6,4},{4,6},{7,5},{5,7},{10,8},{8,10},{11,... | collective-permute-start | bytes 589832 | tf_op jit(solution)/shard_map/ppermute | solution.py:197
  60.9 13.5 %collective-permute-start.13 = (bf16[256,768]{1,0:T(8,128)(2,1)S(1)}, bf16[256,768]{1,0:T(8,128)(2,1)S(1)}, u32[]{:S(2)}, u32[]{:S(2)}) collective-permute-start(bf16[256,768]{1,0:T(8,128)(2,1)S(1)} %copy-done.3), channel_id=1, source_target_pairs={{2,0},{0,2},{3,1},{1,3},{6,4},{4,6},{7,5},{5,7},{10,8},{8,10},{11,... | collective-permute-start | bytes 1179656 | tf_op jit(solution)/shard_map/ppermute | solution.py:197
  62.5 11.9 %collective-permute-start.14 = (bf16[384,256]{1,0:T(8,128)(2,1)S(1)}, bf16[384,256]{1,0:T(8,128)(2,1)S(1)}, u32[]{:S(2)}, u32[]{:S(2)}) collective-permute-start(bf16[384,256]{1,0:T(8,128)(2,1)S(1)} %copy-done.5), channel_id=1, source_target_pairs={{2,0},{0,2},{3,1},{1,3},{6,4},{4,6},{7,5},{5,7},{10,8},{8,10},{11,... | collective-permute-start | bytes 589832 | tf_op jit(solution)/shard_map/ppermute | solution.py:197
  70.4 8.2 %collective-permute-start.12 = (bf16[384,256]{1,0:T(8,128)(2,1)S(1)}, bf16[384,256]{1,0:T(8,128)(2,1)S(1)}, u32[]{:S(2)}, u32[]{:S(2)}) collective-permute-start(bf16[384,256]{1,0:T(8,128)(2,1)S(1)} %attend.7.refs_0_), channel_id=1, source_target_pairs={{2,0},{0,2},{3,1},{1,3},{6,4},{4,6},{7,5},{5,7},{10,8},{8,10},{11,... | collective-permute-start | bytes 589832 | tf_op jit(solution)/shard_map/ppermute | solution.py:197
  78.6 19.8 %copy-start.1 = (bf16[3,3,256,256]{3,2,1,0:T(8,128)(2,1)S(1)}, bf16[3,3,256,256]{3,2,1,0:T(8,128)(2,1)}, u32[]{:S(2)}) copy-start(bf16[3,3,256,256]{3,2,1,0:T(8,128)(2,1)} %weight.1) | copy-start | bytes 3538948
  79.7 18.7 %collective-permute-start.15 = (bf16[3,96,256]{2,1,0:T(8,128)(2,1)S(1)}, bf16[3,96,256]{2,1,0:T(8,128)(2,1)S(1)}, u32[]{:S(2)}, u32[]{:S(2)}) collective-permute-start(bf16[3,96,256]{2,1,0:T(8,128)(2,1)S(1)} %finish.1), channel_id=1, source_target_pairs={{0,0},{8,1},{4,4},{12,5},{1,8},{9,9},{5,12},{13,13},{2,2},{10,3},{... | collective-permute-start | bytes 442376 | tf_op jit(solution)/shard_map/ppermute | solution.py:290
  87.8 5.3 %collective-permute-start.16 = (bf16[1,96,256]{2,1,0:T(8,128)(2,1)S(1)}, bf16[1,96,256]{2,1,0:T(8,128)(2,1)S(1)}, u32[]{:S(2)}, u32[]{:S(2)}) collective-permute-start(bf16[1,96,256]{2,1,0:T(8,128)(2,1)S(1)} %get-tuple-element.48), channel_id=1, source_target_pairs={{0,4},{8,5},{4,8},{12,9},{1,12},{9,13},{2,6},{10,7},{6,10},{14,11}... | collective-permute-start | bytes 147464 | tf_op jit(solution)/shard_map/ppermute | solution.py:291
  91.2 7.2 %collective-permute-start.17 = (bf16[1,96,256]{2,1,0:T(8,128)(2,1)S(1)}, bf16[1,96,256]{2,1,0:T(8,128)(2,1)S(1)}, u32[]{:S(2)}, u32[]{:S(2)}) collective-permute-start(bf16[1,96,256]{2,1,0:T(8,128)(2,1)S(1)} %get-tuple-element.47), channel_id=1, source_target_pairs={{4,0},{12,1},{1,4},{9,5},{5,8},{13,9},{6,2},{14,3},{3,6},{11,7},{7... | collective-permute-start | bytes 147464 | tf_op jit(solution)/shard_map/ppermute | solution.py:294

commit v3 on v2

--- a/solution.py
+++ b/solution.py
@@ -251,32 +251,37 @@
     right_pack = moved(right_pack)
     left = tile_pieces(left_here)
     query, pack = project(left, self_qkv, True)
+    near = [pack, *across(pack)]
+    beside = neighbours(pack)
+    query_weight = cross_qkv[0].reshape(tiles, share, columns)
+    near, right_pack, query_weight = lax.optimization_barrier((near, right_pack, query_weight))
     self_out_pieces = tile_pieces(tied(self_out, left))
-    beside = neighbours(pack)
-    state = attend(query, [pack, *across(pack)])
-    beside = tied(beside, state)
+    state = attend(query, near)
+    beside, right_pack = tied((beside, right_pack), state)
     far = [*beside, *[p for b in beside for p in across(b)]]
+    right_near = [right_pack, *across(right_pack)]
+    right_beside = neighbours(right_pack)
     far, self_out_pieces = lax.optimization_barrier((far, self_out_pieces))
     (own_mixed,) = attend(query, far if len(far) < 3 else joined_packs(far), state, True)
 
     mixed = tile_pieces(own_mixed)
-    right_pack = tied(right_pack, own_mixed)
-    right_beside = neighbours(right_pack)
-    near = [right_pack, *across(right_pack)]
-    far = [*right_beside, *[p for b in right_beside for p in across(b)]]
     reassemble_pieces = tile_pieces(tied(reassemble, mixed))
     cross_out_pieces = tile_pieces(tied(cross_out, mixed))
+    right_beside = tied(right_beside, mixed)
+    right_far = [*right_beside, *[p for b in right_beside for p in across(b)]]
     updated, cross_query = run_kernel(
         functools.partial(update_kernel, count=tiles),
         "update",
         [((tiles, rows, share), BF16), ((rows, columns), BF16)],
-        [*mixed, *self_out_pieces, *left, cross_qkv[0].reshape(tiles, share, columns)],
+        [*mixed, *self_out_pieces, *left, query_weight],
         0,
         place,
     )
-    state = attend(cross_query, near)
-    far = tied(far, state)
-    (mixed,) = attend(cross_query, far if len(far) < 3 else joined_packs(far), state, True)
+    state = attend(cross_query, right_near)
+    right_far = tied(right_far, state)
+    (mixed,) = attend(
+        cross_query, right_far if len(right_far) < 3 else joined_packs(right_far), state, True
+    )
     mixed = tile_pieces(mixed)
     (window,) = run_kernel(
         functools.partial(finish_kernel, count=tiles, width=width),

time: 99.8 us -> 84.2 us (0.84)
  waiting for transfers between devices: 47 us -> 36 us
  starting transfers between devices: 33.6 us -> 29.1 us
    ppermute x7, waiting for transfers between devices: 19 us -> 13.3 us  [tile_pieces(): lax.ppermute(own, 'tile', [((i + s) % tiles, i) for i in range(tiles)])]
    ppermute x2, waiting for transfers between devices: 11.4 us -> 7.21 us  [neighbours(): lax.ppermute(pack, 'blk', [(g + (i + s) % half, g + i) for g, i in ring])]
    ppermute x1, starting transfers between devices: 8.09 us -> 4.37 us  [body(): back = lax.ppermute(window, both, [(worker(*p), home(*p)) for p in places])]
    ppermute x2, starting transfers between devices: 10.7 us -> 7.17 us  [moved(): return lax.ppermute(tokens, both, [(home(*p), worker(*p)) for p in places])]
    ppermute x2, waiting for transfers between devices: 11.3 us -> 8.92 us  [moved(): return lax.ppermute(tokens, both, [(home(*p), worker(*p)) for p in places])]
    ppermute x4, starting transfers between devices: 1.34 us -> 3.18 us  [across(): lax.ppermute(pack, 'pair', [((i + s) % cores, i) for i in range(cores)])]
    ppermute x7, starting transfers between devices: 6.22 us -> 7.93 us  [tile_pieces(): lax.ppermute(own, 'tile', [((i + s) % tiles, i) for i in range(tiles)])]
    ppermute x4, waiting for transfers between devices: 0.01 us -> 1.35 us  [across(): lax.ppermute(pack, 'pair', [((i + s) % cores, i) for i in range(cores)])]
  transfers between devices with their start and end apart: 18 -> 18, of which waited for: 10 -> 10; matrix products, arithmetic and copies ran while one was open for 2% -> 3% of each run, Pallas kernels for 13% -> 17%
where the time goes in v3:
time: 84.2 us; the launch traced here: 83.9 us
  waiting for transfers between devices  36 us (43%)
  starting transfers between devices  29.1 us (35%)
  Pallas kernels  16.4 us (19%)
  local copies, waits for them, and re-layouts  2.24 us (3%)
    pallas_call x9, Pallas kernels, run_kernel(): pl.pallas_call(kernel, out_shape=[jax.ShapeDtypeStruct(*s) for s in shape...  16.4 us
    ppermute x7, waiting for transfers between devices, tile_pieces(): lax.ppermute(own, 'tile', [((i + s) % tiles, i) for i in range(tiles)])  13.3 us
    ppermute x2, waiting for transfers between devices, moved(): return lax.ppermute(tokens, both, [(home(*p), worker(*p)) for p in places])  8.92 us
    ppermute x7, starting transfers between devices, tile_pieces(): lax.ppermute(own, 'tile', [((i + s) % tiles, i) for i in range(tiles)])  7.93 us
    ppermute x2, waiting for transfers between devices, neighbours(): lax.ppermute(pack, 'blk', [(g + (i + s) % half, g + i) for g, i in ring])  7.21 us
    ppermute x2, starting transfers between devices, moved(): return lax.ppermute(tokens, both, [(home(*p), worker(*p)) for p in places])  7.17 us
    ppermute x1, waiting for transfers between devices, body(): lax.ppermute(window[:1], both, [(worker(b, p), home(b - 1, p)) for b, p i...  5.27 us
    ppermute x1, starting transfers between devices, body(): back = lax.ppermute(window, both, [(worker(*p), home(*p)) for p in places])  4.37 us
  transfers between devices with their start and end apart: 18, of which 10 were waited for; matrix products, arithmetic and copies ran while one was open for 3% of the time, Pallas kernels for 17%

profile of v3, /device:TPU:1, one launch (start us, length us, event | category | flops | bytes accessed | tf_op | source)
XLA Modules:
  0.0 83.9 jit_solution(10131953609896844005)
XLA Ops:
  0.0 2.0 %collective-permute-start.1 = (bf16[384,384]{1,0:T(8,128)(2,1)}, bf16[384,384]{1,0:T(8,128)(2,1)S(1)}, u32[]{:S(2)}, u32[]{:S(2)}) collective-permute-start(bf16[384,384]{1,0:T(8,128)(2,1)} %bitcast.10), channel_id=1, source_target_pairs={{2,0},{0,2},{3,1},{1,3},{6,4},{4,6},{7,5},{5,7},{10,8},{8,10},{11,... | collective-permute-start | bytes 884744 | tf_op jit(solution)/shard_map/ppermute | solution.py:197
  2.0 5.0 %collective-permute-start = (bf16[384,384]{1,0:T(8,128)(2,1)}, bf16[384,384]{1,0:T(8,128)(2,1)S(1)}, u32[]{:S(2)}, u32[]{:S(2)}) collective-permute-start(bf16[384,384]{1,0:T(8,128)(2,1)} %bitcast.12), channel_id=1, source_target_pairs={{0,0},{1,8},{4,4},{5,12},{8,1},{9,9},{12,5},{13,13},{2,2},{3,10},{... | collective-permute-start | bytes 884744 | tf_op jit(solution)/shard_map/ppermute | solution.py:219
  9.9 4.9 %collective-permute-done.refs_0_.refs_4_ = bf16[384,384]{1,0:T(8,128)(2,1)S(1)} collective-permute-done((bf16[384,384]{1,0:T(8,128)(2,1)}, bf16[384,384]{1,0:T(8,128)(2,1)S(1)}, u32[]{:S(2)}, u32[]{:S(2)}) %collective-permute-start) | collective-permute-done | bytes 294944 | tf_op jit(solution)/shard_map/ppermute | solution.py:219
  15.1 2.1 %collective-permute-start.5 = (bf16[384,512]{1,0:T(8,128)(2,1)S(1)}, bf16[384,512]{1,0:T(8,128)(2,1)S(1)}, u32[]{:S(2)}, u32[]{:S(2)}) collective-permute-start(bf16[384,512]{1,0:T(8,128)(2,1)S(1)} %project.2), channel_id=1, source_target_pairs={{0,0},{1,8},{4,4},{5,12},{8,1},{9,9},{12,5},{13,13},{2,2},{3,10},{... | collective-permute-start | bytes 1179656 | tf_op jit(solution)/shard_map/ppermute | solution.py:219
  17.2 3.2 %collective-permute-done.2.refs_1_.refs_5_ = bf16[384,384]{1,0:T(8,128)(2,1)S(1)} collective-permute-done((bf16[384,384]{1,0:T(8,128)(2,1)S(1)}, bf16[384,384]{1,0:T(8,128)(2,1)S(1)}, u32[]{:S(2)}, u32[]{:S(2)}) %collective-permute-start.2) | collective-permute-done | bytes 294944 | tf_op jit(solution)/shard_map/ppermute | solution.py:197
  21.6 1.5 %collective-permute-start.3 = (bf16[384,512]{1,0:T(8,128)(2,1)S(1)}, bf16[384,512]{1,0:T(8,128)(2,1)S(1)}, u32[]{:S(2)}, u32[]{:S(2)}) collective-permute-start(bf16[384,512]{1,0:T(8,128)(2,1)S(1)} %get-tuple-element.36.refs_0_), channel_id=1, source_target_pairs={{4,0},{0,4},{12,8},{8,12},{5,1},{1,5},{13,9},{9,13},{6,2},{2,6},{1... | collective-permute-start | bytes 1179656 | tf_op jit(solution)/shard_map/ppermute | solution.py:205
  25.4 4.0 %collective-permute-done.5.refs_0_ = bf16[384,512]{1,0:T(8,128)(2,1)S(1)} collective-permute-done((bf16[384,512]{1,0:T(8,128)(2,1)S(1)}, bf16[384,512]{1,0:T(8,128)(2,1)S(1)}, u32[]{:S(2)}, u32[]{:S(2)}) %collective-permute-start.5) | collective-permute-done | bytes 393248 | tf_op jit(solution)/shard_map/ppermute | solution.py:219
  29.4 2.3 %attend.4 = (f32[4,384,64]{2,1,0:T(8,128)S(1)}, f32[4,384,2]{2,1,0:T(8,128)S(1)}) custom-call(bf16[384,256]{1,0:T(8,128)(2,1)S(1)} %get-tuple-element.32.query, bf16[384,512]{1,0:T(8,128)(2,1)S(1)} %get-tuple-element.36.refs_0_, bf16[384,512]{1,0:T(8,128)(2,1)S(1)} %collective-permute-done.4.refs_1_), custom_call_target="tpu_custom_call" | custom-call | tf_op jit(solution)/shard_map/attend/pallas_call | solution.py:23
  31.7 3.1 %collective-permute-done.3.refs_0_ = bf16[384,512]{1,0:T(8,128)(2,1)S(1)} collective-permute-done((bf16[384,512]{1,0:T(8,128)(2,1)S(1)}, bf16[384,512]{1,0:T(8,128)(2,1)S(1)}, u32[]{:S(2)}, u32[]{:S(2)}) %collective-permute-start.3) | collective-permute-done | bytes 393248 | tf_op jit(solution)/shard_map/ppermute | solution.py:205
  36.1 1.3 %collective-permute-done.6.refs_1_ = bf16[384,512]{1,0:T(8,128)(2,1)S(1)} collective-permute-done((bf16[384,512]{1,0:T(8,128)(2,1)S(1)}, bf16[384,512]{1,0:T(8,128)(2,1)S(1)}, u32[]{:S(2)}, u32[]{:S(2)}) %collective-permute-start.6) | collective-permute-done | bytes 393248 | tf_op jit(solution)/shard_map/ppermute | solution.py:211
  37.5 3.1 %attend.5.refs_0_ = bf16[384,256]{1,0:T(8,128)(2,1)S(1)} custom-call(bf16[384,256]{1,0:T(8,128)(2,1)S(1)} %get-tuple-element.32.query, bf16[384,512]{1,0:T(8,128)(2,1)S(1)} %collective-permute-done.3.refs_0_, bf16[384,512]{1,0:T(8,128)(2,1)S(1)} %collective-permute-done.6.refs_1_, f32[4,384,64]{2,1,0:T(8,128)S(1)} %get-tuple-element.38.refs_2_, ...), custom_call_target="tpu_custom_call" | custom-call | tf_op jit(solution)/shard_map/attend/pallas_call | solution.py:23
  40.6 1.4 %collective-permute-start.8 = (bf16[384,256]{1,0:T(8,128)(2,1)S(1)}, bf16[384,256]{1,0:T(8,128)(2,1)S(1)}, u32[]{:S(2)}, u32[]{:S(2)}) collective-permute-start(bf16[384,256]{1,0:T(8,128)(2,1)S(1)} %attend.5.refs_0_), channel_id=1, source_target_pairs={{2,0},{0,2},{3,1},{1,3},{6,4},{4,6},{7,5},{5,7},{10,8},{8,10},{11,... | collective-permute-start | bytes 589832 | tf_op jit(solution)/shard_map/ppermute | solution.py:197
  42.7 4.1 %collective-permute-done.9.refs_0_ = bf16[384,512]{1,0:T(8,128)(2,1)S(1)} collective-permute-done((bf16[384,512]{1,0:T(8,128)(2,1)S(1)}, bf16[384,512]{1,0:T(8,128)(2,1)S(1)}, u32[]{:S(2)}, u32[]{:S(2)}) %collective-permute-start.9) | collective-permute-done | bytes 393248 | tf_op jit(solution)/shard_map/ppermute | solution.py:205
  48.0 1.4 %collective-permute-start.13 = (bf16[256,768]{1,0:T(8,128)(2,1)S(1)}, bf16[256,768]{1,0:T(8,128)(2,1)S(1)}, u32[]{:S(2)}, u32[]{:S(2)}) collective-permute-start(bf16[256,768]{1,0:T(8,128)(2,1)S(1)} %copy-done.3), channel_id=1, source_target_pairs={{2,0},{0,2},{3,1},{1,3},{6,4},{4,6},{7,5},{5,7},{10,8},{8,10},{11,... | collective-permute-start | bytes 1179656 | tf_op jit(solution)/shard_map/ppermute | solution.py:197
  49.5 1.5 %update.1 = (bf16[2,384,384]{2,1,0:T(8,128)(2,1)S(1)}, bf16[384,256]{1,0:T(8,128)(2,1)S(1)}) custom-call(s32[1]{0:T(128)} %bitcast.place, bf16[384,256]{1,0:T(8,128)(2,1)S(1)} %attend.5.refs_0_, bf16[384,256]{1,0:T(8,128)(2,1)S(1)} %collective-permute-done.8.refs_1_, bf16[256,768]{1,0:T(8,128)(2,1)S(1)} %copy-done.2, ...), custom_call_target="tpu_custom_call" | custom-call | tf_op jit(solution)/shard_map/update/pallas_call | solution.py:23
  51.0 2.3 %attend.6 = (f32[4,384,64]{2,1,0:T(8,128)S(1)}, f32[4,384,2]{2,1,0:T(8,128)S(1)}) custom-call(bf16[384,256]{1,0:T(8,128)(2,1)S(1)} %get-tuple-element.47.query, bf16[384,512]{1,0:T(8,128)(2,1)S(1)} %collective-permute-done.5.refs_0_, bf16[384,512]{1,0:T(8,128)(2,1)S(1)} %collective-permute-done.11.refs_1_), custom_call_target="tpu_custom_call" | custom-call | tf_op jit(solution)/shard_map/attend/pallas_call | solution.py:23
  53.3 3.1 %attend.7.refs_0_ = bf16[384,256]{1,0:T(8,128)(2,1)S(1)} custom-call(bf16[384,256]{1,0:T(8,128)(2,1)S(1)} %get-tuple-element.47.query, bf16[384,512]{1,0:T(8,128)(2,1)S(1)} %collective-permute-done.9.refs_0_, bf16[384,512]{1,0:T(8,128)(2,1)S(1)} %collective-permute-done.10.refs_1_, f32[4,384,64]{2,1,0:T(8,128)S(1)} %get-tuple-element.50.refs_2_, ...), custom_call_target="tpu_custom_call" | custom-call | tf_op jit(solution)/shard_map/attend/pallas_call | solution.py:23
  56.4 1.4 %collective-permute-start.12 = (bf16[384,256]{1,0:T(8,128)(2,1)S(1)}, bf16[384,256]{1,0:T(8,128)(2,1)S(1)}, u32[]{:S(2)}, u32[]{:S(2)}) collective-permute-start(bf16[384,256]{1,0:T(8,128)(2,1)S(1)} %attend.7.refs_0_), channel_id=1, source_target_pairs={{2,0},{0,2},{3,1},{1,3},{6,4},{4,6},{7,5},{5,7},{10,8},{8,10},{11,... | collective-permute-start | bytes 589832 | tf_op jit(solution)/shard_map/ppermute | solution.py:197
  57.8 5.1 %collective-permute-done.14.refs_6_ = bf16[384,256]{1,0:T(8,128)(2,1)S(1)} collective-permute-done((bf16[384,256]{1,0:T(8,128)(2,1)S(1)}, bf16[384,256]{1,0:T(8,128)(2,1)S(1)}, u32[]{:S(2)}, u32[]{:S(2)}) %collective-permute-start.14) | collective-permute-done | bytes 196640 | tf_op jit(solution)/shard_map/ppermute | solution.py:197
  63.0 4.2 %collective-permute-done.12.refs_1_ = bf16[384,256]{1,0:T(8,128)(2,1)S(1)} collective-permute-done((bf16[384,256]{1,0:T(8,128)(2,1)S(1)}, bf16[384,256]{1,0:T(8,128)(2,1)S(1)}, u32[]{:S(2)}, u32[]{:S(2)}) %collective-permute-start.12) | collective-permute-done | bytes 196640 | tf_op jit(solution)/shard_map/ppermute | solution.py:197
  68.3 4.4 %collective-permute-start.15 = (bf16[3,96,256]{2,1,0:T(8,128)(2,1)S(1)}, bf16[3,96,256]{2,1,0:T(8,128)(2,1)S(1)}, u32[]{:S(2)}, u32[]{:S(2)}) collective-permute-start(bf16[3,96,256]{2,1,0:T(8,128)(2,1)S(1)} %finish.1), channel_id=1, source_target_pairs={{0,0},{8,1},{4,4},{12,5},{1,8},{9,9},{5,12},{13,13},{2,2},{10,3},{... | collective-permute-start | bytes 442376 | tf_op jit(solution)/shard_map/ppermute | solution.py:295
  72.7 3.0 %collective-permute-start.16 = (bf16[1,96,256]{2,1,0:T(8,128)(2,1)S(1)}, bf16[1,96,256]{2,1,0:T(8,128)(2,1)S(1)}, u32[]{:S(2)}, u32[]{:S(2)}) collective-permute-start(bf16[1,96,256]{2,1,0:T(8,128)(2,1)S(1)} %get-tuple-element.58), channel_id=1, source_target_pairs={{0,4},{8,5},{4,8},{12,9},{1,12},{9,13},{2,6},{10,7},{6,10},{14,11}... | collective-permute-start | bytes 147464 | tf_op jit(solution)/shard_map/ppermute | solution.py:296
  75.7 1.9 %collective-permute-start.17 = (bf16[1,96,256]{2,1,0:T(8,128)(2,1)S(1)}, bf16[1,96,256]{2,1,0:T(8,128)(2,1)S(1)}, u32[]{:S(2)}, u32[]{:S(2)}) collective-permute-start(bf16[1,96,256]{2,1,0:T(8,128)(2,1)S(1)} %get-tuple-element.57), channel_id=1, source_target_pairs={{4,0},{12,1},{1,4},{9,5},{5,8},{13,9},{6,2},{14,3},{3,6},{11,7},{7... | collective-permute-start | bytes 147464 | tf_op jit(solution)/shard_map/ppermute | solution.py:299
  77.6 5.3 %collective-permute-done.17.below = bf16[1,96,256]{2,1,0:T(8,128)(2,1)S(1)} collective-permute-done((bf16[1,96,256]{2,1,0:T(8,128)(2,1)S(1)}, bf16[1,96,256]{2,1,0:T(8,128)(2,1)S(1)}, u32[]{:S(2)}, u32[]{:S(2)}) %collective-permute-start.17) | collective-permute-done | bytes 49184 | tf_op jit(solution)/shard_map/ppermute | solution.py:299
  (36 shorter events, 11.9 us)
Async XLA Ops:
  0.0 9.1 %copy-start.4 = (bf16[1,384,384]{2,1,0:T(8,128)(2,1)S(1)}, bf16[1,384,384]{2,1,0:T(8,128)(2,1)}, u32[]{:S(2)}) copy-start(bf16[1,384,384]{2,1,0:T(8,128)(2,1)} %param.9) | copy-start | bytes 884740
  0.0 9.1 %collective-permute-start.1 = (bf16[384,384]{1,0:T(8,128)(2,1)}, bf16[384,384]{1,0:T(8,128)(2,1)S(1)}, u32[]{:S(2)}, u32[]{:S(2)}) collective-permute-start(bf16[384,384]{1,0:T(8,128)(2,1)} %bitcast.10), channel_id=1, source_target_pairs={{2,0},{0,2},{3,1},{1,3},{6,4},{4,6},{7,5},{5,7},{10,8},{8,10},{11,... | collective-permute-start | bytes 884744 | tf_op jit(solution)/shard_map/ppermute | solution.py:197
  2.0 12.8 %collective-permute-start = (bf16[384,384]{1,0:T(8,128)(2,1)}, bf16[384,384]{1,0:T(8,128)(2,1)S(1)}, u32[]{:S(2)}, u32[]{:S(2)}) collective-permute-start(bf16[384,384]{1,0:T(8,128)(2,1)} %bitcast.12), channel_id=1, source_target_pairs={{0,0},{1,8},{4,4},{5,12},{8,1},{9,9},{12,5},{13,13},{2,2},{3,10},{... | collective-permute-start | bytes 884744 | tf_op jit(solution)/shard_map/ppermute | solution.py:219
  8.3 12.1 %copy-start = (bf16[3,768,256]{2,1,0:T(8,128)(2,1)S(1)}, bf16[3,768,256]{2,1,0:T(8,128)(2,1)}, u32[]{:S(2)}) copy-start(bf16[3,768,256]{2,1,0:T(8,128)(2,1)} %param.10) | copy-start | bytes 3538948
  14.9 5.6 %collective-permute-start.2 = (bf16[384,384]{1,0:T(8,128)(2,1)S(1)}, bf16[384,384]{1,0:T(8,128)(2,1)S(1)}, u32[]{:S(2)}, u32[]{:S(2)}) collective-permute-start(bf16[384,384]{1,0:T(8,128)(2,1)S(1)} %collective-permute-done.refs_0_.refs_4_), channel_id=1, source_target_pairs={{2,0},{0,2},{3,1},{1,3},{6,4},{4,6},{7,5},{5,7},{10,8},{8,10},{11,... | collective-permute-start | bytes 884744 | tf_op jit(solution)/shard_map/ppermute | solution.py:197
  15.1 14.3 %collective-permute-start.5 = (bf16[384,512]{1,0:T(8,128)(2,1)S(1)}, bf16[384,512]{1,0:T(8,128)(2,1)S(1)}, u32[]{:S(2)}, u32[]{:S(2)}) collective-permute-start(bf16[384,512]{1,0:T(8,128)(2,1)S(1)} %project.2), channel_id=1, source_target_pairs={{0,0},{1,8},{4,4},{5,12},{8,1},{9,9},{12,5},{13,13},{2,2},{3,10},{... | collective-permute-start | bytes 1179656 | tf_op jit(solution)/shard_map/ppermute | solution.py:219
  20.4 3.7 %copy-start.2 = (bf16[256,768]{1,0:T(8,128)(2,1)S(1)}, bf16[256,768]{1,0:T(8,128)(2,1)}, u32[]{:S(2)}) copy-start(bf16[256,768]{1,0:T(8,128)(2,1)} %refs_2_) | copy-start | bytes 1179652
  21.5 7.9 %collective-permute-start.4 = (bf16[384,512]{1,0:T(8,128)(2,1)S(1)}, bf16[384,512]{1,0:T(8,128)(2,1)S(1)}, u32[]{:S(2)}, u32[]{:S(2)}) collective-permute-start(bf16[384,512]{1,0:T(8,128)(2,1)S(1)} %get-tuple-element.36.refs_0_), channel_id=1, source_target_pairs={{1,0},{0,1},{3,2},{2,3},{5,4},{4,5},{7,6},{6,7},{9,8},{8,9},{11,10... | collective-permute-start | bytes 1179656 | tf_op jit(solution)/shard_map/ppermute | solution.py:211
  21.6 13.3 %collective-permute-start.3 = (bf16[384,512]{1,0:T(8,128)(2,1)S(1)}, bf16[384,512]{1,0:T(8,128)(2,1)S(1)}, u32[]{:S(2)}, u32[]{:S(2)}) collective-permute-start(bf16[384,512]{1,0:T(8,128)(2,1)S(1)} %get-tuple-element.36.refs_0_), channel_id=1, source_target_pairs={{4,0},{0,4},{12,8},{8,12},{5,1},{1,5},{13,9},{9,13},{6,2},{2,6},{1... | collective-permute-start | bytes 1179656 | tf_op jit(solution)/shard_map/ppermute | solution.py:205
  24.2 12.0 %collective-permute-start.7 = (bf16[256,768]{1,0:T(8,128)(2,1)S(1)}, bf16[256,768]{1,0:T(8,128)(2,1)S(1)}, u32[]{:S(2)}, u32[]{:S(2)}) collective-permute-start(bf16[256,768]{1,0:T(8,128)(2,1)S(1)} %copy-done.2), channel_id=1, source_target_pairs={{2,0},{0,2},{3,1},{1,3},{6,4},{4,6},{7,5},{5,7},{10,8},{8,10},{11,... | collective-permute-start | bytes 1179656 | tf_op jit(solution)/shard_map/ppermute | solution.py:197
  34.9 13.1 %copy-start.3 = (bf16[256,768]{1,0:T(8,128)(2,1)S(1)}, bf16[256,768]{1,0:T(8,128)(2,1)}, u32[]{:S(2)}) copy-start(bf16[256,768]{1,0:T(8,128)(2,1)} %refs_2_.1) | copy-start | bytes 1179652
  34.9 14.5 %copy-start.5 = (bf16[384,256]{1,0:T(8,128)(2,1)S(1)}, bf16[384,256]{1,0:T(8,128)(2,1)}, u32[]{:S(2)}) copy-start(bf16[384,256]{1,0:T(8,128)(2,1)} %refs_5_) | copy-start | bytes 589828
  34.9 2.6 %collective-permute-start.6 = (bf16[384,512]{1,0:T(8,128)(2,1)S(1)}, bf16[384,512]{1,0:T(8,128)(2,1)S(1)}, u32[]{:S(2)}, u32[]{:S(2)}) collective-permute-start(bf16[384,512]{1,0:T(8,128)(2,1)S(1)} %collective-permute-done.3.refs_0_), channel_id=1, source_target_pairs={{1,0},{0,1},{3,2},{2,3},{5,4},{4,5},{7,6},{6,7},{9,8},{8,9},{11,10... | collective-permute-start | bytes 1179656 | tf_op jit(solution)/shard_map/ppermute | solution.py:211
  36.1 10.7 %collective-permute-start.9 = (bf16[384,512]{1,0:T(8,128)(2,1)S(1)}, bf16[384,512]{1,0:T(8,128)(2,1)S(1)}, u32[]{:S(2)}, u32[]{:S(2)}) collective-permute-start(bf16[384,512]{1,0:T(8,128)(2,1)S(1)} %collective-permute-done.5.refs_0_), channel_id=1, source_target_pairs={{4,0},{0,4},{12,8},{8,12},{5,1},{1,5},{13,9},{9,13},{6,2},{2,6},{1... | collective-permute-start | bytes 1179656 | tf_op jit(solution)/shard_map/ppermute | solution.py:205
  40.6 6.2 %collective-permute-start.8 = (bf16[384,256]{1,0:T(8,128)(2,1)S(1)}, bf16[384,256]{1,0:T(8,128)(2,1)S(1)}, u32[]{:S(2)}, u32[]{:S(2)}) collective-permute-start(bf16[384,256]{1,0:T(8,128)(2,1)S(1)} %attend.5.refs_0_), channel_id=1, source_target_pairs={{2,0},{0,2},{3,1},{1,3},{6,4},{4,6},{7,5},{5,7},{10,8},{8,10},{11,... | collective-permute-start | bytes 589832 | tf_op jit(solution)/shard_map/ppermute | solution.py:197
  42.1 8.9 %collective-permute-start.11 = (bf16[384,512]{1,0:T(8,128)(2,1)S(1)}, bf16[384,512]{1,0:T(8,128)(2,1)S(1)}, u32[]{:S(2)}, u32[]{:S(2)}) collective-permute-start(bf16[384,512]{1,0:T(8,128)(2,1)S(1)} %collective-permute-done.5.refs_0_), channel_id=1, source_target_pairs={{1,0},{0,1},{3,2},{2,3},{5,4},{4,5},{7,6},{6,7},{9,8},{8,9},{11,10... | collective-permute-start | bytes 1179656 | tf_op jit(solution)/shard_map/ppermute | solution.py:211
  46.8 6.5 %collective-permute-start.10 = (bf16[384,512]{1,0:T(8,128)(2,1)S(1)}, bf16[384,512]{1,0:T(8,128)(2,1)S(1)}, u32[]{:S(2)}, u32[]{:S(2)}) collective-permute-start(bf16[384,512]{1,0:T(8,128)(2,1)S(1)} %collective-permute-done.9.refs_0_), channel_id=1, source_target_pairs={{1,0},{0,1},{3,2},{2,3},{5,4},{4,5},{7,6},{6,7},{9,8},{8,9},{11,10... | collective-permute-start | bytes 1179656 | tf_op jit(solution)/shard_map/ppermute | solution.py:211
  48.0 15.0 %collective-permute-start.13 = (bf16[256,768]{1,0:T(8,128)(2,1)S(1)}, bf16[256,768]{1,0:T(8,128)(2,1)S(1)}, u32[]{:S(2)}, u32[]{:S(2)}) collective-permute-start(bf16[256,768]{1,0:T(8,128)(2,1)S(1)} %copy-done.3), channel_id=1, source_target_pairs={{2,0},{0,2},{3,1},{1,3},{6,4},{4,6},{7,5},{5,7},{10,8},{8,10},{11,... | collective-permute-start | bytes 1179656 | tf_op jit(solution)/shard_map/ppermute | solution.py:197
  49.4 13.6 %collective-permute-start.14 = (bf16[384,256]{1,0:T(8,128)(2,1)S(1)}, bf16[384,256]{1,0:T(8,128)(2,1)S(1)}, u32[]{:S(2)}, u32[]{:S(2)}) collective-permute-start(bf16[384,256]{1,0:T(8,128)(2,1)S(1)} %copy-done.5), channel_id=1, source_target_pairs={{2,0},{0,2},{3,1},{1,3},{6,4},{4,6},{7,5},{5,7},{10,8},{8,10},{11,... | collective-permute-start | bytes 589832 | tf_op jit(solution)/shard_map/ppermute | solution.py:197
  56.4 10.8 %collective-permute-start.12 = (bf16[384,256]{1,0:T(8,128)(2,1)S(1)}, bf16[384,256]{1,0:T(8,128)(2,1)S(1)}, u32[]{:S(2)}, u32[]{:S(2)}) collective-permute-start(bf16[384,256]{1,0:T(8,128)(2,1)S(1)} %attend.7.refs_0_), channel_id=1, source_target_pairs={{2,0},{0,2},{3,1},{1,3},{6,4},{4,6},{7,5},{5,7},{10,8},{8,10},{11,... | collective-permute-start | bytes 589832 | tf_op jit(solution)/shard_map/ppermute | solution.py:197
  67.2 15.7 %copy-start.1 = (bf16[3,3,256,256]{3,2,1,0:T(8,128)(2,1)S(1)}, bf16[3,3,256,256]{3,2,1,0:T(8,128)(2,1)}, u32[]{:S(2)}) copy-start(bf16[3,3,256,256]{3,2,1,0:T(8,128)(2,1)} %weight.1) | copy-start | bytes 3538948
  68.3 14.6 %collective-permute-start.15 = (bf16[3,96,256]{2,1,0:T(8,128)(2,1)S(1)}, bf16[3,96,256]{2,1,0:T(8,128)(2,1)S(1)}, u32[]{:S(2)}, u32[]{:S(2)}) collective-permute-start(bf16[3,96,256]{2,1,0:T(8,128)(2,1)S(1)} %finish.1), channel_id=1, source_target_pairs={{0,0},{8,1},{4,4},{12,5},{1,8},{9,9},{5,12},{13,13},{2,2},{10,3},{... | collective-permute-start | bytes 442376 | tf_op jit(solution)/shard_map/ppermute | solution.py:295
  72.7 4.9 %collective-permute-start.16 = (bf16[1,96,256]{2,1,0:T(8,128)(2,1)S(1)}, bf16[1,96,256]{2,1,0:T(8,128)(2,1)S(1)}, u32[]{:S(2)}, u32[]{:S(2)}) collective-permute-start(bf16[1,96,256]{2,1,0:T(8,128)(2,1)S(1)} %get-tuple-element.58), channel_id=1, source_target_pairs={{0,4},{8,5},{4,8},{12,9},{1,12},{9,13},{2,6},{10,7},{6,10},{14,11}... | collective-permute-start | bytes 147464 | tf_op jit(solution)/shard_map/ppermute | solution.py:296
  75.7 7.2 %collective-permute-start.17 = (bf16[1,96,256]{2,1,0:T(8,128)(2,1)S(1)}, bf16[1,96,256]{2,1,0:T(8,128)(2,1)S(1)}, u32[]{:S(2)}, u32[]{:S(2)}) collective-permute-start(bf16[1,96,256]{2,1,0:T(8,128)(2,1)S(1)} %get-tuple-element.57), channel_id=1, source_target_pairs={{4,0},{12,1},{1,4},{9,5},{5,8},{13,9},{6,2},{14,3},{3,6},{11,7},{7... | collective-permute-start | bytes 147464 | tf_op jit(solution)/shard_map/ppermute | solution.py:299

commit v4 on v3

--- a/solution.py
+++ b/solution.py
@@ -212,8 +212,8 @@
             for s in range(1, cores)
         ]
 
-    def joined_packs(packs):
-        return [packs[0] if len(packs) == 1 else jnp.concatenate(packs)]
+    def grouped(packs):
+        return packs if len(packs) < 3 else [jnp.concatenate(packs)]
 
     def moved(tokens):
         return lax.ppermute(tokens, both, [(home(*p), worker(*p)) for p in places])
@@ -245,30 +245,27 @@
         )
 
     left_here = moved(left_tokens[0])
+    left = tile_pieces(left_here)
     right = tile_pieces(right_tokens[0])
     (right_pack,) = project(right, cross_qkv[1:], False)
-    left_here, right_pack = lax.optimization_barrier((left_here, right_pack))
     right_pack = moved(right_pack)
-    left = tile_pieces(left_here)
     query, pack = project(left, self_qkv, True)
-    near = [pack, *across(pack)]
-    beside = neighbours(pack)
     query_weight = cross_qkv[0].reshape(tiles, share, columns)
-    near, right_pack, query_weight = lax.optimization_barrier((near, right_pack, query_weight))
+    near, right_pack, query_weight = lax.optimization_barrier(
+        ([pack, *neighbours(pack)], right_pack, query_weight)
+    )
+    far = [q for p in near for q in across(p)]
     self_out_pieces = tile_pieces(tied(self_out, left))
-    state = attend(query, near)
-    beside, right_pack = tied((beside, right_pack), state)
-    far = [*beside, *[p for b in beside for p in across(b)]]
-    right_near = [right_pack, *across(right_pack)]
-    right_beside = neighbours(right_pack)
-    far, self_out_pieces = lax.optimization_barrier((far, self_out_pieces))
-    (own_mixed,) = attend(query, far if len(far) < 3 else joined_packs(far), state, True)
+    reassemble_pieces = tile_pieces(tied(reassemble, left))
+    state = attend(query, grouped(near))
+    right_pack = tied(right_pack, state)
+    right_near = [right_pack, *neighbours(right_pack)]
+    far, self_out_pieces, reassemble_pieces = lax.optimization_barrier(
+        (far, self_out_pieces, reassemble_pieces)
+    )
+    (own_mixed,) = attend(query, grouped(far), state, True)
 
     mixed = tile_pieces(own_mixed)
-    reassemble_pieces = tile_pieces(tied(reassemble, mixed))
-    cross_out_pieces = tile_pieces(tied(cross_out, mixed))
-    right_beside = tied(right_beside, mixed)
-    right_far = [*right_beside, *[p for b in right_beside for p in across(b)]]
     updated, cross_query = run_kernel(
         functools.partial(update_kernel, count=tiles),
         "update",
@@ -277,11 +274,12 @@
         0,
         place,
     )
-    state = attend(cross_query, right_near)
+    cross_out_pieces = tile_pieces(tied(cross_out, updated))
+    right_near = tied(right_near, updated)
+    right_far = [q for p in right_near for q in across(p)]
+    state = attend(cross_query, grouped(right_near))
     right_far = tied(right_far, state)
-    (mixed,) = attend(
-        cross_query, right_far if len(right_far) < 3 else joined_packs(right_far), state, True
-    )
+    (mixed,) = attend(cross_query, grouped(right_far), state, True)
     mixed = tile_pieces(mixed)
     (window,) = run_kernel(
         functools.partial(finish_kernel, count=tiles, width=width),

time: 84.2 us -> 83.5 us (level)
  waiting for transfers between devices: 36 us -> 34.1 us
  starting transfers between devices: 29.1 us -> 30.3 us
    ppermute x2, waiting for transfers between devices: 7.21 us -> 2.15 us  [neighbours(): lax.ppermute(pack, 'blk', [(g + (i + s) % half, g + i) for g, i in ring])]
    ppermute x2, waiting for transfers between devices: 8.92 us -> 12.3 us  [moved(): return lax.ppermute(tokens, both, [(home(*p), worker(*p)) for p in places])]
    ppermute x2, starting transfers between devices: 1.53 us -> 4.37 us  [neighbours(): lax.ppermute(pack, 'blk', [(g + (i + s) % half, g + i) for g, i in ring])]
    ppermute x4, waiting for transfers between devices: 1.35 us -> 0.01 us  [across(): lax.ppermute(pack, 'pair', [((i + s) % cores, i) for i in range(cores)])]
    ppermute x7, waiting for transfers between devices: 13.3 us -> 14.6 us  [tile_pieces(): lax.ppermute(own, 'tile', [((i + s) % tiles, i) for i in range(tiles)])]
    ppermute x7, starting transfers between devices: 7.93 us -> 6.84 us  [tile_pieces(): lax.ppermute(own, 'tile', [((i + s) % tiles, i) for i in range(tiles)])]
    ppermute x1, starting transfers between devices: 4.37 us -> 3.38 us  [body(): back = lax.ppermute(window, both, [(worker(*p), home(*p)) for p in places])]
    ppermute x4, starting transfers between devices: 3.18 us -> 2.33 us  [across(): lax.ppermute(pack, 'pair', [((i + s) % cores, i) for i in range(cores)])]
  transfers between devices with their start and end apart: 18 -> 18, of which waited for: 10 -> 9; matrix products, arithmetic and copies ran while one was open for 3% -> 3% of each run, Pallas kernels for 17% -> 17%
where the time goes in v4:
time: 83.5 us; the launch traced here: 83.2 us
  waiting for transfers between devices  34.1 us (41%)
  starting transfers between devices  30.3 us (36%)
  Pallas kernels  16.3 us (20%)
  local copies, waits for them, and re-layouts  2.24 us (3%)
    pallas_call x9, Pallas kernels, run_kernel(): pl.pallas_call(kernel, out_shape=[jax.ShapeDtypeStruct(*s) for s in shape...  16.3 us
    ppermute x7, waiting for transfers between devices, tile_pieces(): lax.ppermute(own, 'tile', [((i + s) % tiles, i) for i in range(tiles)])  14.6 us
    ppermute x2, waiting for transfers between devices, moved(): return lax.ppermute(tokens, both, [(home(*p), worker(*p)) for p in places])  12.3 us
    ppermute x2, starting transfers between devices, moved(): return lax.ppermute(tokens, both, [(home(*p), worker(*p)) for p in places])  7.86 us
    ppermute x7, starting transfers between devices, tile_pieces(): lax.ppermute(own, 'tile', [((i + s) % tiles, i) for i in range(tiles)])  6.84 us
    ppermute x1, waiting for transfers between devices, body(): lax.ppermute(window[:1], both, [(worker(b, p), home(b - 1, p)) for b, p i...  5.09 us
    ppermute x2, starting transfers between devices, neighbours(): lax.ppermute(pack, 'blk', [(g + (i + s) % half, g + i) for g, i in ring])  4.37 us
    ppermute x1, starting transfers between devices, body(): lax.ppermute(window[-1:], both, [(worker(b, p), home(b + 1, p)) for b, p...  3.45 us
  transfers between devices with their start and end apart: 18, of which 9 were waited for; matrix products, arithmetic and copies ran while one was open for 3% of the time, Pallas kernels for 17%

profile of v4, /device:TPU:1, one launch (start us, length us, event | category | flops | bytes accessed | tf_op | source)
XLA Modules:
  0.0 83.2 jit_solution(15175509859612697190)
XLA Ops:
  0.0 5.7 %collective-permute-start = (bf16[384,384]{1,0:T(8,128)(2,1)}, bf16[384,384]{1,0:T(8,128)(2,1)S(1)}, u32[]{:S(2)}, u32[]{:S(2)}) collective-permute-start(bf16[384,384]{1,0:T(8,128)(2,1)} %bitcast.12), channel_id=1, source_target_pairs={{0,0},{1,8},{4,4},{5,12},{8,1},{9,9},{12,5},{13,13},{2,2},{3,10},{... | collective-permute-start | bytes 884744 | tf_op jit(solution)/shard_map/ppermute | solution.py:219
  5.7 1.3 %collective-permute-start.3 = (bf16[384,384]{1,0:T(8,128)(2,1)}, bf16[384,384]{1,0:T(8,128)(2,1)S(1)}, u32[]{:S(2)}, u32[]{:S(2)}) collective-permute-start(bf16[384,384]{1,0:T(8,128)(2,1)} %bitcast.10), channel_id=1, source_target_pairs={{2,0},{0,2},{3,1},{1,3},{6,4},{4,6},{7,5},{5,7},{10,8},{8,10},{11,... | collective-permute-start | bytes 884744 | tf_op jit(solution)/shard_map/ppermute | solution.py:197
  7.0 6.5 %collective-permute-done.refs_0_.refs_4_ = bf16[384,384]{1,0:T(8,128)(2,1)S(1)} collective-permute-done((bf16[384,384]{1,0:T(8,128)(2,1)}, bf16[384,384]{1,0:T(8,128)(2,1)S(1)}, u32[]{:S(2)}, u32[]{:S(2)}) %collective-permute-start) | collective-permute-done | bytes 294944 | tf_op jit(solution)/shard_map/ppermute | solution.py:219
  13.5 1.2 %collective-permute-start.1 = (bf16[384,384]{1,0:T(8,128)(2,1)S(1)}, bf16[384,384]{1,0:T(8,128)(2,1)S(1)}, u32[]{:S(2)}, u32[]{:S(2)}) collective-permute-start(bf16[384,384]{1,0:T(8,128)(2,1)S(1)} %collective-permute-done.refs_0_.refs_4_), channel_id=1, source_target_pairs={{2,0},{0,2},{3,1},{1,3},{6,4},{4,6},{7,5},{5,7},{10,8},{8,10},{11,... | collective-permute-start | bytes 884744 | tf_op jit(solution)/shard_map/ppermute | solution.py:197
  16.8 2.1 %collective-permute-start.4 = (bf16[384,512]{1,0:T(8,128)(2,1)S(1)}, bf16[384,512]{1,0:T(8,128)(2,1)S(1)}, u32[]{:S(2)}, u32[]{:S(2)}) collective-permute-start(bf16[384,512]{1,0:T(8,128)(2,1)S(1)} %project.3), channel_id=1, source_target_pairs={{0,0},{1,8},{4,4},{5,12},{8,1},{9,9},{12,5},{13,13},{2,2},{3,10},{... | collective-permute-start | bytes 1179656 | tf_op jit(solution)/shard_map/ppermute | solution.py:219
  20.2 3.8 %collective-permute-start.2 = (bf16[384,512]{1,0:T(8,128)(2,1)S(1)}, bf16[384,512]{1,0:T(8,128)(2,1)S(1)}, u32[]{:S(2)}, u32[]{:S(2)}) collective-permute-start(bf16[384,512]{1,0:T(8,128)(2,1)S(1)} %get-tuple-element.33.refs_0_), channel_id=1, source_target_pairs={{4,0},{0,4},{12,8},{8,12},{5,1},{1,5},{13,9},{9,13},{6,2},{2,6},{1... | collective-permute-start | bytes 1179656 | tf_op jit(solution)/shard_map/ppermute | solution.py:205
  25.4 5.8 %collective-permute-done.4.refs_0_ = bf16[384,512]{1,0:T(8,128)(2,1)S(1)} collective-permute-done((bf16[384,512]{1,0:T(8,128)(2,1)S(1)}, bf16[384,512]{1,0:T(8,128)(2,1)S(1)}, u32[]{:S(2)}, u32[]{:S(2)}) %collective-permute-start.4) | collective-permute-done | bytes 393248 | tf_op jit(solution)/shard_map/ppermute | solution.py:219
  31.2 2.1 %collective-permute-done.2.refs_1_ = bf16[384,512]{1,0:T(8,128)(2,1)S(1)} collective-permute-done((bf16[384,512]{1,0:T(8,128)(2,1)S(1)}, bf16[384,512]{1,0:T(8,128)(2,1)S(1)}, u32[]{:S(2)}, u32[]{:S(2)}) %collective-permute-start.2) | collective-permute-done | bytes 393248 | tf_op jit(solution)/shard_map/ppermute | solution.py:205
  35.0 2.3 %attend.4 = (f32[4,384,64]{2,1,0:T(8,128)S(1)}, f32[4,384,2]{2,1,0:T(8,128)S(1)}) custom-call(bf16[384,256]{1,0:T(8,128)(2,1)S(1)} %get-tuple-element.31.query, bf16[384,512]{1,0:T(8,128)(2,1)S(1)} %get-tuple-element.33.refs_0_, bf16[384,512]{1,0:T(8,128)(2,1)S(1)} %collective-permute-done.2.refs_1_), custom_call_target="tpu_custom_call" | custom-call | tf_op jit(solution)/shard_map/attend/pallas_call | solution.py:23
  37.9 2.5 %collective-permute-done.8.refs_6_ = bf16[384,256]{1,0:T(8,128)(2,1)S(1)} collective-permute-done((bf16[384,256]{1,0:T(8,128)(2,1)S(1)}, bf16[384,256]{1,0:T(8,128)(2,1)S(1)}, u32[]{:S(2)}, u32[]{:S(2)}) %collective-permute-start.8) | collective-permute-done | bytes 196640 | tf_op jit(solution)/shard_map/ppermute | solution.py:197
  40.4 3.1 %attend.5.refs_0_ = bf16[384,256]{1,0:T(8,128)(2,1)S(1)} custom-call(bf16[384,256]{1,0:T(8,128)(2,1)S(1)} %get-tuple-element.31.query, bf16[384,512]{1,0:T(8,128)(2,1)S(1)} %collective-permute-done.5.refs_0_, bf16[384,512]{1,0:T(8,128)(2,1)S(1)} %collective-permute-done.6.refs_1_, f32[4,384,64]{2,1,0:T(8,128)S(1)} %get-tuple-element.39.refs_2_, ...), custom_call_target="tpu_custom_call" | custom-call | tf_op jit(solution)/shard_map/attend/pallas_call | solution.py:23
  43.5 1.3 %collective-permute-start.9 = (bf16[384,256]{1,0:T(8,128)(2,1)S(1)}, bf16[384,256]{1,0:T(8,128)(2,1)S(1)}, u32[]{:S(2)}, u32[]{:S(2)}) collective-permute-start(bf16[384,256]{1,0:T(8,128)(2,1)S(1)} %attend.5.refs_0_), channel_id=1, source_target_pairs={{2,0},{0,2},{3,1},{1,3},{6,4},{4,6},{7,5},{5,7},{10,8},{8,10},{11,... | collective-permute-start | bytes 589832 | tf_op jit(solution)/shard_map/ppermute | solution.py:197
  44.8 4.4 %collective-permute-done.9.refs_1_ = bf16[384,256]{1,0:T(8,128)(2,1)S(1)} collective-permute-done((bf16[384,256]{1,0:T(8,128)(2,1)S(1)}, bf16[384,256]{1,0:T(8,128)(2,1)S(1)}, u32[]{:S(2)}, u32[]{:S(2)}) %collective-permute-start.9) | collective-permute-done | bytes 196640 | tf_op jit(solution)/shard_map/ppermute | solution.py:197
  49.2 1.5 %update.1 = (bf16[2,384,384]{2,1,0:T(8,128)(2,1)S(1)}, bf16[384,256]{1,0:T(8,128)(2,1)S(1)}) custom-call(s32[1]{0:T(128)} %bitcast.place, bf16[384,256]{1,0:T(8,128)(2,1)S(1)} %attend.5.refs_0_, bf16[384,256]{1,0:T(8,128)(2,1)S(1)} %collective-permute-done.9.refs_1_, bf16[256,768]{1,0:T(8,128)(2,1)S(1)} %copy-done.2, ...), custom_call_target="tpu_custom_call" | custom-call | tf_op jit(solution)/shard_map/update/pallas_call | solution.py:23
  50.7 1.7 %collective-permute-start.11 = (bf16[384,512]{1,0:T(8,128)(2,1)S(1)}, bf16[384,512]{1,0:T(8,128)(2,1)S(1)}, u32[]{:S(2)}, u32[]{:S(2)}) collective-permute-start(bf16[384,512]{1,0:T(8,128)(2,1)S(1)} %collective-permute-done.4.refs_0_), channel_id=1, source_target_pairs={{1,0},{0,1},{3,2},{2,3},{5,4},{4,5},{7,6},{6,7},{9,8},{8,9},{11,10... | collective-permute-start | bytes 1179656 | tf_op jit(solution)/shard_map/ppermute | solution.py:211
  52.5 1.2 %collective-permute-start.14 = (bf16[256,768]{1,0:T(8,128)(2,1)S(1)}, bf16[256,768]{1,0:T(8,128)(2,1)S(1)}, u32[]{:S(2)}, u32[]{:S(2)}) collective-permute-start(bf16[256,768]{1,0:T(8,128)(2,1)S(1)} %copy-done.3), channel_id=1, source_target_pairs={{2,0},{0,2},{3,1},{1,3},{6,4},{4,6},{7,5},{5,7},{10,8},{8,10},{11,... | collective-permute-start | bytes 1179656 | tf_op jit(solution)/shard_map/ppermute | solution.py:197
  53.7 2.3 %attend.6 = (f32[4,384,64]{2,1,0:T(8,128)S(1)}, f32[4,384,2]{2,1,0:T(8,128)S(1)}) custom-call(bf16[384,256]{1,0:T(8,128)(2,1)S(1)} %get-tuple-element.44.query, bf16[384,512]{1,0:T(8,128)(2,1)S(1)} %collective-permute-done.4.refs_0_, bf16[384,512]{1,0:T(8,128)(2,1)S(1)} %collective-permute-done.10.refs_1_), custom_call_target="tpu_custom_call" | custom-call | tf_op jit(solution)/shard_map/attend/pallas_call | solution.py:23
  56.0 3.1 %attend.7.refs_0_ = bf16[384,256]{1,0:T(8,128)(2,1)S(1)} custom-call(bf16[384,256]{1,0:T(8,128)(2,1)S(1)} %get-tuple-element.44.query, bf16[384,512]{1,0:T(8,128)(2,1)S(1)} %collective-permute-done.11.refs_0_, bf16[384,512]{1,0:T(8,128)(2,1)S(1)} %collective-permute-done.12.refs_1_, f32[4,384,64]{2,1,0:T(8,128)S(1)} %get-tuple-element.50.refs_2_, ...), custom_call_target="tpu_custom_call" | custom-call | tf_op jit(solution)/shard_map/attend/pallas_call | solution.py:23
  59.5 3.3 %collective-permute-done.14.refs_3_ = bf16[256,768]{1,0:T(8,128)(2,1)S(1)} collective-permute-done((bf16[256,768]{1,0:T(8,128)(2,1)S(1)}, bf16[256,768]{1,0:T(8,128)(2,1)S(1)}, u32[]{:S(2)}, u32[]{:S(2)}) %collective-permute-start.14) | collective-permute-done | bytes 393248 | tf_op jit(solution)/shard_map/ppermute | solution.py:197
  62.8 4.2 %collective-permute-done.13.refs_1_ = bf16[384,256]{1,0:T(8,128)(2,1)S(1)} collective-permute-done((bf16[384,256]{1,0:T(8,128)(2,1)S(1)}, bf16[384,256]{1,0:T(8,128)(2,1)S(1)}, u32[]{:S(2)}, u32[]{:S(2)}) %collective-permute-start.13) | collective-permute-done | bytes 196640 | tf_op jit(solution)/shard_map/ppermute | solution.py:197
  68.1 3.4 %collective-permute-start.15 = (bf16[3,96,256]{2,1,0:T(8,128)(2,1)S(1)}, bf16[3,96,256]{2,1,0:T(8,128)(2,1)S(1)}, u32[]{:S(2)}, u32[]{:S(2)}) collective-permute-start(bf16[3,96,256]{2,1,0:T(8,128)(2,1)S(1)} %finish.1), channel_id=1, source_target_pairs={{0,0},{8,1},{4,4},{12,5},{1,8},{9,9},{5,12},{13,13},{2,2},{10,3},{... | collective-permute-start | bytes 442376 | tf_op jit(solution)/shard_map/ppermute | solution.py:293
  71.5 3.5 %collective-permute-start.16 = (bf16[1,96,256]{2,1,0:T(8,128)(2,1)S(1)}, bf16[1,96,256]{2,1,0:T(8,128)(2,1)S(1)}, u32[]{:S(2)}, u32[]{:S(2)}) collective-permute-start(bf16[1,96,256]{2,1,0:T(8,128)(2,1)S(1)} %get-tuple-element.58), channel_id=1, source_target_pairs={{0,4},{8,5},{4,8},{12,9},{1,12},{9,13},{2,6},{10,7},{6,10},{14,11}... | collective-permute-start | bytes 147464 | tf_op jit(solution)/shard_map/ppermute | solution.py:294
  75.0 2.1 %collective-permute-start.17 = (bf16[1,96,256]{2,1,0:T(8,128)(2,1)S(1)}, bf16[1,96,256]{2,1,0:T(8,128)(2,1)S(1)}, u32[]{:S(2)}, u32[]{:S(2)}) collective-permute-start(bf16[1,96,256]{2,1,0:T(8,128)(2,1)S(1)} %get-tuple-element.57), channel_id=1, source_target_pairs={{4,0},{12,1},{1,4},{9,5},{5,8},{13,9},{6,2},{14,3},{3,6},{11,7},{7... | collective-permute-start | bytes 147464 | tf_op jit(solution)/shard_map/ppermute | solution.py:297
  77.1 5.1 %collective-permute-done.17.below = bf16[1,96,256]{2,1,0:T(8,128)(2,1)S(1)} collective-permute-done((bf16[1,96,256]{2,1,0:T(8,128)(2,1)S(1)}, bf16[1,96,256]{2,1,0:T(8,128)(2,1)S(1)}, u32[]{:S(2)}, u32[]{:S(2)}) %collective-permute-start.17) | collective-permute-done | bytes 49184 | tf_op jit(solution)/shard_map/ppermute | solution.py:297
  (36 shorter events, 9.5 us)
Async XLA Ops:
  0.0 15.9 %copy-start.4 = (bf16[1,384,384]{2,1,0:T(8,128)(2,1)S(1)}, bf16[1,384,384]{2,1,0:T(8,128)(2,1)}, u32[]{:S(2)}) copy-start(bf16[1,384,384]{2,1,0:T(8,128)(2,1)} %param.9) | copy-start | bytes 884740
  0.0 13.5 %collective-permute-start = (bf16[384,384]{1,0:T(8,128)(2,1)}, bf16[384,384]{1,0:T(8,128)(2,1)S(1)}, u32[]{:S(2)}, u32[]{:S(2)}) collective-permute-start(bf16[384,384]{1,0:T(8,128)(2,1)} %bitcast.12), channel_id=1, source_target_pairs={{0,0},{1,8},{4,4},{5,12},{8,1},{9,9},{12,5},{13,13},{2,2},{3,10},{... | collective-permute-start | bytes 884744 | tf_op jit(solution)/shard_map/ppermute | solution.py:219
  5.7 10.2 %collective-permute-start.3 = (bf16[384,384]{1,0:T(8,128)(2,1)}, bf16[384,384]{1,0:T(8,128)(2,1)S(1)}, u32[]{:S(2)}, u32[]{:S(2)}) collective-permute-start(bf16[384,384]{1,0:T(8,128)(2,1)} %bitcast.10), channel_id=1, source_target_pairs={{2,0},{0,2},{3,1},{1,3},{6,4},{4,6},{7,5},{5,7},{10,8},{8,10},{11,... | collective-permute-start | bytes 884744 | tf_op jit(solution)/shard_map/ppermute | solution.py:197
  13.5 5.6 %collective-permute-start.1 = (bf16[384,384]{1,0:T(8,128)(2,1)S(1)}, bf16[384,384]{1,0:T(8,128)(2,1)S(1)}, u32[]{:S(2)}, u32[]{:S(2)}) collective-permute-start(bf16[384,384]{1,0:T(8,128)(2,1)S(1)} %collective-permute-done.refs_0_.refs_4_), channel_id=1, source_target_pairs={{2,0},{0,2},{3,1},{1,3},{6,4},{4,6},{7,5},{5,7},{10,8},{8,10},{11,... | collective-permute-start | bytes 884744 | tf_op jit(solution)/shard_map/ppermute | solution.py:197
  15.9 3.2 %copy-start = (bf16[3,768,256]{2,1,0:T(8,128)(2,1)S(1)}, bf16[3,768,256]{2,1,0:T(8,128)(2,1)}, u32[]{:S(2)}) copy-start(bf16[3,768,256]{2,1,0:T(8,128)(2,1)} %param.10) | copy-start | bytes 3538948
  16.8 14.4 %collective-permute-start.4 = (bf16[384,512]{1,0:T(8,128)(2,1)S(1)}, bf16[384,512]{1,0:T(8,128)(2,1)S(1)}, u32[]{:S(2)}, u32[]{:S(2)}) collective-permute-start(bf16[384,512]{1,0:T(8,128)(2,1)S(1)} %project.3), channel_id=1, source_target_pairs={{0,0},{1,8},{4,4},{5,12},{8,1},{9,9},{12,5},{13,13},{2,2},{3,10},{... | collective-permute-start | bytes 1179656 | tf_op jit(solution)/shard_map/ppermute | solution.py:219
  19.1 5.9 %copy-start.2 = (bf16[256,768]{1,0:T(8,128)(2,1)S(1)}, bf16[256,768]{1,0:T(8,128)(2,1)}, u32[]{:S(2)}) copy-start(bf16[256,768]{1,0:T(8,128)(2,1)} %refs_2_) | copy-start | bytes 1179652
  19.1 14.7 %copy-start.5 = (bf16[384,256]{1,0:T(8,128)(2,1)S(1)}, bf16[384,256]{1,0:T(8,128)(2,1)}, u32[]{:S(2)}) copy-start(bf16[384,256]{1,0:T(8,128)(2,1)} %refs_5_) | copy-start | bytes 589828
  20.2 13.1 %collective-permute-start.2 = (bf16[384,512]{1,0:T(8,128)(2,1)S(1)}, bf16[384,512]{1,0:T(8,128)(2,1)S(1)}, u32[]{:S(2)}, u32[]{:S(2)}) collective-permute-start(bf16[384,512]{1,0:T(8,128)(2,1)S(1)} %get-tuple-element.33.refs_0_), channel_id=1, source_target_pairs={{4,0},{0,4},{12,8},{8,12},{5,1},{1,5},{13,9},{9,13},{6,2},{2,6},{1... | collective-permute-start | bytes 1179656 | tf_op jit(solution)/shard_map/ppermute | solution.py:205
  25.0 15.3 %collective-permute-start.7 = (bf16[256,768]{1,0:T(8,128)(2,1)S(1)}, bf16[256,768]{1,0:T(8,128)(2,1)S(1)}, u32[]{:S(2)}, u32[]{:S(2)}) collective-permute-start(bf16[256,768]{1,0:T(8,128)(2,1)S(1)} %copy-done.2), channel_id=1, source_target_pairs={{2,0},{0,2},{3,1},{1,3},{6,4},{4,6},{7,5},{5,7},{10,8},{8,10},{11,... | collective-permute-start | bytes 1179656 | tf_op jit(solution)/shard_map/ppermute | solution.py:197
  33.3 7.1 %collective-permute-start.5 = (bf16[384,512]{1,0:T(8,128)(2,1)S(1)}, bf16[384,512]{1,0:T(8,128)(2,1)S(1)}, u32[]{:S(2)}, u32[]{:S(2)}) collective-permute-start(bf16[384,512]{1,0:T(8,128)(2,1)S(1)} %get-tuple-element.33.refs_0_), channel_id=1, source_target_pairs={{1,0},{0,1},{3,2},{2,3},{5,4},{4,5},{7,6},{6,7},{9,8},{8,9},{11,10... | collective-permute-start | bytes 1179656 | tf_op jit(solution)/shard_map/ppermute | solution.py:211
  33.3 7.1 %collective-permute-start.6 = (bf16[384,512]{1,0:T(8,128)(2,1)S(1)}, bf16[384,512]{1,0:T(8,128)(2,1)S(1)}, u32[]{:S(2)}, u32[]{:S(2)}) collective-permute-start(bf16[384,512]{1,0:T(8,128)(2,1)S(1)} %collective-permute-done.2.refs_1_), channel_id=1, source_target_pairs={{1,0},{0,1},{3,2},{2,3},{5,4},{4,5},{7,6},{6,7},{9,8},{8,9},{11,10... | collective-permute-start | bytes 1179656 | tf_op jit(solution)/shard_map/ppermute | solution.py:211
  33.8 6.5 %collective-permute-start.8 = (bf16[384,256]{1,0:T(8,128)(2,1)S(1)}, bf16[384,256]{1,0:T(8,128)(2,1)S(1)}, u32[]{:S(2)}, u32[]{:S(2)}) collective-permute-start(bf16[384,256]{1,0:T(8,128)(2,1)S(1)} %copy-done.5), channel_id=1, source_target_pairs={{2,0},{0,2},{3,1},{1,3},{6,4},{4,6},{7,5},{5,7},{10,8},{8,10},{11,... | collective-permute-start | bytes 589832 | tf_op jit(solution)/shard_map/ppermute | solution.py:197
  37.3 13.4 %collective-permute-start.10 = (bf16[384,512]{1,0:T(8,128)(2,1)S(1)}, bf16[384,512]{1,0:T(8,128)(2,1)S(1)}, u32[]{:S(2)}, u32[]{:S(2)}) collective-permute-start(bf16[384,512]{1,0:T(8,128)(2,1)S(1)} %collective-permute-done.4.refs_0_), channel_id=1, source_target_pairs={{4,0},{0,4},{12,8},{8,12},{5,1},{1,5},{13,9},{9,13},{6,2},{2,6},{1... | collective-permute-start | bytes 1179656 | tf_op jit(solution)/shard_map/ppermute | solution.py:205
  43.5 9.0 %copy-start.3 = (bf16[256,768]{1,0:T(8,128)(2,1)S(1)}, bf16[256,768]{1,0:T(8,128)(2,1)}, u32[]{:S(2)}) copy-start(bf16[256,768]{1,0:T(8,128)(2,1)} %refs_2_.1) | copy-start | bytes 1179652
  43.5 5.7 %collective-permute-start.9 = (bf16[384,256]{1,0:T(8,128)(2,1)S(1)}, bf16[384,256]{1,0:T(8,128)(2,1)S(1)}, u32[]{:S(2)}, u32[]{:S(2)}) collective-permute-start(bf16[384,256]{1,0:T(8,128)(2,1)S(1)} %attend.5.refs_0_), channel_id=1, source_target_pairs={{2,0},{0,2},{3,1},{1,3},{6,4},{4,6},{7,5},{5,7},{10,8},{8,10},{11,... | collective-permute-start | bytes 589832 | tf_op jit(solution)/shard_map/ppermute | solution.py:197
  50.7 5.3 %collective-permute-start.11 = (bf16[384,512]{1,0:T(8,128)(2,1)S(1)}, bf16[384,512]{1,0:T(8,128)(2,1)S(1)}, u32[]{:S(2)}, u32[]{:S(2)}) collective-permute-start(bf16[384,512]{1,0:T(8,128)(2,1)S(1)} %collective-permute-done.4.refs_0_), channel_id=1, source_target_pairs={{1,0},{0,1},{3,2},{2,3},{5,4},{4,5},{7,6},{6,7},{9,8},{8,9},{11,10... | collective-permute-start | bytes 1179656 | tf_op jit(solution)/shard_map/ppermute | solution.py:211
  52.4 3.6 %collective-permute-start.12 = (bf16[384,512]{1,0:T(8,128)(2,1)S(1)}, bf16[384,512]{1,0:T(8,128)(2,1)S(1)}, u32[]{:S(2)}, u32[]{:S(2)}) collective-permute-start(bf16[384,512]{1,0:T(8,128)(2,1)S(1)} %collective-permute-done.10.refs_1_), channel_id=1, source_target_pairs={{1,0},{0,1},{3,2},{2,3},{5,4},{4,5},{7,6},{6,7},{9,8},{8,9},{11,10... | collective-permute-start | bytes 1179656 | tf_op jit(solution)/shard_map/ppermute | solution.py:211
  52.5 10.3 %collective-permute-start.14 = (bf16[256,768]{1,0:T(8,128)(2,1)S(1)}, bf16[256,768]{1,0:T(8,128)(2,1)S(1)}, u32[]{:S(2)}, u32[]{:S(2)}) collective-permute-start(bf16[256,768]{1,0:T(8,128)(2,1)S(1)} %copy-done.3), channel_id=1, source_target_pairs={{2,0},{0,2},{3,1},{1,3},{6,4},{4,6},{7,5},{5,7},{10,8},{8,10},{11,... | collective-permute-start | bytes 1179656 | tf_op jit(solution)/shard_map/ppermute | solution.py:197
  59.1 23.0 %copy-start.1 = (bf16[3,3,256,256]{3,2,1,0:T(8,128)(2,1)S(1)}, bf16[3,3,256,256]{3,2,1,0:T(8,128)(2,1)}, u32[]{:S(2)}) copy-start(bf16[3,3,256,256]{3,2,1,0:T(8,128)(2,1)} %weight.1) | copy-start | bytes 3538948
  59.2 7.8 %collective-permute-start.13 = (bf16[384,256]{1,0:T(8,128)(2,1)S(1)}, bf16[384,256]{1,0:T(8,128)(2,1)S(1)}, u32[]{:S(2)}, u32[]{:S(2)}) collective-permute-start(bf16[384,256]{1,0:T(8,128)(2,1)S(1)} %attend.7.refs_0_), channel_id=1, source_target_pairs={{2,0},{0,2},{3,1},{1,3},{6,4},{4,6},{7,5},{5,7},{10,8},{8,10},{11,... | collective-permute-start | bytes 589832 | tf_op jit(solution)/shard_map/ppermute | solution.py:197
  68.1 14.1 %collective-permute-start.15 = (bf16[3,96,256]{2,1,0:T(8,128)(2,1)S(1)}, bf16[3,96,256]{2,1,0:T(8,128)(2,1)S(1)}, u32[]{:S(2)}, u32[]{:S(2)}) collective-permute-start(bf16[3,96,256]{2,1,0:T(8,128)(2,1)S(1)} %finish.1), channel_id=1, source_target_pairs={{0,0},{8,1},{4,4},{12,5},{1,8},{9,9},{5,12},{13,13},{2,2},{10,3},{... | collective-permute-start | bytes 442376 | tf_op jit(solution)/shard_map/ppermute | solution.py:293
  71.5 5.6 %collective-permute-start.16 = (bf16[1,96,256]{2,1,0:T(8,128)(2,1)S(1)}, bf16[1,96,256]{2,1,0:T(8,128)(2,1)S(1)}, u32[]{:S(2)}, u32[]{:S(2)}) collective-permute-start(bf16[1,96,256]{2,1,0:T(8,128)(2,1)S(1)} %get-tuple-element.58), channel_id=1, source_target_pairs={{0,4},{8,5},{4,8},{12,9},{1,12},{9,13},{2,6},{10,7},{6,10},{14,11}... | collective-permute-start | bytes 147464 | tf_op jit(solution)/shard_map/ppermute | solution.py:294
  75.0 7.2 %collective-permute-start.17 = (bf16[1,96,256]{2,1,0:T(8,128)(2,1)S(1)}, bf16[1,96,256]{2,1,0:T(8,128)(2,1)S(1)}, u32[]{:S(2)}, u32[]{:S(2)}) collective-permute-start(bf16[1,96,256]{2,1,0:T(8,128)(2,1)S(1)} %get-tuple-element.57), channel_id=1, source_target_pairs={{4,0},{12,1},{1,4},{9,5},{5,8},{13,9},{6,2},{14,3},{3,6},{11,7},{7... | collective-permute-start | bytes 147464 | tf_op jit(solution)/shard_map/ppermute | solution.py:297

commit v5 on v4

--- a/solution.py
+++ b/solution.py
@@ -46,11 +46,11 @@
     return jnp.dot(left, right, preferred_element_type=F32)
 
 
-def project_kernel(place, *refs, count, scaled):
+def project_kernel(place, *refs, count, scaled, first):
     pieces, weight, outs = refs[:count], refs[count], refs[count + 1 :]
     normed = normalized([piece[...] for piece in pieces])
     products = []
-    for which in range(weight.shape[0]):
+    for which in range(first, weight.shape[0]):
         products.append(
             sum(
                 dot(normed[step], weight[which, lax.rem(place[0] + step, count)])
@@ -103,6 +103,24 @@
         outs[0][...] = jnp.concatenate(heads, axis=1).astype(BF16)
 
 
+def unpack_kernel(place, *refs):
+    halves, outs = refs[:-3], refs[-3:]
+    for step, half in enumerate(halves):
+        core = lax.rem(place[1] + step, len(halves))
+        start = 0
+        for out in outs[:2]:
+            rows = out.shape[0] // len(halves)
+            out[pl.ds(pl.multiple_of(core * rows, rows), rows), :] = half[start : start + rows, :]
+            start += rows
+        blocks = half.shape[1] // outs[2].shape[1]
+        block = outs[2].shape[0] // blocks
+        rows = block // len(halves)
+        for index in range(blocks):
+            first = pl.multiple_of(core * rows + index * block, rows)
+            lanes = slice(index * outs[2].shape[1], (index + 1) * outs[2].shape[1])
+            outs[2][pl.ds(first, rows), :] = half[start : start + rows, lanes]
+
+
 def pick(options, slot):
     chosen = options[0]
     for index in range(1, len(options)):
@@ -173,7 +191,7 @@
     bands, tiles, cores = (lax.axis_size(axis) for axis in ("blk", "tile", "pair"))
     half = bands // cores
     both = ("blk", "pair")
-    place = lax.axis_index("tile").astype(jnp.int32).reshape(1)
+    place = jnp.stack([lax.axis_index("tile"), lax.axis_index("pair")]).astype(jnp.int32)
     rows, share = left_tokens.shape[1:]
     columns = self_qkv.shape[2]
     channels = reassemble.shape[1]
@@ -218,14 +236,41 @@
     def moved(tokens):
         return lax.ppermute(tokens, both, [(home(*p), worker(*p)) for p in places])
 
-    def project(pieces, weights, scaled):
+    def project(pieces, weights, scaled, first):
         shapes = [((rows, columns), BF16)] * scaled + [((rows, 2 * columns), BF16)]
         stacked = weights.reshape(weights.shape[0], tiles, share, columns)
         return run_kernel(
-            functools.partial(project_kernel, count=tiles, scaled=scaled),
+            functools.partial(project_kernel, count=tiles, scaled=scaled, first=first),
             "project",
             shapes,
             [*pieces, stacked],
+            0,
+            place,
+        )
+
+    def packed_half():
+        parts = [self_out, cross_out]
+        blocks = self_out.shape[1] // channels
+        height = share // blocks
+        parts.append(
+            jnp.concatenate(
+                [reassemble[i * height : (i + 1) * height] for i in range(blocks)], axis=1
+            )
+        )
+        core = lax.axis_index("pair")
+        return jnp.concatenate(
+            [
+                lax.dynamic_slice_in_dim(p, core * (p.shape[0] // cores), p.shape[0] // cores)
+                for p in parts
+            ]
+        )
+
+    def unpacked(half):
+        return run_kernel(
+            unpack_kernel,
+            "unpack",
+            [(w.shape, BF16) for w in (self_out, cross_out, reassemble)],
+            [half, *across(half)],
             0,
             place,
         )
@@ -247,22 +292,21 @@
     left_here = moved(left_tokens[0])
     left = tile_pieces(left_here)
     right = tile_pieces(right_tokens[0])
-    (right_pack,) = project(right, cross_qkv[1:], False)
+    (right_pack,) = project(right, cross_qkv, False, 1)
     right_pack = moved(right_pack)
-    query, pack = project(left, self_qkv, True)
+    query, pack = project(left, self_qkv, True, 0)
     query_weight = cross_qkv[0].reshape(tiles, share, columns)
-    near, right_pack, query_weight = lax.optimization_barrier(
-        ([pack, *neighbours(pack)], right_pack, query_weight)
+    beside = neighbours(tied(pack, right_pack))
+    halves = tile_pieces(tied(packed_half(), left_here))[1:]
+    near, query_weight, halves = lax.optimization_barrier(
+        ([pack, *beside], query_weight, halves)
     )
     far = [q for p in near for q in across(p)]
-    self_out_pieces = tile_pieces(tied(self_out, left))
-    reassemble_pieces = tile_pieces(tied(reassemble, left))
     state = attend(query, grouped(near))
     right_pack = tied(right_pack, state)
     right_near = [right_pack, *neighbours(right_pack)]
-    far, self_out_pieces, reassemble_pieces = lax.optimization_barrier(
-        (far, self_out_pieces, reassemble_pieces)
-    )
+    far, halves = lax.optimization_barrier((far, halves))
+    others = [unpacked(half) for half in halves]
     (own_mixed,) = attend(query, grouped(far), state, True)
 
     mixed = tile_pieces(own_mixed)
@@ -270,11 +314,10 @@
         functools.partial(update_kernel, count=tiles),
         "update",
         [((tiles, rows, share), BF16), ((rows, columns), BF16)],
-        [*mixed, *self_out_pieces, *left, query_weight],
+        [*mixed, self_out, *[o[0] for o in others], *left, query_weight],
         0,
         place,
     )
-    cross_out_pieces = tile_pieces(tied(cross_out, updated))
     right_near = tied(right_near, updated)
     right_far = [q for p in right_near for q in across(p)]
     state = attend(cross_query, grouped(right_near))
@@ -285,7 +328,14 @@
         functools.partial(finish_kernel, count=tiles, width=width),
         "finish",
         [((band_rows, width + 2 * EDGE, channels), BF16)],
-        [*mixed, *cross_out_pieces, updated, *reassemble_pieces],
+        [
+            *mixed,
+            cross_out,
+            *[o[1] for o in others],
+            updated,
+            reassemble,
+            *[o[2] for o in others],
+        ],
         0,
         place,
         [pltpu.VMEM((band_rows, GRID_W + 2 * EDGE, channels), BF16)],

time: 83.5 us -> 86.1 us (1.031)
  waiting for transfers between devices: 34.1 us -> 29.5 us
  Pallas kernels: 16.3 us -> 19.5 us
  local copies, waits for them, and re-layouts: 2.24 us -> 4.93 us
  other arithmetic: 0 us -> 0.89 us
    ppermute x2, waiting for transfers between devices: 12.3 us -> 0.01 us  [moved(): return lax.ppermute(tokens, both, [(home(*p), worker(*p)) for p in places])]
    ppermute x7 -> x5, waiting for transfers between devices: 14.6 us -> 20.6 us  [tile_pieces(): lax.ppermute(own, 'tile', [((i + s) % tiles, i) for i in range(tiles)])]
    pallas_call x9 -> x10, Pallas kernels: 16.3 us -> 19.5 us  [run_kernel(): pl.pallas_call(kernel, out_shape=[jax.ShapeDtypeStruct(*s) for s in shape...]
    ppermute x1, starting transfers between devices: 3.38 us -> 5.95 us  [body(): back = lax.ppermute(window, both, [(worker(*p), home(*p)) for p in places])]
    unnamed x12 -> x14, local copies, waits for them, and re-layouts: 0.03 us -> 2.26 us
    ppermute x2, starting transfers between devices: 7.86 us -> 9.92 us  [moved(): return lax.ppermute(tokens, both, [(home(*p), worker(*p)) for p in places])]
    ppermute x1, starting transfers between devices: 3.45 us -> 1.64 us  [body(): lax.ppermute(window[-1:], both, [(worker(b, p), home(b + 1, p)) for b, p...]
    ppermute x4 -> x5, waiting for transfers between devices: 0.01 us -> 1.78 us  [across(): lax.ppermute(pack, 'pair', [((i + s) % cores, i) for i in range(cores)])]
  transfers between devices with their start and end apart: 18 -> 17, of which waited for: 9 -> 9; matrix products, arithmetic and copies ran while one was open for 3% -> 4% of each run, Pallas kernels for 17% -> 16%
where the time goes in v5:
time: 86.1 us; the launch traced here: 85.7 us
  starting transfers between devices  30.7 us (36%)
  waiting for transfers between devices  29.5 us (34%)
  Pallas kernels  19.5 us (23%)
  local copies, waits for them, and re-layouts  4.93 us (6%)
  other arithmetic  0.89 us (1%)
    ppermute x5, waiting for transfers between devices, tile_pieces(): lax.ppermute(own, 'tile', [((i + s) % tiles, i) for i in range(tiles)])  20.6 us
    pallas_call x10, Pallas kernels, run_kernel(): pl.pallas_call(kernel, out_shape=[jax.ShapeDtypeStruct(*s) for s in shape...  19.5 us
    ppermute x2, starting transfers between devices, moved(): return lax.ppermute(tokens, both, [(home(*p), worker(*p)) for p in places])  9.92 us
    ppermute x1, starting transfers between devices, body(): back = lax.ppermute(window, both, [(worker(*p), home(*p)) for p in places])  5.95 us
    ppermute x5, starting transfers between devices, tile_pieces(): lax.ppermute(own, 'tile', [((i + s) % tiles, i) for i in range(tiles)])  5.44 us
    ppermute x1, waiting for transfers between devices, body(): lax.ppermute(window[:1], both, [(worker(b, p), home(b - 1, p)) for b, p i...  4.44 us
    ppermute x1, starting transfers between devices, body(): lax.ppermute(window[:1], both, [(worker(b, p), home(b - 1, p)) for b, p i...  2.75 us
    ppermute x2, starting transfers between devices, neighbours(): lax.ppermute(pack, 'blk', [(g + (i + s) % half, g + i) for g, i in ring])  2.73 us
  transfers between devices with their start and end apart: 17, of which 9 were waited for; matrix products, arithmetic and copies ran while one was open for 4% of the time, Pallas kernels for 16%

profile of v5, /device:TPU:1, one launch (start us, length us, event | category | flops | bytes accessed | tf_op | source)
XLA Modules:
  0.0 85.7 jit_solution(14601302184440381820)
XLA Ops:
  0.0 5.6 %collective-permute-start = (bf16[384,384]{1,0:T(8,128)(2,1)}, bf16[384,384]{1,0:T(8,128)(2,1)S(1)}, u32[]{:S(2)}, u32[]{:S(2)}) collective-permute-start(bf16[384,384]{1,0:T(8,128)(2,1)} %bitcast.13), channel_id=1, source_target_pairs={{0,0},{1,8},{4,4},{5,12},{8,1},{9,9},{12,5},{13,13},{2,2},{3,10},{... | collective-permute-start | bytes 884744 | tf_op jit(solution)/shard_map/ppermute | solution.py:237
  7.0 1.6 %fusion.2 = (bf16[128,256]{1,0:T(8,128)(2,1)S(1)}, bf16[128,256]{1,0:T(8,128)(2,1)}, bf16[128,256]{1,0:T(8,128)(2,1)}) fusion(bf16[384,256]{1,0:T(8,128)(2,1)} %refs_5_.1), kind=kLoop, calls=%fused_computation.9 | loop fusion | bytes 393216 | tf_op jit(solution)/shard_map/slice | solution.py:257
  8.6 3.4 %collective-permute-done.2.refs_1_ = bf16[384,384]{1,0:T(8,128)(2,1)S(1)} collective-permute-done((bf16[384,384]{1,0:T(8,128)(2,1)}, bf16[384,384]{1,0:T(8,128)(2,1)S(1)}, u32[]{:S(2)}, u32[]{:S(2)}) %collective-permute-start.2) | collective-permute-done | bytes 294944 | tf_op jit(solution)/shard_map/ppermute | solution.py:215
  14.2 1.4 %project.3 = bf16[384,512]{1,0:T(8,128)(2,1)S(1)} custom-call(s32[2]{0:T(128)S(1)} %pad_add_fusion.place, bf16[384,384]{1,0:T(8,128)(2,1)S(1)} %bitcast.12, bf16[384,384]{1,0:T(8,128)(2,1)S(1)} %collective-permute-done.2.refs_1_, bf16[3,2,384,256]{3,2,1,0:T(8,128)(2,1)S(1)} %bitcast.8), custom_call_target="tpu_custom_call" | custom-call | tf_op jit(solution)/shard_map/project/pallas_call | solution.py:23
  15.6 4.3 %collective-permute-start.3 = (bf16[384,512]{1,0:T(8,128)(2,1)S(1)}, bf16[384,512]{1,0:T(8,128)(2,1)S(1)}, u32[]{:S(2)}, u32[]{:S(2)}) collective-permute-start(bf16[384,512]{1,0:T(8,128)(2,1)S(1)} %project.3), channel_id=1, source_target_pairs={{0,0},{1,8},{4,4},{5,12},{8,1},{9,9},{12,5},{13,13},{2,2},{3,10},{... | collective-permute-start | bytes 1179656 | tf_op jit(solution)/shard_map/ppermute | solution.py:237
  22.5 6.7 %collective-permute-done.1.refs_1_.refs_5_ = bf16[384,384]{1,0:T(8,128)(2,1)S(1)} collective-permute-done((bf16[384,384]{1,0:T(8,128)(2,1)S(1)}, bf16[384,384]{1,0:T(8,128)(2,1)S(1)}, u32[]{:S(2)}, u32[]{:S(2)}) %collective-permute-start.1) | collective-permute-done | bytes 294944 | tf_op jit(solution)/shard_map/ppermute | solution.py:215
  29.2 1.6 %project.2 = (bf16[384,256]{1,0:T(8,128)(2,1)S(1)}, bf16[384,512]{1,0:T(8,128)(2,1)S(1)}) custom-call(s32[2]{0:T(128)S(1)} %pad_add_fusion.place, bf16[384,384]{1,0:T(8,128)(2,1)S(1)} %collective-permute-done.refs_0_.refs_4_, bf16[384,384]{1,0:T(8,128)(2,1)S(1)} %collective-permute-done.1.refs_1_.refs_5_, bf16[3,2,384,256]{3,2,1,0:T(8,128)(2,1)S(1)} %bitcast.10), custom_call_target="tpu_custom_call" | custom-call | tf_op jit(solution)/shard_map/project/pallas_call | solution.py:23
  30.8 1.4 %collective-permute-start.4 = (bf16[384,512]{1,0:T(8,128)(2,1)S(1)}, bf16[384,512]{1,0:T(8,128)(2,1)S(1)}, u32[]{:S(2)}, u32[]{:S(2)}) collective-permute-start(bf16[384,512]{1,0:T(8,128)(2,1)S(1)} %get-tuple-element.34.refs_0_), channel_id=1, source_target_pairs={{4,0},{0,4},{12,8},{8,12},{5,1},{1,5},{13,9},{9,13},{6,2},{2,6},{1... | collective-permute-start | bytes 1179656 | tf_op jit(solution)/shard_map/ppermute | solution.py:223
  33.2 1.6 %collective-permute-done.5.refs_0_ = bf16[320,768]{1,0:T(8,128)(2,1)S(1)} collective-permute-done((bf16[320,768]{1,0:T(8,128)(2,1)S(1)}, bf16[320,768]{1,0:T(8,128)(2,1)S(1)}, u32[]{:S(2)}, u32[]{:S(2)}) %collective-permute-start.5) | collective-permute-done | bytes 491552 | tf_op jit(solution)/shard_map/ppermute | solution.py:215
  34.9 2.7 %collective-permute-done.4.refs_1_ = bf16[384,512]{1,0:T(8,128)(2,1)S(1)} collective-permute-done((bf16[384,512]{1,0:T(8,128)(2,1)S(1)}, bf16[384,512]{1,0:T(8,128)(2,1)S(1)}, u32[]{:S(2)}, u32[]{:S(2)}) %collective-permute-start.4) | collective-permute-done | bytes 393248 | tf_op jit(solution)/shard_map/ppermute | solution.py:223
  39.9 2.3 %attend.4 = (f32[4,384,64]{2,1,0:T(8,128)S(1)}, f32[4,384,2]{2,1,0:T(8,128)S(1)}) custom-call(bf16[384,256]{1,0:T(8,128)(2,1)S(1)} %get-tuple-element.30.query, bf16[384,512]{1,0:T(8,128)(2,1)S(1)} %get-tuple-element.34.refs_0_, bf16[384,512]{1,0:T(8,128)(2,1)S(1)} %collective-permute-done.4.refs_1_), custom_call_target="tpu_custom_call" | custom-call | tf_op jit(solution)/shard_map/attend/pallas_call | solution.py:23
  42.3 1.4 %collective-permute-start.10 = (bf16[384,512]{1,0:T(8,128)(2,1)S(1)}, bf16[384,512]{1,0:T(8,128)(2,1)S(1)}, u32[]{:S(2)}, u32[]{:S(2)}) collective-permute-start(bf16[384,512]{1,0:T(8,128)(2,1)S(1)} %collective-permute-done.3.refs_0_), channel_id=1, source_target_pairs={{4,0},{0,4},{12,8},{8,12},{5,1},{1,5},{13,9},{9,13},{6,2},{2,6},{1... | collective-permute-start | bytes 1179656 | tf_op jit(solution)/shard_map/ppermute | solution.py:223
  43.6 3.2 %attend.5.refs_0_ = bf16[384,256]{1,0:T(8,128)(2,1)S(1)} custom-call(bf16[384,256]{1,0:T(8,128)(2,1)S(1)} %get-tuple-element.30.query, bf16[384,512]{1,0:T(8,128)(2,1)S(1)} %collective-permute-done.6.refs_0_, bf16[384,512]{1,0:T(8,128)(2,1)S(1)} %collective-permute-done.7.refs_1_, f32[4,384,64]{2,1,0:T(8,128)S(1)} %get-tuple-element.39.refs_2_, ...), custom_call_target="tpu_custom_call" | custom-call | tf_op jit(solution)/shard_map/attend/pallas_call | solution.py:23
  48.7 3.9 %collective-permute-done.8.refs_1_ = bf16[384,256]{1,0:T(8,128)(2,1)S(1)} collective-permute-done((bf16[384,256]{1,0:T(8,128)(2,1)S(1)}, bf16[384,256]{1,0:T(8,128)(2,1)S(1)}, u32[]{:S(2)}, u32[]{:S(2)}) %collective-permute-start.8) | collective-permute-done | bytes 196640 | tf_op jit(solution)/shard_map/ppermute | solution.py:215
  52.6 2.0 %update.1 = (bf16[2,384,384]{2,1,0:T(8,128)(2,1)S(1)}, bf16[384,256]{1,0:T(8,128)(2,1)S(1)}) custom-call(s32[2]{0:T(128)S(1)} %pad_add_fusion.place, bf16[384,256]{1,0:T(8,128)(2,1)S(1)} %attend.5.refs_0_, bf16[384,256]{1,0:T(8,128)(2,1)S(1)} %collective-permute-done.8.refs_1_, bf16[256,768]{1,0:T(8,128)(2,1)S(1)} %copy-done.3, ...), custom_call_target="tpu_custom_call" | custom-call | tf_op jit(solution)/shard_map/update/pallas_call | solution.py:23
  54.7 1.6 %collective-permute-start.11 = (bf16[384,512]{1,0:T(8,128)(2,1)S(1)}, bf16[384,512]{1,0:T(8,128)(2,1)S(1)}, u32[]{:S(2)}, u32[]{:S(2)}) collective-permute-start(bf16[384,512]{1,0:T(8,128)(2,1)S(1)} %collective-permute-done.3.refs_0_), channel_id=1, source_target_pairs={{1,0},{0,1},{3,2},{2,3},{5,4},{4,5},{7,6},{6,7},{9,8},{8,9},{11,10... | collective-permute-start | bytes 1179656 | tf_op jit(solution)/shard_map/ppermute | solution.py:229
  56.4 2.3 %attend.6 = (f32[4,384,64]{2,1,0:T(8,128)S(1)}, f32[4,384,2]{2,1,0:T(8,128)S(1)}) custom-call(bf16[384,256]{1,0:T(8,128)(2,1)S(1)} %get-tuple-element.44.query, bf16[384,512]{1,0:T(8,128)(2,1)S(1)} %collective-permute-done.3.refs_0_, bf16[384,512]{1,0:T(8,128)(2,1)S(1)} %collective-permute-done.10.refs_1_), custom_call_target="tpu_custom_call" | custom-call | tf_op jit(solution)/shard_map/attend/pallas_call | solution.py:23
  58.7 3.3 %attend.7.refs_0_ = bf16[384,256]{1,0:T(8,128)(2,1)S(1)} custom-call(bf16[384,256]{1,0:T(8,128)(2,1)S(1)} %get-tuple-element.44.query, bf16[384,512]{1,0:T(8,128)(2,1)S(1)} %collective-permute-done.11.refs_0_, bf16[384,512]{1,0:T(8,128)(2,1)S(1)} %collective-permute-done.12.refs_1_, f32[4,384,64]{2,1,0:T(8,128)S(1)} %get-tuple-element.49.refs_2_, ...), custom_call_target="tpu_custom_call" | custom-call | tf_op jit(solution)/shard_map/attend/pallas_call | solution.py:23
  63.3 4.8 %collective-permute-done.13.refs_1_ = bf16[384,256]{1,0:T(8,128)(2,1)S(1)} collective-permute-done((bf16[384,256]{1,0:T(8,128)(2,1)S(1)}, bf16[384,256]{1,0:T(8,128)(2,1)S(1)}, u32[]{:S(2)}, u32[]{:S(2)}) %collective-permute-start.13) | collective-permute-done | bytes 196640 | tf_op jit(solution)/shard_map/ppermute | solution.py:215
  68.2 1.6 %finish.1 = bf16[3,96,256]{2,1,0:T(8,128)(2,1)S(1)} custom-call(s32[2]{0:T(128)S(1)} %pad_add_fusion.place, bf16[384,256]{1,0:T(8,128)(2,1)S(1)} %attend.7.refs_0_, bf16[384,256]{1,0:T(8,128)(2,1)S(1)} %collective-permute-done.13.refs_1_, bf16[256,768]{1,0:T(8,128)(2,1)S(1)} %copy-done.4, bf16[256,768]{1,0:T(8,128)(2,1)S(1)} %get-tuple-element.53.refs_3_, ...), custom_call_target="tpu_custom_call" | custom-call | tf_op jit(solution)/shard_map/finish/pallas_call | solution.py:23
  69.8 5.9 %collective-permute-start.14 = (bf16[3,96,256]{2,1,0:T(8,128)(2,1)S(1)}, bf16[3,96,256]{2,1,0:T(8,128)(2,1)S(1)}, u32[]{:S(2)}, u32[]{:S(2)}) collective-permute-start(bf16[3,96,256]{2,1,0:T(8,128)(2,1)S(1)} %finish.1), channel_id=1, source_target_pairs={{0,0},{8,1},{4,4},{12,5},{1,8},{9,9},{5,12},{13,13},{2,2},{10,3},{... | collective-permute-start | bytes 442376 | tf_op jit(solution)/shard_map/ppermute | solution.py:343
  75.8 1.6 %collective-permute-start.15 = (bf16[1,96,256]{2,1,0:T(8,128)(2,1)S(1)}, bf16[1,96,256]{2,1,0:T(8,128)(2,1)S(1)}, u32[]{:S(2)}, u32[]{:S(2)}) collective-permute-start(bf16[1,96,256]{2,1,0:T(8,128)(2,1)S(1)} %get-tuple-element.59), channel_id=1, source_target_pairs={{0,4},{8,5},{4,8},{12,9},{1,12},{9,13},{2,6},{10,7},{6,10},{14,11}... | collective-permute-start | bytes 147464 | tf_op jit(solution)/shard_map/ppermute | solution.py:344
  77.5 2.8 %collective-permute-start.16 = (bf16[1,96,256]{2,1,0:T(8,128)(2,1)S(1)}, bf16[1,96,256]{2,1,0:T(8,128)(2,1)S(1)}, u32[]{:S(2)}, u32[]{:S(2)}) collective-permute-start(bf16[1,96,256]{2,1,0:T(8,128)(2,1)S(1)} %get-tuple-element.58), channel_id=1, source_target_pairs={{4,0},{12,1},{1,4},{9,5},{5,8},{13,9},{6,2},{14,3},{3,6},{11,7},{7... | collective-permute-start | bytes 147464 | tf_op jit(solution)/shard_map/ppermute | solution.py:347
  80.2 4.4 %collective-permute-done.16.below = bf16[1,96,256]{2,1,0:T(8,128)(2,1)S(1)} collective-permute-done((bf16[1,96,256]{2,1,0:T(8,128)(2,1)S(1)}, bf16[1,96,256]{2,1,0:T(8,128)(2,1)S(1)}, u32[]{:S(2)}, u32[]{:S(2)}) %collective-permute-start.16) | collective-permute-done | bytes 49184 | tf_op jit(solution)/shard_map/ppermute | solution.py:347
  (41 shorter events, 13.8 us)
Async XLA Ops:
  0.0 20.0 %collective-permute-start = (bf16[384,384]{1,0:T(8,128)(2,1)}, bf16[384,384]{1,0:T(8,128)(2,1)S(1)}, u32[]{:S(2)}, u32[]{:S(2)}) collective-permute-start(bf16[384,384]{1,0:T(8,128)(2,1)} %bitcast.13), channel_id=1, source_target_pairs={{0,0},{1,8},{4,4},{5,12},{8,1},{9,9},{12,5},{13,13},{2,2},{3,10},{... | collective-permute-start | bytes 884744 | tf_op jit(solution)/shard_map/ppermute | solution.py:237
  5.6 6.4 %collective-permute-start.2 = (bf16[384,384]{1,0:T(8,128)(2,1)}, bf16[384,384]{1,0:T(8,128)(2,1)S(1)}, u32[]{:S(2)}, u32[]{:S(2)}) collective-permute-start(bf16[384,384]{1,0:T(8,128)(2,1)} %bitcast.11), channel_id=1, source_target_pairs={{2,0},{0,2},{3,1},{1,3},{6,4},{4,6},{7,5},{5,7},{10,8},{8,10},{11,... | collective-permute-start | bytes 884744 | tf_op jit(solution)/shard_map/ppermute | solution.py:215
  7.0 13.0 %copy-start.3 = (bf16[256,768]{1,0:T(8,128)(2,1)S(1)}, bf16[256,768]{1,0:T(8,128)(2,1)}, u32[]{:S(2)}) copy-start(bf16[256,768]{1,0:T(8,128)(2,1)} %refs_2_.2) | copy-start | bytes 1179652
  12.0 1.3 %copy-start = (bf16[3,768,256]{2,1,0:T(8,128)(2,1)S(1)}, bf16[3,768,256]{2,1,0:T(8,128)(2,1)}, u32[]{:S(2)}) copy-start(bf16[3,768,256]{2,1,0:T(8,128)(2,1)} %param.12) | copy-start | bytes 3538948
  13.3 1.0 %copy-start.6 = (bf16[1,384,384]{2,1,0:T(8,128)(2,1)S(1)}, bf16[1,384,384]{2,1,0:T(8,128)(2,1)}, u32[]{:S(2)}) copy-start(bf16[1,384,384]{2,1,0:T(8,128)(2,1)} %param.9) | copy-start | bytes 884740
  14.2 5.8 %copy-start.4 = (bf16[256,768]{1,0:T(8,128)(2,1)S(1)}, bf16[256,768]{1,0:T(8,128)(2,1)}, u32[]{:S(2)}) copy-start(bf16[256,768]{1,0:T(8,128)(2,1)} %refs_2_.3) | copy-start | bytes 1179652
  15.6 13.6 %copy-start.1 = (bf16[3,768,256]{2,1,0:T(8,128)(2,1)S(1)}, bf16[3,768,256]{2,1,0:T(8,128)(2,1)}, u32[]{:S(2)}) copy-start(bf16[3,768,256]{2,1,0:T(8,128)(2,1)} %param.10) | copy-start | bytes 3538948
  15.6 15.2 %collective-permute-start.3 = (bf16[384,512]{1,0:T(8,128)(2,1)S(1)}, bf16[384,512]{1,0:T(8,128)(2,1)S(1)}, u32[]{:S(2)}, u32[]{:S(2)}) collective-permute-start(bf16[384,512]{1,0:T(8,128)(2,1)S(1)} %project.3), channel_id=1, source_target_pairs={{0,0},{1,8},{4,4},{5,12},{8,1},{9,9},{12,5},{13,13},{2,2},{3,10},{... | collective-permute-start | bytes 1179656 | tf_op jit(solution)/shard_map/ppermute | solution.py:237
  20.0 9.2 %collective-permute-start.1 = (bf16[384,384]{1,0:T(8,128)(2,1)S(1)}, bf16[384,384]{1,0:T(8,128)(2,1)S(1)}, u32[]{:S(2)}, u32[]{:S(2)}) collective-permute-start(bf16[384,384]{1,0:T(8,128)(2,1)S(1)} %collective-permute-done.refs_0_.refs_4_), channel_id=1, source_target_pairs={{2,0},{0,2},{3,1},{1,3},{6,4},{4,6},{7,5},{5,7},{10,8},{8,10},{11,... | collective-permute-start | bytes 884744 | tf_op jit(solution)/shard_map/ppermute | solution.py:215
  22.1 12.7 %collective-permute-start.5 = (bf16[320,768]{1,0:T(8,128)(2,1)S(1)}, bf16[320,768]{1,0:T(8,128)(2,1)S(1)}, u32[]{:S(2)}, u32[]{:S(2)}) collective-permute-start(bf16[320,768]{1,0:T(8,128)(2,1)S(1)} %pad_maximum_fusion), channel_id=1, source_target_pairs={{2,0},{0,2},{3,1},{1,3},{6,4},{4,6},{7,5},{5,7},{10,8},{8,10},{11,... | collective-permute-start | bytes 1474568 | tf_op jit(solution)/shard_map/ppermute | solution.py:215
  30.8 6.7 %collective-permute-start.4 = (bf16[384,512]{1,0:T(8,128)(2,1)S(1)}, bf16[384,512]{1,0:T(8,128)(2,1)S(1)}, u32[]{:S(2)}, u32[]{:S(2)}) collective-permute-start(bf16[384,512]{1,0:T(8,128)(2,1)S(1)} %get-tuple-element.34.refs_0_), channel_id=1, source_target_pairs={{4,0},{0,4},{12,8},{8,12},{5,1},{1,5},{13,9},{9,13},{6,2},{2,6},{1... | collective-permute-start | bytes 1179656 | tf_op jit(solution)/shard_map/ppermute | solution.py:223
  37.5 1.7 %collective-permute-start.6 = (bf16[384,512]{1,0:T(8,128)(2,1)S(1)}, bf16[384,512]{1,0:T(8,128)(2,1)S(1)}, u32[]{:S(2)}, u32[]{:S(2)}) collective-permute-start(bf16[384,512]{1,0:T(8,128)(2,1)S(1)} %get-tuple-element.34.refs_0_), channel_id=1, source_target_pairs={{1,0},{0,1},{3,2},{2,3},{5,4},{4,5},{7,6},{6,7},{9,8},{8,9},{11,10... | collective-permute-start | bytes 1179656 | tf_op jit(solution)/shard_map/ppermute | solution.py:229
  37.5 2.3 %collective-permute-start.7 = (bf16[384,512]{1,0:T(8,128)(2,1)S(1)}, bf16[384,512]{1,0:T(8,128)(2,1)S(1)}, u32[]{:S(2)}, u32[]{:S(2)}) collective-permute-start(bf16[384,512]{1,0:T(8,128)(2,1)S(1)} %collective-permute-done.4.refs_1_), channel_id=1, source_target_pairs={{1,0},{0,1},{3,2},{2,3},{5,4},{4,5},{7,6},{6,7},{9,8},{8,9},{11,10... | collective-permute-start | bytes 1179656 | tf_op jit(solution)/shard_map/ppermute | solution.py:229
  39.8 8.3 %collective-permute-start.9 = (bf16[320,768]{1,0:T(8,128)(2,1)S(1)}, bf16[320,768]{1,0:T(8,128)(2,1)S(1)}, u32[]{:S(2)}, u32[]{:S(2)}) collective-permute-start(bf16[320,768]{1,0:T(8,128)(2,1)S(1)} %collective-permute-done.5.refs_0_), channel_id=1, source_target_pairs={{1,0},{0,1},{3,2},{2,3},{5,4},{4,5},{7,6},{6,7},{9,8},{8,9},{11,10... | collective-permute-start | bytes 1474568 | tf_op jit(solution)/shard_map/ppermute | solution.py:229
  42.3 12.4 %collective-permute-start.10 = (bf16[384,512]{1,0:T(8,128)(2,1)S(1)}, bf16[384,512]{1,0:T(8,128)(2,1)S(1)}, u32[]{:S(2)}, u32[]{:S(2)}) collective-permute-start(bf16[384,512]{1,0:T(8,128)(2,1)S(1)} %collective-permute-done.3.refs_0_), channel_id=1, source_target_pairs={{4,0},{0,4},{12,8},{8,12},{5,1},{1,5},{13,9},{9,13},{6,2},{2,6},{1... | collective-permute-start | bytes 1179656 | tf_op jit(solution)/shard_map/ppermute | solution.py:223
  46.8 5.8 %collective-permute-start.8 = (bf16[384,256]{1,0:T(8,128)(2,1)S(1)}, bf16[384,256]{1,0:T(8,128)(2,1)S(1)}, u32[]{:S(2)}, u32[]{:S(2)}) collective-permute-start(bf16[384,256]{1,0:T(8,128)(2,1)S(1)} %attend.5.refs_0_), channel_id=1, source_target_pairs={{2,0},{0,2},{3,1},{1,3},{6,4},{4,6},{7,5},{5,7},{10,8},{8,10},{11,... | collective-permute-start | bytes 589832 | tf_op jit(solution)/shard_map/ppermute | solution.py:215
  54.7 4.0 %collective-permute-start.11 = (bf16[384,512]{1,0:T(8,128)(2,1)S(1)}, bf16[384,512]{1,0:T(8,128)(2,1)S(1)}, u32[]{:S(2)}, u32[]{:S(2)}) collective-permute-start(bf16[384,512]{1,0:T(8,128)(2,1)S(1)} %collective-permute-done.3.refs_0_), channel_id=1, source_target_pairs={{1,0},{0,1},{3,2},{2,3},{5,4},{4,5},{7,6},{6,7},{9,8},{8,9},{11,10... | collective-permute-start | bytes 1179656 | tf_op jit(solution)/shard_map/ppermute | solution.py:229
  56.3 2.4 %collective-permute-start.12 = (bf16[384,512]{1,0:T(8,128)(2,1)S(1)}, bf16[384,512]{1,0:T(8,128)(2,1)S(1)}, u32[]{:S(2)}, u32[]{:S(2)}) collective-permute-start(bf16[384,512]{1,0:T(8,128)(2,1)S(1)} %collective-permute-done.10.refs_1_), channel_id=1, source_target_pairs={{1,0},{0,1},{3,2},{2,3},{5,4},{4,5},{7,6},{6,7},{9,8},{8,9},{11,10... | collective-permute-start | bytes 1179656 | tf_op jit(solution)/shard_map/ppermute | solution.py:229
  58.7 9.5 %copy-start.5 = (bf16[384,256]{1,0:T(8,128)(2,1)S(1)}, bf16[384,256]{1,0:T(8,128)(2,1)}, u32[]{:S(2)}) copy-start(bf16[384,256]{1,0:T(8,128)(2,1)} %refs_5_.1) | copy-start | bytes 589828
  62.1 6.1 %collective-permute-start.13 = (bf16[384,256]{1,0:T(8,128)(2,1)S(1)}, bf16[384,256]{1,0:T(8,128)(2,1)S(1)}, u32[]{:S(2)}, u32[]{:S(2)}) collective-permute-start(bf16[384,256]{1,0:T(8,128)(2,1)S(1)} %attend.7.refs_0_), channel_id=1, source_target_pairs={{2,0},{0,2},{3,1},{1,3},{6,4},{4,6},{7,5},{5,7},{10,8},{8,10},{11,... | collective-permute-start | bytes 589832 | tf_op jit(solution)/shard_map/ppermute | solution.py:215
  68.2 16.5 %copy-start.2 = (bf16[3,3,256,256]{3,2,1,0:T(8,128)(2,1)S(1)}, bf16[3,3,256,256]{3,2,1,0:T(8,128)(2,1)}, u32[]{:S(2)}) copy-start(bf16[3,3,256,256]{3,2,1,0:T(8,128)(2,1)} %weight.1) | copy-start | bytes 3538948
  69.8 14.8 %collective-permute-start.14 = (bf16[3,96,256]{2,1,0:T(8,128)(2,1)S(1)}, bf16[3,96,256]{2,1,0:T(8,128)(2,1)S(1)}, u32[]{:S(2)}, u32[]{:S(2)}) collective-permute-start(bf16[3,96,256]{2,1,0:T(8,128)(2,1)S(1)} %finish.1), channel_id=1, source_target_pairs={{0,0},{8,1},{4,4},{12,5},{1,8},{9,9},{5,12},{13,13},{2,2},{10,3},{... | collective-permute-start | bytes 442376 | tf_op jit(solution)/shard_map/ppermute | solution.py:343
  75.8 4.4 %collective-permute-start.15 = (bf16[1,96,256]{2,1,0:T(8,128)(2,1)S(1)}, bf16[1,96,256]{2,1,0:T(8,128)(2,1)S(1)}, u32[]{:S(2)}, u32[]{:S(2)}) collective-permute-start(bf16[1,96,256]{2,1,0:T(8,128)(2,1)S(1)} %get-tuple-element.59), channel_id=1, source_target_pairs={{0,4},{8,5},{4,8},{12,9},{1,12},{9,13},{2,6},{10,7},{6,10},{14,11}... | collective-permute-start | bytes 147464 | tf_op jit(solution)/shard_map/ppermute | solution.py:344
  77.5 7.2 %collective-permute-start.16 = (bf16[1,96,256]{2,1,0:T(8,128)(2,1)S(1)}, bf16[1,96,256]{2,1,0:T(8,128)(2,1)S(1)}, u32[]{:S(2)}, u32[]{:S(2)}) collective-permute-start(bf16[1,96,256]{2,1,0:T(8,128)(2,1)S(1)} %get-tuple-element.58), channel_id=1, source_target_pairs={{4,0},{12,1},{1,4},{9,5},{5,8},{13,9},{6,2},{14,3},{3,6},{11,7},{7... | collective-permute-start | bytes 147464 | tf_op jit(solution)/shard_map/ppermute | solution.py:347

commit v6 on v5

--- a/solution.py
+++ b/solution.py
@@ -16,14 +16,15 @@
 QUERY_SCALE = math.log2(math.e) * HD**-0.5
 VMEM = pl.BlockSpec(memory_space=pltpu.VMEM)
 SMEM = pl.BlockSpec(memory_space=pltpu.SMEM)
-
-
-def run_kernel(kernel, name, shapes, operands, flops=0, place=None, scratch=()):
+HBM = pl.BlockSpec(memory_space=pl.ANY)
+
+
+def run_kernel(kernel, name, shapes, operands, flops=0, place=None, scratch=(), space=VMEM):
     leading = () if place is None else (place,)
     return pl.pallas_call(
         kernel,
         out_shape=[jax.ShapeDtypeStruct(*s) for s in shapes],
-        in_specs=[SMEM] * len(leading) + [VMEM] * len(operands),
+        in_specs=[SMEM] * len(leading) + [space] * len(operands),
         out_specs=[VMEM] * len(shapes),
         scratch_shapes=scratch,
         compiler_params=pltpu.CompilerParams(vmem_limit_bytes=24 << 20),
@@ -103,6 +104,33 @@
         outs[0][...] = jnp.concatenate(heads, axis=1).astype(BF16)
 
 
+def stage_kernel(place, *refs, cores):
+    count = (len(refs) - 2) // 2
+    sources, outs, half, sems = refs[:count], refs[count : 2 * count], refs[-2], refs[-1]
+    pairs = []
+    for source, out in zip(sources, outs):
+        pairs.append((source, out))
+    first_out, second_out, rows_out = sources[:3]
+    start = 0
+    for source in (first_out, second_out):
+        rows = source.shape[0] // cores
+        begin = pl.multiple_of(place[1] * rows, rows)
+        pairs.append((source.at[pl.ds(begin, rows)], half.at[pl.ds(start, rows)]))
+        start += rows
+    blocks = half.shape[1] // rows_out.shape[1]
+    block = rows_out.shape[0] // blocks
+    rows = block // cores
+    for index in range(blocks):
+        begin = pl.multiple_of(place[1] * rows + index * block, rows)
+        lanes = pl.ds(index * rows_out.shape[1], rows_out.shape[1])
+        pairs.append((rows_out.at[pl.ds(begin, rows)], half.at[pl.ds(start, rows), lanes]))
+    copies = [pltpu.make_async_copy(a, b, sems.at[i]) for i, (a, b) in enumerate(pairs)]
+    for copy in copies:
+        copy.start()
+    for copy in copies:
+        copy.wait()
+
+
 def unpack_kernel(place, *refs):
     halves, outs = refs[:-3], refs[-3:]
     for step, half in enumerate(halves):
@@ -147,7 +175,8 @@
         pieces.append(piece)
     normed = normalized(pieces)
     product = sum(
-        dot(normed[step], query_weight[lax.rem(place[0] + step, count)]) for step in range(count)
+        dot(normed[step], query_weight[0, lax.rem(place[0] + step, count)])
+        for step in range(count)
     )
     query[...] = (product * QUERY_SCALE).astype(BF16)
 
@@ -185,11 +214,9 @@
     out[...] = total.reshape(out.shape).astype(BF16)
 
 
-def body(
-    left_tokens, right_tokens, self_qkv, self_out, cross_qkv, cross_out, reassemble, conv_weight
-):
+def body(left_tokens, right_tokens, self_qkv, self_out, cross_qkv, cross_out, reassemble, taps):
     bands, tiles, cores = (lax.axis_size(axis) for axis in ("blk", "tile", "pair"))
-    half = bands // cores
+    span = bands // cores
     both = ("blk", "pair")
     place = jnp.stack([lax.axis_index("tile"), lax.axis_index("pair")]).astype(jnp.int32)
     rows, share = left_tokens.shape[1:]
@@ -202,8 +229,8 @@
         return band * cores + pair
 
     def worker(band, pair):
-        shift = (pair - band // half) % cores
-        return ((band + shift * half) % bands) * cores + (pair - shift) % cores
+        shift = (pair - band // span) % cores
+        return ((band + shift * span) % bands) * cores + (pair - shift) % cores
 
     places = [(band, pair) for band in range(bands) for pair in range(cores)]
 
@@ -218,10 +245,10 @@
         return [own, *others]
 
     def neighbours(pack):
-        ring = [(g * half, i) for g in range(cores) for i in range(half)]
+        ring = [(g * span, i) for g in range(cores) for i in range(span)]
         return [
-            lax.ppermute(pack, "blk", [(g + (i + s) % half, g + i) for g, i in ring])
-            for s in range(1, half)
+            lax.ppermute(pack, "blk", [(g + (i + s) % span, g + i) for g, i in ring])
+            for s in range(1, span)
         ]
 
     def across(pack):
@@ -248,21 +275,19 @@
             place,
         )
 
-    def packed_half():
-        parts = [self_out, cross_out]
-        blocks = self_out.shape[1] // channels
-        height = share // blocks
-        parts.append(
-            jnp.concatenate(
-                [reassemble[i * height : (i + 1) * height] for i in range(blocks)], axis=1
-            )
-        )
-        core = lax.axis_index("pair")
-        return jnp.concatenate(
-            [
-                lax.dynamic_slice_in_dim(p, core * (p.shape[0] // cores), p.shape[0] // cores)
-                for p in parts
-            ]
+    def staged(weights):
+        blocks = weights[0].shape[1] // channels
+        height = (weights[0].shape[0] + weights[1].shape[0] + share // blocks) // cores
+        shapes = [(w.shape, BF16) for w in weights] + [((height, weights[0].shape[1]), BF16)]
+        return run_kernel(
+            functools.partial(stage_kernel, cores=cores),
+            "stage",
+            shapes,
+            [pltpu.with_memory_space_constraint(w, pltpu.HBM) for w in weights],
+            0,
+            place,
+            [pltpu.SemaphoreType.DMA((len(weights) + 2 + blocks,))],
+            HBM,
         )
 
     def unpacked(half):
@@ -290,17 +315,17 @@
         )
 
     left_here = moved(left_tokens[0])
+    self_out, cross_out, reassemble, right_own, self_qkv, cross_qkv, taps, half = staged(
+        [self_out, cross_out, reassemble, right_tokens[0], self_qkv, cross_qkv, taps]
+    )
     left = tile_pieces(left_here)
-    right = tile_pieces(right_tokens[0])
+    right = [right_own, *tile_pieces(right_tokens[0])[1:]]
     (right_pack,) = project(right, cross_qkv, False, 1)
     right_pack = moved(right_pack)
     query, pack = project(left, self_qkv, True, 0)
-    query_weight = cross_qkv[0].reshape(tiles, share, columns)
     beside = neighbours(tied(pack, right_pack))
-    halves = tile_pieces(tied(packed_half(), left_here))[1:]
-    near, query_weight, halves = lax.optimization_barrier(
-        ([pack, *beside], query_weight, halves)
-    )
+    halves = tile_pieces(tied(half, left_here))[1:]
+    near, halves = lax.optimization_barrier(([pack, *beside], halves))
     far = [q for p in near for q in across(p)]
     state = attend(query, grouped(near))
     right_pack = tied(right_pack, state)
@@ -314,7 +339,8 @@
         functools.partial(update_kernel, count=tiles),
         "update",
         [((tiles, rows, share), BF16), ((rows, columns), BF16)],
-        [*mixed, self_out, *[o[0] for o in others], *left, query_weight],
+        [*mixed, self_out, *[o[0] for o in others], *left,
+            cross_qkv.reshape(3, tiles, share, columns)],
         0,
         place,
     )
@@ -351,7 +377,7 @@
         conv_kernel,
         "join",
         [((band_rows, width, channels), BF16)],
-        [back, above, below, conv_weight],
+        [back, above, below, taps],
     )
     return joined[None]
 

time: 86.1 us -> 82 us (0.952)
  local copies, waits for them, and re-layouts: 4.93 us -> 0.01 us
  Pallas kernels: 19.5 us -> 22.3 us
    pallas_call x10 -> x11, Pallas kernels: 19.5 us -> 22.3 us  [run_kernel(): pl.pallas_call(kernel, out_shape=[jax.ShapeDtypeStruct(*s) for s in shape...]
    slice x2 -> x0, local copies, waits for them, and re-layouts: 2.63 us -> none  [the longest x1 1.61 us: packed_half(): reassemble[i * height:(i + 1) * height]]
    unnamed x14 -> x0, local copies, waits for them, and re-layouts: 2.26 us -> none
    ppermute x2, starting transfers between devices: 2.73 us -> 1.79 us  [neighbours(): lax.ppermute(pack, 'blk', [(g + (i + s) % span, g + i) for g, i in ring])]
  transfers between devices with their start and end apart: 17 -> 17, of which waited for: 9 -> 8; matrix products, arithmetic and copies ran while one was open for 4% -> 0% of each run, Pallas kernels for 16% -> 20%
where the time goes in v6:
time: 82 us; the launch traced here: 81.8 us
  starting transfers between devices  30.2 us (37%)
  waiting for transfers between devices  28.9 us (35%)
  Pallas kernels  22.3 us (27%)
    pallas_call x11, Pallas kernels, run_kernel(): pl.pallas_call(kernel, out_shape=[jax.ShapeDtypeStruct(*s) for s in shape...  22.3 us
    ppermute x5, waiting for transfers between devices, tile_pieces(): lax.ppermute(own, 'tile', [((i + s) % tiles, i) for i in range(tiles)])  20.4 us
    ppermute x2, starting transfers between devices, moved(): return lax.ppermute(tokens, both, [(home(*p), worker(*p)) for p in places])  9.25 us
    ppermute x1, starting transfers between devices, body(): back = lax.ppermute(window, both, [(worker(*p), home(*p)) for p in places])  6.38 us
    ppermute x5, starting transfers between devices, tile_pieces(): lax.ppermute(own, 'tile', [((i + s) % tiles, i) for i in range(tiles)])  6.12 us
    ppermute x1, waiting for transfers between devices, body(): lax.ppermute(window[:1], both, [(worker(b, p), home(b - 1, p)) for b, p i...  4.46 us
    ppermute x1, starting transfers between devices, body(): lax.ppermute(window[:1], both, [(worker(b, p), home(b - 1, p)) for b, p i...  2.73 us
    ppermute x5, starting transfers between devices, across(): lax.ppermute(pack, 'pair', [((i + s) % cores, i) for i in range(cores)])  2.31 us
  transfers between devices with their start and end apart: 17, of which 8 were waited for; matrix products, arithmetic and copies ran while one was open for 0% of the time, Pallas kernels for 20%

profile of v6, /device:TPU:1, one launch (start us, length us, event | category | flops | bytes accessed | tf_op | source)
XLA Modules:
  0.0 81.8 jit_solution(8102879338603292714)
XLA Ops:
  0.0 2.0 %collective-permute-start.2 = (bf16[384,384]{1,0:T(8,128)(2,1)}, bf16[384,384]{1,0:T(8,128)(2,1)S(1)}, u32[]{:S(2)}, u32[]{:S(2)}) collective-permute-start(bf16[384,384]{1,0:T(8,128)(2,1)} %bitcast.10), channel_id=1, source_target_pairs={{2,0},{0,2},{3,1},{1,3},{6,4},{4,6},{7,5},{5,7},{10,8},{8,10},{11,... | collective-permute-start | bytes 884744 | tf_op jit(solution)/shard_map/ppermute | solution.py:242
  2.0 5.0 %collective-permute-start = (bf16[384,384]{1,0:T(8,128)(2,1)}, bf16[384,384]{1,0:T(8,128)(2,1)S(1)}, u32[]{:S(2)}, u32[]{:S(2)}) collective-permute-start(bf16[384,384]{1,0:T(8,128)(2,1)} %bitcast.12), channel_id=1, source_target_pairs={{0,0},{1,8},{4,4},{5,12},{8,1},{9,9},{12,5},{13,13},{2,2},{3,10},{... | collective-permute-start | bytes 884744 | tf_op jit(solution)/shard_map/ppermute | solution.py:264
  7.2 3.2 %stage.1 = (bf16[256,768]{1,0:T(8,128)(2,1)S(1)}, bf16[256,768]{1,0:T(8,128)(2,1)S(1)}, bf16[384,256]{1,0:T(8,128)(2,1)S(1)}, bf16[384,384]{1,0:T(8,128)(2,1)S(1...) custom-call(s32[2]{0:T(128)S(1)} %pad_add_fusion.place, ...), custom_call_target="tpu_custom_call" | custom-call | tf_op jit(solution)/shard_map/stage/pallas_call | solution.py:24
  10.4 1.4 %project.3 = bf16[384,512]{1,0:T(8,128)(2,1)S(1)} custom-call(s32[2]{0:T(128)S(1)} %pad_add_fusion.place, bf16[384,384]{1,0:T(8,128)(2,1)S(1)} %get-tuple-element.40.refs_0_, bf16[384,384]{1,0:T(8,128)(2,1)S(1)} %collective-permute-done.2.refs_1_, bf16[3,2,384,256]{3,2,1,0:T(8,128)(2,1)S(1)} %bitcast.7), custom_call_target="tpu_custom_call" | custom-call | tf_op jit(solution)/shard_map/project/pallas_call | solution.py:24
  11.8 4.2 %collective-permute-start.3 = (bf16[384,512]{1,0:T(8,128)(2,1)S(1)}, bf16[384,512]{1,0:T(8,128)(2,1)S(1)}, u32[]{:S(2)}, u32[]{:S(2)}) collective-permute-start(bf16[384,512]{1,0:T(8,128)(2,1)S(1)} %project.3), channel_id=1, source_target_pairs={{0,0},{1,8},{4,4},{5,12},{8,1},{9,9},{12,5},{13,13},{2,2},{3,10},{... | collective-permute-start | bytes 1179656 | tf_op jit(solution)/shard_map/ppermute | solution.py:264
  17.5 7.6 %collective-permute-done.1.refs_1_.refs_5_ = bf16[384,384]{1,0:T(8,128)(2,1)S(1)} collective-permute-done((bf16[384,384]{1,0:T(8,128)(2,1)S(1)}, bf16[384,384]{1,0:T(8,128)(2,1)S(1)}, u32[]{:S(2)}, u32[]{:S(2)}) %collective-permute-start.1) | collective-permute-done | bytes 294944 | tf_op jit(solution)/shard_map/ppermute | solution.py:242
  25.1 1.6 %project.2 = (bf16[384,256]{1,0:T(8,128)(2,1)S(1)}, bf16[384,512]{1,0:T(8,128)(2,1)S(1)}) custom-call(s32[2]{0:T(128)S(1)} %pad_add_fusion.place, bf16[384,384]{1,0:T(8,128)(2,1)S(1)} %collective-permute-done.refs_0_.refs_4_, bf16[384,384]{1,0:T(8,128)(2,1)S(1)} %collective-permute-done.1.refs_1_.refs_5_, bf16[3,2,384,256]{3,2,1,0:T(8,128)(2,1)S(1)} %bitcast.9), custom_call_target="tpu_custom_call" | custom-call | tf_op jit(solution)/shard_map/project/pallas_call | solution.py:24
  26.8 1.4 %collective-permute-start.4 = (bf16[384,512]{1,0:T(8,128)(2,1)S(1)}, bf16[384,512]{1,0:T(8,128)(2,1)S(1)}, u32[]{:S(2)}, u32[]{:S(2)}) collective-permute-start(bf16[384,512]{1,0:T(8,128)(2,1)S(1)} %get-tuple-element.45.refs_0_), channel_id=1, source_target_pairs={{4,0},{0,4},{12,8},{8,12},{5,1},{1,5},{13,9},{9,13},{6,2},{2,6},{1... | collective-permute-start | bytes 1179656 | tf_op jit(solution)/shard_map/ppermute | solution.py:250
  28.1 4.0 %collective-permute-done.5.refs_0_ = bf16[320,768]{1,0:T(8,128)(2,1)S(1)} collective-permute-done((bf16[320,768]{1,0:T(8,128)(2,1)S(1)}, bf16[320,768]{1,0:T(8,128)(2,1)S(1)}, u32[]{:S(2)}, u32[]{:S(2)}) %collective-permute-start.5) | collective-permute-done | bytes 491552 | tf_op jit(solution)/shard_map/ppermute | solution.py:242
  32.1 2.3 %collective-permute-done.4.refs_1_ = bf16[384,512]{1,0:T(8,128)(2,1)S(1)} collective-permute-done((bf16[384,512]{1,0:T(8,128)(2,1)S(1)}, bf16[384,512]{1,0:T(8,128)(2,1)S(1)}, u32[]{:S(2)}, u32[]{:S(2)}) %collective-permute-start.4) | collective-permute-done | bytes 393248 | tf_op jit(solution)/shard_map/ppermute | solution.py:250
  36.8 2.3 %attend.4 = (f32[4,384,64]{2,1,0:T(8,128)S(1)}, f32[4,384,2]{2,1,0:T(8,128)S(1)}) custom-call(bf16[384,256]{1,0:T(8,128)(2,1)S(1)} %get-tuple-element.38.query, bf16[384,512]{1,0:T(8,128)(2,1)S(1)} %get-tuple-element.45.refs_0_, bf16[384,512]{1,0:T(8,128)(2,1)S(1)} %collective-permute-done.4.refs_1_), custom_call_target="tpu_custom_call" | custom-call | tf_op jit(solution)/shard_map/attend/pallas_call | solution.py:24
  39.6 3.1 %attend.5.refs_0_ = bf16[384,256]{1,0:T(8,128)(2,1)S(1)} custom-call(bf16[384,256]{1,0:T(8,128)(2,1)S(1)} %get-tuple-element.38.query, bf16[384,512]{1,0:T(8,128)(2,1)S(1)} %collective-permute-done.6.refs_0_, bf16[384,512]{1,0:T(8,128)(2,1)S(1)} %collective-permute-done.7.refs_1_, f32[4,384,64]{2,1,0:T(8,128)S(1)} %get-tuple-element.50.refs_2_, ...), custom_call_target="tpu_custom_call" | custom-call | tf_op jit(solution)/shard_map/attend/pallas_call | solution.py:24
  42.7 1.3 %collective-permute-start.8 = (bf16[384,256]{1,0:T(8,128)(2,1)S(1)}, bf16[384,256]{1,0:T(8,128)(2,1)S(1)}, u32[]{:S(2)}, u32[]{:S(2)}) collective-permute-start(bf16[384,256]{1,0:T(8,128)(2,1)S(1)} %attend.5.refs_0_), channel_id=1, source_target_pairs={{2,0},{0,2},{3,1},{1,3},{6,4},{4,6},{7,5},{5,7},{10,8},{8,10},{11,... | collective-permute-start | bytes 589832 | tf_op jit(solution)/shard_map/ppermute | solution.py:242
  44.6 4.0 %collective-permute-done.8.refs_1_ = bf16[384,256]{1,0:T(8,128)(2,1)S(1)} collective-permute-done((bf16[384,256]{1,0:T(8,128)(2,1)S(1)}, bf16[384,256]{1,0:T(8,128)(2,1)S(1)}, u32[]{:S(2)}, u32[]{:S(2)}) %collective-permute-start.8) | collective-permute-done | bytes 196640 | tf_op jit(solution)/shard_map/ppermute | solution.py:242
  48.5 2.0 %update.1 = (bf16[2,384,384]{2,1,0:T(8,128)(2,1)S(1)}, bf16[384,256]{1,0:T(8,128)(2,1)S(1)}) custom-call(s32[2]{0:T(128)S(1)} %pad_add_fusion.place, bf16[384,256]{1,0:T(8,128)(2,1)S(1)} %attend.5.refs_0_, bf16[384,256]{1,0:T(8,128)(2,1)S(1)} %collective-permute-done.8.refs_1_, bf16[256,768]{1,0:T(8,128)(2,1)S(1)} %get-tuple-element.52.refs_2_, ...), custom_call_target="tpu_custom_call" | custom-call | tf_op jit(solution)/shard_map/update/pallas_call | solution.py:24
  50.6 1.6 %collective-permute-start.11 = (bf16[384,512]{1,0:T(8,128)(2,1)S(1)}, bf16[384,512]{1,0:T(8,128)(2,1)S(1)}, u32[]{:S(2)}, u32[]{:S(2)}) collective-permute-start(bf16[384,512]{1,0:T(8,128)(2,1)S(1)} %collective-permute-done.3.refs_0_), channel_id=1, source_target_pairs={{1,0},{0,1},{3,2},{2,3},{5,4},{4,5},{7,6},{6,7},{9,8},{8,9},{11,10... | collective-permute-start | bytes 1179656 | tf_op jit(solution)/shard_map/ppermute | solution.py:256
  52.2 2.3 %attend.6 = (f32[4,384,64]{2,1,0:T(8,128)S(1)}, f32[4,384,2]{2,1,0:T(8,128)S(1)}) custom-call(bf16[384,256]{1,0:T(8,128)(2,1)S(1)} %get-tuple-element.55.query, bf16[384,512]{1,0:T(8,128)(2,1)S(1)} %collective-permute-done.3.refs_0_, bf16[384,512]{1,0:T(8,128)(2,1)S(1)} %collective-permute-done.10.refs_1_), custom_call_target="tpu_custom_call" | custom-call | tf_op jit(solution)/shard_map/attend/pallas_call | solution.py:24
  54.6 3.1 %attend.7.refs_0_ = bf16[384,256]{1,0:T(8,128)(2,1)S(1)} custom-call(bf16[384,256]{1,0:T(8,128)(2,1)S(1)} %get-tuple-element.55.query, bf16[384,512]{1,0:T(8,128)(2,1)S(1)} %collective-permute-done.11.refs_0_, bf16[384,512]{1,0:T(8,128)(2,1)S(1)} %collective-permute-done.12.refs_1_, f32[4,384,64]{2,1,0:T(8,128)S(1)} %get-tuple-element.60.refs_2_, ...), custom_call_target="tpu_custom_call" | custom-call | tf_op jit(solution)/shard_map/attend/pallas_call | solution.py:24
  58.9 4.8 %collective-permute-done.13.refs_1_ = bf16[384,256]{1,0:T(8,128)(2,1)S(1)} collective-permute-done((bf16[384,256]{1,0:T(8,128)(2,1)S(1)}, bf16[384,256]{1,0:T(8,128)(2,1)S(1)}, u32[]{:S(2)}, u32[]{:S(2)}) %collective-permute-start.13) | collective-permute-done | bytes 196640 | tf_op jit(solution)/shard_map/ppermute | solution.py:242
  63.8 1.6 %finish.1 = bf16[3,96,256]{2,1,0:T(8,128)(2,1)S(1)} custom-call(s32[2]{0:T(128)S(1)} %pad_add_fusion.place, bf16[384,256]{1,0:T(8,128)(2,1)S(1)} %attend.7.refs_0_, bf16[384,256]{1,0:T(8,128)(2,1)S(1)} %collective-permute-done.13.refs_1_, bf16[256,768]{1,0:T(8,128)(2,1)S(1)} %get-tuple-element.64.refs_2_, bf16[256,768]{1,0:T(8,128)(2,1)S(1)} %get-tuple-element.65.refs_3_, ...), custom_call_target="tpu_custom_call" | custom-call | tf_op jit(solution)/shard_map/finish/pallas_call | solution.py:24
  65.4 6.4 %collective-permute-start.14 = (bf16[3,96,256]{2,1,0:T(8,128)(2,1)S(1)}, bf16[3,96,256]{2,1,0:T(8,128)(2,1)S(1)}, u32[]{:S(2)}, u32[]{:S(2)}) collective-permute-start(bf16[3,96,256]{2,1,0:T(8,128)(2,1)S(1)} %finish.1), channel_id=1, source_target_pairs={{0,0},{8,1},{4,4},{12,5},{1,8},{9,9},{5,12},{13,13},{2,2},{10,3},{... | collective-permute-start | bytes 442376 | tf_op jit(solution)/shard_map/ppermute | solution.py:369
  71.8 1.7 %collective-permute-start.15 = (bf16[1,96,256]{2,1,0:T(8,128)(2,1)S(1)}, bf16[1,96,256]{2,1,0:T(8,128)(2,1)S(1)}, u32[]{:S(2)}, u32[]{:S(2)}) collective-permute-start(bf16[1,96,256]{2,1,0:T(8,128)(2,1)S(1)} %get-tuple-element.70), channel_id=1, source_target_pairs={{0,4},{8,5},{4,8},{12,9},{1,12},{9,13},{2,6},{10,7},{6,10},{14,11}... | collective-permute-start | bytes 147464 | tf_op jit(solution)/shard_map/ppermute | solution.py:370
  73.5 2.7 %collective-permute-start.16 = (bf16[1,96,256]{2,1,0:T(8,128)(2,1)S(1)}, bf16[1,96,256]{2,1,0:T(8,128)(2,1)S(1)}, u32[]{:S(2)}, u32[]{:S(2)}) collective-permute-start(bf16[1,96,256]{2,1,0:T(8,128)(2,1)S(1)} %get-tuple-element.69), channel_id=1, source_target_pairs={{4,0},{12,1},{1,4},{9,5},{5,8},{13,9},{6,2},{14,3},{3,6},{11,7},{7... | collective-permute-start | bytes 147464 | tf_op jit(solution)/shard_map/ppermute | solution.py:373
  76.3 4.5 %collective-permute-done.16.below = bf16[1,96,256]{2,1,0:T(8,128)(2,1)S(1)} collective-permute-done((bf16[1,96,256]{2,1,0:T(8,128)(2,1)S(1)}, bf16[1,96,256]{2,1,0:T(8,128)(2,1)S(1)}, u32[]{:S(2)}, u32[]{:S(2)}) %collective-permute-start.16) | collective-permute-done | bytes 49184 | tf_op jit(solution)/shard_map/ppermute | solution.py:373
  (23 shorter events, 7.5 us)
Async XLA Ops:
  0.0 10.4 %collective-permute-start.2 = (bf16[384,384]{1,0:T(8,128)(2,1)}, bf16[384,384]{1,0:T(8,128)(2,1)S(1)}, u32[]{:S(2)}, u32[]{:S(2)}) collective-permute-start(bf16[384,384]{1,0:T(8,128)(2,1)} %bitcast.10), channel_id=1, source_target_pairs={{2,0},{0,2},{3,1},{1,3},{6,4},{4,6},{7,5},{5,7},{10,8},{8,10},{11,... | collective-permute-start | bytes 884744 | tf_op jit(solution)/shard_map/ppermute | solution.py:242
  2.0 13.9 %collective-permute-start = (bf16[384,384]{1,0:T(8,128)(2,1)}, bf16[384,384]{1,0:T(8,128)(2,1)S(1)}, u32[]{:S(2)}, u32[]{:S(2)}) collective-permute-start(bf16[384,384]{1,0:T(8,128)(2,1)} %bitcast.12), channel_id=1, source_target_pairs={{0,0},{1,8},{4,4},{5,12},{8,1},{9,9},{12,5},{13,13},{2,2},{3,10},{... | collective-permute-start | bytes 884744 | tf_op jit(solution)/shard_map/ppermute | solution.py:264
  11.8 15.0 %collective-permute-start.3 = (bf16[384,512]{1,0:T(8,128)(2,1)S(1)}, bf16[384,512]{1,0:T(8,128)(2,1)S(1)}, u32[]{:S(2)}, u32[]{:S(2)}) collective-permute-start(bf16[384,512]{1,0:T(8,128)(2,1)S(1)} %project.3), channel_id=1, source_target_pairs={{0,0},{1,8},{4,4},{5,12},{8,1},{9,9},{12,5},{13,13},{2,2},{3,10},{... | collective-permute-start | bytes 1179656 | tf_op jit(solution)/shard_map/ppermute | solution.py:264
  16.0 9.2 %collective-permute-start.1 = (bf16[384,384]{1,0:T(8,128)(2,1)S(1)}, bf16[384,384]{1,0:T(8,128)(2,1)S(1)}, u32[]{:S(2)}, u32[]{:S(2)}) collective-permute-start(bf16[384,384]{1,0:T(8,128)(2,1)S(1)} %collective-permute-done.refs_0_.refs_4_), channel_id=1, source_target_pairs={{2,0},{0,2},{3,1},{1,3},{6,4},{4,6},{7,5},{5,7},{10,8},{8,10},{11,... | collective-permute-start | bytes 884744 | tf_op jit(solution)/shard_map/ppermute | solution.py:242
  17.3 14.8 %collective-permute-start.5 = (bf16[320,768]{1,0:T(8,128)(2,1)S(1)}, bf16[320,768]{1,0:T(8,128)(2,1)S(1)}, u32[]{:S(2)}, u32[]{:S(2)}) collective-permute-start(bf16[320,768]{1,0:T(8,128)(2,1)S(1)} %get-tuple-element.44), channel_id=1, source_target_pairs={{2,0},{0,2},{3,1},{1,3},{6,4},{4,6},{7,5},{5,7},{10,8},{8,10},{11,... | collective-permute-start | bytes 1474568 | tf_op jit(solution)/shard_map/ppermute | solution.py:242
  26.8 7.6 %collective-permute-start.4 = (bf16[384,512]{1,0:T(8,128)(2,1)S(1)}, bf16[384,512]{1,0:T(8,128)(2,1)S(1)}, u32[]{:S(2)}, u32[]{:S(2)}) collective-permute-start(bf16[384,512]{1,0:T(8,128)(2,1)S(1)} %get-tuple-element.45.refs_0_), channel_id=1, source_target_pairs={{4,0},{0,4},{12,8},{8,12},{5,1},{1,5},{13,9},{9,13},{6,2},{2,6},{1... | collective-permute-start | bytes 1179656 | tf_op jit(solution)/shard_map/ppermute | solution.py:250
  34.4 1.7 %collective-permute-start.6 = (bf16[384,512]{1,0:T(8,128)(2,1)S(1)}, bf16[384,512]{1,0:T(8,128)(2,1)S(1)}, u32[]{:S(2)}, u32[]{:S(2)}) collective-permute-start(bf16[384,512]{1,0:T(8,128)(2,1)S(1)} %get-tuple-element.45.refs_0_), channel_id=1, source_target_pairs={{1,0},{0,1},{3,2},{2,3},{5,4},{4,5},{7,6},{6,7},{9,8},{8,9},{11,10... | collective-permute-start | bytes 1179656 | tf_op jit(solution)/shard_map/ppermute | solution.py:256
  34.4 2.3 %collective-permute-start.7 = (bf16[384,512]{1,0:T(8,128)(2,1)S(1)}, bf16[384,512]{1,0:T(8,128)(2,1)S(1)}, u32[]{:S(2)}, u32[]{:S(2)}) collective-permute-start(bf16[384,512]{1,0:T(8,128)(2,1)S(1)} %collective-permute-done.4.refs_1_), channel_id=1, source_target_pairs={{1,0},{0,1},{3,2},{2,3},{5,4},{4,5},{7,6},{6,7},{9,8},{8,9},{11,10... | collective-permute-start | bytes 1179656 | tf_op jit(solution)/shard_map/ppermute | solution.py:256
  36.7 7.3 %collective-permute-start.9 = (bf16[320,768]{1,0:T(8,128)(2,1)S(1)}, bf16[320,768]{1,0:T(8,128)(2,1)S(1)}, u32[]{:S(2)}, u32[]{:S(2)}) collective-permute-start(bf16[320,768]{1,0:T(8,128)(2,1)S(1)} %collective-permute-done.5.refs_0_), channel_id=1, source_target_pairs={{1,0},{0,1},{3,2},{2,3},{5,4},{4,5},{7,6},{6,7},{9,8},{8,9},{11,10... | collective-permute-start | bytes 1474568 | tf_op jit(solution)/shard_map/ppermute | solution.py:256
  39.1 11.4 %collective-permute-start.10 = (bf16[384,512]{1,0:T(8,128)(2,1)S(1)}, bf16[384,512]{1,0:T(8,128)(2,1)S(1)}, u32[]{:S(2)}, u32[]{:S(2)}) collective-permute-start(bf16[384,512]{1,0:T(8,128)(2,1)S(1)} %collective-permute-done.3.refs_0_), channel_id=1, source_target_pairs={{4,0},{0,4},{12,8},{8,12},{5,1},{1,5},{13,9},{9,13},{6,2},{2,6},{1... | collective-permute-start | bytes 1179656 | tf_op jit(solution)/shard_map/ppermute | solution.py:250
  42.7 5.9 %collective-permute-start.8 = (bf16[384,256]{1,0:T(8,128)(2,1)S(1)}, bf16[384,256]{1,0:T(8,128)(2,1)S(1)}, u32[]{:S(2)}, u32[]{:S(2)}) collective-permute-start(bf16[384,256]{1,0:T(8,128)(2,1)S(1)} %attend.5.refs_0_), channel_id=1, source_target_pairs={{2,0},{0,2},{3,1},{1,3},{6,4},{4,6},{7,5},{5,7},{10,8},{8,10},{11,... | collective-permute-start | bytes 589832 | tf_op jit(solution)/shard_map/ppermute | solution.py:242
  50.6 4.0 %collective-permute-start.11 = (bf16[384,512]{1,0:T(8,128)(2,1)S(1)}, bf16[384,512]{1,0:T(8,128)(2,1)S(1)}, u32[]{:S(2)}, u32[]{:S(2)}) collective-permute-start(bf16[384,512]{1,0:T(8,128)(2,1)S(1)} %collective-permute-done.3.refs_0_), channel_id=1, source_target_pairs={{1,0},{0,1},{3,2},{2,3},{5,4},{4,5},{7,6},{6,7},{9,8},{8,9},{11,10... | collective-permute-start | bytes 1179656 | tf_op jit(solution)/shard_map/ppermute | solution.py:256
  52.1 2.4 %collective-permute-start.12 = (bf16[384,512]{1,0:T(8,128)(2,1)S(1)}, bf16[384,512]{1,0:T(8,128)(2,1)S(1)}, u32[]{:S(2)}, u32[]{:S(2)}) collective-permute-start(bf16[384,512]{1,0:T(8,128)(2,1)S(1)} %collective-permute-done.10.refs_1_), channel_id=1, source_target_pairs={{1,0},{0,1},{3,2},{2,3},{5,4},{4,5},{7,6},{6,7},{9,8},{8,9},{11,10... | collective-permute-start | bytes 1179656 | tf_op jit(solution)/shard_map/ppermute | solution.py:256
  57.7 6.1 %collective-permute-start.13 = (bf16[384,256]{1,0:T(8,128)(2,1)S(1)}, bf16[384,256]{1,0:T(8,128)(2,1)S(1)}, u32[]{:S(2)}, u32[]{:S(2)}) collective-permute-start(bf16[384,256]{1,0:T(8,128)(2,1)S(1)} %attend.7.refs_0_), channel_id=1, source_target_pairs={{2,0},{0,2},{3,1},{1,3},{6,4},{4,6},{7,5},{5,7},{10,8},{8,10},{11,... | collective-permute-start | bytes 589832 | tf_op jit(solution)/shard_map/ppermute | solution.py:242
  65.4 15.3 %collective-permute-start.14 = (bf16[3,96,256]{2,1,0:T(8,128)(2,1)S(1)}, bf16[3,96,256]{2,1,0:T(8,128)(2,1)S(1)}, u32[]{:S(2)}, u32[]{:S(2)}) collective-permute-start(bf16[3,96,256]{2,1,0:T(8,128)(2,1)S(1)} %finish.1), channel_id=1, source_target_pairs={{0,0},{8,1},{4,4},{12,5},{1,8},{9,9},{5,12},{13,13},{2,2},{10,3},{... | collective-permute-start | bytes 442376 | tf_op jit(solution)/shard_map/ppermute | solution.py:369
  71.8 4.4 %collective-permute-start.15 = (bf16[1,96,256]{2,1,0:T(8,128)(2,1)S(1)}, bf16[1,96,256]{2,1,0:T(8,128)(2,1)S(1)}, u32[]{:S(2)}, u32[]{:S(2)}) collective-permute-start(bf16[1,96,256]{2,1,0:T(8,128)(2,1)S(1)} %get-tuple-element.70), channel_id=1, source_target_pairs={{0,4},{8,5},{4,8},{12,9},{1,12},{9,13},{2,6},{10,7},{6,10},{14,11}... | collective-permute-start | bytes 147464 | tf_op jit(solution)/shard_map/ppermute | solution.py:370
  73.5 7.2 %collective-permute-start.16 = (bf16[1,96,256]{2,1,0:T(8,128)(2,1)S(1)}, bf16[1,96,256]{2,1,0:T(8,128)(2,1)S(1)}, u32[]{:S(2)}, u32[]{:S(2)}) collective-permute-start(bf16[1,96,256]{2,1,0:T(8,128)(2,1)S(1)} %get-tuple-element.69), channel_id=1, source_target_pairs={{4,0},{12,1},{1,4},{9,5},{5,8},{13,9},{6,2},{14,3},{3,6},{11,7},{7... | collective-permute-start | bytes 147464 | tf_op jit(solution)/shard_map/ppermute | solution.py:373

commit v7 on v4

v7 whole, which is shorter than its diff:
```python
import functools
import math

import jax
import jax.numpy as jnp
from jax import lax
from jax.experimental import pallas as pl
from jax.experimental.pallas import tpu as pltpu
from jax.sharding import PartitionSpec as P

HD = 64
GRID_W = 128
EDGE = 16
F32 = jnp.float32
BF16 = jnp.bfloat16
QUERY_SCALE = math.log2(math.e) * HD**-0.5
VMEM = pl.BlockSpec(memory_space=pltpu.VMEM)
HBM = pl.BlockSpec(memory_space=pl.ANY)


def run_kernel(kernel, name, shapes, operands, scratch=(), space=VMEM):
    return pl.pallas_call(
        kernel,
        out_shape=[jax.ShapeDtypeStruct(*s) for s in shapes],
        in_specs=[space] * len(operands),
        out_specs=[VMEM] * len(shapes),
        scratch_shapes=scratch,
        compiler_params=pltpu.CompilerParams(vmem_limit_bytes=24 << 20),
        cost_estimate=pl.CostEstimate(flops=0, bytes_accessed=0, transcendentals=0),
        name=name,
    )(*operands)


def slot_of(step, count):
    return lax.rem(lax.axis_index("tile") + step, count)


def normalized(pieces):
    widened = [piece.astype(F32) for piece in pieces]
    width = sum(piece.shape[1] for piece in widened)
    mean = sum(jnp.sum(piece, axis=1, keepdims=True) for piece in widened) / width
    centred = [piece - mean for piece in widened]
    variance = sum(jnp.sum(piece * piece, axis=1, keepdims=True) for piece in centred) / width
    scale = lax.rsqrt(variance + 1e-06)
    return [(piece * scale).astype(BF16) for piece in centred]


def dot(left, right):
    return jnp.dot(left, right, preferred_element_type=F32)


def project_kernel(*refs, count, scaled, first):
    pieces, weight, outs = refs[:count], refs[count], refs[count + 1 :]
    normed = normalized([piece[...] for piece in pieces])
    products = []
    for which in range(first, weight.shape[0]):
        products.append(
            sum(dot(normed[step], weight[which, slot_of(step, count)]) for step in range(count))
        )
    if scaled:
        outs[0][...] = (products.pop(0) * QUERY_SCALE).astype(BF16)
    columns = weight.shape[3]
    for which, product in enumerate(products):
        outs[-1][:, which * columns : (which + 1) * columns] = product.astype(BF16)


def attended(query, packs, state, index):
    columns = query.shape[1]
    start = index * HD
    head = slice(start, start + HD)
    values = slice(columns + start, columns + start + HD)
    asked = query[:, head]
    scores = [
        lax.dot_general(asked, pack[:, head], (((1,), (1,)), ((), ())), preferred_element_type=F32)
        for pack in packs
    ]
    tops = [jnp.max(score, axis=1, keepdims=True) for score in scores]
    total, mixed = 0.0, 0.0
    if state:
        before, stats = state[0][index], state[1][index]
        tops.append(stats[:, :1])
    maxima = functools.reduce(jnp.maximum, tops)
    if state:
        correction = jnp.exp2(stats[:, :1] - maxima)
        total = stats[:, 1:2] * correction
        mixed = before * correction
    for score, pack in zip(scores, packs):
        expanded = jnp.exp2(score - maxima)
        total = total + jnp.sum(expanded, axis=1, keepdims=True)
        mixed = mixed + dot(expanded.astype(BF16), pack[:, values])
    return mixed, maxima, total


def begin_kernel(query, *refs):
    packs, (mixed_out, stats_out) = refs[:-2], refs[-2:]
    for index in range(query.shape[1] // HD):
        mixed, maxima, total = attended(query, packs, (), index)
        mixed_out[index] = mixed
        stats_out[index] = jnp.concatenate([maxima, total], axis=1)


def ended(query, packs, state):
    heads = []
    for index in range(query.shape[1] // HD):
        mixed, maxima, total = attended(query, packs, state, index)
        heads.append(mixed / total)
    return jnp.concatenate(heads, axis=1).astype(BF16)


def end_kernel(query, *refs):
    refs[-1][...] = ended(query, refs[:-3], refs[-3:-1])


def fill_board(board, values):
    band_rows, channels = board.shape[0], board.shape[2]
    edge = jnp.zeros((band_rows, EDGE, channels), board.dtype)
    board[:, :EDGE, :] = edge
    board[:, EDGE + GRID_W :, :] = edge
    inner = values.reshape(band_rows, GRID_W, channels)
    board[:, EDGE : EDGE + GRID_W, :] = inner.astype(board.dtype)


def window_of(board, slot, out):
    start = pl.multiple_of(slot * (out.shape[1] - 2 * EDGE), EDGE)
    out[...] = board[:, pl.ds(start, out.shape[1]), :]


def end_map_kernel(query, *refs, count):
    composed, outs, board = refs[-2 - count], refs[-1 - count : -1], refs[-1]
    packs, state = refs[: -4 - count], refs[-4 - count : -2 - count]
    fill_board(board, dot(ended(query, packs, state), composed[...]))
    for step, out in enumerate(outs):
        window_of(board, slot_of(count - step, count), out)


def carry_kernel(updated, *refs):
    pieces, out, board = refs[:-2], refs[-2], refs[-1]
    fill_board(board, sum(dot(updated[i], piece[...]) for i, piece in enumerate(pieces)))
    window_of(board, lax.axis_index("tile"), out)


def add_kernel(*refs):
    refs[-1][...] = sum(ref[...].astype(F32) for ref in refs[:-1]).astype(BF16)


def stage_kernel(*refs, cores):
    count = (len(refs) - 2) // 2
    sources, outs, half, sems = refs[:count], refs[count : 2 * count], refs[-2], refs[-1]
    core = lax.axis_index("pair")
    pairs = list(zip(sources, outs))
    rows = sources[0].shape[0] // cores
    begin = pl.multiple_of(core * rows, rows)
    pairs.append((sources[0].at[pl.ds(begin, rows)], half.at[pl.ds(0, rows)]))
    start = rows
    blocks = half.shape[1] // sources[1].shape[1]
    block = sources[1].shape[0] // blocks
    rows = block // cores
    for index in range(blocks):
        begin = pl.multiple_of(core * rows + index * block, rows)
        lanes = pl.ds(index * sources[1].shape[1], sources[1].shape[1])
        pairs.append((sources[1].at[pl.ds(begin, rows)], half.at[pl.ds(start, rows), lanes]))
    copies = [pltpu.make_async_copy(a, b, sems.at[i]) for i, (a, b) in enumerate(pairs)]
    for copy in copies:
        copy.start()
    for copy in copies:
        copy.wait()


def unpack_kernel(*refs):
    halves, outs = refs[:-2], refs[-2:]
    for step, half in enumerate(halves):
        core = lax.rem(lax.axis_index("pair") + step, len(halves))
        rows = outs[0].shape[0] // len(halves)
        outs[0][pl.ds(pl.multiple_of(core * rows, rows), rows), :] = half[:rows, :]
        start = rows
        blocks = half.shape[1] // outs[1].shape[1]
        block = outs[1].shape[0] // blocks
        rows = block // len(halves)
        for index in range(blocks):
            first = pl.multiple_of(core * rows + index * block, rows)
            lanes = slice(index * outs[1].shape[1], (index + 1) * outs[1].shape[1])
            outs[1][pl.ds(first, rows), :] = half[start : start + rows, lanes]


def pick(options, slot):
    chosen = options[0]
    for index in range(1, len(options)):
        chosen = jnp.where(slot == index, options[index], chosen)
    return chosen


def feature_shares(whole, count):
    share = whole.shape[1] // count
    options = [whole[:, i * share : (i + 1) * share] for i in range(count)]
    return [pick(options, slot_of(step, count)) for step in range(count)]


def compose_kernel(weight, *refs):
    pieces, out = refs[:-1], refs[-1]
    shares = feature_shares(weight[...].astype(F32), len(pieces))
    out[...] = sum(dot(s.astype(BF16), p[...]) for s, p in zip(shares, pieces)).astype(BF16)


def update_kernel(*refs, count):
    mixed, weights = refs[:count], refs[count : 2 * count]
    tokens, query_weight = refs[2 * count : 3 * count], refs[3 * count]
    updated, query = refs[3 * count + 1 :]
    whole = sum(dot(m[...], w[...]) for m, w in zip(mixed, weights))
    pieces = []
    for step, term in enumerate(feature_shares(whole, count)):
        piece = (tokens[step][...].astype(F32) + term).astype(BF16)
        updated[step] = piece
        pieces.append(piece)
    normed = normalized(pieces)
    product = sum(
        dot(normed[step], query_weight[0, slot_of(step, count)]) for step in range(count)
    )
    query[...] = (product * QUERY_SCALE).astype(BF16)


def conv_kernel(window, above, below, weight, out):
    width = out.shape[1]
    band_rows, channels = out.shape[0], out.shape[2]
    grid = jnp.concatenate([above[...], window[...], below[...]], axis=0).astype(F32)
    active = jnp.maximum(grid, 0.0)
    total = grid[1 : 1 + band_rows, EDGE : EDGE + width, :].reshape(band_rows * width, channels)
    for column in range(3):
        first = EDGE - 1 + column
        shifted = active[:, first : first + width, :].astype(BF16)
        for row in range(3):
            rows = shifted[row : row + band_rows].reshape(band_rows * width, channels)
            total = total + dot(rows, weight[row, column])
    out[...] = total.reshape(out.shape).astype(BF16)


def body(left_tokens, right_tokens, self_qkv, self_out, cross_qkv, cross_out, reassemble, taps):
    bands, tiles, cores = (lax.axis_size(axis) for axis in ("blk", "tile", "pair"))
    span = bands // cores
    both = ("blk", "pair")
    rows, share = left_tokens.shape[1:]
    columns = self_qkv.shape[2]
    channels = reassemble.shape[1]
    width = GRID_W // tiles
    band_rows = rows // GRID_W
    heads = columns // HD
    window = (band_rows, width + 2 * EDGE, channels)
    board = (band_rows, GRID_W + 2 * EDGE, channels)

    def home(band, pair):
        return band * cores + pair

    def worker(band, pair):
        shift = (pair - band // span) % cores
        return ((band + shift * span) % bands) * cores + (pair - shift) % cores

    places = [(band, pair) for band in range(bands) for pair in range(cores)]
    there = [(home(*p), worker(*p)) for p in places]
    back = [(worker(*p), home(*p)) for p in places]
    down = [(worker(b, p), worker(b + 1, p)) for b, p in places if b + 1 < bands]
    up = [(worker(b, p), worker(b - 1, p)) for b, p in places if b > 0]

    def tied(values, *others):
        return lax.optimization_barrier((values, others))[0]

    def from_tile(value, step):
        return lax.ppermute(value, "tile", [((i + step) % tiles, i) for i in range(tiles)])

    def tile_pieces(own):
        return [own, *[from_tile(own, s) for s in range(1, tiles)]]

    def neighbours(pack):
        ring = [(g * span, i) for g in range(cores) for i in range(span)]
        return [
            lax.ppermute(pack, "blk", [(g + (i + s) % span, g + i) for g, i in ring])
            for s in range(1, span)
        ]

    def across(pack):
        return [
            lax.ppermute(pack, "pair", [((i + s) % cores, i) for i in range(cores)])
            for s in range(1, cores)
        ]

    def grouped(packs):
        return packs if len(packs) < 3 else [jnp.concatenate(packs)]

    def project(pieces, weights, scaled, first):
        return run_kernel(
            functools.partial(project_kernel, count=tiles, scaled=scaled, first=first),
            "project",
            [((rows, columns), BF16)] * scaled + [((rows, 2 * columns), BF16)],
            [*pieces, weights.reshape(3, tiles, share, columns)],
        )

    def begin(query, packs):
        shapes = [((heads, rows, HD), F32), ((heads, rows, 2), F32)]
        return run_kernel(begin_kernel, "begin", shapes, [query, *grouped(packs)])

    def staged(weights):
        blocks = weights[0].shape[1] // channels
        height = (weights[0].shape[0] + share // blocks) // cores
        return run_kernel(
            functools.partial(stage_kernel, cores=cores),
            "stage",
            [(w.shape, BF16) for w in weights] + [((height, weights[0].shape[1]), BF16)],
            [pltpu.with_memory_space_constraint(w, pltpu.HBM) for w in weights],
            [pltpu.SemaphoreType.DMA((len(weights) + 1 + blocks,))],
            pl.BlockSpec(memory_space=pl.ANY),
        )

    left_here = lax.ppermute(left_tokens[0], both, there)
    self_out, reassemble, cross_out, right_own, self_qkv, cross_qkv, taps, half = staged(
        [self_out, reassemble, cross_out, right_tokens[0], self_qkv, cross_qkv, taps]
    )
    left = tile_pieces(left_here)
    right = [right_own, *[from_tile(right_tokens[0], s) for s in range(1, tiles)]]
    (right_pack,) = project(right, cross_qkv, False, 1)
    right_pack = lax.ppermute(right_pack, both, there)
    query, pack = project(left, self_qkv, True, 0)
    beside = neighbours(tied(pack, right_pack))
    halves = tile_pieces(tied(half, left))[1:]
    near, halves = lax.optimization_barrier(([pack, *beside], halves))
    far = [q for p in near for q in across(p)]
    state = begin(query, near)
    right_pack = tied(right_pack, state)
    right_near = [right_pack, *neighbours(right_pack)]
    others = [
        run_kernel(
            unpack_kernel,
            "unpack",
            [(w.shape, BF16) for w in (self_out, reassemble)],
            [half, *across(half)],
        )
        for half in halves
    ]
    (mixed,) = run_kernel(
        end_kernel, "end", [((rows, columns), BF16)], [query, *grouped(far), *state]
    )

    map_weights = [reassemble, *[other[1] for other in others]]
    (composed,) = run_kernel(
        compose_kernel, "compose", [((columns, channels), BF16)], [cross_out, *map_weights]
    )
    mixed, composed = lax.optimization_barrier((tile_pieces(mixed), composed))
    updated, cross_query = run_kernel(
        functools.partial(update_kernel, count=tiles),
        "update",
        [((tiles, rows, share), BF16), ((rows, columns), BF16)],
        [
            *mixed,
            self_out,
            *[other[0] for other in others],
            *left,
            cross_qkv.reshape(3, tiles, share, columns),
        ],
    )
    right_near = tied(right_near, updated)
    right_far = [q for p in right_near for q in across(p)]
    state = begin(cross_query, right_near)
    right_far = tied(right_far, state)
    maps = run_kernel(
        functools.partial(end_map_kernel, count=tiles),
        "end_map",
        [(window, BF16)] * tiles,
        [cross_query, *grouped(right_far), *state, composed],
        [pltpu.VMEM(board, BF16)],
    )
    (carried,) = run_kernel(
        carry_kernel,
        "carry",
        [(window, F32)],
        [tied(updated, maps), *map_weights],
        [pltpu.VMEM(board, F32)],
    )
    received = [from_tile(part, s) for s, part in enumerate(maps) if s > 0]
    (features,) = run_kernel(add_kernel, "add", [(window, BF16)], [carried, maps[0], *received])
    above = lax.ppermute(features[-1:], both, down)
    below = lax.ppermute(features[:1], both, up)
    (joined,) = run_kernel(
        conv_kernel,
        "join",
        [((band_rows, width, channels), BF16)],
        [features, above, below, taps],
    )
    return lax.ppermute(joined, both, back)[None]


def solution(mesh):
    placed = (
        P(("groups", "pair"), "blk", "tile"),
        P(("groups", "pair"), "blk", "tile"),
        P(None, None, "tile"),
        P("tile", None),
        P(None, None, "tile"),
        P("tile", None),
        P("tile", None),
        P(),
    )
    return jax.shard_map(
        body,
        mesh=mesh,
        in_specs=placed,
        out_specs=P(("groups", "pair"), "blk", "tile", None),
        check_vma=False,
    )
```

time: 83.5 us -> 80.2 us (0.960)
  waiting for transfers between devices: 34.1 us -> 26.1 us
  Pallas kernels: 16.3 us -> 19.7 us
  starting transfers between devices: 30.3 us -> 33.3 us
  local copies, waits for them, and re-layouts: 2.24 us -> 0.65 us
    ppermute x14 -> x12, waiting for transfers between devices: 34.1 us -> 26.1 us  [the longest x5 16.6 us: from_tile(): lax.ppermute(value, 'tile', [((i + step) % tiles, i) for i in range(tiles)])]
    pallas_call x9 -> x13, Pallas kernels: 16.3 us -> 19.7 us  [run_kernel(): pl.pallas_call(kernel, out_shape=[jax.ShapeDtypeStruct(*s) for s in shape...]
    ppermute x14 -> x12, starting transfers between devices: 28 us -> 31.2 us  [the longest x1 7.11 us: body(): return lax.ppermute(joined, both, back)[None]]
    slice x3 -> x1, local copies, waits for them, and re-layouts: 2.21 us -> 0.01 us  [body(): below = lax.ppermute(features[:1], both, up)]
    ppermute x4 -> x5, starting transfers between devices: 2.33 us -> 2.06 us  [across(): lax.ppermute(pack, 'pair', [((i + s) % cores, i) for i in range(cores)])]
  transfers between devices with their start and end apart: 18 -> 17, of which waited for: 9 -> 8; matrix products, arithmetic and copies ran while one was open for 3% -> 0% of each run, Pallas kernels for 17% -> 18%
where the time goes in v7:
time: 80.2 us; the launch traced here: 80 us
  starting transfers between devices  33.3 us (42%)
  waiting for transfers between devices  26.1 us (33%)
  Pallas kernels  19.7 us (25%)
    pallas_call x13, Pallas kernels, run_kernel(): pl.pallas_call(kernel, out_shape=[jax.ShapeDtypeStruct(*s) for s in shape...  19.7 us
    ppermute x5, waiting for transfers between devices, from_tile(): lax.ppermute(value, 'tile', [((i + step) % tiles, i) for i in range(tiles)])  16.6 us
    ppermute x1, starting transfers between devices, body(): return lax.ppermute(joined, both, back)[None]  7.11 us
    ppermute x5, starting transfers between devices, from_tile(): lax.ppermute(value, 'tile', [((i + step) % tiles, i) for i in range(tiles)])  7.06 us
    ppermute x1, starting transfers between devices, body(): left_here = lax.ppermute(left_tokens[0], both, there)  5.05 us
    ppermute x1, starting transfers between devices, body(): right_pack = lax.ppermute(right_pack, both, there)  4.9 us
    ppermute x1, starting transfers between devices, body(): above = lax.ppermute(features[-1:], both, down)  3.56 us
    ppermute x1, starting transfers between devices, body(): below = lax.ppermute(features[:1], both, up)  3.08 us
  transfers between devices with their start and end apart: 17, of which 8 were waited for; matrix products, arithmetic and copies ran while one was open for 0% of the time, Pallas kernels for 18%

profile of v7, /device:TPU:1, one launch (start us, length us, event | category | flops | bytes accessed | tf_op | source)
XLA Modules:
  0.0 80.0 jit_solution(17638006944481650969)
XLA Ops:
  0.0 2.0 %collective-permute-start.2 = (bf16[384,384]{1,0:T(8,128)(2,1)}, bf16[384,384]{1,0:T(8,128)(2,1)S(1)}, u32[]{:S(2)}, u32[]{:S(2)}) collective-permute-start(bf16[384,384]{1,0:T(8,128)(2,1)} %bitcast.8), channel_id=1, source_target_pairs={{2,0},{0,2},{3,1},{1,3},{6,4},{4,6},{7,5},{5,7},{10,8},{8,10},{11,... | collective-permute-start | bytes 884744 | tf_op jit(solution)/shard_map/ppermute | solution.py:266
  2.0 5.0 %collective-permute-start = (bf16[384,384]{1,0:T(8,128)(2,1)}, bf16[384,384]{1,0:T(8,128)(2,1)S(1)}, u32[]{:S(2)}, u32[]{:S(2)}) collective-permute-start(bf16[384,384]{1,0:T(8,128)(2,1)} %bitcast.11), channel_id=1, source_target_pairs={{0,0},{1,8},{4,4},{5,12},{8,1},{9,9},{12,5},{13,13},{2,2},{3,10},{... | collective-permute-start | bytes 884744 | tf_op jit(solution)/shard_map/ppermute | solution.py:311
  7.1 2.6 %stage.1 = (bf16[256,768]{1,0:T(8,128)(2,1)S(1)}, bf16[384,256]{1,0:T(8,128)(2,1)S(1)}, bf16[256,768]{1,0:T(8,128)(2,1)S(1)}, bf16[384,384]{1,0:T(8,128)(2,1)S(1...) custom-call(bf16[256,768]{1,0:T(8,128)(2,1)} %refs_0_.1, ...), custom_call_target="tpu_custom_call" | custom-call | tf_op jit(solution)/shard_map/stage/pallas_call | solution.py:22
  10.5 4.9 %collective-permute-start.3 = (bf16[384,512]{1,0:T(8,128)(2,1)S(1)}, bf16[384,512]{1,0:T(8,128)(2,1)S(1)}, u32[]{:S(2)}, u32[]{:S(2)}) collective-permute-start(bf16[384,512]{1,0:T(8,128)(2,1)S(1)} %project.3), channel_id=1, source_target_pairs={{0,0},{1,8},{4,4},{5,12},{8,1},{9,9},{12,5},{13,13},{2,2},{3,10},{... | collective-permute-start | bytes 1179656 | tf_op jit(solution)/shard_map/ppermute | solution.py:318
  15.4 1.3 %collective-permute-start.1 = (bf16[384,384]{1,0:T(8,128)(2,1)S(1)}, bf16[384,384]{1,0:T(8,128)(2,1)S(1)}, u32[]{:S(2)}, u32[]{:S(2)}) collective-permute-start(bf16[384,384]{1,0:T(8,128)(2,1)S(1)} %collective-permute-done.refs_0_.refs_4_), channel_id=1, source_target_pairs={{2,0},{0,2},{3,1},{1,3},{6,4},{4,6},{7,5},{5,7},{10,8},{8,10},{11,... | collective-permute-start | bytes 884744 | tf_op jit(solution)/shard_map/ppermute | solution.py:266
  16.7 4.4 %collective-permute-done.1.refs_1_.refs_5_ = bf16[384,384]{1,0:T(8,128)(2,1)S(1)} collective-permute-done((bf16[384,384]{1,0:T(8,128)(2,1)S(1)}, bf16[384,384]{1,0:T(8,128)(2,1)S(1)}, u32[]{:S(2)}, u32[]{:S(2)}) %collective-permute-start.1) | collective-permute-done | bytes 294944 | tf_op jit(solution)/shard_map/ppermute | solution.py:266
  22.1 3.0 %collective-permute-done.3.refs_0_ = bf16[384,512]{1,0:T(8,128)(2,1)S(1)} collective-permute-done((bf16[384,512]{1,0:T(8,128)(2,1)S(1)}, bf16[384,512]{1,0:T(8,128)(2,1)S(1)}, u32[]{:S(2)}, u32[]{:S(2)}) %collective-permute-start.3) | collective-permute-done | bytes 393248 | tf_op jit(solution)/shard_map/ppermute | solution.py:318
  26.8 4.4 %collective-permute-done.5.refs_0_ = bf16[192,768]{1,0:T(8,128)(2,1)S(1)} collective-permute-done((bf16[192,768]{1,0:T(8,128)(2,1)S(1)}, bf16[192,768]{1,0:T(8,128)(2,1)S(1)}, u32[]{:S(2)}, u32[]{:S(2)}) %collective-permute-start.5) | collective-permute-done | bytes 294944 | tf_op jit(solution)/shard_map/ppermute | solution.py:266
  31.2 2.3 %collective-permute-done.4.refs_1_ = bf16[384,512]{1,0:T(8,128)(2,1)S(1)} collective-permute-done((bf16[384,512]{1,0:T(8,128)(2,1)S(1)}, bf16[384,512]{1,0:T(8,128)(2,1)S(1)}, u32[]{:S(2)}, u32[]{:S(2)}) %collective-permute-start.4) | collective-permute-done | bytes 393248 | tf_op jit(solution)/shard_map/ppermute | solution.py:274
  34.0 2.3 %begin.2 = (f32[4,384,64]{2,1,0:T(8,128)S(1)}, f32[4,384,2]{2,1,0:T(8,128)S(1)}) custom-call(bf16[384,256]{1,0:T(8,128)(2,1)S(1)} %get-tuple-element.40.query, bf16[384,512]{1,0:T(8,128)(2,1)S(1)} %get-tuple-element.47.refs_0_, bf16[384,512]{1,0:T(8,128)(2,1)S(1)} %collective-permute-done.4.refs_1_), custom_call_target="tpu_custom_call" | custom-call | tf_op jit(solution)/shard_map/begin/pallas_call | solution.py:22
  36.5 3.1 %end.1.refs_0_ = bf16[384,256]{1,0:T(8,128)(2,1)S(1)} custom-call(bf16[384,256]{1,0:T(8,128)(2,1)S(1)} %get-tuple-element.40.query, bf16[384,512]{1,0:T(8,128)(2,1)S(1)} %collective-permute-done.6.refs_0_, bf16[384,512]{1,0:T(8,128)(2,1)S(1)} %collective-permute-done.7.refs_1_, f32[4,384,64]{2,1,0:T(8,128)S(1)} %get-tuple-element.49.refs_2_, ...), custom_call_target="tpu_custom_call" | custom-call | tf_op jit(solution)/shard_map/end/pallas_call | solution.py:22
  39.6 1.3 %collective-permute-start.8 = (bf16[384,256]{1,0:T(8,128)(2,1)S(1)}, bf16[384,256]{1,0:T(8,128)(2,1)S(1)}, u32[]{:S(2)}, u32[]{:S(2)}) collective-permute-start(bf16[384,256]{1,0:T(8,128)(2,1)S(1)} %end.1.refs_0_), channel_id=1, source_target_pairs={{2,0},{0,2},{3,1},{1,3},{6,4},{4,6},{7,5},{5,7},{10,8},{8,10},{11,... | collective-permute-start | bytes 589832 | tf_op jit(solution)/shard_map/ppermute | solution.py:266
  41.2 4.4 %collective-permute-done.8.refs_1_ = bf16[384,256]{1,0:T(8,128)(2,1)S(1)} collective-permute-done((bf16[384,256]{1,0:T(8,128)(2,1)S(1)}, bf16[384,256]{1,0:T(8,128)(2,1)S(1)}, u32[]{:S(2)}, u32[]{:S(2)}) %collective-permute-start.8) | collective-permute-done | bytes 196640 | tf_op jit(solution)/shard_map/ppermute | solution.py:266
  45.6 1.5 %update.1 = (bf16[2,384,384]{2,1,0:T(8,128)(2,1)S(1)}, bf16[384,256]{1,0:T(8,128)(2,1)S(1)}) custom-call(bf16[384,256]{1,0:T(8,128)(2,1)S(1)} %end.1.refs_0_, bf16[384,256]{1,0:T(8,128)(2,1)S(1)} %collective-permute-done.8.refs_1_, bf16[256,768]{1,0:T(8,128)(2,1)S(1)} %get-tuple-element.57.refs_2_, bf16[256,768]{1,0:T(8,128)(2,1)S(1)} %get-tuple-element.58.refs_3_, ...), custom_call_target="tpu_custom_call" | custom-call | tf_op jit(solution)/shard_map/update/pallas_call | solution.py:22
  47.1 1.4 %collective-permute-start.11 = (bf16[384,512]{1,0:T(8,128)(2,1)S(1)}, bf16[384,512]{1,0:T(8,128)(2,1)S(1)}, u32[]{:S(2)}, u32[]{:S(2)}) collective-permute-start(bf16[384,512]{1,0:T(8,128)(2,1)S(1)} %collective-permute-done.3.refs_0_), channel_id=1, source_target_pairs={{1,0},{0,1},{3,2},{2,3},{5,4},{4,5},{7,6},{6,7},{9,8},{8,9},{11,10... | collective-permute-start | bytes 1179656 | tf_op jit(solution)/shard_map/ppermute | solution.py:280
  48.6 2.3 %begin.3 = (f32[4,384,64]{2,1,0:T(8,128)S(1)}, f32[4,384,2]{2,1,0:T(8,128)S(1)}) custom-call(bf16[384,256]{1,0:T(8,128)(2,1)S(1)} %get-tuple-element.60.query, bf16[384,512]{1,0:T(8,128)(2,1)S(1)} %collective-permute-done.3.refs_0_, bf16[384,512]{1,0:T(8,128)(2,1)S(1)} %collective-permute-done.10.refs_1_), custom_call_target="tpu_custom_call" | custom-call | tf_op jit(solution)/shard_map/begin/pallas_call | solution.py:22
  50.9 5.0 %end_map.1 = (bf16[3,96,256]{2,1,0:T(8,128)(2,1)S(1)}, bf16[3,96,256]{2,1,0:T(8,128)(2,1)S(1)}) custom-call(bf16[384,256]{1,0:T(8,128)(2,1)S(1)} %get-tuple-element.60.query, bf16[384,512]{1,0:T(8,128)(2,1)S(1)} %collective-permute-done.11.refs_0_, bf16[384,512]{1,0:T(8,128)(2,1)S(1)} %collective-permute-done.12.refs_1_, ...), custom_call_target="tpu_custom_call" | custom-call | tf_op jit(solution)/shard_map/end_map/pallas_call | solution.py:22
  55.9 1.3 %collective-permute-start.13 = (bf16[3,96,256]{2,1,0:T(8,128)(2,1)S(1)}, bf16[3,96,256]{2,1,0:T(8,128)(2,1)S(1)}, u32[]{:S(2)}, u32[]{:S(2)}) collective-permute-start(bf16[3,96,256]{2,1,0:T(8,128)(2,1)S(1)} %get-tuple-element.70), channel_id=1, source_target_pairs={{2,0},{0,2},{3,1},{1,3},{6,4},{4,6},{7,5},{5,7},{10,8},{8,10},{11,... | collective-permute-start | bytes 442376 | tf_op jit(solution)/shard_map/ppermute | solution.py:266
  57.5 3.4 %collective-permute-done.13.refs_2_ = bf16[3,96,256]{2,1,0:T(8,128)(2,1)S(1)} collective-permute-done((bf16[3,96,256]{2,1,0:T(8,128)(2,1)S(1)}, bf16[3,96,256]{2,1,0:T(8,128)(2,1)S(1)}, u32[]{:S(2)}, u32[]{:S(2)}) %collective-permute-start.13) | collective-permute-done | bytes 147488 | tf_op jit(solution)/shard_map/ppermute | solution.py:266
  61.0 3.6 %collective-permute-start.14 = (bf16[1,96,256]{2,1,0:T(8,128)(2,1)S(1)}, bf16[1,96,256]{2,1,0:T(8,128)(2,1)S(1)}, u32[]{:S(2)}, u32[]{:S(2)}) collective-permute-start(bf16[1,96,256]{2,1,0:T(8,128)(2,1)S(1)} %get-tuple-element.74), channel_id=1, source_target_pairs={{0,4},{8,12},{4,1},{12,9},{1,5},{9,13},{2,6},{10,14},{6,3},{14,11}... | collective-permute-start | bytes 147464 | tf_op jit(solution)/shard_map/ppermute | solution.py:377
  64.5 3.1 %collective-permute-start.15 = (bf16[1,96,256]{2,1,0:T(8,128)(2,1)S(1)}, bf16[1,96,256]{2,1,0:T(8,128)(2,1)S(1)}, u32[]{:S(2)}, u32[]{:S(2)}) collective-permute-start(bf16[1,96,256]{2,1,0:T(8,128)(2,1)S(1)} %get-tuple-element.73), channel_id=1, source_target_pairs={{4,0},{12,8},{1,4},{9,12},{5,1},{13,9},{6,2},{14,10},{3,6},{11,14}... | collective-permute-start | bytes 147464 | tf_op jit(solution)/shard_map/ppermute | solution.py:378
  67.6 1.7 %collective-permute-done.15.below = bf16[1,96,256]{2,1,0:T(8,128)(2,1)S(1)} collective-permute-done((bf16[1,96,256]{2,1,0:T(8,128)(2,1)S(1)}, bf16[1,96,256]{2,1,0:T(8,128)(2,1)S(1)}, u32[]{:S(2)}, u32[]{:S(2)}) %collective-permute-start.15) | collective-permute-done | bytes 49184 | tf_op jit(solution)/shard_map/ppermute | solution.py:378
  69.8 7.1 %collective-permute-start.16 = (bf16[3,64,256]{2,1,0:T(8,128)(2,1)S(1)}, bf16[3,64,256]{2,1,0:T(8,128)(2,1)S(1)}, u32[]{:S(2)}, u32[]{:S(2)}) collective-permute-start(bf16[3,64,256]{2,1,0:T(8,128)(2,1)S(1)} %join.1), channel_id=1, source_target_pairs={{0,0},{8,1},{4,4},{12,5},{1,8},{9,9},{5,12},{13,13},{2,2},{10,3},{... | collective-permute-start | bytes 294920 | tf_op jit(solution)/shard_map/ppermute | solution.py:385
  76.9 2.5 %collective-permute-done.16 = bf16[3,64,256]{2,1,0:T(8,128)(2,1)S(1)} collective-permute-done((bf16[3,64,256]{2,1,0:T(8,128)(2,1)S(1)}, bf16[3,64,256]{2,1,0:T(8,128)(2,1)S(1)}, u32[]{:S(2)}, u32[]{:S(2)}) %collective-permute-start.16) | collective-permute-done | bytes 98336 | tf_op jit(solution)/shard_map/ppermute | solution.py:385
  (25 shorter events, 6.1 us)
Async XLA Ops:
  0.0 9.7 %collective-permute-start.2 = (bf16[384,384]{1,0:T(8,128)(2,1)}, bf16[384,384]{1,0:T(8,128)(2,1)S(1)}, u32[]{:S(2)}, u32[]{:S(2)}) collective-permute-start(bf16[384,384]{1,0:T(8,128)(2,1)} %bitcast.8), channel_id=1, source_target_pairs={{2,0},{0,2},{3,1},{1,3},{6,4},{4,6},{7,5},{5,7},{10,8},{8,10},{11,... | collective-permute-start | bytes 884744 | tf_op jit(solution)/shard_map/ppermute | solution.py:266
  2.0 13.4 %collective-permute-start = (bf16[384,384]{1,0:T(8,128)(2,1)}, bf16[384,384]{1,0:T(8,128)(2,1)S(1)}, u32[]{:S(2)}, u32[]{:S(2)}) collective-permute-start(bf16[384,384]{1,0:T(8,128)(2,1)} %bitcast.11), channel_id=1, source_target_pairs={{0,0},{1,8},{4,4},{5,12},{8,1},{9,9},{12,5},{13,13},{2,2},{3,10},{... | collective-permute-start | bytes 884744 | tf_op jit(solution)/shard_map/ppermute | solution.py:311
  10.5 14.7 %collective-permute-start.3 = (bf16[384,512]{1,0:T(8,128)(2,1)S(1)}, bf16[384,512]{1,0:T(8,128)(2,1)S(1)}, u32[]{:S(2)}, u32[]{:S(2)}) collective-permute-start(bf16[384,512]{1,0:T(8,128)(2,1)S(1)} %project.3), channel_id=1, source_target_pairs={{0,0},{1,8},{4,4},{5,12},{8,1},{9,9},{12,5},{13,13},{2,2},{3,10},{... | collective-permute-start | bytes 1179656 | tf_op jit(solution)/shard_map/ppermute | solution.py:318
  15.4 5.6 %collective-permute-start.1 = (bf16[384,384]{1,0:T(8,128)(2,1)S(1)}, bf16[384,384]{1,0:T(8,128)(2,1)S(1)}, u32[]{:S(2)}, u32[]{:S(2)}) collective-permute-start(bf16[384,384]{1,0:T(8,128)(2,1)S(1)} %collective-permute-done.refs_0_.refs_4_), channel_id=1, source_target_pairs={{2,0},{0,2},{3,1},{1,3},{6,4},{4,6},{7,5},{5,7},{10,8},{8,10},{11,... | collective-permute-start | bytes 884744 | tf_op jit(solution)/shard_map/ppermute | solution.py:266
  25.2 8.3 %collective-permute-start.4 = (bf16[384,512]{1,0:T(8,128)(2,1)S(1)}, bf16[384,512]{1,0:T(8,128)(2,1)S(1)}, u32[]{:S(2)}, u32[]{:S(2)}) collective-permute-start(bf16[384,512]{1,0:T(8,128)(2,1)S(1)} %get-tuple-element.47.refs_0_), channel_id=1, source_target_pairs={{4,0},{0,4},{12,8},{8,12},{5,1},{1,5},{13,9},{9,13},{6,2},{2,6},{1... | collective-permute-start | bytes 1179656 | tf_op jit(solution)/shard_map/ppermute | solution.py:274
  25.6 5.6 %collective-permute-start.5 = (bf16[192,768]{1,0:T(8,128)(2,1)S(1)}, bf16[192,768]{1,0:T(8,128)(2,1)S(1)}, u32[]{:S(2)}, u32[]{:S(2)}) collective-permute-start(bf16[192,768]{1,0:T(8,128)(2,1)S(1)} %get-tuple-element.46), channel_id=1, source_target_pairs={{2,0},{0,2},{3,1},{1,3},{6,4},{4,6},{7,5},{5,7},{10,8},{8,10},{11,... | collective-permute-start | bytes 884744 | tf_op jit(solution)/shard_map/ppermute | solution.py:266
  33.5 3.0 %collective-permute-start.6 = (bf16[384,512]{1,0:T(8,128)(2,1)S(1)}, bf16[384,512]{1,0:T(8,128)(2,1)S(1)}, u32[]{:S(2)}, u32[]{:S(2)}) collective-permute-start(bf16[384,512]{1,0:T(8,128)(2,1)S(1)} %get-tuple-element.47.refs_0_), channel_id=1, source_target_pairs={{1,0},{0,1},{3,2},{2,3},{5,4},{4,5},{7,6},{6,7},{9,8},{8,9},{11,10... | collective-permute-start | bytes 1179656 | tf_op jit(solution)/shard_map/ppermute | solution.py:280
  33.5 3.0 %collective-permute-start.7 = (bf16[384,512]{1,0:T(8,128)(2,1)S(1)}, bf16[384,512]{1,0:T(8,128)(2,1)S(1)}, u32[]{:S(2)}, u32[]{:S(2)}) collective-permute-start(bf16[384,512]{1,0:T(8,128)(2,1)S(1)} %collective-permute-done.4.refs_1_), channel_id=1, source_target_pairs={{1,0},{0,1},{3,2},{2,3},{5,4},{4,5},{7,6},{6,7},{9,8},{8,9},{11,10... | collective-permute-start | bytes 1179656 | tf_op jit(solution)/shard_map/ppermute | solution.py:280
  36.3 10.8 %collective-permute-start.10 = (bf16[384,512]{1,0:T(8,128)(2,1)S(1)}, bf16[384,512]{1,0:T(8,128)(2,1)S(1)}, u32[]{:S(2)}, u32[]{:S(2)}) collective-permute-start(bf16[384,512]{1,0:T(8,128)(2,1)S(1)} %collective-permute-done.3.refs_0_), channel_id=1, source_target_pairs={{4,0},{0,4},{12,8},{8,12},{5,1},{1,5},{13,9},{9,13},{6,2},{2,6},{1... | collective-permute-start | bytes 1179656 | tf_op jit(solution)/shard_map/ppermute | solution.py:274
  36.4 4.5 %collective-permute-start.9 = (bf16[192,768]{1,0:T(8,128)(2,1)S(1)}, bf16[192,768]{1,0:T(8,128)(2,1)S(1)}, u32[]{:S(2)}, u32[]{:S(2)}) collective-permute-start(bf16[192,768]{1,0:T(8,128)(2,1)S(1)} %collective-permute-done.5.refs_0_), channel_id=1, source_target_pairs={{1,0},{0,1},{3,2},{2,3},{5,4},{4,5},{7,6},{6,7},{9,8},{8,9},{11,10... | collective-permute-start | bytes 884744 | tf_op jit(solution)/shard_map/ppermute | solution.py:280
  39.6 6.0 %collective-permute-start.8 = (bf16[384,256]{1,0:T(8,128)(2,1)S(1)}, bf16[384,256]{1,0:T(8,128)(2,1)S(1)}, u32[]{:S(2)}, u32[]{:S(2)}) collective-permute-start(bf16[384,256]{1,0:T(8,128)(2,1)S(1)} %end.1.refs_0_), channel_id=1, source_target_pairs={{2,0},{0,2},{3,1},{1,3},{6,4},{4,6},{7,5},{5,7},{10,8},{8,10},{11,... | collective-permute-start | bytes 589832 | tf_op jit(solution)/shard_map/ppermute | solution.py:266
  47.1 3.8 %collective-permute-start.11 = (bf16[384,512]{1,0:T(8,128)(2,1)S(1)}, bf16[384,512]{1,0:T(8,128)(2,1)S(1)}, u32[]{:S(2)}, u32[]{:S(2)}) collective-permute-start(bf16[384,512]{1,0:T(8,128)(2,1)S(1)} %collective-permute-done.3.refs_0_), channel_id=1, source_target_pairs={{1,0},{0,1},{3,2},{2,3},{5,4},{4,5},{7,6},{6,7},{9,8},{8,9},{11,10... | collective-permute-start | bytes 1179656 | tf_op jit(solution)/shard_map/ppermute | solution.py:280
  48.5 2.4 %collective-permute-start.12 = (bf16[384,512]{1,0:T(8,128)(2,1)S(1)}, bf16[384,512]{1,0:T(8,128)(2,1)S(1)}, u32[]{:S(2)}, u32[]{:S(2)}) collective-permute-start(bf16[384,512]{1,0:T(8,128)(2,1)S(1)} %collective-permute-done.10.refs_1_), channel_id=1, source_target_pairs={{1,0},{0,1},{3,2},{2,3},{5,4},{4,5},{7,6},{6,7},{9,8},{8,9},{11,10... | collective-permute-start | bytes 1179656 | tf_op jit(solution)/shard_map/ppermute | solution.py:280
  55.9 5.0 %collective-permute-start.13 = (bf16[3,96,256]{2,1,0:T(8,128)(2,1)S(1)}, bf16[3,96,256]{2,1,0:T(8,128)(2,1)S(1)}, u32[]{:S(2)}, u32[]{:S(2)}) collective-permute-start(bf16[3,96,256]{2,1,0:T(8,128)(2,1)S(1)} %get-tuple-element.70), channel_id=1, source_target_pairs={{2,0},{0,2},{3,1},{1,3},{6,4},{4,6},{7,5},{5,7},{10,8},{8,10},{11,... | collective-permute-start | bytes 442376 | tf_op jit(solution)/shard_map/ppermute | solution.py:266
  61.0 6.7 %collective-permute-start.14 = (bf16[1,96,256]{2,1,0:T(8,128)(2,1)S(1)}, bf16[1,96,256]{2,1,0:T(8,128)(2,1)S(1)}, u32[]{:S(2)}, u32[]{:S(2)}) collective-permute-start(bf16[1,96,256]{2,1,0:T(8,128)(2,1)S(1)} %get-tuple-element.74), channel_id=1, source_target_pairs={{0,4},{8,12},{4,1},{12,9},{1,5},{9,13},{2,6},{10,14},{6,3},{14,11}... | collective-permute-start | bytes 147464 | tf_op jit(solution)/shard_map/ppermute | solution.py:377
  64.5 4.8 %collective-permute-start.15 = (bf16[1,96,256]{2,1,0:T(8,128)(2,1)S(1)}, bf16[1,96,256]{2,1,0:T(8,128)(2,1)S(1)}, u32[]{:S(2)}, u32[]{:S(2)}) collective-permute-start(bf16[1,96,256]{2,1,0:T(8,128)(2,1)S(1)} %get-tuple-element.73), channel_id=1, source_target_pairs={{4,0},{12,8},{1,4},{9,12},{5,1},{13,9},{6,2},{14,10},{3,6},{11,14}... | collective-permute-start | bytes 147464 | tf_op jit(solution)/shard_map/ppermute | solution.py:378
  69.8 9.6 %collective-permute-start.16 = (bf16[3,64,256]{2,1,0:T(8,128)(2,1)S(1)}, bf16[3,64,256]{2,1,0:T(8,128)(2,1)S(1)}, u32[]{:S(2)}, u32[]{:S(2)}) collective-permute-start(bf16[3,64,256]{2,1,0:T(8,128)(2,1)S(1)} %join.1), channel_id=1, source_target_pairs={{0,0},{8,1},{4,4},{12,5},{1,8},{9,9},{5,12},{13,13},{2,2},{10,3},{... | collective-permute-start | bytes 294920 | tf_op jit(solution)/shard_map/ppermute | solution.py:385

commit v8 on v7

--- a/solution.py
+++ b/solution.py
@@ -122,7 +122,7 @@
 
 def window_of(board, slot, out):
     start = pl.multiple_of(slot * (out.shape[1] - 2 * EDGE), EDGE)
-    out[...] = board[:, pl.ds(start, out.shape[1]), :]
+    out[...] = board[:, pl.ds(start, out.shape[1]), :].astype(out.dtype)
 
 
 def end_map_kernel(query, *refs, count):
@@ -256,8 +256,17 @@
     places = [(band, pair) for band in range(bands) for pair in range(cores)]
     there = [(home(*p), worker(*p)) for p in places]
     back = [(worker(*p), home(*p)) for p in places]
-    down = [(worker(b, p), worker(b + 1, p)) for b, p in places if b + 1 < bands]
-    up = [(worker(b, p), worker(b - 1, p)) for b, p in places if b > 0]
+    down = [(worker(b, p), home(b + 1, p)) for b, p in places if b + 1 < bands]
+    up = [(worker(b, p), home(b - 1, p)) for b, p in places if b > 0]
+    stays = [home(*p) for p in places if home(*p) == worker(*p)]
+    comes = [worker(*p) for p in places if home(*p) != worker(*p)]
+
+    def tile_swaps(value, members, step):
+        def flat(position, tile):
+            return (position // cores * tiles + tile) * cores + position % cores
+
+        pairs = [(flat(m, (i + step) % tiles), flat(m, i)) for m in members for i in range(tiles)]
+        return lax.ppermute(value, ("blk", "tile", "pair"), pairs)
 
     def tied(values, *others):
         return lax.optimization_barrier((values, others))[0]
@@ -309,17 +318,21 @@
         )
 
     left_here = lax.ppermute(left_tokens[0], both, there)
+    steps = range(1, tiles)
+    left_early = [tile_swaps(left_tokens[0], stays, s) for s in steps]
     self_out, reassemble, cross_out, right_own, self_qkv, cross_qkv, taps, half = staged(
         [self_out, reassemble, cross_out, right_tokens[0], self_qkv, cross_qkv, taps]
     )
-    left = tile_pieces(left_here)
-    right = [right_own, *[from_tile(right_tokens[0], s) for s in range(1, tiles)]]
+    right = [right_own, *[from_tile(right_tokens[0], s) for s in steps]]
     (right_pack,) = project(right, cross_qkv, False, 1)
+    left_here, right_pack = lax.optimization_barrier((left_here, right_pack))
     right_pack = lax.ppermute(right_pack, both, there)
+    left_late = [tile_swaps(left_here, comes, s) for s in steps]
+    left = [left_here, *[a + b for a, b in zip(left_early, left_late)]]
     query, pack = project(left, self_qkv, True, 0)
-    beside = neighbours(tied(pack, right_pack))
+    beside = neighbours(pack)
     halves = tile_pieces(tied(half, left))[1:]
-    near, halves = lax.optimization_barrier(([pack, *beside], halves))
+    near, halves, right_pack = lax.optimization_barrier(([pack, *beside], halves, right_pack))
     far = [q for p in near for q in across(p)]
     state = begin(query, near)
     right_pack = tied(right_pack, state)
@@ -363,7 +376,7 @@
         "end_map",
         [(window, BF16)] * tiles,
         [cross_query, *grouped(right_far), *state, composed],
-        [pltpu.VMEM(board, BF16)],
+        [pltpu.VMEM(board, F32)],
     )
     (carried,) = run_kernel(
         carry_kernel,
@@ -376,13 +389,14 @@
     (features,) = run_kernel(add_kernel, "add", [(window, BF16)], [carried, maps[0], *received])
     above = lax.ppermute(features[-1:], both, down)
     below = lax.ppermute(features[:1], both, up)
+    features = lax.ppermute(features, both, back)
     (joined,) = run_kernel(
         conv_kernel,
         "join",
         [((band_rows, width, channels), BF16)],
         [features, above, below, taps],
     )
-    return lax.ppermute(joined, both, back)[None]
+    return joined[None]
 
 
 def solution(mesh):

time: 80.2 us -> 79.3 us (0.989)
  starting transfers between devices: 33.3 us -> 26.8 us
  waiting for transfers between devices: 26.1 us -> 31.5 us
    ppermute x5 -> x4, waiting for transfers between devices: 16.6 us -> 10.8 us  [from_tile(): lax.ppermute(value, 'tile', [((i + step) % tiles, i) for i in range(tiles)])]
    ppermute x5 -> x4, starting transfers between devices: 7.06 us -> 2.94 us  [from_tile(): lax.ppermute(value, 'tile', [((i + step) % tiles, i) for i in range(tiles)])]
    ppermute x1, waiting for transfers between devices: 0.01 us -> 3.65 us  [body(): left_here = lax.ppermute(left_tokens[0], both, there)]
    ppermute x1 -> x3, waiting for transfers between devices: 2.47 us -> 5.63 us  [the longest x2 5.63 us: tile_swaps(): return lax.ppermute(value, ('blk', 'tile', 'pair'), pairs)]
    ppermute x1, waiting for transfers between devices: 1.73 us -> 4.23 us  [body(): below = lax.ppermute(features[:1], both, up)]
    ppermute x1 -> x3, starting transfers between devices: 7.11 us -> 9.29 us  [the longest x1 6.46 us: body(): features = lax.ppermute(features, both, back)]
    ppermute x1, starting transfers between devices: 3.56 us -> 1.43 us  [body(): above = lax.ppermute(features[-1:], both, down)]
    ppermute x1, starting transfers between devices: 4.9 us -> 2.97 us  [body(): right_pack = lax.ppermute(right_pack, both, there)]
  transfers between devices with their start and end apart: 17 -> 18, of which waited for: 8 -> 8; matrix products, arithmetic and copies ran while one was open for 0% -> 0% of each run, Pallas kernels for 18% -> 18%
where the time goes in v8:
time: 79.3 us; the launch traced here: 79.1 us
  waiting for transfers between devices  31.5 us (40%)
  starting transfers between devices  26.8 us (34%)
  Pallas kernels  20.4 us (26%)
    pallas_call x13, Pallas kernels, run_kernel(): pl.pallas_call(kernel, out_shape=[jax.ShapeDtypeStruct(*s) for s in shape...  20.4 us
    ppermute x4, waiting for transfers between devices, from_tile(): lax.ppermute(value, 'tile', [((i + step) % tiles, i) for i in range(tiles)])  10.8 us
    ppermute x1, starting transfers between devices, body(): features = lax.ppermute(features, both, back)  6.46 us
    ppermute x2, waiting for transfers between devices, tile_swaps(): return lax.ppermute(value, ('blk', 'tile', 'pair'), pairs)  5.63 us
    ppermute x1, starting transfers between devices, body(): left_here = lax.ppermute(left_tokens[0], both, there)  5.05 us
    ppermute x1, waiting for transfers between devices, body(): right_pack = lax.ppermute(right_pack, both, there)  4.23 us
    ppermute x1, waiting for transfers between devices, body(): below = lax.ppermute(features[:1], both, up)  4.23 us
    ppermute x1, waiting for transfers between devices, body(): left_here = lax.ppermute(left_tokens[0], both, there)  3.65 us
  transfers between devices with their start and end apart: 18, of which 8 were waited for; matrix products, arithmetic and copies ran while one was open for 0% of the time, Pallas kernels for 18%

profile of v8, /device:TPU:1, one launch (start us, length us, event | category | flops | bytes accessed | tf_op | source)
XLA Modules:
  0.0 79.1 jit_solution(14084591348134536468)
XLA Ops:
  0.0 2.0 %collective-permute-start.1 = (bf16[384,384]{1,0:T(8,128)(2,1)}, bf16[384,384]{1,0:T(8,128)(2,1)S(1)}, u32[]{:S(2)}, u32[]{:S(2)}) collective-permute-start(bf16[384,384]{1,0:T(8,128)(2,1)} %bitcast.8), channel_id=1, source_target_pairs={{2,0},{0,2},{3,1},{1,3},{6,4},{4,6},{7,5},{5,7},{10,8},{8,10},{11,... | collective-permute-start | bytes 884744 | tf_op jit(solution)/shard_map/ppermute | solution.py:275
  2.0 5.0 %collective-permute-start = (bf16[384,384]{1,0:T(8,128)(2,1)}, bf16[384,384]{1,0:T(8,128)(2,1)S(1)}, u32[]{:S(2)}, u32[]{:S(2)}) collective-permute-start(bf16[384,384]{1,0:T(8,128)(2,1)} %bitcast.10), channel_id=1, source_target_pairs={{0,0},{1,8},{4,4},{5,12},{8,1},{9,9},{12,5},{13,13},{2,2},{3,10},{... | collective-permute-start | bytes 884744 | tf_op jit(solution)/shard_map/ppermute | solution.py:320
  7.8 2.6 %stage.1 = (bf16[256,768]{1,0:T(8,128)(2,1)S(1)}, bf16[384,256]{1,0:T(8,128)(2,1)S(1)}, bf16[256,768]{1,0:T(8,128)(2,1)S(1)}, bf16[384,384]{1,0:T(8,128)(2,1)S(1...) custom-call(bf16[256,768]{1,0:T(8,128)(2,1)} %refs_0_.1, ...), custom_call_target="tpu_custom_call" | custom-call | tf_op jit(solution)/shard_map/stage/pallas_call | solution.py:22
  11.2 3.6 %collective-permute-done.refs_0_.refs_4_ = bf16[384,384]{1,0:T(8,128)(2,1)S(1)} collective-permute-done((bf16[384,384]{1,0:T(8,128)(2,1)}, bf16[384,384]{1,0:T(8,128)(2,1)S(1)}, u32[]{:S(2)}, u32[]{:S(2)}) %collective-permute-start) | collective-permute-done | bytes 294944 | tf_op jit(solution)/shard_map/ppermute | solution.py:320
  14.9 2.2 %collective-permute-start.3 = (bf16[384,384]{1,0:T(8,128)(2,1)S(1)}, bf16[384,384]{1,0:T(8,128)(2,1)S(1)}, u32[]{:S(2)}, u32[]{:S(2)}) collective-permute-start(bf16[384,384]{1,0:T(8,128)(2,1)S(1)} %collective-permute-done.refs_0_.refs_4_), channel_id=1, source_target_pairs={{10,8},{8,10},{14,12},{12,14},{3,1},{1,3},{7,5},{5,7},{26,24},{24,... | collective-permute-start | bytes 884744 | tf_op jit(solution)/shard_map/ppermute | solution.py:269
  17.0 3.0 %collective-permute-start.6 = (bf16[384,512]{1,0:T(8,128)(2,1)S(1)}, bf16[384,512]{1,0:T(8,128)(2,1)S(1)}, u32[]{:S(2)}, u32[]{:S(2)}) collective-permute-start(bf16[384,512]{1,0:T(8,128)(2,1)S(1)} %project.2), channel_id=1, source_target_pairs={{0,0},{1,8},{4,4},{5,12},{8,1},{9,9},{12,5},{13,13},{2,2},{3,10},{... | collective-permute-start | bytes 1179656 | tf_op jit(solution)/shard_map/ppermute | solution.py:329
  20.0 5.6 %collective-permute-done.3 = bf16[384,384]{1,0:T(8,128)(2,1)S(1)} collective-permute-done((bf16[384,384]{1,0:T(8,128)(2,1)S(1)}, bf16[384,384]{1,0:T(8,128)(2,1)S(1)}, u32[]{:S(2)}, u32[]{:S(2)}) %collective-permute-start.3) | collective-permute-done | bytes 294944 | tf_op jit(solution)/shard_map/ppermute | solution.py:269
  25.7 1.1 %project.3 = (bf16[384,256]{1,0:T(8,128)(2,1)S(1)}, bf16[384,512]{1,0:T(8,128)(2,1)S(1)}) custom-call(bf16[384,384]{1,0:T(8,128)(2,1)S(1)} %collective-permute-done.refs_0_.refs_4_, bf16[384,384]{1,0:T(8,128)(2,1)S(1)} %add.4.refs_1_.refs_5_, bf16[3,2,384,256]{3,2,1,0:T(8,128)(2,1)S(1)} %bitcast.7), custom_call_target="tpu_custom_call" | custom-call | tf_op jit(solution)/shard_map/project/pallas_call | solution.py:22
  27.1 4.2 %collective-permute-done.6.refs_0_ = bf16[384,512]{1,0:T(8,128)(2,1)S(1)} collective-permute-done((bf16[384,512]{1,0:T(8,128)(2,1)S(1)}, bf16[384,512]{1,0:T(8,128)(2,1)S(1)}, u32[]{:S(2)}, u32[]{:S(2)}) %collective-permute-start.6) | collective-permute-done | bytes 393248 | tf_op jit(solution)/shard_map/ppermute | solution.py:329
  31.3 1.2 %collective-permute-done.5.refs_0_ = bf16[192,768]{1,0:T(8,128)(2,1)S(1)} collective-permute-done((bf16[192,768]{1,0:T(8,128)(2,1)S(1)}, bf16[192,768]{1,0:T(8,128)(2,1)S(1)}, u32[]{:S(2)}, u32[]{:S(2)}) %collective-permute-start.5) | collective-permute-done | bytes 294944 | tf_op jit(solution)/shard_map/ppermute | solution.py:275
  32.5 2.9 %collective-permute-done.4.refs_1_ = bf16[384,512]{1,0:T(8,128)(2,1)S(1)} collective-permute-done((bf16[384,512]{1,0:T(8,128)(2,1)S(1)}, bf16[384,512]{1,0:T(8,128)(2,1)S(1)}, u32[]{:S(2)}, u32[]{:S(2)}) %collective-permute-start.4) | collective-permute-done | bytes 393248 | tf_op jit(solution)/shard_map/ppermute | solution.py:283
  36.0 2.3 %begin.2 = (f32[4,384,64]{2,1,0:T(8,128)S(1)}, f32[4,384,2]{2,1,0:T(8,128)S(1)}) custom-call(bf16[384,256]{1,0:T(8,128)(2,1)S(1)} %get-tuple-element.45.query, bf16[384,512]{1,0:T(8,128)(2,1)S(1)} %get-tuple-element.50.refs_0_, bf16[384,512]{1,0:T(8,128)(2,1)S(1)} %collective-permute-done.4.refs_1_), custom_call_target="tpu_custom_call" | custom-call | tf_op jit(solution)/shard_map/begin/pallas_call | solution.py:22
  38.4 3.1 %end.1.refs_0_ = bf16[384,256]{1,0:T(8,128)(2,1)S(1)} custom-call(bf16[384,256]{1,0:T(8,128)(2,1)S(1)} %get-tuple-element.45.query, bf16[384,512]{1,0:T(8,128)(2,1)S(1)} %collective-permute-done.7.refs_0_, bf16[384,512]{1,0:T(8,128)(2,1)S(1)} %collective-permute-done.8.refs_1_, f32[4,384,64]{2,1,0:T(8,128)S(1)} %get-tuple-element.52.refs_2_, ...), custom_call_target="tpu_custom_call" | custom-call | tf_op jit(solution)/shard_map/end/pallas_call | solution.py:22
  42.2 5.4 %collective-permute-done.9.refs_1_ = bf16[384,256]{1,0:T(8,128)(2,1)S(1)} collective-permute-done((bf16[384,256]{1,0:T(8,128)(2,1)S(1)}, bf16[384,256]{1,0:T(8,128)(2,1)S(1)}, u32[]{:S(2)}, u32[]{:S(2)}) %collective-permute-start.9) | collective-permute-done | bytes 196640 | tf_op jit(solution)/shard_map/ppermute | solution.py:275
  47.6 1.5 %update.1 = (bf16[2,384,384]{2,1,0:T(8,128)(2,1)S(1)}, bf16[384,256]{1,0:T(8,128)(2,1)S(1)}) custom-call(bf16[384,256]{1,0:T(8,128)(2,1)S(1)} %end.1.refs_0_, bf16[384,256]{1,0:T(8,128)(2,1)S(1)} %collective-permute-done.9.refs_1_, bf16[256,768]{1,0:T(8,128)(2,1)S(1)} %get-tuple-element.60.refs_2_, bf16[256,768]{1,0:T(8,128)(2,1)S(1)} %get-tuple-element.61.refs_3_, ...), custom_call_target="tpu_custom_call" | custom-call | tf_op jit(solution)/shard_map/update/pallas_call | solution.py:22
  49.1 1.4 %collective-permute-start.12 = (bf16[384,512]{1,0:T(8,128)(2,1)S(1)}, bf16[384,512]{1,0:T(8,128)(2,1)S(1)}, u32[]{:S(2)}, u32[]{:S(2)}) collective-permute-start(bf16[384,512]{1,0:T(8,128)(2,1)S(1)} %collective-permute-done.6.refs_0_), channel_id=1, source_target_pairs={{1,0},{0,1},{3,2},{2,3},{5,4},{4,5},{7,6},{6,7},{9,8},{8,9},{11,10... | collective-permute-start | bytes 1179656 | tf_op jit(solution)/shard_map/ppermute | solution.py:289
  50.5 2.3 %begin.3 = (f32[4,384,64]{2,1,0:T(8,128)S(1)}, f32[4,384,2]{2,1,0:T(8,128)S(1)}) custom-call(bf16[384,256]{1,0:T(8,128)(2,1)S(1)} %get-tuple-element.63.query, bf16[384,512]{1,0:T(8,128)(2,1)S(1)} %collective-permute-done.6.refs_0_, bf16[384,512]{1,0:T(8,128)(2,1)S(1)} %collective-permute-done.11.refs_1_), custom_call_target="tpu_custom_call" | custom-call | tf_op jit(solution)/shard_map/begin/pallas_call | solution.py:22
  52.8 5.0 %end_map.1 = (bf16[3,96,256]{2,1,0:T(8,128)(2,1)S(1)}, bf16[3,96,256]{2,1,0:T(8,128)(2,1)S(1)}) custom-call(bf16[384,256]{1,0:T(8,128)(2,1)S(1)} %get-tuple-element.63.query, bf16[384,512]{1,0:T(8,128)(2,1)S(1)} %collective-permute-done.12.refs_0_, bf16[384,512]{1,0:T(8,128)(2,1)S(1)} %collective-permute-done.13.refs_1_, ...), custom_call_target="tpu_custom_call" | custom-call | tf_op jit(solution)/shard_map/end_map/pallas_call | solution.py:22
  58.6 4.3 %collective-permute-done.14.refs_2_ = bf16[3,96,256]{2,1,0:T(8,128)(2,1)S(1)} collective-permute-done((bf16[3,96,256]{2,1,0:T(8,128)(2,1)S(1)}, bf16[3,96,256]{2,1,0:T(8,128)(2,1)S(1)}, u32[]{:S(2)}, u32[]{:S(2)}) %collective-permute-start.14) | collective-permute-done | bytes 147488 | tf_op jit(solution)/shard_map/ppermute | solution.py:275
  62.9 6.5 %collective-permute-start.15 = (bf16[3,96,256]{2,1,0:T(8,128)(2,1)S(1)}, bf16[3,96,256]{2,1,0:T(8,128)(2,1)S(1)}, u32[]{:S(2)}, u32[]{:S(2)}) collective-permute-start(bf16[3,96,256]{2,1,0:T(8,128)(2,1)S(1)} %add.5), channel_id=1, source_target_pairs={{0,0},{8,1},{4,4},{12,5},{1,8},{9,9},{5,12},{13,13},{2,2},{10,3},{... | collective-permute-start | bytes 442376 | tf_op jit(solution)/shard_map/ppermute | solution.py:392
  69.4 1.4 %collective-permute-start.16 = (bf16[1,96,256]{2,1,0:T(8,128)(2,1)S(1)}, bf16[1,96,256]{2,1,0:T(8,128)(2,1)S(1)}, u32[]{:S(2)}, u32[]{:S(2)}) collective-permute-start(bf16[1,96,256]{2,1,0:T(8,128)(2,1)S(1)} %get-tuple-element.78), channel_id=1, source_target_pairs={{0,4},{8,5},{4,8},{12,9},{1,12},{9,13},{2,6},{10,7},{6,10},{14,11}... | collective-permute-start | bytes 147464 | tf_op jit(solution)/shard_map/ppermute | solution.py:390
  70.8 3.0 %collective-permute-start.17 = (bf16[1,96,256]{2,1,0:T(8,128)(2,1)S(1)}, bf16[1,96,256]{2,1,0:T(8,128)(2,1)S(1)}, u32[]{:S(2)}, u32[]{:S(2)}) collective-permute-start(bf16[1,96,256]{2,1,0:T(8,128)(2,1)S(1)} %get-tuple-element.77), channel_id=1, source_target_pairs={{4,0},{12,1},{1,4},{9,5},{5,8},{13,9},{6,2},{14,3},{3,6},{11,7},{7... | collective-permute-start | bytes 147464 | tf_op jit(solution)/shard_map/ppermute | solution.py:391
  73.8 4.2 %collective-permute-done.17.below = bf16[1,96,256]{2,1,0:T(8,128)(2,1)S(1)} collective-permute-done((bf16[1,96,256]{2,1,0:T(8,128)(2,1)S(1)}, bf16[1,96,256]{2,1,0:T(8,128)(2,1)S(1)}, u32[]{:S(2)}, u32[]{:S(2)}) %collective-permute-start.17) | collective-permute-done | bytes 49184 | tf_op jit(solution)/shard_map/ppermute | solution.py:391
  78.1 1.0 %join.1 = bf16[3,64,256]{2,1,0:T(8,128)(2,1)} custom-call(bf16[3,96,256]{2,1,0:T(8,128)(2,1)S(1)} %collective-permute-done.15.window, bf16[1,96,256]{2,1,0:T(8,128)(2,1)S(1)} %collective-permute-done.16.above, bf16[1,96,256]{2,1,0:T(8,128)(2,1)S(1)} %collective-permute-done.17.below, bf16[3,3,256,256]{3,2,1,0:T(8,128)(2,1)S(1)} %get-tuple-element.76.weight), custom_call_target="tpu_custom_call" | custom-call | tf_op jit(solution)/shard_map/join/pallas_call | solution.py:22
  (27 shorter events, 4.1 us)
Async XLA Ops:
  0.0 10.3 %collective-permute-start.1 = (bf16[384,384]{1,0:T(8,128)(2,1)}, bf16[384,384]{1,0:T(8,128)(2,1)S(1)}, u32[]{:S(2)}, u32[]{:S(2)}) collective-permute-start(bf16[384,384]{1,0:T(8,128)(2,1)} %bitcast.8), channel_id=1, source_target_pairs={{2,0},{0,2},{3,1},{1,3},{6,4},{4,6},{7,5},{5,7},{10,8},{8,10},{11,... | collective-permute-start | bytes 884744 | tf_op jit(solution)/shard_map/ppermute | solution.py:275
  2.0 12.8 %collective-permute-start = (bf16[384,384]{1,0:T(8,128)(2,1)}, bf16[384,384]{1,0:T(8,128)(2,1)S(1)}, u32[]{:S(2)}, u32[]{:S(2)}) collective-permute-start(bf16[384,384]{1,0:T(8,128)(2,1)} %bitcast.10), channel_id=1, source_target_pairs={{0,0},{1,8},{4,4},{5,12},{8,1},{9,9},{12,5},{13,13},{2,2},{3,10},{... | collective-permute-start | bytes 884744 | tf_op jit(solution)/shard_map/ppermute | solution.py:320
  7.1 12.9 %collective-permute-start.2 = (bf16[384,384]{1,0:T(8,128)(2,1)}, bf16[384,384]{1,0:T(8,128)(2,1)S(1)}, u32[]{:S(2)}, u32[]{:S(2)}) collective-permute-start(bf16[384,384]{1,0:T(8,128)(2,1)} %bitcast.11), channel_id=1, source_target_pairs={{2,0},{0,2},{6,4},{4,6},{11,9},{9,11},{15,13},{13,15},{18,16},{16,... | collective-permute-start | bytes 884744 | tf_op jit(solution)/shard_map/ppermute | solution.py:269
  14.9 10.8 %collective-permute-start.3 = (bf16[384,384]{1,0:T(8,128)(2,1)S(1)}, bf16[384,384]{1,0:T(8,128)(2,1)S(1)}, u32[]{:S(2)}, u32[]{:S(2)}) collective-permute-start(bf16[384,384]{1,0:T(8,128)(2,1)S(1)} %collective-permute-done.refs_0_.refs_4_), channel_id=1, source_target_pairs={{10,8},{8,10},{14,12},{12,14},{3,1},{1,3},{7,5},{5,7},{26,24},{24,... | collective-permute-start | bytes 884744 | tf_op jit(solution)/shard_map/ppermute | solution.py:269
  17.0 14.3 %collective-permute-start.6 = (bf16[384,512]{1,0:T(8,128)(2,1)S(1)}, bf16[384,512]{1,0:T(8,128)(2,1)S(1)}, u32[]{:S(2)}, u32[]{:S(2)}) collective-permute-start(bf16[384,512]{1,0:T(8,128)(2,1)S(1)} %project.2), channel_id=1, source_target_pairs={{0,0},{1,8},{4,4},{5,12},{8,1},{9,9},{12,5},{13,13},{2,2},{3,10},{... | collective-permute-start | bytes 1179656 | tf_op jit(solution)/shard_map/ppermute | solution.py:329
  26.8 8.7 %collective-permute-start.4 = (bf16[384,512]{1,0:T(8,128)(2,1)S(1)}, bf16[384,512]{1,0:T(8,128)(2,1)S(1)}, u32[]{:S(2)}, u32[]{:S(2)}) collective-permute-start(bf16[384,512]{1,0:T(8,128)(2,1)S(1)} %get-tuple-element.50.refs_0_), channel_id=1, source_target_pairs={{4,0},{0,4},{12,8},{8,12},{5,1},{1,5},{13,9},{9,13},{6,2},{2,6},{1... | collective-permute-start | bytes 1179656 | tf_op jit(solution)/shard_map/ppermute | solution.py:283
  26.9 5.6 %collective-permute-start.5 = (bf16[192,768]{1,0:T(8,128)(2,1)S(1)}, bf16[192,768]{1,0:T(8,128)(2,1)S(1)}, u32[]{:S(2)}, u32[]{:S(2)}) collective-permute-start(bf16[192,768]{1,0:T(8,128)(2,1)S(1)} %get-tuple-element.48), channel_id=1, source_target_pairs={{2,0},{0,2},{3,1},{1,3},{6,4},{4,6},{7,5},{5,7},{10,8},{8,10},{11,... | collective-permute-start | bytes 884744 | tf_op jit(solution)/shard_map/ppermute | solution.py:275
  35.4 3.0 %collective-permute-start.7 = (bf16[384,512]{1,0:T(8,128)(2,1)S(1)}, bf16[384,512]{1,0:T(8,128)(2,1)S(1)}, u32[]{:S(2)}, u32[]{:S(2)}) collective-permute-start(bf16[384,512]{1,0:T(8,128)(2,1)S(1)} %get-tuple-element.50.refs_0_), channel_id=1, source_target_pairs={{1,0},{0,1},{3,2},{2,3},{5,4},{4,5},{7,6},{6,7},{9,8},{8,9},{11,10... | collective-permute-start | bytes 1179656 | tf_op jit(solution)/shard_map/ppermute | solution.py:289
  35.4 3.0 %collective-permute-start.8 = (bf16[384,512]{1,0:T(8,128)(2,1)S(1)}, bf16[384,512]{1,0:T(8,128)(2,1)S(1)}, u32[]{:S(2)}, u32[]{:S(2)}) collective-permute-start(bf16[384,512]{1,0:T(8,128)(2,1)S(1)} %collective-permute-done.4.refs_1_), channel_id=1, source_target_pairs={{1,0},{0,1},{3,2},{2,3},{5,4},{4,5},{7,6},{6,7},{9,8},{8,9},{11,10... | collective-permute-start | bytes 1179656 | tf_op jit(solution)/shard_map/ppermute | solution.py:289
  38.2 10.8 %collective-permute-start.11 = (bf16[384,512]{1,0:T(8,128)(2,1)S(1)}, bf16[384,512]{1,0:T(8,128)(2,1)S(1)}, u32[]{:S(2)}, u32[]{:S(2)}) collective-permute-start(bf16[384,512]{1,0:T(8,128)(2,1)S(1)} %collective-permute-done.6.refs_0_), channel_id=1, source_target_pairs={{4,0},{0,4},{12,8},{8,12},{5,1},{1,5},{13,9},{9,13},{6,2},{2,6},{1... | collective-permute-start | bytes 1179656 | tf_op jit(solution)/shard_map/ppermute | solution.py:283
  38.3 3.5 %collective-permute-start.10 = (bf16[192,768]{1,0:T(8,128)(2,1)S(1)}, bf16[192,768]{1,0:T(8,128)(2,1)S(1)}, u32[]{:S(2)}, u32[]{:S(2)}) collective-permute-start(bf16[192,768]{1,0:T(8,128)(2,1)S(1)} %collective-permute-done.5.refs_0_), channel_id=1, source_target_pairs={{1,0},{0,1},{3,2},{2,3},{5,4},{4,5},{7,6},{6,7},{9,8},{8,9},{11,10... | collective-permute-start | bytes 884744 | tf_op jit(solution)/shard_map/ppermute | solution.py:289
  41.5 6.1 %collective-permute-start.9 = (bf16[384,256]{1,0:T(8,128)(2,1)S(1)}, bf16[384,256]{1,0:T(8,128)(2,1)S(1)}, u32[]{:S(2)}, u32[]{:S(2)}) collective-permute-start(bf16[384,256]{1,0:T(8,128)(2,1)S(1)} %end.1.refs_0_), channel_id=1, source_target_pairs={{2,0},{0,2},{3,1},{1,3},{6,4},{4,6},{7,5},{5,7},{10,8},{8,10},{11,... | collective-permute-start | bytes 589832 | tf_op jit(solution)/shard_map/ppermute | solution.py:275
  49.1 3.8 %collective-permute-start.12 = (bf16[384,512]{1,0:T(8,128)(2,1)S(1)}, bf16[384,512]{1,0:T(8,128)(2,1)S(1)}, u32[]{:S(2)}, u32[]{:S(2)}) collective-permute-start(bf16[384,512]{1,0:T(8,128)(2,1)S(1)} %collective-permute-done.6.refs_0_), channel_id=1, source_target_pairs={{1,0},{0,1},{3,2},{2,3},{5,4},{4,5},{7,6},{6,7},{9,8},{8,9},{11,10... | collective-permute-start | bytes 1179656 | tf_op jit(solution)/shard_map/ppermute | solution.py:289
  50.4 2.4 %collective-permute-start.13 = (bf16[384,512]{1,0:T(8,128)(2,1)S(1)}, bf16[384,512]{1,0:T(8,128)(2,1)S(1)}, u32[]{:S(2)}, u32[]{:S(2)}) collective-permute-start(bf16[384,512]{1,0:T(8,128)(2,1)S(1)} %collective-permute-done.11.refs_1_), channel_id=1, source_target_pairs={{1,0},{0,1},{3,2},{2,3},{5,4},{4,5},{7,6},{6,7},{9,8},{8,9},{11,10... | collective-permute-start | bytes 1179656 | tf_op jit(solution)/shard_map/ppermute | solution.py:289
  57.8 5.0 %collective-permute-start.14 = (bf16[3,96,256]{2,1,0:T(8,128)(2,1)S(1)}, bf16[3,96,256]{2,1,0:T(8,128)(2,1)S(1)}, u32[]{:S(2)}, u32[]{:S(2)}) collective-permute-start(bf16[3,96,256]{2,1,0:T(8,128)(2,1)S(1)} %get-tuple-element.74), channel_id=1, source_target_pairs={{2,0},{0,2},{3,1},{1,3},{6,4},{4,6},{7,5},{5,7},{10,8},{8,10},{11,... | collective-permute-start | bytes 442376 | tf_op jit(solution)/shard_map/ppermute | solution.py:275
  62.9 15.1 %collective-permute-start.15 = (bf16[3,96,256]{2,1,0:T(8,128)(2,1)S(1)}, bf16[3,96,256]{2,1,0:T(8,128)(2,1)S(1)}, u32[]{:S(2)}, u32[]{:S(2)}) collective-permute-start(bf16[3,96,256]{2,1,0:T(8,128)(2,1)S(1)} %add.5), channel_id=1, source_target_pairs={{0,0},{8,1},{4,4},{12,5},{1,8},{9,9},{5,12},{13,13},{2,2},{10,3},{... | collective-permute-start | bytes 442376 | tf_op jit(solution)/shard_map/ppermute | solution.py:392
  69.4 4.4 %collective-permute-start.16 = (bf16[1,96,256]{2,1,0:T(8,128)(2,1)S(1)}, bf16[1,96,256]{2,1,0:T(8,128)(2,1)S(1)}, u32[]{:S(2)}, u32[]{:S(2)}) collective-permute-start(bf16[1,96,256]{2,1,0:T(8,128)(2,1)S(1)} %get-tuple-element.78), channel_id=1, source_target_pairs={{0,4},{8,5},{4,8},{12,9},{1,12},{9,13},{2,6},{10,7},{6,10},{14,11}... | collective-permute-start | bytes 147464 | tf_op jit(solution)/shard_map/ppermute | solution.py:390
  70.8 7.2 %collective-permute-start.17 = (bf16[1,96,256]{2,1,0:T(8,128)(2,1)S(1)}, bf16[1,96,256]{2,1,0:T(8,128)(2,1)S(1)}, u32[]{:S(2)}, u32[]{:S(2)}) collective-permute-start(bf16[1,96,256]{2,1,0:T(8,128)(2,1)S(1)} %get-tuple-element.77), channel_id=1, source_target_pairs={{4,0},{12,1},{1,4},{9,5},{5,8},{13,9},{6,2},{14,3},{3,6},{11,7},{7... | collective-permute-start | bytes 147464 | tf_op jit(solution)/shard_map/ppermute | solution.py:391

commit v9 on v8

--- a/solution.py
+++ b/solution.py
@@ -324,15 +324,16 @@
         [self_out, reassemble, cross_out, right_tokens[0], self_qkv, cross_qkv, taps]
     )
     right = [right_own, *[from_tile(right_tokens[0], s) for s in steps]]
+    right, left_early = lax.optimization_barrier((right, left_early))
     (right_pack,) = project(right, cross_qkv, False, 1)
-    left_here, right_pack = lax.optimization_barrier((left_here, right_pack))
     right_pack = lax.ppermute(right_pack, both, there)
     left_late = [tile_swaps(left_here, comes, s) for s in steps]
     left = [left_here, *[a + b for a, b in zip(left_early, left_late)]]
     query, pack = project(left, self_qkv, True, 0)
-    beside = neighbours(pack)
-    halves = tile_pieces(tied(half, left))[1:]
-    near, halves, right_pack = lax.optimization_barrier(([pack, *beside], halves, right_pack))
+    halves = tile_pieces(half)[1:]
+    pack, halves = lax.optimization_barrier((pack, halves))
+    beside = neighbours(tied(pack, right_pack))
+    near = [pack, *beside]
     far = [q for p in near for q in across(p)]
     state = begin(query, near)
     right_pack = tied(right_pack, state)

time: 79.3 us -> 79.8 us (level)
  starting transfers between devices: 26.8 us -> 33.9 us
  waiting for transfers between devices: 31.5 us -> 25 us
    ppermute x1, waiting for transfers between devices: 4.23 us -> 0.01 us  [body(): right_pack = lax.ppermute(right_pack, both, there)]
    ppermute x1, waiting for transfers between devices: 3.65 us -> 0.01 us  [body(): left_here = lax.ppermute(left_tokens[0], both, there)]
    ppermute x2, starting transfers between devices: 0.14 us -> 3.08 us  [neighbours(): lax.ppermute(pack, 'blk', [(g + (i + s) % span, g + i) for g, i in ring])]
    ppermute x1, starting transfers between devices: 2.97 us -> 5.35 us  [body(): right_pack = lax.ppermute(right_pack, both, there)]
    ppermute x2, waiting for transfers between devices: 2.95 us -> 5.16 us  [neighbours(): lax.ppermute(pack, 'blk', [(g + (i + s) % span, g + i) for g, i in ring])]
    ppermute x4, starting transfers between devices: 2.94 us -> 4.91 us  [from_tile(): lax.ppermute(value, 'tile', [((i + step) % tiles, i) for i in range(tiles)])]
    ppermute x2, starting transfers between devices: 2.83 us -> 3.78 us  [tile_swaps(): return lax.ppermute(value, ('blk', 'tile', 'pair'), pairs)]
    ppermute x1, starting transfers between devices: 6.46 us -> 5.55 us  [body(): features = lax.ppermute(features, both, back)]
  transfers between devices with their start and end apart: 18 -> 18, of which waited for: 8 -> 6; matrix products, arithmetic and copies ran while one was open for 0% -> 0% of each run, Pallas kernels for 18% -> 18%
where the time goes in v9:
time: 79.8 us; the launch traced here: 79.5 us
  starting transfers between devices  33.9 us (42%)
  waiting for transfers between devices  25 us (31%)
  Pallas kernels  20.4 us (26%)
    pallas_call x13, Pallas kernels, run_kernel(): pl.pallas_call(kernel, out_shape=[jax.ShapeDtypeStruct(*s) for s in shape...  20.4 us
    ppermute x4, waiting for transfers between devices, from_tile(): lax.ppermute(value, 'tile', [((i + step) % tiles, i) for i in range(tiles)])  10.6 us
    ppermute x1, starting transfers between devices, body(): features = lax.ppermute(features, both, back)  5.55 us
    ppermute x1, starting transfers between devices, body(): right_pack = lax.ppermute(right_pack, both, there)  5.35 us
    ppermute x2, waiting for transfers between devices, neighbours(): lax.ppermute(pack, 'blk', [(g + (i + s) % span, g + i) for g, i in ring])  5.16 us
    ppermute x1, starting transfers between devices, body(): left_here = lax.ppermute(left_tokens[0], both, there)  5.06 us
    ppermute x4, starting transfers between devices, from_tile(): lax.ppermute(value, 'tile', [((i + step) % tiles, i) for i in range(tiles)])  4.91 us
    ppermute x2, waiting for transfers between devices, tile_swaps(): return lax.ppermute(value, ('blk', 'tile', 'pair'), pairs)  4.84 us
  transfers between devices with their start and end apart: 18, of which 6 were waited for; matrix products, arithmetic and copies ran while one was open for 0% of the time, Pallas kernels for 18%

profile of v9, /device:TPU:1, one launch (start us, length us, event | category | flops | bytes accessed | tf_op | source)
XLA Modules:
  0.0 79.5 jit_solution(14614760158929493503)
XLA Ops:
  0.0 2.0 %collective-permute-start.1 = (bf16[384,384]{1,0:T(8,128)(2,1)}, bf16[384,384]{1,0:T(8,128)(2,1)S(1)}, u32[]{:S(2)}, u32[]{:S(2)}) collective-permute-start(bf16[384,384]{1,0:T(8,128)(2,1)} %bitcast.8), channel_id=1, source_target_pairs={{2,0},{0,2},{3,1},{1,3},{6,4},{4,6},{7,5},{5,7},{10,8},{8,10},{11,... | collective-permute-start | bytes 884744 | tf_op jit(solution)/shard_map/ppermute | solution.py:275
  2.7 5.1 %collective-permute-start = (bf16[384,384]{1,0:T(8,128)(2,1)}, bf16[384,384]{1,0:T(8,128)(2,1)S(1)}, u32[]{:S(2)}, u32[]{:S(2)}) collective-permute-start(bf16[384,384]{1,0:T(8,128)(2,1)} %bitcast.11), channel_id=1, source_target_pairs={{0,0},{1,8},{4,4},{5,12},{8,1},{9,9},{12,5},{13,13},{2,2},{3,10},{... | collective-permute-start | bytes 884744 | tf_op jit(solution)/shard_map/ppermute | solution.py:320
  7.8 2.6 %stage.1 = (bf16[256,768]{1,0:T(8,128)(2,1)S(1)}, bf16[384,256]{1,0:T(8,128)(2,1)S(1)}, bf16[256,768]{1,0:T(8,128)(2,1)S(1)}, bf16[384,384]{1,0:T(8,128)(2,1)S(1...) custom-call(bf16[256,768]{1,0:T(8,128)(2,1)} %refs_0_.1, ...), custom_call_target="tpu_custom_call" | custom-call | tf_op jit(solution)/shard_map/stage/pallas_call | solution.py:22
  11.2 5.4 %collective-permute-start.6 = (bf16[384,512]{1,0:T(8,128)(2,1)S(1)}, bf16[384,512]{1,0:T(8,128)(2,1)S(1)}, u32[]{:S(2)}, u32[]{:S(2)}) collective-permute-start(bf16[384,512]{1,0:T(8,128)(2,1)S(1)} %project.3), channel_id=1, source_target_pairs={{0,0},{1,8},{4,4},{5,12},{8,1},{9,9},{12,5},{13,13},{2,2},{3,10},{... | collective-permute-start | bytes 1179656 | tf_op jit(solution)/shard_map/ppermute | solution.py:329
  16.6 3.1 %collective-permute-start.3 = (bf16[384,384]{1,0:T(8,128)(2,1)S(1)}, bf16[384,384]{1,0:T(8,128)(2,1)S(1)}, u32[]{:S(2)}, u32[]{:S(2)}) collective-permute-start(bf16[384,384]{1,0:T(8,128)(2,1)S(1)} %collective-permute-done.refs_0_.refs_4_), channel_id=1, source_target_pairs={{10,8},{8,10},{14,12},{12,14},{3,1},{1,3},{7,5},{5,7},{26,24},{24,... | collective-permute-start | bytes 884744 | tf_op jit(solution)/shard_map/ppermute | solution.py:269
  20.0 4.8 %collective-permute-done.3 = bf16[384,384]{1,0:T(8,128)(2,1)S(1)} collective-permute-done((bf16[384,384]{1,0:T(8,128)(2,1)S(1)}, bf16[384,384]{1,0:T(8,128)(2,1)S(1)}, u32[]{:S(2)}, u32[]{:S(2)}) %collective-permute-start.3) | collective-permute-done | bytes 294944 | tf_op jit(solution)/shard_map/ppermute | solution.py:269
  25.0 1.1 %project.2 = (bf16[384,256]{1,0:T(8,128)(2,1)S(1)}, bf16[384,512]{1,0:T(8,128)(2,1)S(1)}) custom-call(bf16[384,384]{1,0:T(8,128)(2,1)S(1)} %collective-permute-done.refs_0_.refs_4_, bf16[384,384]{1,0:T(8,128)(2,1)S(1)} %add.4.refs_1_.refs_5_, bf16[3,2,384,256]{3,2,1,0:T(8,128)(2,1)S(1)} %bitcast.7), custom_call_target="tpu_custom_call" | custom-call | tf_op jit(solution)/shard_map/project/pallas_call | solution.py:22
  26.0 2.3 %collective-permute-done.4.refs_0_ = bf16[192,768]{1,0:T(8,128)(2,1)S(1)} collective-permute-done((bf16[192,768]{1,0:T(8,128)(2,1)S(1)}, bf16[192,768]{1,0:T(8,128)(2,1)S(1)}, u32[]{:S(2)}, u32[]{:S(2)}) %collective-permute-start.4) | collective-permute-done | bytes 294944 | tf_op jit(solution)/shard_map/ppermute | solution.py:275
  28.3 1.5 %collective-permute-start.7 = (bf16[384,512]{1,0:T(8,128)(2,1)S(1)}, bf16[384,512]{1,0:T(8,128)(2,1)S(1)}, u32[]{:S(2)}, u32[]{:S(2)}) collective-permute-start(bf16[384,512]{1,0:T(8,128)(2,1)S(1)} %get-tuple-element.50.refs_0_), channel_id=1, source_target_pairs={{4,0},{0,4},{12,8},{8,12},{5,1},{1,5},{13,9},{9,13},{6,2},{2,6},{1... | collective-permute-start | bytes 1179656 | tf_op jit(solution)/shard_map/ppermute | solution.py:283
  29.9 5.2 %collective-permute-done.7.refs_1_ = bf16[384,512]{1,0:T(8,128)(2,1)S(1)} collective-permute-done((bf16[384,512]{1,0:T(8,128)(2,1)S(1)}, bf16[384,512]{1,0:T(8,128)(2,1)S(1)}, u32[]{:S(2)}, u32[]{:S(2)}) %collective-permute-start.7) | collective-permute-done | bytes 393248 | tf_op jit(solution)/shard_map/ppermute | solution.py:283
  35.1 2.3 %begin.2 = (f32[4,384,64]{2,1,0:T(8,128)S(1)}, f32[4,384,2]{2,1,0:T(8,128)S(1)}) custom-call(bf16[384,256]{1,0:T(8,128)(2,1)S(1)} %get-tuple-element.43.query, bf16[384,512]{1,0:T(8,128)(2,1)S(1)} %get-tuple-element.50.refs_0_, bf16[384,512]{1,0:T(8,128)(2,1)S(1)} %collective-permute-done.7.refs_1_), custom_call_target="tpu_custom_call" | custom-call | tf_op jit(solution)/shard_map/begin/pallas_call | solution.py:22
  37.4 1.5 %collective-permute-start.11 = (bf16[384,512]{1,0:T(8,128)(2,1)S(1)}, bf16[384,512]{1,0:T(8,128)(2,1)S(1)}, u32[]{:S(2)}, u32[]{:S(2)}) collective-permute-start(bf16[384,512]{1,0:T(8,128)(2,1)S(1)} %collective-permute-done.6.refs_0_), channel_id=1, source_target_pairs={{4,0},{0,4},{12,8},{8,12},{5,1},{1,5},{13,9},{9,13},{6,2},{2,6},{1... | collective-permute-start | bytes 1179656 | tf_op jit(solution)/shard_map/ppermute | solution.py:283
  39.7 3.1 %end.1.refs_0_ = bf16[384,256]{1,0:T(8,128)(2,1)S(1)} custom-call(bf16[384,256]{1,0:T(8,128)(2,1)S(1)} %get-tuple-element.43.query, bf16[384,512]{1,0:T(8,128)(2,1)S(1)} %collective-permute-done.5.refs_0_, bf16[384,512]{1,0:T(8,128)(2,1)S(1)} %collective-permute-done.8.refs_1_, f32[4,384,64]{2,1,0:T(8,128)S(1)} %get-tuple-element.51.refs_2_, ...), custom_call_target="tpu_custom_call" | custom-call | tf_op jit(solution)/shard_map/end/pallas_call | solution.py:22
  42.8 1.3 %collective-permute-start.9 = (bf16[384,256]{1,0:T(8,128)(2,1)S(1)}, bf16[384,256]{1,0:T(8,128)(2,1)S(1)}, u32[]{:S(2)}, u32[]{:S(2)}) collective-permute-start(bf16[384,256]{1,0:T(8,128)(2,1)S(1)} %end.1.refs_0_), channel_id=1, source_target_pairs={{2,0},{0,2},{3,1},{1,3},{6,4},{4,6},{7,5},{5,7},{10,8},{8,10},{11,... | collective-permute-start | bytes 589832 | tf_op jit(solution)/shard_map/ppermute | solution.py:275
  44.4 4.9 %collective-permute-done.9.refs_1_ = bf16[384,256]{1,0:T(8,128)(2,1)S(1)} collective-permute-done((bf16[384,256]{1,0:T(8,128)(2,1)S(1)}, bf16[384,256]{1,0:T(8,128)(2,1)S(1)}, u32[]{:S(2)}, u32[]{:S(2)}) %collective-permute-start.9) | collective-permute-done | bytes 196640 | tf_op jit(solution)/shard_map/ppermute | solution.py:275
  49.4 1.5 %update.1 = (bf16[2,384,384]{2,1,0:T(8,128)(2,1)S(1)}, bf16[384,256]{1,0:T(8,128)(2,1)S(1)}) custom-call(bf16[384,256]{1,0:T(8,128)(2,1)S(1)} %end.1.refs_0_, bf16[384,256]{1,0:T(8,128)(2,1)S(1)} %collective-permute-done.9.refs_1_, bf16[256,768]{1,0:T(8,128)(2,1)S(1)} %get-tuple-element.59.refs_2_, bf16[256,768]{1,0:T(8,128)(2,1)S(1)} %get-tuple-element.60.refs_3_, ...), custom_call_target="tpu_custom_call" | custom-call | tf_op jit(solution)/shard_map/update/pallas_call | solution.py:22
  51.8 2.3 %begin.3 = (f32[4,384,64]{2,1,0:T(8,128)S(1)}, f32[4,384,2]{2,1,0:T(8,128)S(1)}) custom-call(bf16[384,256]{1,0:T(8,128)(2,1)S(1)} %get-tuple-element.62.query, bf16[384,512]{1,0:T(8,128)(2,1)S(1)} %collective-permute-done.6.refs_0_, bf16[384,512]{1,0:T(8,128)(2,1)S(1)} %collective-permute-done.11.refs_1_), custom_call_target="tpu_custom_call" | custom-call | tf_op jit(solution)/shard_map/begin/pallas_call | solution.py:22
  54.1 5.0 %end_map.1 = (bf16[3,96,256]{2,1,0:T(8,128)(2,1)S(1)}, bf16[3,96,256]{2,1,0:T(8,128)(2,1)S(1)}) custom-call(bf16[384,256]{1,0:T(8,128)(2,1)S(1)} %get-tuple-element.62.query, bf16[384,512]{1,0:T(8,128)(2,1)S(1)} %collective-permute-done.12.refs_0_, bf16[384,512]{1,0:T(8,128)(2,1)S(1)} %collective-permute-done.13.refs_1_, ...), custom_call_target="tpu_custom_call" | custom-call | tf_op jit(solution)/shard_map/end_map/pallas_call | solution.py:22
  59.1 1.3 %collective-permute-start.14 = (bf16[3,96,256]{2,1,0:T(8,128)(2,1)S(1)}, bf16[3,96,256]{2,1,0:T(8,128)(2,1)S(1)}, u32[]{:S(2)}, u32[]{:S(2)}) collective-permute-start(bf16[3,96,256]{2,1,0:T(8,128)(2,1)S(1)} %get-tuple-element.72), channel_id=1, source_target_pairs={{2,0},{0,2},{3,1},{1,3},{6,4},{4,6},{7,5},{5,7},{10,8},{8,10},{11,... | collective-permute-start | bytes 442376 | tf_op jit(solution)/shard_map/ppermute | solution.py:275
  60.8 3.4 %collective-permute-done.14.refs_2_ = bf16[3,96,256]{2,1,0:T(8,128)(2,1)S(1)} collective-permute-done((bf16[3,96,256]{2,1,0:T(8,128)(2,1)S(1)}, bf16[3,96,256]{2,1,0:T(8,128)(2,1)S(1)}, u32[]{:S(2)}, u32[]{:S(2)}) %collective-permute-start.14) | collective-permute-done | bytes 147488 | tf_op jit(solution)/shard_map/ppermute | solution.py:275
  64.2 5.5 %collective-permute-start.15 = (bf16[3,96,256]{2,1,0:T(8,128)(2,1)S(1)}, bf16[3,96,256]{2,1,0:T(8,128)(2,1)S(1)}, u32[]{:S(2)}, u32[]{:S(2)}) collective-permute-start(bf16[3,96,256]{2,1,0:T(8,128)(2,1)S(1)} %add.5), channel_id=1, source_target_pairs={{0,0},{8,1},{4,4},{12,5},{1,8},{9,9},{5,12},{13,13},{2,2},{10,3},{... | collective-permute-start | bytes 442376 | tf_op jit(solution)/shard_map/ppermute | solution.py:393
  69.8 1.5 %collective-permute-start.16 = (bf16[1,96,256]{2,1,0:T(8,128)(2,1)S(1)}, bf16[1,96,256]{2,1,0:T(8,128)(2,1)S(1)}, u32[]{:S(2)}, u32[]{:S(2)}) collective-permute-start(bf16[1,96,256]{2,1,0:T(8,128)(2,1)S(1)} %get-tuple-element.76), channel_id=1, source_target_pairs={{0,4},{8,5},{4,8},{12,9},{1,12},{9,13},{2,6},{10,7},{6,10},{14,11}... | collective-permute-start | bytes 147464 | tf_op jit(solution)/shard_map/ppermute | solution.py:391
  71.3 2.9 %collective-permute-start.17 = (bf16[1,96,256]{2,1,0:T(8,128)(2,1)S(1)}, bf16[1,96,256]{2,1,0:T(8,128)(2,1)S(1)}, u32[]{:S(2)}, u32[]{:S(2)}) collective-permute-start(bf16[1,96,256]{2,1,0:T(8,128)(2,1)S(1)} %get-tuple-element.75), channel_id=1, source_target_pairs={{4,0},{12,1},{1,4},{9,5},{5,8},{13,9},{6,2},{14,3},{3,6},{11,7},{7... | collective-permute-start | bytes 147464 | tf_op jit(solution)/shard_map/ppermute | solution.py:392
  74.2 4.3 %collective-permute-done.17.below = bf16[1,96,256]{2,1,0:T(8,128)(2,1)S(1)} collective-permute-done((bf16[1,96,256]{2,1,0:T(8,128)(2,1)S(1)}, bf16[1,96,256]{2,1,0:T(8,128)(2,1)S(1)}, u32[]{:S(2)}, u32[]{:S(2)}) %collective-permute-start.17) | collective-permute-done | bytes 49184 | tf_op jit(solution)/shard_map/ppermute | solution.py:392
  (27 shorter events, 5.5 us)
Async XLA Ops:
  0.0 10.3 %collective-permute-start.1 = (bf16[384,384]{1,0:T(8,128)(2,1)}, bf16[384,384]{1,0:T(8,128)(2,1)S(1)}, u32[]{:S(2)}, u32[]{:S(2)}) collective-permute-start(bf16[384,384]{1,0:T(8,128)(2,1)} %bitcast.8), channel_id=1, source_target_pairs={{2,0},{0,2},{3,1},{1,3},{6,4},{4,6},{7,5},{5,7},{10,8},{8,10},{11,... | collective-permute-start | bytes 884744 | tf_op jit(solution)/shard_map/ppermute | solution.py:275
  2.0 8.3 %collective-permute-start.2 = (bf16[384,384]{1,0:T(8,128)(2,1)}, bf16[384,384]{1,0:T(8,128)(2,1)S(1)}, u32[]{:S(2)}, u32[]{:S(2)}) collective-permute-start(bf16[384,384]{1,0:T(8,128)(2,1)} %bitcast.10), channel_id=1, source_target_pairs={{2,0},{0,2},{6,4},{4,6},{11,9},{9,11},{15,13},{13,15},{18,16},{16,... | collective-permute-start | bytes 884744 | tf_op jit(solution)/shard_map/ppermute | solution.py:269
  2.7 13.9 %collective-permute-start = (bf16[384,384]{1,0:T(8,128)(2,1)}, bf16[384,384]{1,0:T(8,128)(2,1)S(1)}, u32[]{:S(2)}, u32[]{:S(2)}) collective-permute-start(bf16[384,384]{1,0:T(8,128)(2,1)} %bitcast.11), channel_id=1, source_target_pairs={{0,0},{1,8},{4,4},{5,12},{8,1},{9,9},{12,5},{13,13},{2,2},{3,10},{... | collective-permute-start | bytes 884744 | tf_op jit(solution)/shard_map/ppermute | solution.py:320
  11.2 17.1 %collective-permute-start.6 = (bf16[384,512]{1,0:T(8,128)(2,1)S(1)}, bf16[384,512]{1,0:T(8,128)(2,1)S(1)}, u32[]{:S(2)}, u32[]{:S(2)}) collective-permute-start(bf16[384,512]{1,0:T(8,128)(2,1)S(1)} %project.3), channel_id=1, source_target_pairs={{0,0},{1,8},{4,4},{5,12},{8,1},{9,9},{12,5},{13,13},{2,2},{3,10},{... | collective-permute-start | bytes 1179656 | tf_op jit(solution)/shard_map/ppermute | solution.py:329
  16.6 8.3 %collective-permute-start.3 = (bf16[384,384]{1,0:T(8,128)(2,1)S(1)}, bf16[384,384]{1,0:T(8,128)(2,1)S(1)}, u32[]{:S(2)}, u32[]{:S(2)}) collective-permute-start(bf16[384,384]{1,0:T(8,128)(2,1)S(1)} %collective-permute-done.refs_0_.refs_4_), channel_id=1, source_target_pairs={{10,8},{8,10},{14,12},{12,14},{3,1},{1,3},{7,5},{5,7},{26,24},{24,... | collective-permute-start | bytes 884744 | tf_op jit(solution)/shard_map/ppermute | solution.py:269
  19.7 8.6 %collective-permute-start.4 = (bf16[192,768]{1,0:T(8,128)(2,1)S(1)}, bf16[192,768]{1,0:T(8,128)(2,1)S(1)}, u32[]{:S(2)}, u32[]{:S(2)}) collective-permute-start(bf16[192,768]{1,0:T(8,128)(2,1)S(1)} %get-tuple-element.45), channel_id=1, source_target_pairs={{2,0},{0,2},{3,1},{1,3},{6,4},{4,6},{7,5},{5,7},{10,8},{8,10},{11,... | collective-permute-start | bytes 884744 | tf_op jit(solution)/shard_map/ppermute | solution.py:275
  28.3 6.7 %collective-permute-start.7 = (bf16[384,512]{1,0:T(8,128)(2,1)S(1)}, bf16[384,512]{1,0:T(8,128)(2,1)S(1)}, u32[]{:S(2)}, u32[]{:S(2)}) collective-permute-start(bf16[384,512]{1,0:T(8,128)(2,1)S(1)} %get-tuple-element.50.refs_0_), channel_id=1, source_target_pairs={{4,0},{0,4},{12,8},{8,12},{5,1},{1,5},{13,9},{9,13},{6,2},{2,6},{1... | collective-permute-start | bytes 1179656 | tf_op jit(solution)/shard_map/ppermute | solution.py:283
  29.9 9.8 %collective-permute-start.5 = (bf16[384,512]{1,0:T(8,128)(2,1)S(1)}, bf16[384,512]{1,0:T(8,128)(2,1)S(1)}, u32[]{:S(2)}, u32[]{:S(2)}) collective-permute-start(bf16[384,512]{1,0:T(8,128)(2,1)S(1)} %get-tuple-element.50.refs_0_), channel_id=1, source_target_pairs={{1,0},{0,1},{3,2},{2,3},{5,4},{4,5},{7,6},{6,7},{9,8},{8,9},{11,10... | collective-permute-start | bytes 1179656 | tf_op jit(solution)/shard_map/ppermute | solution.py:289
  35.1 4.6 %collective-permute-start.8 = (bf16[384,512]{1,0:T(8,128)(2,1)S(1)}, bf16[384,512]{1,0:T(8,128)(2,1)S(1)}, u32[]{:S(2)}, u32[]{:S(2)}) collective-permute-start(bf16[384,512]{1,0:T(8,128)(2,1)S(1)} %collective-permute-done.7.refs_1_), channel_id=1, source_target_pairs={{1,0},{0,1},{3,2},{2,3},{5,4},{4,5},{7,6},{6,7},{9,8},{8,9},{11,10... | collective-permute-start | bytes 1179656 | tf_op jit(solution)/shard_map/ppermute | solution.py:289
  37.4 13.5 %collective-permute-start.11 = (bf16[384,512]{1,0:T(8,128)(2,1)S(1)}, bf16[384,512]{1,0:T(8,128)(2,1)S(1)}, u32[]{:S(2)}, u32[]{:S(2)}) collective-permute-start(bf16[384,512]{1,0:T(8,128)(2,1)S(1)} %collective-permute-done.6.refs_0_), channel_id=1, source_target_pairs={{4,0},{0,4},{12,8},{8,12},{5,1},{1,5},{13,9},{9,13},{6,2},{2,6},{1... | collective-permute-start | bytes 1179656 | tf_op jit(solution)/shard_map/ppermute | solution.py:283
  38.9 5.2 %collective-permute-start.10 = (bf16[192,768]{1,0:T(8,128)(2,1)S(1)}, bf16[192,768]{1,0:T(8,128)(2,1)S(1)}, u32[]{:S(2)}, u32[]{:S(2)}) collective-permute-start(bf16[192,768]{1,0:T(8,128)(2,1)S(1)} %collective-permute-done.4.refs_0_), channel_id=1, source_target_pairs={{1,0},{0,1},{3,2},{2,3},{5,4},{4,5},{7,6},{6,7},{9,8},{8,9},{11,10... | collective-permute-start | bytes 884744 | tf_op jit(solution)/shard_map/ppermute | solution.py:289
  42.8 6.6 %collective-permute-start.9 = (bf16[384,256]{1,0:T(8,128)(2,1)S(1)}, bf16[384,256]{1,0:T(8,128)(2,1)S(1)}, u32[]{:S(2)}, u32[]{:S(2)}) collective-permute-start(bf16[384,256]{1,0:T(8,128)(2,1)S(1)} %end.1.refs_0_), channel_id=1, source_target_pairs={{2,0},{0,2},{3,1},{1,3},{6,4},{4,6},{7,5},{5,7},{10,8},{8,10},{11,... | collective-permute-start | bytes 589832 | tf_op jit(solution)/shard_map/ppermute | solution.py:275
  50.8 3.2 %collective-permute-start.12 = (bf16[384,512]{1,0:T(8,128)(2,1)S(1)}, bf16[384,512]{1,0:T(8,128)(2,1)S(1)}, u32[]{:S(2)}, u32[]{:S(2)}) collective-permute-start(bf16[384,512]{1,0:T(8,128)(2,1)S(1)} %collective-permute-done.6.refs_0_), channel_id=1, source_target_pairs={{1,0},{0,1},{3,2},{2,3},{5,4},{4,5},{7,6},{6,7},{9,8},{8,9},{11,10... | collective-permute-start | bytes 1179656 | tf_op jit(solution)/shard_map/ppermute | solution.py:289
  51.7 2.4 %collective-permute-start.13 = (bf16[384,512]{1,0:T(8,128)(2,1)S(1)}, bf16[384,512]{1,0:T(8,128)(2,1)S(1)}, u32[]{:S(2)}, u32[]{:S(2)}) collective-permute-start(bf16[384,512]{1,0:T(8,128)(2,1)S(1)} %collective-permute-done.11.refs_1_), channel_id=1, source_target_pairs={{1,0},{0,1},{3,2},{2,3},{5,4},{4,5},{7,6},{6,7},{9,8},{8,9},{11,10... | collective-permute-start | bytes 1179656 | tf_op jit(solution)/shard_map/ppermute | solution.py:289
  59.1 5.1 %collective-permute-start.14 = (bf16[3,96,256]{2,1,0:T(8,128)(2,1)S(1)}, bf16[3,96,256]{2,1,0:T(8,128)(2,1)S(1)}, u32[]{:S(2)}, u32[]{:S(2)}) collective-permute-start(bf16[3,96,256]{2,1,0:T(8,128)(2,1)S(1)} %get-tuple-element.72), channel_id=1, source_target_pairs={{2,0},{0,2},{3,1},{1,3},{6,4},{4,6},{7,5},{5,7},{10,8},{8,10},{11,... | collective-permute-start | bytes 442376 | tf_op jit(solution)/shard_map/ppermute | solution.py:275
  64.2 14.3 %collective-permute-start.15 = (bf16[3,96,256]{2,1,0:T(8,128)(2,1)S(1)}, bf16[3,96,256]{2,1,0:T(8,128)(2,1)S(1)}, u32[]{:S(2)}, u32[]{:S(2)}) collective-permute-start(bf16[3,96,256]{2,1,0:T(8,128)(2,1)S(1)} %add.5), channel_id=1, source_target_pairs={{0,0},{8,1},{4,4},{12,5},{1,8},{9,9},{5,12},{13,13},{2,2},{10,3},{... | collective-permute-start | bytes 442376 | tf_op jit(solution)/shard_map/ppermute | solution.py:393
  69.8 4.4 %collective-permute-start.16 = (bf16[1,96,256]{2,1,0:T(8,128)(2,1)S(1)}, bf16[1,96,256]{2,1,0:T(8,128)(2,1)S(1)}, u32[]{:S(2)}, u32[]{:S(2)}) collective-permute-start(bf16[1,96,256]{2,1,0:T(8,128)(2,1)S(1)} %get-tuple-element.76), channel_id=1, source_target_pairs={{0,4},{8,5},{4,8},{12,9},{1,12},{9,13},{2,6},{10,7},{6,10},{14,11}... | collective-permute-start | bytes 147464 | tf_op jit(solution)/shard_map/ppermute | solution.py:391
  71.3 7.2 %collective-permute-start.17 = (bf16[1,96,256]{2,1,0:T(8,128)(2,1)S(1)}, bf16[1,96,256]{2,1,0:T(8,128)(2,1)S(1)}, u32[]{:S(2)}, u32[]{:S(2)}) collective-permute-start(bf16[1,96,256]{2,1,0:T(8,128)(2,1)S(1)} %get-tuple-element.75), channel_id=1, source_target_pairs={{4,0},{12,1},{1,4},{9,5},{5,8},{13,9},{6,2},{14,3},{3,6},{11,7},{7... | collective-permute-start | bytes 147464 | tf_op jit(solution)/shard_map/ppermute | solution.py:392

commit v10 on v8

--- a/solution.py
+++ b/solution.py
@@ -49,19 +49,17 @@
     return jnp.dot(left, right, preferred_element_type=F32)
 
 
-def project_kernel(*refs, count, scaled, first):
+def project_kernel(*refs, count, wanted):
     pieces, weight, outs = refs[:count], refs[count], refs[count + 1 :]
     normed = normalized([piece[...] for piece in pieces])
     products = []
-    for which in range(first, weight.shape[0]):
+    for which in wanted:
         products.append(
             sum(dot(normed[step], weight[which, slot_of(step, count)]) for step in range(count))
         )
-    if scaled:
-        outs[0][...] = (products.pop(0) * QUERY_SCALE).astype(BF16)
-    columns = weight.shape[3]
-    for which, product in enumerate(products):
-        outs[-1][:, which * columns : (which + 1) * columns] = product.astype(BF16)
+    if wanted[0] == 0:
+        products[0] = products[0] * QUERY_SCALE
+    outs[0][...] = jnp.concatenate([p.astype(BF16) for p in products], axis=1)
 
 
 def attended(query, packs, state, index):
@@ -258,7 +256,6 @@
     back = [(worker(*p), home(*p)) for p in places]
     down = [(worker(b, p), home(b + 1, p)) for b, p in places if b + 1 < bands]
     up = [(worker(b, p), home(b - 1, p)) for b, p in places if b > 0]
-    stays = [home(*p) for p in places if home(*p) == worker(*p)]
     comes = [worker(*p) for p in places if home(*p) != worker(*p)]
 
     def tile_swaps(value, members, step):
@@ -293,13 +290,14 @@
     def grouped(packs):
         return packs if len(packs) < 3 else [jnp.concatenate(packs)]
 
-    def project(pieces, weights, scaled, first):
-        return run_kernel(
-            functools.partial(project_kernel, count=tiles, scaled=scaled, first=first),
+    def project(pieces, weights, wanted):
+        (projected,) = run_kernel(
+            functools.partial(project_kernel, count=tiles, wanted=wanted),
             "project",
-            [((rows, columns), BF16)] * scaled + [((rows, 2 * columns), BF16)],
+            [((rows, columns * len(wanted)), BF16)],
             [*pieces, weights.reshape(3, tiles, share, columns)],
         )
+        return projected
 
     def begin(query, packs):
         shapes = [((heads, rows, HD), F32), ((heads, rows, 2), F32)]
@@ -319,20 +317,27 @@
 
     left_here = lax.ppermute(left_tokens[0], both, there)
     steps = range(1, tiles)
-    left_early = [tile_swaps(left_tokens[0], stays, s) for s in steps]
-    self_out, reassemble, cross_out, right_own, self_qkv, cross_qkv, taps, half = staged(
-        [self_out, reassemble, cross_out, right_tokens[0], self_qkv, cross_qkv, taps]
-    )
-    right = [right_own, *[from_tile(right_tokens[0], s) for s in steps]]
-    (right_pack,) = project(right, cross_qkv, False, 1)
+    left_home = [from_tile(left_tokens[0], s) for s in steps]
+    right = [from_tile(right_tokens[0], s) for s in steps]
+    self_out, reassemble, cross_out, left_own, right_own, self_qkv, cross_qkv, taps, half = staged(
+        [self_out, reassemble, cross_out, left_tokens[0], right_tokens[0], self_qkv, cross_qkv, taps]
+    )
+    pack = project([left_own, *left_home], self_qkv, (1, 2))
+    right = tied([right_own, *right], pack)
+    right_pack = project(right, cross_qkv, (1, 2))
+    pack = lax.ppermute(pack, both, there)
     left_here, right_pack = lax.optimization_barrier((left_here, right_pack))
     right_pack = lax.ppermute(right_pack, both, there)
-    left_late = [tile_swaps(left_here, comes, s) for s in steps]
-    left = [left_here, *[a + b for a, b in zip(left_early, left_late)]]
-    query, pack = project(left, self_qkv, True, 0)
+    settled = lax.axis_index("pair") == lax.axis_index("blk") // span
+    left = [left_here]
+    for step, early in zip(steps, left_home):
+        left.append(jnp.where(settled, early, tile_swaps(left_here, comes, step)))
+    query = project(left, self_qkv, (0,))
+    halves = tile_pieces(half)[1:]
     beside = neighbours(pack)
-    halves = tile_pieces(tied(half, left))[1:]
-    near, halves, right_pack = lax.optimization_barrier(([pack, *beside], halves, right_pack))
+    near, right_pack, query, halves = lax.optimization_barrier(
+        ([pack, *beside], right_pack, query, halves)
+    )
     far = [q for p in near for q in across(p)]
     state = begin(query, near)
     right_pack = tied(right_pack, state)

time: 79.3 us -> 86.8 us (1.095)
  waiting for transfers between devices: 31.5 us -> 25.4 us
  starting transfers between devices: 26.8 us -> 32.4 us
  Pallas kernels: 20.4 us -> 25.5 us
  local copies, waits for them, and re-layouts: 0.01 us -> 1.78 us
  other arithmetic: 0.07 us -> 1 us
    ppermute x2 -> x1, waiting for transfers between devices: 5.63 us -> 0.01 us  [tile_swaps(): return lax.ppermute(value, ('blk', 'tile', 'pair'), pairs)]
    pallas_call x13 -> x14, Pallas kernels: 20.4 us -> 25.5 us  [run_kernel(): pl.pallas_call(kernel, out_shape=[jax.ShapeDtypeStruct(*s) for s in shape...]
    ppermute x1, waiting for transfers between devices: 3.65 us -> 0.01 us  [body(): left_here = lax.ppermute(left_tokens[0], both, there)]
    ppermute x1, waiting for transfers between devices: 4.23 us -> 0.81 us  [body(): right_pack = lax.ppermute(right_pack, both, there)]
    ppermute x0 -> x1, starting transfers between devices: none -> 2.97 us  [body(): pack = lax.ppermute(pack, both, there)]
    ppermute x4 -> x5, waiting for transfers between devices: 10.8 us -> 13.4 us  [from_tile(): lax.ppermute(value, 'tile', [((i + step) % tiles, i) for i in range(tiles)])]
    ppermute x0 -> x1, waiting for transfers between devices: none -> 2.07 us  [body(): pack = lax.ppermute(pack, both, there)]
    unnamed x0 -> x8, local copies, waits for them, and re-layouts: none -> 1.78 us
  transfers between devices with their start and end apart: 18 -> 19, of which waited for: 8 -> 7; matrix products, arithmetic and copies ran while one was open for 0% -> 1% of each run, Pallas kernels for 18% -> 22%
where the time goes in v10:
time: 86.8 us; the launch traced here: 86.3 us
  starting transfers between devices  32.4 us (37%)
  Pallas kernels  25.5 us (29%)
  waiting for transfers between devices  25.4 us (29%)
  local copies, waits for them, and re-layouts  1.78 us (2%)
  other arithmetic  1 us (1%)
    pallas_call x14, Pallas kernels, run_kernel(): pl.pallas_call(kernel, out_shape=[jax.ShapeDtypeStruct(*s) for s in shape...  25.5 us
    ppermute x5, waiting for transfers between devices, from_tile(): lax.ppermute(value, 'tile', [((i + step) % tiles, i) for i in range(tiles)])  13.4 us
    ppermute x1, starting transfers between devices, body(): left_here = lax.ppermute(left_tokens[0], both, there)  5.55 us
    ppermute x1, waiting for transfers between devices, body(): below = lax.ppermute(features[:1], both, up)  5.02 us
    ppermute x1, starting transfers between devices, body(): features = lax.ppermute(features, both, back)  4.7 us
    ppermute x1, starting transfers between devices, body(): right_pack = lax.ppermute(right_pack, both, there)  4.58 us
    ppermute x5, starting transfers between devices, from_tile(): lax.ppermute(value, 'tile', [((i + step) % tiles, i) for i in range(tiles)])  4.34 us
    ppermute x2, waiting for transfers between devices, neighbours(): lax.ppermute(pack, 'blk', [(g + (i + s) % span, g + i) for g, i in ring])  4.11 us
  transfers between devices with their start and end apart: 19, of which 7 were waited for; matrix products, arithmetic and copies ran while one was open for 1% of the time, Pallas kernels for 22%

profile of v10, /device:TPU:1, one launch (start us, length us, event | category | flops | bytes accessed | tf_op | source)
XLA Modules:
  0.0 86.3 jit_solution(692694428694753831)
XLA Ops:
  0.0 2.0 %collective-permute-start = (bf16[384,384]{1,0:T(8,128)(2,1)}, bf16[384,384]{1,0:T(8,128)(2,1)S(1)}, u32[]{:S(2)}, u32[]{:S(2)}) collective-permute-start(bf16[384,384]{1,0:T(8,128)(2,1)} %bitcast.11), channel_id=1, source_target_pairs={{2,0},{0,2},{3,1},{1,3},{6,4},{4,6},{7,5},{5,7},{10,8},{8,10},{11,... | collective-permute-start | bytes 884744 | tf_op jit(solution)/shard_map/ppermute | solution.py:272
  2.1 5.5 %collective-permute-start.3 = (bf16[384,384]{1,0:T(8,128)(2,1)}, bf16[384,384]{1,0:T(8,128)(2,1)S(1)}, u32[]{:S(2)}, u32[]{:S(2)}) collective-permute-start(bf16[384,384]{1,0:T(8,128)(2,1)} %bitcast.12), channel_id=1, source_target_pairs={{0,0},{1,8},{4,4},{5,12},{8,1},{9,9},{12,5},{13,13},{2,2},{3,10},{... | collective-permute-start | bytes 884744 | tf_op jit(solution)/shard_map/ppermute | solution.py:318
  7.6 3.3 %stage.1 = (bf16[256,768]{1,0:T(8,128)(2,1)S(1)}, bf16[384,256]{1,0:T(8,128)(2,1)S(1)}, bf16[256,768]{1,0:T(8,128)(2,1)S(1)}, bf16[384,384]{1,0:T(8,128)(2,1)S(1...) custom-call(bf16[256,768]{1,0:T(8,128)(2,1)} %refs_0_.1, ...), custom_call_target="tpu_custom_call" | custom-call | tf_op jit(solution)/shard_map/stage/pallas_call | solution.py:22
  13.6 3.0 %collective-permute-start.1 = (bf16[384,512]{1,0:T(8,128)(2,1)S(1)}, bf16[384,512]{1,0:T(8,128)(2,1)}, u32[]{:S(2)}, u32[]{:S(2)}) collective-permute-start(bf16[384,512]{1,0:T(8,128)(2,1)S(1)} %project.3), channel_id=1, source_target_pairs={{0,0},{1,8},{4,4},{5,12},{8,1},{9,9},{12,5},{13,13},{2,2},{3,10},{... | collective-permute-start | bytes 1179656 | tf_op jit(solution)/shard_map/ppermute | solution.py:328
  16.6 1.6 %project.4 = bf16[384,512]{1,0:T(8,128)(2,1)} custom-call(bf16[384,384]{1,0:T(8,128)(2,1)S(1)} %get-tuple-element.45.refs_0_, bf16[384,384]{1,0:T(8,128)(2,1)S(1)} %collective-permute-done.4.refs_1_, bf16[3,2,384,256]{3,2,1,0:T(8,128)(2,1)S(1)} %bitcast.7), custom_call_target="tpu_custom_call" | custom-call | tf_op jit(solution)/shard_map/project/pallas_call | solution.py:22
  18.2 3.1 %collective-permute-start.6 = (bf16[384,384]{1,0:T(8,128)(2,1)S(1)}, bf16[384,384]{1,0:T(8,128)(2,1)}, u32[]{:S(2)}, u32[]{:S(2)}) collective-permute-start(bf16[384,384]{1,0:T(8,128)(2,1)S(1)} %collective-permute-done.3.refs_0_.refs_4_), channel_id=1, source_target_pairs={{10,8},{8,10},{14,12},{12,14},{3,1},{1,3},{7,5},{5,7},{26,24},{24,... | collective-permute-start | bytes 884744 | tf_op jit(solution)/shard_map/ppermute | solution.py:266
  21.3 4.6 %collective-permute-start.5 = (bf16[384,512]{1,0:T(8,128)(2,1)}, bf16[384,512]{1,0:T(8,128)(2,1)}, u32[]{:S(2)}, u32[]{:S(2)}) collective-permute-start(bf16[384,512]{1,0:T(8,128)(2,1)} %project.4), channel_id=1, source_target_pairs={{0,0},{1,8},{4,4},{5,12},{8,1},{9,9},{12,5},{13,13},{2,2},{3,10},{... | collective-permute-start | bytes 1179656 | tf_op jit(solution)/shard_map/ppermute | solution.py:330
  25.9 2.1 %collective-permute-done.1.refs_0_ = bf16[384,512]{1,0:T(8,128)(2,1)} collective-permute-done((bf16[384,512]{1,0:T(8,128)(2,1)S(1)}, bf16[384,512]{1,0:T(8,128)(2,1)}, u32[]{:S(2)}, u32[]{:S(2)}) %collective-permute-start.1) | collective-permute-done | bytes 393248 | tf_op jit(solution)/shard_map/ppermute | solution.py:328
  28.0 1.5 %collective-permute-start.7 = (bf16[192,768]{1,0:T(8,128)(2,1)}, bf16[192,768]{1,0:T(8,128)(2,1)}, u32[]{:S(2)}, u32[]{:S(2)}) collective-permute-start(bf16[192,768]{1,0:T(8,128)(2,1)} %get-tuple-element.50), channel_id=1, source_target_pairs={{2,0},{0,2},{3,1},{1,3},{6,4},{4,6},{7,5},{5,7},{10,8},{8,10},{11,... | collective-permute-start | bytes 884744 | tf_op jit(solution)/shard_map/ppermute | solution.py:272
  31.2 4.5 %collective-permute-done.7.refs_0_ = bf16[192,768]{1,0:T(8,128)(2,1)} collective-permute-done((bf16[192,768]{1,0:T(8,128)(2,1)}, bf16[192,768]{1,0:T(8,128)(2,1)}, u32[]{:S(2)}, u32[]{:S(2)}) %collective-permute-start.7) | collective-permute-done | bytes 294944 | tf_op jit(solution)/shard_map/ppermute | solution.py:272
  36.4 4.1 %collective-permute-done.2.refs_1_ = bf16[384,512]{1,0:T(8,128)(2,1)} collective-permute-done((bf16[384,512]{1,0:T(8,128)(2,1)}, bf16[384,512]{1,0:T(8,128)(2,1)}, u32[]{:S(2)}, u32[]{:S(2)}) %collective-permute-start.2) | collective-permute-done | bytes 393248 | tf_op jit(solution)/shard_map/ppermute | solution.py:280
  41.1 3.4 %begin.2 = (f32[4,384,64]{2,1,0:T(8,128)S(1)}, f32[4,384,2]{2,1,0:T(8,128)S(1)}) custom-call(bf16[384,256]{1,0:T(8,128)(2,1)S(1)} %project.5.query, bf16[384,512]{1,0:T(8,128)(2,1)} %collective-permute-done.1.refs_0_, bf16[384,512]{1,0:T(8,128)(2,1)} %collective-permute-done.2.refs_1_), custom_call_target="tpu_custom_call" | custom-call | tf_op jit(solution)/shard_map/begin/pallas_call | solution.py:22
  45.5 3.1 %end.1.refs_0_ = bf16[384,256]{1,0:T(8,128)(2,1)S(1)} custom-call(bf16[384,256]{1,0:T(8,128)(2,1)S(1)} %project.5.query, bf16[384,512]{1,0:T(8,128)(2,1)S(1)} %collective-permute-done.8.refs_0_, bf16[384,512]{1,0:T(8,128)(2,1)S(1)} %collective-permute-done.9.refs_1_, f32[4,384,64]{2,1,0:T(8,128)S(1)} %get-tuple-element.54.refs_2_, ...), custom_call_target="tpu_custom_call" | custom-call | tf_op jit(solution)/shard_map/end/pallas_call | solution.py:22
  50.4 4.6 %collective-permute-done.10.refs_1_ = bf16[384,256]{1,0:T(8,128)(2,1)S(1)} collective-permute-done((bf16[384,256]{1,0:T(8,128)(2,1)S(1)}, bf16[384,256]{1,0:T(8,128)(2,1)S(1)}, u32[]{:S(2)}, u32[]{:S(2)}) %collective-permute-start.10) | collective-permute-done | bytes 196640 | tf_op jit(solution)/shard_map/ppermute | solution.py:272
  55.0 1.5 %update.1 = (bf16[2,384,384]{2,1,0:T(8,128)(2,1)S(1)}, bf16[384,256]{1,0:T(8,128)(2,1)S(1)}) custom-call(bf16[384,256]{1,0:T(8,128)(2,1)S(1)} %end.1.refs_0_, bf16[384,256]{1,0:T(8,128)(2,1)S(1)} %collective-permute-done.10.refs_1_, bf16[256,768]{1,0:T(8,128)(2,1)S(1)} %copy-done.3, bf16[256,768]{1,0:T(8,128)(2,1)S(1)} %get-tuple-element.63.refs_3_, ...), custom_call_target="tpu_custom_call" | custom-call | tf_op jit(solution)/shard_map/update/pallas_call | solution.py:22
  56.5 1.1 %collective-permute-start.13 = (bf16[384,512]{1,0:T(8,128)(2,1)}, bf16[384,512]{1,0:T(8,128)(2,1)S(1)}, u32[]{:S(2)}, u32[]{:S(2)}) collective-permute-start(bf16[384,512]{1,0:T(8,128)(2,1)} %collective-permute-done.5.refs_0_), channel_id=1, source_target_pairs={{1,0},{0,1},{3,2},{2,3},{5,4},{4,5},{7,6},{6,7},{9,8},{8,9},{11,10... | collective-permute-start | bytes 1179656 | tf_op jit(solution)/shard_map/ppermute | solution.py:286
  57.7 3.3 %begin.3 = (f32[4,384,64]{2,1,0:T(8,128)S(1)}, f32[4,384,2]{2,1,0:T(8,128)S(1)}) custom-call(bf16[384,256]{1,0:T(8,128)(2,1)S(1)} %get-tuple-element.65.query, bf16[384,512]{1,0:T(8,128)(2,1)} %collective-permute-done.5.refs_0_, bf16[384,512]{1,0:T(8,128)(2,1)S(1)} %collective-permute-done.12.refs_1_), custom_call_target="tpu_custom_call" | custom-call | tf_op jit(solution)/shard_map/begin/pallas_call | solution.py:22
  61.0 5.0 %end_map.1 = (bf16[3,96,256]{2,1,0:T(8,128)(2,1)S(1)}, bf16[3,96,256]{2,1,0:T(8,128)(2,1)S(1)}) custom-call(bf16[384,256]{1,0:T(8,128)(2,1)S(1)} %get-tuple-element.65.query, bf16[384,512]{1,0:T(8,128)(2,1)S(1)} %collective-permute-done.13.refs_0_, bf16[384,512]{1,0:T(8,128)(2,1)S(1)} %collective-permute-done.14.refs_1_, ...), custom_call_target="tpu_custom_call" | custom-call | tf_op jit(solution)/shard_map/end_map/pallas_call | solution.py:22
  66.7 4.3 %collective-permute-done.15.refs_2_ = bf16[3,96,256]{2,1,0:T(8,128)(2,1)S(1)} collective-permute-done((bf16[3,96,256]{2,1,0:T(8,128)(2,1)S(1)}, bf16[3,96,256]{2,1,0:T(8,128)(2,1)S(1)}, u32[]{:S(2)}, u32[]{:S(2)}) %collective-permute-start.15) | collective-permute-done | bytes 147488 | tf_op jit(solution)/shard_map/ppermute | solution.py:272
  71.1 4.7 %collective-permute-start.16 = (bf16[3,96,256]{2,1,0:T(8,128)(2,1)S(1)}, bf16[3,96,256]{2,1,0:T(8,128)(2,1)S(1)}, u32[]{:S(2)}, u32[]{:S(2)}) collective-permute-start(bf16[3,96,256]{2,1,0:T(8,128)(2,1)S(1)} %add.2), channel_id=1, source_target_pairs={{0,0},{8,1},{4,4},{12,5},{1,8},{9,9},{5,12},{13,13},{2,2},{10,3},{... | collective-permute-start | bytes 442376 | tf_op jit(solution)/shard_map/ppermute | solution.py:397
  75.8 2.2 %collective-permute-start.17 = (bf16[1,96,256]{2,1,0:T(8,128)(2,1)S(1)}, bf16[1,96,256]{2,1,0:T(8,128)(2,1)S(1)}, u32[]{:S(2)}, u32[]{:S(2)}) collective-permute-start(bf16[1,96,256]{2,1,0:T(8,128)(2,1)S(1)} %get-tuple-element.80), channel_id=1, source_target_pairs={{0,4},{8,5},{4,8},{12,9},{1,12},{9,13},{2,6},{10,7},{6,10},{14,11}... | collective-permute-start | bytes 147464 | tf_op jit(solution)/shard_map/ppermute | solution.py:395
  78.0 2.2 %collective-permute-start.18 = (bf16[1,96,256]{2,1,0:T(8,128)(2,1)S(1)}, bf16[1,96,256]{2,1,0:T(8,128)(2,1)S(1)}, u32[]{:S(2)}, u32[]{:S(2)}) collective-permute-start(bf16[1,96,256]{2,1,0:T(8,128)(2,1)S(1)} %get-tuple-element.79), channel_id=1, source_target_pairs={{4,0},{12,1},{1,4},{9,5},{5,8},{13,9},{6,2},{14,3},{3,6},{11,7},{7... | collective-permute-start | bytes 147464 | tf_op jit(solution)/shard_map/ppermute | solution.py:396
  80.2 5.0 %collective-permute-done.18.below = bf16[1,96,256]{2,1,0:T(8,128)(2,1)S(1)} collective-permute-done((bf16[1,96,256]{2,1,0:T(8,128)(2,1)S(1)}, bf16[1,96,256]{2,1,0:T(8,128)(2,1)S(1)}, u32[]{:S(2)}, u32[]{:S(2)}) %collective-permute-start.18) | collective-permute-done | bytes 49184 | tf_op jit(solution)/shard_map/ppermute | solution.py:396
  85.2 1.0 %join.1 = bf16[3,64,256]{2,1,0:T(8,128)(2,1)} custom-call(bf16[3,96,256]{2,1,0:T(8,128)(2,1)S(1)} %collective-permute-done.16.window, bf16[1,96,256]{2,1,0:T(8,128)(2,1)S(1)} %collective-permute-done.17.above, bf16[1,96,256]{2,1,0:T(8,128)(2,1)S(1)} %collective-permute-done.18.below, bf16[3,3,256,256]{3,2,1,0:T(8,128)(2,1)S(1)} %copy-done.1), custom_call_target="tpu_custom_call" | custom-call | tf_op jit(solution)/shard_map/join/pallas_call | solution.py:22
  (38 shorter events, 9.3 us)
Async XLA Ops:
  0.0 12.7 %collective-permute-start = (bf16[384,384]{1,0:T(8,128)(2,1)}, bf16[384,384]{1,0:T(8,128)(2,1)S(1)}, u32[]{:S(2)}, u32[]{:S(2)}) collective-permute-start(bf16[384,384]{1,0:T(8,128)(2,1)} %bitcast.11), channel_id=1, source_target_pairs={{2,0},{0,2},{3,1},{1,3},{6,4},{4,6},{7,5},{5,7},{10,8},{8,10},{11,... | collective-permute-start | bytes 884744 | tf_op jit(solution)/shard_map/ppermute | solution.py:272
  2.0 14.5 %collective-permute-start.4 = (bf16[384,384]{1,0:T(8,128)(2,1)}, bf16[384,384]{1,0:T(8,128)(2,1)S(1)}, u32[]{:S(2)}, u32[]{:S(2)}) collective-permute-start(bf16[384,384]{1,0:T(8,128)(2,1)} %bitcast.9), channel_id=1, source_target_pairs={{2,0},{0,2},{3,1},{1,3},{6,4},{4,6},{7,5},{5,7},{10,8},{8,10},{11,... | collective-permute-start | bytes 884744 | tf_op jit(solution)/shard_map/ppermute | solution.py:272
  2.1 16.1 %collective-permute-start.3 = (bf16[384,384]{1,0:T(8,128)(2,1)}, bf16[384,384]{1,0:T(8,128)(2,1)S(1)}, u32[]{:S(2)}, u32[]{:S(2)}) collective-permute-start(bf16[384,384]{1,0:T(8,128)(2,1)} %bitcast.12), channel_id=1, source_target_pairs={{0,0},{1,8},{4,4},{5,12},{8,1},{9,9},{12,5},{13,13},{2,2},{3,10},{... | collective-permute-start | bytes 884744 | tf_op jit(solution)/shard_map/ppermute | solution.py:318
  11.0 1.0 %copy-start = (bf16[3,3,256,256]{3,2,1,0:T(8,128)(2,1)}, bf16[3,3,256,256]{3,2,1,0:T(8,128)(2,1)S(1)}, u32[]{:S(2)}) copy-start(bf16[3,3,256,256]{3,2,1,0:T(8,128)(2,1)S(1)} %get-tuple-element.78.weight) | copy-start | bytes 3538948
  12.0 0.7 copy-start.2
  13.6 14.4 %collective-permute-start.1 = (bf16[384,512]{1,0:T(8,128)(2,1)S(1)}, bf16[384,512]{1,0:T(8,128)(2,1)}, u32[]{:S(2)}, u32[]{:S(2)}) collective-permute-start(bf16[384,512]{1,0:T(8,128)(2,1)S(1)} %project.3), channel_id=1, source_target_pairs={{0,0},{1,8},{4,4},{5,12},{8,1},{9,9},{12,5},{13,13},{2,2},{3,10},{... | collective-permute-start | bytes 1179656 | tf_op jit(solution)/shard_map/ppermute | solution.py:328
  18.2 11.3 %collective-permute-start.6 = (bf16[384,384]{1,0:T(8,128)(2,1)S(1)}, bf16[384,384]{1,0:T(8,128)(2,1)}, u32[]{:S(2)}, u32[]{:S(2)}) collective-permute-start(bf16[384,384]{1,0:T(8,128)(2,1)S(1)} %collective-permute-done.3.refs_0_.refs_4_), channel_id=1, source_target_pairs={{10,8},{8,10},{14,12},{12,14},{3,1},{1,3},{7,5},{5,7},{26,24},{24,... | collective-permute-start | bytes 884744 | tf_op jit(solution)/shard_map/ppermute | solution.py:266
  21.3 15.1 %collective-permute-start.5 = (bf16[384,512]{1,0:T(8,128)(2,1)}, bf16[384,512]{1,0:T(8,128)(2,1)}, u32[]{:S(2)}, u32[]{:S(2)}) collective-permute-start(bf16[384,512]{1,0:T(8,128)(2,1)} %project.4), channel_id=1, source_target_pairs={{0,0},{1,8},{4,4},{5,12},{8,1},{9,9},{12,5},{13,13},{2,2},{3,10},{... | collective-permute-start | bytes 1179656 | tf_op jit(solution)/shard_map/ppermute | solution.py:330
  28.0 12.6 %collective-permute-start.2 = (bf16[384,512]{1,0:T(8,128)(2,1)}, bf16[384,512]{1,0:T(8,128)(2,1)}, u32[]{:S(2)}, u32[]{:S(2)}) collective-permute-start(bf16[384,512]{1,0:T(8,128)(2,1)} %collective-permute-done.1.refs_0_), channel_id=1, source_target_pairs={{4,0},{0,4},{12,8},{8,12},{5,1},{1,5},{13,9},{9,13},{6,2},{2,6},{1... | collective-permute-start | bytes 1179656 | tf_op jit(solution)/shard_map/ppermute | solution.py:280
  28.0 7.6 %collective-permute-start.7 = (bf16[192,768]{1,0:T(8,128)(2,1)}, bf16[192,768]{1,0:T(8,128)(2,1)}, u32[]{:S(2)}, u32[]{:S(2)}) collective-permute-start(bf16[192,768]{1,0:T(8,128)(2,1)} %get-tuple-element.50), channel_id=1, source_target_pairs={{2,0},{0,2},{3,1},{1,3},{6,4},{4,6},{7,5},{5,7},{10,8},{8,10},{11,... | collective-permute-start | bytes 884744 | tf_op jit(solution)/shard_map/ppermute | solution.py:272
  40.6 5.0 %collective-permute-start.8 = (bf16[384,512]{1,0:T(8,128)(2,1)}, bf16[384,512]{1,0:T(8,128)(2,1)S(1)}, u32[]{:S(2)}, u32[]{:S(2)}) collective-permute-start(bf16[384,512]{1,0:T(8,128)(2,1)} %collective-permute-done.1.refs_0_), channel_id=1, source_target_pairs={{1,0},{0,1},{3,2},{2,3},{5,4},{4,5},{7,6},{6,7},{9,8},{8,9},{11,10... | collective-permute-start | bytes 1179656 | tf_op jit(solution)/shard_map/ppermute | solution.py:286
  40.6 5.0 %collective-permute-start.9 = (bf16[384,512]{1,0:T(8,128)(2,1)}, bf16[384,512]{1,0:T(8,128)(2,1)S(1)}, u32[]{:S(2)}, u32[]{:S(2)}) collective-permute-start(bf16[384,512]{1,0:T(8,128)(2,1)} %collective-permute-done.2.refs_1_), channel_id=1, source_target_pairs={{1,0},{0,1},{3,2},{2,3},{5,4},{4,5},{7,6},{6,7},{9,8},{8,9},{11,10... | collective-permute-start | bytes 1179656 | tf_op jit(solution)/shard_map/ppermute | solution.py:286
  44.5 12.0 %collective-permute-start.12 = (bf16[384,512]{1,0:T(8,128)(2,1)}, bf16[384,512]{1,0:T(8,128)(2,1)S(1)}, u32[]{:S(2)}, u32[]{:S(2)}) collective-permute-start(bf16[384,512]{1,0:T(8,128)(2,1)} %collective-permute-done.5.refs_0_), channel_id=1, source_target_pairs={{4,0},{0,4},{12,8},{8,12},{5,1},{1,5},{13,9},{9,13},{6,2},{2,6},{1... | collective-permute-start | bytes 1179656 | tf_op jit(solution)/shard_map/ppermute | solution.py:280
  45.2 3.8 %collective-permute-start.11 = (bf16[192,768]{1,0:T(8,128)(2,1)}, bf16[192,768]{1,0:T(8,128)(2,1)S(1)}, u32[]{:S(2)}, u32[]{:S(2)}) collective-permute-start(bf16[192,768]{1,0:T(8,128)(2,1)} %collective-permute-done.7.refs_0_), channel_id=1, source_target_pairs={{1,0},{0,1},{3,2},{2,3},{5,4},{4,5},{7,6},{6,7},{9,8},{8,9},{11,10... | collective-permute-start | bytes 884744 | tf_op jit(solution)/shard_map/ppermute | solution.py:286
  48.7 6.4 %copy-start.3 = (bf16[256,768]{1,0:T(8,128)(2,1)S(1)}, bf16[256,768]{1,0:T(8,128)(2,1)}, u32[]{:S(2)}) copy-start(bf16[256,768]{1,0:T(8,128)(2,1)} %copy-done.2) | copy-start | bytes 1179652
  48.7 6.4 %collective-permute-start.10 = (bf16[384,256]{1,0:T(8,128)(2,1)S(1)}, bf16[384,256]{1,0:T(8,128)(2,1)S(1)}, u32[]{:S(2)}, u32[]{:S(2)}) collective-permute-start(bf16[384,256]{1,0:T(8,128)(2,1)S(1)} %end.1.refs_0_), channel_id=1, source_target_pairs={{2,0},{0,2},{3,1},{1,3},{6,4},{4,6},{7,5},{5,7},{10,8},{8,10},{11,... | collective-permute-start | bytes 589832 | tf_op jit(solution)/shard_map/ppermute | solution.py:272
  56.5 4.5 %collective-permute-start.13 = (bf16[384,512]{1,0:T(8,128)(2,1)}, bf16[384,512]{1,0:T(8,128)(2,1)S(1)}, u32[]{:S(2)}, u32[]{:S(2)}) collective-permute-start(bf16[384,512]{1,0:T(8,128)(2,1)} %collective-permute-done.5.refs_0_), channel_id=1, source_target_pairs={{1,0},{0,1},{3,2},{2,3},{5,4},{4,5},{7,6},{6,7},{9,8},{8,9},{11,10... | collective-permute-start | bytes 1179656 | tf_op jit(solution)/shard_map/ppermute | solution.py:286
  57.6 3.4 %collective-permute-start.14 = (bf16[384,512]{1,0:T(8,128)(2,1)S(1)}, bf16[384,512]{1,0:T(8,128)(2,1)S(1)}, u32[]{:S(2)}, u32[]{:S(2)}) collective-permute-start(bf16[384,512]{1,0:T(8,128)(2,1)S(1)} %collective-permute-done.12.refs_1_), channel_id=1, source_target_pairs={{1,0},{0,1},{3,2},{2,3},{5,4},{4,5},{7,6},{6,7},{9,8},{8,9},{11,10... | collective-permute-start | bytes 1179656 | tf_op jit(solution)/shard_map/ppermute | solution.py:286
  66.0 19.3 %copy-start.1 = (bf16[3,3,256,256]{3,2,1,0:T(8,128)(2,1)S(1)}, bf16[3,3,256,256]{3,2,1,0:T(8,128)(2,1)}, u32[]{:S(2)}) copy-start(bf16[3,3,256,256]{3,2,1,0:T(8,128)(2,1)} %copy-done) | copy-start | bytes 3538948
  66.0 5.1 %collective-permute-start.15 = (bf16[3,96,256]{2,1,0:T(8,128)(2,1)S(1)}, bf16[3,96,256]{2,1,0:T(8,128)(2,1)S(1)}, u32[]{:S(2)}, u32[]{:S(2)}) collective-permute-start(bf16[3,96,256]{2,1,0:T(8,128)(2,1)S(1)} %get-tuple-element.76), channel_id=1, source_target_pairs={{2,0},{0,2},{3,1},{1,3},{6,4},{4,6},{7,5},{5,7},{10,8},{8,10},{11,... | collective-permute-start | bytes 442376 | tf_op jit(solution)/shard_map/ppermute | solution.py:272
  71.1 14.2 %collective-permute-start.16 = (bf16[3,96,256]{2,1,0:T(8,128)(2,1)S(1)}, bf16[3,96,256]{2,1,0:T(8,128)(2,1)S(1)}, u32[]{:S(2)}, u32[]{:S(2)}) collective-permute-start(bf16[3,96,256]{2,1,0:T(8,128)(2,1)S(1)} %add.2), channel_id=1, source_target_pairs={{0,0},{8,1},{4,4},{12,5},{1,8},{9,9},{5,12},{13,13},{2,2},{10,3},{... | collective-permute-start | bytes 442376 | tf_op jit(solution)/shard_map/ppermute | solution.py:397
  75.8 4.4 %collective-permute-start.17 = (bf16[1,96,256]{2,1,0:T(8,128)(2,1)S(1)}, bf16[1,96,256]{2,1,0:T(8,128)(2,1)S(1)}, u32[]{:S(2)}, u32[]{:S(2)}) collective-permute-start(bf16[1,96,256]{2,1,0:T(8,128)(2,1)S(1)} %get-tuple-element.80), channel_id=1, source_target_pairs={{0,4},{8,5},{4,8},{12,9},{1,12},{9,13},{2,6},{10,7},{6,10},{14,11}... | collective-permute-start | bytes 147464 | tf_op jit(solution)/shard_map/ppermute | solution.py:395
  78.0 7.2 %collective-permute-start.18 = (bf16[1,96,256]{2,1,0:T(8,128)(2,1)S(1)}, bf16[1,96,256]{2,1,0:T(8,128)(2,1)S(1)}, u32[]{:S(2)}, u32[]{:S(2)}) collective-permute-start(bf16[1,96,256]{2,1,0:T(8,128)(2,1)S(1)} %get-tuple-element.79), channel_id=1, source_target_pairs={{4,0},{12,1},{1,4},{9,5},{5,8},{13,9},{6,2},{14,3},{3,6},{11,7},{7... | collective-permute-start | bytes 147464 | tf_op jit(solution)/shard_map/ppermute | solution.py:396

commit v11 on v8

--- a/solution.py
+++ b/solution.py
@@ -49,9 +49,16 @@
     return jnp.dot(left, right, preferred_element_type=F32)
 
 
-def project_kernel(*refs, count, scaled, first):
-    pieces, weight, outs = refs[:count], refs[count], refs[count + 1 :]
-    normed = normalized([piece[...] for piece in pieces])
+def project_kernel(*refs, count, pairs, scaled, first):
+    pieces = [piece[...] for piece in refs[:count]]
+    weight, outs = refs[count + pairs], refs[count + pairs + 1 :]
+    for index in range(pairs):
+        place = count - pairs + index
+        pieces[place] = pieces[place] + refs[count + index][...]
+    normed = normalized(pieces)
+    if scaled:
+        for out, piece in zip(outs[2:], pieces[1:]):
+            out[...] = piece
     products = []
     for which in range(first, weight.shape[0]):
         products.append(
@@ -61,7 +68,7 @@
         outs[0][...] = (products.pop(0) * QUERY_SCALE).astype(BF16)
     columns = weight.shape[3]
     for which, product in enumerate(products):
-        outs[-1][:, which * columns : (which + 1) * columns] = product.astype(BF16)
+        outs[scaled][:, which * columns : (which + 1) * columns] = product.astype(BF16)
 
 
 def attended(query, packs, state, index):
@@ -277,6 +284,13 @@
     def tile_pieces(own):
         return [own, *[from_tile(own, s) for s in range(1, tiles)]]
 
+    def beside_swaps(value, members, step):
+        def source(member):
+            band, core = member // cores, member % cores
+            return (band // span * span + (band % span + step) % span) * cores + core
+
+        return lax.ppermute(value, both, [(source(m), m) for m in members])
+
     def neighbours(pack):
         ring = [(g * span, i) for g in range(cores) for i in range(span)]
         return [
@@ -293,12 +307,15 @@
     def grouped(packs):
         return packs if len(packs) < 3 else [jnp.concatenate(packs)]
 
-    def project(pieces, weights, scaled, first):
+    def project(pieces, weights, scaled, first, pairs=()):
+        shapes = [((rows, columns), BF16)] * scaled + [((rows, 2 * columns), BF16)]
         return run_kernel(
-            functools.partial(project_kernel, count=tiles, scaled=scaled, first=first),
+            functools.partial(
+                project_kernel, count=tiles, pairs=len(pairs), scaled=scaled, first=first
+            ),
             "project",
-            [((rows, columns), BF16)] * scaled + [((rows, 2 * columns), BF16)],
-            [*pieces, weights.reshape(3, tiles, share, columns)],
+            shapes + [((rows, share), BF16)] * (scaled * (tiles - 1)),
+            [*pieces, *pairs, weights.reshape(3, tiles, share, columns)],
         )
 
     def begin(query, packs):
@@ -317,26 +334,43 @@
             pl.BlockSpec(memory_space=pl.ANY),
         )
 
+    steps, hops = range(1, tiles), range(1, span)
     left_here = lax.ppermute(left_tokens[0], both, there)
-    steps = range(1, tiles)
+    beside_early = [beside_swaps(left_tokens[0], stays, s) for s in hops]
     left_early = [tile_swaps(left_tokens[0], stays, s) for s in steps]
     self_out, reassemble, cross_out, right_own, self_qkv, cross_qkv, taps, half = staged(
         [self_out, reassemble, cross_out, right_tokens[0], self_qkv, cross_qkv, taps]
     )
     right = [right_own, *[from_tile(right_tokens[0], s) for s in steps]]
+    right, left_early, beside_early = lax.optimization_barrier((right, left_early, beside_early))
+    far_early = [[tile_swaps(b, stays, s) for s in steps] for b in beside_early]
     (right_pack,) = project(right, cross_qkv, False, 1)
-    left_here, right_pack = lax.optimization_barrier((left_here, right_pack))
     right_pack = lax.ppermute(right_pack, both, there)
+    beside_late = [beside_swaps(left_here, comes, s) for s in hops]
     left_late = [tile_swaps(left_here, comes, s) for s in steps]
-    left = [left_here, *[a + b for a, b in zip(left_early, left_late)]]
-    query, pack = project(left, self_qkv, True, 0)
-    beside = neighbours(pack)
-    halves = tile_pieces(tied(half, left))[1:]
-    near, halves, right_pack = lax.optimization_barrier(([pack, *beside], halves, right_pack))
-    far = [q for p in near for q in across(p)]
+    left_late, beside_late, far_early = lax.optimization_barrier(
+        (left_late, beside_late, far_early)
+    )
+    far_late = [[tile_swaps(b, comes, s) for s in steps] for b in beside_late]
+    query, pack, *left_rest = project(
+        [left_here, *left_early], self_qkv, True, 0, left_late
+    )
+    left = [left_here, *left_rest]
+    near, right_pack = lax.optimization_barrier(([pack, *across(pack)], right_pack))
     state = begin(query, near)
+    far_late = tied(far_late, state)
+    beside = [
+        project([early, *more], self_qkv, False, 1, [late, *rest])[0]
+        for early, late, more, rest in zip(beside_early, beside_late, far_early, far_late)
+    ]
+    far = [*beside, *[q for p in beside for q in across(p)]]
+    halves = tile_pieces(tied(half, far))[1:]
     right_pack = tied(right_pack, state)
     right_near = [right_pack, *neighbours(right_pack)]
+    (mixed,) = run_kernel(
+        end_kernel, "end", [((rows, columns), BF16)], [query, *grouped(far), *state]
+    )
+    halves = tied(halves, mixed)
     others = [
         run_kernel(
             unpack_kernel,
@@ -346,9 +380,6 @@
         )
         for half in halves
     ]
-    (mixed,) = run_kernel(
-        end_kernel, "end", [((rows, columns), BF16)], [query, *grouped(far), *state]
-    )
 
     map_weights = [reassemble, *[other[1] for other in others]]
     (composed,) = run_kernel(

time: 79.3 us -> 86.9 us (1.096)
  starting transfers between devices: 26.8 us -> 39.1 us
  waiting for transfers between devices: 31.5 us -> 25.9 us
  Pallas kernels: 20.4 us -> 21.3 us
    ppermute x2 -> x4, waiting for transfers between devices: 5.63 us -> 1.29 us  [tile_swaps(): return lax.ppermute(value, ('blk', 'tile', 'pair'), pairs)]
    ppermute x1, waiting for transfers between devices: 4.23 us -> 0.01 us  [body(): below = lax.ppermute(features[:1], both, up)]
    ppermute x1, starting transfers between devices: 1.43 us -> 5.44 us  [body(): above = lax.ppermute(features[-1:], both, down)]
    ppermute x2 -> x4, starting transfers between devices: 2.83 us -> 6.03 us  [tile_swaps(): return lax.ppermute(value, ('blk', 'tile', 'pair'), pairs)]
    ppermute x0 -> x2, starting transfers between devices: none -> 3.11 us  [beside_swaps(): return lax.ppermute(value, both, [(source(m), m) for m in members])]
    ppermute x2 -> x1, waiting for transfers between devices: 2.95 us -> 0.01 us  [neighbours(): lax.ppermute(pack, 'blk', [(g + (i + s) % span, g + i) for g, i in ring])]
    ppermute x1, starting transfers between devices: 2.97 us -> 5.74 us  [body(): right_pack = lax.ppermute(right_pack, both, there)]
    ppermute x1, starting transfers between devices: 6.46 us -> 3.79 us  [body(): features = lax.ppermute(features, both, back)]
  transfers between devices with their start and end apart: 18 -> 21, of which waited for: 8 -> 9; matrix products, arithmetic and copies ran while one was open for 0% -> 0% of each run, Pallas kernels for 18% -> 17%
where the time goes in v11:
time: 86.9 us; the launch traced here: 86.5 us
  starting transfers between devices  39.1 us (45%)
  waiting for transfers between devices  25.9 us (30%)
  Pallas kernels  21.3 us (25%)
    pallas_call x14, Pallas kernels, run_kernel(): pl.pallas_call(kernel, out_shape=[jax.ShapeDtypeStruct(*s) for s in shape...  21.3 us
    ppermute x4, waiting for transfers between devices, from_tile(): lax.ppermute(value, 'tile', [((i + step) % tiles, i) for i in range(tiles)])  12.7 us
    ppermute x4, starting transfers between devices, tile_swaps(): return lax.ppermute(value, ('blk', 'tile', 'pair'), pairs)  6.03 us
    ppermute x1, starting transfers between devices, body(): right_pack = lax.ppermute(right_pack, both, there)  5.74 us
    ppermute x4, starting transfers between devices, from_tile(): lax.ppermute(value, 'tile', [((i + step) % tiles, i) for i in range(tiles)])  5.55 us
    ppermute x1, starting transfers between devices, body(): above = lax.ppermute(features[-1:], both, down)  5.44 us
    ppermute x1, waiting for transfers between devices, body(): left_here = lax.ppermute(left_tokens[0], both, there)  5.21 us
    ppermute x1, starting transfers between devices, body(): left_here = lax.ppermute(left_tokens[0], both, there)  5.05 us
  transfers between devices with their start and end apart: 21, of which 9 were waited for; matrix products, arithmetic and copies ran while one was open for 0% of the time, Pallas kernels for 17%

profile of v11, /device:TPU:1, one launch (start us, length us, event | category | flops | bytes accessed | tf_op | source)
XLA Modules:
  0.0 86.5 jit_solution(2883560137992612632)
XLA Ops:
  1.4 2.1 %collective-permute-start.1 = (bf16[384,384]{1,0:T(8,128)(2,1)}, bf16[384,384]{1,0:T(8,128)(2,1)S(1)}, u32[]{:S(2)}, u32[]{:S(2)}) collective-permute-start(bf16[384,384]{1,0:T(8,128)(2,1)} %bitcast.9), channel_id=1, source_target_pairs={{2,0},{0,2},{3,1},{1,3},{6,4},{4,6},{7,5},{5,7},{10,8},{8,10},{11,... | collective-permute-start | bytes 884744 | tf_op jit(solution)/shard_map/ppermute | solution.py:282
  3.5 5.0 %collective-permute-start = (bf16[384,384]{1,0:T(8,128)(2,1)}, bf16[384,384]{1,0:T(8,128)(2,1)S(1)}, u32[]{:S(2)}, u32[]{:S(2)}) collective-permute-start(bf16[384,384]{1,0:T(8,128)(2,1)} %bitcast.13), channel_id=1, source_target_pairs={{0,0},{1,8},{4,4},{5,12},{8,1},{9,9},{12,5},{13,13},{2,2},{3,10},{... | collective-permute-start | bytes 884744 | tf_op jit(solution)/shard_map/ppermute | solution.py:338
  8.5 2.5 %stage.1 = (bf16[256,768]{1,0:T(8,128)(2,1)S(1)}, bf16[384,256]{1,0:T(8,128)(2,1)S(1)}, bf16[256,768]{1,0:T(8,128)(2,1)S(1)}, bf16[384,384]{1,0:T(8,128)(2,1)S(1...) custom-call(bf16[256,768]{1,0:T(8,128)(2,1)} %refs_0_.1, ...), custom_call_target="tpu_custom_call" | custom-call | tf_op jit(solution)/shard_map/stage/pallas_call | solution.py:22
  11.1 5.2 %collective-permute-done.refs_0_.refs_4_ = bf16[384,384]{1,0:T(8,128)(2,1)S(1)} collective-permute-done((bf16[384,384]{1,0:T(8,128)(2,1)}, bf16[384,384]{1,0:T(8,128)(2,1)S(1)}, u32[]{:S(2)}, u32[]{:S(2)}) %collective-permute-start) | collective-permute-done | bytes 294944 | tf_op jit(solution)/shard_map/ppermute | solution.py:338
  16.3 2.4 %collective-permute-start.5 = (bf16[384,384]{1,0:T(8,128)(2,1)S(1)}, bf16[384,384]{1,0:T(8,128)(2,1)S(1)}, u32[]{:S(2)}, u32[]{:S(2)}) collective-permute-start(bf16[384,384]{1,0:T(8,128)(2,1)S(1)} %collective-permute-done.refs_0_.refs_4_), channel_id=1, source_target_pairs={{12,8},{8,12},{5,1},{1,5},{14,10},{10,14},{7,3},{3,7},{28,24},{24,... | collective-permute-start | bytes 884744 | tf_op jit(solution)/shard_map/ppermute | solution.py:292
  18.7 2.3 %collective-permute-start.4 = (bf16[384,384]{1,0:T(8,128)(2,1)S(1)}, bf16[384,384]{1,0:T(8,128)(2,1)S(1)}, u32[]{:S(2)}, u32[]{:S(2)}) collective-permute-start(bf16[384,384]{1,0:T(8,128)(2,1)S(1)} %collective-permute-done.refs_0_.refs_4_), channel_id=1, source_target_pairs={{10,8},{8,10},{14,12},{12,14},{3,1},{1,3},{7,5},{5,7},{26,24},{24,... | collective-permute-start | bytes 884744 | tf_op jit(solution)/shard_map/ppermute | solution.py:276
  22.5 5.7 %collective-permute-start.9 = (bf16[384,512]{1,0:T(8,128)(2,1)S(1)}, bf16[384,512]{1,0:T(8,128)(2,1)S(1)}, u32[]{:S(2)}, u32[]{:S(2)}) collective-permute-start(bf16[384,512]{1,0:T(8,128)(2,1)S(1)} %project.4), channel_id=1, source_target_pairs={{0,0},{1,8},{4,4},{5,12},{8,1},{9,9},{12,5},{13,13},{2,2},{3,10},{... | collective-permute-start | bytes 1179656 | tf_op jit(solution)/shard_map/ppermute | solution.py:348
  28.3 1.3 %collective-permute-done.4.refs_2_ = bf16[384,384]{1,0:T(8,128)(2,1)S(1)} collective-permute-done((bf16[384,384]{1,0:T(8,128)(2,1)S(1)}, bf16[384,384]{1,0:T(8,128)(2,1)S(1)}, u32[]{:S(2)}, u32[]{:S(2)}) %collective-permute-start.4) | collective-permute-done | bytes 294944 | tf_op jit(solution)/shard_map/ppermute | solution.py:276
  31.2 2.4 %collective-permute-start.7 = (bf16[384,384]{1,0:T(8,128)(2,1)S(1)}, bf16[384,384]{1,0:T(8,128)(2,1)S(1)}, u32[]{:S(2)}, u32[]{:S(2)}) collective-permute-start(bf16[384,384]{1,0:T(8,128)(2,1)S(1)} %collective-permute-done.5.refs_2_), channel_id=1, source_target_pairs={{10,8},{8,10},{14,12},{12,14},{3,1},{1,3},{7,5},{5,7},{26,24},{24,... | collective-permute-start | bytes 884744 | tf_op jit(solution)/shard_map/ppermute | solution.py:276
  33.6 3.8 %collective-permute-done.9.refs_0_ = bf16[384,512]{1,0:T(8,128)(2,1)S(1)} collective-permute-done((bf16[384,512]{1,0:T(8,128)(2,1)S(1)}, bf16[384,512]{1,0:T(8,128)(2,1)S(1)}, u32[]{:S(2)}, u32[]{:S(2)}) %collective-permute-start.9) | collective-permute-done | bytes 393248 | tf_op jit(solution)/shard_map/ppermute | solution.py:348
  37.4 2.3 %begin.2 = (f32[4,384,64]{2,1,0:T(8,128)S(1)}, f32[4,384,2]{2,1,0:T(8,128)S(1)}) custom-call(bf16[384,256]{1,0:T(8,128)(2,1)S(1)} %get-tuple-element.53.query, bf16[384,512]{1,0:T(8,128)(2,1)S(1)} %get-tuple-element.60.refs_0_, bf16[384,512]{1,0:T(8,128)(2,1)S(1)} %collective-permute-done.8.refs_1_), custom_call_target="tpu_custom_call" | custom-call | tf_op jit(solution)/shard_map/begin/pallas_call | solution.py:22
  40.6 1.7 %collective-permute-done.10.refs_1_ = bf16[384,512]{1,0:T(8,128)(2,1)S(1)} collective-permute-done((bf16[384,512]{1,0:T(8,128)(2,1)S(1)}, bf16[384,512]{1,0:T(8,128)(2,1)S(1)}, u32[]{:S(2)}, u32[]{:S(2)}) %collective-permute-start.10) | collective-permute-done | bytes 393248 | tf_op jit(solution)/shard_map/ppermute | solution.py:303
  43.5 3.1 %end.1.refs_0_ = bf16[384,256]{1,0:T(8,128)(2,1)S(1)} custom-call(bf16[384,256]{1,0:T(8,128)(2,1)S(1)} %get-tuple-element.53.query, bf16[384,512]{1,0:T(8,128)(2,1)S(1)} %project.5.refs_0_, bf16[384,512]{1,0:T(8,128)(2,1)S(1)} %collective-permute-done.10.refs_1_, f32[4,384,64]{2,1,0:T(8,128)S(1)} %get-tuple-element.62.refs_2_, ...), custom_call_target="tpu_custom_call" | custom-call | tf_op jit(solution)/shard_map/end/pallas_call | solution.py:22
  46.6 4.2 %collective-permute-done.12.refs_0_ = bf16[192,768]{1,0:T(8,128)(2,1)S(1)} collective-permute-done((bf16[192,768]{1,0:T(8,128)(2,1)S(1)}, bf16[192,768]{1,0:T(8,128)(2,1)S(1)}, u32[]{:S(2)}, u32[]{:S(2)}) %collective-permute-start.12) | collective-permute-done | bytes 294944 | tf_op jit(solution)/shard_map/ppermute | solution.py:282
  53.3 5.0 %collective-permute-done.11.refs_1_ = bf16[384,256]{1,0:T(8,128)(2,1)S(1)} collective-permute-done((bf16[384,256]{1,0:T(8,128)(2,1)S(1)}, bf16[384,256]{1,0:T(8,128)(2,1)S(1)}, u32[]{:S(2)}, u32[]{:S(2)}) %collective-permute-start.11) | collective-permute-done | bytes 196640 | tf_op jit(solution)/shard_map/ppermute | solution.py:282
  58.3 1.5 %update.1 = (bf16[2,384,384]{2,1,0:T(8,128)(2,1)S(1)}, bf16[384,256]{1,0:T(8,128)(2,1)S(1)}) custom-call(bf16[384,256]{1,0:T(8,128)(2,1)S(1)} %end.1.refs_0_, bf16[384,256]{1,0:T(8,128)(2,1)S(1)} %collective-permute-done.11.refs_1_, bf16[256,768]{1,0:T(8,128)(2,1)S(1)} %get-tuple-element.73.refs_2_, bf16[256,768]{1,0:T(8,128)(2,1)S(1)} %get-tuple-element.74.refs_3_, ...), custom_call_target="tpu_custom_call" | custom-call | tf_op jit(solution)/shard_map/update/pallas_call | solution.py:22
  60.7 2.3 %begin.3 = (f32[4,384,64]{2,1,0:T(8,128)S(1)}, f32[4,384,2]{2,1,0:T(8,128)S(1)}) custom-call(bf16[384,256]{1,0:T(8,128)(2,1)S(1)} %get-tuple-element.77.query, bf16[384,512]{1,0:T(8,128)(2,1)S(1)} %collective-permute-done.9.refs_0_, bf16[384,512]{1,0:T(8,128)(2,1)S(1)} %collective-permute-done.14.refs_1_), custom_call_target="tpu_custom_call" | custom-call | tf_op jit(solution)/shard_map/begin/pallas_call | solution.py:22
  63.0 5.0 %end_map.1 = (bf16[3,96,256]{2,1,0:T(8,128)(2,1)S(1)}, bf16[3,96,256]{2,1,0:T(8,128)(2,1)S(1)}) custom-call(bf16[384,256]{1,0:T(8,128)(2,1)S(1)} %get-tuple-element.77.query, bf16[384,512]{1,0:T(8,128)(2,1)S(1)} %collective-permute-done.15.refs_0_, bf16[384,512]{1,0:T(8,128)(2,1)S(1)} %collective-permute-done.16.refs_1_, ...), custom_call_target="tpu_custom_call" | custom-call | tf_op jit(solution)/shard_map/end_map/pallas_call | solution.py:22
  68.0 1.2 %collective-permute-start.17 = (bf16[3,96,256]{2,1,0:T(8,128)(2,1)S(1)}, bf16[3,96,256]{2,1,0:T(8,128)(2,1)S(1)}, u32[]{:S(2)}, u32[]{:S(2)}) collective-permute-start(bf16[3,96,256]{2,1,0:T(8,128)(2,1)S(1)} %get-tuple-element.88), channel_id=1, source_target_pairs={{2,0},{0,2},{3,1},{1,3},{6,4},{4,6},{7,5},{5,7},{10,8},{8,10},{11,... | collective-permute-start | bytes 442376 | tf_op jit(solution)/shard_map/ppermute | solution.py:282
  69.6 3.5 %collective-permute-done.17.refs_2_ = bf16[3,96,256]{2,1,0:T(8,128)(2,1)S(1)} collective-permute-done((bf16[3,96,256]{2,1,0:T(8,128)(2,1)S(1)}, bf16[3,96,256]{2,1,0:T(8,128)(2,1)S(1)}, u32[]{:S(2)}, u32[]{:S(2)}) %collective-permute-start.17) | collective-permute-done | bytes 147488 | tf_op jit(solution)/shard_map/ppermute | solution.py:282
  73.1 3.8 %collective-permute-start.18 = (bf16[3,96,256]{2,1,0:T(8,128)(2,1)S(1)}, bf16[3,96,256]{2,1,0:T(8,128)(2,1)S(1)}, u32[]{:S(2)}, u32[]{:S(2)}) collective-permute-start(bf16[3,96,256]{2,1,0:T(8,128)(2,1)S(1)} %add.1), channel_id=1, source_target_pairs={{0,0},{8,1},{4,4},{12,5},{1,8},{9,9},{5,12},{13,13},{2,2},{10,3},{... | collective-permute-start | bytes 442376 | tf_op jit(solution)/shard_map/ppermute | solution.py:423
  77.0 1.9 %collective-permute-start.20 = (bf16[1,96,256]{2,1,0:T(8,128)(2,1)S(1)}, bf16[1,96,256]{2,1,0:T(8,128)(2,1)S(1)}, u32[]{:S(2)}, u32[]{:S(2)}) collective-permute-start(bf16[1,96,256]{2,1,0:T(8,128)(2,1)S(1)} %get-tuple-element.91), channel_id=1, source_target_pairs={{4,0},{12,1},{1,4},{9,5},{5,8},{13,9},{6,2},{14,3},{3,6},{11,7},{7... | collective-permute-start | bytes 147464 | tf_op jit(solution)/shard_map/ppermute | solution.py:422
  78.9 5.4 %collective-permute-start.19 = (bf16[1,96,256]{2,1,0:T(8,128)(2,1)S(1)}, bf16[1,96,256]{2,1,0:T(8,128)(2,1)S(1)}, u32[]{:S(2)}, u32[]{:S(2)}) collective-permute-start(bf16[1,96,256]{2,1,0:T(8,128)(2,1)S(1)} %get-tuple-element.92), channel_id=1, source_target_pairs={{0,4},{8,5},{4,8},{12,9},{1,12},{9,13},{2,6},{10,7},{6,10},{14,11}... | collective-permute-start | bytes 147464 | tf_op jit(solution)/shard_map/ppermute | solution.py:421
  84.3 1.1 %collective-permute-done.19.above = bf16[1,96,256]{2,1,0:T(8,128)(2,1)S(1)} collective-permute-done((bf16[1,96,256]{2,1,0:T(8,128)(2,1)S(1)}, bf16[1,96,256]{2,1,0:T(8,128)(2,1)S(1)}, u32[]{:S(2)}, u32[]{:S(2)}) %collective-permute-start.19) | collective-permute-done | bytes 49184 | tf_op jit(solution)/shard_map/ppermute | solution.py:421
  (33 shorter events, 11.5 us)
Async XLA Ops:
  0.0 11.1 %collective-permute-start.3 = (bf16[384,384]{1,0:T(8,128)(2,1)}, bf16[384,384]{1,0:T(8,128)(2,1)S(1)}, u32[]{:S(2)}, u32[]{:S(2)}) collective-permute-start(bf16[384,384]{1,0:T(8,128)(2,1)} %bitcast.11), channel_id=1, source_target_pairs={{4,0},{0,4},{13,9},{9,13},{6,2},{2,6},{15,11},{11,15},{20,16},{16,... | collective-permute-start | bytes 884744 | tf_op jit(solution)/shard_map/ppermute | solution.py:292
  0.7 10.4 %collective-permute-start.2 = (bf16[384,384]{1,0:T(8,128)(2,1)}, bf16[384,384]{1,0:T(8,128)(2,1)S(1)}, u32[]{:S(2)}, u32[]{:S(2)}) collective-permute-start(bf16[384,384]{1,0:T(8,128)(2,1)} %bitcast.12), channel_id=1, source_target_pairs={{2,0},{0,2},{6,4},{4,6},{11,9},{9,11},{15,13},{13,15},{18,16},{16,... | collective-permute-start | bytes 884744 | tf_op jit(solution)/shard_map/ppermute | solution.py:276
  1.4 9.7 %collective-permute-start.1 = (bf16[384,384]{1,0:T(8,128)(2,1)}, bf16[384,384]{1,0:T(8,128)(2,1)S(1)}, u32[]{:S(2)}, u32[]{:S(2)}) collective-permute-start(bf16[384,384]{1,0:T(8,128)(2,1)} %bitcast.9), channel_id=1, source_target_pairs={{2,0},{0,2},{3,1},{1,3},{6,4},{4,6},{7,5},{5,7},{10,8},{8,10},{11,... | collective-permute-start | bytes 884744 | tf_op jit(solution)/shard_map/ppermute | solution.py:282
  3.5 12.8 %collective-permute-start = (bf16[384,384]{1,0:T(8,128)(2,1)}, bf16[384,384]{1,0:T(8,128)(2,1)S(1)}, u32[]{:S(2)}, u32[]{:S(2)}) collective-permute-start(bf16[384,384]{1,0:T(8,128)(2,1)} %bitcast.13), channel_id=1, source_target_pairs={{0,0},{1,8},{4,4},{5,12},{8,1},{9,9},{12,5},{13,13},{2,2},{3,10},{... | collective-permute-start | bytes 884744 | tf_op jit(solution)/shard_map/ppermute | solution.py:338
  16.3 12.0 %collective-permute-start.5 = (bf16[384,384]{1,0:T(8,128)(2,1)S(1)}, bf16[384,384]{1,0:T(8,128)(2,1)S(1)}, u32[]{:S(2)}, u32[]{:S(2)}) collective-permute-start(bf16[384,384]{1,0:T(8,128)(2,1)S(1)} %collective-permute-done.refs_0_.refs_4_), channel_id=1, source_target_pairs={{12,8},{8,12},{5,1},{1,5},{14,10},{10,14},{7,3},{3,7},{28,24},{24,... | collective-permute-start | bytes 884744 | tf_op jit(solution)/shard_map/ppermute | solution.py:292
  18.7 10.9 %collective-permute-start.4 = (bf16[384,384]{1,0:T(8,128)(2,1)S(1)}, bf16[384,384]{1,0:T(8,128)(2,1)S(1)}, u32[]{:S(2)}, u32[]{:S(2)}) collective-permute-start(bf16[384,384]{1,0:T(8,128)(2,1)S(1)} %collective-permute-done.refs_0_.refs_4_), channel_id=1, source_target_pairs={{10,8},{8,10},{14,12},{12,14},{3,1},{1,3},{7,5},{5,7},{26,24},{24,... | collective-permute-start | bytes 884744 | tf_op jit(solution)/shard_map/ppermute | solution.py:276
  21.0 8.6 %collective-permute-start.6 = (bf16[384,384]{1,0:T(8,128)(2,1)S(1)}, bf16[384,384]{1,0:T(8,128)(2,1)S(1)}, u32[]{:S(2)}, u32[]{:S(2)}) collective-permute-start(bf16[384,384]{1,0:T(8,128)(2,1)S(1)} %collective-permute-done.3.refs_0_), channel_id=1, source_target_pairs={{2,0},{0,2},{6,4},{4,6},{11,9},{9,11},{15,13},{13,15},{18,16},{16,... | collective-permute-start | bytes 884744 | tf_op jit(solution)/shard_map/ppermute | solution.py:276
  22.5 14.9 %collective-permute-start.9 = (bf16[384,512]{1,0:T(8,128)(2,1)S(1)}, bf16[384,512]{1,0:T(8,128)(2,1)S(1)}, u32[]{:S(2)}, u32[]{:S(2)}) collective-permute-start(bf16[384,512]{1,0:T(8,128)(2,1)S(1)} %project.4), channel_id=1, source_target_pairs={{0,0},{1,8},{4,4},{5,12},{8,1},{9,9},{12,5},{13,13},{2,2},{3,10},{... | collective-permute-start | bytes 1179656 | tf_op jit(solution)/shard_map/ppermute | solution.py:348
  30.7 6.7 %collective-permute-start.8 = (bf16[384,512]{1,0:T(8,128)(2,1)S(1)}, bf16[384,512]{1,0:T(8,128)(2,1)S(1)}, u32[]{:S(2)}, u32[]{:S(2)}) collective-permute-start(bf16[384,512]{1,0:T(8,128)(2,1)S(1)} %get-tuple-element.60.refs_0_), channel_id=1, source_target_pairs={{1,0},{0,1},{3,2},{2,3},{5,4},{4,5},{7,6},{6,7},{9,8},{8,9},{11,10... | collective-permute-start | bytes 1179656 | tf_op jit(solution)/shard_map/ppermute | solution.py:303
  31.2 8.5 %collective-permute-start.7 = (bf16[384,384]{1,0:T(8,128)(2,1)S(1)}, bf16[384,384]{1,0:T(8,128)(2,1)S(1)}, u32[]{:S(2)}, u32[]{:S(2)}) collective-permute-start(bf16[384,384]{1,0:T(8,128)(2,1)S(1)} %collective-permute-done.5.refs_2_), channel_id=1, source_target_pairs={{10,8},{8,10},{14,12},{12,14},{3,1},{1,3},{7,5},{5,7},{26,24},{24,... | collective-permute-start | bytes 884744 | tf_op jit(solution)/shard_map/ppermute | solution.py:276
  40.5 1.8 %collective-permute-start.10 = (bf16[384,512]{1,0:T(8,128)(2,1)S(1)}, bf16[384,512]{1,0:T(8,128)(2,1)S(1)}, u32[]{:S(2)}, u32[]{:S(2)}) collective-permute-start(bf16[384,512]{1,0:T(8,128)(2,1)S(1)} %project.5.refs_0_), channel_id=1, source_target_pairs={{1,0},{0,1},{3,2},{2,3},{5,4},{4,5},{7,6},{6,7},{9,8},{8,9},{11,10... | collective-permute-start | bytes 1179656 | tf_op jit(solution)/shard_map/ppermute | solution.py:303
  42.3 8.5 %collective-permute-start.12 = (bf16[192,768]{1,0:T(8,128)(2,1)S(1)}, bf16[192,768]{1,0:T(8,128)(2,1)S(1)}, u32[]{:S(2)}, u32[]{:S(2)}) collective-permute-start(bf16[192,768]{1,0:T(8,128)(2,1)S(1)} %get-tuple-element.68), channel_id=1, source_target_pairs={{2,0},{0,2},{3,1},{1,3},{6,4},{4,6},{7,5},{5,7},{10,8},{8,10},{11,... | collective-permute-start | bytes 884744 | tf_op jit(solution)/shard_map/ppermute | solution.py:282
  43.5 16.3 %collective-permute-start.14 = (bf16[384,512]{1,0:T(8,128)(2,1)S(1)}, bf16[384,512]{1,0:T(8,128)(2,1)S(1)}, u32[]{:S(2)}, u32[]{:S(2)}) collective-permute-start(bf16[384,512]{1,0:T(8,128)(2,1)S(1)} %collective-permute-done.9.refs_0_), channel_id=1, source_target_pairs={{4,0},{0,4},{12,8},{8,12},{5,1},{1,5},{13,9},{9,13},{6,2},{2,6},{1... | collective-permute-start | bytes 1179656 | tf_op jit(solution)/shard_map/ppermute | solution.py:297
  50.8 2.2 %collective-permute-start.13 = (bf16[192,768]{1,0:T(8,128)(2,1)S(1)}, bf16[192,768]{1,0:T(8,128)(2,1)S(1)}, u32[]{:S(2)}, u32[]{:S(2)}) collective-permute-start(bf16[192,768]{1,0:T(8,128)(2,1)S(1)} %collective-permute-done.12.refs_0_), channel_id=1, source_target_pairs={{1,0},{0,1},{3,2},{2,3},{5,4},{4,5},{7,6},{6,7},{9,8},{8,9},{11,10... | collective-permute-start | bytes 884744 | tf_op jit(solution)/shard_map/ppermute | solution.py:303
  51.8 6.5 %collective-permute-start.11 = (bf16[384,256]{1,0:T(8,128)(2,1)S(1)}, bf16[384,256]{1,0:T(8,128)(2,1)S(1)}, u32[]{:S(2)}, u32[]{:S(2)}) collective-permute-start(bf16[384,256]{1,0:T(8,128)(2,1)S(1)} %end.1.refs_0_), channel_id=1, source_target_pairs={{2,0},{0,2},{3,1},{1,3},{6,4},{4,6},{7,5},{5,7},{10,8},{8,10},{11,... | collective-permute-start | bytes 589832 | tf_op jit(solution)/shard_map/ppermute | solution.py:282
  59.8 3.2 %collective-permute-start.15 = (bf16[384,512]{1,0:T(8,128)(2,1)S(1)}, bf16[384,512]{1,0:T(8,128)(2,1)S(1)}, u32[]{:S(2)}, u32[]{:S(2)}) collective-permute-start(bf16[384,512]{1,0:T(8,128)(2,1)S(1)} %collective-permute-done.9.refs_0_), channel_id=1, source_target_pairs={{1,0},{0,1},{3,2},{2,3},{5,4},{4,5},{7,6},{6,7},{9,8},{8,9},{11,10... | collective-permute-start | bytes 1179656 | tf_op jit(solution)/shard_map/ppermute | solution.py:303
  60.6 2.4 %collective-permute-start.16 = (bf16[384,512]{1,0:T(8,128)(2,1)S(1)}, bf16[384,512]{1,0:T(8,128)(2,1)S(1)}, u32[]{:S(2)}, u32[]{:S(2)}) collective-permute-start(bf16[384,512]{1,0:T(8,128)(2,1)S(1)} %collective-permute-done.14.refs_1_), channel_id=1, source_target_pairs={{1,0},{0,1},{3,2},{2,3},{5,4},{4,5},{7,6},{6,7},{9,8},{8,9},{11,10... | collective-permute-start | bytes 1179656 | tf_op jit(solution)/shard_map/ppermute | solution.py:303
  68.0 5.1 %collective-permute-start.17 = (bf16[3,96,256]{2,1,0:T(8,128)(2,1)S(1)}, bf16[3,96,256]{2,1,0:T(8,128)(2,1)S(1)}, u32[]{:S(2)}, u32[]{:S(2)}) collective-permute-start(bf16[3,96,256]{2,1,0:T(8,128)(2,1)S(1)} %get-tuple-element.88), channel_id=1, source_target_pairs={{2,0},{0,2},{3,1},{1,3},{6,4},{4,6},{7,5},{5,7},{10,8},{8,10},{11,... | collective-permute-start | bytes 442376 | tf_op jit(solution)/shard_map/ppermute | solution.py:282
  73.1 12.3 %collective-permute-start.18 = (bf16[3,96,256]{2,1,0:T(8,128)(2,1)S(1)}, bf16[3,96,256]{2,1,0:T(8,128)(2,1)S(1)}, u32[]{:S(2)}, u32[]{:S(2)}) collective-permute-start(bf16[3,96,256]{2,1,0:T(8,128)(2,1)S(1)} %add.1), channel_id=1, source_target_pairs={{0,0},{8,1},{4,4},{12,5},{1,8},{9,9},{5,12},{13,13},{2,2},{10,3},{... | collective-permute-start | bytes 442376 | tf_op jit(solution)/shard_map/ppermute | solution.py:423
  77.0 7.4 %collective-permute-start.20 = (bf16[1,96,256]{2,1,0:T(8,128)(2,1)S(1)}, bf16[1,96,256]{2,1,0:T(8,128)(2,1)S(1)}, u32[]{:S(2)}, u32[]{:S(2)}) collective-permute-start(bf16[1,96,256]{2,1,0:T(8,128)(2,1)S(1)} %get-tuple-element.91), channel_id=1, source_target_pairs={{4,0},{12,1},{1,4},{9,5},{5,8},{13,9},{6,2},{14,3},{3,6},{11,7},{7... | collective-permute-start | bytes 147464 | tf_op jit(solution)/shard_map/ppermute | solution.py:422
  78.9 6.6 %collective-permute-start.19 = (bf16[1,96,256]{2,1,0:T(8,128)(2,1)S(1)}, bf16[1,96,256]{2,1,0:T(8,128)(2,1)S(1)}, u32[]{:S(2)}, u32[]{:S(2)}) collective-permute-start(bf16[1,96,256]{2,1,0:T(8,128)(2,1)S(1)} %get-tuple-element.92), channel_id=1, source_target_pairs={{0,4},{8,5},{4,8},{12,9},{1,12},{9,13},{2,6},{10,7},{6,10},{14,11}... | collective-permute-start | bytes 147464 | tf_op jit(solution)/shard_map/ppermute | solution.py:421

commit v12 on v8

--- a/solution.py
+++ b/solution.py
@@ -258,14 +258,12 @@
     back = [(worker(*p), home(*p)) for p in places]
     down = [(worker(b, p), home(b + 1, p)) for b, p in places if b + 1 < bands]
     up = [(worker(b, p), home(b - 1, p)) for b, p in places if b > 0]
-    stays = [home(*p) for p in places if home(*p) == worker(*p)]
-    comes = [worker(*p) for p in places if home(*p) != worker(*p)]
-
-    def tile_swaps(value, members, step):
+
+    def fetched(value, step):
         def flat(position, tile):
             return (position // cores * tiles + tile) * cores + position % cores
 
-        pairs = [(flat(m, (i + step) % tiles), flat(m, i)) for m in members for i in range(tiles)]
+        pairs = [(flat(s, (i + step) % tiles), flat(d, i)) for s, d in there for i in range(tiles)]
         return lax.ppermute(value, ("blk", "tile", "pair"), pairs)
 
     def tied(values, *others):
@@ -317,26 +315,27 @@
             pl.BlockSpec(memory_space=pl.ANY),
         )
 
-    left_here = lax.ppermute(left_tokens[0], both, there)
     steps = range(1, tiles)
-    left_early = [tile_swaps(left_tokens[0], stays, s) for s in steps]
+    left = [fetched(left_tokens[0], step) for step in range(tiles)]
     self_out, reassemble, cross_out, right_own, self_qkv, cross_qkv, taps, half = staged(
         [self_out, reassemble, cross_out, right_tokens[0], self_qkv, cross_qkv, taps]
     )
     right = [right_own, *[from_tile(right_tokens[0], s) for s in steps]]
     (right_pack,) = project(right, cross_qkv, False, 1)
-    left_here, right_pack = lax.optimization_barrier((left_here, right_pack))
-    right_pack = lax.ppermute(right_pack, both, there)
-    left_late = [tile_swaps(left_here, comes, s) for s in steps]
-    left = [left_here, *[a + b for a, b in zip(left_early, left_late)]]
+    left, right_pack = lax.optimization_barrier((left, right_pack))
     query, pack = project(left, self_qkv, True, 0)
+    right_pack = lax.ppermute(tied(right_pack, pack), both, there)
     beside = neighbours(pack)
-    halves = tile_pieces(tied(half, left))[1:]
-    near, halves, right_pack = lax.optimization_barrier(([pack, *beside], halves, right_pack))
+    near = [pack, *beside]
     far = [q for p in near for q in across(p)]
     state = begin(query, near)
     right_pack = tied(right_pack, state)
     right_near = [right_pack, *neighbours(right_pack)]
+    halves = tile_pieces(tied(half, beside))[1:]
+    (mixed,) = run_kernel(
+        end_kernel, "end", [((rows, columns), BF16)], [query, *grouped(far), *state]
+    )
+    halves = tied(halves, mixed)
     others = [
         run_kernel(
             unpack_kernel,
@@ -346,10 +345,6 @@
         )
         for half in halves
     ]
-    (mixed,) = run_kernel(
-        end_kernel, "end", [((rows, columns), BF16)], [query, *grouped(far), *state]
-    )
-
     map_weights = [reassemble, *[other[1] for other in others]]
     (composed,) = run_kernel(
         compose_kernel, "compose", [((columns, channels), BF16)], [cross_out, *map_weights]

time: 79.3 us -> 77.3 us (0.975)
  waiting for transfers between devices: 31.5 us -> 24 us
  starting transfers between devices: 26.8 us -> 32.7 us
    ppermute x1, waiting for transfers between devices: 4.23 us -> 0.01 us  [body(): below = lax.ppermute(features[:1], both, up)]
    ppermute x1, starting transfers between devices: 1.43 us -> 5.44 us  [body(): above = lax.ppermute(features[-1:], both, down)]
    ppermute x4 -> x3, waiting for transfers between devices: 13.5 us -> 9.55 us  [the longest x2 8.33 us: fetched(): return lax.ppermute(value, ('blk', 'tile', 'pair'), pairs)]
    ppermute x4, starting transfers between devices: 2.94 us -> 6.22 us  [from_tile(): lax.ppermute(value, 'tile', [((i + step) % tiles, i) for i in range(tiles)])]
    ppermute x4, waiting for transfers between devices: 10.8 us -> 8.5 us  [from_tile(): lax.ppermute(value, 'tile', [((i + step) % tiles, i) for i in range(tiles)])]
    ppermute x2, waiting for transfers between devices: 2.95 us -> 4.75 us  [neighbours(): lax.ppermute(pack, 'blk', [(g + (i + s) % span, g + i) for g, i in ring])]
    ppermute x1, waiting for transfers between devices: 0.01 us -> 1.15 us  [body(): above = lax.ppermute(features[-1:], both, down)]
    ppermute x1, starting transfers between devices: 2.96 us -> 1.92 us  [body(): below = lax.ppermute(features[:1], both, up)]
  transfers between devices with their start and end apart: 18 -> 17, of which waited for: 8 -> 9; matrix products, arithmetic and copies ran while one was open for 0% -> 0% of each run, Pallas kernels for 18% -> 17%
where the time goes in v12:
time: 77.3 us; the launch traced here: 77.1 us
  starting transfers between devices  32.7 us (42%)
  waiting for transfers between devices  24 us (31%)
  Pallas kernels  20.3 us (26%)
    pallas_call x13, Pallas kernels, run_kernel(): pl.pallas_call(kernel, out_shape=[jax.ShapeDtypeStruct(*s) for s in shape...  20.3 us
    ppermute x4, waiting for transfers between devices, from_tile(): lax.ppermute(value, 'tile', [((i + step) % tiles, i) for i in range(tiles)])  8.5 us
    ppermute x2, waiting for transfers between devices, fetched(): return lax.ppermute(value, ('blk', 'tile', 'pair'), pairs)  8.33 us
    ppermute x4, starting transfers between devices, from_tile(): lax.ppermute(value, 'tile', [((i + step) % tiles, i) for i in range(tiles)])  6.22 us
    ppermute x1, starting transfers between devices, body(): features = lax.ppermute(features, both, back)  5.61 us
    ppermute x1, starting transfers between devices, body(): right_pack = lax.ppermute(tied(right_pack, pack), both, there)  5.5 us
    ppermute x1, starting transfers between devices, body(): above = lax.ppermute(features[-1:], both, down)  5.44 us
    ppermute x2, starting transfers between devices, fetched(): return lax.ppermute(value, ('blk', 'tile', 'pair'), pairs)  5.05 us
  transfers between devices with their start and end apart: 17, of which 9 were waited for; matrix products, arithmetic and copies ran while one was open for 0% of the time, Pallas kernels for 17%

profile of v12, /device:TPU:1, one launch (start us, length us, event | category | flops | bytes accessed | tf_op | source)
XLA Modules:
  0.0 77.1 jit_solution(7587890552629979402)
XLA Ops:
  0.0 2.0 %collective-permute-start.2 = (bf16[384,384]{1,0:T(8,128)(2,1)}, bf16[384,384]{1,0:T(8,128)(2,1)S(1)}, u32[]{:S(2)}, u32[]{:S(2)}) collective-permute-start(bf16[384,384]{1,0:T(8,128)(2,1)} %bitcast.8), channel_id=1, source_target_pairs={{2,0},{0,2},{3,1},{1,3},{6,4},{4,6},{7,5},{5,7},{10,8},{8,10},{11,... | collective-permute-start | bytes 884744 | tf_op jit(solution)/shard_map/ppermute | solution.py:273
  2.0 3.1 %collective-permute-start.1 = (bf16[384,384]{1,0:T(8,128)(2,1)}, bf16[384,384]{1,0:T(8,128)(2,1)S(1)}, u32[]{:S(2)}, u32[]{:S(2)}) collective-permute-start(bf16[384,384]{1,0:T(8,128)(2,1)} %bitcast.10), channel_id=1, source_target_pairs={{2,0},{0,2},{3,8},{1,10},{6,4},{4,6},{7,12},{5,14},{10,1},{8,3},{1... | collective-permute-start | bytes 884744 | tf_op jit(solution)/shard_map/ppermute | solution.py:267
  5.2 1.9 %collective-permute-start = (bf16[384,384]{1,0:T(8,128)(2,1)}, bf16[384,384]{1,0:T(8,128)(2,1)S(1)}, u32[]{:S(2)}, u32[]{:S(2)}) collective-permute-start(bf16[384,384]{1,0:T(8,128)(2,1)} %bitcast.11), channel_id=1, source_target_pairs={{0,0},{2,2},{1,8},{3,10},{4,4},{6,6},{5,12},{7,14},{8,1},{10,3},{9... | collective-permute-start | bytes 884744 | tf_op jit(solution)/shard_map/ppermute | solution.py:267
  7.1 2.6 %stage.1 = (bf16[256,768]{1,0:T(8,128)(2,1)S(1)}, bf16[384,256]{1,0:T(8,128)(2,1)S(1)}, bf16[256,768]{1,0:T(8,128)(2,1)S(1)}, bf16[384,384]{1,0:T(8,128)(2,1)S(1...) custom-call(bf16[256,768]{1,0:T(8,128)(2,1)} %refs_0_.1, ...), custom_call_target="tpu_custom_call" | custom-call | tf_op jit(solution)/shard_map/stage/pallas_call | solution.py:22
  11.0 5.6 %collective-permute-done.1.refs_1_.refs_5_ = bf16[384,384]{1,0:T(8,128)(2,1)S(1)} collective-permute-done((bf16[384,384]{1,0:T(8,128)(2,1)}, bf16[384,384]{1,0:T(8,128)(2,1)S(1)}, u32[]{:S(2)}, u32[]{:S(2)}) %collective-permute-start.1) | collective-permute-done | bytes 294944 | tf_op jit(solution)/shard_map/ppermute | solution.py:267
  16.5 2.8 %collective-permute-done.refs_0_.refs_4_ = bf16[384,384]{1,0:T(8,128)(2,1)S(1)} collective-permute-done((bf16[384,384]{1,0:T(8,128)(2,1)}, bf16[384,384]{1,0:T(8,128)(2,1)S(1)}, u32[]{:S(2)}, u32[]{:S(2)}) %collective-permute-start) | collective-permute-done | bytes 294944 | tf_op jit(solution)/shard_map/ppermute | solution.py:267
  20.9 5.5 %collective-permute-start.9 = (bf16[384,512]{1,0:T(8,128)(2,1)S(1)}, bf16[384,512]{1,0:T(8,128)(2,1)S(1)}, u32[]{:S(2)}, u32[]{:S(2)}) collective-permute-start(bf16[384,512]{1,0:T(8,128)(2,1)S(1)} %project.2), channel_id=1, source_target_pairs={{0,0},{1,8},{4,4},{5,12},{8,1},{9,9},{12,5},{13,13},{2,2},{3,10},{... | collective-permute-start | bytes 1179656 | tf_op jit(solution)/shard_map/ppermute | solution.py:327
  26.5 4.7 %collective-permute-done.4.refs_1_ = bf16[384,512]{1,0:T(8,128)(2,1)S(1)} collective-permute-done((bf16[384,512]{1,0:T(8,128)(2,1)S(1)}, bf16[384,512]{1,0:T(8,128)(2,1)S(1)}, u32[]{:S(2)}, u32[]{:S(2)}) %collective-permute-start.4) | collective-permute-done | bytes 393248 | tf_op jit(solution)/shard_map/ppermute | solution.py:281
  31.3 1.4 %collective-permute-start.7 = (bf16[192,768]{1,0:T(8,128)(2,1)S(1)}, bf16[192,768]{1,0:T(8,128)(2,1)S(1)}, u32[]{:S(2)}, u32[]{:S(2)}) collective-permute-start(bf16[192,768]{1,0:T(8,128)(2,1)S(1)} %get-tuple-element.52), channel_id=1, source_target_pairs={{2,0},{0,2},{3,1},{1,3},{6,4},{4,6},{7,5},{5,7},{10,8},{8,10},{11,... | collective-permute-start | bytes 884744 | tf_op jit(solution)/shard_map/ppermute | solution.py:273
  32.6 2.3 %begin.2 = (f32[4,384,64]{2,1,0:T(8,128)S(1)}, f32[4,384,2]{2,1,0:T(8,128)S(1)}) custom-call(bf16[384,256]{1,0:T(8,128)(2,1)S(1)} %get-tuple-element.45.query, bf16[384,512]{1,0:T(8,128)(2,1)S(1)} %get-tuple-element.46.refs_0_, bf16[384,512]{1,0:T(8,128)(2,1)S(1)} %collective-permute-done.4.refs_1_), custom_call_target="tpu_custom_call" | custom-call | tf_op jit(solution)/shard_map/begin/pallas_call | solution.py:22
  34.9 1.2 %collective-permute-done.9.refs_0_ = bf16[384,512]{1,0:T(8,128)(2,1)S(1)} collective-permute-done((bf16[384,512]{1,0:T(8,128)(2,1)S(1)}, bf16[384,512]{1,0:T(8,128)(2,1)S(1)}, u32[]{:S(2)}, u32[]{:S(2)}) %collective-permute-start.9) | collective-permute-done | bytes 393248 | tf_op jit(solution)/shard_map/ppermute | solution.py:327
  36.2 3.1 %end.1.refs_0_ = bf16[384,256]{1,0:T(8,128)(2,1)S(1)} custom-call(bf16[384,256]{1,0:T(8,128)(2,1)S(1)} %get-tuple-element.45.query, bf16[384,512]{1,0:T(8,128)(2,1)S(1)} %collective-permute-done.3.refs_0_, bf16[384,512]{1,0:T(8,128)(2,1)S(1)} %collective-permute-done.5.refs_1_, f32[4,384,64]{2,1,0:T(8,128)S(1)} %get-tuple-element.47.refs_2_, ...), custom_call_target="tpu_custom_call" | custom-call | tf_op jit(solution)/shard_map/end/pallas_call | solution.py:22
  39.3 1.4 %collective-permute-start.8 = (bf16[192,768]{1,0:T(8,128)(2,1)S(1)}, bf16[192,768]{1,0:T(8,128)(2,1)S(1)}, u32[]{:S(2)}, u32[]{:S(2)}) collective-permute-start(bf16[192,768]{1,0:T(8,128)(2,1)S(1)} %collective-permute-done.7.refs_0_), channel_id=1, source_target_pairs={{1,0},{0,1},{3,2},{2,3},{5,4},{4,5},{7,6},{6,7},{9,8},{8,9},{11,10... | collective-permute-start | bytes 884744 | tf_op jit(solution)/shard_map/ppermute | solution.py:287
  40.7 1.4 %collective-permute-start.6 = (bf16[384,256]{1,0:T(8,128)(2,1)S(1)}, bf16[384,256]{1,0:T(8,128)(2,1)S(1)}, u32[]{:S(2)}, u32[]{:S(2)}) collective-permute-start(bf16[384,256]{1,0:T(8,128)(2,1)S(1)} %end.1.refs_0_), channel_id=1, source_target_pairs={{2,0},{0,2},{3,1},{1,3},{6,4},{4,6},{7,5},{5,7},{10,8},{8,10},{11,... | collective-permute-start | bytes 589832 | tf_op jit(solution)/shard_map/ppermute | solution.py:273
  42.4 4.8 %collective-permute-done.6.refs_1_ = bf16[384,256]{1,0:T(8,128)(2,1)S(1)} collective-permute-done((bf16[384,256]{1,0:T(8,128)(2,1)S(1)}, bf16[384,256]{1,0:T(8,128)(2,1)S(1)}, u32[]{:S(2)}, u32[]{:S(2)}) %collective-permute-start.6) | collective-permute-done | bytes 196640 | tf_op jit(solution)/shard_map/ppermute | solution.py:273
  47.2 1.5 %update.1 = (bf16[2,384,384]{2,1,0:T(8,128)(2,1)S(1)}, bf16[384,256]{1,0:T(8,128)(2,1)S(1)}) custom-call(bf16[384,256]{1,0:T(8,128)(2,1)S(1)} %end.1.refs_0_, bf16[384,256]{1,0:T(8,128)(2,1)S(1)} %collective-permute-done.6.refs_1_, bf16[256,768]{1,0:T(8,128)(2,1)S(1)} %get-tuple-element.57.refs_2_, bf16[256,768]{1,0:T(8,128)(2,1)S(1)} %get-tuple-element.58.refs_3_, ...), custom_call_target="tpu_custom_call" | custom-call | tf_op jit(solution)/shard_map/update/pallas_call | solution.py:22
  49.6 2.3 %begin.3 = (f32[4,384,64]{2,1,0:T(8,128)S(1)}, f32[4,384,2]{2,1,0:T(8,128)S(1)}) custom-call(bf16[384,256]{1,0:T(8,128)(2,1)S(1)} %get-tuple-element.60.query, bf16[384,512]{1,0:T(8,128)(2,1)S(1)} %collective-permute-done.9.refs_0_, bf16[384,512]{1,0:T(8,128)(2,1)S(1)} %collective-permute-done.10.refs_1_), custom_call_target="tpu_custom_call" | custom-call | tf_op jit(solution)/shard_map/begin/pallas_call | solution.py:22
  51.9 4.8 %end_map.1 = (bf16[3,96,256]{2,1,0:T(8,128)(2,1)S(1)}, bf16[3,96,256]{2,1,0:T(8,128)(2,1)S(1)}) custom-call(bf16[384,256]{1,0:T(8,128)(2,1)S(1)} %get-tuple-element.60.query, bf16[384,512]{1,0:T(8,128)(2,1)S(1)} %collective-permute-done.11.refs_0_, bf16[384,512]{1,0:T(8,128)(2,1)S(1)} %collective-permute-done.12.refs_1_, ...), custom_call_target="tpu_custom_call" | custom-call | tf_op jit(solution)/shard_map/end_map/pallas_call | solution.py:22
  56.8 1.4 %collective-permute-start.13 = (bf16[3,96,256]{2,1,0:T(8,128)(2,1)S(1)}, bf16[3,96,256]{2,1,0:T(8,128)(2,1)S(1)}, u32[]{:S(2)}, u32[]{:S(2)}) collective-permute-start(bf16[3,96,256]{2,1,0:T(8,128)(2,1)S(1)} %get-tuple-element.72), channel_id=1, source_target_pairs={{2,0},{0,2},{3,1},{1,3},{6,4},{4,6},{7,5},{5,7},{10,8},{8,10},{11,... | collective-permute-start | bytes 442376 | tf_op jit(solution)/shard_map/ppermute | solution.py:273
  58.6 3.2 %collective-permute-done.13.refs_2_ = bf16[3,96,256]{2,1,0:T(8,128)(2,1)S(1)} collective-permute-done((bf16[3,96,256]{2,1,0:T(8,128)(2,1)S(1)}, bf16[3,96,256]{2,1,0:T(8,128)(2,1)S(1)}, u32[]{:S(2)}, u32[]{:S(2)}) %collective-permute-start.13) | collective-permute-done | bytes 147488 | tf_op jit(solution)/shard_map/ppermute | solution.py:273
  61.9 5.6 %collective-permute-start.14 = (bf16[3,96,256]{2,1,0:T(8,128)(2,1)S(1)}, bf16[3,96,256]{2,1,0:T(8,128)(2,1)S(1)}, u32[]{:S(2)}, u32[]{:S(2)}) collective-permute-start(bf16[3,96,256]{2,1,0:T(8,128)(2,1)S(1)} %add.1), channel_id=1, source_target_pairs={{0,0},{8,1},{4,4},{12,5},{1,8},{9,9},{5,12},{13,13},{2,2},{10,3},{... | collective-permute-start | bytes 442376 | tf_op jit(solution)/shard_map/ppermute | solution.py:387
  67.5 1.9 %collective-permute-start.16 = (bf16[1,96,256]{2,1,0:T(8,128)(2,1)S(1)}, bf16[1,96,256]{2,1,0:T(8,128)(2,1)S(1)}, u32[]{:S(2)}, u32[]{:S(2)}) collective-permute-start(bf16[1,96,256]{2,1,0:T(8,128)(2,1)S(1)} %get-tuple-element.75), channel_id=1, source_target_pairs={{4,0},{12,1},{1,4},{9,5},{5,8},{13,9},{6,2},{14,3},{3,6},{11,7},{7... | collective-permute-start | bytes 147464 | tf_op jit(solution)/shard_map/ppermute | solution.py:386
  69.4 5.4 %collective-permute-start.15 = (bf16[1,96,256]{2,1,0:T(8,128)(2,1)S(1)}, bf16[1,96,256]{2,1,0:T(8,128)(2,1)S(1)}, u32[]{:S(2)}, u32[]{:S(2)}) collective-permute-start(bf16[1,96,256]{2,1,0:T(8,128)(2,1)S(1)} %get-tuple-element.76), channel_id=1, source_target_pairs={{0,4},{8,5},{4,8},{12,9},{1,12},{9,13},{2,6},{10,7},{6,10},{14,11}... | collective-permute-start | bytes 147464 | tf_op jit(solution)/shard_map/ppermute | solution.py:385
  74.9 1.1 %collective-permute-done.15.above = bf16[1,96,256]{2,1,0:T(8,128)(2,1)S(1)} collective-permute-done((bf16[1,96,256]{2,1,0:T(8,128)(2,1)S(1)}, bf16[1,96,256]{2,1,0:T(8,128)(2,1)S(1)}, u32[]{:S(2)}, u32[]{:S(2)}) %collective-permute-start.15) | collective-permute-done | bytes 49184 | tf_op jit(solution)/shard_map/ppermute | solution.py:385
  (24 shorter events, 5.9 us)
Async XLA Ops:
  0.0 10.1 %collective-permute-start.2 = (bf16[384,384]{1,0:T(8,128)(2,1)}, bf16[384,384]{1,0:T(8,128)(2,1)S(1)}, u32[]{:S(2)}, u32[]{:S(2)}) collective-permute-start(bf16[384,384]{1,0:T(8,128)(2,1)} %bitcast.8), channel_id=1, source_target_pairs={{2,0},{0,2},{3,1},{1,3},{6,4},{4,6},{7,5},{5,7},{10,8},{8,10},{11,... | collective-permute-start | bytes 884744 | tf_op jit(solution)/shard_map/ppermute | solution.py:273
  2.0 14.5 %collective-permute-start.1 = (bf16[384,384]{1,0:T(8,128)(2,1)}, bf16[384,384]{1,0:T(8,128)(2,1)S(1)}, u32[]{:S(2)}, u32[]{:S(2)}) collective-permute-start(bf16[384,384]{1,0:T(8,128)(2,1)} %bitcast.10), channel_id=1, source_target_pairs={{2,0},{0,2},{3,8},{1,10},{6,4},{4,6},{7,12},{5,14},{10,1},{8,3},{1... | collective-permute-start | bytes 884744 | tf_op jit(solution)/shard_map/ppermute | solution.py:267
  5.2 14.1 %collective-permute-start = (bf16[384,384]{1,0:T(8,128)(2,1)}, bf16[384,384]{1,0:T(8,128)(2,1)S(1)}, u32[]{:S(2)}, u32[]{:S(2)}) collective-permute-start(bf16[384,384]{1,0:T(8,128)(2,1)} %bitcast.11), channel_id=1, source_target_pairs={{0,0},{2,2},{1,8},{3,10},{4,4},{6,6},{5,12},{7,14},{8,1},{10,3},{9... | collective-permute-start | bytes 884744 | tf_op jit(solution)/shard_map/ppermute | solution.py:267
  20.4 10.9 %collective-permute-start.4 = (bf16[384,512]{1,0:T(8,128)(2,1)S(1)}, bf16[384,512]{1,0:T(8,128)(2,1)S(1)}, u32[]{:S(2)}, u32[]{:S(2)}) collective-permute-start(bf16[384,512]{1,0:T(8,128)(2,1)S(1)} %get-tuple-element.46.refs_0_), channel_id=1, source_target_pairs={{4,0},{0,4},{12,8},{8,12},{5,1},{1,5},{13,9},{9,13},{6,2},{2,6},{1... | collective-permute-start | bytes 1179656 | tf_op jit(solution)/shard_map/ppermute | solution.py:281
  20.9 15.2 %collective-permute-start.9 = (bf16[384,512]{1,0:T(8,128)(2,1)S(1)}, bf16[384,512]{1,0:T(8,128)(2,1)S(1)}, u32[]{:S(2)}, u32[]{:S(2)}) collective-permute-start(bf16[384,512]{1,0:T(8,128)(2,1)S(1)} %project.2), channel_id=1, source_target_pairs={{0,0},{1,8},{4,4},{5,12},{8,1},{9,9},{12,5},{13,13},{2,2},{3,10},{... | collective-permute-start | bytes 1179656 | tf_op jit(solution)/shard_map/ppermute | solution.py:327
  26.4 9.7 %collective-permute-start.3 = (bf16[384,512]{1,0:T(8,128)(2,1)S(1)}, bf16[384,512]{1,0:T(8,128)(2,1)S(1)}, u32[]{:S(2)}, u32[]{:S(2)}) collective-permute-start(bf16[384,512]{1,0:T(8,128)(2,1)S(1)} %get-tuple-element.46.refs_0_), channel_id=1, source_target_pairs={{1,0},{0,1},{3,2},{2,3},{5,4},{4,5},{7,6},{6,7},{9,8},{8,9},{11,10... | collective-permute-start | bytes 1179656 | tf_op jit(solution)/shard_map/ppermute | solution.py:287
  31.3 4.9 %collective-permute-start.5 = (bf16[384,512]{1,0:T(8,128)(2,1)S(1)}, bf16[384,512]{1,0:T(8,128)(2,1)S(1)}, u32[]{:S(2)}, u32[]{:S(2)}) collective-permute-start(bf16[384,512]{1,0:T(8,128)(2,1)S(1)} %collective-permute-done.4.refs_1_), channel_id=1, source_target_pairs={{1,0},{0,1},{3,2},{2,3},{5,4},{4,5},{7,6},{6,7},{9,8},{8,9},{11,10... | collective-permute-start | bytes 1179656 | tf_op jit(solution)/shard_map/ppermute | solution.py:287
  31.3 8.1 %collective-permute-start.7 = (bf16[192,768]{1,0:T(8,128)(2,1)S(1)}, bf16[192,768]{1,0:T(8,128)(2,1)S(1)}, u32[]{:S(2)}, u32[]{:S(2)}) collective-permute-start(bf16[192,768]{1,0:T(8,128)(2,1)S(1)} %get-tuple-element.52), channel_id=1, source_target_pairs={{2,0},{0,2},{3,1},{1,3},{6,4},{4,6},{7,5},{5,7},{10,8},{8,10},{11,... | collective-permute-start | bytes 884744 | tf_op jit(solution)/shard_map/ppermute | solution.py:273
  36.1 12.5 %collective-permute-start.10 = (bf16[384,512]{1,0:T(8,128)(2,1)S(1)}, bf16[384,512]{1,0:T(8,128)(2,1)S(1)}, u32[]{:S(2)}, u32[]{:S(2)}) collective-permute-start(bf16[384,512]{1,0:T(8,128)(2,1)S(1)} %collective-permute-done.9.refs_0_), channel_id=1, source_target_pairs={{4,0},{0,4},{12,8},{8,12},{5,1},{1,5},{13,9},{9,13},{6,2},{2,6},{1... | collective-permute-start | bytes 1179656 | tf_op jit(solution)/shard_map/ppermute | solution.py:281
  39.3 2.7 %collective-permute-start.8 = (bf16[192,768]{1,0:T(8,128)(2,1)S(1)}, bf16[192,768]{1,0:T(8,128)(2,1)S(1)}, u32[]{:S(2)}, u32[]{:S(2)}) collective-permute-start(bf16[192,768]{1,0:T(8,128)(2,1)S(1)} %collective-permute-done.7.refs_0_), channel_id=1, source_target_pairs={{1,0},{0,1},{3,2},{2,3},{5,4},{4,5},{7,6},{6,7},{9,8},{8,9},{11,10... | collective-permute-start | bytes 884744 | tf_op jit(solution)/shard_map/ppermute | solution.py:287
  40.7 6.5 %collective-permute-start.6 = (bf16[384,256]{1,0:T(8,128)(2,1)S(1)}, bf16[384,256]{1,0:T(8,128)(2,1)S(1)}, u32[]{:S(2)}, u32[]{:S(2)}) collective-permute-start(bf16[384,256]{1,0:T(8,128)(2,1)S(1)} %end.1.refs_0_), channel_id=1, source_target_pairs={{2,0},{0,2},{3,1},{1,3},{6,4},{4,6},{7,5},{5,7},{10,8},{8,10},{11,... | collective-permute-start | bytes 589832 | tf_op jit(solution)/shard_map/ppermute | solution.py:273
  48.7 3.2 %collective-permute-start.11 = (bf16[384,512]{1,0:T(8,128)(2,1)S(1)}, bf16[384,512]{1,0:T(8,128)(2,1)S(1)}, u32[]{:S(2)}, u32[]{:S(2)}) collective-permute-start(bf16[384,512]{1,0:T(8,128)(2,1)S(1)} %collective-permute-done.9.refs_0_), channel_id=1, source_target_pairs={{1,0},{0,1},{3,2},{2,3},{5,4},{4,5},{7,6},{6,7},{9,8},{8,9},{11,10... | collective-permute-start | bytes 1179656 | tf_op jit(solution)/shard_map/ppermute | solution.py:287
  49.5 2.4 %collective-permute-start.12 = (bf16[384,512]{1,0:T(8,128)(2,1)S(1)}, bf16[384,512]{1,0:T(8,128)(2,1)S(1)}, u32[]{:S(2)}, u32[]{:S(2)}) collective-permute-start(bf16[384,512]{1,0:T(8,128)(2,1)S(1)} %collective-permute-done.10.refs_1_), channel_id=1, source_target_pairs={{1,0},{0,1},{3,2},{2,3},{5,4},{4,5},{7,6},{6,7},{9,8},{8,9},{11,10... | collective-permute-start | bytes 1179656 | tf_op jit(solution)/shard_map/ppermute | solution.py:287
  56.8 5.1 %collective-permute-start.13 = (bf16[3,96,256]{2,1,0:T(8,128)(2,1)S(1)}, bf16[3,96,256]{2,1,0:T(8,128)(2,1)S(1)}, u32[]{:S(2)}, u32[]{:S(2)}) collective-permute-start(bf16[3,96,256]{2,1,0:T(8,128)(2,1)S(1)} %get-tuple-element.72), channel_id=1, source_target_pairs={{2,0},{0,2},{3,1},{1,3},{6,4},{4,6},{7,5},{5,7},{10,8},{8,10},{11,... | collective-permute-start | bytes 442376 | tf_op jit(solution)/shard_map/ppermute | solution.py:273
  61.9 14.2 %collective-permute-start.14 = (bf16[3,96,256]{2,1,0:T(8,128)(2,1)S(1)}, bf16[3,96,256]{2,1,0:T(8,128)(2,1)S(1)}, u32[]{:S(2)}, u32[]{:S(2)}) collective-permute-start(bf16[3,96,256]{2,1,0:T(8,128)(2,1)S(1)} %add.1), channel_id=1, source_target_pairs={{0,0},{8,1},{4,4},{12,5},{1,8},{9,9},{5,12},{13,13},{2,2},{10,3},{... | collective-permute-start | bytes 442376 | tf_op jit(solution)/shard_map/ppermute | solution.py:387
  67.5 7.4 %collective-permute-start.16 = (bf16[1,96,256]{2,1,0:T(8,128)(2,1)S(1)}, bf16[1,96,256]{2,1,0:T(8,128)(2,1)S(1)}, u32[]{:S(2)}, u32[]{:S(2)}) collective-permute-start(bf16[1,96,256]{2,1,0:T(8,128)(2,1)S(1)} %get-tuple-element.75), channel_id=1, source_target_pairs={{4,0},{12,1},{1,4},{9,5},{5,8},{13,9},{6,2},{14,3},{3,6},{11,7},{7... | collective-permute-start | bytes 147464 | tf_op jit(solution)/shard_map/ppermute | solution.py:386
  69.4 6.6 %collective-permute-start.15 = (bf16[1,96,256]{2,1,0:T(8,128)(2,1)S(1)}, bf16[1,96,256]{2,1,0:T(8,128)(2,1)S(1)}, u32[]{:S(2)}, u32[]{:S(2)}) collective-permute-start(bf16[1,96,256]{2,1,0:T(8,128)(2,1)S(1)} %get-tuple-element.76), channel_id=1, source_target_pairs={{0,4},{8,5},{4,8},{12,9},{1,12},{9,13},{2,6},{10,7},{6,10},{14,11}... | collective-permute-start | bytes 147464 | tf_op jit(solution)/shard_map/ppermute | solution.py:385

commit v13 on v12

--- a/solution.py
+++ b/solution.py
@@ -324,18 +324,16 @@
     (right_pack,) = project(right, cross_qkv, False, 1)
     left, right_pack = lax.optimization_barrier((left, right_pack))
     query, pack = project(left, self_qkv, True, 0)
-    right_pack = lax.ppermute(tied(right_pack, pack), both, there)
     beside = neighbours(pack)
-    near = [pack, *beside]
+    halves = tile_pieces(tied(half, pack))[1:]
+    right_pack = lax.ppermute(tied(right_pack, beside), both, there)
+    near, halves = lax.optimization_barrier(([pack, *beside], halves))
     far = [q for p in near for q in across(p)]
     state = begin(query, near)
-    right_pack = tied(right_pack, state)
-    right_near = [right_pack, *neighbours(right_pack)]
-    halves = tile_pieces(tied(half, beside))[1:]
+    halves = tied(halves, state)
     (mixed,) = run_kernel(
         end_kernel, "end", [((rows, columns), BF16)], [query, *grouped(far), *state]
     )
-    halves = tied(halves, mixed)
     others = [
         run_kernel(
             unpack_kernel,
@@ -349,6 +347,9 @@
     (composed,) = run_kernel(
         compose_kernel, "compose", [((columns, channels), BF16)], [cross_out, *map_weights]
     )
+    right_pack = tied(right_pack, composed)
+    right_near = [right_pack, *across(right_pack)]
+    right_beside = neighbours(right_pack)
     mixed, composed = lax.optimization_barrier((tile_pieces(mixed), composed))
     updated, cross_query = run_kernel(
         functools.partial(update_kernel, count=tiles),
@@ -362,10 +363,9 @@
             cross_qkv.reshape(3, tiles, share, columns),
         ],
     )
-    right_near = tied(right_near, updated)
-    right_far = [q for p in right_near for q in across(p)]
     state = begin(cross_query, right_near)
-    right_far = tied(right_far, state)
+    right_beside = tied(right_beside, state)
+    right_far = [*right_beside, *[q for p in right_beside for q in across(p)]]
     maps = run_kernel(
         functools.partial(end_map_kernel, count=tiles),
         "end_map",

time: 77.3 us -> 84.9 us (1.098)
  waiting for transfers between devices: 24 us -> 32.6 us
  starting transfers between devices: 32.7 us -> 31.6 us
    ppermute x1, waiting for transfers between devices: 1.21 us -> 5.81 us  [body(): right_pack = lax.ppermute(tied(right_pack, beside), both, there)]
    ppermute x5, waiting for transfers between devices: 0.01 us -> 2.35 us  [across(): lax.ppermute(pack, 'pair', [((i + s) % cores, i) for i in range(cores)])]
    ppermute x2, waiting for transfers between devices: 4.75 us -> 6.64 us  [neighbours(): lax.ppermute(pack, 'blk', [(g + (i + s) % span, g + i) for g, i in ring])]
    ppermute x1, starting transfers between devices: 5.5 us -> 4.06 us  [body(): right_pack = lax.ppermute(tied(right_pack, beside), both, there)]
  transfers between devices with their start and end apart: 17 -> 17, of which waited for: 9 -> 10; matrix products, arithmetic and copies ran while one was open for 0% -> 0% of each run, Pallas kernels for 17% -> 16%
where the time goes in v13:
time: 84.9 us; the launch traced here: 84.6 us
  waiting for transfers between devices  32.6 us (38%)
  starting transfers between devices  31.6 us (37%)
  Pallas kernels  20.3 us (24%)
    pallas_call x13, Pallas kernels, run_kernel(): pl.pallas_call(kernel, out_shape=[jax.ShapeDtypeStruct(*s) for s in shape...  20.3 us
    ppermute x2, waiting for transfers between devices, fetched(): return lax.ppermute(value, ('blk', 'tile', 'pair'), pairs)  8.33 us
    ppermute x4, waiting for transfers between devices, from_tile(): lax.ppermute(value, 'tile', [((i + step) % tiles, i) for i in range(tiles)])  8.32 us
    ppermute x2, waiting for transfers between devices, neighbours(): lax.ppermute(pack, 'blk', [(g + (i + s) % span, g + i) for g, i in ring])  6.64 us
    ppermute x1, starting transfers between devices, body(): features = lax.ppermute(features, both, back)  6.34 us
    ppermute x4, starting transfers between devices, from_tile(): lax.ppermute(value, 'tile', [((i + step) % tiles, i) for i in range(tiles)])  5.99 us
    ppermute x1, waiting for transfers between devices, body(): right_pack = lax.ppermute(tied(right_pack, beside), both, there)  5.81 us
    ppermute x1, starting transfers between devices, body(): above = lax.ppermute(features[-1:], both, down)  5.44 us
  transfers between devices with their start and end apart: 17, of which 10 were waited for; matrix products, arithmetic and copies ran while one was open for 0% of the time, Pallas kernels for 16%

profile of v13, /device:TPU:1, one launch (start us, length us, event | category | flops | bytes accessed | tf_op | source)
XLA Modules:
  0.0 84.6 jit_solution(16021833039201607784)
XLA Ops:
  0.0 2.0 %collective-permute-start.2 = (bf16[384,384]{1,0:T(8,128)(2,1)}, bf16[384,384]{1,0:T(8,128)(2,1)S(1)}, u32[]{:S(2)}, u32[]{:S(2)}) collective-permute-start(bf16[384,384]{1,0:T(8,128)(2,1)} %bitcast.8), channel_id=1, source_target_pairs={{2,0},{0,2},{3,1},{1,3},{6,4},{4,6},{7,5},{5,7},{10,8},{8,10},{11,... | collective-permute-start | bytes 884744 | tf_op jit(solution)/shard_map/ppermute | solution.py:273
  2.0 3.1 %collective-permute-start.1 = (bf16[384,384]{1,0:T(8,128)(2,1)}, bf16[384,384]{1,0:T(8,128)(2,1)S(1)}, u32[]{:S(2)}, u32[]{:S(2)}) collective-permute-start(bf16[384,384]{1,0:T(8,128)(2,1)} %bitcast.10), channel_id=1, source_target_pairs={{2,0},{0,2},{3,8},{1,10},{6,4},{4,6},{7,12},{5,14},{10,1},{8,3},{1... | collective-permute-start | bytes 884744 | tf_op jit(solution)/shard_map/ppermute | solution.py:267
  5.2 1.9 %collective-permute-start = (bf16[384,384]{1,0:T(8,128)(2,1)}, bf16[384,384]{1,0:T(8,128)(2,1)S(1)}, u32[]{:S(2)}, u32[]{:S(2)}) collective-permute-start(bf16[384,384]{1,0:T(8,128)(2,1)} %bitcast.11), channel_id=1, source_target_pairs={{0,0},{2,2},{1,8},{3,10},{4,4},{6,6},{5,12},{7,14},{8,1},{10,3},{9... | collective-permute-start | bytes 884744 | tf_op jit(solution)/shard_map/ppermute | solution.py:267
  7.1 2.6 %stage.1 = (bf16[256,768]{1,0:T(8,128)(2,1)S(1)}, bf16[384,256]{1,0:T(8,128)(2,1)S(1)}, bf16[256,768]{1,0:T(8,128)(2,1)S(1)}, bf16[384,384]{1,0:T(8,128)(2,1)S(1...) custom-call(bf16[256,768]{1,0:T(8,128)(2,1)} %refs_0_.1, ...), custom_call_target="tpu_custom_call" | custom-call | tf_op jit(solution)/shard_map/stage/pallas_call | solution.py:22
  11.0 5.6 %collective-permute-done.1.refs_1_.refs_5_ = bf16[384,384]{1,0:T(8,128)(2,1)S(1)} collective-permute-done((bf16[384,384]{1,0:T(8,128)(2,1)}, bf16[384,384]{1,0:T(8,128)(2,1)S(1)}, u32[]{:S(2)}, u32[]{:S(2)}) %collective-permute-start.1) | collective-permute-done | bytes 294944 | tf_op jit(solution)/shard_map/ppermute | solution.py:267
  16.5 2.8 %collective-permute-done.refs_0_.refs_4_ = bf16[384,384]{1,0:T(8,128)(2,1)S(1)} collective-permute-done((bf16[384,384]{1,0:T(8,128)(2,1)}, bf16[384,384]{1,0:T(8,128)(2,1)S(1)}, u32[]{:S(2)}, u32[]{:S(2)}) %collective-permute-start) | collective-permute-done | bytes 294944 | tf_op jit(solution)/shard_map/ppermute | solution.py:267
  20.9 1.2 %collective-permute-start.4 = (bf16[192,768]{1,0:T(8,128)(2,1)S(1)}, bf16[192,768]{1,0:T(8,128)(2,1)S(1)}, u32[]{:S(2)}, u32[]{:S(2)}) collective-permute-start(bf16[192,768]{1,0:T(8,128)(2,1)S(1)} %get-tuple-element.48), channel_id=1, source_target_pairs={{2,0},{0,2},{3,1},{1,3},{6,4},{4,6},{7,5},{5,7},{10,8},{8,10},{11,... | collective-permute-start | bytes 884744 | tf_op jit(solution)/shard_map/ppermute | solution.py:273
  22.2 6.6 %collective-permute-done.3.refs_1_ = bf16[384,512]{1,0:T(8,128)(2,1)S(1)} collective-permute-done((bf16[384,512]{1,0:T(8,128)(2,1)S(1)}, bf16[384,512]{1,0:T(8,128)(2,1)S(1)}, u32[]{:S(2)}, u32[]{:S(2)}) %collective-permute-start.3) | collective-permute-done | bytes 393248 | tf_op jit(solution)/shard_map/ppermute | solution.py:281
  28.8 4.1 %collective-permute-start.9 = (bf16[384,512]{1,0:T(8,128)(2,1)S(1)}, bf16[384,512]{1,0:T(8,128)(2,1)S(1)}, u32[]{:S(2)}, u32[]{:S(2)}) collective-permute-start(bf16[384,512]{1,0:T(8,128)(2,1)S(1)} %project.2), channel_id=1, source_target_pairs={{0,0},{1,8},{4,4},{5,12},{8,1},{9,9},{12,5},{13,13},{2,2},{3,10},{... | collective-permute-start | bytes 1179656 | tf_op jit(solution)/shard_map/ppermute | solution.py:329
  32.9 2.3 %begin.2 = (f32[4,384,64]{2,1,0:T(8,128)S(1)}, f32[4,384,2]{2,1,0:T(8,128)S(1)}) custom-call(bf16[384,256]{1,0:T(8,128)(2,1)S(1)} %get-tuple-element.45.query, bf16[384,512]{1,0:T(8,128)(2,1)S(1)} %get-tuple-element.49.refs_0_, bf16[384,512]{1,0:T(8,128)(2,1)S(1)} %collective-permute-done.3.refs_1_), custom_call_target="tpu_custom_call" | custom-call | tf_op jit(solution)/shard_map/begin/pallas_call | solution.py:22
  37.2 5.8 %collective-permute-done.9.refs_0_ = bf16[384,512]{1,0:T(8,128)(2,1)S(1)} collective-permute-done((bf16[384,512]{1,0:T(8,128)(2,1)S(1)}, bf16[384,512]{1,0:T(8,128)(2,1)S(1)}, u32[]{:S(2)}, u32[]{:S(2)}) %collective-permute-start.9) | collective-permute-done | bytes 393248 | tf_op jit(solution)/shard_map/ppermute | solution.py:329
  43.0 3.1 %end.1.refs_0_ = bf16[384,256]{1,0:T(8,128)(2,1)S(1)} custom-call(bf16[384,256]{1,0:T(8,128)(2,1)S(1)} %get-tuple-element.45.query, bf16[384,512]{1,0:T(8,128)(2,1)S(1)} %collective-permute-done.5.refs_0_, bf16[384,512]{1,0:T(8,128)(2,1)S(1)} %collective-permute-done.6.refs_1_, f32[4,384,64]{2,1,0:T(8,128)S(1)} %get-tuple-element.51.refs_2_, ...), custom_call_target="tpu_custom_call" | custom-call | tf_op jit(solution)/shard_map/end/pallas_call | solution.py:22
  46.1 1.4 %collective-permute-start.7 = (bf16[384,256]{1,0:T(8,128)(2,1)S(1)}, bf16[384,256]{1,0:T(8,128)(2,1)S(1)}, u32[]{:S(2)}, u32[]{:S(2)}) collective-permute-start(bf16[384,256]{1,0:T(8,128)(2,1)S(1)} %end.1.refs_0_), channel_id=1, source_target_pairs={{2,0},{0,2},{3,1},{1,3},{6,4},{4,6},{7,5},{5,7},{10,8},{8,10},{11,... | collective-permute-start | bytes 589832 | tf_op jit(solution)/shard_map/ppermute | solution.py:273
  47.5 4.5 %collective-permute-done.7.refs_1_ = bf16[384,256]{1,0:T(8,128)(2,1)S(1)} collective-permute-done((bf16[384,256]{1,0:T(8,128)(2,1)S(1)}, bf16[384,256]{1,0:T(8,128)(2,1)S(1)}, u32[]{:S(2)}, u32[]{:S(2)}) %collective-permute-start.7) | collective-permute-done | bytes 196640 | tf_op jit(solution)/shard_map/ppermute | solution.py:273
  52.0 1.5 %update.1 = (bf16[2,384,384]{2,1,0:T(8,128)(2,1)S(1)}, bf16[384,256]{1,0:T(8,128)(2,1)S(1)}) custom-call(bf16[384,256]{1,0:T(8,128)(2,1)S(1)} %end.1.refs_0_, bf16[384,256]{1,0:T(8,128)(2,1)S(1)} %collective-permute-done.7.refs_1_, bf16[256,768]{1,0:T(8,128)(2,1)S(1)} %get-tuple-element.60.refs_2_, bf16[256,768]{1,0:T(8,128)(2,1)S(1)} %get-tuple-element.61.refs_3_, ...), custom_call_target="tpu_custom_call" | custom-call | tf_op jit(solution)/shard_map/update/pallas_call | solution.py:22
  53.5 2.3 %begin.3 = (f32[4,384,64]{2,1,0:T(8,128)S(1)}, f32[4,384,2]{2,1,0:T(8,128)S(1)}) custom-call(bf16[384,256]{1,0:T(8,128)(2,1)S(1)} %get-tuple-element.63.query, bf16[384,512]{1,0:T(8,128)(2,1)S(1)} %collective-permute-done.9.refs_0_, bf16[384,512]{1,0:T(8,128)(2,1)S(1)} %collective-permute-done.11.refs_1_), custom_call_target="tpu_custom_call" | custom-call | tf_op jit(solution)/shard_map/begin/pallas_call | solution.py:22
  55.8 1.6 %collective-permute-start.12 = (bf16[384,512]{1,0:T(8,128)(2,1)S(1)}, bf16[384,512]{1,0:T(8,128)(2,1)S(1)}, u32[]{:S(2)}, u32[]{:S(2)}) collective-permute-start(bf16[384,512]{1,0:T(8,128)(2,1)S(1)} %collective-permute-done.10.refs_0_), channel_id=1, source_target_pairs={{1,0},{0,1},{3,2},{2,3},{5,4},{4,5},{7,6},{6,7},{9,8},{8,9},{11,10... | collective-permute-start | bytes 1179656 | tf_op jit(solution)/shard_map/ppermute | solution.py:287
  57.3 1.3 %collective-permute-done.12.refs_1_ = bf16[384,512]{1,0:T(8,128)(2,1)S(1)} collective-permute-done((bf16[384,512]{1,0:T(8,128)(2,1)S(1)}, bf16[384,512]{1,0:T(8,128)(2,1)S(1)}, u32[]{:S(2)}, u32[]{:S(2)}) %collective-permute-start.12) | collective-permute-done | bytes 393248 | tf_op jit(solution)/shard_map/ppermute | solution.py:287
  58.7 4.8 %end_map.1 = (bf16[3,96,256]{2,1,0:T(8,128)(2,1)S(1)}, bf16[3,96,256]{2,1,0:T(8,128)(2,1)S(1)}) custom-call(bf16[384,256]{1,0:T(8,128)(2,1)S(1)} %get-tuple-element.63.query, bf16[384,512]{1,0:T(8,128)(2,1)S(1)} %collective-permute-done.10.refs_0_, bf16[384,512]{1,0:T(8,128)(2,1)S(1)} %collective-permute-done.12.refs_1_, ...), custom_call_target="tpu_custom_call" | custom-call | tf_op jit(solution)/shard_map/end_map/pallas_call | solution.py:22
  63.5 1.4 %collective-permute-start.13 = (bf16[3,96,256]{2,1,0:T(8,128)(2,1)S(1)}, bf16[3,96,256]{2,1,0:T(8,128)(2,1)S(1)}, u32[]{:S(2)}, u32[]{:S(2)}) collective-permute-start(bf16[3,96,256]{2,1,0:T(8,128)(2,1)S(1)} %get-tuple-element.72), channel_id=1, source_target_pairs={{2,0},{0,2},{3,1},{1,3},{6,4},{4,6},{7,5},{5,7},{10,8},{8,10},{11,... | collective-permute-start | bytes 442376 | tf_op jit(solution)/shard_map/ppermute | solution.py:273
  65.3 3.4 %collective-permute-done.13.refs_2_ = bf16[3,96,256]{2,1,0:T(8,128)(2,1)S(1)} collective-permute-done((bf16[3,96,256]{2,1,0:T(8,128)(2,1)S(1)}, bf16[3,96,256]{2,1,0:T(8,128)(2,1)S(1)}, u32[]{:S(2)}, u32[]{:S(2)}) %collective-permute-start.13) | collective-permute-done | bytes 147488 | tf_op jit(solution)/shard_map/ppermute | solution.py:273
  68.7 6.3 %collective-permute-start.14 = (bf16[3,96,256]{2,1,0:T(8,128)(2,1)S(1)}, bf16[3,96,256]{2,1,0:T(8,128)(2,1)S(1)}, u32[]{:S(2)}, u32[]{:S(2)}) collective-permute-start(bf16[3,96,256]{2,1,0:T(8,128)(2,1)S(1)} %add.1), channel_id=1, source_target_pairs={{0,0},{8,1},{4,4},{12,5},{1,8},{9,9},{5,12},{13,13},{2,2},{10,3},{... | collective-permute-start | bytes 442376 | tf_op jit(solution)/shard_map/ppermute | solution.py:387
  75.1 1.9 %collective-permute-start.16 = (bf16[1,96,256]{2,1,0:T(8,128)(2,1)S(1)}, bf16[1,96,256]{2,1,0:T(8,128)(2,1)S(1)}, u32[]{:S(2)}, u32[]{:S(2)}) collective-permute-start(bf16[1,96,256]{2,1,0:T(8,128)(2,1)S(1)} %get-tuple-element.75), channel_id=1, source_target_pairs={{4,0},{12,1},{1,4},{9,5},{5,8},{13,9},{6,2},{14,3},{3,6},{11,7},{7... | collective-permute-start | bytes 147464 | tf_op jit(solution)/shard_map/ppermute | solution.py:386
  77.0 5.4 %collective-permute-start.15 = (bf16[1,96,256]{2,1,0:T(8,128)(2,1)S(1)}, bf16[1,96,256]{2,1,0:T(8,128)(2,1)S(1)}, u32[]{:S(2)}, u32[]{:S(2)}) collective-permute-start(bf16[1,96,256]{2,1,0:T(8,128)(2,1)S(1)} %get-tuple-element.76), channel_id=1, source_target_pairs={{0,4},{8,5},{4,8},{12,9},{1,12},{9,13},{2,6},{10,7},{6,10},{14,11}... | collective-permute-start | bytes 147464 | tf_op jit(solution)/shard_map/ppermute | solution.py:385
  (24 shorter events, 7.6 us)
Async XLA Ops:
  0.0 10.1 %collective-permute-start.2 = (bf16[384,384]{1,0:T(8,128)(2,1)}, bf16[384,384]{1,0:T(8,128)(2,1)S(1)}, u32[]{:S(2)}, u32[]{:S(2)}) collective-permute-start(bf16[384,384]{1,0:T(8,128)(2,1)} %bitcast.8), channel_id=1, source_target_pairs={{2,0},{0,2},{3,1},{1,3},{6,4},{4,6},{7,5},{5,7},{10,8},{8,10},{11,... | collective-permute-start | bytes 884744 | tf_op jit(solution)/shard_map/ppermute | solution.py:273
  2.0 14.5 %collective-permute-start.1 = (bf16[384,384]{1,0:T(8,128)(2,1)}, bf16[384,384]{1,0:T(8,128)(2,1)S(1)}, u32[]{:S(2)}, u32[]{:S(2)}) collective-permute-start(bf16[384,384]{1,0:T(8,128)(2,1)} %bitcast.10), channel_id=1, source_target_pairs={{2,0},{0,2},{3,8},{1,10},{6,4},{4,6},{7,12},{5,14},{10,1},{8,3},{1... | collective-permute-start | bytes 884744 | tf_op jit(solution)/shard_map/ppermute | solution.py:267
  5.2 14.1 %collective-permute-start = (bf16[384,384]{1,0:T(8,128)(2,1)}, bf16[384,384]{1,0:T(8,128)(2,1)S(1)}, u32[]{:S(2)}, u32[]{:S(2)}) collective-permute-start(bf16[384,384]{1,0:T(8,128)(2,1)} %bitcast.11), channel_id=1, source_target_pairs={{0,0},{2,2},{1,8},{3,10},{4,4},{6,6},{5,12},{7,14},{8,1},{10,3},{9... | collective-permute-start | bytes 884744 | tf_op jit(solution)/shard_map/ppermute | solution.py:267
  20.4 8.4 %collective-permute-start.3 = (bf16[384,512]{1,0:T(8,128)(2,1)S(1)}, bf16[384,512]{1,0:T(8,128)(2,1)S(1)}, u32[]{:S(2)}, u32[]{:S(2)}) collective-permute-start(bf16[384,512]{1,0:T(8,128)(2,1)S(1)} %get-tuple-element.49.refs_0_), channel_id=1, source_target_pairs={{4,0},{0,4},{12,8},{8,12},{5,1},{1,5},{13,9},{9,13},{6,2},{2,6},{1... | collective-permute-start | bytes 1179656 | tf_op jit(solution)/shard_map/ppermute | solution.py:281
  20.9 11.9 %collective-permute-start.4 = (bf16[192,768]{1,0:T(8,128)(2,1)S(1)}, bf16[192,768]{1,0:T(8,128)(2,1)S(1)}, u32[]{:S(2)}, u32[]{:S(2)}) collective-permute-start(bf16[192,768]{1,0:T(8,128)(2,1)S(1)} %get-tuple-element.48), channel_id=1, source_target_pairs={{2,0},{0,2},{3,1},{1,3},{6,4},{4,6},{7,5},{5,7},{10,8},{8,10},{11,... | collective-permute-start | bytes 884744 | tf_op jit(solution)/shard_map/ppermute | solution.py:273
  28.8 14.2 %collective-permute-start.9 = (bf16[384,512]{1,0:T(8,128)(2,1)S(1)}, bf16[384,512]{1,0:T(8,128)(2,1)S(1)}, u32[]{:S(2)}, u32[]{:S(2)}) collective-permute-start(bf16[384,512]{1,0:T(8,128)(2,1)S(1)} %project.2), channel_id=1, source_target_pairs={{0,0},{1,8},{4,4},{5,12},{8,1},{9,9},{12,5},{13,13},{2,2},{3,10},{... | collective-permute-start | bytes 1179656 | tf_op jit(solution)/shard_map/ppermute | solution.py:329
  35.2 1.6 %collective-permute-start.8 = (bf16[192,768]{1,0:T(8,128)(2,1)S(1)}, bf16[192,768]{1,0:T(8,128)(2,1)S(1)}, u32[]{:S(2)}, u32[]{:S(2)}) collective-permute-start(bf16[192,768]{1,0:T(8,128)(2,1)S(1)} %collective-permute-done.4.refs_0_), channel_id=1, source_target_pairs={{1,0},{0,1},{3,2},{2,3},{5,4},{4,5},{7,6},{6,7},{9,8},{8,9},{11,10... | collective-permute-start | bytes 884744 | tf_op jit(solution)/shard_map/ppermute | solution.py:287
  35.2 7.8 %collective-permute-start.5 = (bf16[384,512]{1,0:T(8,128)(2,1)S(1)}, bf16[384,512]{1,0:T(8,128)(2,1)S(1)}, u32[]{:S(2)}, u32[]{:S(2)}) collective-permute-start(bf16[384,512]{1,0:T(8,128)(2,1)S(1)} %get-tuple-element.49.refs_0_), channel_id=1, source_target_pairs={{1,0},{0,1},{3,2},{2,3},{5,4},{4,5},{7,6},{6,7},{9,8},{8,9},{11,10... | collective-permute-start | bytes 1179656 | tf_op jit(solution)/shard_map/ppermute | solution.py:287
  35.7 7.3 %collective-permute-start.6 = (bf16[384,512]{1,0:T(8,128)(2,1)S(1)}, bf16[384,512]{1,0:T(8,128)(2,1)S(1)}, u32[]{:S(2)}, u32[]{:S(2)}) collective-permute-start(bf16[384,512]{1,0:T(8,128)(2,1)S(1)} %collective-permute-done.3.refs_1_), channel_id=1, source_target_pairs={{1,0},{0,1},{3,2},{2,3},{5,4},{4,5},{7,6},{6,7},{9,8},{8,9},{11,10... | collective-permute-start | bytes 1179656 | tf_op jit(solution)/shard_map/ppermute | solution.py:287
  43.0 10.5 %collective-permute-start.11 = (bf16[384,512]{1,0:T(8,128)(2,1)S(1)}, bf16[384,512]{1,0:T(8,128)(2,1)S(1)}, u32[]{:S(2)}, u32[]{:S(2)}) collective-permute-start(bf16[384,512]{1,0:T(8,128)(2,1)S(1)} %collective-permute-done.9.refs_0_), channel_id=1, source_target_pairs={{1,0},{0,1},{3,2},{2,3},{5,4},{4,5},{7,6},{6,7},{9,8},{8,9},{11,10... | collective-permute-start | bytes 1179656 | tf_op jit(solution)/shard_map/ppermute | solution.py:287
  43.0 12.8 %collective-permute-start.10 = (bf16[384,512]{1,0:T(8,128)(2,1)S(1)}, bf16[384,512]{1,0:T(8,128)(2,1)S(1)}, u32[]{:S(2)}, u32[]{:S(2)}) collective-permute-start(bf16[384,512]{1,0:T(8,128)(2,1)S(1)} %collective-permute-done.9.refs_0_), channel_id=1, source_target_pairs={{4,0},{0,4},{12,8},{8,12},{5,1},{1,5},{13,9},{9,13},{6,2},{2,6},{1... | collective-permute-start | bytes 1179656 | tf_op jit(solution)/shard_map/ppermute | solution.py:281
  46.1 5.9 %collective-permute-start.7 = (bf16[384,256]{1,0:T(8,128)(2,1)S(1)}, bf16[384,256]{1,0:T(8,128)(2,1)S(1)}, u32[]{:S(2)}, u32[]{:S(2)}) collective-permute-start(bf16[384,256]{1,0:T(8,128)(2,1)S(1)} %end.1.refs_0_), channel_id=1, source_target_pairs={{2,0},{0,2},{3,1},{1,3},{6,4},{4,6},{7,5},{5,7},{10,8},{8,10},{11,... | collective-permute-start | bytes 589832 | tf_op jit(solution)/shard_map/ppermute | solution.py:273
  55.8 2.9 %collective-permute-start.12 = (bf16[384,512]{1,0:T(8,128)(2,1)S(1)}, bf16[384,512]{1,0:T(8,128)(2,1)S(1)}, u32[]{:S(2)}, u32[]{:S(2)}) collective-permute-start(bf16[384,512]{1,0:T(8,128)(2,1)S(1)} %collective-permute-done.10.refs_0_), channel_id=1, source_target_pairs={{1,0},{0,1},{3,2},{2,3},{5,4},{4,5},{7,6},{6,7},{9,8},{8,9},{11,10... | collective-permute-start | bytes 1179656 | tf_op jit(solution)/shard_map/ppermute | solution.py:287
  63.5 5.1 %collective-permute-start.13 = (bf16[3,96,256]{2,1,0:T(8,128)(2,1)S(1)}, bf16[3,96,256]{2,1,0:T(8,128)(2,1)S(1)}, u32[]{:S(2)}, u32[]{:S(2)}) collective-permute-start(bf16[3,96,256]{2,1,0:T(8,128)(2,1)S(1)} %get-tuple-element.72), channel_id=1, source_target_pairs={{2,0},{0,2},{3,1},{1,3},{6,4},{4,6},{7,5},{5,7},{10,8},{8,10},{11,... | collective-permute-start | bytes 442376 | tf_op jit(solution)/shard_map/ppermute | solution.py:273
  68.7 14.9 %collective-permute-start.14 = (bf16[3,96,256]{2,1,0:T(8,128)(2,1)S(1)}, bf16[3,96,256]{2,1,0:T(8,128)(2,1)S(1)}, u32[]{:S(2)}, u32[]{:S(2)}) collective-permute-start(bf16[3,96,256]{2,1,0:T(8,128)(2,1)S(1)} %add.1), channel_id=1, source_target_pairs={{0,0},{8,1},{4,4},{12,5},{1,8},{9,9},{5,12},{13,13},{2,2},{10,3},{... | collective-permute-start | bytes 442376 | tf_op jit(solution)/shard_map/ppermute | solution.py:387
  75.1 7.4 %collective-permute-start.16 = (bf16[1,96,256]{2,1,0:T(8,128)(2,1)S(1)}, bf16[1,96,256]{2,1,0:T(8,128)(2,1)S(1)}, u32[]{:S(2)}, u32[]{:S(2)}) collective-permute-start(bf16[1,96,256]{2,1,0:T(8,128)(2,1)S(1)} %get-tuple-element.75), channel_id=1, source_target_pairs={{4,0},{12,1},{1,4},{9,5},{5,8},{13,9},{6,2},{14,3},{3,6},{11,7},{7... | collective-permute-start | bytes 147464 | tf_op jit(solution)/shard_map/ppermute | solution.py:386
  77.0 6.6 %collective-permute-start.15 = (bf16[1,96,256]{2,1,0:T(8,128)(2,1)S(1)}, bf16[1,96,256]{2,1,0:T(8,128)(2,1)S(1)}, u32[]{:S(2)}, u32[]{:S(2)}) collective-permute-start(bf16[1,96,256]{2,1,0:T(8,128)(2,1)S(1)} %get-tuple-element.76), channel_id=1, source_target_pairs={{0,4},{8,5},{4,8},{12,9},{1,12},{9,13},{2,6},{10,7},{6,10},{14,11}... | collective-permute-start | bytes 147464 | tf_op jit(solution)/shard_map/ppermute | solution.py:385

commit v14 on v12

--- a/solution.py
+++ b/solution.py
@@ -64,7 +64,7 @@
         outs[-1][:, which * columns : (which + 1) * columns] = product.astype(BF16)
 
 
-def attended(query, packs, state, index):
+def attended(query, packs, index):
     columns = query.shape[1]
     start = index * HD
     head = slice(start, start + HD)
@@ -74,36 +74,33 @@
         lax.dot_general(asked, pack[:, head], (((1,), (1,)), ((), ())), preferred_element_type=F32)
         for pack in packs
     ]
-    tops = [jnp.max(score, axis=1, keepdims=True) for score in scores]
-    total, mixed = 0.0, 0.0
-    if state:
-        before, stats = state[0][index], state[1][index]
-        tops.append(stats[:, :1])
-    maxima = functools.reduce(jnp.maximum, tops)
-    if state:
-        correction = jnp.exp2(stats[:, :1] - maxima)
-        total = stats[:, 1:2] * correction
-        mixed = before * correction
+    maxima = functools.reduce(
+        jnp.maximum, [jnp.max(score, axis=1, keepdims=True) for score in scores]
+    )
+    mixed = 0.0
     for score, pack in zip(scores, packs):
-        expanded = jnp.exp2(score - maxima)
-        total = total + jnp.sum(expanded, axis=1, keepdims=True)
-        mixed = mixed + dot(expanded.astype(BF16), pack[:, values])
-    return mixed, maxima, total
+        value = pack[:, values]
+        widened = jnp.concatenate([value, jnp.ones_like(value)], axis=1)
+        mixed = mixed + dot(jnp.exp2(score - maxima).astype(BF16), widened)
+    return mixed, maxima
 
 
 def begin_kernel(query, *refs):
-    packs, (mixed_out, stats_out) = refs[:-2], refs[-2:]
+    packs, (mixed_out, maxima_out) = refs[:-2], refs[-2:]
     for index in range(query.shape[1] // HD):
-        mixed, maxima, total = attended(query, packs, (), index)
-        mixed_out[index] = mixed
-        stats_out[index] = jnp.concatenate([maxima, total], axis=1)
+        mixed_out[index], maxima_out[index] = attended(query, packs, index)
 
 
 def ended(query, packs, state):
     heads = []
     for index in range(query.shape[1] // HD):
-        mixed, maxima, total = attended(query, packs, state, index)
-        heads.append(mixed / total)
+        mixed, maxima = attended(query, packs, index)
+        if state:
+            before = state[1][index]
+            highest = jnp.maximum(maxima, before)
+            mixed = mixed * jnp.exp2(maxima - highest)
+            mixed = mixed + state[0][index] * jnp.exp2(before - highest)
+        heads.append(mixed[:, :HD] / mixed[:, HD:])
     return jnp.concatenate(heads, axis=1).astype(BF16)
 
 
@@ -127,8 +124,7 @@
 
 def end_map_kernel(query, *refs, count):
     composed, outs, board = refs[-2 - count], refs[-1 - count : -1], refs[-1]
-    packs, state = refs[: -4 - count], refs[-4 - count : -2 - count]
-    fill_board(board, dot(ended(query, packs, state), composed[...]))
+    fill_board(board, dot(ended(query, refs[: -2 - count], ()), composed[...]))
     for step, out in enumerate(outs):
         window_of(board, slot_of(count - step, count), out)
 
@@ -289,7 +285,7 @@
         ]
 
     def grouped(packs):
-        return packs if len(packs) < 3 else [jnp.concatenate(packs)]
+        return packs if len(packs) < 5 else [jnp.concatenate(packs)]
 
     def project(pieces, weights, scaled, first):
         return run_kernel(
@@ -300,7 +296,7 @@
         )
 
     def begin(query, packs):
-        shapes = [((heads, rows, HD), F32), ((heads, rows, 2), F32)]
+        shapes = [((heads, rows, 2 * HD), F32), ((heads, rows, 1), F32)]
         return run_kernel(begin_kernel, "begin", shapes, [query, *grouped(packs)])
 
     def staged(weights):
@@ -326,16 +322,7 @@
     query, pack = project(left, self_qkv, True, 0)
     right_pack = lax.ppermute(tied(right_pack, pack), both, there)
     beside = neighbours(pack)
-    near = [pack, *beside]
-    far = [q for p in near for q in across(p)]
-    state = begin(query, near)
-    right_pack = tied(right_pack, state)
-    right_near = [right_pack, *neighbours(right_pack)]
-    halves = tile_pieces(tied(half, beside))[1:]
-    (mixed,) = run_kernel(
-        end_kernel, "end", [((rows, columns), BF16)], [query, *grouped(far), *state]
-    )
-    halves = tied(halves, mixed)
+    halves = tile_pieces(half)[1:]
     others = [
         run_kernel(
             unpack_kernel,
@@ -349,7 +336,19 @@
     (composed,) = run_kernel(
         compose_kernel, "compose", [((columns, channels), BF16)], [cross_out, *map_weights]
     )
-    mixed, composed = lax.optimization_barrier((tile_pieces(mixed), composed))
+    near, others, composed, map_weights = lax.optimization_barrier(
+        ([pack, *beside], others, composed, map_weights)
+    )
+    far = [q for p in near for q in across(p)]
+    state = begin(query, near)
+    right_pack = tied(right_pack, state)
+    right_near = [right_pack, *neighbours(right_pack)]
+    (mixed,) = run_kernel(
+        end_kernel, "end", [((rows, columns), BF16)], [query, *grouped(far), *state]
+    )
+    mixed = tile_pieces(mixed)
+    right_near = tied(right_near, mixed)
+    right_far = [q for p in right_near for q in across(p)]
     updated, cross_query = run_kernel(
         functools.partial(update_kernel, count=tiles),
         "update",
@@ -362,15 +361,11 @@
             cross_qkv.reshape(3, tiles, share, columns),
         ],
     )
-    right_near = tied(right_near, updated)
-    right_far = [q for p in right_near for q in across(p)]
-    state = begin(cross_query, right_near)
-    right_far = tied(right_far, state)
     maps = run_kernel(
         functools.partial(end_map_kernel, count=tiles),
         "end_map",
         [(window, BF16)] * tiles,
-        [cross_query, *grouped(right_far), *state, composed],
+        [cross_query, *grouped([*right_near, *right_far]), composed],
         [pltpu.VMEM(board, F32)],
     )
     (carried,) = run_kernel(

time: 77.3 us -> 73.4 us (0.950)
  Pallas kernels: 20.3 us -> 16.4 us
  starting transfers between devices: 32.7 us -> 28.9 us
  waiting for transfers between devices: 24 us -> 27.7 us
    ppermute x2, waiting for transfers between devices: 4.75 us -> 14.4 us  [neighbours(): lax.ppermute(pack, 'blk', [(g + (i + s) % span, g + i) for g, i in ring])]
    ppermute x4, waiting for transfers between devices: 8.5 us -> 4.19 us  [from_tile(): lax.ppermute(value, 'tile', [((i + step) % tiles, i) for i in range(tiles)])]
    pallas_call x13 -> x12, Pallas kernels: 20.3 us -> 16.4 us  [run_kernel(): pl.pallas_call(kernel, out_shape=[jax.ShapeDtypeStruct(*s) for s in shape...]
    ppermute x1, starting transfers between devices: 5.61 us -> 3.08 us  [body(): features = lax.ppermute(features, both, back)]
    ppermute x5, starting transfers between devices: 2.36 us -> 4.3 us  [across(): lax.ppermute(pack, 'pair', [((i + s) % cores, i) for i in range(cores)])]
    ppermute x4, starting transfers between devices: 6.22 us -> 4.34 us  [from_tile(): lax.ppermute(value, 'tile', [((i + step) % tiles, i) for i in range(tiles)])]
    ppermute x1, starting transfers between devices: 5.5 us -> 4.16 us  [body(): right_pack = lax.ppermute(tied(right_pack, pack), both, there)]
    ppermute x1, waiting for transfers between devices: 1.21 us -> 0.01 us  [body(): right_pack = lax.ppermute(tied(right_pack, pack), both, there)]
  transfers between devices with their start and end apart: 17 -> 17, of which waited for: 9 -> 7; matrix products, arithmetic and copies ran while one was open for 0% -> 0% of each run, Pallas kernels for 17% -> 16%
where the time goes in v14:
time: 73.4 us; the launch traced here: 73.2 us
  starting transfers between devices  28.9 us (39%)
  waiting for transfers between devices  27.7 us (38%)
  Pallas kernels  16.4 us (22%)
    pallas_call x12, Pallas kernels, run_kernel(): pl.pallas_call(kernel, out_shape=[jax.ShapeDtypeStruct(*s) for s in shape...  16.4 us
    ppermute x2, waiting for transfers between devices, neighbours(): lax.ppermute(pack, 'blk', [(g + (i + s) % span, g + i) for g, i in ring])  14.4 us
    ppermute x2, waiting for transfers between devices, fetched(): return lax.ppermute(value, ('blk', 'tile', 'pair'), pairs)  7.51 us
    ppermute x1, starting transfers between devices, body(): above = lax.ppermute(features[-1:], both, down)  5.44 us
    ppermute x2, starting transfers between devices, fetched(): return lax.ppermute(value, ('blk', 'tile', 'pair'), pairs)  5.05 us
    ppermute x4, starting transfers between devices, from_tile(): lax.ppermute(value, 'tile', [((i + step) % tiles, i) for i in range(tiles)])  4.34 us
    ppermute x5, starting transfers between devices, across(): lax.ppermute(pack, 'pair', [((i + s) % cores, i) for i in range(cores)])  4.3 us
    ppermute x4, waiting for transfers between devices, from_tile(): lax.ppermute(value, 'tile', [((i + step) % tiles, i) for i in range(tiles)])  4.19 us
  transfers between devices with their start and end apart: 17, of which 7 were waited for; matrix products, arithmetic and copies ran while one was open for 0% of the time, Pallas kernels for 16%

profile of v14, /device:TPU:1, one launch (start us, length us, event | category | flops | bytes accessed | tf_op | source)
XLA Modules:
  0.0 73.2 jit_solution(11383702764547786638)
XLA Ops:
  0.0 2.0 %collective-permute-start.2 = (bf16[384,384]{1,0:T(8,128)(2,1)}, bf16[384,384]{1,0:T(8,128)(2,1)S(1)}, u32[]{:S(2)}, u32[]{:S(2)}) collective-permute-start(bf16[384,384]{1,0:T(8,128)(2,1)} %bitcast.8), channel_id=1, source_target_pairs={{2,0},{0,2},{3,1},{1,3},{6,4},{4,6},{7,5},{5,7},{10,8},{8,10},{11,... | collective-permute-start | bytes 884744 | tf_op jit(solution)/shard_map/ppermute | solution.py:269
  2.0 3.1 %collective-permute-start.1 = (bf16[384,384]{1,0:T(8,128)(2,1)}, bf16[384,384]{1,0:T(8,128)(2,1)S(1)}, u32[]{:S(2)}, u32[]{:S(2)}) collective-permute-start(bf16[384,384]{1,0:T(8,128)(2,1)} %bitcast.10), channel_id=1, source_target_pairs={{2,0},{0,2},{3,8},{1,10},{6,4},{4,6},{7,12},{5,14},{10,1},{8,3},{1... | collective-permute-start | bytes 884744 | tf_op jit(solution)/shard_map/ppermute | solution.py:263
  5.2 1.9 %collective-permute-start = (bf16[384,384]{1,0:T(8,128)(2,1)}, bf16[384,384]{1,0:T(8,128)(2,1)S(1)}, u32[]{:S(2)}, u32[]{:S(2)}) collective-permute-start(bf16[384,384]{1,0:T(8,128)(2,1)} %bitcast.11), channel_id=1, source_target_pairs={{0,0},{2,2},{1,8},{3,10},{4,4},{6,6},{5,12},{7,14},{8,1},{10,3},{9... | collective-permute-start | bytes 884744 | tf_op jit(solution)/shard_map/ppermute | solution.py:263
  7.1 2.6 %stage.1 = (bf16[256,768]{1,0:T(8,128)(2,1)S(1)}, bf16[384,256]{1,0:T(8,128)(2,1)S(1)}, bf16[256,768]{1,0:T(8,128)(2,1)S(1)}, bf16[384,384]{1,0:T(8,128)(2,1)S(1...) custom-call(bf16[256,768]{1,0:T(8,128)(2,1)} %refs_0_.1, ...), custom_call_target="tpu_custom_call" | custom-call | tf_op jit(solution)/shard_map/stage/pallas_call | solution.py:22
  9.7 1.3 %collective-permute-start.4 = (bf16[192,768]{1,0:T(8,128)(2,1)S(1)}, bf16[192,768]{1,0:T(8,128)(2,1)S(1)}, u32[]{:S(2)}, u32[]{:S(2)}) collective-permute-start(bf16[192,768]{1,0:T(8,128)(2,1)S(1)} %get-tuple-element.44), channel_id=1, source_target_pairs={{2,0},{0,2},{3,1},{1,3},{6,4},{4,6},{7,5},{5,7},{10,8},{8,10},{11,... | collective-permute-start | bytes 884744 | tf_op jit(solution)/shard_map/ppermute | solution.py:269
  11.8 4.8 %collective-permute-done.1.refs_1_.refs_5_ = bf16[384,384]{1,0:T(8,128)(2,1)S(1)} collective-permute-done((bf16[384,384]{1,0:T(8,128)(2,1)}, bf16[384,384]{1,0:T(8,128)(2,1)S(1)}, u32[]{:S(2)}, u32[]{:S(2)}) %collective-permute-start.1) | collective-permute-done | bytes 294944 | tf_op jit(solution)/shard_map/ppermute | solution.py:263
  16.6 2.7 %collective-permute-done.refs_0_.refs_4_ = bf16[384,384]{1,0:T(8,128)(2,1)S(1)} collective-permute-done((bf16[384,384]{1,0:T(8,128)(2,1)}, bf16[384,384]{1,0:T(8,128)(2,1)S(1)}, u32[]{:S(2)}, u32[]{:S(2)}) %collective-permute-start) | collective-permute-done | bytes 294944 | tf_op jit(solution)/shard_map/ppermute | solution.py:263
  19.3 1.1 %project.3 = (bf16[384,256]{1,0:T(8,128)(2,1)S(1)}, bf16[384,512]{1,0:T(8,128)(2,1)S(1)}) custom-call(bf16[384,384]{1,0:T(8,128)(2,1)S(1)} %collective-permute-done.refs_0_.refs_4_, bf16[384,384]{1,0:T(8,128)(2,1)S(1)} %collective-permute-done.1.refs_1_.refs_5_, bf16[3,2,384,256]{3,2,1,0:T(8,128)(2,1)S(1)} %bitcast.7), custom_call_target="tpu_custom_call" | custom-call | tf_op jit(solution)/shard_map/project/pallas_call | solution.py:22
  20.9 1.9 %collective-permute-start.5 = (bf16[192,768]{1,0:T(8,128)(2,1)S(1)}, bf16[192,768]{1,0:T(8,128)(2,1)S(1)}, u32[]{:S(2)}, u32[]{:S(2)}) collective-permute-start(bf16[192,768]{1,0:T(8,128)(2,1)S(1)} %collective-permute-done.4.refs_0_), channel_id=1, source_target_pairs={{1,0},{0,1},{3,2},{2,3},{5,4},{4,5},{7,6},{6,7},{9,8},{8,9},{11,10... | collective-permute-start | bytes 884744 | tf_op jit(solution)/shard_map/ppermute | solution.py:283
  22.9 4.2 %collective-permute-start.9 = (bf16[384,512]{1,0:T(8,128)(2,1)S(1)}, bf16[384,512]{1,0:T(8,128)(2,1)S(1)}, u32[]{:S(2)}, u32[]{:S(2)}) collective-permute-start(bf16[384,512]{1,0:T(8,128)(2,1)S(1)} %project.2), channel_id=1, source_target_pairs={{0,0},{1,8},{4,4},{5,12},{8,1},{9,9},{12,5},{13,13},{2,2},{3,10},{... | collective-permute-start | bytes 1179656 | tf_op jit(solution)/shard_map/ppermute | solution.py:323
  27.4 7.3 %collective-permute-done.3.refs_1_ = bf16[384,512]{1,0:T(8,128)(2,1)S(1)} collective-permute-done((bf16[384,512]{1,0:T(8,128)(2,1)S(1)}, bf16[384,512]{1,0:T(8,128)(2,1)S(1)}, u32[]{:S(2)}, u32[]{:S(2)}) %collective-permute-start.3) | collective-permute-done | bytes 393248 | tf_op jit(solution)/shard_map/ppermute | solution.py:277
  34.8 1.0 %collective-permute-start.6 = (bf16[384,512]{1,0:T(8,128)(2,1)S(1)}, bf16[384,512]{1,0:T(8,128)(2,1)S(1)}, u32[]{:S(2)}, u32[]{:S(2)}) collective-permute-start(bf16[384,512]{1,0:T(8,128)(2,1)S(1)} %get-tuple-element.49.refs_0_), channel_id=1, source_target_pairs={{1,0},{0,1},{3,2},{2,3},{5,4},{4,5},{7,6},{6,7},{9,8},{8,9},{11,10... | collective-permute-start | bytes 1179656 | tf_op jit(solution)/shard_map/ppermute | solution.py:283
  35.8 2.2 %begin.1 = (f32[4,384,128]{2,1,0:T(8,128)S(1)}, f32[4,384,1]{2,1,0:T(8,128)S(1)}) custom-call(bf16[384,256]{1,0:T(8,128)(2,1)S(1)} %get-tuple-element.42.query, bf16[384,512]{1,0:T(8,128)(2,1)S(1)} %get-tuple-element.49.refs_0_, bf16[384,512]{1,0:T(8,128)(2,1)S(1)} %collective-permute-done.3.refs_1_), custom_call_target="tpu_custom_call" | custom-call | tf_op jit(solution)/shard_map/begin/pallas_call | solution.py:22
  38.1 2.6 %end.1.refs_0_ = bf16[384,256]{1,0:T(8,128)(2,1)S(1)} custom-call(bf16[384,256]{1,0:T(8,128)(2,1)S(1)} %get-tuple-element.42.query, bf16[384,512]{1,0:T(8,128)(2,1)S(1)} %collective-permute-done.6.refs_0_, bf16[384,512]{1,0:T(8,128)(2,1)S(1)} %collective-permute-done.7.refs_1_, f32[4,384,128]{2,1,0:T(8,128)S(1)} %get-tuple-element.51.refs_2_, ...), custom_call_target="tpu_custom_call" | custom-call | tf_op jit(solution)/shard_map/end/pallas_call | solution.py:22
  41.2 7.0 %collective-permute-done.10.refs_1_ = bf16[384,512]{1,0:T(8,128)(2,1)S(1)} collective-permute-done((bf16[384,512]{1,0:T(8,128)(2,1)S(1)}, bf16[384,512]{1,0:T(8,128)(2,1)S(1)}, u32[]{:S(2)}, u32[]{:S(2)}) %collective-permute-start.10) | collective-permute-done | bytes 393248 | tf_op jit(solution)/shard_map/ppermute | solution.py:277
  48.3 1.4 %collective-permute-start.11 = (bf16[384,512]{1,0:T(8,128)(2,1)S(1)}, bf16[384,512]{1,0:T(8,128)(2,1)S(1)}, u32[]{:S(2)}, u32[]{:S(2)}) collective-permute-start(bf16[384,512]{1,0:T(8,128)(2,1)S(1)} %collective-permute-done.9.refs_0_), channel_id=1, source_target_pairs={{1,0},{0,1},{3,2},{2,3},{5,4},{4,5},{7,6},{6,7},{9,8},{8,9},{11,10... | collective-permute-start | bytes 1179656 | tf_op jit(solution)/shard_map/ppermute | solution.py:283
  49.6 1.5 %update.1 = (bf16[2,384,384]{2,1,0:T(8,128)(2,1)S(1)}, bf16[384,256]{1,0:T(8,128)(2,1)S(1)}) custom-call(bf16[384,256]{1,0:T(8,128)(2,1)S(1)} %end.1.refs_0_, bf16[384,256]{1,0:T(8,128)(2,1)S(1)} %collective-permute-done.8.refs_1_, bf16[256,768]{1,0:T(8,128)(2,1)S(1)} %get-tuple-element.53.refs_2_, bf16[256,768]{1,0:T(8,128)(2,1)S(1)} %get-tuple-element.54.refs_3_, ...), custom_call_target="tpu_custom_call" | custom-call | tf_op jit(solution)/shard_map/update/pallas_call | solution.py:22
  51.5 3.8 %end_map.1 = (bf16[3,96,256]{2,1,0:T(8,128)(2,1)S(1)}, bf16[3,96,256]{2,1,0:T(8,128)(2,1)S(1)}) custom-call(bf16[384,256]{1,0:T(8,128)(2,1)S(1)} %get-tuple-element.56.query, bf16[384,512]{1,0:T(8,128)(2,1)S(1)} %collective-permute-done.9.refs_0_, bf16[384,512]{1,0:T(8,128)(2,1)S(1)} %collective-permute-done.10.refs_1_, ...), custom_call_target="tpu_custom_call" | custom-call | tf_op jit(solution)/shard_map/end_map/pallas_call | solution.py:22
  56.3 4.2 %collective-permute-done.13.refs_2_ = bf16[3,96,256]{2,1,0:T(8,128)(2,1)S(1)} collective-permute-done((bf16[3,96,256]{2,1,0:T(8,128)(2,1)S(1)}, bf16[3,96,256]{2,1,0:T(8,128)(2,1)S(1)}, u32[]{:S(2)}, u32[]{:S(2)}) %collective-permute-start.13) | collective-permute-done | bytes 147488 | tf_op jit(solution)/shard_map/ppermute | solution.py:269
  60.5 3.1 %collective-permute-start.14 = (bf16[3,96,256]{2,1,0:T(8,128)(2,1)S(1)}, bf16[3,96,256]{2,1,0:T(8,128)(2,1)S(1)}, u32[]{:S(2)}, u32[]{:S(2)}) collective-permute-start(bf16[3,96,256]{2,1,0:T(8,128)(2,1)S(1)} %add.1), channel_id=1, source_target_pairs={{0,0},{8,1},{4,4},{12,5},{1,8},{9,9},{5,12},{13,13},{2,2},{10,3},{... | collective-permute-start | bytes 442376 | tf_op jit(solution)/shard_map/ppermute | solution.py:382
  63.7 1.9 %collective-permute-start.16 = (bf16[1,96,256]{2,1,0:T(8,128)(2,1)S(1)}, bf16[1,96,256]{2,1,0:T(8,128)(2,1)S(1)}, u32[]{:S(2)}, u32[]{:S(2)}) collective-permute-start(bf16[1,96,256]{2,1,0:T(8,128)(2,1)S(1)} %get-tuple-element.69), channel_id=1, source_target_pairs={{4,0},{12,1},{1,4},{9,5},{5,8},{13,9},{6,2},{14,3},{3,6},{11,7},{7... | collective-permute-start | bytes 147464 | tf_op jit(solution)/shard_map/ppermute | solution.py:381
  65.6 5.4 %collective-permute-start.15 = (bf16[1,96,256]{2,1,0:T(8,128)(2,1)S(1)}, bf16[1,96,256]{2,1,0:T(8,128)(2,1)S(1)}, u32[]{:S(2)}, u32[]{:S(2)}) collective-permute-start(bf16[1,96,256]{2,1,0:T(8,128)(2,1)S(1)} %get-tuple-element.70), channel_id=1, source_target_pairs={{0,4},{8,5},{4,8},{12,9},{1,12},{9,13},{2,6},{10,7},{6,10},{14,11}... | collective-permute-start | bytes 147464 | tf_op jit(solution)/shard_map/ppermute | solution.py:380
  71.0 1.1 %collective-permute-done.15.above = bf16[1,96,256]{2,1,0:T(8,128)(2,1)S(1)} collective-permute-done((bf16[1,96,256]{2,1,0:T(8,128)(2,1)S(1)}, bf16[1,96,256]{2,1,0:T(8,128)(2,1)S(1)}, u32[]{:S(2)}, u32[]{:S(2)}) %collective-permute-start.15) | collective-permute-done | bytes 49184 | tf_op jit(solution)/shard_map/ppermute | solution.py:380
  72.2 1.0 %join.1 = bf16[3,64,256]{2,1,0:T(8,128)(2,1)} custom-call(bf16[3,96,256]{2,1,0:T(8,128)(2,1)S(1)} %collective-permute-done.14.window, bf16[1,96,256]{2,1,0:T(8,128)(2,1)S(1)} %collective-permute-done.15.above, bf16[1,96,256]{2,1,0:T(8,128)(2,1)S(1)} %collective-permute-done.16.below, bf16[3,3,256,256]{3,2,1,0:T(8,128)(2,1)S(1)} %get-tuple-element.68.weight), custom_call_target="tpu_custom_call" | custom-call | tf_op jit(solution)/shard_map/join/pallas_call | solution.py:22
  (23 shorter events, 3.8 us)
Async XLA Ops:
  0.0 10.9 %collective-permute-start.2 = (bf16[384,384]{1,0:T(8,128)(2,1)}, bf16[384,384]{1,0:T(8,128)(2,1)S(1)}, u32[]{:S(2)}, u32[]{:S(2)}) collective-permute-start(bf16[384,384]{1,0:T(8,128)(2,1)} %bitcast.8), channel_id=1, source_target_pairs={{2,0},{0,2},{3,1},{1,3},{6,4},{4,6},{7,5},{5,7},{10,8},{8,10},{11,... | collective-permute-start | bytes 884744 | tf_op jit(solution)/shard_map/ppermute | solution.py:269
  2.0 14.6 %collective-permute-start.1 = (bf16[384,384]{1,0:T(8,128)(2,1)}, bf16[384,384]{1,0:T(8,128)(2,1)S(1)}, u32[]{:S(2)}, u32[]{:S(2)}) collective-permute-start(bf16[384,384]{1,0:T(8,128)(2,1)} %bitcast.10), channel_id=1, source_target_pairs={{2,0},{0,2},{3,8},{1,10},{6,4},{4,6},{7,12},{5,14},{10,1},{8,3},{1... | collective-permute-start | bytes 884744 | tf_op jit(solution)/shard_map/ppermute | solution.py:263
  5.2 14.1 %collective-permute-start = (bf16[384,384]{1,0:T(8,128)(2,1)}, bf16[384,384]{1,0:T(8,128)(2,1)S(1)}, u32[]{:S(2)}, u32[]{:S(2)}) collective-permute-start(bf16[384,384]{1,0:T(8,128)(2,1)} %bitcast.11), channel_id=1, source_target_pairs={{0,0},{2,2},{1,8},{3,10},{4,4},{6,6},{5,12},{7,14},{8,1},{10,3},{9... | collective-permute-start | bytes 884744 | tf_op jit(solution)/shard_map/ppermute | solution.py:263
  9.7 11.3 %collective-permute-start.4 = (bf16[192,768]{1,0:T(8,128)(2,1)S(1)}, bf16[192,768]{1,0:T(8,128)(2,1)S(1)}, u32[]{:S(2)}, u32[]{:S(2)}) collective-permute-start(bf16[192,768]{1,0:T(8,128)(2,1)S(1)} %get-tuple-element.44), channel_id=1, source_target_pairs={{2,0},{0,2},{3,1},{1,3},{6,4},{4,6},{7,5},{5,7},{10,8},{8,10},{11,... | collective-permute-start | bytes 884744 | tf_op jit(solution)/shard_map/ppermute | solution.py:269
  20.4 14.4 %collective-permute-start.3 = (bf16[384,512]{1,0:T(8,128)(2,1)S(1)}, bf16[384,512]{1,0:T(8,128)(2,1)S(1)}, u32[]{:S(2)}, u32[]{:S(2)}) collective-permute-start(bf16[384,512]{1,0:T(8,128)(2,1)S(1)} %get-tuple-element.49.refs_0_), channel_id=1, source_target_pairs={{4,0},{0,4},{12,8},{8,12},{5,1},{1,5},{13,9},{9,13},{6,2},{2,6},{1... | collective-permute-start | bytes 1179656 | tf_op jit(solution)/shard_map/ppermute | solution.py:277
  20.9 6.1 %collective-permute-start.5 = (bf16[192,768]{1,0:T(8,128)(2,1)S(1)}, bf16[192,768]{1,0:T(8,128)(2,1)S(1)}, u32[]{:S(2)}, u32[]{:S(2)}) collective-permute-start(bf16[192,768]{1,0:T(8,128)(2,1)S(1)} %collective-permute-done.4.refs_0_), channel_id=1, source_target_pairs={{1,0},{0,1},{3,2},{2,3},{5,4},{4,5},{7,6},{6,7},{9,8},{8,9},{11,10... | collective-permute-start | bytes 884744 | tf_op jit(solution)/shard_map/ppermute | solution.py:283
  22.9 15.2 %collective-permute-start.9 = (bf16[384,512]{1,0:T(8,128)(2,1)S(1)}, bf16[384,512]{1,0:T(8,128)(2,1)S(1)}, u32[]{:S(2)}, u32[]{:S(2)}) collective-permute-start(bf16[384,512]{1,0:T(8,128)(2,1)S(1)} %project.2), channel_id=1, source_target_pairs={{0,0},{1,8},{4,4},{5,12},{8,1},{9,9},{12,5},{13,13},{2,2},{3,10},{... | collective-permute-start | bytes 1179656 | tf_op jit(solution)/shard_map/ppermute | solution.py:323
  34.8 3.4 %collective-permute-start.6 = (bf16[384,512]{1,0:T(8,128)(2,1)S(1)}, bf16[384,512]{1,0:T(8,128)(2,1)S(1)}, u32[]{:S(2)}, u32[]{:S(2)}) collective-permute-start(bf16[384,512]{1,0:T(8,128)(2,1)S(1)} %get-tuple-element.49.refs_0_), channel_id=1, source_target_pairs={{1,0},{0,1},{3,2},{2,3},{5,4},{4,5},{7,6},{6,7},{9,8},{8,9},{11,10... | collective-permute-start | bytes 1179656 | tf_op jit(solution)/shard_map/ppermute | solution.py:283
  35.8 2.3 %collective-permute-start.7 = (bf16[384,512]{1,0:T(8,128)(2,1)S(1)}, bf16[384,512]{1,0:T(8,128)(2,1)S(1)}, u32[]{:S(2)}, u32[]{:S(2)}) collective-permute-start(bf16[384,512]{1,0:T(8,128)(2,1)S(1)} %collective-permute-done.3.refs_1_), channel_id=1, source_target_pairs={{1,0},{0,1},{3,2},{2,3},{5,4},{4,5},{7,6},{6,7},{9,8},{8,9},{11,10... | collective-permute-start | bytes 1179656 | tf_op jit(solution)/shard_map/ppermute | solution.py:283
  38.0 10.2 %collective-permute-start.10 = (bf16[384,512]{1,0:T(8,128)(2,1)S(1)}, bf16[384,512]{1,0:T(8,128)(2,1)S(1)}, u32[]{:S(2)}, u32[]{:S(2)}) collective-permute-start(bf16[384,512]{1,0:T(8,128)(2,1)S(1)} %collective-permute-done.9.refs_0_), channel_id=1, source_target_pairs={{4,0},{0,4},{12,8},{8,12},{5,1},{1,5},{13,9},{9,13},{6,2},{2,6},{1... | collective-permute-start | bytes 1179656 | tf_op jit(solution)/shard_map/ppermute | solution.py:277
  40.7 7.5 %collective-permute-start.8 = (bf16[384,256]{1,0:T(8,128)(2,1)S(1)}, bf16[384,256]{1,0:T(8,128)(2,1)S(1)}, u32[]{:S(2)}, u32[]{:S(2)}) collective-permute-start(bf16[384,256]{1,0:T(8,128)(2,1)S(1)} %end.1.refs_0_), channel_id=1, source_target_pairs={{2,0},{0,2},{3,1},{1,3},{6,4},{4,6},{7,5},{5,7},{10,8},{8,10},{11,... | collective-permute-start | bytes 589832 | tf_op jit(solution)/shard_map/ppermute | solution.py:269
  48.3 2.8 %collective-permute-start.11 = (bf16[384,512]{1,0:T(8,128)(2,1)S(1)}, bf16[384,512]{1,0:T(8,128)(2,1)S(1)}, u32[]{:S(2)}, u32[]{:S(2)}) collective-permute-start(bf16[384,512]{1,0:T(8,128)(2,1)S(1)} %collective-permute-done.9.refs_0_), channel_id=1, source_target_pairs={{1,0},{0,1},{3,2},{2,3},{5,4},{4,5},{7,6},{6,7},{9,8},{8,9},{11,10... | collective-permute-start | bytes 1179656 | tf_op jit(solution)/shard_map/ppermute | solution.py:283
  49.6 1.9 %collective-permute-start.12 = (bf16[384,512]{1,0:T(8,128)(2,1)S(1)}, bf16[384,512]{1,0:T(8,128)(2,1)S(1)}, u32[]{:S(2)}, u32[]{:S(2)}) collective-permute-start(bf16[384,512]{1,0:T(8,128)(2,1)S(1)} %collective-permute-done.10.refs_1_), channel_id=1, source_target_pairs={{1,0},{0,1},{3,2},{2,3},{5,4},{4,5},{7,6},{6,7},{9,8},{8,9},{11,10... | collective-permute-start | bytes 1179656 | tf_op jit(solution)/shard_map/ppermute | solution.py:283
  55.4 5.1 %collective-permute-start.13 = (bf16[3,96,256]{2,1,0:T(8,128)(2,1)S(1)}, bf16[3,96,256]{2,1,0:T(8,128)(2,1)S(1)}, u32[]{:S(2)}, u32[]{:S(2)}) collective-permute-start(bf16[3,96,256]{2,1,0:T(8,128)(2,1)S(1)} %get-tuple-element.64), channel_id=1, source_target_pairs={{2,0},{0,2},{3,1},{1,3},{6,4},{4,6},{7,5},{5,7},{10,8},{8,10},{11,... | collective-permute-start | bytes 442376 | tf_op jit(solution)/shard_map/ppermute | solution.py:269
  60.5 11.6 %collective-permute-start.14 = (bf16[3,96,256]{2,1,0:T(8,128)(2,1)S(1)}, bf16[3,96,256]{2,1,0:T(8,128)(2,1)S(1)}, u32[]{:S(2)}, u32[]{:S(2)}) collective-permute-start(bf16[3,96,256]{2,1,0:T(8,128)(2,1)S(1)} %add.1), channel_id=1, source_target_pairs={{0,0},{8,1},{4,4},{12,5},{1,8},{9,9},{5,12},{13,13},{2,2},{10,3},{... | collective-permute-start | bytes 442376 | tf_op jit(solution)/shard_map/ppermute | solution.py:382
  63.7 7.4 %collective-permute-start.16 = (bf16[1,96,256]{2,1,0:T(8,128)(2,1)S(1)}, bf16[1,96,256]{2,1,0:T(8,128)(2,1)S(1)}, u32[]{:S(2)}, u32[]{:S(2)}) collective-permute-start(bf16[1,96,256]{2,1,0:T(8,128)(2,1)S(1)} %get-tuple-element.69), channel_id=1, source_target_pairs={{4,0},{12,1},{1,4},{9,5},{5,8},{13,9},{6,2},{14,3},{3,6},{11,7},{7... | collective-permute-start | bytes 147464 | tf_op jit(solution)/shard_map/ppermute | solution.py:381
  65.6 6.6 %collective-permute-start.15 = (bf16[1,96,256]{2,1,0:T(8,128)(2,1)S(1)}, bf16[1,96,256]{2,1,0:T(8,128)(2,1)S(1)}, u32[]{:S(2)}, u32[]{:S(2)}) collective-permute-start(bf16[1,96,256]{2,1,0:T(8,128)(2,1)S(1)} %get-tuple-element.70), channel_id=1, source_target_pairs={{0,4},{8,5},{4,8},{12,9},{1,12},{9,13},{2,6},{10,7},{6,10},{14,11}... | collective-permute-start | bytes 147464 | tf_op jit(solution)/shard_map/ppermute | solution.py:380

commit v15 on v14

--- a/solution.py
+++ b/solution.py
@@ -123,20 +123,18 @@
 
 
 def end_map_kernel(query, *refs, count):
-    composed, outs, board = refs[-2 - count], refs[-1 - count : -1], refs[-1]
-    fill_board(board, dot(ended(query, refs[: -2 - count], ()), composed[...]))
+    carried, composed, outs, board = refs[-3 - count], refs[-2 - count], refs[-1 - count : -1], refs[-1]
+    fill_board(board, dot(ended(query, refs[: -3 - count], ()), composed[...]))
     for step, out in enumerate(outs):
-        window_of(board, slot_of(count - step, count), out)
+        start = pl.multiple_of(slot_of(count - step, count) * (out.shape[1] - 2 * EDGE), EDGE)
+        part = board[:, pl.ds(start, out.shape[1]), :]
+        out[...] = (part if step else part + carried[...]).astype(BF16)
 
 
 def carry_kernel(updated, *refs):
     pieces, out, board = refs[:-2], refs[-2], refs[-1]
     fill_board(board, sum(dot(updated[i], piece[...]) for i, piece in enumerate(pieces)))
     window_of(board, lax.axis_index("tile"), out)
-
-
-def add_kernel(*refs):
-    refs[-1][...] = sum(ref[...].astype(F32) for ref in refs[:-1]).astype(BF16)
 
 
 def stage_kernel(*refs, cores):
@@ -214,10 +212,17 @@
     query[...] = (product * QUERY_SCALE).astype(BF16)
 
 
-def conv_kernel(window, above, below, weight, out):
+def conv_kernel(*refs):
+    weight, out = refs[-2:]
     width = out.shape[1]
     band_rows, channels = out.shape[0], out.shape[2]
-    grid = jnp.concatenate([above[...], window[...], below[...]], axis=0).astype(F32)
+    count = (len(refs) - 2) // 3
+
+    def summed(parts):
+        return sum(part[...].astype(F32) for part in parts).astype(BF16)
+
+    above, window, below = (summed(refs[i * count : (i + 1) * count]) for i in range(3))
+    grid = jnp.concatenate([above, window, below], axis=0).astype(F32)
     active = jnp.maximum(grid, 0.0)
     total = grid[1 : 1 + band_rows, EDGE : EDGE + width, :].reshape(band_rows * width, channels)
     for column in range(3):
@@ -255,11 +260,11 @@
     down = [(worker(b, p), home(b + 1, p)) for b, p in places if b + 1 < bands]
     up = [(worker(b, p), home(b - 1, p)) for b, p in places if b > 0]
 
-    def fetched(value, step):
+    def fetched(value, step, moves=there):
         def flat(position, tile):
             return (position // cores * tiles + tile) * cores + position % cores
 
-        pairs = [(flat(s, (i + step) % tiles), flat(d, i)) for s, d in there for i in range(tiles)]
+        pairs = [(flat(s, (i + step) % tiles), flat(d, i)) for s, d in moves for i in range(tiles)]
         return lax.ppermute(value, ("blk", "tile", "pair"), pairs)
 
     def tied(values, *others):
@@ -361,30 +366,28 @@
             cross_qkv.reshape(3, tiles, share, columns),
         ],
     )
+    (carried,) = run_kernel(
+        carry_kernel,
+        "carry",
+        [(window, F32)],
+        [updated, *map_weights],
+        [pltpu.VMEM(board, F32)],
+    )
     maps = run_kernel(
         functools.partial(end_map_kernel, count=tiles),
         "end_map",
         [(window, BF16)] * tiles,
-        [cross_query, *grouped([*right_near, *right_far]), composed],
+        [cross_query, *grouped([*right_near, *right_far]), carried, composed],
         [pltpu.VMEM(board, F32)],
     )
-    (carried,) = run_kernel(
-        carry_kernel,
-        "carry",
-        [(window, F32)],
-        [tied(updated, maps), *map_weights],
-        [pltpu.VMEM(board, F32)],
-    )
-    received = [from_tile(part, s) for s, part in enumerate(maps) if s > 0]
-    (features,) = run_kernel(add_kernel, "add", [(window, BF16)], [carried, maps[0], *received])
-    above = lax.ppermute(features[-1:], both, down)
-    below = lax.ppermute(features[:1], both, up)
-    features = lax.ppermute(features, both, back)
+    above = [fetched(part[-1:], s, down) for s, part in enumerate(maps)]
+    below = [fetched(part[:1], s, up) for s, part in enumerate(maps)]
+    middle = [fetched(part, s, back) for s, part in enumerate(maps)]
     (joined,) = run_kernel(
         conv_kernel,
         "join",
         [((band_rows, width, channels), BF16)],
-        [features, above, below, taps],
+        [*above, *middle, *below, taps],
     )
     return joined[None]
 

time: 73.4 us -> 77.6 us (1.057)
  starting transfers between devices: 28.9 us -> 37.5 us
  waiting for transfers between devices: 27.7 us -> 23.1 us
    ppermute x2 -> x8, starting transfers between devices: 5.05 us -> 24.6 us  [fetched(): return lax.ppermute(value, ('blk', 'tile', 'pair'), pairs)]
    ppermute x3 -> x0, starting transfers between devices: 10.4 us -> none  [the longest x1 5.44 us: body(): above = lax.ppermute(features[-1:], both, down)]
    ppermute x4 -> x3, waiting for transfers between devices: 4.19 us -> 0.01 us  [from_tile(): lax.ppermute(value, 'tile', [((i + step) % tiles, i) for i in range(tiles)])]
    ppermute x3 -> x0, waiting for transfers between devices: 1.15 us -> none  [the longest x1 1.15 us: body(): above = lax.ppermute(features[-1:], both, down)]
    ppermute x2 -> x8, waiting for transfers between devices: 7.51 us -> 8.66 us  [fetched(): return lax.ppermute(value, ('blk', 'tile', 'pair'), pairs)]
    ppermute x4 -> x3, starting transfers between devices: 4.34 us -> 3.81 us  [from_tile(): lax.ppermute(value, 'tile', [((i + step) % tiles, i) for i in range(tiles)])]
    pallas_call x12 -> x11, Pallas kernels: 16.4 us -> 16.4 us  [run_kernel(): pl.pallas_call(kernel, out_shape=[jax.ShapeDtypeStruct(*s) for s in shape...]
  transfers between devices with their start and end apart: 17 -> 19, of which waited for: 7 -> 5; matrix products, arithmetic and copies ran while one was open for 0% -> 0% of each run, Pallas kernels for 16% -> 15%
where the time goes in v15:
time: 77.6 us; the launch traced here: 77.2 us
  starting transfers between devices  37.5 us (48%)
  waiting for transfers between devices  23.1 us (30%)
  Pallas kernels  16.4 us (21%)
    ppermute x8, starting transfers between devices, fetched(): return lax.ppermute(value, ('blk', 'tile', 'pair'), pairs)  24.6 us
    pallas_call x11, Pallas kernels, run_kernel(): pl.pallas_call(kernel, out_shape=[jax.ShapeDtypeStruct(*s) for s in shape...  16.4 us
    ppermute x2, waiting for transfers between devices, neighbours(): lax.ppermute(pack, 'blk', [(g + (i + s) % span, g + i) for g, i in ring])  14.4 us
    ppermute x8, waiting for transfers between devices, fetched(): return lax.ppermute(value, ('blk', 'tile', 'pair'), pairs)  8.66 us
    ppermute x5, starting transfers between devices, across(): lax.ppermute(pack, 'pair', [((i + s) % cores, i) for i in range(cores)])  4.3 us
    ppermute x1, starting transfers between devices, body(): right_pack = lax.ppermute(tied(right_pack, pack), both, there)  4.16 us
    ppermute x3, starting transfers between devices, from_tile(): lax.ppermute(value, 'tile', [((i + step) % tiles, i) for i in range(tiles)])  3.81 us
  transfers between devices with their start and end apart: 19, of which 5 were waited for; matrix products, arithmetic and copies ran while one was open for 0% of the time, Pallas kernels for 15%

profile of v15, /device:TPU:1, one launch (start us, length us, event | category | flops | bytes accessed | tf_op | source)
XLA Modules:
  0.0 77.2 jit_solution(11728975409800240528)
XLA Ops:
  0.0 2.0 %collective-permute-start.2 = (bf16[384,384]{1,0:T(8,128)(2,1)}, bf16[384,384]{1,0:T(8,128)(2,1)S(1)}, u32[]{:S(2)}, u32[]{:S(2)}) collective-permute-start(bf16[384,384]{1,0:T(8,128)(2,1)} %bitcast.8), channel_id=1, source_target_pairs={{2,0},{0,2},{3,1},{1,3},{6,4},{4,6},{7,5},{5,7},{10,8},{8,10},{11,... | collective-permute-start | bytes 884744 | tf_op jit(solution)/shard_map/ppermute | solution.py:274
  2.0 3.1 %collective-permute-start.1 = (bf16[384,384]{1,0:T(8,128)(2,1)}, bf16[384,384]{1,0:T(8,128)(2,1)S(1)}, u32[]{:S(2)}, u32[]{:S(2)}) collective-permute-start(bf16[384,384]{1,0:T(8,128)(2,1)} %bitcast.10), channel_id=1, source_target_pairs={{2,0},{0,2},{3,8},{1,10},{6,4},{4,6},{7,12},{5,14},{10,1},{8,3},{1... | collective-permute-start | bytes 884744 | tf_op jit(solution)/shard_map/ppermute | solution.py:268
  5.2 1.9 %collective-permute-start = (bf16[384,384]{1,0:T(8,128)(2,1)}, bf16[384,384]{1,0:T(8,128)(2,1)S(1)}, u32[]{:S(2)}, u32[]{:S(2)}) collective-permute-start(bf16[384,384]{1,0:T(8,128)(2,1)} %bitcast.11), channel_id=1, source_target_pairs={{0,0},{2,2},{1,8},{3,10},{4,4},{6,6},{5,12},{7,14},{8,1},{10,3},{9... | collective-permute-start | bytes 884744 | tf_op jit(solution)/shard_map/ppermute | solution.py:268
  7.1 2.6 %stage.1 = (bf16[256,768]{1,0:T(8,128)(2,1)S(1)}, bf16[384,256]{1,0:T(8,128)(2,1)S(1)}, bf16[256,768]{1,0:T(8,128)(2,1)S(1)}, bf16[384,384]{1,0:T(8,128)(2,1)S(1...) custom-call(bf16[256,768]{1,0:T(8,128)(2,1)} %refs_0_.1, ...), custom_call_target="tpu_custom_call" | custom-call | tf_op jit(solution)/shard_map/stage/pallas_call | solution.py:22
  9.7 1.3 %collective-permute-start.4 = (bf16[192,768]{1,0:T(8,128)(2,1)S(1)}, bf16[192,768]{1,0:T(8,128)(2,1)S(1)}, u32[]{:S(2)}, u32[]{:S(2)}) collective-permute-start(bf16[192,768]{1,0:T(8,128)(2,1)S(1)} %get-tuple-element.43), channel_id=1, source_target_pairs={{2,0},{0,2},{3,1},{1,3},{6,4},{4,6},{7,5},{5,7},{10,8},{8,10},{11,... | collective-permute-start | bytes 884744 | tf_op jit(solution)/shard_map/ppermute | solution.py:274
  11.8 4.8 %collective-permute-done.1.refs_1_.refs_5_ = bf16[384,384]{1,0:T(8,128)(2,1)S(1)} collective-permute-done((bf16[384,384]{1,0:T(8,128)(2,1)}, bf16[384,384]{1,0:T(8,128)(2,1)S(1)}, u32[]{:S(2)}, u32[]{:S(2)}) %collective-permute-start.1) | collective-permute-done | bytes 294944 | tf_op jit(solution)/shard_map/ppermute | solution.py:268
  16.6 2.7 %collective-permute-done.refs_0_.refs_4_ = bf16[384,384]{1,0:T(8,128)(2,1)S(1)} collective-permute-done((bf16[384,384]{1,0:T(8,128)(2,1)}, bf16[384,384]{1,0:T(8,128)(2,1)S(1)}, u32[]{:S(2)}, u32[]{:S(2)}) %collective-permute-start) | collective-permute-done | bytes 294944 | tf_op jit(solution)/shard_map/ppermute | solution.py:268
  20.9 1.9 %collective-permute-start.5 = (bf16[192,768]{1,0:T(8,128)(2,1)S(1)}, bf16[192,768]{1,0:T(8,128)(2,1)S(1)}, u32[]{:S(2)}, u32[]{:S(2)}) collective-permute-start(bf16[192,768]{1,0:T(8,128)(2,1)S(1)} %collective-permute-done.4.refs_0_), channel_id=1, source_target_pairs={{1,0},{0,1},{3,2},{2,3},{5,4},{4,5},{7,6},{6,7},{9,8},{8,9},{11,10... | collective-permute-start | bytes 884744 | tf_op jit(solution)/shard_map/ppermute | solution.py:288
  22.9 4.2 %collective-permute-start.9 = (bf16[384,512]{1,0:T(8,128)(2,1)S(1)}, bf16[384,512]{1,0:T(8,128)(2,1)S(1)}, u32[]{:S(2)}, u32[]{:S(2)}) collective-permute-start(bf16[384,512]{1,0:T(8,128)(2,1)S(1)} %project.2), channel_id=1, source_target_pairs={{0,0},{1,8},{4,4},{5,12},{8,1},{9,9},{12,5},{13,13},{2,2},{3,10},{... | collective-permute-start | bytes 1179656 | tf_op jit(solution)/shard_map/ppermute | solution.py:328
  27.4 7.3 %collective-permute-done.3.refs_1_ = bf16[384,512]{1,0:T(8,128)(2,1)S(1)} collective-permute-done((bf16[384,512]{1,0:T(8,128)(2,1)S(1)}, bf16[384,512]{1,0:T(8,128)(2,1)S(1)}, u32[]{:S(2)}, u32[]{:S(2)}) %collective-permute-start.3) | collective-permute-done | bytes 393248 | tf_op jit(solution)/shard_map/ppermute | solution.py:282
  35.8 2.2 %begin.1 = (f32[4,384,128]{2,1,0:T(8,128)S(1)}, f32[4,384,1]{2,1,0:T(8,128)S(1)}) custom-call(bf16[384,256]{1,0:T(8,128)(2,1)S(1)} %get-tuple-element.41.query, bf16[384,512]{1,0:T(8,128)(2,1)S(1)} %get-tuple-element.48.refs_0_, bf16[384,512]{1,0:T(8,128)(2,1)S(1)} %collective-permute-done.3.refs_1_), custom_call_target="tpu_custom_call" | custom-call | tf_op jit(solution)/shard_map/begin/pallas_call | solution.py:22
  38.1 2.6 %end.1.refs_0_ = bf16[384,256]{1,0:T(8,128)(2,1)S(1)} custom-call(bf16[384,256]{1,0:T(8,128)(2,1)S(1)} %get-tuple-element.41.query, bf16[384,512]{1,0:T(8,128)(2,1)S(1)} %collective-permute-done.6.refs_0_, bf16[384,512]{1,0:T(8,128)(2,1)S(1)} %collective-permute-done.7.refs_1_, f32[4,384,128]{2,1,0:T(8,128)S(1)} %get-tuple-element.50.refs_2_, ...), custom_call_target="tpu_custom_call" | custom-call | tf_op jit(solution)/shard_map/end/pallas_call | solution.py:22
  41.2 7.0 %collective-permute-done.10.refs_1_ = bf16[384,512]{1,0:T(8,128)(2,1)S(1)} collective-permute-done((bf16[384,512]{1,0:T(8,128)(2,1)S(1)}, bf16[384,512]{1,0:T(8,128)(2,1)S(1)}, u32[]{:S(2)}, u32[]{:S(2)}) %collective-permute-start.10) | collective-permute-done | bytes 393248 | tf_op jit(solution)/shard_map/ppermute | solution.py:282
  48.3 1.4 %collective-permute-start.11 = (bf16[384,512]{1,0:T(8,128)(2,1)S(1)}, bf16[384,512]{1,0:T(8,128)(2,1)S(1)}, u32[]{:S(2)}, u32[]{:S(2)}) collective-permute-start(bf16[384,512]{1,0:T(8,128)(2,1)S(1)} %collective-permute-done.9.refs_0_), channel_id=1, source_target_pairs={{1,0},{0,1},{3,2},{2,3},{5,4},{4,5},{7,6},{6,7},{9,8},{8,9},{11,10... | collective-permute-start | bytes 1179656 | tf_op jit(solution)/shard_map/ppermute | solution.py:288
  49.6 1.5 %update.1 = (bf16[2,384,384]{2,1,0:T(8,128)(2,1)S(1)}, bf16[384,256]{1,0:T(8,128)(2,1)S(1)}) custom-call(bf16[384,256]{1,0:T(8,128)(2,1)S(1)} %end.1.refs_0_, bf16[384,256]{1,0:T(8,128)(2,1)S(1)} %collective-permute-done.8.refs_1_, bf16[256,768]{1,0:T(8,128)(2,1)S(1)} %get-tuple-element.52.refs_2_, bf16[256,768]{1,0:T(8,128)(2,1)S(1)} %get-tuple-element.53.refs_3_, ...), custom_call_target="tpu_custom_call" | custom-call | tf_op jit(solution)/shard_map/update/pallas_call | solution.py:22
  51.5 3.8 %end_map.1 = (bf16[3,96,256]{2,1,0:T(8,128)(2,1)S(1)}, bf16[3,96,256]{2,1,0:T(8,128)(2,1)S(1)}) custom-call(bf16[384,256]{1,0:T(8,128)(2,1)S(1)} %get-tuple-element.54.query, bf16[384,512]{1,0:T(8,128)(2,1)S(1)} %collective-permute-done.9.refs_0_, bf16[384,512]{1,0:T(8,128)(2,1)S(1)} %collective-permute-done.10.refs_1_, ...), custom_call_target="tpu_custom_call" | custom-call | tf_op jit(solution)/shard_map/end_map/pallas_call | solution.py:22
  55.4 2.3 %collective-permute-start.15 = (bf16[3,96,256]{2,1,0:T(8,128)(2,1)S(1)}, bf16[3,96,256]{2,1,0:T(8,128)(2,1)S(1)}, u32[]{:S(2)}, u32[]{:S(2)}) collective-permute-start(bf16[3,96,256]{2,1,0:T(8,128)(2,1)S(1)} %get-tuple-element.64), channel_id=1, source_target_pairs={{0,0},{2,2},{8,1},{10,3},{4,4},{6,6},{12,5},{14,7},{1,8},{3,10},{9... | collective-permute-start | bytes 442376 | tf_op jit(solution)/shard_map/ppermute | solution.py:268
  57.7 1.9 %collective-permute-start.17 = (bf16[1,96,256]{2,1,0:T(8,128)(2,1)S(1)}, bf16[1,96,256]{2,1,0:T(8,128)(2,1)S(1)}, u32[]{:S(2)}, u32[]{:S(2)}) collective-permute-start(bf16[1,96,256]{2,1,0:T(8,128)(2,1)S(1)} %get-tuple-element.69), channel_id=1, source_target_pairs={{4,0},{6,2},{12,1},{14,3},{1,4},{3,6},{9,5},{11,7},{5,8},{7,10},{1... | collective-permute-start | bytes 147464 | tf_op jit(solution)/shard_map/ppermute | solution.py:268
  59.7 1.8 %collective-permute-start.16 = (bf16[3,96,256]{2,1,0:T(8,128)(2,1)S(1)}, bf16[3,96,256]{2,1,0:T(8,128)(2,1)S(1)}, u32[]{:S(2)}, u32[]{:S(2)}) collective-permute-start(bf16[3,96,256]{2,1,0:T(8,128)(2,1)S(1)} %get-tuple-element.65), channel_id=1, source_target_pairs={{2,0},{0,2},{10,1},{8,3},{6,4},{4,6},{14,5},{12,7},{3,8},{1,10},{1... | collective-permute-start | bytes 442376 | tf_op jit(solution)/shard_map/ppermute | solution.py:268
  61.5 5.2 %collective-permute-start.13 = (bf16[1,96,256]{2,1,0:T(8,128)(2,1)S(1)}, bf16[1,96,256]{2,1,0:T(8,128)(2,1)S(1)}, u32[]{:S(2)}, u32[]{:S(2)}) collective-permute-start(bf16[1,96,256]{2,1,0:T(8,128)(2,1)S(1)} %get-tuple-element.70), channel_id=1, source_target_pairs={{0,4},{2,6},{8,5},{10,7},{4,8},{6,10},{12,9},{14,11},{1,12},{3,14}... | collective-permute-start | bytes 147464 | tf_op jit(solution)/shard_map/ppermute | solution.py:268
  66.7 1.9 %collective-permute-start.18 = (bf16[1,96,256]{2,1,0:T(8,128)(2,1)S(1)}, bf16[1,96,256]{2,1,0:T(8,128)(2,1)S(1)}, u32[]{:S(2)}, u32[]{:S(2)}) collective-permute-start(bf16[1,96,256]{2,1,0:T(8,128)(2,1)S(1)} %get-tuple-element.67), channel_id=1, source_target_pairs={{6,0},{4,2},{14,1},{12,3},{3,4},{1,6},{11,5},{9,7},{7,8},{5,10},{1... | collective-permute-start | bytes 147464 | tf_op jit(solution)/shard_map/ppermute | solution.py:268
  68.6 6.3 %collective-permute-start.14 = (bf16[1,96,256]{2,1,0:T(8,128)(2,1)S(1)}, bf16[1,96,256]{2,1,0:T(8,128)(2,1)S(1)}, u32[]{:S(2)}, u32[]{:S(2)}) collective-permute-start(bf16[1,96,256]{2,1,0:T(8,128)(2,1)S(1)} %get-tuple-element.68), channel_id=1, source_target_pairs={{2,4},{0,6},{10,5},{8,7},{6,8},{4,10},{14,9},{12,11},{3,12},{1,14}... | collective-permute-start | bytes 147464 | tf_op jit(solution)/shard_map/ppermute | solution.py:268
  75.0 1.1 %collective-permute-done.14.refs_1_ = bf16[1,96,256]{2,1,0:T(8,128)(2,1)S(1)} collective-permute-done((bf16[1,96,256]{2,1,0:T(8,128)(2,1)S(1)}, bf16[1,96,256]{2,1,0:T(8,128)(2,1)S(1)}, u32[]{:S(2)}, u32[]{:S(2)}) %collective-permute-start.14) | collective-permute-done | bytes 49184 | tf_op jit(solution)/shard_map/ppermute | solution.py:268
  76.1 1.1 %join.1 = bf16[3,64,256]{2,1,0:T(8,128)(2,1)} custom-call(bf16[1,96,256]{2,1,0:T(8,128)(2,1)S(1)} %collective-permute-done.13.refs_0_, bf16[1,96,256]{2,1,0:T(8,128)(2,1)S(1)} %collective-permute-done.14.refs_1_, bf16[3,96,256]{2,1,0:T(8,128)(2,1)S(1)} %collective-permute-done.15.refs_2_, bf16[3,96,256]{2,1,0:T(8,128)(2,1)S(1)} %collective-permute-done.16.refs_3_, ...), custom_call_target="tpu_custom_call" | custom-call | tf_op jit(solution)/shard_map/join/pallas_call | solution.py:22
  (27 shorter events, 4.9 us)
Async XLA Ops:
  0.0 10.9 %collective-permute-start.2 = (bf16[384,384]{1,0:T(8,128)(2,1)}, bf16[384,384]{1,0:T(8,128)(2,1)S(1)}, u32[]{:S(2)}, u32[]{:S(2)}) collective-permute-start(bf16[384,384]{1,0:T(8,128)(2,1)} %bitcast.8), channel_id=1, source_target_pairs={{2,0},{0,2},{3,1},{1,3},{6,4},{4,6},{7,5},{5,7},{10,8},{8,10},{11,... | collective-permute-start | bytes 884744 | tf_op jit(solution)/shard_map/ppermute | solution.py:274
  2.0 14.6 %collective-permute-start.1 = (bf16[384,384]{1,0:T(8,128)(2,1)}, bf16[384,384]{1,0:T(8,128)(2,1)S(1)}, u32[]{:S(2)}, u32[]{:S(2)}) collective-permute-start(bf16[384,384]{1,0:T(8,128)(2,1)} %bitcast.10), channel_id=1, source_target_pairs={{2,0},{0,2},{3,8},{1,10},{6,4},{4,6},{7,12},{5,14},{10,1},{8,3},{1... | collective-permute-start | bytes 884744 | tf_op jit(solution)/shard_map/ppermute | solution.py:268
  5.2 14.1 %collective-permute-start = (bf16[384,384]{1,0:T(8,128)(2,1)}, bf16[384,384]{1,0:T(8,128)(2,1)S(1)}, u32[]{:S(2)}, u32[]{:S(2)}) collective-permute-start(bf16[384,384]{1,0:T(8,128)(2,1)} %bitcast.11), channel_id=1, source_target_pairs={{0,0},{2,2},{1,8},{3,10},{4,4},{6,6},{5,12},{7,14},{8,1},{10,3},{9... | collective-permute-start | bytes 884744 | tf_op jit(solution)/shard_map/ppermute | solution.py:268
  9.7 11.3 %collective-permute-start.4 = (bf16[192,768]{1,0:T(8,128)(2,1)S(1)}, bf16[192,768]{1,0:T(8,128)(2,1)S(1)}, u32[]{:S(2)}, u32[]{:S(2)}) collective-permute-start(bf16[192,768]{1,0:T(8,128)(2,1)S(1)} %get-tuple-element.43), channel_id=1, source_target_pairs={{2,0},{0,2},{3,1},{1,3},{6,4},{4,6},{7,5},{5,7},{10,8},{8,10},{11,... | collective-permute-start | bytes 884744 | tf_op jit(solution)/shard_map/ppermute | solution.py:274
  20.4 14.4 %collective-permute-start.3 = (bf16[384,512]{1,0:T(8,128)(2,1)S(1)}, bf16[384,512]{1,0:T(8,128)(2,1)S(1)}, u32[]{:S(2)}, u32[]{:S(2)}) collective-permute-start(bf16[384,512]{1,0:T(8,128)(2,1)S(1)} %get-tuple-element.48.refs_0_), channel_id=1, source_target_pairs={{4,0},{0,4},{12,8},{8,12},{5,1},{1,5},{13,9},{9,13},{6,2},{2,6},{1... | collective-permute-start | bytes 1179656 | tf_op jit(solution)/shard_map/ppermute | solution.py:282
  20.9 6.1 %collective-permute-start.5 = (bf16[192,768]{1,0:T(8,128)(2,1)S(1)}, bf16[192,768]{1,0:T(8,128)(2,1)S(1)}, u32[]{:S(2)}, u32[]{:S(2)}) collective-permute-start(bf16[192,768]{1,0:T(8,128)(2,1)S(1)} %collective-permute-done.4.refs_0_), channel_id=1, source_target_pairs={{1,0},{0,1},{3,2},{2,3},{5,4},{4,5},{7,6},{6,7},{9,8},{8,9},{11,10... | collective-permute-start | bytes 884744 | tf_op jit(solution)/shard_map/ppermute | solution.py:288
  22.9 15.2 %collective-permute-start.9 = (bf16[384,512]{1,0:T(8,128)(2,1)S(1)}, bf16[384,512]{1,0:T(8,128)(2,1)S(1)}, u32[]{:S(2)}, u32[]{:S(2)}) collective-permute-start(bf16[384,512]{1,0:T(8,128)(2,1)S(1)} %project.2), channel_id=1, source_target_pairs={{0,0},{1,8},{4,4},{5,12},{8,1},{9,9},{12,5},{13,13},{2,2},{3,10},{... | collective-permute-start | bytes 1179656 | tf_op jit(solution)/shard_map/ppermute | solution.py:328
  34.8 3.4 %collective-permute-start.6 = (bf16[384,512]{1,0:T(8,128)(2,1)S(1)}, bf16[384,512]{1,0:T(8,128)(2,1)S(1)}, u32[]{:S(2)}, u32[]{:S(2)}) collective-permute-start(bf16[384,512]{1,0:T(8,128)(2,1)S(1)} %get-tuple-element.48.refs_0_), channel_id=1, source_target_pairs={{1,0},{0,1},{3,2},{2,3},{5,4},{4,5},{7,6},{6,7},{9,8},{8,9},{11,10... | collective-permute-start | bytes 1179656 | tf_op jit(solution)/shard_map/ppermute | solution.py:288
  35.8 2.3 %collective-permute-start.7 = (bf16[384,512]{1,0:T(8,128)(2,1)S(1)}, bf16[384,512]{1,0:T(8,128)(2,1)S(1)}, u32[]{:S(2)}, u32[]{:S(2)}) collective-permute-start(bf16[384,512]{1,0:T(8,128)(2,1)S(1)} %collective-permute-done.3.refs_1_), channel_id=1, source_target_pairs={{1,0},{0,1},{3,2},{2,3},{5,4},{4,5},{7,6},{6,7},{9,8},{8,9},{11,10... | collective-permute-start | bytes 1179656 | tf_op jit(solution)/shard_map/ppermute | solution.py:288
  38.0 10.2 %collective-permute-start.10 = (bf16[384,512]{1,0:T(8,128)(2,1)S(1)}, bf16[384,512]{1,0:T(8,128)(2,1)S(1)}, u32[]{:S(2)}, u32[]{:S(2)}) collective-permute-start(bf16[384,512]{1,0:T(8,128)(2,1)S(1)} %collective-permute-done.9.refs_0_), channel_id=1, source_target_pairs={{4,0},{0,4},{12,8},{8,12},{5,1},{1,5},{13,9},{9,13},{6,2},{2,6},{1... | collective-permute-start | bytes 1179656 | tf_op jit(solution)/shard_map/ppermute | solution.py:282
  40.7 7.5 %collective-permute-start.8 = (bf16[384,256]{1,0:T(8,128)(2,1)S(1)}, bf16[384,256]{1,0:T(8,128)(2,1)S(1)}, u32[]{:S(2)}, u32[]{:S(2)}) collective-permute-start(bf16[384,256]{1,0:T(8,128)(2,1)S(1)} %end.1.refs_0_), channel_id=1, source_target_pairs={{2,0},{0,2},{3,1},{1,3},{6,4},{4,6},{7,5},{5,7},{10,8},{8,10},{11,... | collective-permute-start | bytes 589832 | tf_op jit(solution)/shard_map/ppermute | solution.py:274
  48.3 3.2 %collective-permute-start.11 = (bf16[384,512]{1,0:T(8,128)(2,1)S(1)}, bf16[384,512]{1,0:T(8,128)(2,1)S(1)}, u32[]{:S(2)}, u32[]{:S(2)}) collective-permute-start(bf16[384,512]{1,0:T(8,128)(2,1)S(1)} %collective-permute-done.9.refs_0_), channel_id=1, source_target_pairs={{1,0},{0,1},{3,2},{2,3},{5,4},{4,5},{7,6},{6,7},{9,8},{8,9},{11,10... | collective-permute-start | bytes 1179656 | tf_op jit(solution)/shard_map/ppermute | solution.py:288
  49.6 1.9 %collective-permute-start.12 = (bf16[384,512]{1,0:T(8,128)(2,1)S(1)}, bf16[384,512]{1,0:T(8,128)(2,1)S(1)}, u32[]{:S(2)}, u32[]{:S(2)}) collective-permute-start(bf16[384,512]{1,0:T(8,128)(2,1)S(1)} %collective-permute-done.10.refs_1_), channel_id=1, source_target_pairs={{1,0},{0,1},{3,2},{2,3},{5,4},{4,5},{7,6},{6,7},{9,8},{8,9},{11,10... | collective-permute-start | bytes 1179656 | tf_op jit(solution)/shard_map/ppermute | solution.py:288
  55.4 20.7 %collective-permute-start.15 = (bf16[3,96,256]{2,1,0:T(8,128)(2,1)S(1)}, bf16[3,96,256]{2,1,0:T(8,128)(2,1)S(1)}, u32[]{:S(2)}, u32[]{:S(2)}) collective-permute-start(bf16[3,96,256]{2,1,0:T(8,128)(2,1)S(1)} %get-tuple-element.64), channel_id=1, source_target_pairs={{0,0},{2,2},{8,1},{10,3},{4,4},{6,6},{12,5},{14,7},{1,8},{3,10},{9... | collective-permute-start | bytes 442376 | tf_op jit(solution)/shard_map/ppermute | solution.py:268
  57.7 10.9 %collective-permute-start.17 = (bf16[1,96,256]{2,1,0:T(8,128)(2,1)S(1)}, bf16[1,96,256]{2,1,0:T(8,128)(2,1)S(1)}, u32[]{:S(2)}, u32[]{:S(2)}) collective-permute-start(bf16[1,96,256]{2,1,0:T(8,128)(2,1)S(1)} %get-tuple-element.69), channel_id=1, source_target_pairs={{4,0},{6,2},{12,1},{14,3},{1,4},{3,6},{9,5},{11,7},{5,8},{7,10},{1... | collective-permute-start | bytes 147464 | tf_op jit(solution)/shard_map/ppermute | solution.py:268
  59.7 16.5 %collective-permute-start.16 = (bf16[3,96,256]{2,1,0:T(8,128)(2,1)S(1)}, bf16[3,96,256]{2,1,0:T(8,128)(2,1)S(1)}, u32[]{:S(2)}, u32[]{:S(2)}) collective-permute-start(bf16[3,96,256]{2,1,0:T(8,128)(2,1)S(1)} %get-tuple-element.65), channel_id=1, source_target_pairs={{2,0},{0,2},{10,1},{8,3},{6,4},{4,6},{14,5},{12,7},{3,8},{1,10},{1... | collective-permute-start | bytes 442376 | tf_op jit(solution)/shard_map/ppermute | solution.py:268
  61.5 13.5 %collective-permute-start.13 = (bf16[1,96,256]{2,1,0:T(8,128)(2,1)S(1)}, bf16[1,96,256]{2,1,0:T(8,128)(2,1)S(1)}, u32[]{:S(2)}, u32[]{:S(2)}) collective-permute-start(bf16[1,96,256]{2,1,0:T(8,128)(2,1)S(1)} %get-tuple-element.70), channel_id=1, source_target_pairs={{0,4},{2,6},{8,5},{10,7},{4,8},{6,10},{12,9},{14,11},{1,12},{3,14}... | collective-permute-start | bytes 147464 | tf_op jit(solution)/shard_map/ppermute | solution.py:268
  66.7 8.3 %collective-permute-start.18 = (bf16[1,96,256]{2,1,0:T(8,128)(2,1)S(1)}, bf16[1,96,256]{2,1,0:T(8,128)(2,1)S(1)}, u32[]{:S(2)}, u32[]{:S(2)}) collective-permute-start(bf16[1,96,256]{2,1,0:T(8,128)(2,1)S(1)} %get-tuple-element.67), channel_id=1, source_target_pairs={{6,0},{4,2},{14,1},{12,3},{3,4},{1,6},{11,5},{9,7},{7,8},{5,10},{1... | collective-permute-start | bytes 147464 | tf_op jit(solution)/shard_map/ppermute | solution.py:268
  68.6 7.5 %collective-permute-start.14 = (bf16[1,96,256]{2,1,0:T(8,128)(2,1)S(1)}, bf16[1,96,256]{2,1,0:T(8,128)(2,1)S(1)}, u32[]{:S(2)}, u32[]{:S(2)}) collective-permute-start(bf16[1,96,256]{2,1,0:T(8,128)(2,1)S(1)} %get-tuple-element.68), channel_id=1, source_target_pairs={{2,4},{0,6},{10,5},{8,7},{6,8},{4,10},{14,9},{12,11},{3,12},{1,14}... | collective-permute-start | bytes 147464 | tf_op jit(solution)/shard_map/ppermute | solution.py:268

commit v16 on v14

--- a/solution.py
+++ b/solution.py
@@ -246,8 +246,11 @@
         return band * cores + pair
 
     def worker(band, pair):
-        shift = (pair - band // span) % cores
-        return ((band + shift * span) % bands) * cores + (pair - shift) % cores
+        part, index = divmod(band, span)
+        if part == pair:
+            return band * cores + pair
+        shift = (pair - part) % cores
+        return (pair * span + span - 1 - index) * cores + (pair - shift) % cores
 
     places = [(band, pair) for band in range(bands) for pair in range(cores)]
     there = [(home(*p), worker(*p)) for p in places]

time: 73.4 us -> 70.4 us (0.959)
  waiting for transfers between devices: 27.7 us -> 19.9 us
  starting transfers between devices: 28.9 us -> 33.1 us
    ppermute x2, waiting for transfers between devices: 14.4 us -> 5.36 us  [neighbours(): lax.ppermute(pack, 'blk', [(g + (i + s) % span, g + i) for g, i in ring])]
    ppermute x1, starting transfers between devices: 5.44 us -> 0.66 us  [body(): above = lax.ppermute(features[-1:], both, down)]
    ppermute x2, waiting for transfers between devices: 7.51 us -> 3.31 us  [fetched(): return lax.ppermute(value, ('blk', 'tile', 'pair'), pairs)]
    ppermute x2, starting transfers between devices: 0.66 us -> 4.69 us  [neighbours(): lax.ppermute(pack, 'blk', [(g + (i + s) % span, g + i) for g, i in ring])]
    ppermute x1, waiting for transfers between devices: 0.01 us -> 3.17 us  [body(): below = lax.ppermute(features[:1], both, up)]
    ppermute x1, waiting for transfers between devices: 0.01 us -> 2.92 us  [body(): right_pack = lax.ppermute(tied(right_pack, pack), both, there)]
    ppermute x1, starting transfers between devices: 4.16 us -> 5.47 us  [body(): right_pack = lax.ppermute(tied(right_pack, pack), both, there)]
    ppermute x1, starting transfers between devices: 3.08 us -> 4.31 us  [body(): features = lax.ppermute(features, both, back)]
  transfers between devices with their start and end apart: 17 -> 17, of which waited for: 7 -> 9; matrix products, arithmetic and copies ran while one was open for 0% -> 0% of each run, Pallas kernels for 16% -> 17%
where the time goes in v16:
time: 70.4 us; the launch traced here: 69.6 us
  starting transfers between devices  33.1 us (47%)
  waiting for transfers between devices  19.9 us (28%)
  Pallas kernels  16.4 us (23%)
    pallas_call x12, Pallas kernels, run_kernel(): pl.pallas_call(kernel, out_shape=[jax.ShapeDtypeStruct(*s) for s in shape...  16.4 us
    ppermute x2, starting transfers between devices, fetched(): return lax.ppermute(value, ('blk', 'tile', 'pair'), pairs)  6.06 us
    ppermute x1, starting transfers between devices, body(): right_pack = lax.ppermute(tied(right_pack, pack), both, there)  5.47 us
    ppermute x2, waiting for transfers between devices, neighbours(): lax.ppermute(pack, 'blk', [(g + (i + s) % span, g + i) for g, i in ring])  5.36 us
    ppermute x4, starting transfers between devices, from_tile(): lax.ppermute(value, 'tile', [((i + step) % tiles, i) for i in range(tiles)])  4.88 us
    ppermute x4, waiting for transfers between devices, from_tile(): lax.ppermute(value, 'tile', [((i + step) % tiles, i) for i in range(tiles)])  4.82 us
    ppermute x2, starting transfers between devices, neighbours(): lax.ppermute(pack, 'blk', [(g + (i + s) % span, g + i) for g, i in ring])  4.69 us
    ppermute x5, starting transfers between devices, across(): lax.ppermute(pack, 'pair', [((i + s) % cores, i) for i in range(cores)])  4.6 us
  transfers between devices with their start and end apart: 17, of which 9 were waited for; matrix products, arithmetic and copies ran while one was open for 0% of the time, Pallas kernels for 17%

profile of v16, /device:TPU:1, one launch (start us, length us, event | category | flops | bytes accessed | tf_op | source)
XLA Modules:
  0.0 69.6 jit_solution(17775381888230458398)
XLA Ops:
  0.0 2.0 %collective-permute-start.2 = (bf16[384,384]{1,0:T(8,128)(2,1)}, bf16[384,384]{1,0:T(8,128)(2,1)S(1)}, u32[]{:S(2)}, u32[]{:S(2)}) collective-permute-start(bf16[384,384]{1,0:T(8,128)(2,1)} %bitcast.8), channel_id=1, source_target_pairs={{2,0},{0,2},{3,1},{1,3},{6,4},{4,6},{7,5},{5,7},{10,8},{8,10},{11,... | collective-permute-start | bytes 884744 | tf_op jit(solution)/shard_map/ppermute | solution.py:272
  2.0 4.1 %collective-permute-start.1 = (bf16[384,384]{1,0:T(8,128)(2,1)}, bf16[384,384]{1,0:T(8,128)(2,1)S(1)}, u32[]{:S(2)}, u32[]{:S(2)}) collective-permute-start(bf16[384,384]{1,0:T(8,128)(2,1)} %bitcast.10), channel_id=1, source_target_pairs={{2,0},{0,2},{3,12},{1,14},{6,4},{4,6},{7,8},{5,10},{10,5},{8,7},{1... | collective-permute-start | bytes 884744 | tf_op jit(solution)/shard_map/ppermute | solution.py:266
  6.2 1.9 %collective-permute-start = (bf16[384,384]{1,0:T(8,128)(2,1)}, bf16[384,384]{1,0:T(8,128)(2,1)S(1)}, u32[]{:S(2)}, u32[]{:S(2)}) collective-permute-start(bf16[384,384]{1,0:T(8,128)(2,1)} %bitcast.11), channel_id=1, source_target_pairs={{0,0},{2,2},{1,12},{3,14},{4,4},{6,6},{5,8},{7,10},{8,5},{10,7},{9... | collective-permute-start | bytes 884744 | tf_op jit(solution)/shard_map/ppermute | solution.py:266
  8.1 2.6 %stage.1 = (bf16[256,768]{1,0:T(8,128)(2,1)S(1)}, bf16[384,256]{1,0:T(8,128)(2,1)S(1)}, bf16[256,768]{1,0:T(8,128)(2,1)S(1)}, bf16[384,384]{1,0:T(8,128)(2,1)S(1...) custom-call(bf16[256,768]{1,0:T(8,128)(2,1)} %refs_0_.1, ...), custom_call_target="tpu_custom_call" | custom-call | tf_op jit(solution)/shard_map/stage/pallas_call | solution.py:22
  10.7 1.3 %collective-permute-start.4 = (bf16[192,768]{1,0:T(8,128)(2,1)S(1)}, bf16[192,768]{1,0:T(8,128)(2,1)S(1)}, u32[]{:S(2)}, u32[]{:S(2)}) collective-permute-start(bf16[192,768]{1,0:T(8,128)(2,1)S(1)} %get-tuple-element.44), channel_id=1, source_target_pairs={{2,0},{0,2},{3,1},{1,3},{6,4},{4,6},{7,5},{5,7},{10,8},{8,10},{11,... | collective-permute-start | bytes 884744 | tf_op jit(solution)/shard_map/ppermute | solution.py:272
  13.0 3.3 %collective-permute-done.refs_0_.refs_4_ = bf16[384,384]{1,0:T(8,128)(2,1)S(1)} collective-permute-done((bf16[384,384]{1,0:T(8,128)(2,1)}, bf16[384,384]{1,0:T(8,128)(2,1)S(1)}, u32[]{:S(2)}, u32[]{:S(2)}) %collective-permute-start) | collective-permute-done | bytes 294944 | tf_op jit(solution)/shard_map/ppermute | solution.py:266
  16.3 1.1 %project.3 = (bf16[384,256]{1,0:T(8,128)(2,1)S(1)}, bf16[384,512]{1,0:T(8,128)(2,1)S(1)}) custom-call(bf16[384,384]{1,0:T(8,128)(2,1)S(1)} %collective-permute-done.refs_0_.refs_4_, bf16[384,384]{1,0:T(8,128)(2,1)S(1)} %collective-permute-done.1.refs_1_.refs_5_, bf16[3,2,384,256]{3,2,1,0:T(8,128)(2,1)S(1)} %bitcast.7), custom_call_target="tpu_custom_call" | custom-call | tf_op jit(solution)/shard_map/project/pallas_call | solution.py:22
  17.4 3.7 %collective-permute-start.3 = (bf16[384,512]{1,0:T(8,128)(2,1)S(1)}, bf16[384,512]{1,0:T(8,128)(2,1)S(1)}, u32[]{:S(2)}, u32[]{:S(2)}) collective-permute-start(bf16[384,512]{1,0:T(8,128)(2,1)S(1)} %get-tuple-element.49.refs_0_), channel_id=1, source_target_pairs={{4,0},{0,4},{12,8},{8,12},{5,1},{1,5},{13,9},{9,13},{6,2},{2,6},{1... | collective-permute-start | bytes 1179656 | tf_op jit(solution)/shard_map/ppermute | solution.py:280
  21.1 1.8 %collective-permute-start.5 = (bf16[192,768]{1,0:T(8,128)(2,1)S(1)}, bf16[192,768]{1,0:T(8,128)(2,1)S(1)}, u32[]{:S(2)}, u32[]{:S(2)}) collective-permute-start(bf16[192,768]{1,0:T(8,128)(2,1)S(1)} %collective-permute-done.4.refs_0_), channel_id=1, source_target_pairs={{1,0},{0,1},{3,2},{2,3},{5,4},{4,5},{7,6},{6,7},{9,8},{8,9},{11,10... | collective-permute-start | bytes 884744 | tf_op jit(solution)/shard_map/ppermute | solution.py:286
  22.9 5.5 %collective-permute-start.9 = (bf16[384,512]{1,0:T(8,128)(2,1)S(1)}, bf16[384,512]{1,0:T(8,128)(2,1)S(1)}, u32[]{:S(2)}, u32[]{:S(2)}) collective-permute-start(bf16[384,512]{1,0:T(8,128)(2,1)S(1)} %project.2), channel_id=1, source_target_pairs={{0,0},{1,12},{4,4},{5,8},{8,5},{9,9},{12,1},{13,13},{2,2},{3,14},{... | collective-permute-start | bytes 1179656 | tf_op jit(solution)/shard_map/ppermute | solution.py:326
  29.2 2.3 %collective-permute-start.6 = (bf16[384,512]{1,0:T(8,128)(2,1)S(1)}, bf16[384,512]{1,0:T(8,128)(2,1)S(1)}, u32[]{:S(2)}, u32[]{:S(2)}) collective-permute-start(bf16[384,512]{1,0:T(8,128)(2,1)S(1)} %get-tuple-element.49.refs_0_), channel_id=1, source_target_pairs={{1,0},{0,1},{3,2},{2,3},{5,4},{4,5},{7,6},{6,7},{9,8},{8,9},{11,10... | collective-permute-start | bytes 1179656 | tf_op jit(solution)/shard_map/ppermute | solution.py:286
  31.6 2.2 %begin.1 = (f32[4,384,128]{2,1,0:T(8,128)S(1)}, f32[4,384,1]{2,1,0:T(8,128)S(1)}) custom-call(bf16[384,256]{1,0:T(8,128)(2,1)S(1)} %get-tuple-element.42.query, bf16[384,512]{1,0:T(8,128)(2,1)S(1)} %get-tuple-element.49.refs_0_, bf16[384,512]{1,0:T(8,128)(2,1)S(1)} %collective-permute-done.3.refs_1_), custom_call_target="tpu_custom_call" | custom-call | tf_op jit(solution)/shard_map/begin/pallas_call | solution.py:22
  33.8 2.9 %collective-permute-done.9.refs_0_ = bf16[384,512]{1,0:T(8,128)(2,1)S(1)} collective-permute-done((bf16[384,512]{1,0:T(8,128)(2,1)S(1)}, bf16[384,512]{1,0:T(8,128)(2,1)S(1)}, u32[]{:S(2)}, u32[]{:S(2)}) %collective-permute-start.9) | collective-permute-done | bytes 393248 | tf_op jit(solution)/shard_map/ppermute | solution.py:326
  36.7 1.0 %collective-permute-start.10 = (bf16[384,512]{1,0:T(8,128)(2,1)S(1)}, bf16[384,512]{1,0:T(8,128)(2,1)S(1)}, u32[]{:S(2)}, u32[]{:S(2)}) collective-permute-start(bf16[384,512]{1,0:T(8,128)(2,1)S(1)} %collective-permute-done.9.refs_0_), channel_id=1, source_target_pairs={{4,0},{0,4},{12,8},{8,12},{5,1},{1,5},{13,9},{9,13},{6,2},{2,6},{1... | collective-permute-start | bytes 1179656 | tf_op jit(solution)/shard_map/ppermute | solution.py:280
  37.7 2.6 %end.1.refs_0_ = bf16[384,256]{1,0:T(8,128)(2,1)S(1)} custom-call(bf16[384,256]{1,0:T(8,128)(2,1)S(1)} %get-tuple-element.42.query, bf16[384,512]{1,0:T(8,128)(2,1)S(1)} %collective-permute-done.6.refs_0_, bf16[384,512]{1,0:T(8,128)(2,1)S(1)} %collective-permute-done.7.refs_1_, f32[4,384,128]{2,1,0:T(8,128)S(1)} %get-tuple-element.51.refs_2_, ...), custom_call_target="tpu_custom_call" | custom-call | tf_op jit(solution)/shard_map/end/pallas_call | solution.py:22
  40.3 1.3 %collective-permute-start.8 = (bf16[384,256]{1,0:T(8,128)(2,1)S(1)}, bf16[384,256]{1,0:T(8,128)(2,1)S(1)}, u32[]{:S(2)}, u32[]{:S(2)}) collective-permute-start(bf16[384,256]{1,0:T(8,128)(2,1)S(1)} %end.1.refs_0_), channel_id=1, source_target_pairs={{2,0},{0,2},{3,1},{1,3},{6,4},{4,6},{7,5},{5,7},{10,8},{8,10},{11,... | collective-permute-start | bytes 589832 | tf_op jit(solution)/shard_map/ppermute | solution.py:272
  41.6 4.9 %collective-permute-done.10.refs_1_ = bf16[384,512]{1,0:T(8,128)(2,1)S(1)} collective-permute-done((bf16[384,512]{1,0:T(8,128)(2,1)S(1)}, bf16[384,512]{1,0:T(8,128)(2,1)S(1)}, u32[]{:S(2)}, u32[]{:S(2)}) %collective-permute-start.10) | collective-permute-done | bytes 393248 | tf_op jit(solution)/shard_map/ppermute | solution.py:280
  47.1 1.5 %update.1 = (bf16[2,384,384]{2,1,0:T(8,128)(2,1)S(1)}, bf16[384,256]{1,0:T(8,128)(2,1)S(1)}) custom-call(bf16[384,256]{1,0:T(8,128)(2,1)S(1)} %end.1.refs_0_, bf16[384,256]{1,0:T(8,128)(2,1)S(1)} %collective-permute-done.8.refs_1_, bf16[256,768]{1,0:T(8,128)(2,1)S(1)} %get-tuple-element.53.refs_2_, bf16[256,768]{1,0:T(8,128)(2,1)S(1)} %get-tuple-element.54.refs_3_, ...), custom_call_target="tpu_custom_call" | custom-call | tf_op jit(solution)/shard_map/update/pallas_call | solution.py:22
  48.9 3.8 %end_map.1 = (bf16[3,96,256]{2,1,0:T(8,128)(2,1)S(1)}, bf16[3,96,256]{2,1,0:T(8,128)(2,1)S(1)}) custom-call(bf16[384,256]{1,0:T(8,128)(2,1)S(1)} %get-tuple-element.56.query, bf16[384,512]{1,0:T(8,128)(2,1)S(1)} %collective-permute-done.9.refs_0_, bf16[384,512]{1,0:T(8,128)(2,1)S(1)} %collective-permute-done.10.refs_1_, ...), custom_call_target="tpu_custom_call" | custom-call | tf_op jit(solution)/shard_map/end_map/pallas_call | solution.py:22
  53.5 4.4 %collective-permute-done.13.refs_2_ = bf16[3,96,256]{2,1,0:T(8,128)(2,1)S(1)} collective-permute-done((bf16[3,96,256]{2,1,0:T(8,128)(2,1)S(1)}, bf16[3,96,256]{2,1,0:T(8,128)(2,1)S(1)}, u32[]{:S(2)}, u32[]{:S(2)}) %collective-permute-start.13) | collective-permute-done | bytes 147488 | tf_op jit(solution)/shard_map/ppermute | solution.py:272
  57.9 4.3 %collective-permute-start.14 = (bf16[3,96,256]{2,1,0:T(8,128)(2,1)S(1)}, bf16[3,96,256]{2,1,0:T(8,128)(2,1)S(1)}, u32[]{:S(2)}, u32[]{:S(2)}) collective-permute-start(bf16[3,96,256]{2,1,0:T(8,128)(2,1)S(1)} %add.1), channel_id=1, source_target_pairs={{0,0},{12,1},{4,4},{8,5},{5,8},{9,9},{1,12},{13,13},{2,2},{14,3},{... | collective-permute-start | bytes 442376 | tf_op jit(solution)/shard_map/ppermute | solution.py:385
  62.3 2.5 %collective-permute-start.16 = (bf16[1,96,256]{2,1,0:T(8,128)(2,1)S(1)}, bf16[1,96,256]{2,1,0:T(8,128)(2,1)S(1)}, u32[]{:S(2)}, u32[]{:S(2)}) collective-permute-start(bf16[1,96,256]{2,1,0:T(8,128)(2,1)S(1)} %get-tuple-element.69), channel_id=1, source_target_pairs={{4,0},{8,1},{5,4},{9,5},{1,8},{13,9},{6,2},{10,3},{7,6},{11,7},{3,... | collective-permute-start | bytes 147464 | tf_op jit(solution)/shard_map/ppermute | solution.py:384
  65.4 3.2 %collective-permute-done.16.below = bf16[1,96,256]{2,1,0:T(8,128)(2,1)S(1)} collective-permute-done((bf16[1,96,256]{2,1,0:T(8,128)(2,1)S(1)}, bf16[1,96,256]{2,1,0:T(8,128)(2,1)S(1)}, u32[]{:S(2)}, u32[]{:S(2)}) %collective-permute-start.16) | collective-permute-done | bytes 49184 | tf_op jit(solution)/shard_map/ppermute | solution.py:384
  68.6 1.0 %join.1 = bf16[3,64,256]{2,1,0:T(8,128)(2,1)} custom-call(bf16[3,96,256]{2,1,0:T(8,128)(2,1)S(1)} %collective-permute-done.14.window, bf16[1,96,256]{2,1,0:T(8,128)(2,1)S(1)} %collective-permute-done.15.above, bf16[1,96,256]{2,1,0:T(8,128)(2,1)S(1)} %collective-permute-done.16.below, bf16[3,3,256,256]{3,2,1,0:T(8,128)(2,1)S(1)} %get-tuple-element.68.weight), custom_call_target="tpu_custom_call" | custom-call | tf_op jit(solution)/shard_map/join/pallas_call | solution.py:22
  (23 shorter events, 4.4 us)
Async XLA Ops:
  0.0 12.1 %collective-permute-start.2 = (bf16[384,384]{1,0:T(8,128)(2,1)}, bf16[384,384]{1,0:T(8,128)(2,1)S(1)}, u32[]{:S(2)}, u32[]{:S(2)}) collective-permute-start(bf16[384,384]{1,0:T(8,128)(2,1)} %bitcast.8), channel_id=1, source_target_pairs={{2,0},{0,2},{3,1},{1,3},{6,4},{4,6},{7,5},{5,7},{10,8},{8,10},{11,... | collective-permute-start | bytes 884744 | tf_op jit(solution)/shard_map/ppermute | solution.py:272
  2.0 11.0 %collective-permute-start.1 = (bf16[384,384]{1,0:T(8,128)(2,1)}, bf16[384,384]{1,0:T(8,128)(2,1)S(1)}, u32[]{:S(2)}, u32[]{:S(2)}) collective-permute-start(bf16[384,384]{1,0:T(8,128)(2,1)} %bitcast.10), channel_id=1, source_target_pairs={{2,0},{0,2},{3,12},{1,14},{6,4},{4,6},{7,8},{5,10},{10,5},{8,7},{1... | collective-permute-start | bytes 884744 | tf_op jit(solution)/shard_map/ppermute | solution.py:266
  6.2 10.1 %collective-permute-start = (bf16[384,384]{1,0:T(8,128)(2,1)}, bf16[384,384]{1,0:T(8,128)(2,1)S(1)}, u32[]{:S(2)}, u32[]{:S(2)}) collective-permute-start(bf16[384,384]{1,0:T(8,128)(2,1)} %bitcast.11), channel_id=1, source_target_pairs={{0,0},{2,2},{1,12},{3,14},{4,4},{6,6},{5,8},{7,10},{8,5},{10,7},{9... | collective-permute-start | bytes 884744 | tf_op jit(solution)/shard_map/ppermute | solution.py:266
  10.7 10.4 %collective-permute-start.4 = (bf16[192,768]{1,0:T(8,128)(2,1)S(1)}, bf16[192,768]{1,0:T(8,128)(2,1)S(1)}, u32[]{:S(2)}, u32[]{:S(2)}) collective-permute-start(bf16[192,768]{1,0:T(8,128)(2,1)S(1)} %get-tuple-element.44), channel_id=1, source_target_pairs={{2,0},{0,2},{3,1},{1,3},{6,4},{4,6},{7,5},{5,7},{10,8},{8,10},{11,... | collective-permute-start | bytes 884744 | tf_op jit(solution)/shard_map/ppermute | solution.py:272
  17.4 11.8 %collective-permute-start.3 = (bf16[384,512]{1,0:T(8,128)(2,1)S(1)}, bf16[384,512]{1,0:T(8,128)(2,1)S(1)}, u32[]{:S(2)}, u32[]{:S(2)}) collective-permute-start(bf16[384,512]{1,0:T(8,128)(2,1)S(1)} %get-tuple-element.49.refs_0_), channel_id=1, source_target_pairs={{4,0},{0,4},{12,8},{8,12},{5,1},{1,5},{13,9},{9,13},{6,2},{2,6},{1... | collective-permute-start | bytes 1179656 | tf_op jit(solution)/shard_map/ppermute | solution.py:280
  21.1 7.2 %collective-permute-start.5 = (bf16[192,768]{1,0:T(8,128)(2,1)S(1)}, bf16[192,768]{1,0:T(8,128)(2,1)S(1)}, u32[]{:S(2)}, u32[]{:S(2)}) collective-permute-start(bf16[192,768]{1,0:T(8,128)(2,1)S(1)} %collective-permute-done.4.refs_0_), channel_id=1, source_target_pairs={{1,0},{0,1},{3,2},{2,3},{5,4},{4,5},{7,6},{6,7},{9,8},{8,9},{11,10... | collective-permute-start | bytes 884744 | tf_op jit(solution)/shard_map/ppermute | solution.py:286
  22.9 13.9 %collective-permute-start.9 = (bf16[384,512]{1,0:T(8,128)(2,1)S(1)}, bf16[384,512]{1,0:T(8,128)(2,1)S(1)}, u32[]{:S(2)}, u32[]{:S(2)}) collective-permute-start(bf16[384,512]{1,0:T(8,128)(2,1)S(1)} %project.2), channel_id=1, source_target_pairs={{0,0},{1,12},{4,4},{5,8},{8,5},{9,9},{12,1},{13,13},{2,2},{3,14},{... | collective-permute-start | bytes 1179656 | tf_op jit(solution)/shard_map/ppermute | solution.py:326
  29.2 8.5 %collective-permute-start.6 = (bf16[384,512]{1,0:T(8,128)(2,1)S(1)}, bf16[384,512]{1,0:T(8,128)(2,1)S(1)}, u32[]{:S(2)}, u32[]{:S(2)}) collective-permute-start(bf16[384,512]{1,0:T(8,128)(2,1)S(1)} %get-tuple-element.49.refs_0_), channel_id=1, source_target_pairs={{1,0},{0,1},{3,2},{2,3},{5,4},{4,5},{7,6},{6,7},{9,8},{8,9},{11,10... | collective-permute-start | bytes 1179656 | tf_op jit(solution)/shard_map/ppermute | solution.py:286
  31.6 6.2 %collective-permute-start.7 = (bf16[384,512]{1,0:T(8,128)(2,1)S(1)}, bf16[384,512]{1,0:T(8,128)(2,1)S(1)}, u32[]{:S(2)}, u32[]{:S(2)}) collective-permute-start(bf16[384,512]{1,0:T(8,128)(2,1)S(1)} %collective-permute-done.3.refs_1_), channel_id=1, source_target_pairs={{1,0},{0,1},{3,2},{2,3},{5,4},{4,5},{7,6},{6,7},{9,8},{8,9},{11,10... | collective-permute-start | bytes 1179656 | tf_op jit(solution)/shard_map/ppermute | solution.py:286
  36.7 9.7 %collective-permute-start.10 = (bf16[384,512]{1,0:T(8,128)(2,1)S(1)}, bf16[384,512]{1,0:T(8,128)(2,1)S(1)}, u32[]{:S(2)}, u32[]{:S(2)}) collective-permute-start(bf16[384,512]{1,0:T(8,128)(2,1)S(1)} %collective-permute-done.9.refs_0_), channel_id=1, source_target_pairs={{4,0},{0,4},{12,8},{8,12},{5,1},{1,5},{13,9},{9,13},{6,2},{2,6},{1... | collective-permute-start | bytes 1179656 | tf_op jit(solution)/shard_map/ppermute | solution.py:280
  40.3 6.3 %collective-permute-start.8 = (bf16[384,256]{1,0:T(8,128)(2,1)S(1)}, bf16[384,256]{1,0:T(8,128)(2,1)S(1)}, u32[]{:S(2)}, u32[]{:S(2)}) collective-permute-start(bf16[384,256]{1,0:T(8,128)(2,1)S(1)} %end.1.refs_0_), channel_id=1, source_target_pairs={{2,0},{0,2},{3,1},{1,3},{6,4},{4,6},{7,5},{5,7},{10,8},{8,10},{11,... | collective-permute-start | bytes 589832 | tf_op jit(solution)/shard_map/ppermute | solution.py:272
  46.6 2.0 %collective-permute-start.11 = (bf16[384,512]{1,0:T(8,128)(2,1)S(1)}, bf16[384,512]{1,0:T(8,128)(2,1)S(1)}, u32[]{:S(2)}, u32[]{:S(2)}) collective-permute-start(bf16[384,512]{1,0:T(8,128)(2,1)S(1)} %collective-permute-done.9.refs_0_), channel_id=1, source_target_pairs={{1,0},{0,1},{3,2},{2,3},{5,4},{4,5},{7,6},{6,7},{9,8},{8,9},{11,10... | collective-permute-start | bytes 1179656 | tf_op jit(solution)/shard_map/ppermute | solution.py:286
  47.0 1.9 %collective-permute-start.12 = (bf16[384,512]{1,0:T(8,128)(2,1)S(1)}, bf16[384,512]{1,0:T(8,128)(2,1)S(1)}, u32[]{:S(2)}, u32[]{:S(2)}) collective-permute-start(bf16[384,512]{1,0:T(8,128)(2,1)S(1)} %collective-permute-done.10.refs_1_), channel_id=1, source_target_pairs={{1,0},{0,1},{3,2},{2,3},{5,4},{4,5},{7,6},{6,7},{9,8},{8,9},{11,10... | collective-permute-start | bytes 1179656 | tf_op jit(solution)/shard_map/ppermute | solution.py:286
  52.8 5.1 %collective-permute-start.13 = (bf16[3,96,256]{2,1,0:T(8,128)(2,1)S(1)}, bf16[3,96,256]{2,1,0:T(8,128)(2,1)S(1)}, u32[]{:S(2)}, u32[]{:S(2)}) collective-permute-start(bf16[3,96,256]{2,1,0:T(8,128)(2,1)S(1)} %get-tuple-element.64), channel_id=1, source_target_pairs={{2,0},{0,2},{3,1},{1,3},{6,4},{4,6},{7,5},{5,7},{10,8},{8,10},{11,... | collective-permute-start | bytes 442376 | tf_op jit(solution)/shard_map/ppermute | solution.py:272
  57.9 10.7 %collective-permute-start.14 = (bf16[3,96,256]{2,1,0:T(8,128)(2,1)S(1)}, bf16[3,96,256]{2,1,0:T(8,128)(2,1)S(1)}, u32[]{:S(2)}, u32[]{:S(2)}) collective-permute-start(bf16[3,96,256]{2,1,0:T(8,128)(2,1)S(1)} %add.1), channel_id=1, source_target_pairs={{0,0},{12,1},{4,4},{8,5},{5,8},{9,9},{1,12},{13,13},{2,2},{14,3},{... | collective-permute-start | bytes 442376 | tf_op jit(solution)/shard_map/ppermute | solution.py:385
  62.3 6.3 %collective-permute-start.16 = (bf16[1,96,256]{2,1,0:T(8,128)(2,1)S(1)}, bf16[1,96,256]{2,1,0:T(8,128)(2,1)S(1)}, u32[]{:S(2)}, u32[]{:S(2)}) collective-permute-start(bf16[1,96,256]{2,1,0:T(8,128)(2,1)S(1)} %get-tuple-element.69), channel_id=1, source_target_pairs={{4,0},{8,1},{5,4},{9,5},{1,8},{13,9},{6,2},{10,3},{7,6},{11,7},{3,... | collective-permute-start | bytes 147464 | tf_op jit(solution)/shard_map/ppermute | solution.py:384
  64.7 3.8 %collective-permute-start.15 = (bf16[1,96,256]{2,1,0:T(8,128)(2,1)S(1)}, bf16[1,96,256]{2,1,0:T(8,128)(2,1)S(1)}, u32[]{:S(2)}, u32[]{:S(2)}) collective-permute-start(bf16[1,96,256]{2,1,0:T(8,128)(2,1)S(1)} %get-tuple-element.70), channel_id=1, source_target_pairs={{0,4},{12,5},{4,8},{8,9},{5,12},{9,13},{2,6},{14,7},{6,10},{10,11}... | collective-permute-start | bytes 147464 | tf_op jit(solution)/shard_map/ppermute | solution.py:383

commit v17 on v14

--- a/solution.py
+++ b/solution.py
@@ -246,8 +246,7 @@
         return band * cores + pair
 
     def worker(band, pair):
-        shift = (pair - band // span) % cores
-        return ((band + shift * span) % bands) * cores + (pair - shift) % cores
+        return pair * bands + band
 
     places = [(band, pair) for band in range(bands) for pair in range(cores)]
     there = [(home(*p), worker(*p)) for p in places]

time: 73.4 us -> 71.3 us (0.971)
  the two profiles are of different devices: /device:TPU:1 before, /device:TPU:30 now
where the time goes in v17:
time: 71.3 us; the launch traced here: 71.1 us
  waiting for transfers between devices  30.3 us (42%)
  starting transfers between devices  24.2 us (34%)
  Pallas kernels  16.4 us (23%)
    pallas_call x12, Pallas kernels, run_kernel(): pl.pallas_call(kernel, out_shape=[jax.ShapeDtypeStruct(*s) for s in shape...  16.4 us
    ppermute x4, waiting for transfers between devices, from_tile(): lax.ppermute(value, 'tile', [((i + step) % tiles, i) for i in range(tiles)])  11.6 us
    ppermute x2, waiting for transfers between devices, neighbours(): lax.ppermute(pack, 'blk', [(g + (i + s) % span, g + i) for g, i in ring])  11.3 us
    ppermute x1, waiting for transfers between devices, body(): above = lax.ppermute(features[-1:], both, down)  4.94 us
    ppermute x1, starting transfers between devices, body(): below = lax.ppermute(features[:1], both, up)  4.54 us
    ppermute x2, starting transfers between devices, neighbours(): lax.ppermute(pack, 'blk', [(g + (i + s) % span, g + i) for g, i in ring])  4.5 us
    ppermute x2, starting transfers between devices, fetched(): return lax.ppermute(value, ('blk', 'tile', 'pair'), pairs)  3.62 us
    ppermute x5, starting transfers between devices, across(): lax.ppermute(pack, 'pair', [((i + s) % cores, i) for i in range(cores)])  3.15 us
  transfers between devices with their start and end apart: 17, of which 8 were waited for; matrix products, arithmetic and copies ran while one was open for 0% of the time, Pallas kernels for 16%

profile of v17, /device:TPU:30, one launch (start us, length us, event | category | flops | bytes accessed | tf_op | source)
XLA Modules:
  0.0 71.1 jit_solution(11427356452411502888)
XLA Ops:
  1.0 3.2 %collective-permute-start = (bf16[384,384]{1,0:T(8,128)(2,1)}, bf16[384,384]{1,0:T(8,128)(2,1)S(1)}, u32[]{:S(2)}, u32[]{:S(2)}) collective-permute-start(bf16[384,384]{1,0:T(8,128)(2,1)} %bitcast.11), channel_id=1, source_target_pairs={{0,0},{2,2},{1,8},{3,10},{4,1},{6,3},{5,9},{7,11},{8,4},{10,6},{9,... | collective-permute-start | bytes 884744 | tf_op jit(solution)/shard_map/ppermute | solution.py:262
  4.2 2.5 %stage.1 = (bf16[256,768]{1,0:T(8,128)(2,1)S(1)}, bf16[384,256]{1,0:T(8,128)(2,1)S(1)}, bf16[256,768]{1,0:T(8,128)(2,1)S(1)}, bf16[384,384]{1,0:T(8,128)(2,1)S(1...) custom-call(bf16[256,768]{1,0:T(8,128)(2,1)} %refs_0_.1, ...), custom_call_target="tpu_custom_call" | custom-call | tf_op jit(solution)/shard_map/stage/pallas_call | solution.py:22
  6.7 0.6 collective-permute-start.4
  7.3 6.0 %collective-permute-done.2.refs_1_ = bf16[384,384]{1,0:T(8,128)(2,1)S(1)} collective-permute-done((bf16[384,384]{1,0:T(8,128)(2,1)}, bf16[384,384]{1,0:T(8,128)(2,1)S(1)}, u32[]{:S(2)}, u32[]{:S(2)}) %collective-permute-start.2) | collective-permute-done | bytes 294944 | tf_op jit(solution)/shard_map/ppermute | solution.py:268
  13.3 0.8 %project.2 = bf16[384,512]{1,0:T(8,128)(2,1)S(1)} custom-call(bf16[384,384]{1,0:T(8,128)(2,1)S(1)} %get-tuple-element.37.refs_0_, bf16[384,384]{1,0:T(8,128)(2,1)S(1)} %collective-permute-done.2.refs_1_, bf16[3,2,384,256]{3,2,1,0:T(8,128)(2,1)S(1)} %bitcast.5), custom_call_target="tpu_custom_call" | custom-call | tf_op jit(solution)/shard_map/project/pallas_call | solution.py:22
  14.1 1.1 %project.3 = (bf16[384,256]{1,0:T(8,128)(2,1)S(1)}, bf16[384,512]{1,0:T(8,128)(2,1)S(1)}) custom-call(bf16[384,384]{1,0:T(8,128)(2,1)S(1)} %collective-permute-done.refs_0_.refs_4_, bf16[384,384]{1,0:T(8,128)(2,1)S(1)} %collective-permute-done.1.refs_1_.refs_5_, bf16[3,2,384,256]{3,2,1,0:T(8,128)(2,1)S(1)} %bitcast.7), custom_call_target="tpu_custom_call" | custom-call | tf_op jit(solution)/shard_map/project/pallas_call | solution.py:22
  15.2 3.7 %collective-permute-start.3 = (bf16[384,512]{1,0:T(8,128)(2,1)S(1)}, bf16[384,512]{1,0:T(8,128)(2,1)S(1)}, u32[]{:S(2)}, u32[]{:S(2)}) collective-permute-start(bf16[384,512]{1,0:T(8,128)(2,1)S(1)} %get-tuple-element.49.refs_0_), channel_id=1, source_target_pairs={{4,0},{0,4},{12,8},{8,12},{5,1},{1,5},{13,9},{9,13},{6,2},{2,6},{1... | collective-permute-start | bytes 1179656 | tf_op jit(solution)/shard_map/ppermute | solution.py:276
  18.9 0.7 collective-permute-done.4.refs_0_
  19.6 2.1 %collective-permute-start.5 = (bf16[192,768]{1,0:T(8,128)(2,1)S(1)}, bf16[192,768]{1,0:T(8,128)(2,1)S(1)}, u32[]{:S(2)}, u32[]{:S(2)}) collective-permute-start(bf16[192,768]{1,0:T(8,128)(2,1)S(1)} %collective-permute-done.4.refs_0_), channel_id=1, source_target_pairs={{1,0},{0,1},{3,2},{2,3},{5,4},{4,5},{7,6},{6,7},{9,8},{8,9},{11,10... | collective-permute-start | bytes 884744 | tf_op jit(solution)/shard_map/ppermute | solution.py:282
  21.7 2.2 %collective-permute-start.9 = (bf16[384,512]{1,0:T(8,128)(2,1)S(1)}, bf16[384,512]{1,0:T(8,128)(2,1)S(1)}, u32[]{:S(2)}, u32[]{:S(2)}) collective-permute-start(bf16[384,512]{1,0:T(8,128)(2,1)S(1)} %project.2), channel_id=1, source_target_pairs={{0,0},{1,8},{4,1},{5,9},{8,4},{9,12},{12,5},{13,13},{2,2},{3,10},{... | collective-permute-start | bytes 1179656 | tf_op jit(solution)/shard_map/ppermute | solution.py:322
  24.3 3.8 %collective-permute-done.3.refs_1_ = bf16[384,512]{1,0:T(8,128)(2,1)S(1)} collective-permute-done((bf16[384,512]{1,0:T(8,128)(2,1)S(1)}, bf16[384,512]{1,0:T(8,128)(2,1)S(1)}, u32[]{:S(2)}, u32[]{:S(2)}) %collective-permute-start.3) | collective-permute-done | bytes 393248 | tf_op jit(solution)/shard_map/ppermute | solution.py:276
  28.7 2.2 %begin.1 = (f32[4,384,128]{2,1,0:T(8,128)S(1)}, f32[4,384,1]{2,1,0:T(8,128)S(1)}) custom-call(bf16[384,256]{1,0:T(8,128)(2,1)S(1)} %get-tuple-element.42.query, bf16[384,512]{1,0:T(8,128)(2,1)S(1)} %get-tuple-element.49.refs_0_, bf16[384,512]{1,0:T(8,128)(2,1)S(1)} %collective-permute-done.3.refs_1_), custom_call_target="tpu_custom_call" | custom-call | tf_op jit(solution)/shard_map/begin/pallas_call | solution.py:22
  30.9 2.1 %collective-permute-done.9.refs_0_ = bf16[384,512]{1,0:T(8,128)(2,1)S(1)} collective-permute-done((bf16[384,512]{1,0:T(8,128)(2,1)S(1)}, bf16[384,512]{1,0:T(8,128)(2,1)S(1)}, u32[]{:S(2)}, u32[]{:S(2)}) %collective-permute-start.9) | collective-permute-done | bytes 393248 | tf_op jit(solution)/shard_map/ppermute | solution.py:322
  33.1 0.8 %collective-permute-start.10 = (bf16[384,512]{1,0:T(8,128)(2,1)S(1)}, bf16[384,512]{1,0:T(8,128)(2,1)S(1)}, u32[]{:S(2)}, u32[]{:S(2)}) collective-permute-start(bf16[384,512]{1,0:T(8,128)(2,1)S(1)} %collective-permute-done.9.refs_0_), channel_id=1, source_target_pairs={{4,0},{0,4},{12,8},{8,12},{5,1},{1,5},{13,9},{9,13},{6,2},{2,6},{1... | collective-permute-start | bytes 1179656 | tf_op jit(solution)/shard_map/ppermute | solution.py:276
  33.9 2.6 %end.1.refs_0_ = bf16[384,256]{1,0:T(8,128)(2,1)S(1)} custom-call(bf16[384,256]{1,0:T(8,128)(2,1)S(1)} %get-tuple-element.42.query, bf16[384,512]{1,0:T(8,128)(2,1)S(1)} %collective-permute-done.6.refs_0_, bf16[384,512]{1,0:T(8,128)(2,1)S(1)} %collective-permute-done.7.refs_1_, f32[4,384,128]{2,1,0:T(8,128)S(1)} %get-tuple-element.51.refs_2_, ...), custom_call_target="tpu_custom_call" | custom-call | tf_op jit(solution)/shard_map/end/pallas_call | solution.py:22
  37.1 7.5 %collective-permute-done.10.refs_1_ = bf16[384,512]{1,0:T(8,128)(2,1)S(1)} collective-permute-done((bf16[384,512]{1,0:T(8,128)(2,1)S(1)}, bf16[384,512]{1,0:T(8,128)(2,1)S(1)}, u32[]{:S(2)}, u32[]{:S(2)}) %collective-permute-start.10) | collective-permute-done | bytes 393248 | tf_op jit(solution)/shard_map/ppermute | solution.py:276
  45.1 1.5 %update.1 = (bf16[2,384,384]{2,1,0:T(8,128)(2,1)S(1)}, bf16[384,256]{1,0:T(8,128)(2,1)S(1)}) custom-call(bf16[384,256]{1,0:T(8,128)(2,1)S(1)} %end.1.refs_0_, bf16[384,256]{1,0:T(8,128)(2,1)S(1)} %collective-permute-done.8.refs_1_, bf16[256,768]{1,0:T(8,128)(2,1)S(1)} %get-tuple-element.53.refs_2_, bf16[256,768]{1,0:T(8,128)(2,1)S(1)} %get-tuple-element.54.refs_3_, ...), custom_call_target="tpu_custom_call" | custom-call | tf_op jit(solution)/shard_map/update/pallas_call | solution.py:22
  46.9 3.8 %end_map.1 = (bf16[3,96,256]{2,1,0:T(8,128)(2,1)S(1)}, bf16[3,96,256]{2,1,0:T(8,128)(2,1)S(1)}) custom-call(bf16[384,256]{1,0:T(8,128)(2,1)S(1)} %get-tuple-element.56.query, bf16[384,512]{1,0:T(8,128)(2,1)S(1)} %collective-permute-done.9.refs_0_, bf16[384,512]{1,0:T(8,128)(2,1)S(1)} %collective-permute-done.10.refs_1_, ...), custom_call_target="tpu_custom_call" | custom-call | tf_op jit(solution)/shard_map/end_map/pallas_call | solution.py:22
  51.7 4.9 %collective-permute-done.13.refs_2_ = bf16[3,96,256]{2,1,0:T(8,128)(2,1)S(1)} collective-permute-done((bf16[3,96,256]{2,1,0:T(8,128)(2,1)S(1)}, bf16[3,96,256]{2,1,0:T(8,128)(2,1)S(1)}, u32[]{:S(2)}, u32[]{:S(2)}) %collective-permute-start.13) | collective-permute-done | bytes 147488 | tf_op jit(solution)/shard_map/ppermute | solution.py:268
  56.7 1.9 %collective-permute-start.14 = (bf16[3,96,256]{2,1,0:T(8,128)(2,1)S(1)}, bf16[3,96,256]{2,1,0:T(8,128)(2,1)S(1)}, u32[]{:S(2)}, u32[]{:S(2)}) collective-permute-start(bf16[3,96,256]{2,1,0:T(8,128)(2,1)S(1)} %add.1), channel_id=1, source_target_pairs={{0,0},{8,1},{1,4},{9,5},{4,8},{12,9},{5,12},{13,13},{2,2},{10,3},{... | collective-permute-start | bytes 442376 | tf_op jit(solution)/shard_map/ppermute | solution.py:381
  58.6 4.5 %collective-permute-start.16 = (bf16[1,96,256]{2,1,0:T(8,128)(2,1)S(1)}, bf16[1,96,256]{2,1,0:T(8,128)(2,1)S(1)}, u32[]{:S(2)}, u32[]{:S(2)}) collective-permute-start(bf16[1,96,256]{2,1,0:T(8,128)(2,1)S(1)} %get-tuple-element.69), channel_id=1, source_target_pairs={{1,0},{9,1},{4,4},{12,5},{5,8},{13,9},{3,2},{11,3},{6,6},{14,7},{7... | collective-permute-start | bytes 147464 | tf_op jit(solution)/shard_map/ppermute | solution.py:380
  63.2 1.9 %collective-permute-start.15 = (bf16[1,96,256]{2,1,0:T(8,128)(2,1)S(1)}, bf16[1,96,256]{2,1,0:T(8,128)(2,1)S(1)}, u32[]{:S(2)}, u32[]{:S(2)}) collective-permute-start(bf16[1,96,256]{2,1,0:T(8,128)(2,1)S(1)} %get-tuple-element.70), channel_id=1, source_target_pairs={{0,4},{8,5},{1,8},{9,9},{4,12},{12,13},{2,6},{10,7},{3,10},{11,11}... | collective-permute-start | bytes 147464 | tf_op jit(solution)/shard_map/ppermute | solution.py:379
  65.1 4.9 %collective-permute-done.15.above = bf16[1,96,256]{2,1,0:T(8,128)(2,1)S(1)} collective-permute-done((bf16[1,96,256]{2,1,0:T(8,128)(2,1)S(1)}, bf16[1,96,256]{2,1,0:T(8,128)(2,1)S(1)}, u32[]{:S(2)}, u32[]{:S(2)}) %collective-permute-start.15) | collective-permute-done | bytes 49184 | tf_op jit(solution)/shard_map/ppermute | solution.py:379
  70.1 1.0 %join.1 = bf16[3,64,256]{2,1,0:T(8,128)(2,1)} custom-call(bf16[3,96,256]{2,1,0:T(8,128)(2,1)S(1)} %collective-permute-done.14.window, bf16[1,96,256]{2,1,0:T(8,128)(2,1)S(1)} %collective-permute-done.15.above, bf16[1,96,256]{2,1,0:T(8,128)(2,1)S(1)} %collective-permute-done.16.below, bf16[3,3,256,256]{3,2,1,0:T(8,128)(2,1)S(1)} %get-tuple-element.68.weight), custom_call_target="tpu_custom_call" | custom-call | tf_op jit(solution)/shard_map/join/pallas_call | solution.py:22
  (23 shorter events, 4.3 us)
Async XLA Ops:
  0.0 13.3 %collective-permute-start.2 = (bf16[384,384]{1,0:T(8,128)(2,1)}, bf16[384,384]{1,0:T(8,128)(2,1)S(1)}, u32[]{:S(2)}, u32[]{:S(2)}) collective-permute-start(bf16[384,384]{1,0:T(8,128)(2,1)} %bitcast.8), channel_id=1, source_target_pairs={{2,0},{0,2},{3,1},{1,3},{6,4},{4,6},{7,5},{5,7},{10,8},{8,10},{11,... | collective-permute-start | bytes 884744 | tf_op jit(solution)/shard_map/ppermute | solution.py:268
  0.5 13.6 %collective-permute-start.1 = (bf16[384,384]{1,0:T(8,128)(2,1)}, bf16[384,384]{1,0:T(8,128)(2,1)S(1)}, u32[]{:S(2)}, u32[]{:S(2)}) collective-permute-start(bf16[384,384]{1,0:T(8,128)(2,1)} %bitcast.10), channel_id=1, source_target_pairs={{2,0},{0,2},{3,8},{1,10},{6,1},{4,3},{7,9},{5,11},{10,4},{8,6},{11... | collective-permute-start | bytes 884744 | tf_op jit(solution)/shard_map/ppermute | solution.py:262
  1.0 13.2 %collective-permute-start = (bf16[384,384]{1,0:T(8,128)(2,1)}, bf16[384,384]{1,0:T(8,128)(2,1)S(1)}, u32[]{:S(2)}, u32[]{:S(2)}) collective-permute-start(bf16[384,384]{1,0:T(8,128)(2,1)} %bitcast.11), channel_id=1, source_target_pairs={{0,0},{2,2},{1,8},{3,10},{4,1},{6,3},{5,9},{7,11},{8,4},{10,6},{9,... | collective-permute-start | bytes 884744 | tf_op jit(solution)/shard_map/ppermute | solution.py:262
  6.7 12.9 %collective-permute-start.4 = (bf16[192,768]{1,0:T(8,128)(2,1)S(1)}, bf16[192,768]{1,0:T(8,128)(2,1)S(1)}, u32[]{:S(2)}, u32[]{:S(2)}) collective-permute-start(bf16[192,768]{1,0:T(8,128)(2,1)S(1)} %get-tuple-element.44), channel_id=1, source_target_pairs={{2,0},{0,2},{3,1},{1,3},{6,4},{4,6},{7,5},{5,7},{10,8},{8,10},{11,... | collective-permute-start | bytes 884744 | tf_op jit(solution)/shard_map/ppermute | solution.py:268
  15.2 13.0 %collective-permute-start.3 = (bf16[384,512]{1,0:T(8,128)(2,1)S(1)}, bf16[384,512]{1,0:T(8,128)(2,1)S(1)}, u32[]{:S(2)}, u32[]{:S(2)}) collective-permute-start(bf16[384,512]{1,0:T(8,128)(2,1)S(1)} %get-tuple-element.49.refs_0_), channel_id=1, source_target_pairs={{4,0},{0,4},{12,8},{8,12},{5,1},{1,5},{13,9},{9,13},{6,2},{2,6},{1... | collective-permute-start | bytes 1179656 | tf_op jit(solution)/shard_map/ppermute | solution.py:276
  19.6 4.4 %collective-permute-start.5 = (bf16[192,768]{1,0:T(8,128)(2,1)S(1)}, bf16[192,768]{1,0:T(8,128)(2,1)S(1)}, u32[]{:S(2)}, u32[]{:S(2)}) collective-permute-start(bf16[192,768]{1,0:T(8,128)(2,1)S(1)} %collective-permute-done.4.refs_0_), channel_id=1, source_target_pairs={{1,0},{0,1},{3,2},{2,3},{5,4},{4,5},{7,6},{6,7},{9,8},{8,9},{11,10... | collective-permute-start | bytes 884744 | tf_op jit(solution)/shard_map/ppermute | solution.py:282
  21.7 11.4 %collective-permute-start.9 = (bf16[384,512]{1,0:T(8,128)(2,1)S(1)}, bf16[384,512]{1,0:T(8,128)(2,1)S(1)}, u32[]{:S(2)}, u32[]{:S(2)}) collective-permute-start(bf16[384,512]{1,0:T(8,128)(2,1)S(1)} %project.2), channel_id=1, source_target_pairs={{0,0},{1,8},{4,1},{5,9},{8,4},{9,12},{12,5},{13,13},{2,2},{3,10},{... | collective-permute-start | bytes 1179656 | tf_op jit(solution)/shard_map/ppermute | solution.py:322
  28.2 5.7 %collective-permute-start.6 = (bf16[384,512]{1,0:T(8,128)(2,1)S(1)}, bf16[384,512]{1,0:T(8,128)(2,1)S(1)}, u32[]{:S(2)}, u32[]{:S(2)}) collective-permute-start(bf16[384,512]{1,0:T(8,128)(2,1)S(1)} %get-tuple-element.49.refs_0_), channel_id=1, source_target_pairs={{1,0},{0,1},{3,2},{2,3},{5,4},{4,5},{7,6},{6,7},{9,8},{8,9},{11,10... | collective-permute-start | bytes 1179656 | tf_op jit(solution)/shard_map/ppermute | solution.py:282
  28.7 5.2 %collective-permute-start.7 = (bf16[384,512]{1,0:T(8,128)(2,1)S(1)}, bf16[384,512]{1,0:T(8,128)(2,1)S(1)}, u32[]{:S(2)}, u32[]{:S(2)}) collective-permute-start(bf16[384,512]{1,0:T(8,128)(2,1)S(1)} %collective-permute-done.3.refs_1_), channel_id=1, source_target_pairs={{1,0},{0,1},{3,2},{2,3},{5,4},{4,5},{7,6},{6,7},{9,8},{8,9},{11,10... | collective-permute-start | bytes 1179656 | tf_op jit(solution)/shard_map/ppermute | solution.py:282
  33.1 11.5 %collective-permute-start.10 = (bf16[384,512]{1,0:T(8,128)(2,1)S(1)}, bf16[384,512]{1,0:T(8,128)(2,1)S(1)}, u32[]{:S(2)}, u32[]{:S(2)}) collective-permute-start(bf16[384,512]{1,0:T(8,128)(2,1)S(1)} %collective-permute-done.9.refs_0_), channel_id=1, source_target_pairs={{4,0},{0,4},{12,8},{8,12},{5,1},{1,5},{13,9},{9,13},{6,2},{2,6},{1... | collective-permute-start | bytes 1179656 | tf_op jit(solution)/shard_map/ppermute | solution.py:276
  36.5 8.1 %collective-permute-start.8 = (bf16[384,256]{1,0:T(8,128)(2,1)S(1)}, bf16[384,256]{1,0:T(8,128)(2,1)S(1)}, u32[]{:S(2)}, u32[]{:S(2)}) collective-permute-start(bf16[384,256]{1,0:T(8,128)(2,1)S(1)} %end.1.refs_0_), channel_id=1, source_target_pairs={{2,0},{0,2},{3,1},{1,3},{6,4},{4,6},{7,5},{5,7},{10,8},{8,10},{11,... | collective-permute-start | bytes 589832 | tf_op jit(solution)/shard_map/ppermute | solution.py:268
  44.6 2.0 %collective-permute-start.11 = (bf16[384,512]{1,0:T(8,128)(2,1)S(1)}, bf16[384,512]{1,0:T(8,128)(2,1)S(1)}, u32[]{:S(2)}, u32[]{:S(2)}) collective-permute-start(bf16[384,512]{1,0:T(8,128)(2,1)S(1)} %collective-permute-done.9.refs_0_), channel_id=1, source_target_pairs={{1,0},{0,1},{3,2},{2,3},{5,4},{4,5},{7,6},{6,7},{9,8},{8,9},{11,10... | collective-permute-start | bytes 1179656 | tf_op jit(solution)/shard_map/ppermute | solution.py:282
  44.6 2.3 %collective-permute-start.12 = (bf16[384,512]{1,0:T(8,128)(2,1)S(1)}, bf16[384,512]{1,0:T(8,128)(2,1)S(1)}, u32[]{:S(2)}, u32[]{:S(2)}) collective-permute-start(bf16[384,512]{1,0:T(8,128)(2,1)S(1)} %collective-permute-done.10.refs_1_), channel_id=1, source_target_pairs={{1,0},{0,1},{3,2},{2,3},{5,4},{4,5},{7,6},{6,7},{9,8},{8,9},{11,10... | collective-permute-start | bytes 1179656 | tf_op jit(solution)/shard_map/ppermute | solution.py:282
  50.7 6.0 %collective-permute-start.13 = (bf16[3,96,256]{2,1,0:T(8,128)(2,1)S(1)}, bf16[3,96,256]{2,1,0:T(8,128)(2,1)S(1)}, u32[]{:S(2)}, u32[]{:S(2)}) collective-permute-start(bf16[3,96,256]{2,1,0:T(8,128)(2,1)S(1)} %get-tuple-element.64), channel_id=1, source_target_pairs={{2,0},{0,2},{3,1},{1,3},{6,4},{4,6},{7,5},{5,7},{10,8},{8,10},{11,... | collective-permute-start | bytes 442376 | tf_op jit(solution)/shard_map/ppermute | solution.py:268
  56.7 13.4 %collective-permute-start.14 = (bf16[3,96,256]{2,1,0:T(8,128)(2,1)S(1)}, bf16[3,96,256]{2,1,0:T(8,128)(2,1)S(1)}, u32[]{:S(2)}, u32[]{:S(2)}) collective-permute-start(bf16[3,96,256]{2,1,0:T(8,128)(2,1)S(1)} %add.1), channel_id=1, source_target_pairs={{0,0},{8,1},{1,4},{9,5},{4,8},{12,9},{5,12},{13,13},{2,2},{10,3},{... | collective-permute-start | bytes 442376 | tf_op jit(solution)/shard_map/ppermute | solution.py:381
  58.6 6.5 %collective-permute-start.16 = (bf16[1,96,256]{2,1,0:T(8,128)(2,1)S(1)}, bf16[1,96,256]{2,1,0:T(8,128)(2,1)S(1)}, u32[]{:S(2)}, u32[]{:S(2)}) collective-permute-start(bf16[1,96,256]{2,1,0:T(8,128)(2,1)S(1)} %get-tuple-element.69), channel_id=1, source_target_pairs={{1,0},{9,1},{4,4},{12,5},{5,8},{13,9},{3,2},{11,3},{6,6},{14,7},{7... | collective-permute-start | bytes 147464 | tf_op jit(solution)/shard_map/ppermute | solution.py:380
  63.2 6.9 %collective-permute-start.15 = (bf16[1,96,256]{2,1,0:T(8,128)(2,1)S(1)}, bf16[1,96,256]{2,1,0:T(8,128)(2,1)S(1)}, u32[]{:S(2)}, u32[]{:S(2)}) collective-permute-start(bf16[1,96,256]{2,1,0:T(8,128)(2,1)S(1)} %get-tuple-element.70), channel_id=1, source_target_pairs={{0,4},{8,5},{1,8},{9,9},{4,12},{12,13},{2,6},{10,7},{3,10},{11,11}... | collective-permute-start | bytes 147464 | tf_op jit(solution)/shard_map/ppermute | solution.py:379

commit v18 on v16

--- a/solution.py
+++ b/solution.py
@@ -339,12 +339,11 @@
     (composed,) = run_kernel(
         compose_kernel, "compose", [((columns, channels), BF16)], [cross_out, *map_weights]
     )
-    near, others, composed, map_weights = lax.optimization_barrier(
-        ([pack, *beside], others, composed, map_weights)
+    near, others, composed, map_weights, right_pack = lax.optimization_barrier(
+        ([pack, *beside], others, composed, map_weights, right_pack)
     )
     far = [q for p in near for q in across(p)]
     state = begin(query, near)
-    right_pack = tied(right_pack, state)
     right_near = [right_pack, *neighbours(right_pack)]
     (mixed,) = run_kernel(
         end_kernel, "end", [((rows, columns), BF16)], [query, *grouped(far), *state]

time: 70.4 us -> 72.7 us (1.033)
  waiting for transfers between devices: 19.9 us -> 25.9 us
  starting transfers between devices: 33.1 us -> 30 us
    ppermute x5, starting transfers between devices: 4.6 us -> 1.63 us  [across(): lax.ppermute(pack, 'pair', [((i + s) % cores, i) for i in range(cores)])]
    ppermute x2, waiting for transfers between devices: 5.36 us -> 8.12 us  [neighbours(): lax.ppermute(pack, 'blk', [(g + (i + s) % span, g + i) for g, i in ring])]
    ppermute x5, waiting for transfers between devices: 0.33 us -> 2.03 us  [across(): lax.ppermute(pack, 'pair', [((i + s) % cores, i) for i in range(cores)])]
    ppermute x1, starting transfers between devices: 5.47 us -> 4.1 us  [body(): right_pack = lax.ppermute(tied(right_pack, pack), both, there)]
    ppermute x2, waiting for transfers between devices: 3.31 us -> 4.53 us  [fetched(): return lax.ppermute(value, ('blk', 'tile', 'pair'), pairs)]
    ppermute x1, starting transfers between devices: 4.31 us -> 5.29 us  [body(): features = lax.ppermute(features, both, back)]
    ppermute x1, starting transfers between devices: 2.46 us -> 3.4 us  [body(): below = lax.ppermute(features[:1], both, up)]
  transfers between devices with their start and end apart: 17 -> 17, of which waited for: 9 -> 9; matrix products, arithmetic and copies ran while one was open for 0% -> 0% of each run, Pallas kernels for 17% -> 16%
where the time goes in v18:
time: 72.7 us; the launch traced here: 72.5 us
  starting transfers between devices  30 us (41%)
  waiting for transfers between devices  25.9 us (36%)
  Pallas kernels  16.4 us (23%)
    pallas_call x12, Pallas kernels, run_kernel(): pl.pallas_call(kernel, out_shape=[jax.ShapeDtypeStruct(*s) for s in shape...  16.4 us
    ppermute x2, waiting for transfers between devices, neighbours(): lax.ppermute(pack, 'blk', [(g + (i + s) % span, g + i) for g, i in ring])  8.12 us
    ppermute x2, starting transfers between devices, fetched(): return lax.ppermute(value, ('blk', 'tile', 'pair'), pairs)  6.13 us
    ppermute x1, starting transfers between devices, body(): features = lax.ppermute(features, both, back)  5.29 us
    ppermute x4, starting transfers between devices, from_tile(): lax.ppermute(value, 'tile', [((i + step) % tiles, i) for i in range(tiles)])  4.83 us
    ppermute x4, waiting for transfers between devices, from_tile(): lax.ppermute(value, 'tile', [((i + step) % tiles, i) for i in range(tiles)])  4.57 us
    ppermute x2, waiting for transfers between devices, fetched(): return lax.ppermute(value, ('blk', 'tile', 'pair'), pairs)  4.53 us
    ppermute x1, starting transfers between devices, body(): right_pack = lax.ppermute(tied(right_pack, pack), both, there)  4.1 us
  transfers between devices with their start and end apart: 17, of which 9 were waited for; matrix products, arithmetic and copies ran while one was open for 0% of the time, Pallas kernels for 16%

profile of v18, /device:TPU:1, one launch (start us, length us, event | category | flops | bytes accessed | tf_op | source)
XLA Modules:
  0.0 72.5 jit_solution(11965646619578282231)
XLA Ops:
  0.0 2.0 %collective-permute-start.2 = (bf16[384,384]{1,0:T(8,128)(2,1)}, bf16[384,384]{1,0:T(8,128)(2,1)S(1)}, u32[]{:S(2)}, u32[]{:S(2)}) collective-permute-start(bf16[384,384]{1,0:T(8,128)(2,1)} %bitcast.8), channel_id=1, source_target_pairs={{2,0},{0,2},{3,1},{1,3},{6,4},{4,6},{7,5},{5,7},{10,8},{8,10},{11,... | collective-permute-start | bytes 884744 | tf_op jit(solution)/shard_map/ppermute | solution.py:272
  2.0 6.1 %collective-permute-start = (bf16[384,384]{1,0:T(8,128)(2,1)}, bf16[384,384]{1,0:T(8,128)(2,1)S(1)}, u32[]{:S(2)}, u32[]{:S(2)}) collective-permute-start(bf16[384,384]{1,0:T(8,128)(2,1)} %bitcast.10), channel_id=1, source_target_pairs={{0,0},{2,2},{1,12},{3,14},{4,4},{6,6},{5,8},{7,10},{8,5},{10,7},{9... | collective-permute-start | bytes 884744 | tf_op jit(solution)/shard_map/ppermute | solution.py:266
  8.2 2.6 %stage.1 = (bf16[256,768]{1,0:T(8,128)(2,1)S(1)}, bf16[384,256]{1,0:T(8,128)(2,1)S(1)}, bf16[256,768]{1,0:T(8,128)(2,1)S(1)}, bf16[384,384]{1,0:T(8,128)(2,1)S(1...) custom-call(bf16[256,768]{1,0:T(8,128)(2,1)} %refs_0_.1, ...), custom_call_target="tpu_custom_call" | custom-call | tf_op jit(solution)/shard_map/stage/pallas_call | solution.py:22
  10.7 1.2 %collective-permute-start.4 = (bf16[192,768]{1,0:T(8,128)(2,1)S(1)}, bf16[192,768]{1,0:T(8,128)(2,1)S(1)}, u32[]{:S(2)}, u32[]{:S(2)}) collective-permute-start(bf16[192,768]{1,0:T(8,128)(2,1)S(1)} %get-tuple-element.44), channel_id=1, source_target_pairs={{2,0},{0,2},{3,1},{1,3},{6,4},{4,6},{7,5},{5,7},{10,8},{8,10},{11,... | collective-permute-start | bytes 884744 | tf_op jit(solution)/shard_map/ppermute | solution.py:272
  12.0 0.8 %project.2 = bf16[384,512]{1,0:T(8,128)(2,1)S(1)} custom-call(bf16[384,384]{1,0:T(8,128)(2,1)S(1)} %get-tuple-element.37.refs_0_, bf16[384,384]{1,0:T(8,128)(2,1)S(1)} %collective-permute-done.2.refs_1_, bf16[3,2,384,256]{3,2,1,0:T(8,128)(2,1)S(1)} %bitcast.5), custom_call_target="tpu_custom_call" | custom-call | tf_op jit(solution)/shard_map/project/pallas_call | solution.py:22
  12.9 4.5 %collective-permute-done.1.refs_1_.refs_5_ = bf16[384,384]{1,0:T(8,128)(2,1)S(1)} collective-permute-done((bf16[384,384]{1,0:T(8,128)(2,1)}, bf16[384,384]{1,0:T(8,128)(2,1)S(1)}, u32[]{:S(2)}, u32[]{:S(2)}) %collective-permute-start.1) | collective-permute-done | bytes 294944 | tf_op jit(solution)/shard_map/ppermute | solution.py:266
  17.4 1.1 %project.3 = (bf16[384,256]{1,0:T(8,128)(2,1)S(1)}, bf16[384,512]{1,0:T(8,128)(2,1)S(1)}) custom-call(bf16[384,384]{1,0:T(8,128)(2,1)S(1)} %collective-permute-done.refs_0_.refs_4_, bf16[384,384]{1,0:T(8,128)(2,1)S(1)} %collective-permute-done.1.refs_1_.refs_5_, bf16[3,2,384,256]{3,2,1,0:T(8,128)(2,1)S(1)} %bitcast.7), custom_call_target="tpu_custom_call" | custom-call | tf_op jit(solution)/shard_map/project/pallas_call | solution.py:22
  18.5 4.1 %collective-permute-start.6 = (bf16[384,512]{1,0:T(8,128)(2,1)S(1)}, bf16[384,512]{1,0:T(8,128)(2,1)S(1)}, u32[]{:S(2)}, u32[]{:S(2)}) collective-permute-start(bf16[384,512]{1,0:T(8,128)(2,1)S(1)} %project.2), channel_id=1, source_target_pairs={{0,0},{1,12},{4,4},{5,8},{8,5},{9,9},{12,1},{13,13},{2,2},{3,14},{... | collective-permute-start | bytes 1179656 | tf_op jit(solution)/shard_map/ppermute | solution.py:326
  22.6 3.8 %collective-permute-start.3 = (bf16[384,512]{1,0:T(8,128)(2,1)S(1)}, bf16[384,512]{1,0:T(8,128)(2,1)S(1)}, u32[]{:S(2)}, u32[]{:S(2)}) collective-permute-start(bf16[384,512]{1,0:T(8,128)(2,1)S(1)} %get-tuple-element.51.refs_0_), channel_id=1, source_target_pairs={{4,0},{0,4},{12,8},{8,12},{5,1},{1,5},{13,9},{9,13},{6,2},{2,6},{1... | collective-permute-start | bytes 1179656 | tf_op jit(solution)/shard_map/ppermute | solution.py:280
  26.3 1.6 %collective-permute-done.5.refs_1_ = bf16[192,768]{1,0:T(8,128)(2,1)S(1)} collective-permute-done((bf16[192,768]{1,0:T(8,128)(2,1)S(1)}, bf16[192,768]{1,0:T(8,128)(2,1)S(1)}, u32[]{:S(2)}, u32[]{:S(2)}) %collective-permute-start.5) | collective-permute-done | bytes 294944 | tf_op jit(solution)/shard_map/ppermute | solution.py:286
  28.3 3.1 %collective-permute-done.6.refs_0_ = bf16[384,512]{1,0:T(8,128)(2,1)S(1)} collective-permute-done((bf16[384,512]{1,0:T(8,128)(2,1)S(1)}, bf16[384,512]{1,0:T(8,128)(2,1)S(1)}, u32[]{:S(2)}, u32[]{:S(2)}) %collective-permute-start.6) | collective-permute-done | bytes 393248 | tf_op jit(solution)/shard_map/ppermute | solution.py:326
  31.4 3.2 %collective-permute-done.3.refs_1_ = bf16[384,512]{1,0:T(8,128)(2,1)S(1)} collective-permute-done((bf16[384,512]{1,0:T(8,128)(2,1)S(1)}, bf16[384,512]{1,0:T(8,128)(2,1)S(1)}, u32[]{:S(2)}, u32[]{:S(2)}) %collective-permute-start.3) | collective-permute-done | bytes 393248 | tf_op jit(solution)/shard_map/ppermute | solution.py:280
  35.4 2.2 %begin.1 = (f32[4,384,128]{2,1,0:T(8,128)S(1)}, f32[4,384,1]{2,1,0:T(8,128)S(1)}) custom-call(bf16[384,256]{1,0:T(8,128)(2,1)S(1)} %get-tuple-element.42.query, bf16[384,512]{1,0:T(8,128)(2,1)S(1)} %get-tuple-element.51.refs_0_, bf16[384,512]{1,0:T(8,128)(2,1)S(1)} %collective-permute-done.3.refs_1_), custom_call_target="tpu_custom_call" | custom-call | tf_op jit(solution)/shard_map/begin/pallas_call | solution.py:22
  37.7 2.6 %end.1.refs_0_ = bf16[384,256]{1,0:T(8,128)(2,1)S(1)} custom-call(bf16[384,256]{1,0:T(8,128)(2,1)S(1)} %get-tuple-element.42.query, bf16[384,512]{1,0:T(8,128)(2,1)S(1)} %collective-permute-done.7.refs_0_, bf16[384,512]{1,0:T(8,128)(2,1)S(1)} %collective-permute-done.8.refs_1_, f32[4,384,128]{2,1,0:T(8,128)S(1)} %get-tuple-element.53.refs_2_, ...), custom_call_target="tpu_custom_call" | custom-call | tf_op jit(solution)/shard_map/end/pallas_call | solution.py:22
  41.1 4.9 %collective-permute-done.10.refs_1_ = bf16[384,512]{1,0:T(8,128)(2,1)S(1)} collective-permute-done((bf16[384,512]{1,0:T(8,128)(2,1)S(1)}, bf16[384,512]{1,0:T(8,128)(2,1)S(1)}, u32[]{:S(2)}, u32[]{:S(2)}) %collective-permute-start.10) | collective-permute-done | bytes 393248 | tf_op jit(solution)/shard_map/ppermute | solution.py:280
  46.6 1.1 %collective-permute-start.11 = (bf16[384,512]{1,0:T(8,128)(2,1)S(1)}, bf16[384,512]{1,0:T(8,128)(2,1)S(1)}, u32[]{:S(2)}, u32[]{:S(2)}) collective-permute-start(bf16[384,512]{1,0:T(8,128)(2,1)S(1)} %collective-permute-done.6.refs_0_), channel_id=1, source_target_pairs={{1,0},{0,1},{3,2},{2,3},{5,4},{4,5},{7,6},{6,7},{9,8},{8,9},{11,10... | collective-permute-start | bytes 1179656 | tf_op jit(solution)/shard_map/ppermute | solution.py:286
  47.7 1.5 %update.1 = (bf16[2,384,384]{2,1,0:T(8,128)(2,1)S(1)}, bf16[384,256]{1,0:T(8,128)(2,1)S(1)}) custom-call(bf16[384,256]{1,0:T(8,128)(2,1)S(1)} %end.1.refs_0_, bf16[384,256]{1,0:T(8,128)(2,1)S(1)} %collective-permute-done.9.refs_1_, bf16[256,768]{1,0:T(8,128)(2,1)S(1)} %get-tuple-element.55.refs_2_, bf16[256,768]{1,0:T(8,128)(2,1)S(1)} %get-tuple-element.56.refs_3_, ...), custom_call_target="tpu_custom_call" | custom-call | tf_op jit(solution)/shard_map/update/pallas_call | solution.py:22
  49.6 3.8 %end_map.1 = (bf16[3,96,256]{2,1,0:T(8,128)(2,1)S(1)}, bf16[3,96,256]{2,1,0:T(8,128)(2,1)S(1)}) custom-call(bf16[384,256]{1,0:T(8,128)(2,1)S(1)} %get-tuple-element.58.query, bf16[384,512]{1,0:T(8,128)(2,1)S(1)} %collective-permute-done.6.refs_0_, bf16[384,512]{1,0:T(8,128)(2,1)S(1)} %collective-permute-done.10.refs_1_, ...), custom_call_target="tpu_custom_call" | custom-call | tf_op jit(solution)/shard_map/end_map/pallas_call | solution.py:22
  53.4 0.8 %collective-permute-start.13 = (bf16[3,96,256]{2,1,0:T(8,128)(2,1)S(1)}, bf16[3,96,256]{2,1,0:T(8,128)(2,1)S(1)}, u32[]{:S(2)}, u32[]{:S(2)}) collective-permute-start(bf16[3,96,256]{2,1,0:T(8,128)(2,1)S(1)} %get-tuple-element.64), channel_id=1, source_target_pairs={{2,0},{0,2},{3,1},{1,3},{6,4},{4,6},{7,5},{5,7},{10,8},{8,10},{11,... | collective-permute-start | bytes 442376 | tf_op jit(solution)/shard_map/ppermute | solution.py:272
  54.6 3.9 %collective-permute-done.13.refs_2_ = bf16[3,96,256]{2,1,0:T(8,128)(2,1)S(1)} collective-permute-done((bf16[3,96,256]{2,1,0:T(8,128)(2,1)S(1)}, bf16[3,96,256]{2,1,0:T(8,128)(2,1)S(1)}, u32[]{:S(2)}, u32[]{:S(2)}) %collective-permute-start.13) | collective-permute-done | bytes 147488 | tf_op jit(solution)/shard_map/ppermute | solution.py:272
  58.6 5.3 %collective-permute-start.14 = (bf16[3,96,256]{2,1,0:T(8,128)(2,1)S(1)}, bf16[3,96,256]{2,1,0:T(8,128)(2,1)S(1)}, u32[]{:S(2)}, u32[]{:S(2)}) collective-permute-start(bf16[3,96,256]{2,1,0:T(8,128)(2,1)S(1)} %add.1), channel_id=1, source_target_pairs={{0,0},{12,1},{4,4},{8,5},{5,8},{9,9},{1,12},{13,13},{2,2},{14,3},{... | collective-permute-start | bytes 442376 | tf_op jit(solution)/shard_map/ppermute | solution.py:384
  64.5 3.4 %collective-permute-start.16 = (bf16[1,96,256]{2,1,0:T(8,128)(2,1)S(1)}, bf16[1,96,256]{2,1,0:T(8,128)(2,1)S(1)}, u32[]{:S(2)}, u32[]{:S(2)}) collective-permute-start(bf16[1,96,256]{2,1,0:T(8,128)(2,1)S(1)} %get-tuple-element.69), channel_id=1, source_target_pairs={{4,0},{8,1},{5,4},{9,5},{1,8},{13,9},{6,2},{10,3},{7,6},{11,7},{3,... | collective-permute-start | bytes 147464 | tf_op jit(solution)/shard_map/ppermute | solution.py:383
  68.0 3.5 %collective-permute-done.16.below = bf16[1,96,256]{2,1,0:T(8,128)(2,1)S(1)} collective-permute-done((bf16[1,96,256]{2,1,0:T(8,128)(2,1)S(1)}, bf16[1,96,256]{2,1,0:T(8,128)(2,1)S(1)}, u32[]{:S(2)}, u32[]{:S(2)}) %collective-permute-start.16) | collective-permute-done | bytes 49184 | tf_op jit(solution)/shard_map/ppermute | solution.py:383
  71.5 1.0 %join.1 = bf16[3,64,256]{2,1,0:T(8,128)(2,1)} custom-call(bf16[3,96,256]{2,1,0:T(8,128)(2,1)S(1)} %collective-permute-done.14.window, bf16[1,96,256]{2,1,0:T(8,128)(2,1)S(1)} %collective-permute-done.15.above, bf16[1,96,256]{2,1,0:T(8,128)(2,1)S(1)} %collective-permute-done.16.below, bf16[3,3,256,256]{3,2,1,0:T(8,128)(2,1)S(1)} %get-tuple-element.68.weight), custom_call_target="tpu_custom_call" | custom-call | tf_op jit(solution)/shard_map/join/pallas_call | solution.py:22
  (23 shorter events, 4.2 us)
Async XLA Ops:
  0.0 12.0 %collective-permute-start.2 = (bf16[384,384]{1,0:T(8,128)(2,1)}, bf16[384,384]{1,0:T(8,128)(2,1)S(1)}, u32[]{:S(2)}, u32[]{:S(2)}) collective-permute-start(bf16[384,384]{1,0:T(8,128)(2,1)} %bitcast.8), channel_id=1, source_target_pairs={{2,0},{0,2},{3,1},{1,3},{6,4},{4,6},{7,5},{5,7},{10,8},{8,10},{11,... | collective-permute-start | bytes 884744 | tf_op jit(solution)/shard_map/ppermute | solution.py:272
  2.0 10.8 %collective-permute-start = (bf16[384,384]{1,0:T(8,128)(2,1)}, bf16[384,384]{1,0:T(8,128)(2,1)S(1)}, u32[]{:S(2)}, u32[]{:S(2)}) collective-permute-start(bf16[384,384]{1,0:T(8,128)(2,1)} %bitcast.10), channel_id=1, source_target_pairs={{0,0},{2,2},{1,12},{3,14},{4,4},{6,6},{5,8},{7,10},{8,5},{10,7},{9... | collective-permute-start | bytes 884744 | tf_op jit(solution)/shard_map/ppermute | solution.py:266
  8.1 9.3 %collective-permute-start.1 = (bf16[384,384]{1,0:T(8,128)(2,1)}, bf16[384,384]{1,0:T(8,128)(2,1)S(1)}, u32[]{:S(2)}, u32[]{:S(2)}) collective-permute-start(bf16[384,384]{1,0:T(8,128)(2,1)} %bitcast.11), channel_id=1, source_target_pairs={{2,0},{0,2},{3,12},{1,14},{6,4},{4,6},{7,8},{5,10},{10,5},{8,7},{1... | collective-permute-start | bytes 884744 | tf_op jit(solution)/shard_map/ppermute | solution.py:266
  10.7 15.6 %collective-permute-start.4 = (bf16[192,768]{1,0:T(8,128)(2,1)S(1)}, bf16[192,768]{1,0:T(8,128)(2,1)S(1)}, u32[]{:S(2)}, u32[]{:S(2)}) collective-permute-start(bf16[192,768]{1,0:T(8,128)(2,1)S(1)} %get-tuple-element.44), channel_id=1, source_target_pairs={{2,0},{0,2},{3,1},{1,3},{6,4},{4,6},{7,5},{5,7},{10,8},{8,10},{11,... | collective-permute-start | bytes 884744 | tf_op jit(solution)/shard_map/ppermute | solution.py:272
  18.5 13.0 %collective-permute-start.6 = (bf16[384,512]{1,0:T(8,128)(2,1)S(1)}, bf16[384,512]{1,0:T(8,128)(2,1)S(1)}, u32[]{:S(2)}, u32[]{:S(2)}) collective-permute-start(bf16[384,512]{1,0:T(8,128)(2,1)S(1)} %project.2), channel_id=1, source_target_pairs={{0,0},{1,12},{4,4},{5,8},{8,5},{9,9},{12,1},{13,13},{2,2},{3,14},{... | collective-permute-start | bytes 1179656 | tf_op jit(solution)/shard_map/ppermute | solution.py:326
  22.6 12.1 %collective-permute-start.3 = (bf16[384,512]{1,0:T(8,128)(2,1)S(1)}, bf16[384,512]{1,0:T(8,128)(2,1)S(1)}, u32[]{:S(2)}, u32[]{:S(2)}) collective-permute-start(bf16[384,512]{1,0:T(8,128)(2,1)S(1)} %get-tuple-element.51.refs_0_), channel_id=1, source_target_pairs={{4,0},{0,4},{12,8},{8,12},{5,1},{1,5},{13,9},{9,13},{6,2},{2,6},{1... | collective-permute-start | bytes 1179656 | tf_op jit(solution)/shard_map/ppermute | solution.py:280
  26.3 1.6 %collective-permute-start.5 = (bf16[192,768]{1,0:T(8,128)(2,1)S(1)}, bf16[192,768]{1,0:T(8,128)(2,1)S(1)}, u32[]{:S(2)}, u32[]{:S(2)}) collective-permute-start(bf16[192,768]{1,0:T(8,128)(2,1)S(1)} %collective-permute-done.4.refs_0_), channel_id=1, source_target_pairs={{1,0},{0,1},{3,2},{2,3},{5,4},{4,5},{7,6},{6,7},{9,8},{8,9},{11,10... | collective-permute-start | bytes 884744 | tf_op jit(solution)/shard_map/ppermute | solution.py:286
  34.7 3.0 %collective-permute-start.7 = (bf16[384,512]{1,0:T(8,128)(2,1)S(1)}, bf16[384,512]{1,0:T(8,128)(2,1)S(1)}, u32[]{:S(2)}, u32[]{:S(2)}) collective-permute-start(bf16[384,512]{1,0:T(8,128)(2,1)S(1)} %get-tuple-element.51.refs_0_), channel_id=1, source_target_pairs={{1,0},{0,1},{3,2},{2,3},{5,4},{4,5},{7,6},{6,7},{9,8},{8,9},{11,10... | collective-permute-start | bytes 1179656 | tf_op jit(solution)/shard_map/ppermute | solution.py:286
  34.7 3.0 %collective-permute-start.8 = (bf16[384,512]{1,0:T(8,128)(2,1)S(1)}, bf16[384,512]{1,0:T(8,128)(2,1)S(1)}, u32[]{:S(2)}, u32[]{:S(2)}) collective-permute-start(bf16[384,512]{1,0:T(8,128)(2,1)S(1)} %collective-permute-done.3.refs_1_), channel_id=1, source_target_pairs={{1,0},{0,1},{3,2},{2,3},{5,4},{4,5},{7,6},{6,7},{9,8},{8,9},{11,10... | collective-permute-start | bytes 1179656 | tf_op jit(solution)/shard_map/ppermute | solution.py:286
  35.2 10.7 %collective-permute-start.10 = (bf16[384,512]{1,0:T(8,128)(2,1)S(1)}, bf16[384,512]{1,0:T(8,128)(2,1)S(1)}, u32[]{:S(2)}, u32[]{:S(2)}) collective-permute-start(bf16[384,512]{1,0:T(8,128)(2,1)S(1)} %collective-permute-done.6.refs_0_), channel_id=1, source_target_pairs={{4,0},{0,4},{12,8},{8,12},{5,1},{1,5},{13,9},{9,13},{6,2},{2,6},{1... | collective-permute-start | bytes 1179656 | tf_op jit(solution)/shard_map/ppermute | solution.py:280
  40.3 6.3 %collective-permute-start.9 = (bf16[384,256]{1,0:T(8,128)(2,1)S(1)}, bf16[384,256]{1,0:T(8,128)(2,1)S(1)}, u32[]{:S(2)}, u32[]{:S(2)}) collective-permute-start(bf16[384,256]{1,0:T(8,128)(2,1)S(1)} %end.1.refs_0_), channel_id=1, source_target_pairs={{2,0},{0,2},{3,1},{1,3},{6,4},{4,6},{7,5},{5,7},{10,8},{8,10},{11,... | collective-permute-start | bytes 589832 | tf_op jit(solution)/shard_map/ppermute | solution.py:272
  46.6 2.6 %collective-permute-start.11 = (bf16[384,512]{1,0:T(8,128)(2,1)S(1)}, bf16[384,512]{1,0:T(8,128)(2,1)S(1)}, u32[]{:S(2)}, u32[]{:S(2)}) collective-permute-start(bf16[384,512]{1,0:T(8,128)(2,1)S(1)} %collective-permute-done.6.refs_0_), channel_id=1, source_target_pairs={{1,0},{0,1},{3,2},{2,3},{5,4},{4,5},{7,6},{6,7},{9,8},{8,9},{11,10... | collective-permute-start | bytes 1179656 | tf_op jit(solution)/shard_map/ppermute | solution.py:286
  47.7 1.9 %collective-permute-start.12 = (bf16[384,512]{1,0:T(8,128)(2,1)S(1)}, bf16[384,512]{1,0:T(8,128)(2,1)S(1)}, u32[]{:S(2)}, u32[]{:S(2)}) collective-permute-start(bf16[384,512]{1,0:T(8,128)(2,1)S(1)} %collective-permute-done.10.refs_1_), channel_id=1, source_target_pairs={{1,0},{0,1},{3,2},{2,3},{5,4},{4,5},{7,6},{6,7},{9,8},{8,9},{11,10... | collective-permute-start | bytes 1179656 | tf_op jit(solution)/shard_map/ppermute | solution.py:286
  53.4 5.1 %collective-permute-start.13 = (bf16[3,96,256]{2,1,0:T(8,128)(2,1)S(1)}, bf16[3,96,256]{2,1,0:T(8,128)(2,1)S(1)}, u32[]{:S(2)}, u32[]{:S(2)}) collective-permute-start(bf16[3,96,256]{2,1,0:T(8,128)(2,1)S(1)} %get-tuple-element.64), channel_id=1, source_target_pairs={{2,0},{0,2},{3,1},{1,3},{6,4},{4,6},{7,5},{5,7},{10,8},{8,10},{11,... | collective-permute-start | bytes 442376 | tf_op jit(solution)/shard_map/ppermute | solution.py:272
  58.6 12.9 %collective-permute-start.14 = (bf16[3,96,256]{2,1,0:T(8,128)(2,1)S(1)}, bf16[3,96,256]{2,1,0:T(8,128)(2,1)S(1)}, u32[]{:S(2)}, u32[]{:S(2)}) collective-permute-start(bf16[3,96,256]{2,1,0:T(8,128)(2,1)S(1)} %add.1), channel_id=1, source_target_pairs={{0,0},{12,1},{4,4},{8,5},{5,8},{9,9},{1,12},{13,13},{2,2},{14,3},{... | collective-permute-start | bytes 442376 | tf_op jit(solution)/shard_map/ppermute | solution.py:384
  63.9 4.1 %collective-permute-start.15 = (bf16[1,96,256]{2,1,0:T(8,128)(2,1)S(1)}, bf16[1,96,256]{2,1,0:T(8,128)(2,1)S(1)}, u32[]{:S(2)}, u32[]{:S(2)}) collective-permute-start(bf16[1,96,256]{2,1,0:T(8,128)(2,1)S(1)} %get-tuple-element.70), channel_id=1, source_target_pairs={{0,4},{12,5},{4,8},{8,9},{5,12},{9,13},{2,6},{14,7},{6,10},{10,11}... | collective-permute-start | bytes 147464 | tf_op jit(solution)/shard_map/ppermute | solution.py:382
  64.5 6.9 %collective-permute-start.16 = (bf16[1,96,256]{2,1,0:T(8,128)(2,1)S(1)}, bf16[1,96,256]{2,1,0:T(8,128)(2,1)S(1)}, u32[]{:S(2)}, u32[]{:S(2)}) collective-permute-start(bf16[1,96,256]{2,1,0:T(8,128)(2,1)S(1)} %get-tuple-element.69), channel_id=1, source_target_pairs={{4,0},{8,1},{5,4},{9,5},{1,8},{13,9},{6,2},{10,3},{7,6},{11,7},{3,... | collective-permute-start | bytes 147464 | tf_op jit(solution)/shard_map/ppermute | solution.py:383

commit v19 on v18

--- a/solution.py
+++ b/solution.py
@@ -325,6 +325,7 @@
     query, pack = project(left, self_qkv, True, 0)
     right_pack = lax.ppermute(tied(right_pack, pack), both, there)
     beside = neighbours(pack)
+    near = [pack, *across(pack)]
     halves = tile_pieces(half)[1:]
     others = [
         run_kernel(
@@ -339,11 +340,12 @@
     (composed,) = run_kernel(
         compose_kernel, "compose", [((columns, channels), BF16)], [cross_out, *map_weights]
     )
-    near, others, composed, map_weights, right_pack = lax.optimization_barrier(
-        ([pack, *beside], others, composed, map_weights, right_pack)
-    )
-    far = [q for p in near for q in across(p)]
     state = begin(query, near)
+    beside, others, composed, map_weights, state = lax.optimization_barrier(
+        (beside, others, composed, map_weights, state)
+    )
+    far = [*beside, *[q for p in beside for q in across(p)]]
+    right_pack = tied(right_pack, beside)
     right_near = [right_pack, *neighbours(right_pack)]
     (mixed,) = run_kernel(
         end_kernel, "end", [((rows, columns), BF16)], [query, *grouped(far), *state]

time: 72.7 us -> 70.6 us (0.971)
  waiting for transfers between devices: 25.9 us -> 20.9 us
  starting transfers between devices: 30 us -> 32.2 us
    ppermute x2, waiting for transfers between devices: 8.12 us -> 4.43 us  [neighbours(): lax.ppermute(pack, 'blk', [(g + (i + s) % span, g + i) for g, i in ring])]
    ppermute x5, starting transfers between devices: 1.63 us -> 4.53 us  [across(): lax.ppermute(pack, 'pair', [((i + s) % cores, i) for i in range(cores)])]
    ppermute x1, waiting for transfers between devices: 3.14 us -> 5.8 us  [body(): right_pack = lax.ppermute(tied(right_pack, pack), both, there)]
    ppermute x2, starting transfers between devices: 4.01 us -> 2.1 us  [neighbours(): lax.ppermute(pack, 'blk', [(g + (i + s) % span, g + i) for g, i in ring])]
    ppermute x5, waiting for transfers between devices: 2.03 us -> 0.31 us  [across(): lax.ppermute(pack, 'pair', [((i + s) % cores, i) for i in range(cores)])]
    ppermute x1, starting transfers between devices: 4.1 us -> 5.36 us  [body(): right_pack = lax.ppermute(tied(right_pack, pack), both, there)]
    ppermute x2, waiting for transfers between devices: 4.53 us -> 3.31 us  [fetched(): return lax.ppermute(value, ('blk', 'tile', 'pair'), pairs)]
    ppermute x4, starting transfers between devices: 4.83 us -> 5.88 us  [from_tile(): lax.ppermute(value, 'tile', [((i + step) % tiles, i) for i in range(tiles)])]
  transfers between devices with their start and end apart: 17 -> 17, of which waited for: 9 -> 8; matrix products, arithmetic and copies ran while one was open for 0% -> 0% of each run, Pallas kernels for 16% -> 17%
where the time goes in v19:
time: 70.6 us; the launch traced here: 69.7 us
  starting transfers between devices  32.2 us (46%)
  waiting for transfers between devices  20.9 us (30%)
  Pallas kernels  16.4 us (23%)
    pallas_call x12, Pallas kernels, run_kernel(): pl.pallas_call(kernel, out_shape=[jax.ShapeDtypeStruct(*s) for s in shape...  16.4 us
    ppermute x2, starting transfers between devices, fetched(): return lax.ppermute(value, ('blk', 'tile', 'pair'), pairs)  6.06 us
    ppermute x4, starting transfers between devices, from_tile(): lax.ppermute(value, 'tile', [((i + step) % tiles, i) for i in range(tiles)])  5.88 us
    ppermute x1, waiting for transfers between devices, body(): right_pack = lax.ppermute(tied(right_pack, pack), both, there)  5.8 us
    ppermute x1, starting transfers between devices, body(): right_pack = lax.ppermute(tied(right_pack, pack), both, there)  5.36 us
    ppermute x1, starting transfers between devices, body(): features = lax.ppermute(features, both, back)  5.12 us
    ppermute x5, starting transfers between devices, across(): lax.ppermute(pack, 'pair', [((i + s) % cores, i) for i in range(cores)])  4.53 us
    ppermute x2, waiting for transfers between devices, neighbours(): lax.ppermute(pack, 'blk', [(g + (i + s) % span, g + i) for g, i in ring])  4.43 us
  transfers between devices with their start and end apart: 17, of which 8 were waited for; matrix products, arithmetic and copies ran while one was open for 0% of the time, Pallas kernels for 17%

profile of v19, /device:TPU:1, one launch (start us, length us, event | category | flops | bytes accessed | tf_op | source)
XLA Modules:
  0.0 69.7 jit_solution(7473489610525089579)
XLA Ops:
  0.0 2.0 %collective-permute-start.2 = (bf16[384,384]{1,0:T(8,128)(2,1)}, bf16[384,384]{1,0:T(8,128)(2,1)S(1)}, u32[]{:S(2)}, u32[]{:S(2)}) collective-permute-start(bf16[384,384]{1,0:T(8,128)(2,1)} %bitcast.8), channel_id=1, source_target_pairs={{2,0},{0,2},{3,1},{1,3},{6,4},{4,6},{7,5},{5,7},{10,8},{8,10},{11,... | collective-permute-start | bytes 884744 | tf_op jit(solution)/shard_map/ppermute | solution.py:272
  2.0 4.1 %collective-permute-start.1 = (bf16[384,384]{1,0:T(8,128)(2,1)}, bf16[384,384]{1,0:T(8,128)(2,1)S(1)}, u32[]{:S(2)}, u32[]{:S(2)}) collective-permute-start(bf16[384,384]{1,0:T(8,128)(2,1)} %bitcast.10), channel_id=1, source_target_pairs={{2,0},{0,2},{3,12},{1,14},{6,4},{4,6},{7,8},{5,10},{10,5},{8,7},{1... | collective-permute-start | bytes 884744 | tf_op jit(solution)/shard_map/ppermute | solution.py:266
  6.2 1.9 %collective-permute-start = (bf16[384,384]{1,0:T(8,128)(2,1)}, bf16[384,384]{1,0:T(8,128)(2,1)S(1)}, u32[]{:S(2)}, u32[]{:S(2)}) collective-permute-start(bf16[384,384]{1,0:T(8,128)(2,1)} %bitcast.11), channel_id=1, source_target_pairs={{0,0},{2,2},{1,12},{3,14},{4,4},{6,6},{5,8},{7,10},{8,5},{10,7},{9... | collective-permute-start | bytes 884744 | tf_op jit(solution)/shard_map/ppermute | solution.py:266
  8.1 2.6 %stage.1 = (bf16[256,768]{1,0:T(8,128)(2,1)S(1)}, bf16[384,256]{1,0:T(8,128)(2,1)S(1)}, bf16[256,768]{1,0:T(8,128)(2,1)S(1)}, bf16[384,384]{1,0:T(8,128)(2,1)S(1...) custom-call(bf16[256,768]{1,0:T(8,128)(2,1)} %refs_0_.1, ...), custom_call_target="tpu_custom_call" | custom-call | tf_op jit(solution)/shard_map/stage/pallas_call | solution.py:22
  10.7 1.3 %collective-permute-start.4 = (bf16[192,768]{1,0:T(8,128)(2,1)S(1)}, bf16[192,768]{1,0:T(8,128)(2,1)S(1)}, u32[]{:S(2)}, u32[]{:S(2)}) collective-permute-start(bf16[192,768]{1,0:T(8,128)(2,1)S(1)} %get-tuple-element.45), channel_id=1, source_target_pairs={{2,0},{0,2},{3,1},{1,3},{6,4},{4,6},{7,5},{5,7},{10,8},{8,10},{11,... | collective-permute-start | bytes 884744 | tf_op jit(solution)/shard_map/ppermute | solution.py:272
  13.0 3.3 %collective-permute-done.refs_0_.refs_4_ = bf16[384,384]{1,0:T(8,128)(2,1)S(1)} collective-permute-done((bf16[384,384]{1,0:T(8,128)(2,1)}, bf16[384,384]{1,0:T(8,128)(2,1)S(1)}, u32[]{:S(2)}, u32[]{:S(2)}) %collective-permute-start) | collective-permute-done | bytes 294944 | tf_op jit(solution)/shard_map/ppermute | solution.py:266
  16.3 1.1 %project.3 = (bf16[384,256]{1,0:T(8,128)(2,1)S(1)}, bf16[384,512]{1,0:T(8,128)(2,1)S(1)}) custom-call(bf16[384,384]{1,0:T(8,128)(2,1)S(1)} %collective-permute-done.refs_0_.refs_4_, bf16[384,384]{1,0:T(8,128)(2,1)S(1)} %collective-permute-done.1.refs_1_.refs_5_, bf16[3,2,384,256]{3,2,1,0:T(8,128)(2,1)S(1)} %bitcast.7), custom_call_target="tpu_custom_call" | custom-call | tf_op jit(solution)/shard_map/project/pallas_call | solution.py:22
  17.4 2.9 %collective-permute-start.6 = (bf16[384,512]{1,0:T(8,128)(2,1)S(1)}, bf16[384,512]{1,0:T(8,128)(2,1)S(1)}, u32[]{:S(2)}, u32[]{:S(2)}) collective-permute-start(bf16[384,512]{1,0:T(8,128)(2,1)S(1)} %get-tuple-element.44.refs_0_), channel_id=1, source_target_pairs={{1,0},{0,1},{3,2},{2,3},{5,4},{4,5},{7,6},{6,7},{9,8},{8,9},{11,10... | collective-permute-start | bytes 1179656 | tf_op jit(solution)/shard_map/ppermute | solution.py:286
  20.3 2.1 %collective-permute-start.3 = (bf16[384,512]{1,0:T(8,128)(2,1)S(1)}, bf16[384,512]{1,0:T(8,128)(2,1)S(1)}, u32[]{:S(2)}, u32[]{:S(2)}) collective-permute-start(bf16[384,512]{1,0:T(8,128)(2,1)S(1)} %get-tuple-element.44.refs_0_), channel_id=1, source_target_pairs={{4,0},{0,4},{12,8},{8,12},{5,1},{1,5},{13,9},{9,13},{6,2},{2,6},{1... | collective-permute-start | bytes 1179656 | tf_op jit(solution)/shard_map/ppermute | solution.py:280
  22.9 5.4 %collective-permute-start.9 = (bf16[384,512]{1,0:T(8,128)(2,1)S(1)}, bf16[384,512]{1,0:T(8,128)(2,1)S(1)}, u32[]{:S(2)}, u32[]{:S(2)}) collective-permute-start(bf16[384,512]{1,0:T(8,128)(2,1)S(1)} %project.2), channel_id=1, source_target_pairs={{0,0},{1,12},{4,4},{5,8},{8,5},{9,9},{12,1},{13,13},{2,2},{3,14},{... | collective-permute-start | bytes 1179656 | tf_op jit(solution)/shard_map/ppermute | solution.py:326
  28.6 2.2 %begin.1 = (f32[4,384,128]{2,1,0:T(8,128)S(1)}, f32[4,384,1]{2,1,0:T(8,128)S(1)}) custom-call(bf16[384,256]{1,0:T(8,128)(2,1)S(1)} %get-tuple-element.43.query, bf16[384,512]{1,0:T(8,128)(2,1)S(1)} %get-tuple-element.44.refs_0_, bf16[384,512]{1,0:T(8,128)(2,1)S(1)} %collective-permute-done.6.refs_1_), custom_call_target="tpu_custom_call" | custom-call | tf_op jit(solution)/shard_map/begin/pallas_call | solution.py:22
  30.9 0.9 %collective-permute-done.3.refs_0_ = bf16[384,512]{1,0:T(8,128)(2,1)S(1)} collective-permute-done((bf16[384,512]{1,0:T(8,128)(2,1)S(1)}, bf16[384,512]{1,0:T(8,128)(2,1)S(1)}, u32[]{:S(2)}, u32[]{:S(2)}) %collective-permute-start.3) | collective-permute-done | bytes 393248 | tf_op jit(solution)/shard_map/ppermute | solution.py:280
  32.4 5.8 %collective-permute-done.9.refs_0_ = bf16[384,512]{1,0:T(8,128)(2,1)S(1)} collective-permute-done((bf16[384,512]{1,0:T(8,128)(2,1)S(1)}, bf16[384,512]{1,0:T(8,128)(2,1)S(1)}, u32[]{:S(2)}, u32[]{:S(2)}) %collective-permute-start.9) | collective-permute-done | bytes 393248 | tf_op jit(solution)/shard_map/ppermute | solution.py:326
  38.3 2.6 %end.1.refs_0_ = bf16[384,256]{1,0:T(8,128)(2,1)S(1)} custom-call(bf16[384,256]{1,0:T(8,128)(2,1)S(1)} %get-tuple-element.43.query, bf16[384,512]{1,0:T(8,128)(2,1)S(1)} %collective-permute-done.3.refs_0_, bf16[384,512]{1,0:T(8,128)(2,1)S(1)} %collective-permute-done.7.refs_1_, f32[4,384,128]{2,1,0:T(8,128)S(1)} %get-tuple-element.53.refs_2_, ...), custom_call_target="tpu_custom_call" | custom-call | tf_op jit(solution)/shard_map/end/pallas_call | solution.py:22
  40.9 1.3 %collective-permute-start.8 = (bf16[384,256]{1,0:T(8,128)(2,1)S(1)}, bf16[384,256]{1,0:T(8,128)(2,1)S(1)}, u32[]{:S(2)}, u32[]{:S(2)}) collective-permute-start(bf16[384,256]{1,0:T(8,128)(2,1)S(1)} %end.1.refs_0_), channel_id=1, source_target_pairs={{2,0},{0,2},{3,1},{1,3},{6,4},{4,6},{7,5},{5,7},{10,8},{8,10},{11,... | collective-permute-start | bytes 589832 | tf_op jit(solution)/shard_map/ppermute | solution.py:272
  42.1 3.5 %collective-permute-done.10.refs_1_ = bf16[384,512]{1,0:T(8,128)(2,1)S(1)} collective-permute-done((bf16[384,512]{1,0:T(8,128)(2,1)S(1)}, bf16[384,512]{1,0:T(8,128)(2,1)S(1)}, u32[]{:S(2)}, u32[]{:S(2)}) %collective-permute-start.10) | collective-permute-done | bytes 393248 | tf_op jit(solution)/shard_map/ppermute | solution.py:280
  46.2 1.5 %update.1 = (bf16[2,384,384]{2,1,0:T(8,128)(2,1)S(1)}, bf16[384,256]{1,0:T(8,128)(2,1)S(1)}) custom-call(bf16[384,256]{1,0:T(8,128)(2,1)S(1)} %end.1.refs_0_, bf16[384,256]{1,0:T(8,128)(2,1)S(1)} %collective-permute-done.8.refs_1_, bf16[256,768]{1,0:T(8,128)(2,1)S(1)} %get-tuple-element.55.refs_2_, bf16[256,768]{1,0:T(8,128)(2,1)S(1)} %get-tuple-element.56.refs_3_, ...), custom_call_target="tpu_custom_call" | custom-call | tf_op jit(solution)/shard_map/update/pallas_call | solution.py:22
  47.9 3.8 %end_map.1 = (bf16[3,96,256]{2,1,0:T(8,128)(2,1)S(1)}, bf16[3,96,256]{2,1,0:T(8,128)(2,1)S(1)}) custom-call(bf16[384,256]{1,0:T(8,128)(2,1)S(1)} %get-tuple-element.58.query, bf16[384,512]{1,0:T(8,128)(2,1)S(1)} %collective-permute-done.9.refs_0_, bf16[384,512]{1,0:T(8,128)(2,1)S(1)} %collective-permute-done.10.refs_1_, ...), custom_call_target="tpu_custom_call" | custom-call | tf_op jit(solution)/shard_map/end_map/pallas_call | solution.py:22
  51.8 1.3 %collective-permute-start.13 = (bf16[3,96,256]{2,1,0:T(8,128)(2,1)S(1)}, bf16[3,96,256]{2,1,0:T(8,128)(2,1)S(1)}, u32[]{:S(2)}, u32[]{:S(2)}) collective-permute-start(bf16[3,96,256]{2,1,0:T(8,128)(2,1)S(1)} %get-tuple-element.66), channel_id=1, source_target_pairs={{2,0},{0,2},{3,1},{1,3},{6,4},{4,6},{7,5},{5,7},{10,8},{8,10},{11,... | collective-permute-start | bytes 442376 | tf_op jit(solution)/shard_map/ppermute | solution.py:272
  53.5 3.7 %collective-permute-done.13.refs_2_ = bf16[3,96,256]{2,1,0:T(8,128)(2,1)S(1)} collective-permute-done((bf16[3,96,256]{2,1,0:T(8,128)(2,1)S(1)}, bf16[3,96,256]{2,1,0:T(8,128)(2,1)S(1)}, u32[]{:S(2)}, u32[]{:S(2)}) %collective-permute-start.13) | collective-permute-done | bytes 147488 | tf_op jit(solution)/shard_map/ppermute | solution.py:272
  57.2 5.1 %collective-permute-start.14 = (bf16[3,96,256]{2,1,0:T(8,128)(2,1)S(1)}, bf16[3,96,256]{2,1,0:T(8,128)(2,1)S(1)}, u32[]{:S(2)}, u32[]{:S(2)}) collective-permute-start(bf16[3,96,256]{2,1,0:T(8,128)(2,1)S(1)} %add.1), channel_id=1, source_target_pairs={{0,0},{12,1},{4,4},{8,5},{5,8},{9,9},{1,12},{13,13},{2,2},{14,3},{... | collective-permute-start | bytes 442376 | tf_op jit(solution)/shard_map/ppermute | solution.py:386
  62.3 2.5 %collective-permute-start.16 = (bf16[1,96,256]{2,1,0:T(8,128)(2,1)S(1)}, bf16[1,96,256]{2,1,0:T(8,128)(2,1)S(1)}, u32[]{:S(2)}, u32[]{:S(2)}) collective-permute-start(bf16[1,96,256]{2,1,0:T(8,128)(2,1)S(1)} %get-tuple-element.71), channel_id=1, source_target_pairs={{4,0},{8,1},{5,4},{9,5},{1,8},{13,9},{6,2},{10,3},{7,6},{11,7},{3,... | collective-permute-start | bytes 147464 | tf_op jit(solution)/shard_map/ppermute | solution.py:385
  65.5 3.1 %collective-permute-done.16.below = bf16[1,96,256]{2,1,0:T(8,128)(2,1)S(1)} collective-permute-done((bf16[1,96,256]{2,1,0:T(8,128)(2,1)S(1)}, bf16[1,96,256]{2,1,0:T(8,128)(2,1)S(1)}, u32[]{:S(2)}, u32[]{:S(2)}) %collective-permute-start.16) | collective-permute-done | bytes 49184 | tf_op jit(solution)/shard_map/ppermute | solution.py:385
  68.7 1.0 %join.1 = bf16[3,64,256]{2,1,0:T(8,128)(2,1)} custom-call(bf16[3,96,256]{2,1,0:T(8,128)(2,1)S(1)} %collective-permute-done.14.window, bf16[1,96,256]{2,1,0:T(8,128)(2,1)S(1)} %collective-permute-done.15.above, bf16[1,96,256]{2,1,0:T(8,128)(2,1)S(1)} %collective-permute-done.16.below, bf16[3,3,256,256]{3,2,1,0:T(8,128)(2,1)S(1)} %get-tuple-element.70.weight), custom_call_target="tpu_custom_call" | custom-call | tf_op jit(solution)/shard_map/join/pallas_call | solution.py:22
  (23 shorter events, 4.5 us)
Async XLA Ops:
  0.0 12.1 %collective-permute-start.2 = (bf16[384,384]{1,0:T(8,128)(2,1)}, bf16[384,384]{1,0:T(8,128)(2,1)S(1)}, u32[]{:S(2)}, u32[]{:S(2)}) collective-permute-start(bf16[384,384]{1,0:T(8,128)(2,1)} %bitcast.8), channel_id=1, source_target_pairs={{2,0},{0,2},{3,1},{1,3},{6,4},{4,6},{7,5},{5,7},{10,8},{8,10},{11,... | collective-permute-start | bytes 884744 | tf_op jit(solution)/shard_map/ppermute | solution.py:272
  2.0 11.0 %collective-permute-start.1 = (bf16[384,384]{1,0:T(8,128)(2,1)}, bf16[384,384]{1,0:T(8,128)(2,1)S(1)}, u32[]{:S(2)}, u32[]{:S(2)}) collective-permute-start(bf16[384,384]{1,0:T(8,128)(2,1)} %bitcast.10), channel_id=1, source_target_pairs={{2,0},{0,2},{3,12},{1,14},{6,4},{4,6},{7,8},{5,10},{10,5},{8,7},{1... | collective-permute-start | bytes 884744 | tf_op jit(solution)/shard_map/ppermute | solution.py:266
  6.2 10.1 %collective-permute-start = (bf16[384,384]{1,0:T(8,128)(2,1)}, bf16[384,384]{1,0:T(8,128)(2,1)S(1)}, u32[]{:S(2)}, u32[]{:S(2)}) collective-permute-start(bf16[384,384]{1,0:T(8,128)(2,1)} %bitcast.11), channel_id=1, source_target_pairs={{0,0},{2,2},{1,12},{3,14},{4,4},{6,6},{5,8},{7,10},{8,5},{10,7},{9... | collective-permute-start | bytes 884744 | tf_op jit(solution)/shard_map/ppermute | solution.py:266
  10.7 11.7 %collective-permute-start.4 = (bf16[192,768]{1,0:T(8,128)(2,1)S(1)}, bf16[192,768]{1,0:T(8,128)(2,1)S(1)}, u32[]{:S(2)}, u32[]{:S(2)}) collective-permute-start(bf16[192,768]{1,0:T(8,128)(2,1)S(1)} %get-tuple-element.45), channel_id=1, source_target_pairs={{2,0},{0,2},{3,1},{1,3},{6,4},{4,6},{7,5},{5,7},{10,8},{8,10},{11,... | collective-permute-start | bytes 884744 | tf_op jit(solution)/shard_map/ppermute | solution.py:272
  17.4 11.2 %collective-permute-start.6 = (bf16[384,512]{1,0:T(8,128)(2,1)S(1)}, bf16[384,512]{1,0:T(8,128)(2,1)S(1)}, u32[]{:S(2)}, u32[]{:S(2)}) collective-permute-start(bf16[384,512]{1,0:T(8,128)(2,1)S(1)} %get-tuple-element.44.refs_0_), channel_id=1, source_target_pairs={{1,0},{0,1},{3,2},{2,3},{5,4},{4,5},{7,6},{6,7},{9,8},{8,9},{11,10... | collective-permute-start | bytes 1179656 | tf_op jit(solution)/shard_map/ppermute | solution.py:286
  20.3 11.5 %collective-permute-start.3 = (bf16[384,512]{1,0:T(8,128)(2,1)S(1)}, bf16[384,512]{1,0:T(8,128)(2,1)S(1)}, u32[]{:S(2)}, u32[]{:S(2)}) collective-permute-start(bf16[384,512]{1,0:T(8,128)(2,1)S(1)} %get-tuple-element.44.refs_0_), channel_id=1, source_target_pairs={{4,0},{0,4},{12,8},{8,12},{5,1},{1,5},{13,9},{9,13},{6,2},{2,6},{1... | collective-permute-start | bytes 1179656 | tf_op jit(solution)/shard_map/ppermute | solution.py:280
  22.4 5.8 %collective-permute-start.5 = (bf16[192,768]{1,0:T(8,128)(2,1)S(1)}, bf16[192,768]{1,0:T(8,128)(2,1)S(1)}, u32[]{:S(2)}, u32[]{:S(2)}) collective-permute-start(bf16[192,768]{1,0:T(8,128)(2,1)S(1)} %collective-permute-done.4.refs_0_), channel_id=1, source_target_pairs={{1,0},{0,1},{3,2},{2,3},{5,4},{4,5},{7,6},{6,7},{9,8},{8,9},{11,10... | collective-permute-start | bytes 884744 | tf_op jit(solution)/shard_map/ppermute | solution.py:286
  22.9 15.4 %collective-permute-start.9 = (bf16[384,512]{1,0:T(8,128)(2,1)S(1)}, bf16[384,512]{1,0:T(8,128)(2,1)S(1)}, u32[]{:S(2)}, u32[]{:S(2)}) collective-permute-start(bf16[384,512]{1,0:T(8,128)(2,1)S(1)} %project.2), channel_id=1, source_target_pairs={{0,0},{1,12},{4,4},{5,8},{8,5},{9,9},{12,1},{13,13},{2,2},{3,14},{... | collective-permute-start | bytes 1179656 | tf_op jit(solution)/shard_map/ppermute | solution.py:326
  31.8 6.5 %collective-permute-start.7 = (bf16[384,512]{1,0:T(8,128)(2,1)S(1)}, bf16[384,512]{1,0:T(8,128)(2,1)S(1)}, u32[]{:S(2)}, u32[]{:S(2)}) collective-permute-start(bf16[384,512]{1,0:T(8,128)(2,1)S(1)} %collective-permute-done.3.refs_0_), channel_id=1, source_target_pairs={{1,0},{0,1},{3,2},{2,3},{5,4},{4,5},{7,6},{6,7},{9,8},{8,9},{11,10... | collective-permute-start | bytes 1179656 | tf_op jit(solution)/shard_map/ppermute | solution.py:286
  38.2 7.4 %collective-permute-start.10 = (bf16[384,512]{1,0:T(8,128)(2,1)S(1)}, bf16[384,512]{1,0:T(8,128)(2,1)S(1)}, u32[]{:S(2)}, u32[]{:S(2)}) collective-permute-start(bf16[384,512]{1,0:T(8,128)(2,1)S(1)} %collective-permute-done.9.refs_0_), channel_id=1, source_target_pairs={{4,0},{0,4},{12,8},{8,12},{5,1},{1,5},{13,9},{9,13},{6,2},{2,6},{1... | collective-permute-start | bytes 1179656 | tf_op jit(solution)/shard_map/ppermute | solution.py:280
  40.9 4.8 %collective-permute-start.8 = (bf16[384,256]{1,0:T(8,128)(2,1)S(1)}, bf16[384,256]{1,0:T(8,128)(2,1)S(1)}, u32[]{:S(2)}, u32[]{:S(2)}) collective-permute-start(bf16[384,256]{1,0:T(8,128)(2,1)S(1)} %end.1.refs_0_), channel_id=1, source_target_pairs={{2,0},{0,2},{3,1},{1,3},{6,4},{4,6},{7,5},{5,7},{10,8},{8,10},{11,... | collective-permute-start | bytes 589832 | tf_op jit(solution)/shard_map/ppermute | solution.py:272
  45.7 2.0 %collective-permute-start.11 = (bf16[384,512]{1,0:T(8,128)(2,1)S(1)}, bf16[384,512]{1,0:T(8,128)(2,1)S(1)}, u32[]{:S(2)}, u32[]{:S(2)}) collective-permute-start(bf16[384,512]{1,0:T(8,128)(2,1)S(1)} %collective-permute-done.9.refs_0_), channel_id=1, source_target_pairs={{1,0},{0,1},{3,2},{2,3},{5,4},{4,5},{7,6},{6,7},{9,8},{8,9},{11,10... | collective-permute-start | bytes 1179656 | tf_op jit(solution)/shard_map/ppermute | solution.py:286
  45.7 2.3 %collective-permute-start.12 = (bf16[384,512]{1,0:T(8,128)(2,1)S(1)}, bf16[384,512]{1,0:T(8,128)(2,1)S(1)}, u32[]{:S(2)}, u32[]{:S(2)}) collective-permute-start(bf16[384,512]{1,0:T(8,128)(2,1)S(1)} %collective-permute-done.10.refs_1_), channel_id=1, source_target_pairs={{1,0},{0,1},{3,2},{2,3},{5,4},{4,5},{7,6},{6,7},{9,8},{8,9},{11,10... | collective-permute-start | bytes 1179656 | tf_op jit(solution)/shard_map/ppermute | solution.py:286
  51.8 5.4 %collective-permute-start.13 = (bf16[3,96,256]{2,1,0:T(8,128)(2,1)S(1)}, bf16[3,96,256]{2,1,0:T(8,128)(2,1)S(1)}, u32[]{:S(2)}, u32[]{:S(2)}) collective-permute-start(bf16[3,96,256]{2,1,0:T(8,128)(2,1)S(1)} %get-tuple-element.66), channel_id=1, source_target_pairs={{2,0},{0,2},{3,1},{1,3},{6,4},{4,6},{7,5},{5,7},{10,8},{8,10},{11,... | collective-permute-start | bytes 442376 | tf_op jit(solution)/shard_map/ppermute | solution.py:272
  57.2 11.5 %collective-permute-start.14 = (bf16[3,96,256]{2,1,0:T(8,128)(2,1)S(1)}, bf16[3,96,256]{2,1,0:T(8,128)(2,1)S(1)}, u32[]{:S(2)}, u32[]{:S(2)}) collective-permute-start(bf16[3,96,256]{2,1,0:T(8,128)(2,1)S(1)} %add.1), channel_id=1, source_target_pairs={{0,0},{12,1},{4,4},{8,5},{5,8},{9,9},{1,12},{13,13},{2,2},{14,3},{... | collective-permute-start | bytes 442376 | tf_op jit(solution)/shard_map/ppermute | solution.py:386
  62.3 6.3 %collective-permute-start.16 = (bf16[1,96,256]{2,1,0:T(8,128)(2,1)S(1)}, bf16[1,96,256]{2,1,0:T(8,128)(2,1)S(1)}, u32[]{:S(2)}, u32[]{:S(2)}) collective-permute-start(bf16[1,96,256]{2,1,0:T(8,128)(2,1)S(1)} %get-tuple-element.71), channel_id=1, source_target_pairs={{4,0},{8,1},{5,4},{9,5},{1,8},{13,9},{6,2},{10,3},{7,6},{11,7},{3,... | collective-permute-start | bytes 147464 | tf_op jit(solution)/shard_map/ppermute | solution.py:385
  64.8 3.8 %collective-permute-start.15 = (bf16[1,96,256]{2,1,0:T(8,128)(2,1)S(1)}, bf16[1,96,256]{2,1,0:T(8,128)(2,1)S(1)}, u32[]{:S(2)}, u32[]{:S(2)}) collective-permute-start(bf16[1,96,256]{2,1,0:T(8,128)(2,1)S(1)} %get-tuple-element.72), channel_id=1, source_target_pairs={{0,4},{12,5},{4,8},{8,9},{5,12},{9,13},{2,6},{14,7},{6,10},{10,11}... | collective-permute-start | bytes 147464 | tf_op jit(solution)/shard_map/ppermute | solution.py:384

commit v20 on v19

--- a/solution.py
+++ b/solution.py
@@ -10,7 +10,7 @@
 
 HD = 64
 GRID_W = 128
-EDGE = 16
+EDGE = 8
 F32 = jnp.float32
 BF16 = jnp.bfloat16
 QUERY_SCALE = math.log2(math.e) * HD**-0.5
@@ -118,7 +118,8 @@
 
 
 def window_of(board, slot, out):
-    start = pl.multiple_of(slot * (out.shape[1] - 2 * EDGE), EDGE)
+    width = out.shape[1] - 2 * EDGE
+    start = pl.multiple_of(slot * width, width)
     out[...] = board[:, pl.ds(start, out.shape[1]), :].astype(out.dtype)
 
 
@@ -319,11 +320,10 @@
     self_out, reassemble, cross_out, right_own, self_qkv, cross_qkv, taps, half = staged(
         [self_out, reassemble, cross_out, right_tokens[0], self_qkv, cross_qkv, taps]
     )
-    right = [right_own, *[from_tile(right_tokens[0], s) for s in steps]]
-    (right_pack,) = project(right, cross_qkv, False, 1)
-    left, right_pack = lax.optimization_barrier((left, right_pack))
+    right = [right_own, *[from_tile(tied(right_tokens[0], half), s) for s in steps]]
     query, pack = project(left, self_qkv, True, 0)
-    right_pack = lax.ppermute(tied(right_pack, pack), both, there)
+    (right_pack,) = project(tied(right, pack), cross_qkv, False, 1)
+    right_pack = lax.ppermute(right_pack, both, there)
     beside = neighbours(pack)
     near = [pack, *across(pack)]
     halves = tile_pieces(half)[1:]

time: 70.6 us -> 70.9 us (level)
  waiting for transfers between devices: 20.9 us -> 22.6 us
  starting transfers between devices: 32.2 us -> 31 us
    ppermute x2, starting transfers between devices: 2.1 us -> 5.92 us  [neighbours(): lax.ppermute(pack, 'blk', [(g + (i + s) % span, g + i) for g, i in ring])]
    ppermute x4, waiting for transfers between devices: 3.9 us -> 7.54 us  [from_tile(): lax.ppermute(value, 'tile', [((i + step) % tiles, i) for i in range(tiles)])]
    ppermute x5, starting transfers between devices: 4.53 us -> 1.36 us  [across(): lax.ppermute(pack, 'pair', [((i + s) % cores, i) for i in range(cores)])]
    ppermute x2, waiting for transfers between devices: 4.43 us -> 1.47 us  [neighbours(): lax.ppermute(pack, 'blk', [(g + (i + s) % span, g + i) for g, i in ring])]
    ppermute x4, starting transfers between devices: 5.88 us -> 3.71 us  [from_tile(): lax.ppermute(value, 'tile', [((i + step) % tiles, i) for i in range(tiles)])]
    ppermute x2, starting transfers between devices: 6.06 us -> 7.55 us  [fetched(): return lax.ppermute(value, ('blk', 'tile', 'pair'), pairs)]
    ppermute x2, waiting for transfers between devices: 3.31 us -> 4.11 us  [fetched(): return lax.ppermute(value, ('blk', 'tile', 'pair'), pairs)]
  transfers between devices with their start and end apart: 17 -> 17, of which waited for: 8 -> 8; matrix products, arithmetic and copies ran while one was open for 0% -> 0% of each run, Pallas kernels for 17% -> 16%
where the time goes in v20:
time: 70.9 us; the launch traced here: 70.2 us
  starting transfers between devices  31 us (44%)
  waiting for transfers between devices  22.6 us (32%)
  Pallas kernels  16.4 us (23%)
    pallas_call x12, Pallas kernels, run_kernel(): pl.pallas_call(kernel, out_shape=[jax.ShapeDtypeStruct(*s) for s in shape...  16.4 us
    ppermute x2, starting transfers between devices, fetched(): return lax.ppermute(value, ('blk', 'tile', 'pair'), pairs)  7.55 us
    ppermute x4, waiting for transfers between devices, from_tile(): lax.ppermute(value, 'tile', [((i + step) % tiles, i) for i in range(tiles)])  7.54 us
    ppermute x2, starting transfers between devices, neighbours(): lax.ppermute(pack, 'blk', [(g + (i + s) % span, g + i) for g, i in ring])  5.92 us
    ppermute x1, waiting for transfers between devices, body(): right_pack = lax.ppermute(right_pack, both, there)  5.53 us
    ppermute x1, starting transfers between devices, body(): right_pack = lax.ppermute(right_pack, both, there)  5.28 us
    ppermute x1, starting transfers between devices, body(): features = lax.ppermute(features, both, back)  4.57 us
    ppermute x2, waiting for transfers between devices, fetched(): return lax.ppermute(value, ('blk', 'tile', 'pair'), pairs)  4.11 us
  transfers between devices with their start and end apart: 17, of which 8 were waited for; matrix products, arithmetic and copies ran while one was open for 0% of the time, Pallas kernels for 16%

profile of v20, /device:TPU:1, one launch (start us, length us, event | category | flops | bytes accessed | tf_op | source)
XLA Modules:
  0.0 70.2 jit_solution(16061158108070481485)
XLA Ops:
  0.0 5.6 %collective-permute-start.1 = (bf16[384,384]{1,0:T(8,128)(2,1)}, bf16[384,384]{1,0:T(8,128)(2,1)S(1)}, u32[]{:S(2)}, u32[]{:S(2)}) collective-permute-start(bf16[384,384]{1,0:T(8,128)(2,1)} %bitcast.10), channel_id=1, source_target_pairs={{2,0},{0,2},{3,12},{1,14},{6,4},{4,6},{7,8},{5,10},{10,5},{8,7},{1... | collective-permute-start | bytes 884744 | tf_op jit(solution)/shard_map/ppermute | solution.py:267
  5.6 1.9 %collective-permute-start = (bf16[384,384]{1,0:T(8,128)(2,1)}, bf16[384,384]{1,0:T(8,128)(2,1)S(1)}, u32[]{:S(2)}, u32[]{:S(2)}) collective-permute-start(bf16[384,384]{1,0:T(8,128)(2,1)} %bitcast.11), channel_id=1, source_target_pairs={{0,0},{2,2},{1,12},{3,14},{4,4},{6,6},{5,8},{7,10},{8,5},{10,7},{9... | collective-permute-start | bytes 884744 | tf_op jit(solution)/shard_map/ppermute | solution.py:267
  7.6 2.6 %stage.1 = (bf16[256,768]{1,0:T(8,128)(2,1)S(1)}, bf16[384,256]{1,0:T(8,128)(2,1)S(1)}, bf16[256,768]{1,0:T(8,128)(2,1)S(1)}, bf16[384,384]{1,0:T(8,128)(2,1)S(1...) custom-call(bf16[256,768]{1,0:T(8,128)(2,1)} %refs_0_.1, ...), custom_call_target="tpu_custom_call" | custom-call | tf_op jit(solution)/shard_map/stage/pallas_call | solution.py:22
  10.5 1.2 %collective-permute-start.8 = (bf16[384,384]{1,0:T(8,128)(2,1)S(1)}, bf16[384,384]{1,0:T(8,128)(2,1)S(1)}, u32[]{:S(2)}, u32[]{:S(2)}) collective-permute-start(bf16[384,384]{1,0:T(8,128)(2,1)S(1)} %bitcast.9), channel_id=1, source_target_pairs={{2,0},{0,2},{3,1},{1,3},{6,4},{4,6},{7,5},{5,7},{10,8},{8,10},{11,... | collective-permute-start | bytes 884744 | tf_op jit(solution)/shard_map/ppermute | solution.py:273
  11.7 4.1 %collective-permute-done.refs_0_.refs_4_ = bf16[384,384]{1,0:T(8,128)(2,1)S(1)} collective-permute-done((bf16[384,384]{1,0:T(8,128)(2,1)}, bf16[384,384]{1,0:T(8,128)(2,1)S(1)}, u32[]{:S(2)}, u32[]{:S(2)}) %collective-permute-start) | collective-permute-done | bytes 294944 | tf_op jit(solution)/shard_map/ppermute | solution.py:267
  15.8 1.1 %project.2 = (bf16[384,256]{1,0:T(8,128)(2,1)S(1)}, bf16[384,512]{1,0:T(8,128)(2,1)S(1)}) custom-call(bf16[384,384]{1,0:T(8,128)(2,1)S(1)} %collective-permute-done.refs_0_.refs_4_, bf16[384,384]{1,0:T(8,128)(2,1)S(1)} %collective-permute-done.1.refs_1_.refs_5_, bf16[3,2,384,256]{3,2,1,0:T(8,128)(2,1)S(1)} %bitcast.7), custom_call_target="tpu_custom_call" | custom-call | tf_op jit(solution)/shard_map/project/pallas_call | solution.py:22
  16.9 3.5 %collective-permute-start.2 = (bf16[384,512]{1,0:T(8,128)(2,1)S(1)}, bf16[384,512]{1,0:T(8,128)(2,1)S(1)}, u32[]{:S(2)}, u32[]{:S(2)}) collective-permute-start(bf16[384,512]{1,0:T(8,128)(2,1)S(1)} %get-tuple-element.39.refs_0_), channel_id=1, source_target_pairs={{4,0},{0,4},{12,8},{8,12},{5,1},{1,5},{13,9},{9,13},{6,2},{2,6},{1... | collective-permute-start | bytes 1179656 | tf_op jit(solution)/shard_map/ppermute | solution.py:281
  21.2 2.2 %collective-permute-done.8.refs_1_ = bf16[384,384]{1,0:T(8,128)(2,1)S(1)} collective-permute-done((bf16[384,384]{1,0:T(8,128)(2,1)S(1)}, bf16[384,384]{1,0:T(8,128)(2,1)S(1)}, u32[]{:S(2)}, u32[]{:S(2)}) %collective-permute-start.8) | collective-permute-done | bytes 294944 | tf_op jit(solution)/shard_map/ppermute | solution.py:273
  24.2 5.3 %collective-permute-start.9 = (bf16[384,512]{1,0:T(8,128)(2,1)S(1)}, bf16[384,512]{1,0:T(8,128)(2,1)S(1)}, u32[]{:S(2)}, u32[]{:S(2)}) collective-permute-start(bf16[384,512]{1,0:T(8,128)(2,1)S(1)} %project.3), channel_id=1, source_target_pairs={{0,0},{1,12},{4,4},{5,8},{8,5},{9,9},{12,1},{13,13},{2,2},{3,14},{... | collective-permute-start | bytes 1179656 | tf_op jit(solution)/shard_map/ppermute | solution.py:326
  29.9 2.2 %begin.1 = (f32[4,384,128]{2,1,0:T(8,128)S(1)}, f32[4,384,1]{2,1,0:T(8,128)S(1)}) custom-call(bf16[384,256]{1,0:T(8,128)(2,1)S(1)} %get-tuple-element.38.query, bf16[384,512]{1,0:T(8,128)(2,1)S(1)} %get-tuple-element.39.refs_0_, bf16[384,512]{1,0:T(8,128)(2,1)S(1)} %collective-permute-done.5.refs_1_), custom_call_target="tpu_custom_call" | custom-call | tf_op jit(solution)/shard_map/begin/pallas_call | solution.py:22
  32.2 5.5 %collective-permute-done.9.refs_0_ = bf16[384,512]{1,0:T(8,128)(2,1)S(1)} collective-permute-done((bf16[384,512]{1,0:T(8,128)(2,1)S(1)}, bf16[384,512]{1,0:T(8,128)(2,1)S(1)}, u32[]{:S(2)}, u32[]{:S(2)}) %collective-permute-start.9) | collective-permute-done | bytes 393248 | tf_op jit(solution)/shard_map/ppermute | solution.py:326
  37.7 2.4 %collective-permute-start.10 = (bf16[384,512]{1,0:T(8,128)(2,1)S(1)}, bf16[384,512]{1,0:T(8,128)(2,1)S(1)}, u32[]{:S(2)}, u32[]{:S(2)}) collective-permute-start(bf16[384,512]{1,0:T(8,128)(2,1)S(1)} %collective-permute-done.9.refs_0_), channel_id=1, source_target_pairs={{4,0},{0,4},{12,8},{8,12},{5,1},{1,5},{13,9},{9,13},{6,2},{2,6},{1... | collective-permute-start | bytes 1179656 | tf_op jit(solution)/shard_map/ppermute | solution.py:281
  40.1 2.6 %end.1.refs_0_ = bf16[384,256]{1,0:T(8,128)(2,1)S(1)} custom-call(bf16[384,256]{1,0:T(8,128)(2,1)S(1)} %get-tuple-element.38.query, bf16[384,512]{1,0:T(8,128)(2,1)S(1)} %collective-permute-done.2.refs_0_, bf16[384,512]{1,0:T(8,128)(2,1)S(1)} %collective-permute-done.6.refs_1_, f32[4,384,128]{2,1,0:T(8,128)S(1)} %get-tuple-element.48.refs_2_, ...), custom_call_target="tpu_custom_call" | custom-call | tf_op jit(solution)/shard_map/end/pallas_call | solution.py:22
  42.7 1.1 %collective-permute-start.7 = (bf16[384,256]{1,0:T(8,128)(2,1)S(1)}, bf16[384,256]{1,0:T(8,128)(2,1)S(1)}, u32[]{:S(2)}, u32[]{:S(2)}) collective-permute-start(bf16[384,256]{1,0:T(8,128)(2,1)S(1)} %end.1.refs_0_), channel_id=1, source_target_pairs={{2,0},{0,2},{3,1},{1,3},{6,4},{4,6},{7,5},{5,7},{10,8},{8,10},{11,... | collective-permute-start | bytes 589832 | tf_op jit(solution)/shard_map/ppermute | solution.py:273
  43.8 1.5 %collective-permute-done.10.refs_1_ = bf16[384,512]{1,0:T(8,128)(2,1)S(1)} collective-permute-done((bf16[384,512]{1,0:T(8,128)(2,1)S(1)}, bf16[384,512]{1,0:T(8,128)(2,1)S(1)}, u32[]{:S(2)}, u32[]{:S(2)}) %collective-permute-start.10) | collective-permute-done | bytes 393248 | tf_op jit(solution)/shard_map/ppermute | solution.py:281
  45.3 2.0 %collective-permute-done.7.refs_1_ = bf16[384,256]{1,0:T(8,128)(2,1)S(1)} collective-permute-done((bf16[384,256]{1,0:T(8,128)(2,1)S(1)}, bf16[384,256]{1,0:T(8,128)(2,1)S(1)}, u32[]{:S(2)}, u32[]{:S(2)}) %collective-permute-start.7) | collective-permute-done | bytes 196640 | tf_op jit(solution)/shard_map/ppermute | solution.py:273
  47.8 1.5 %update.1 = (bf16[2,384,384]{2,1,0:T(8,128)(2,1)S(1)}, bf16[384,256]{1,0:T(8,128)(2,1)S(1)}) custom-call(bf16[384,256]{1,0:T(8,128)(2,1)S(1)} %end.1.refs_0_, bf16[384,256]{1,0:T(8,128)(2,1)S(1)} %collective-permute-done.7.refs_1_, bf16[256,768]{1,0:T(8,128)(2,1)S(1)} %get-tuple-element.50.refs_2_, bf16[256,768]{1,0:T(8,128)(2,1)S(1)} %get-tuple-element.51.refs_3_, ...), custom_call_target="tpu_custom_call" | custom-call | tf_op jit(solution)/shard_map/update/pallas_call | solution.py:22
  49.6 3.8 %end_map.1 = (bf16[3,80,256]{2,1,0:T(8,128)(2,1)S(1)}, bf16[3,80,256]{2,1,0:T(8,128)(2,1)S(1)}) custom-call(bf16[384,256]{1,0:T(8,128)(2,1)S(1)} %get-tuple-element.54.query, bf16[384,512]{1,0:T(8,128)(2,1)S(1)} %collective-permute-done.9.refs_0_, bf16[384,512]{1,0:T(8,128)(2,1)S(1)} %collective-permute-done.10.refs_1_, ...), custom_call_target="tpu_custom_call" | custom-call | tf_op jit(solution)/shard_map/end_map/pallas_call | solution.py:22
  53.4 1.1 %collective-permute-start.13 = (bf16[3,80,256]{2,1,0:T(8,128)(2,1)S(1)}, bf16[3,80,256]{2,1,0:T(8,128)(2,1)S(1)}, u32[]{:S(2)}, u32[]{:S(2)}) collective-permute-start(bf16[3,80,256]{2,1,0:T(8,128)(2,1)S(1)} %get-tuple-element.64), channel_id=1, source_target_pairs={{2,0},{0,2},{3,1},{1,3},{6,4},{4,6},{7,5},{5,7},{10,8},{8,10},{11,... | collective-permute-start | bytes 368648 | tf_op jit(solution)/shard_map/ppermute | solution.py:273
  54.9 3.4 %collective-permute-done.13.refs_2_ = bf16[3,80,256]{2,1,0:T(8,128)(2,1)S(1)} collective-permute-done((bf16[3,80,256]{2,1,0:T(8,128)(2,1)S(1)}, bf16[3,80,256]{2,1,0:T(8,128)(2,1)S(1)}, u32[]{:S(2)}, u32[]{:S(2)}) %collective-permute-start.13) | collective-permute-done | bytes 122912 | tf_op jit(solution)/shard_map/ppermute | solution.py:273
  58.3 4.6 %collective-permute-start.14 = (bf16[3,80,256]{2,1,0:T(8,128)(2,1)S(1)}, bf16[3,80,256]{2,1,0:T(8,128)(2,1)S(1)}, u32[]{:S(2)}, u32[]{:S(2)}) collective-permute-start(bf16[3,80,256]{2,1,0:T(8,128)(2,1)S(1)} %add.1), channel_id=1, source_target_pairs={{0,0},{12,1},{4,4},{8,5},{5,8},{9,9},{1,12},{13,13},{2,2},{14,3},{... | collective-permute-start | bytes 368648 | tf_op jit(solution)/shard_map/ppermute | solution.py:386
  62.9 1.9 %collective-permute-start.16 = (bf16[1,80,256]{2,1,0:T(8,128)(2,1)S(1)}, bf16[1,80,256]{2,1,0:T(8,128)(2,1)S(1)}, u32[]{:S(2)}, u32[]{:S(2)}) collective-permute-start(bf16[1,80,256]{2,1,0:T(8,128)(2,1)S(1)} %get-tuple-element.69), channel_id=1, source_target_pairs={{4,0},{8,1},{5,4},{9,5},{1,8},{13,9},{6,2},{10,3},{7,6},{11,7},{3,... | collective-permute-start | bytes 122888 | tf_op jit(solution)/shard_map/ppermute | solution.py:385
  65.5 3.6 %collective-permute-done.16.below = bf16[1,80,256]{2,1,0:T(8,128)(2,1)S(1)} collective-permute-done((bf16[1,80,256]{2,1,0:T(8,128)(2,1)S(1)}, bf16[1,80,256]{2,1,0:T(8,128)(2,1)S(1)}, u32[]{:S(2)}, u32[]{:S(2)}) %collective-permute-start.16) | collective-permute-done | bytes 40992 | tf_op jit(solution)/shard_map/ppermute | solution.py:385
  69.1 1.1 %join.1 = bf16[3,64,256]{2,1,0:T(8,128)(2,1)} custom-call(bf16[3,80,256]{2,1,0:T(8,128)(2,1)S(1)} %collective-permute-done.14.window, bf16[1,80,256]{2,1,0:T(8,128)(2,1)S(1)} %collective-permute-done.15.above, bf16[1,80,256]{2,1,0:T(8,128)(2,1)S(1)} %collective-permute-done.16.below, bf16[3,3,256,256]{3,2,1,0:T(8,128)(2,1)S(1)} %get-tuple-element.68.weight), custom_call_target="tpu_custom_call" | custom-call | tf_op jit(solution)/shard_map/join/pallas_call | solution.py:22
  (25 shorter events, 4.3 us)
Async XLA Ops:
  0.0 11.7 %collective-permute-start.1 = (bf16[384,384]{1,0:T(8,128)(2,1)}, bf16[384,384]{1,0:T(8,128)(2,1)S(1)}, u32[]{:S(2)}, u32[]{:S(2)}) collective-permute-start(bf16[384,384]{1,0:T(8,128)(2,1)} %bitcast.10), channel_id=1, source_target_pairs={{2,0},{0,2},{3,12},{1,14},{6,4},{4,6},{7,8},{5,10},{10,5},{8,7},{1... | collective-permute-start | bytes 884744 | tf_op jit(solution)/shard_map/ppermute | solution.py:267
  5.6 10.1 %collective-permute-start = (bf16[384,384]{1,0:T(8,128)(2,1)}, bf16[384,384]{1,0:T(8,128)(2,1)S(1)}, u32[]{:S(2)}, u32[]{:S(2)}) collective-permute-start(bf16[384,384]{1,0:T(8,128)(2,1)} %bitcast.11), channel_id=1, source_target_pairs={{0,0},{2,2},{1,12},{3,14},{4,4},{6,6},{5,8},{7,10},{8,5},{10,7},{9... | collective-permute-start | bytes 884744 | tf_op jit(solution)/shard_map/ppermute | solution.py:267
  7.6 2.9 %copy-start = (bf16[1,384,384]{2,1,0:T(8,128)(2,1)S(1)}, bf16[1,384,384]{2,1,0:T(8,128)(2,1)}, u32[]{:S(2)}) copy-start(bf16[1,384,384]{2,1,0:T(8,128)(2,1)} %param.9) | copy-start | bytes 884740
  10.1 10.3 %collective-permute-start.3 = (bf16[192,768]{1,0:T(8,128)(2,1)S(1)}, bf16[192,768]{1,0:T(8,128)(2,1)S(1)}, u32[]{:S(2)}, u32[]{:S(2)}) collective-permute-start(bf16[192,768]{1,0:T(8,128)(2,1)S(1)} %get-tuple-element.40), channel_id=1, source_target_pairs={{2,0},{0,2},{3,1},{1,3},{6,4},{4,6},{7,5},{5,7},{10,8},{8,10},{11,... | collective-permute-start | bytes 884744 | tf_op jit(solution)/shard_map/ppermute | solution.py:273
  10.5 12.8 %collective-permute-start.8 = (bf16[384,384]{1,0:T(8,128)(2,1)S(1)}, bf16[384,384]{1,0:T(8,128)(2,1)S(1)}, u32[]{:S(2)}, u32[]{:S(2)}) collective-permute-start(bf16[384,384]{1,0:T(8,128)(2,1)S(1)} %bitcast.9), channel_id=1, source_target_pairs={{2,0},{0,2},{3,1},{1,3},{6,4},{4,6},{7,5},{5,7},{10,8},{8,10},{11,... | collective-permute-start | bytes 884744 | tf_op jit(solution)/shard_map/ppermute | solution.py:273
  16.8 13.0 %collective-permute-start.5 = (bf16[384,512]{1,0:T(8,128)(2,1)S(1)}, bf16[384,512]{1,0:T(8,128)(2,1)S(1)}, u32[]{:S(2)}, u32[]{:S(2)}) collective-permute-start(bf16[384,512]{1,0:T(8,128)(2,1)S(1)} %get-tuple-element.39.refs_0_), channel_id=1, source_target_pairs={{1,0},{0,1},{3,2},{2,3},{5,4},{4,5},{7,6},{6,7},{9,8},{8,9},{11,10... | collective-permute-start | bytes 1179656 | tf_op jit(solution)/shard_map/ppermute | solution.py:287
  16.9 15.2 %collective-permute-start.2 = (bf16[384,512]{1,0:T(8,128)(2,1)S(1)}, bf16[384,512]{1,0:T(8,128)(2,1)S(1)}, u32[]{:S(2)}, u32[]{:S(2)}) collective-permute-start(bf16[384,512]{1,0:T(8,128)(2,1)S(1)} %get-tuple-element.39.refs_0_), channel_id=1, source_target_pairs={{4,0},{0,4},{12,8},{8,12},{5,1},{1,5},{13,9},{9,13},{6,2},{2,6},{1... | collective-permute-start | bytes 1179656 | tf_op jit(solution)/shard_map/ppermute | solution.py:281
  20.4 9.0 %collective-permute-start.4 = (bf16[192,768]{1,0:T(8,128)(2,1)S(1)}, bf16[192,768]{1,0:T(8,128)(2,1)S(1)}, u32[]{:S(2)}, u32[]{:S(2)}) collective-permute-start(bf16[192,768]{1,0:T(8,128)(2,1)S(1)} %collective-permute-done.3.refs_0_), channel_id=1, source_target_pairs={{1,0},{0,1},{3,2},{2,3},{5,4},{4,5},{7,6},{6,7},{9,8},{8,9},{11,10... | collective-permute-start | bytes 884744 | tf_op jit(solution)/shard_map/ppermute | solution.py:287
  24.2 13.5 %collective-permute-start.9 = (bf16[384,512]{1,0:T(8,128)(2,1)S(1)}, bf16[384,512]{1,0:T(8,128)(2,1)S(1)}, u32[]{:S(2)}, u32[]{:S(2)}) collective-permute-start(bf16[384,512]{1,0:T(8,128)(2,1)S(1)} %project.3), channel_id=1, source_target_pairs={{0,0},{1,12},{4,4},{5,8},{8,5},{9,9},{12,1},{13,13},{2,2},{3,14},{... | collective-permute-start | bytes 1179656 | tf_op jit(solution)/shard_map/ppermute | solution.py:326
  32.1 8.0 %collective-permute-start.6 = (bf16[384,512]{1,0:T(8,128)(2,1)S(1)}, bf16[384,512]{1,0:T(8,128)(2,1)S(1)}, u32[]{:S(2)}, u32[]{:S(2)}) collective-permute-start(bf16[384,512]{1,0:T(8,128)(2,1)S(1)} %collective-permute-done.2.refs_0_), channel_id=1, source_target_pairs={{1,0},{0,1},{3,2},{2,3},{5,4},{4,5},{7,6},{6,7},{9,8},{8,9},{11,10... | collective-permute-start | bytes 1179656 | tf_op jit(solution)/shard_map/ppermute | solution.py:287
  37.7 7.6 %collective-permute-start.10 = (bf16[384,512]{1,0:T(8,128)(2,1)S(1)}, bf16[384,512]{1,0:T(8,128)(2,1)S(1)}, u32[]{:S(2)}, u32[]{:S(2)}) collective-permute-start(bf16[384,512]{1,0:T(8,128)(2,1)S(1)} %collective-permute-done.9.refs_0_), channel_id=1, source_target_pairs={{4,0},{0,4},{12,8},{8,12},{5,1},{1,5},{13,9},{9,13},{6,2},{2,6},{1... | collective-permute-start | bytes 1179656 | tf_op jit(solution)/shard_map/ppermute | solution.py:281
  42.7 4.6 %collective-permute-start.7 = (bf16[384,256]{1,0:T(8,128)(2,1)S(1)}, bf16[384,256]{1,0:T(8,128)(2,1)S(1)}, u32[]{:S(2)}, u32[]{:S(2)}) collective-permute-start(bf16[384,256]{1,0:T(8,128)(2,1)S(1)} %end.1.refs_0_), channel_id=1, source_target_pairs={{2,0},{0,2},{3,1},{1,3},{6,4},{4,6},{7,5},{5,7},{10,8},{8,10},{11,... | collective-permute-start | bytes 589832 | tf_op jit(solution)/shard_map/ppermute | solution.py:273
  47.3 2.0 %collective-permute-start.11 = (bf16[384,512]{1,0:T(8,128)(2,1)S(1)}, bf16[384,512]{1,0:T(8,128)(2,1)S(1)}, u32[]{:S(2)}, u32[]{:S(2)}) collective-permute-start(bf16[384,512]{1,0:T(8,128)(2,1)S(1)} %collective-permute-done.9.refs_0_), channel_id=1, source_target_pairs={{1,0},{0,1},{3,2},{2,3},{5,4},{4,5},{7,6},{6,7},{9,8},{8,9},{11,10... | collective-permute-start | bytes 1179656 | tf_op jit(solution)/shard_map/ppermute | solution.py:287
  47.3 2.3 %collective-permute-start.12 = (bf16[384,512]{1,0:T(8,128)(2,1)S(1)}, bf16[384,512]{1,0:T(8,128)(2,1)S(1)}, u32[]{:S(2)}, u32[]{:S(2)}) collective-permute-start(bf16[384,512]{1,0:T(8,128)(2,1)S(1)} %collective-permute-done.10.refs_1_), channel_id=1, source_target_pairs={{1,0},{0,1},{3,2},{2,3},{5,4},{4,5},{7,6},{6,7},{9,8},{8,9},{11,10... | collective-permute-start | bytes 1179656 | tf_op jit(solution)/shard_map/ppermute | solution.py:287
  53.4 4.8 %collective-permute-start.13 = (bf16[3,80,256]{2,1,0:T(8,128)(2,1)S(1)}, bf16[3,80,256]{2,1,0:T(8,128)(2,1)S(1)}, u32[]{:S(2)}, u32[]{:S(2)}) collective-permute-start(bf16[3,80,256]{2,1,0:T(8,128)(2,1)S(1)} %get-tuple-element.64), channel_id=1, source_target_pairs={{2,0},{0,2},{3,1},{1,3},{6,4},{4,6},{7,5},{5,7},{10,8},{8,10},{11,... | collective-permute-start | bytes 368648 | tf_op jit(solution)/shard_map/ppermute | solution.py:273
  58.3 10.8 %collective-permute-start.14 = (bf16[3,80,256]{2,1,0:T(8,128)(2,1)S(1)}, bf16[3,80,256]{2,1,0:T(8,128)(2,1)S(1)}, u32[]{:S(2)}, u32[]{:S(2)}) collective-permute-start(bf16[3,80,256]{2,1,0:T(8,128)(2,1)S(1)} %add.1), channel_id=1, source_target_pairs={{0,0},{12,1},{4,4},{8,5},{5,8},{9,9},{1,12},{13,13},{2,2},{14,3},{... | collective-permute-start | bytes 368648 | tf_op jit(solution)/shard_map/ppermute | solution.py:386
  62.9 6.2 %collective-permute-start.16 = (bf16[1,80,256]{2,1,0:T(8,128)(2,1)S(1)}, bf16[1,80,256]{2,1,0:T(8,128)(2,1)S(1)}, u32[]{:S(2)}, u32[]{:S(2)}) collective-permute-start(bf16[1,80,256]{2,1,0:T(8,128)(2,1)S(1)} %get-tuple-element.69), channel_id=1, source_target_pairs={{4,0},{8,1},{5,4},{9,5},{1,8},{13,9},{6,2},{10,3},{7,6},{11,7},{3,... | collective-permute-start | bytes 122888 | tf_op jit(solution)/shard_map/ppermute | solution.py:385
  64.8 4.3 %collective-permute-start.15 = (bf16[1,80,256]{2,1,0:T(8,128)(2,1)S(1)}, bf16[1,80,256]{2,1,0:T(8,128)(2,1)S(1)}, u32[]{:S(2)}, u32[]{:S(2)}) collective-permute-start(bf16[1,80,256]{2,1,0:T(8,128)(2,1)S(1)} %get-tuple-element.70), channel_id=1, source_target_pairs={{0,4},{12,5},{4,8},{8,9},{5,12},{9,13},{2,6},{14,7},{6,10},{10,11}... | collective-permute-start | bytes 122888 | tf_op jit(solution)/shard_map/ppermute | solution.py:384

commit v21 on v20

--- a/solution.py
+++ b/solution.py
@@ -323,10 +323,12 @@
     right = [right_own, *[from_tile(tied(right_tokens[0], half), s) for s in steps]]
     query, pack = project(left, self_qkv, True, 0)
     (right_pack,) = project(tied(right, pack), cross_qkv, False, 1)
+    beside = neighbours(pack)
+    near = [pack, *beside]
+    far = [q for p in near for q in across(p)]
+    state = begin(query, near)
+    halves = tile_pieces(tied(half, right_pack))[1:]
     right_pack = lax.ppermute(right_pack, both, there)
-    beside = neighbours(pack)
-    near = [pack, *across(pack)]
-    halves = tile_pieces(half)[1:]
     others = [
         run_kernel(
             unpack_kernel,
@@ -340,16 +342,14 @@
     (composed,) = run_kernel(
         compose_kernel, "compose", [((columns, channels), BF16)], [cross_out, *map_weights]
     )
-    state = begin(query, near)
-    beside, others, composed, map_weights, state = lax.optimization_barrier(
-        (beside, others, composed, map_weights, state)
-    )
-    far = [*beside, *[q for p in beside for q in across(p)]]
-    right_pack = tied(right_pack, beside)
-    right_near = [right_pack, *neighbours(right_pack)]
+    far, others, composed, map_weights, right_pack = lax.optimization_barrier(
+        (far, others, composed, map_weights, right_pack)
+    )
     (mixed,) = run_kernel(
         end_kernel, "end", [((rows, columns), BF16)], [query, *grouped(far), *state]
     )
+    right_pack = tied(right_pack, mixed)
+    right_near = [right_pack, *neighbours(right_pack)]
     mixed = tile_pieces(mixed)
     right_near = tied(right_near, mixed)
     right_far = [q for p in right_near for q in across(p)]

time: 70.9 us -> 69.2 us (0.976)
  starting transfers between devices: 31 us -> 28.6 us
    ppermute x1, waiting for transfers between devices: 5.53 us -> 3.11 us  [body(): right_pack = lax.ppermute(right_pack, both, there)]
    ppermute x2, waiting for transfers between devices: 4.11 us -> 6.44 us  [fetched(): return lax.ppermute(value, ('blk', 'tile', 'pair'), pairs)]
    ppermute x2, starting transfers between devices: 5.92 us -> 4.53 us  [neighbours(): lax.ppermute(pack, 'blk', [(g + (i + s) % span, g + i) for g, i in ring])]
    ppermute x4, starting transfers between devices: 3.71 us -> 2.83 us  [from_tile(): lax.ppermute(value, 'tile', [((i + step) % tiles, i) for i in range(tiles)])]
  transfers between devices with their start and end apart: 17 -> 17, of which waited for: 8 -> 7; matrix products, arithmetic and copies ran while one was open for 0% -> 0% of each run, Pallas kernels for 16% -> 13%
where the time goes in v21:
time: 69.2 us; the launch traced here: 68.5 us
  starting transfers between devices  28.6 us (41%)
  waiting for transfers between devices  23.3 us (34%)
  Pallas kernels  16.4 us (24%)
    pallas_call x12, Pallas kernels, run_kernel(): pl.pallas_call(kernel, out_shape=[jax.ShapeDtypeStruct(*s) for s in shape...  16.4 us
    ppermute x4, waiting for transfers between devices, from_tile(): lax.ppermute(value, 'tile', [((i + step) % tiles, i) for i in range(tiles)])  8.12 us
    ppermute x2, starting transfers between devices, fetched(): return lax.ppermute(value, ('blk', 'tile', 'pair'), pairs)  7.55 us
    ppermute x2, waiting for transfers between devices, fetched(): return lax.ppermute(value, ('blk', 'tile', 'pair'), pairs)  6.44 us
    ppermute x1, starting transfers between devices, body(): features = lax.ppermute(features, both, back)  4.86 us
    ppermute x1, starting transfers between devices, body(): right_pack = lax.ppermute(right_pack, both, there)  4.83 us
    ppermute x2, starting transfers between devices, neighbours(): lax.ppermute(pack, 'blk', [(g + (i + s) % span, g + i) for g, i in ring])  4.53 us
    ppermute x1, waiting for transfers between devices, body(): below = lax.ppermute(features[:1], both, up)  3.38 us
  transfers between devices with their start and end apart: 17, of which 7 were waited for; matrix products, arithmetic and copies ran while one was open for 0% of the time, Pallas kernels for 13%

profile of v21, /device:TPU:1, one launch (start us, length us, event | category | flops | bytes accessed | tf_op | source)
XLA Modules:
  0.0 68.5 jit_solution(9946076957535132823)
XLA Ops:
  0.0 5.6 %collective-permute-start.1 = (bf16[384,384]{1,0:T(8,128)(2,1)}, bf16[384,384]{1,0:T(8,128)(2,1)S(1)}, u32[]{:S(2)}, u32[]{:S(2)}) collective-permute-start(bf16[384,384]{1,0:T(8,128)(2,1)} %bitcast.10), channel_id=1, source_target_pairs={{2,0},{0,2},{3,12},{1,14},{6,4},{4,6},{7,8},{5,10},{10,5},{8,7},{1... | collective-permute-start | bytes 884744 | tf_op jit(solution)/shard_map/ppermute | solution.py:267
  5.6 1.9 %collective-permute-start = (bf16[384,384]{1,0:T(8,128)(2,1)}, bf16[384,384]{1,0:T(8,128)(2,1)S(1)}, u32[]{:S(2)}, u32[]{:S(2)}) collective-permute-start(bf16[384,384]{1,0:T(8,128)(2,1)} %bitcast.11), channel_id=1, source_target_pairs={{0,0},{2,2},{1,12},{3,14},{4,4},{6,6},{5,8},{7,10},{8,5},{10,7},{9... | collective-permute-start | bytes 884744 | tf_op jit(solution)/shard_map/ppermute | solution.py:267
  7.6 2.6 %stage.1 = (bf16[256,768]{1,0:T(8,128)(2,1)S(1)}, bf16[384,256]{1,0:T(8,128)(2,1)S(1)}, bf16[256,768]{1,0:T(8,128)(2,1)S(1)}, bf16[384,384]{1,0:T(8,128)(2,1)S(1...) custom-call(bf16[256,768]{1,0:T(8,128)(2,1)} %refs_0_.1, ...), custom_call_target="tpu_custom_call" | custom-call | tf_op jit(solution)/shard_map/stage/pallas_call | solution.py:22
  10.5 6.4 %collective-permute-done.refs_0_.refs_4_ = bf16[384,384]{1,0:T(8,128)(2,1)S(1)} collective-permute-done((bf16[384,384]{1,0:T(8,128)(2,1)}, bf16[384,384]{1,0:T(8,128)(2,1)S(1)}, u32[]{:S(2)}, u32[]{:S(2)}) %collective-permute-start) | collective-permute-done | bytes 294944 | tf_op jit(solution)/shard_map/ppermute | solution.py:267
  16.9 1.1 %project.2 = (bf16[384,256]{1,0:T(8,128)(2,1)S(1)}, bf16[384,512]{1,0:T(8,128)(2,1)S(1)}) custom-call(bf16[384,384]{1,0:T(8,128)(2,1)S(1)} %collective-permute-done.refs_0_.refs_4_, bf16[384,384]{1,0:T(8,128)(2,1)S(1)} %collective-permute-done.1.refs_1_.refs_5_, bf16[3,2,384,256]{3,2,1,0:T(8,128)(2,1)S(1)} %bitcast.7), custom_call_target="tpu_custom_call" | custom-call | tf_op jit(solution)/shard_map/project/pallas_call | solution.py:22
  18.0 2.4 %collective-permute-start.3 = (bf16[384,512]{1,0:T(8,128)(2,1)S(1)}, bf16[384,512]{1,0:T(8,128)(2,1)S(1)}, u32[]{:S(2)}, u32[]{:S(2)}) collective-permute-start(bf16[384,512]{1,0:T(8,128)(2,1)S(1)} %get-tuple-element.40.refs_0_), channel_id=1, source_target_pairs={{4,0},{0,4},{12,8},{8,12},{5,1},{1,5},{13,9},{9,13},{6,2},{2,6},{1... | collective-permute-start | bytes 1179656 | tf_op jit(solution)/shard_map/ppermute | solution.py:281
  20.4 0.8 %project.3 = bf16[384,512]{1,0:T(8,128)(2,1)S(1)} custom-call(bf16[384,384]{1,0:T(8,128)(2,1)S(1)} %get-tuple-element.44.refs_0_, bf16[384,384]{1,0:T(8,128)(2,1)S(1)} %collective-permute-done.5.refs_1_, bf16[3,2,384,256]{3,2,1,0:T(8,128)(2,1)S(1)} %bitcast.5), custom_call_target="tpu_custom_call" | custom-call | tf_op jit(solution)/shard_map/project/pallas_call | solution.py:22
  21.7 4.8 %collective-permute-start.8 = (bf16[384,512]{1,0:T(8,128)(2,1)S(1)}, bf16[384,512]{1,0:T(8,128)(2,1)S(1)}, u32[]{:S(2)}, u32[]{:S(2)}) collective-permute-start(bf16[384,512]{1,0:T(8,128)(2,1)S(1)} %project.3), channel_id=1, source_target_pairs={{0,0},{1,12},{4,4},{5,8},{8,5},{9,9},{12,1},{13,13},{2,2},{3,14},{... | collective-permute-start | bytes 1179656 | tf_op jit(solution)/shard_map/ppermute | solution.py:331
  27.2 2.2 %begin.1 = (f32[4,384,128]{2,1,0:T(8,128)S(1)}, f32[4,384,1]{2,1,0:T(8,128)S(1)}) custom-call(bf16[384,256]{1,0:T(8,128)(2,1)S(1)} %get-tuple-element.39.query, bf16[384,512]{1,0:T(8,128)(2,1)S(1)} %get-tuple-element.40.refs_0_, bf16[384,512]{1,0:T(8,128)(2,1)S(1)} %collective-permute-done.3.refs_1_), custom_call_target="tpu_custom_call" | custom-call | tf_op jit(solution)/shard_map/begin/pallas_call | solution.py:22
  29.8 3.1 %collective-permute-done.8.refs_0_ = bf16[384,512]{1,0:T(8,128)(2,1)S(1)} collective-permute-done((bf16[384,512]{1,0:T(8,128)(2,1)S(1)}, bf16[384,512]{1,0:T(8,128)(2,1)S(1)}, u32[]{:S(2)}, u32[]{:S(2)}) %collective-permute-start.8) | collective-permute-done | bytes 393248 | tf_op jit(solution)/shard_map/ppermute | solution.py:331
  32.9 2.6 %end.1.refs_0_ = bf16[384,256]{1,0:T(8,128)(2,1)S(1)} custom-call(bf16[384,256]{1,0:T(8,128)(2,1)S(1)} %get-tuple-element.39.query, bf16[384,512]{1,0:T(8,128)(2,1)S(1)} %collective-permute-done.2.refs_0_, bf16[384,512]{1,0:T(8,128)(2,1)S(1)} %collective-permute-done.4.refs_1_, f32[4,384,128]{2,1,0:T(8,128)S(1)} %get-tuple-element.54.refs_2_, ...), custom_call_target="tpu_custom_call" | custom-call | tf_op jit(solution)/shard_map/end/pallas_call | solution.py:22
  35.5 2.2 %collective-permute-start.10 = (bf16[384,512]{1,0:T(8,128)(2,1)S(1)}, bf16[384,512]{1,0:T(8,128)(2,1)S(1)}, u32[]{:S(2)}, u32[]{:S(2)}) collective-permute-start(bf16[384,512]{1,0:T(8,128)(2,1)S(1)} %collective-permute-done.8.refs_0_), channel_id=1, source_target_pairs={{4,0},{0,4},{12,8},{8,12},{5,1},{1,5},{13,9},{9,13},{6,2},{2,6},{1... | collective-permute-start | bytes 1179656 | tf_op jit(solution)/shard_map/ppermute | solution.py:281
  37.7 1.2 %collective-permute-start.9 = (bf16[384,256]{1,0:T(8,128)(2,1)S(1)}, bf16[384,256]{1,0:T(8,128)(2,1)S(1)}, u32[]{:S(2)}, u32[]{:S(2)}) collective-permute-start(bf16[384,256]{1,0:T(8,128)(2,1)S(1)} %end.1.refs_0_), channel_id=1, source_target_pairs={{2,0},{0,2},{3,1},{1,3},{6,4},{4,6},{7,5},{5,7},{10,8},{8,10},{11,... | collective-permute-start | bytes 589832 | tf_op jit(solution)/shard_map/ppermute | solution.py:273
  38.9 4.5 %collective-permute-done.9.refs_1_ = bf16[384,256]{1,0:T(8,128)(2,1)S(1)} collective-permute-done((bf16[384,256]{1,0:T(8,128)(2,1)S(1)}, bf16[384,256]{1,0:T(8,128)(2,1)S(1)}, u32[]{:S(2)}, u32[]{:S(2)}) %collective-permute-start.9) | collective-permute-done | bytes 196640 | tf_op jit(solution)/shard_map/ppermute | solution.py:273
  43.4 1.9 %collective-permute-done.10.refs_1_ = bf16[384,512]{1,0:T(8,128)(2,1)S(1)} collective-permute-done((bf16[384,512]{1,0:T(8,128)(2,1)S(1)}, bf16[384,512]{1,0:T(8,128)(2,1)S(1)}, u32[]{:S(2)}, u32[]{:S(2)}) %collective-permute-start.10) | collective-permute-done | bytes 393248 | tf_op jit(solution)/shard_map/ppermute | solution.py:281
  45.8 1.5 %update.1 = (bf16[2,384,384]{2,1,0:T(8,128)(2,1)S(1)}, bf16[384,256]{1,0:T(8,128)(2,1)S(1)}) custom-call(bf16[384,256]{1,0:T(8,128)(2,1)S(1)} %end.1.refs_0_, bf16[384,256]{1,0:T(8,128)(2,1)S(1)} %collective-permute-done.9.refs_1_, bf16[256,768]{1,0:T(8,128)(2,1)S(1)} %get-tuple-element.56.refs_2_, bf16[256,768]{1,0:T(8,128)(2,1)S(1)} %get-tuple-element.57.refs_3_, ...), custom_call_target="tpu_custom_call" | custom-call | tf_op jit(solution)/shard_map/update/pallas_call | solution.py:22
  47.6 3.8 %end_map.1 = (bf16[3,80,256]{2,1,0:T(8,128)(2,1)S(1)}, bf16[3,80,256]{2,1,0:T(8,128)(2,1)S(1)}) custom-call(bf16[384,256]{1,0:T(8,128)(2,1)S(1)} %get-tuple-element.59.query, bf16[384,512]{1,0:T(8,128)(2,1)S(1)} %collective-permute-done.8.refs_0_, bf16[384,512]{1,0:T(8,128)(2,1)S(1)} %collective-permute-done.10.refs_1_, ...), custom_call_target="tpu_custom_call" | custom-call | tf_op jit(solution)/shard_map/end_map/pallas_call | solution.py:22
  51.4 0.8 %collective-permute-start.13 = (bf16[3,80,256]{2,1,0:T(8,128)(2,1)S(1)}, bf16[3,80,256]{2,1,0:T(8,128)(2,1)S(1)}, u32[]{:S(2)}, u32[]{:S(2)}) collective-permute-start(bf16[3,80,256]{2,1,0:T(8,128)(2,1)S(1)} %get-tuple-element.66), channel_id=1, source_target_pairs={{2,0},{0,2},{3,1},{1,3},{6,4},{4,6},{7,5},{5,7},{10,8},{8,10},{11,... | collective-permute-start | bytes 368648 | tf_op jit(solution)/shard_map/ppermute | solution.py:273
  52.6 3.6 %collective-permute-done.13.refs_2_ = bf16[3,80,256]{2,1,0:T(8,128)(2,1)S(1)} collective-permute-done((bf16[3,80,256]{2,1,0:T(8,128)(2,1)S(1)}, bf16[3,80,256]{2,1,0:T(8,128)(2,1)S(1)}, u32[]{:S(2)}, u32[]{:S(2)}) %collective-permute-start.13) | collective-permute-done | bytes 122912 | tf_op jit(solution)/shard_map/ppermute | solution.py:273
  56.3 4.9 %collective-permute-start.14 = (bf16[3,80,256]{2,1,0:T(8,128)(2,1)S(1)}, bf16[3,80,256]{2,1,0:T(8,128)(2,1)S(1)}, u32[]{:S(2)}, u32[]{:S(2)}) collective-permute-start(bf16[3,80,256]{2,1,0:T(8,128)(2,1)S(1)} %add.1), channel_id=1, source_target_pairs={{0,0},{12,1},{4,4},{8,5},{5,8},{9,9},{1,12},{13,13},{2,2},{14,3},{... | collective-permute-start | bytes 368648 | tf_op jit(solution)/shard_map/ppermute | solution.py:386
  61.2 2.2 %collective-permute-start.16 = (bf16[1,80,256]{2,1,0:T(8,128)(2,1)S(1)}, bf16[1,80,256]{2,1,0:T(8,128)(2,1)S(1)}, u32[]{:S(2)}, u32[]{:S(2)}) collective-permute-start(bf16[1,80,256]{2,1,0:T(8,128)(2,1)S(1)} %get-tuple-element.71), channel_id=1, source_target_pairs={{4,0},{8,1},{5,4},{9,5},{1,8},{13,9},{6,2},{10,3},{7,6},{11,7},{3,... | collective-permute-start | bytes 122888 | tf_op jit(solution)/shard_map/ppermute | solution.py:385
  63.3 0.7 collective-permute-start.15
  64.0 3.4 %collective-permute-done.16.below = bf16[1,80,256]{2,1,0:T(8,128)(2,1)S(1)} collective-permute-done((bf16[1,80,256]{2,1,0:T(8,128)(2,1)S(1)}, bf16[1,80,256]{2,1,0:T(8,128)(2,1)S(1)}, u32[]{:S(2)}, u32[]{:S(2)}) %collective-permute-start.16) | collective-permute-done | bytes 40992 | tf_op jit(solution)/shard_map/ppermute | solution.py:385
  67.4 1.1 %join.1 = bf16[3,64,256]{2,1,0:T(8,128)(2,1)} custom-call(bf16[3,80,256]{2,1,0:T(8,128)(2,1)S(1)} %collective-permute-done.14.window, bf16[1,80,256]{2,1,0:T(8,128)(2,1)S(1)} %collective-permute-done.15.above, bf16[1,80,256]{2,1,0:T(8,128)(2,1)S(1)} %collective-permute-done.16.below, bf16[3,3,256,256]{3,2,1,0:T(8,128)(2,1)S(1)} %get-tuple-element.70.weight), custom_call_target="tpu_custom_call" | custom-call | tf_op jit(solution)/shard_map/join/pallas_call | solution.py:22
  (25 shorter events, 3.1 us)
Async XLA Ops:
  0.0 10.5 %collective-permute-start.1 = (bf16[384,384]{1,0:T(8,128)(2,1)}, bf16[384,384]{1,0:T(8,128)(2,1)S(1)}, u32[]{:S(2)}, u32[]{:S(2)}) collective-permute-start(bf16[384,384]{1,0:T(8,128)(2,1)} %bitcast.10), channel_id=1, source_target_pairs={{2,0},{0,2},{3,12},{1,14},{6,4},{4,6},{7,8},{5,10},{10,5},{8,7},{1... | collective-permute-start | bytes 884744 | tf_op jit(solution)/shard_map/ppermute | solution.py:267
  5.6 11.3 %collective-permute-start = (bf16[384,384]{1,0:T(8,128)(2,1)}, bf16[384,384]{1,0:T(8,128)(2,1)S(1)}, u32[]{:S(2)}, u32[]{:S(2)}) collective-permute-start(bf16[384,384]{1,0:T(8,128)(2,1)} %bitcast.11), channel_id=1, source_target_pairs={{0,0},{2,2},{1,12},{3,14},{4,4},{6,6},{5,8},{7,10},{8,5},{10,7},{9... | collective-permute-start | bytes 884744 | tf_op jit(solution)/shard_map/ppermute | solution.py:267
  7.6 2.6 %copy-start = (bf16[1,384,384]{2,1,0:T(8,128)(2,1)S(1)}, bf16[1,384,384]{2,1,0:T(8,128)(2,1)}, u32[]{:S(2)}) copy-start(bf16[1,384,384]{2,1,0:T(8,128)(2,1)} %param.9) | copy-start | bytes 884740
  10.1 10.2 %collective-permute-start.5 = (bf16[384,384]{1,0:T(8,128)(2,1)S(1)}, bf16[384,384]{1,0:T(8,128)(2,1)S(1)}, u32[]{:S(2)}, u32[]{:S(2)}) collective-permute-start(bf16[384,384]{1,0:T(8,128)(2,1)S(1)} %bitcast.9), channel_id=1, source_target_pairs={{2,0},{0,2},{3,1},{1,3},{6,4},{4,6},{7,5},{5,7},{10,8},{8,10},{11,... | collective-permute-start | bytes 884744 | tf_op jit(solution)/shard_map/ppermute | solution.py:273
  18.0 8.6 %collective-permute-start.3 = (bf16[384,512]{1,0:T(8,128)(2,1)S(1)}, bf16[384,512]{1,0:T(8,128)(2,1)S(1)}, u32[]{:S(2)}, u32[]{:S(2)}) collective-permute-start(bf16[384,512]{1,0:T(8,128)(2,1)S(1)} %get-tuple-element.40.refs_0_), channel_id=1, source_target_pairs={{4,0},{0,4},{12,8},{8,12},{5,1},{1,5},{13,9},{9,13},{6,2},{2,6},{1... | collective-permute-start | bytes 1179656 | tf_op jit(solution)/shard_map/ppermute | solution.py:281
  21.2 5.9 %collective-permute-start.6 = (bf16[192,768]{1,0:T(8,128)(2,1)S(1)}, bf16[192,768]{1,0:T(8,128)(2,1)S(1)}, u32[]{:S(2)}, u32[]{:S(2)}) collective-permute-start(bf16[192,768]{1,0:T(8,128)(2,1)S(1)} %get-tuple-element.47), channel_id=1, source_target_pairs={{2,0},{0,2},{3,1},{1,3},{6,4},{4,6},{7,5},{5,7},{10,8},{8,10},{11,... | collective-permute-start | bytes 884744 | tf_op jit(solution)/shard_map/ppermute | solution.py:273
  21.7 11.2 %collective-permute-start.8 = (bf16[384,512]{1,0:T(8,128)(2,1)S(1)}, bf16[384,512]{1,0:T(8,128)(2,1)S(1)}, u32[]{:S(2)}, u32[]{:S(2)}) collective-permute-start(bf16[384,512]{1,0:T(8,128)(2,1)S(1)} %project.3), channel_id=1, source_target_pairs={{0,0},{1,12},{4,4},{5,8},{8,5},{9,9},{12,1},{13,13},{2,2},{3,14},{... | collective-permute-start | bytes 1179656 | tf_op jit(solution)/shard_map/ppermute | solution.py:331
  26.5 6.4 %collective-permute-start.2 = (bf16[384,512]{1,0:T(8,128)(2,1)S(1)}, bf16[384,512]{1,0:T(8,128)(2,1)S(1)}, u32[]{:S(2)}, u32[]{:S(2)}) collective-permute-start(bf16[384,512]{1,0:T(8,128)(2,1)S(1)} %get-tuple-element.40.refs_0_), channel_id=1, source_target_pairs={{1,0},{0,1},{3,2},{2,3},{5,4},{4,5},{7,6},{6,7},{9,8},{8,9},{11,10... | collective-permute-start | bytes 1179656 | tf_op jit(solution)/shard_map/ppermute | solution.py:287
  26.6 6.3 %collective-permute-start.4 = (bf16[384,512]{1,0:T(8,128)(2,1)S(1)}, bf16[384,512]{1,0:T(8,128)(2,1)S(1)}, u32[]{:S(2)}, u32[]{:S(2)}) collective-permute-start(bf16[384,512]{1,0:T(8,128)(2,1)S(1)} %collective-permute-done.3.refs_1_), channel_id=1, source_target_pairs={{1,0},{0,1},{3,2},{2,3},{5,4},{4,5},{7,6},{6,7},{9,8},{8,9},{11,10... | collective-permute-start | bytes 1179656 | tf_op jit(solution)/shard_map/ppermute | solution.py:287
  27.1 2.3 %collective-permute-start.7 = (bf16[192,768]{1,0:T(8,128)(2,1)S(1)}, bf16[192,768]{1,0:T(8,128)(2,1)S(1)}, u32[]{:S(2)}, u32[]{:S(2)}) collective-permute-start(bf16[192,768]{1,0:T(8,128)(2,1)S(1)} %collective-permute-done.6.refs_0_), channel_id=1, source_target_pairs={{1,0},{0,1},{3,2},{2,3},{5,4},{4,5},{7,6},{6,7},{9,8},{8,9},{11,10... | collective-permute-start | bytes 884744 | tf_op jit(solution)/shard_map/ppermute | solution.py:287
  35.5 9.7 %collective-permute-start.10 = (bf16[384,512]{1,0:T(8,128)(2,1)S(1)}, bf16[384,512]{1,0:T(8,128)(2,1)S(1)}, u32[]{:S(2)}, u32[]{:S(2)}) collective-permute-start(bf16[384,512]{1,0:T(8,128)(2,1)S(1)} %collective-permute-done.8.refs_0_), channel_id=1, source_target_pairs={{4,0},{0,4},{12,8},{8,12},{5,1},{1,5},{13,9},{9,13},{6,2},{2,6},{1... | collective-permute-start | bytes 1179656 | tf_op jit(solution)/shard_map/ppermute | solution.py:281
  37.7 5.7 %collective-permute-start.9 = (bf16[384,256]{1,0:T(8,128)(2,1)S(1)}, bf16[384,256]{1,0:T(8,128)(2,1)S(1)}, u32[]{:S(2)}, u32[]{:S(2)}) collective-permute-start(bf16[384,256]{1,0:T(8,128)(2,1)S(1)} %end.1.refs_0_), channel_id=1, source_target_pairs={{2,0},{0,2},{3,1},{1,3},{6,4},{4,6},{7,5},{5,7},{10,8},{8,10},{11,... | collective-permute-start | bytes 589832 | tf_op jit(solution)/shard_map/ppermute | solution.py:273
  45.3 2.0 %collective-permute-start.11 = (bf16[384,512]{1,0:T(8,128)(2,1)S(1)}, bf16[384,512]{1,0:T(8,128)(2,1)S(1)}, u32[]{:S(2)}, u32[]{:S(2)}) collective-permute-start(bf16[384,512]{1,0:T(8,128)(2,1)S(1)} %collective-permute-done.8.refs_0_), channel_id=1, source_target_pairs={{1,0},{0,1},{3,2},{2,3},{5,4},{4,5},{7,6},{6,7},{9,8},{8,9},{11,10... | collective-permute-start | bytes 1179656 | tf_op jit(solution)/shard_map/ppermute | solution.py:287
  45.3 2.3 %collective-permute-start.12 = (bf16[384,512]{1,0:T(8,128)(2,1)S(1)}, bf16[384,512]{1,0:T(8,128)(2,1)S(1)}, u32[]{:S(2)}, u32[]{:S(2)}) collective-permute-start(bf16[384,512]{1,0:T(8,128)(2,1)S(1)} %collective-permute-done.10.refs_1_), channel_id=1, source_target_pairs={{1,0},{0,1},{3,2},{2,3},{5,4},{4,5},{7,6},{6,7},{9,8},{8,9},{11,10... | collective-permute-start | bytes 1179656 | tf_op jit(solution)/shard_map/ppermute | solution.py:287
  51.4 4.8 %collective-permute-start.13 = (bf16[3,80,256]{2,1,0:T(8,128)(2,1)S(1)}, bf16[3,80,256]{2,1,0:T(8,128)(2,1)S(1)}, u32[]{:S(2)}, u32[]{:S(2)}) collective-permute-start(bf16[3,80,256]{2,1,0:T(8,128)(2,1)S(1)} %get-tuple-element.66), channel_id=1, source_target_pairs={{2,0},{0,2},{3,1},{1,3},{6,4},{4,6},{7,5},{5,7},{10,8},{8,10},{11,... | collective-permute-start | bytes 368648 | tf_op jit(solution)/shard_map/ppermute | solution.py:273
  56.3 11.1 %collective-permute-start.14 = (bf16[3,80,256]{2,1,0:T(8,128)(2,1)S(1)}, bf16[3,80,256]{2,1,0:T(8,128)(2,1)S(1)}, u32[]{:S(2)}, u32[]{:S(2)}) collective-permute-start(bf16[3,80,256]{2,1,0:T(8,128)(2,1)S(1)} %add.1), channel_id=1, source_target_pairs={{0,0},{12,1},{4,4},{8,5},{5,8},{9,9},{1,12},{13,13},{2,2},{14,3},{... | collective-permute-start | bytes 368648 | tf_op jit(solution)/shard_map/ppermute | solution.py:386
  61.2 6.2 %collective-permute-start.16 = (bf16[1,80,256]{2,1,0:T(8,128)(2,1)S(1)}, bf16[1,80,256]{2,1,0:T(8,128)(2,1)S(1)}, u32[]{:S(2)}, u32[]{:S(2)}) collective-permute-start(bf16[1,80,256]{2,1,0:T(8,128)(2,1)S(1)} %get-tuple-element.71), channel_id=1, source_target_pairs={{4,0},{8,1},{5,4},{9,5},{1,8},{13,9},{6,2},{10,3},{7,6},{11,7},{3,... | collective-permute-start | bytes 122888 | tf_op jit(solution)/shard_map/ppermute | solution.py:385
  63.3 4.1 %collective-permute-start.15 = (bf16[1,80,256]{2,1,0:T(8,128)(2,1)S(1)}, bf16[1,80,256]{2,1,0:T(8,128)(2,1)S(1)}, u32[]{:S(2)}, u32[]{:S(2)}) collective-permute-start(bf16[1,80,256]{2,1,0:T(8,128)(2,1)S(1)} %get-tuple-element.72), channel_id=1, source_target_pairs={{0,4},{12,5},{4,8},{8,9},{5,12},{9,13},{2,6},{14,7},{6,10},{10,11}... | collective-permute-start | bytes 122888 | tf_op jit(solution)/shard_map/ppermute | solution.py:384

commit v22 on v21

--- a/solution.py
+++ b/solution.py
@@ -259,6 +259,9 @@
     down = [(worker(b, p), home(b + 1, p)) for b, p in places if b + 1 < bands]
     up = [(worker(b, p), home(b - 1, p)) for b, p in places if b > 0]
 
+    stays = [home(*p) for p in places if home(*p) == worker(*p)]
+    comes = [worker(*p) for p in places if home(*p) != worker(*p)]
+
     def fetched(value, step):
         def flat(position, tile):
             return (position // cores * tiles + tile) * cores + position % cores
@@ -275,11 +278,13 @@
     def tile_pieces(own):
         return [own, *[from_tile(own, s) for s in range(1, tiles)]]
 
-    def neighbours(pack):
-        ring = [(g * span, i) for g in range(cores) for i in range(span)]
+    def neighbours(pack, members):
+        def source(member, step):
+            band, core = divmod(member, cores)
+            return (band // span * span + (band % span + step) % span) * cores + core
+
         return [
-            lax.ppermute(pack, "blk", [(g + (i + s) % span, g + i) for g, i in ring])
-            for s in range(1, span)
+            lax.ppermute(pack, both, [(source(m, s), m) for m in members]) for s in range(1, span)
         ]
 
     def across(pack):
@@ -323,7 +328,8 @@
     right = [right_own, *[from_tile(tied(right_tokens[0], half), s) for s in steps]]
     query, pack = project(left, self_qkv, True, 0)
     (right_pack,) = project(tied(right, pack), cross_qkv, False, 1)
-    beside = neighbours(pack)
+    beside = neighbours(pack, [*stays, *comes])
+    right_early = neighbours(right_pack, stays)
     near = [pack, *beside]
     far = [q for p in near for q in across(p)]
     state = begin(query, near)
@@ -342,16 +348,17 @@
     (composed,) = run_kernel(
         compose_kernel, "compose", [((columns, channels), BF16)], [cross_out, *map_weights]
     )
-    far, others, composed, map_weights, right_pack = lax.optimization_barrier(
-        (far, others, composed, map_weights, right_pack)
+    far, others, composed, map_weights, right_pack, right_early = lax.optimization_barrier(
+        (far, others, composed, map_weights, right_pack, right_early)
     )
     (mixed,) = run_kernel(
         end_kernel, "end", [((rows, columns), BF16)], [query, *grouped(far), *state]
     )
     right_pack = tied(right_pack, mixed)
-    right_near = [right_pack, *neighbours(right_pack)]
+    right_late = neighbours(right_pack, comes)
     mixed = tile_pieces(mixed)
-    right_near = tied(right_near, mixed)
+    right_late = tied(right_late, mixed)
+    right_near = [right_pack, *[a + b for a, b in zip(right_early, right_late)]]
     right_far = [q for p in right_near for q in across(p)]
     updated, cross_query = run_kernel(
         functools.partial(update_kernel, count=tiles),

time: 69.2 us -> 71.5 us (1.033)
  starting transfers between devices: 28.6 us -> 30.7 us
    ppermute x1, starting transfers between devices: 4.86 us -> 6.71 us  [body(): features = lax.ppermute(features, both, back)]
    ppermute x1, waiting for transfers between devices: 3.11 us -> 4.57 us  [body(): right_pack = lax.ppermute(right_pack, both, there)]
    ppermute x2 -> x3, starting transfers between devices: 4.53 us -> 5.76 us  [neighbours(): lax.ppermute(pack, both, [(source(m, s), m) for m in members])]
    ppermute x4, waiting for transfers between devices: 8.12 us -> 7.2 us  [from_tile(): lax.ppermute(value, 'tile', [((i + step) % tiles, i) for i in range(tiles)])]
    ppermute x2 -> x3, waiting for transfers between devices: 1.9 us -> 1.21 us  [neighbours(): lax.ppermute(pack, both, [(source(m, s), m) for m in members])]
  transfers between devices with their start and end apart: 17 -> 18, of which waited for: 7 -> 7; matrix products, arithmetic and copies ran while one was open for 0% -> 0% of each run, Pallas kernels for 13% -> 13%
where the time goes in v22:
time: 71.5 us; the launch traced here: 70.7 us
  starting transfers between devices  30.7 us (43%)
  waiting for transfers between devices  23.3 us (33%)
  Pallas kernels  16.4 us (23%)
    pallas_call x12, Pallas kernels, run_kernel(): pl.pallas_call(kernel, out_shape=[jax.ShapeDtypeStruct(*s) for s in shape...  16.4 us
    ppermute x2, starting transfers between devices, fetched(): return lax.ppermute(value, ('blk', 'tile', 'pair'), pairs)  7.55 us
    ppermute x4, waiting for transfers between devices, from_tile(): lax.ppermute(value, 'tile', [((i + step) % tiles, i) for i in range(tiles)])  7.2 us
    ppermute x1, starting transfers between devices, body(): features = lax.ppermute(features, both, back)  6.71 us
    ppermute x2, waiting for transfers between devices, fetched(): return lax.ppermute(value, ('blk', 'tile', 'pair'), pairs)  6.44 us
    ppermute x3, starting transfers between devices, neighbours(): lax.ppermute(pack, both, [(source(m, s), m) for m in members])  5.76 us
    ppermute x1, starting transfers between devices, body(): right_pack = lax.ppermute(right_pack, both, there)  4.84 us
    ppermute x1, waiting for transfers between devices, body(): right_pack = lax.ppermute(right_pack, both, there)  4.57 us
  transfers between devices with their start and end apart: 18, of which 7 were waited for; matrix products, arithmetic and copies ran while one was open for 0% of the time, Pallas kernels for 13%

profile of v22, /device:TPU:1, one launch (start us, length us, event | category | flops | bytes accessed | tf_op | source)
XLA Modules:
  0.0 70.7 jit_solution(13022852629365077848)
XLA Ops:
  0.0 5.6 %collective-permute-start.1 = (bf16[384,384]{1,0:T(8,128)(2,1)}, bf16[384,384]{1,0:T(8,128)(2,1)S(1)}, u32[]{:S(2)}, u32[]{:S(2)}) collective-permute-start(bf16[384,384]{1,0:T(8,128)(2,1)} %bitcast.10), channel_id=1, source_target_pairs={{2,0},{0,2},{3,12},{1,14},{6,4},{4,6},{7,8},{5,10},{10,5},{8,7},{1... | collective-permute-start | bytes 884744 | tf_op jit(solution)/shard_map/ppermute | solution.py:270
  5.6 1.9 %collective-permute-start = (bf16[384,384]{1,0:T(8,128)(2,1)}, bf16[384,384]{1,0:T(8,128)(2,1)S(1)}, u32[]{:S(2)}, u32[]{:S(2)}) collective-permute-start(bf16[384,384]{1,0:T(8,128)(2,1)} %bitcast.11), channel_id=1, source_target_pairs={{0,0},{2,2},{1,12},{3,14},{4,4},{6,6},{5,8},{7,10},{8,5},{10,7},{9... | collective-permute-start | bytes 884744 | tf_op jit(solution)/shard_map/ppermute | solution.py:270
  7.6 2.6 %stage.1 = (bf16[256,768]{1,0:T(8,128)(2,1)S(1)}, bf16[384,256]{1,0:T(8,128)(2,1)S(1)}, bf16[256,768]{1,0:T(8,128)(2,1)S(1)}, bf16[384,384]{1,0:T(8,128)(2,1)S(1...) custom-call(bf16[256,768]{1,0:T(8,128)(2,1)} %refs_0_.1, ...), custom_call_target="tpu_custom_call" | custom-call | tf_op jit(solution)/shard_map/stage/pallas_call | solution.py:22
  10.5 6.4 %collective-permute-done.refs_0_.refs_4_ = bf16[384,384]{1,0:T(8,128)(2,1)S(1)} collective-permute-done((bf16[384,384]{1,0:T(8,128)(2,1)}, bf16[384,384]{1,0:T(8,128)(2,1)S(1)}, u32[]{:S(2)}, u32[]{:S(2)}) %collective-permute-start) | collective-permute-done | bytes 294944 | tf_op jit(solution)/shard_map/ppermute | solution.py:270
  16.9 1.1 %project.2 = (bf16[384,256]{1,0:T(8,128)(2,1)S(1)}, bf16[384,512]{1,0:T(8,128)(2,1)S(1)}) custom-call(bf16[384,384]{1,0:T(8,128)(2,1)S(1)} %collective-permute-done.refs_0_.refs_4_, bf16[384,384]{1,0:T(8,128)(2,1)S(1)} %collective-permute-done.1.refs_1_.refs_5_, bf16[3,2,384,256]{3,2,1,0:T(8,128)(2,1)S(1)} %bitcast.7), custom_call_target="tpu_custom_call" | custom-call | tf_op jit(solution)/shard_map/project/pallas_call | solution.py:22
  18.0 2.4 %collective-permute-start.3 = (bf16[384,512]{1,0:T(8,128)(2,1)S(1)}, bf16[384,512]{1,0:T(8,128)(2,1)S(1)}, u32[]{:S(2)}, u32[]{:S(2)}) collective-permute-start(bf16[384,512]{1,0:T(8,128)(2,1)S(1)} %get-tuple-element.40.refs_0_), channel_id=1, source_target_pairs={{4,0},{0,4},{13,9},{9,13},{8,12},{12,8},{1,5},{5,1},{6,2},{2,6},{1... | collective-permute-start | bytes 1179656 | tf_op jit(solution)/shard_map/ppermute | solution.py:287
  20.4 0.8 %project.3 = bf16[384,512]{1,0:T(8,128)(2,1)S(1)} custom-call(bf16[384,384]{1,0:T(8,128)(2,1)S(1)} %get-tuple-element.44.refs_0_, bf16[384,384]{1,0:T(8,128)(2,1)S(1)} %collective-permute-done.5.refs_1_, bf16[3,2,384,256]{3,2,1,0:T(8,128)(2,1)S(1)} %bitcast.5), custom_call_target="tpu_custom_call" | custom-call | tf_op jit(solution)/shard_map/project/pallas_call | solution.py:22
  21.7 0.7 collective-permute-start.9
  22.4 4.8 %collective-permute-start.8 = (bf16[384,512]{1,0:T(8,128)(2,1)S(1)}, bf16[384,512]{1,0:T(8,128)(2,1)S(1)}, u32[]{:S(2)}, u32[]{:S(2)}) collective-permute-start(bf16[384,512]{1,0:T(8,128)(2,1)S(1)} %project.3), channel_id=1, source_target_pairs={{0,0},{1,12},{4,4},{5,8},{8,5},{9,9},{12,1},{13,13},{2,2},{3,14},{... | collective-permute-start | bytes 1179656 | tf_op jit(solution)/shard_map/ppermute | solution.py:337
  27.9 2.2 %begin.1 = (f32[4,384,128]{2,1,0:T(8,128)S(1)}, f32[4,384,1]{2,1,0:T(8,128)S(1)}) custom-call(bf16[384,256]{1,0:T(8,128)(2,1)S(1)} %get-tuple-element.39.query, bf16[384,512]{1,0:T(8,128)(2,1)S(1)} %get-tuple-element.40.refs_0_, bf16[384,512]{1,0:T(8,128)(2,1)S(1)} %collective-permute-done.3.refs_1_), custom_call_target="tpu_custom_call" | custom-call | tf_op jit(solution)/shard_map/begin/pallas_call | solution.py:22
  30.5 4.6 %collective-permute-done.8.refs_0_ = bf16[384,512]{1,0:T(8,128)(2,1)S(1)} collective-permute-done((bf16[384,512]{1,0:T(8,128)(2,1)S(1)}, bf16[384,512]{1,0:T(8,128)(2,1)S(1)}, u32[]{:S(2)}, u32[]{:S(2)}) %collective-permute-start.8) | collective-permute-done | bytes 393248 | tf_op jit(solution)/shard_map/ppermute | solution.py:337
  35.1 2.6 %end.1.refs_0_ = bf16[384,256]{1,0:T(8,128)(2,1)S(1)} custom-call(bf16[384,256]{1,0:T(8,128)(2,1)S(1)} %get-tuple-element.39.query, bf16[384,512]{1,0:T(8,128)(2,1)S(1)} %collective-permute-done.2.refs_0_, bf16[384,512]{1,0:T(8,128)(2,1)S(1)} %collective-permute-done.4.refs_1_, f32[4,384,128]{2,1,0:T(8,128)S(1)} %get-tuple-element.54.refs_2_, ...), custom_call_target="tpu_custom_call" | custom-call | tf_op jit(solution)/shard_map/end/pallas_call | solution.py:22
  37.7 2.7 %collective-permute-start.11 = (bf16[384,512]{1,0:T(8,128)(2,1)S(1)}, bf16[384,512]{1,0:T(8,128)(2,1)S(1)}, u32[]{:S(2)}, u32[]{:S(2)}) collective-permute-start(bf16[384,512]{1,0:T(8,128)(2,1)S(1)} %collective-permute-done.8.refs_0_), channel_id=1, source_target_pairs={{8,12},{12,8},{1,5},{5,1},{10,14},{14,10},{3,7},{7,3},{24,28},{28,... | collective-permute-start | bytes 1179656 | tf_op jit(solution)/shard_map/ppermute | solution.py:287
  40.4 1.3 %collective-permute-start.10 = (bf16[384,256]{1,0:T(8,128)(2,1)S(1)}, bf16[384,256]{1,0:T(8,128)(2,1)S(1)}, u32[]{:S(2)}, u32[]{:S(2)}) collective-permute-start(bf16[384,256]{1,0:T(8,128)(2,1)S(1)} %end.1.refs_0_), channel_id=1, source_target_pairs={{2,0},{0,2},{3,1},{1,3},{6,4},{4,6},{7,5},{5,7},{10,8},{8,10},{11,... | collective-permute-start | bytes 589832 | tf_op jit(solution)/shard_map/ppermute | solution.py:276
  41.7 3.3 %collective-permute-done.10.refs_1_ = bf16[384,256]{1,0:T(8,128)(2,1)S(1)} collective-permute-done((bf16[384,256]{1,0:T(8,128)(2,1)S(1)}, bf16[384,256]{1,0:T(8,128)(2,1)S(1)}, u32[]{:S(2)}, u32[]{:S(2)}) %collective-permute-start.10) | collective-permute-done | bytes 196640 | tf_op jit(solution)/shard_map/ppermute | solution.py:276
  45.0 1.2 %collective-permute-done.11 = bf16[384,512]{1,0:T(8,128)(2,1)S(1)} collective-permute-done((bf16[384,512]{1,0:T(8,128)(2,1)S(1)}, bf16[384,512]{1,0:T(8,128)(2,1)S(1)}, u32[]{:S(2)}, u32[]{:S(2)}) %collective-permute-start.11) | collective-permute-done | bytes 393248 | tf_op jit(solution)/shard_map/ppermute | solution.py:287
  46.4 1.5 %update.1 = (bf16[2,384,384]{2,1,0:T(8,128)(2,1)S(1)}, bf16[384,256]{1,0:T(8,128)(2,1)S(1)}) custom-call(bf16[384,256]{1,0:T(8,128)(2,1)S(1)} %end.1.refs_0_, bf16[384,256]{1,0:T(8,128)(2,1)S(1)} %collective-permute-done.10.refs_1_, bf16[256,768]{1,0:T(8,128)(2,1)S(1)} %get-tuple-element.56.refs_2_, bf16[256,768]{1,0:T(8,128)(2,1)S(1)} %get-tuple-element.57.refs_3_, ...), custom_call_target="tpu_custom_call" | custom-call | tf_op jit(solution)/shard_map/update/pallas_call | solution.py:22
  48.1 3.8 %end_map.1 = (bf16[3,80,256]{2,1,0:T(8,128)(2,1)S(1)}, bf16[3,80,256]{2,1,0:T(8,128)(2,1)S(1)}) custom-call(bf16[384,256]{1,0:T(8,128)(2,1)S(1)} %get-tuple-element.59.query, bf16[384,512]{1,0:T(8,128)(2,1)S(1)} %collective-permute-done.8.refs_0_, bf16[384,512]{1,0:T(8,128)(2,1)S(1)} %add.4.refs_1_, bf16[384,512]{1,0:T(8,128)(2,1)S(1)} %collective-permute-done.12.refs_2_, ...), custom_call_target="tpu_custom_call" | custom-call | tf_op jit(solution)/shard_map/end_map/pallas_call | solution.py:22
  52.8 3.9 %collective-permute-done.14.refs_2_ = bf16[3,80,256]{2,1,0:T(8,128)(2,1)S(1)} collective-permute-done((bf16[3,80,256]{2,1,0:T(8,128)(2,1)S(1)}, bf16[3,80,256]{2,1,0:T(8,128)(2,1)S(1)}, u32[]{:S(2)}, u32[]{:S(2)}) %collective-permute-start.14) | collective-permute-done | bytes 122912 | tf_op jit(solution)/shard_map/ppermute | solution.py:276
  56.7 6.7 %collective-permute-start.15 = (bf16[3,80,256]{2,1,0:T(8,128)(2,1)S(1)}, bf16[3,80,256]{2,1,0:T(8,128)(2,1)S(1)}, u32[]{:S(2)}, u32[]{:S(2)}) collective-permute-start(bf16[3,80,256]{2,1,0:T(8,128)(2,1)S(1)} %add.5), channel_id=1, source_target_pairs={{0,0},{12,1},{4,4},{8,5},{5,8},{9,9},{1,12},{13,13},{2,2},{14,3},{... | collective-permute-start | bytes 368648 | tf_op jit(solution)/shard_map/ppermute | solution.py:393
  63.4 1.9 %collective-permute-start.17 = (bf16[1,80,256]{2,1,0:T(8,128)(2,1)S(1)}, bf16[1,80,256]{2,1,0:T(8,128)(2,1)S(1)}, u32[]{:S(2)}, u32[]{:S(2)}) collective-permute-start(bf16[1,80,256]{2,1,0:T(8,128)(2,1)S(1)} %get-tuple-element.71), channel_id=1, source_target_pairs={{4,0},{8,1},{5,4},{9,5},{1,8},{13,9},{6,2},{10,3},{7,6},{11,7},{3,... | collective-permute-start | bytes 122888 | tf_op jit(solution)/shard_map/ppermute | solution.py:392
  65.4 0.7 collective-permute-start.16
  66.0 3.6 %collective-permute-done.17.below = bf16[1,80,256]{2,1,0:T(8,128)(2,1)S(1)} collective-permute-done((bf16[1,80,256]{2,1,0:T(8,128)(2,1)S(1)}, bf16[1,80,256]{2,1,0:T(8,128)(2,1)S(1)}, u32[]{:S(2)}, u32[]{:S(2)}) %collective-permute-start.17) | collective-permute-done | bytes 40992 | tf_op jit(solution)/shard_map/ppermute | solution.py:392
  69.7 1.1 %join.1 = bf16[3,64,256]{2,1,0:T(8,128)(2,1)} custom-call(bf16[3,80,256]{2,1,0:T(8,128)(2,1)S(1)} %collective-permute-done.15.window, bf16[1,80,256]{2,1,0:T(8,128)(2,1)S(1)} %collective-permute-done.16.above, bf16[1,80,256]{2,1,0:T(8,128)(2,1)S(1)} %collective-permute-done.17.below, bf16[3,3,256,256]{3,2,1,0:T(8,128)(2,1)S(1)} %get-tuple-element.70.weight), custom_call_target="tpu_custom_call" | custom-call | tf_op jit(solution)/shard_map/join/pallas_call | solution.py:22
  (28 shorter events, 3.1 us)
Async XLA Ops:
  0.0 10.5 %collective-permute-start.1 = (bf16[384,384]{1,0:T(8,128)(2,1)}, bf16[384,384]{1,0:T(8,128)(2,1)S(1)}, u32[]{:S(2)}, u32[]{:S(2)}) collective-permute-start(bf16[384,384]{1,0:T(8,128)(2,1)} %bitcast.10), channel_id=1, source_target_pairs={{2,0},{0,2},{3,12},{1,14},{6,4},{4,6},{7,8},{5,10},{10,5},{8,7},{1... | collective-permute-start | bytes 884744 | tf_op jit(solution)/shard_map/ppermute | solution.py:270
  5.6 11.3 %collective-permute-start = (bf16[384,384]{1,0:T(8,128)(2,1)}, bf16[384,384]{1,0:T(8,128)(2,1)S(1)}, u32[]{:S(2)}, u32[]{:S(2)}) collective-permute-start(bf16[384,384]{1,0:T(8,128)(2,1)} %bitcast.11), channel_id=1, source_target_pairs={{0,0},{2,2},{1,12},{3,14},{4,4},{6,6},{5,8},{7,10},{8,5},{10,7},{9... | collective-permute-start | bytes 884744 | tf_op jit(solution)/shard_map/ppermute | solution.py:270
  7.6 2.6 %copy-start = (bf16[1,384,384]{2,1,0:T(8,128)(2,1)S(1)}, bf16[1,384,384]{2,1,0:T(8,128)(2,1)}, u32[]{:S(2)}) copy-start(bf16[1,384,384]{2,1,0:T(8,128)(2,1)} %param.9) | copy-start | bytes 884740
  10.1 10.2 %collective-permute-start.5 = (bf16[384,384]{1,0:T(8,128)(2,1)S(1)}, bf16[384,384]{1,0:T(8,128)(2,1)S(1)}, u32[]{:S(2)}, u32[]{:S(2)}) collective-permute-start(bf16[384,384]{1,0:T(8,128)(2,1)S(1)} %bitcast.9), channel_id=1, source_target_pairs={{2,0},{0,2},{3,1},{1,3},{6,4},{4,6},{7,5},{5,7},{10,8},{8,10},{11,... | collective-permute-start | bytes 884744 | tf_op jit(solution)/shard_map/ppermute | solution.py:276
  18.0 9.3 %collective-permute-start.3 = (bf16[384,512]{1,0:T(8,128)(2,1)S(1)}, bf16[384,512]{1,0:T(8,128)(2,1)S(1)}, u32[]{:S(2)}, u32[]{:S(2)}) collective-permute-start(bf16[384,512]{1,0:T(8,128)(2,1)S(1)} %get-tuple-element.40.refs_0_), channel_id=1, source_target_pairs={{4,0},{0,4},{13,9},{9,13},{8,12},{12,8},{1,5},{5,1},{6,2},{2,6},{1... | collective-permute-start | bytes 1179656 | tf_op jit(solution)/shard_map/ppermute | solution.py:287
  21.2 6.6 %collective-permute-start.6 = (bf16[192,768]{1,0:T(8,128)(2,1)S(1)}, bf16[192,768]{1,0:T(8,128)(2,1)S(1)}, u32[]{:S(2)}, u32[]{:S(2)}) collective-permute-start(bf16[192,768]{1,0:T(8,128)(2,1)S(1)} %get-tuple-element.47), channel_id=1, source_target_pairs={{2,0},{0,2},{3,1},{1,3},{6,4},{4,6},{7,5},{5,7},{10,8},{8,10},{11,... | collective-permute-start | bytes 884744 | tf_op jit(solution)/shard_map/ppermute | solution.py:276
  21.7 8.8 %collective-permute-start.9 = (bf16[384,512]{1,0:T(8,128)(2,1)S(1)}, bf16[384,512]{1,0:T(8,128)(2,1)S(1)}, u32[]{:S(2)}, u32[]{:S(2)}) collective-permute-start(bf16[384,512]{1,0:T(8,128)(2,1)S(1)} %project.3), channel_id=1, source_target_pairs={{4,0},{0,4},{13,9},{9,13},{6,2},{2,6},{15,11},{11,15},{20,16},{16,... | collective-permute-start | bytes 1179656 | tf_op jit(solution)/shard_map/ppermute | solution.py:287
  22.4 12.7 %collective-permute-start.8 = (bf16[384,512]{1,0:T(8,128)(2,1)S(1)}, bf16[384,512]{1,0:T(8,128)(2,1)S(1)}, u32[]{:S(2)}, u32[]{:S(2)}) collective-permute-start(bf16[384,512]{1,0:T(8,128)(2,1)S(1)} %project.3), channel_id=1, source_target_pairs={{0,0},{1,12},{4,4},{5,8},{8,5},{9,9},{12,1},{13,13},{2,2},{3,14},{... | collective-permute-start | bytes 1179656 | tf_op jit(solution)/shard_map/ppermute | solution.py:337
  27.2 7.9 %collective-permute-start.2 = (bf16[384,512]{1,0:T(8,128)(2,1)S(1)}, bf16[384,512]{1,0:T(8,128)(2,1)S(1)}, u32[]{:S(2)}, u32[]{:S(2)}) collective-permute-start(bf16[384,512]{1,0:T(8,128)(2,1)S(1)} %get-tuple-element.40.refs_0_), channel_id=1, source_target_pairs={{1,0},{0,1},{3,2},{2,3},{5,4},{4,5},{7,6},{6,7},{9,8},{8,9},{11,10... | collective-permute-start | bytes 1179656 | tf_op jit(solution)/shard_map/ppermute | solution.py:292
  27.3 7.8 %collective-permute-start.4 = (bf16[384,512]{1,0:T(8,128)(2,1)S(1)}, bf16[384,512]{1,0:T(8,128)(2,1)S(1)}, u32[]{:S(2)}, u32[]{:S(2)}) collective-permute-start(bf16[384,512]{1,0:T(8,128)(2,1)S(1)} %collective-permute-done.3.refs_1_), channel_id=1, source_target_pairs={{1,0},{0,1},{3,2},{2,3},{5,4},{4,5},{7,6},{6,7},{9,8},{8,9},{11,10... | collective-permute-start | bytes 1179656 | tf_op jit(solution)/shard_map/ppermute | solution.py:292
  27.8 2.3 %collective-permute-start.7 = (bf16[192,768]{1,0:T(8,128)(2,1)S(1)}, bf16[192,768]{1,0:T(8,128)(2,1)S(1)}, u32[]{:S(2)}, u32[]{:S(2)}) collective-permute-start(bf16[192,768]{1,0:T(8,128)(2,1)S(1)} %collective-permute-done.6.refs_0_), channel_id=1, source_target_pairs={{1,0},{0,1},{3,2},{2,3},{5,4},{4,5},{7,6},{6,7},{9,8},{8,9},{11,10... | collective-permute-start | bytes 884744 | tf_op jit(solution)/shard_map/ppermute | solution.py:292
  37.7 8.5 %collective-permute-start.11 = (bf16[384,512]{1,0:T(8,128)(2,1)S(1)}, bf16[384,512]{1,0:T(8,128)(2,1)S(1)}, u32[]{:S(2)}, u32[]{:S(2)}) collective-permute-start(bf16[384,512]{1,0:T(8,128)(2,1)S(1)} %collective-permute-done.8.refs_0_), channel_id=1, source_target_pairs={{8,12},{12,8},{1,5},{5,1},{10,14},{14,10},{3,7},{7,3},{24,28},{28,... | collective-permute-start | bytes 1179656 | tf_op jit(solution)/shard_map/ppermute | solution.py:287
  40.4 4.6 %collective-permute-start.10 = (bf16[384,256]{1,0:T(8,128)(2,1)S(1)}, bf16[384,256]{1,0:T(8,128)(2,1)S(1)}, u32[]{:S(2)}, u32[]{:S(2)}) collective-permute-start(bf16[384,256]{1,0:T(8,128)(2,1)S(1)} %end.1.refs_0_), channel_id=1, source_target_pairs={{2,0},{0,2},{3,1},{1,3},{6,4},{4,6},{7,5},{5,7},{10,8},{8,10},{11,... | collective-permute-start | bytes 589832 | tf_op jit(solution)/shard_map/ppermute | solution.py:276
  41.7 6.2 %collective-permute-start.12 = (bf16[384,512]{1,0:T(8,128)(2,1)S(1)}, bf16[384,512]{1,0:T(8,128)(2,1)S(1)}, u32[]{:S(2)}, u32[]{:S(2)}) collective-permute-start(bf16[384,512]{1,0:T(8,128)(2,1)S(1)} %collective-permute-done.8.refs_0_), channel_id=1, source_target_pairs={{1,0},{0,1},{3,2},{2,3},{5,4},{4,5},{7,6},{6,7},{9,8},{8,9},{11,10... | collective-permute-start | bytes 1179656 | tf_op jit(solution)/shard_map/ppermute | solution.py:292
  46.3 1.8 %collective-permute-start.13 = (bf16[384,512]{1,0:T(8,128)(2,1)S(1)}, bf16[384,512]{1,0:T(8,128)(2,1)S(1)}, u32[]{:S(2)}, u32[]{:S(2)}) collective-permute-start(bf16[384,512]{1,0:T(8,128)(2,1)S(1)} %add.4.refs_1_), channel_id=1, source_target_pairs={{1,0},{0,1},{3,2},{2,3},{5,4},{4,5},{7,6},{6,7},{9,8},{8,9},{11,10... | collective-permute-start | bytes 1179656 | tf_op jit(solution)/shard_map/ppermute | solution.py:292
  51.9 4.7 %collective-permute-start.14 = (bf16[3,80,256]{2,1,0:T(8,128)(2,1)S(1)}, bf16[3,80,256]{2,1,0:T(8,128)(2,1)S(1)}, u32[]{:S(2)}, u32[]{:S(2)}) collective-permute-start(bf16[3,80,256]{2,1,0:T(8,128)(2,1)S(1)} %get-tuple-element.66), channel_id=1, source_target_pairs={{2,0},{0,2},{3,1},{1,3},{6,4},{4,6},{7,5},{5,7},{10,8},{8,10},{11,... | collective-permute-start | bytes 368648 | tf_op jit(solution)/shard_map/ppermute | solution.py:276
  56.7 13.0 %collective-permute-start.15 = (bf16[3,80,256]{2,1,0:T(8,128)(2,1)S(1)}, bf16[3,80,256]{2,1,0:T(8,128)(2,1)S(1)}, u32[]{:S(2)}, u32[]{:S(2)}) collective-permute-start(bf16[3,80,256]{2,1,0:T(8,128)(2,1)S(1)} %add.5), channel_id=1, source_target_pairs={{0,0},{12,1},{4,4},{8,5},{5,8},{9,9},{1,12},{13,13},{2,2},{14,3},{... | collective-permute-start | bytes 368648 | tf_op jit(solution)/shard_map/ppermute | solution.py:393
  63.4 6.2 %collective-permute-start.17 = (bf16[1,80,256]{2,1,0:T(8,128)(2,1)S(1)}, bf16[1,80,256]{2,1,0:T(8,128)(2,1)S(1)}, u32[]{:S(2)}, u32[]{:S(2)}) collective-permute-start(bf16[1,80,256]{2,1,0:T(8,128)(2,1)S(1)} %get-tuple-element.71), channel_id=1, source_target_pairs={{4,0},{8,1},{5,4},{9,5},{1,8},{13,9},{6,2},{10,3},{7,6},{11,7},{3,... | collective-permute-start | bytes 122888 | tf_op jit(solution)/shard_map/ppermute | solution.py:392
  65.4 4.3 %collective-permute-start.16 = (bf16[1,80,256]{2,1,0:T(8,128)(2,1)S(1)}, bf16[1,80,256]{2,1,0:T(8,128)(2,1)S(1)}, u32[]{:S(2)}, u32[]{:S(2)}) collective-permute-start(bf16[1,80,256]{2,1,0:T(8,128)(2,1)S(1)} %get-tuple-element.72), channel_id=1, source_target_pairs={{0,4},{12,5},{4,8},{8,9},{5,12},{9,13},{2,6},{14,7},{6,10},{10,11}... | collective-permute-start | bytes 122888 | tf_op jit(solution)/shard_map/ppermute | solution.py:391

commit v23 on v21

--- a/solution.py
+++ b/solution.py
@@ -342,13 +342,13 @@
     (composed,) = run_kernel(
         compose_kernel, "compose", [((columns, channels), BF16)], [cross_out, *map_weights]
     )
+    right_pack = tied(right_pack, state, composed)
     far, others, composed, map_weights, right_pack = lax.optimization_barrier(
         (far, others, composed, map_weights, right_pack)
     )
     (mixed,) = run_kernel(
         end_kernel, "end", [((rows, columns), BF16)], [query, *grouped(far), *state]
     )
-    right_pack = tied(right_pack, mixed)
     right_near = [right_pack, *neighbours(right_pack)]
     mixed = tile_pieces(mixed)
     right_near = tied(right_near, mixed)

time: 69.2 us -> 70.1 us (1.013)
  starting transfers between devices: 28.6 us -> 33 us
  waiting for transfers between devices: 23.3 us -> 20.3 us
    ppermute x2, starting transfers between devices: 4.53 us -> 6.95 us  [neighbours(): lax.ppermute(pack, 'blk', [(g + (i + s) % span, g + i) for g, i in ring])]
    ppermute x2, waiting for transfers between devices: 1.9 us -> 0.01 us  [neighbours(): lax.ppermute(pack, 'blk', [(g + (i + s) % span, g + i) for g, i in ring])]
    ppermute x4, waiting for transfers between devices: 8.12 us -> 6.48 us  [from_tile(): lax.ppermute(value, 'tile', [((i + step) % tiles, i) for i in range(tiles)])]
    ppermute x1, starting transfers between devices: 4.86 us -> 6.26 us  [body(): features = lax.ppermute(features, both, back)]
    ppermute x1, waiting for transfers between devices: 3.38 us -> 4.5 us  [body(): below = lax.ppermute(features[:1], both, up)]
  transfers between devices with their start and end apart: 17 -> 17, of which waited for: 7 -> 7; matrix products, arithmetic and copies ran while one was open for 0% -> 0% of each run, Pallas kernels for 13% -> 16%
where the time goes in v23:
time: 70.1 us; the launch traced here: 69.9 us
  starting transfers between devices  33 us (47%)
  waiting for transfers between devices  20.3 us (29%)
  Pallas kernels  16.4 us (23%)
    pallas_call x12, Pallas kernels, run_kernel(): pl.pallas_call(kernel, out_shape=[jax.ShapeDtypeStruct(*s) for s in shape...  16.4 us
    ppermute x2, starting transfers between devices, fetched(): return lax.ppermute(value, ('blk', 'tile', 'pair'), pairs)  7.61 us
    ppermute x2, starting transfers between devices, neighbours(): lax.ppermute(pack, 'blk', [(g + (i + s) % span, g + i) for g, i in ring])  6.95 us
    ppermute x4, waiting for transfers between devices, from_tile(): lax.ppermute(value, 'tile', [((i + step) % tiles, i) for i in range(tiles)])  6.48 us
    ppermute x1, starting transfers between devices, body(): features = lax.ppermute(features, both, back)  6.26 us
    ppermute x2, waiting for transfers between devices, fetched(): return lax.ppermute(value, ('blk', 'tile', 'pair'), pairs)  5.83 us
    ppermute x1, starting transfers between devices, body(): right_pack = lax.ppermute(right_pack, both, there)  5.09 us
    ppermute x1, waiting for transfers between devices, body(): below = lax.ppermute(features[:1], both, up)  4.5 us
  transfers between devices with their start and end apart: 17, of which 7 were waited for; matrix products, arithmetic and copies ran while one was open for 0% of the time, Pallas kernels for 16%

profile of v23, /device:TPU:1, one launch (start us, length us, event | category | flops | bytes accessed | tf_op | source)
XLA Modules:
  0.0 69.9 jit_solution(1777677066843354104)
XLA Ops:
  0.0 6.6 %collective-permute-start = (bf16[384,384]{1,0:T(8,128)(2,1)}, bf16[384,384]{1,0:T(8,128)(2,1)S(1)}, u32[]{:S(2)}, u32[]{:S(2)}) collective-permute-start(bf16[384,384]{1,0:T(8,128)(2,1)} %bitcast.10), channel_id=1, source_target_pairs={{0,0},{2,2},{1,12},{3,14},{4,4},{6,6},{5,8},{7,10},{8,5},{10,7},{9... | collective-permute-start | bytes 884744 | tf_op jit(solution)/shard_map/ppermute | solution.py:267
  6.6 1.0 %collective-permute-start.1 = (bf16[384,384]{1,0:T(8,128)(2,1)}, bf16[384,384]{1,0:T(8,128)(2,1)S(1)}, u32[]{:S(2)}, u32[]{:S(2)}) collective-permute-start(bf16[384,384]{1,0:T(8,128)(2,1)} %bitcast.11), channel_id=1, source_target_pairs={{2,0},{0,2},{3,12},{1,14},{6,4},{4,6},{7,8},{5,10},{10,5},{8,7},{1... | collective-permute-start | bytes 884744 | tf_op jit(solution)/shard_map/ppermute | solution.py:267
  7.6 2.6 %stage.1 = (bf16[256,768]{1,0:T(8,128)(2,1)S(1)}, bf16[384,256]{1,0:T(8,128)(2,1)S(1)}, bf16[256,768]{1,0:T(8,128)(2,1)S(1)}, bf16[384,384]{1,0:T(8,128)(2,1)S(1...) custom-call(bf16[256,768]{1,0:T(8,128)(2,1)} %refs_0_.1, ...), custom_call_target="tpu_custom_call" | custom-call | tf_op jit(solution)/shard_map/stage/pallas_call | solution.py:22
  10.6 0.8 %collective-permute-done.refs_0_.refs_4_ = bf16[384,384]{1,0:T(8,128)(2,1)S(1)} collective-permute-done((bf16[384,384]{1,0:T(8,128)(2,1)}, bf16[384,384]{1,0:T(8,128)(2,1)S(1)}, u32[]{:S(2)}, u32[]{:S(2)}) %collective-permute-start) | collective-permute-done | bytes 294944 | tf_op jit(solution)/shard_map/ppermute | solution.py:267
  11.3 5.1 %collective-permute-done.1.refs_1_.refs_5_ = bf16[384,384]{1,0:T(8,128)(2,1)S(1)} collective-permute-done((bf16[384,384]{1,0:T(8,128)(2,1)}, bf16[384,384]{1,0:T(8,128)(2,1)S(1)}, u32[]{:S(2)}, u32[]{:S(2)}) %collective-permute-start.1) | collective-permute-done | bytes 294944 | tf_op jit(solution)/shard_map/ppermute | solution.py:267
  16.4 1.1 %project.2 = (bf16[384,256]{1,0:T(8,128)(2,1)S(1)}, bf16[384,512]{1,0:T(8,128)(2,1)S(1)}) custom-call(bf16[384,384]{1,0:T(8,128)(2,1)S(1)} %collective-permute-done.refs_0_.refs_4_, bf16[384,384]{1,0:T(8,128)(2,1)S(1)} %collective-permute-done.1.refs_1_.refs_5_, bf16[3,2,384,256]{3,2,1,0:T(8,128)(2,1)S(1)} %bitcast.7), custom_call_target="tpu_custom_call" | custom-call | tf_op jit(solution)/shard_map/project/pallas_call | solution.py:22
  17.5 4.6 %collective-permute-start.3 = (bf16[384,512]{1,0:T(8,128)(2,1)S(1)}, bf16[384,512]{1,0:T(8,128)(2,1)S(1)}, u32[]{:S(2)}, u32[]{:S(2)}) collective-permute-start(bf16[384,512]{1,0:T(8,128)(2,1)S(1)} %get-tuple-element.40.refs_0_), channel_id=1, source_target_pairs={{4,0},{0,4},{12,8},{8,12},{5,1},{1,5},{13,9},{9,13},{6,2},{2,6},{1... | collective-permute-start | bytes 1179656 | tf_op jit(solution)/shard_map/ppermute | solution.py:281
  22.0 0.8 %project.3 = bf16[384,512]{1,0:T(8,128)(2,1)S(1)} custom-call(bf16[384,384]{1,0:T(8,128)(2,1)S(1)} %get-tuple-element.44.refs_0_, bf16[384,384]{1,0:T(8,128)(2,1)S(1)} %collective-permute-done.5.refs_1_, bf16[3,2,384,256]{3,2,1,0:T(8,128)(2,1)S(1)} %bitcast.5), custom_call_target="tpu_custom_call" | custom-call | tf_op jit(solution)/shard_map/project/pallas_call | solution.py:22
  23.3 5.1 %collective-permute-start.8 = (bf16[384,512]{1,0:T(8,128)(2,1)S(1)}, bf16[384,512]{1,0:T(8,128)(2,1)S(1)}, u32[]{:S(2)}, u32[]{:S(2)}) collective-permute-start(bf16[384,512]{1,0:T(8,128)(2,1)S(1)} %project.3), channel_id=1, source_target_pairs={{0,0},{1,12},{4,4},{5,8},{8,5},{9,9},{12,1},{13,13},{2,2},{3,14},{... | collective-permute-start | bytes 1179656 | tf_op jit(solution)/shard_map/ppermute | solution.py:331
  29.1 2.2 %begin.1 = (f32[4,384,128]{2,1,0:T(8,128)S(1)}, f32[4,384,1]{2,1,0:T(8,128)S(1)}) custom-call(bf16[384,256]{1,0:T(8,128)(2,1)S(1)} %get-tuple-element.39.query, bf16[384,512]{1,0:T(8,128)(2,1)S(1)} %get-tuple-element.40.refs_0_, bf16[384,512]{1,0:T(8,128)(2,1)S(1)} %collective-permute-done.3.refs_1_), custom_call_target="tpu_custom_call" | custom-call | tf_op jit(solution)/shard_map/begin/pallas_call | solution.py:22
  31.7 3.1 %collective-permute-done.8.refs_0_ = bf16[384,512]{1,0:T(8,128)(2,1)S(1)} collective-permute-done((bf16[384,512]{1,0:T(8,128)(2,1)S(1)}, bf16[384,512]{1,0:T(8,128)(2,1)S(1)}, u32[]{:S(2)}, u32[]{:S(2)}) %collective-permute-start.8) | collective-permute-done | bytes 393248 | tf_op jit(solution)/shard_map/ppermute | solution.py:331
  34.8 2.4 %collective-permute-start.10 = (bf16[384,512]{1,0:T(8,128)(2,1)S(1)}, bf16[384,512]{1,0:T(8,128)(2,1)S(1)}, u32[]{:S(2)}, u32[]{:S(2)}) collective-permute-start(bf16[384,512]{1,0:T(8,128)(2,1)S(1)} %collective-permute-done.8.refs_0_), channel_id=1, source_target_pairs={{4,0},{0,4},{12,8},{8,12},{5,1},{1,5},{13,9},{9,13},{6,2},{2,6},{1... | collective-permute-start | bytes 1179656 | tf_op jit(solution)/shard_map/ppermute | solution.py:281
  37.2 2.6 %end.1.refs_0_ = bf16[384,256]{1,0:T(8,128)(2,1)S(1)} custom-call(bf16[384,256]{1,0:T(8,128)(2,1)S(1)} %get-tuple-element.39.query, bf16[384,512]{1,0:T(8,128)(2,1)S(1)} %collective-permute-done.2.refs_0_, bf16[384,512]{1,0:T(8,128)(2,1)S(1)} %collective-permute-done.4.refs_1_, f32[4,384,128]{2,1,0:T(8,128)S(1)} %get-tuple-element.52.refs_2_, ...), custom_call_target="tpu_custom_call" | custom-call | tf_op jit(solution)/shard_map/end/pallas_call | solution.py:22
  39.8 1.3 %collective-permute-start.9 = (bf16[384,256]{1,0:T(8,128)(2,1)S(1)}, bf16[384,256]{1,0:T(8,128)(2,1)S(1)}, u32[]{:S(2)}, u32[]{:S(2)}) collective-permute-start(bf16[384,256]{1,0:T(8,128)(2,1)S(1)} %end.1.refs_0_), channel_id=1, source_target_pairs={{2,0},{0,2},{3,1},{1,3},{6,4},{4,6},{7,5},{5,7},{10,8},{8,10},{11,... | collective-permute-start | bytes 589832 | tf_op jit(solution)/shard_map/ppermute | solution.py:273
  41.1 3.3 %collective-permute-done.9.refs_1_ = bf16[384,256]{1,0:T(8,128)(2,1)S(1)} collective-permute-done((bf16[384,256]{1,0:T(8,128)(2,1)S(1)}, bf16[384,256]{1,0:T(8,128)(2,1)S(1)}, u32[]{:S(2)}, u32[]{:S(2)}) %collective-permute-start.9) | collective-permute-done | bytes 196640 | tf_op jit(solution)/shard_map/ppermute | solution.py:273
  44.9 1.5 %update.1 = (bf16[2,384,384]{2,1,0:T(8,128)(2,1)S(1)}, bf16[384,256]{1,0:T(8,128)(2,1)S(1)}) custom-call(bf16[384,256]{1,0:T(8,128)(2,1)S(1)} %end.1.refs_0_, bf16[384,256]{1,0:T(8,128)(2,1)S(1)} %collective-permute-done.9.refs_1_, bf16[256,768]{1,0:T(8,128)(2,1)S(1)} %get-tuple-element.57.refs_2_, bf16[256,768]{1,0:T(8,128)(2,1)S(1)} %get-tuple-element.58.refs_3_, ...), custom_call_target="tpu_custom_call" | custom-call | tf_op jit(solution)/shard_map/update/pallas_call | solution.py:22
  46.7 3.8 %end_map.1 = (bf16[3,80,256]{2,1,0:T(8,128)(2,1)S(1)}, bf16[3,80,256]{2,1,0:T(8,128)(2,1)S(1)}) custom-call(bf16[384,256]{1,0:T(8,128)(2,1)S(1)} %get-tuple-element.60.query, bf16[384,512]{1,0:T(8,128)(2,1)S(1)} %collective-permute-done.8.refs_0_, bf16[384,512]{1,0:T(8,128)(2,1)S(1)} %collective-permute-done.10.refs_1_, ...), custom_call_target="tpu_custom_call" | custom-call | tf_op jit(solution)/shard_map/end_map/pallas_call | solution.py:22
  50.5 1.3 %collective-permute-start.13 = (bf16[3,80,256]{2,1,0:T(8,128)(2,1)S(1)}, bf16[3,80,256]{2,1,0:T(8,128)(2,1)S(1)}, u32[]{:S(2)}, u32[]{:S(2)}) collective-permute-start(bf16[3,80,256]{2,1,0:T(8,128)(2,1)S(1)} %get-tuple-element.66), channel_id=1, source_target_pairs={{2,0},{0,2},{3,1},{1,3},{6,4},{4,6},{7,5},{5,7},{10,8},{8,10},{11,... | collective-permute-start | bytes 368648 | tf_op jit(solution)/shard_map/ppermute | solution.py:273
  52.2 3.2 %collective-permute-done.13.refs_2_ = bf16[3,80,256]{2,1,0:T(8,128)(2,1)S(1)} collective-permute-done((bf16[3,80,256]{2,1,0:T(8,128)(2,1)S(1)}, bf16[3,80,256]{2,1,0:T(8,128)(2,1)S(1)}, u32[]{:S(2)}, u32[]{:S(2)}) %collective-permute-start.13) | collective-permute-done | bytes 122912 | tf_op jit(solution)/shard_map/ppermute | solution.py:273
  55.4 6.3 %collective-permute-start.14 = (bf16[3,80,256]{2,1,0:T(8,128)(2,1)S(1)}, bf16[3,80,256]{2,1,0:T(8,128)(2,1)S(1)}, u32[]{:S(2)}, u32[]{:S(2)}) collective-permute-start(bf16[3,80,256]{2,1,0:T(8,128)(2,1)S(1)} %add.1), channel_id=1, source_target_pairs={{0,0},{12,1},{4,4},{8,5},{5,8},{9,9},{1,12},{13,13},{2,2},{14,3},{... | collective-permute-start | bytes 368648 | tf_op jit(solution)/shard_map/ppermute | solution.py:386
  61.7 0.7 collective-permute-start.15
  62.4 1.9 %collective-permute-start.16 = (bf16[1,80,256]{2,1,0:T(8,128)(2,1)S(1)}, bf16[1,80,256]{2,1,0:T(8,128)(2,1)S(1)}, u32[]{:S(2)}, u32[]{:S(2)}) collective-permute-start(bf16[1,80,256]{2,1,0:T(8,128)(2,1)S(1)} %get-tuple-element.71), channel_id=1, source_target_pairs={{4,0},{8,1},{5,4},{9,5},{1,8},{13,9},{6,2},{10,3},{7,6},{11,7},{3,... | collective-permute-start | bytes 122888 | tf_op jit(solution)/shard_map/ppermute | solution.py:385
  64.3 4.5 %collective-permute-done.16.below = bf16[1,80,256]{2,1,0:T(8,128)(2,1)S(1)} collective-permute-done((bf16[1,80,256]{2,1,0:T(8,128)(2,1)S(1)}, bf16[1,80,256]{2,1,0:T(8,128)(2,1)S(1)}, u32[]{:S(2)}, u32[]{:S(2)}) %collective-permute-start.16) | collective-permute-done | bytes 40992 | tf_op jit(solution)/shard_map/ppermute | solution.py:385
  68.8 1.1 %join.1 = bf16[3,64,256]{2,1,0:T(8,128)(2,1)} custom-call(bf16[3,80,256]{2,1,0:T(8,128)(2,1)S(1)} %collective-permute-done.14.window, bf16[1,80,256]{2,1,0:T(8,128)(2,1)S(1)} %collective-permute-done.15.above, bf16[1,80,256]{2,1,0:T(8,128)(2,1)S(1)} %collective-permute-done.16.below, bf16[3,3,256,256]{3,2,1,0:T(8,128)(2,1)S(1)} %get-tuple-element.70.weight), custom_call_target="tpu_custom_call" | custom-call | tf_op jit(solution)/shard_map/join/pallas_call | solution.py:22
  (25 shorter events, 3.1 us)
Async XLA Ops:
  0.0 11.3 %collective-permute-start = (bf16[384,384]{1,0:T(8,128)(2,1)}, bf16[384,384]{1,0:T(8,128)(2,1)S(1)}, u32[]{:S(2)}, u32[]{:S(2)}) collective-permute-start(bf16[384,384]{1,0:T(8,128)(2,1)} %bitcast.10), channel_id=1, source_target_pairs={{0,0},{2,2},{1,12},{3,14},{4,4},{6,6},{5,8},{7,10},{8,5},{10,7},{9... | collective-permute-start | bytes 884744 | tf_op jit(solution)/shard_map/ppermute | solution.py:267
  6.6 9.8 %collective-permute-start.1 = (bf16[384,384]{1,0:T(8,128)(2,1)}, bf16[384,384]{1,0:T(8,128)(2,1)S(1)}, u32[]{:S(2)}, u32[]{:S(2)}) collective-permute-start(bf16[384,384]{1,0:T(8,128)(2,1)} %bitcast.11), channel_id=1, source_target_pairs={{2,0},{0,2},{3,12},{1,14},{6,4},{4,6},{7,8},{5,10},{10,5},{8,7},{1... | collective-permute-start | bytes 884744 | tf_op jit(solution)/shard_map/ppermute | solution.py:267
  7.6 2.6 %copy-start = (bf16[1,384,384]{2,1,0:T(8,128)(2,1)S(1)}, bf16[1,384,384]{2,1,0:T(8,128)(2,1)}, u32[]{:S(2)}) copy-start(bf16[1,384,384]{2,1,0:T(8,128)(2,1)} %param.9) | copy-start | bytes 884740
  10.2 11.8 %collective-permute-start.5 = (bf16[384,384]{1,0:T(8,128)(2,1)S(1)}, bf16[384,384]{1,0:T(8,128)(2,1)S(1)}, u32[]{:S(2)}, u32[]{:S(2)}) collective-permute-start(bf16[384,384]{1,0:T(8,128)(2,1)S(1)} %bitcast.9), channel_id=1, source_target_pairs={{2,0},{0,2},{3,1},{1,3},{6,4},{4,6},{7,5},{5,7},{10,8},{8,10},{11,... | collective-permute-start | bytes 884744 | tf_op jit(solution)/shard_map/ppermute | solution.py:273
  17.5 11.0 %collective-permute-start.3 = (bf16[384,512]{1,0:T(8,128)(2,1)S(1)}, bf16[384,512]{1,0:T(8,128)(2,1)S(1)}, u32[]{:S(2)}, u32[]{:S(2)}) collective-permute-start(bf16[384,512]{1,0:T(8,128)(2,1)S(1)} %get-tuple-element.40.refs_0_), channel_id=1, source_target_pairs={{4,0},{0,4},{12,8},{8,12},{5,1},{1,5},{13,9},{9,13},{6,2},{2,6},{1... | collective-permute-start | bytes 1179656 | tf_op jit(solution)/shard_map/ppermute | solution.py:281
  22.9 6.1 %collective-permute-start.6 = (bf16[192,768]{1,0:T(8,128)(2,1)S(1)}, bf16[192,768]{1,0:T(8,128)(2,1)S(1)}, u32[]{:S(2)}, u32[]{:S(2)}) collective-permute-start(bf16[192,768]{1,0:T(8,128)(2,1)S(1)} %get-tuple-element.47), channel_id=1, source_target_pairs={{2,0},{0,2},{3,1},{1,3},{6,4},{4,6},{7,5},{5,7},{10,8},{8,10},{11,... | collective-permute-start | bytes 884744 | tf_op jit(solution)/shard_map/ppermute | solution.py:273
  23.3 11.5 %collective-permute-start.8 = (bf16[384,512]{1,0:T(8,128)(2,1)S(1)}, bf16[384,512]{1,0:T(8,128)(2,1)S(1)}, u32[]{:S(2)}, u32[]{:S(2)}) collective-permute-start(bf16[384,512]{1,0:T(8,128)(2,1)S(1)} %project.3), channel_id=1, source_target_pairs={{0,0},{1,12},{4,4},{5,8},{8,5},{9,9},{12,1},{13,13},{2,2},{3,14},{... | collective-permute-start | bytes 1179656 | tf_op jit(solution)/shard_map/ppermute | solution.py:331
  28.4 6.4 %collective-permute-start.2 = (bf16[384,512]{1,0:T(8,128)(2,1)S(1)}, bf16[384,512]{1,0:T(8,128)(2,1)S(1)}, u32[]{:S(2)}, u32[]{:S(2)}) collective-permute-start(bf16[384,512]{1,0:T(8,128)(2,1)S(1)} %get-tuple-element.40.refs_0_), channel_id=1, source_target_pairs={{1,0},{0,1},{3,2},{2,3},{5,4},{4,5},{7,6},{6,7},{9,8},{8,9},{11,10... | collective-permute-start | bytes 1179656 | tf_op jit(solution)/shard_map/ppermute | solution.py:287
  28.5 6.3 %collective-permute-start.4 = (bf16[384,512]{1,0:T(8,128)(2,1)S(1)}, bf16[384,512]{1,0:T(8,128)(2,1)S(1)}, u32[]{:S(2)}, u32[]{:S(2)}) collective-permute-start(bf16[384,512]{1,0:T(8,128)(2,1)S(1)} %collective-permute-done.3.refs_1_), channel_id=1, source_target_pairs={{1,0},{0,1},{3,2},{2,3},{5,4},{4,5},{7,6},{6,7},{9,8},{8,9},{11,10... | collective-permute-start | bytes 1179656 | tf_op jit(solution)/shard_map/ppermute | solution.py:287
  29.0 2.3 %collective-permute-start.7 = (bf16[192,768]{1,0:T(8,128)(2,1)S(1)}, bf16[192,768]{1,0:T(8,128)(2,1)S(1)}, u32[]{:S(2)}, u32[]{:S(2)}) collective-permute-start(bf16[192,768]{1,0:T(8,128)(2,1)S(1)} %collective-permute-done.6.refs_0_), channel_id=1, source_target_pairs={{1,0},{0,1},{3,2},{2,3},{5,4},{4,5},{7,6},{6,7},{9,8},{8,9},{11,10... | collective-permute-start | bytes 884744 | tf_op jit(solution)/shard_map/ppermute | solution.py:287
  34.8 9.6 %collective-permute-start.10 = (bf16[384,512]{1,0:T(8,128)(2,1)S(1)}, bf16[384,512]{1,0:T(8,128)(2,1)S(1)}, u32[]{:S(2)}, u32[]{:S(2)}) collective-permute-start(bf16[384,512]{1,0:T(8,128)(2,1)S(1)} %collective-permute-done.8.refs_0_), channel_id=1, source_target_pairs={{4,0},{0,4},{12,8},{8,12},{5,1},{1,5},{13,9},{9,13},{6,2},{2,6},{1... | collective-permute-start | bytes 1179656 | tf_op jit(solution)/shard_map/ppermute | solution.py:281
  39.8 4.6 %collective-permute-start.9 = (bf16[384,256]{1,0:T(8,128)(2,1)S(1)}, bf16[384,256]{1,0:T(8,128)(2,1)S(1)}, u32[]{:S(2)}, u32[]{:S(2)}) collective-permute-start(bf16[384,256]{1,0:T(8,128)(2,1)S(1)} %end.1.refs_0_), channel_id=1, source_target_pairs={{2,0},{0,2},{3,1},{1,3},{6,4},{4,6},{7,5},{5,7},{10,8},{8,10},{11,... | collective-permute-start | bytes 589832 | tf_op jit(solution)/shard_map/ppermute | solution.py:273
  44.4 2.0 %collective-permute-start.11 = (bf16[384,512]{1,0:T(8,128)(2,1)S(1)}, bf16[384,512]{1,0:T(8,128)(2,1)S(1)}, u32[]{:S(2)}, u32[]{:S(2)}) collective-permute-start(bf16[384,512]{1,0:T(8,128)(2,1)S(1)} %collective-permute-done.8.refs_0_), channel_id=1, source_target_pairs={{1,0},{0,1},{3,2},{2,3},{5,4},{4,5},{7,6},{6,7},{9,8},{8,9},{11,10... | collective-permute-start | bytes 1179656 | tf_op jit(solution)/shard_map/ppermute | solution.py:287
  44.4 2.3 %collective-permute-start.12 = (bf16[384,512]{1,0:T(8,128)(2,1)S(1)}, bf16[384,512]{1,0:T(8,128)(2,1)S(1)}, u32[]{:S(2)}, u32[]{:S(2)}) collective-permute-start(bf16[384,512]{1,0:T(8,128)(2,1)S(1)} %collective-permute-done.10.refs_1_), channel_id=1, source_target_pairs={{1,0},{0,1},{3,2},{2,3},{5,4},{4,5},{7,6},{6,7},{9,8},{8,9},{11,10... | collective-permute-start | bytes 1179656 | tf_op jit(solution)/shard_map/ppermute | solution.py:287
  50.5 4.8 %collective-permute-start.13 = (bf16[3,80,256]{2,1,0:T(8,128)(2,1)S(1)}, bf16[3,80,256]{2,1,0:T(8,128)(2,1)S(1)}, u32[]{:S(2)}, u32[]{:S(2)}) collective-permute-start(bf16[3,80,256]{2,1,0:T(8,128)(2,1)S(1)} %get-tuple-element.66), channel_id=1, source_target_pairs={{2,0},{0,2},{3,1},{1,3},{6,4},{4,6},{7,5},{5,7},{10,8},{8,10},{11,... | collective-permute-start | bytes 368648 | tf_op jit(solution)/shard_map/ppermute | solution.py:273
  55.4 13.4 %collective-permute-start.14 = (bf16[3,80,256]{2,1,0:T(8,128)(2,1)S(1)}, bf16[3,80,256]{2,1,0:T(8,128)(2,1)S(1)}, u32[]{:S(2)}, u32[]{:S(2)}) collective-permute-start(bf16[3,80,256]{2,1,0:T(8,128)(2,1)S(1)} %add.1), channel_id=1, source_target_pairs={{0,0},{12,1},{4,4},{8,5},{5,8},{9,9},{1,12},{13,13},{2,2},{14,3},{... | collective-permute-start | bytes 368648 | tf_op jit(solution)/shard_map/ppermute | solution.py:386
  61.7 2.6 %collective-permute-start.15 = (bf16[1,80,256]{2,1,0:T(8,128)(2,1)S(1)}, bf16[1,80,256]{2,1,0:T(8,128)(2,1)S(1)}, u32[]{:S(2)}, u32[]{:S(2)}) collective-permute-start(bf16[1,80,256]{2,1,0:T(8,128)(2,1)S(1)} %get-tuple-element.72), channel_id=1, source_target_pairs={{0,4},{12,5},{4,8},{8,9},{5,12},{9,13},{2,6},{14,7},{6,10},{10,11}... | collective-permute-start | bytes 122888 | tf_op jit(solution)/shard_map/ppermute | solution.py:384
  62.4 6.4 %collective-permute-start.16 = (bf16[1,80,256]{2,1,0:T(8,128)(2,1)S(1)}, bf16[1,80,256]{2,1,0:T(8,128)(2,1)S(1)}, u32[]{:S(2)}, u32[]{:S(2)}) collective-permute-start(bf16[1,80,256]{2,1,0:T(8,128)(2,1)S(1)} %get-tuple-element.71), channel_id=1, source_target_pairs={{4,0},{8,1},{5,4},{9,5},{1,8},{13,9},{6,2},{10,3},{7,6},{11,7},{3,... | collective-permute-start | bytes 122888 | tf_op jit(solution)/shard_map/ppermute | solution.py:385

commit v24 on v23

--- a/solution.py
+++ b/solution.py
@@ -218,7 +218,7 @@
 def conv_kernel(window, above, below, weight, out):
     width = out.shape[1]
     band_rows, channels = out.shape[0], out.shape[2]
-    grid = jnp.concatenate([above[...], window[...], below[...]], axis=0).astype(F32)
+    grid = jnp.concatenate([above[...], window[...], below[:1]], axis=0).astype(F32)
     active = jnp.maximum(grid, 0.0)
     total = grid[1 : 1 + band_rows, EDGE : EDGE + width, :].reshape(band_rows * width, channels)
     for column in range(3):
@@ -316,7 +316,8 @@
         )
 
     steps = range(1, tiles)
-    left = [fetched(left_tokens[0], step) for step in range(tiles)]
+    left = [fetched(left_tokens[0], step) for step in reversed(range(tiles))][::-1]
+    left[0] = tied(left[0], left[1:])
     self_out, reassemble, cross_out, right_own, self_qkv, cross_qkv, taps, half = staged(
         [self_out, reassemble, cross_out, right_tokens[0], self_qkv, cross_qkv, taps]
     )
@@ -381,8 +382,8 @@
     )
     received = [from_tile(part, s) for s, part in enumerate(maps) if s > 0]
     (features,) = run_kernel(add_kernel, "add", [(window, BF16)], [carried, maps[0], *received])
+    below = lax.ppermute(features[:2], both, up)
     above = lax.ppermute(features[-1:], both, down)
-    below = lax.ppermute(features[:1], both, up)
     features = lax.ppermute(features, both, back)
     (joined,) = run_kernel(
         conv_kernel,

time: 70.1 us -> 68.2 us (0.973)
  starting transfers between devices: 33 us -> 29.1 us
  waiting for transfers between devices: 20.3 us -> 22.2 us
    ppermute x2, starting transfers between devices: 6.95 us -> 4.46 us  [neighbours(): lax.ppermute(pack, 'blk', [(g + (i + s) % span, g + i) for g, i in ring])]
    ppermute x4, waiting for transfers between devices: 6.48 us -> 7.87 us  [from_tile(): lax.ppermute(value, 'tile', [((i + step) % tiles, i) for i in range(tiles)])]
  transfers between devices with their start and end apart: 17 -> 17, of which waited for: 7 -> 6; matrix products, arithmetic and copies ran while one was open for 0% -> 0% of each run, Pallas kernels for 16% -> 17%
where the time goes in v24:
time: 68.2 us; the launch traced here: 68 us
  starting transfers between devices  29.1 us (43%)
  waiting for transfers between devices  22.2 us (33%)
  Pallas kernels  16.4 us (24%)
    pallas_call x12, Pallas kernels, run_kernel(): pl.pallas_call(kernel, out_shape=[jax.ShapeDtypeStruct(*s) for s in shape...  16.4 us
    ppermute x4, waiting for transfers between devices, from_tile(): lax.ppermute(value, 'tile', [((i + step) % tiles, i) for i in range(tiles)])  7.87 us
    ppermute x2, starting transfers between devices, fetched(): return lax.ppermute(value, ('blk', 'tile', 'pair'), pairs)  7.55 us
    ppermute x2, waiting for transfers between devices, fetched(): return lax.ppermute(value, ('blk', 'tile', 'pair'), pairs)  6.44 us
    ppermute x1, starting transfers between devices, body(): features = lax.ppermute(features, both, back)  5.63 us
    ppermute x1, starting transfers between devices, body(): right_pack = lax.ppermute(right_pack, both, there)  4.83 us
    ppermute x1, waiting for transfers between devices, body(): below = lax.ppermute(features[:2], both, up)  4.47 us
    ppermute x2, starting transfers between devices, neighbours(): lax.ppermute(pack, 'blk', [(g + (i + s) % span, g + i) for g, i in ring])  4.46 us
  transfers between devices with their start and end apart: 17, of which 6 were waited for; matrix products, arithmetic and copies ran while one was open for 0% of the time, Pallas kernels for 17%

profile of v24, /device:TPU:1, one launch (start us, length us, event | category | flops | bytes accessed | tf_op | source)
XLA Modules:
  0.0 68.0 jit_solution(231136952197339676)
XLA Ops:
  0.0 5.6 %collective-permute-start.1 = (bf16[384,384]{1,0:T(8,128)(2,1)}, bf16[384,384]{1,0:T(8,128)(2,1)S(1)}, u32[]{:S(2)}, u32[]{:S(2)}) collective-permute-start(bf16[384,384]{1,0:T(8,128)(2,1)} %bitcast.10), channel_id=1, source_target_pairs={{2,0},{0,2},{3,12},{1,14},{6,4},{4,6},{7,8},{5,10},{10,5},{8,7},{1... | collective-permute-start | bytes 884744 | tf_op jit(solution)/shard_map/ppermute | solution.py:267
  5.6 1.9 %collective-permute-start = (bf16[384,384]{1,0:T(8,128)(2,1)}, bf16[384,384]{1,0:T(8,128)(2,1)S(1)}, u32[]{:S(2)}, u32[]{:S(2)}) collective-permute-start(bf16[384,384]{1,0:T(8,128)(2,1)} %bitcast.11), channel_id=1, source_target_pairs={{0,0},{2,2},{1,12},{3,14},{4,4},{6,6},{5,8},{7,10},{8,5},{10,7},{9... | collective-permute-start | bytes 884744 | tf_op jit(solution)/shard_map/ppermute | solution.py:267
  7.6 2.6 %stage.1 = (bf16[256,768]{1,0:T(8,128)(2,1)S(1)}, bf16[384,256]{1,0:T(8,128)(2,1)S(1)}, bf16[256,768]{1,0:T(8,128)(2,1)S(1)}, bf16[384,384]{1,0:T(8,128)(2,1)S(1...) custom-call(bf16[256,768]{1,0:T(8,128)(2,1)} %refs_0_.1, ...), custom_call_target="tpu_custom_call" | custom-call | tf_op jit(solution)/shard_map/stage/pallas_call | solution.py:22
  10.5 6.4 %collective-permute-done.refs_0_.refs_4_ = bf16[384,384]{1,0:T(8,128)(2,1)S(1)} collective-permute-done((bf16[384,384]{1,0:T(8,128)(2,1)}, bf16[384,384]{1,0:T(8,128)(2,1)S(1)}, u32[]{:S(2)}, u32[]{:S(2)}) %collective-permute-start) | collective-permute-done | bytes 294944 | tf_op jit(solution)/shard_map/ppermute | solution.py:267
  16.9 1.1 %project.2 = (bf16[384,256]{1,0:T(8,128)(2,1)S(1)}, bf16[384,512]{1,0:T(8,128)(2,1)S(1)}) custom-call(bf16[384,384]{1,0:T(8,128)(2,1)S(1)} %collective-permute-done.refs_0_.refs_4_, bf16[384,384]{1,0:T(8,128)(2,1)S(1)} %collective-permute-done.1.refs_1_.refs_5_, bf16[3,2,384,256]{3,2,1,0:T(8,128)(2,1)S(1)} %bitcast.7), custom_call_target="tpu_custom_call" | custom-call | tf_op jit(solution)/shard_map/project/pallas_call | solution.py:22
  18.0 2.4 %collective-permute-start.3 = (bf16[384,512]{1,0:T(8,128)(2,1)S(1)}, bf16[384,512]{1,0:T(8,128)(2,1)S(1)}, u32[]{:S(2)}, u32[]{:S(2)}) collective-permute-start(bf16[384,512]{1,0:T(8,128)(2,1)S(1)} %get-tuple-element.42.refs_0_), channel_id=1, source_target_pairs={{4,0},{0,4},{12,8},{8,12},{5,1},{1,5},{13,9},{9,13},{6,2},{2,6},{1... | collective-permute-start | bytes 1179656 | tf_op jit(solution)/shard_map/ppermute | solution.py:281
  20.4 0.8 %project.3 = bf16[384,512]{1,0:T(8,128)(2,1)S(1)} custom-call(bf16[384,384]{1,0:T(8,128)(2,1)S(1)} %get-tuple-element.46.refs_0_, bf16[384,384]{1,0:T(8,128)(2,1)S(1)} %collective-permute-done.5.refs_1_, bf16[3,2,384,256]{3,2,1,0:T(8,128)(2,1)S(1)} %bitcast.5), custom_call_target="tpu_custom_call" | custom-call | tf_op jit(solution)/shard_map/project/pallas_call | solution.py:22
  21.7 4.8 %collective-permute-start.8 = (bf16[384,512]{1,0:T(8,128)(2,1)S(1)}, bf16[384,512]{1,0:T(8,128)(2,1)S(1)}, u32[]{:S(2)}, u32[]{:S(2)}) collective-permute-start(bf16[384,512]{1,0:T(8,128)(2,1)S(1)} %project.3), channel_id=1, source_target_pairs={{0,0},{1,12},{4,4},{5,8},{8,5},{9,9},{12,1},{13,13},{2,2},{3,14},{... | collective-permute-start | bytes 1179656 | tf_op jit(solution)/shard_map/ppermute | solution.py:332
  27.2 2.2 %begin.1 = (f32[4,384,128]{2,1,0:T(8,128)S(1)}, f32[4,384,1]{2,1,0:T(8,128)S(1)}) custom-call(bf16[384,256]{1,0:T(8,128)(2,1)S(1)} %get-tuple-element.41.query, bf16[384,512]{1,0:T(8,128)(2,1)S(1)} %get-tuple-element.42.refs_0_, bf16[384,512]{1,0:T(8,128)(2,1)S(1)} %collective-permute-done.3.refs_1_), custom_call_target="tpu_custom_call" | custom-call | tf_op jit(solution)/shard_map/begin/pallas_call | solution.py:22
  29.8 3.1 %collective-permute-done.8.refs_0_ = bf16[384,512]{1,0:T(8,128)(2,1)S(1)} collective-permute-done((bf16[384,512]{1,0:T(8,128)(2,1)S(1)}, bf16[384,512]{1,0:T(8,128)(2,1)S(1)}, u32[]{:S(2)}, u32[]{:S(2)}) %collective-permute-start.8) | collective-permute-done | bytes 393248 | tf_op jit(solution)/shard_map/ppermute | solution.py:332
  32.9 2.1 %collective-permute-start.10 = (bf16[384,512]{1,0:T(8,128)(2,1)S(1)}, bf16[384,512]{1,0:T(8,128)(2,1)S(1)}, u32[]{:S(2)}, u32[]{:S(2)}) collective-permute-start(bf16[384,512]{1,0:T(8,128)(2,1)S(1)} %collective-permute-done.8.refs_0_), channel_id=1, source_target_pairs={{4,0},{0,4},{12,8},{8,12},{5,1},{1,5},{13,9},{9,13},{6,2},{2,6},{1... | collective-permute-start | bytes 1179656 | tf_op jit(solution)/shard_map/ppermute | solution.py:281
  35.0 2.6 %end.1.refs_0_ = bf16[384,256]{1,0:T(8,128)(2,1)S(1)} custom-call(bf16[384,256]{1,0:T(8,128)(2,1)S(1)} %get-tuple-element.41.query, bf16[384,512]{1,0:T(8,128)(2,1)S(1)} %collective-permute-done.2.refs_0_, bf16[384,512]{1,0:T(8,128)(2,1)S(1)} %collective-permute-done.4.refs_1_, f32[4,384,128]{2,1,0:T(8,128)S(1)} %get-tuple-element.54.refs_2_, ...), custom_call_target="tpu_custom_call" | custom-call | tf_op jit(solution)/shard_map/end/pallas_call | solution.py:22
  37.6 1.3 %collective-permute-start.9 = (bf16[384,256]{1,0:T(8,128)(2,1)S(1)}, bf16[384,256]{1,0:T(8,128)(2,1)S(1)}, u32[]{:S(2)}, u32[]{:S(2)}) collective-permute-start(bf16[384,256]{1,0:T(8,128)(2,1)S(1)} %end.1.refs_0_), channel_id=1, source_target_pairs={{2,0},{0,2},{3,1},{1,3},{6,4},{4,6},{7,5},{5,7},{10,8},{8,10},{11,... | collective-permute-start | bytes 589832 | tf_op jit(solution)/shard_map/ppermute | solution.py:273
  38.9 4.2 %collective-permute-done.9.refs_1_ = bf16[384,256]{1,0:T(8,128)(2,1)S(1)} collective-permute-done((bf16[384,256]{1,0:T(8,128)(2,1)S(1)}, bf16[384,256]{1,0:T(8,128)(2,1)S(1)}, u32[]{:S(2)}, u32[]{:S(2)}) %collective-permute-start.9) | collective-permute-done | bytes 196640 | tf_op jit(solution)/shard_map/ppermute | solution.py:273
  43.1 0.5 collective-permute-start.12
  43.7 1.5 %update.1 = (bf16[2,384,384]{2,1,0:T(8,128)(2,1)S(1)}, bf16[384,256]{1,0:T(8,128)(2,1)S(1)}) custom-call(bf16[384,256]{1,0:T(8,128)(2,1)S(1)} %end.1.refs_0_, bf16[384,256]{1,0:T(8,128)(2,1)S(1)} %collective-permute-done.9.refs_1_, bf16[256,768]{1,0:T(8,128)(2,1)S(1)} %get-tuple-element.59.refs_2_, bf16[256,768]{1,0:T(8,128)(2,1)S(1)} %get-tuple-element.60.refs_3_, ...), custom_call_target="tpu_custom_call" | custom-call | tf_op jit(solution)/shard_map/update/pallas_call | solution.py:22
  45.4 3.8 %end_map.1 = (bf16[3,80,256]{2,1,0:T(8,128)(2,1)S(1)}, bf16[3,80,256]{2,1,0:T(8,128)(2,1)S(1)}) custom-call(bf16[384,256]{1,0:T(8,128)(2,1)S(1)} %get-tuple-element.62.query, bf16[384,512]{1,0:T(8,128)(2,1)S(1)} %collective-permute-done.8.refs_0_, bf16[384,512]{1,0:T(8,128)(2,1)S(1)} %collective-permute-done.10.refs_1_, ...), custom_call_target="tpu_custom_call" | custom-call | tf_op jit(solution)/shard_map/end_map/pallas_call | solution.py:22
  49.3 0.8 %collective-permute-start.13 = (bf16[3,80,256]{2,1,0:T(8,128)(2,1)S(1)}, bf16[3,80,256]{2,1,0:T(8,128)(2,1)S(1)}, u32[]{:S(2)}, u32[]{:S(2)}) collective-permute-start(bf16[3,80,256]{2,1,0:T(8,128)(2,1)S(1)} %get-tuple-element.68), channel_id=1, source_target_pairs={{2,0},{0,2},{3,1},{1,3},{6,4},{4,6},{7,5},{5,7},{10,8},{8,10},{11,... | collective-permute-start | bytes 368648 | tf_op jit(solution)/shard_map/ppermute | solution.py:273
  50.5 3.6 %collective-permute-done.13.refs_2_ = bf16[3,80,256]{2,1,0:T(8,128)(2,1)S(1)} collective-permute-done((bf16[3,80,256]{2,1,0:T(8,128)(2,1)S(1)}, bf16[3,80,256]{2,1,0:T(8,128)(2,1)S(1)}, u32[]{:S(2)}, u32[]{:S(2)}) %collective-permute-start.13) | collective-permute-done | bytes 122912 | tf_op jit(solution)/shard_map/ppermute | solution.py:273
  54.2 5.6 %collective-permute-start.14 = (bf16[3,80,256]{2,1,0:T(8,128)(2,1)S(1)}, bf16[3,80,256]{2,1,0:T(8,128)(2,1)S(1)}, u32[]{:S(2)}, u32[]{:S(2)}) collective-permute-start(bf16[3,80,256]{2,1,0:T(8,128)(2,1)S(1)} %add.1), channel_id=1, source_target_pairs={{0,0},{12,1},{4,4},{8,5},{5,8},{9,9},{1,12},{13,13},{2,2},{14,3},{... | collective-permute-start | bytes 368648 | tf_op jit(solution)/shard_map/ppermute | solution.py:387
  59.8 1.9 %collective-permute-start.16 = (bf16[2,80,256]{2,1,0:T(8,128)(2,1)S(1)}, bf16[2,80,256]{2,1,0:T(8,128)(2,1)S(1)}, u32[]{:S(2)}, u32[]{:S(2)}) collective-permute-start(bf16[2,80,256]{2,1,0:T(8,128)(2,1)S(1)} %slice.9), channel_id=1, source_target_pairs={{4,0},{8,1},{5,4},{9,5},{1,8},{13,9},{6,2},{10,3},{7,6},{11,7},{3,... | collective-permute-start | bytes 245768 | tf_op jit(solution)/shard_map/ppermute | solution.py:385
  61.7 0.7 collective-permute-start.15
  62.4 4.5 %collective-permute-done.16.below = bf16[2,80,256]{2,1,0:T(8,128)(2,1)S(1)} collective-permute-done((bf16[2,80,256]{2,1,0:T(8,128)(2,1)S(1)}, bf16[2,80,256]{2,1,0:T(8,128)(2,1)S(1)}, u32[]{:S(2)}, u32[]{:S(2)}) %collective-permute-start.16) | collective-permute-done | bytes 81952 | tf_op jit(solution)/shard_map/ppermute | solution.py:385
  66.9 1.1 %join.1 = bf16[3,64,256]{2,1,0:T(8,128)(2,1)} custom-call(bf16[3,80,256]{2,1,0:T(8,128)(2,1)S(1)} %collective-permute-done.14.window, bf16[1,80,256]{2,1,0:T(8,128)(2,1)S(1)} %collective-permute-done.15.above, bf16[2,80,256]{2,1,0:T(8,128)(2,1)S(1)} %collective-permute-done.16.below, bf16[3,3,256,256]{3,2,1,0:T(8,128)(2,1)S(1)} %get-tuple-element.72.weight), custom_call_target="tpu_custom_call" | custom-call | tf_op jit(solution)/shard_map/join/pallas_call | solution.py:22
  (26 shorter events, 2.6 us)
Async XLA Ops:
  0.0 10.5 %collective-permute-start.1 = (bf16[384,384]{1,0:T(8,128)(2,1)}, bf16[384,384]{1,0:T(8,128)(2,1)S(1)}, u32[]{:S(2)}, u32[]{:S(2)}) collective-permute-start(bf16[384,384]{1,0:T(8,128)(2,1)} %bitcast.10), channel_id=1, source_target_pairs={{2,0},{0,2},{3,12},{1,14},{6,4},{4,6},{7,8},{5,10},{10,5},{8,7},{1... | collective-permute-start | bytes 884744 | tf_op jit(solution)/shard_map/ppermute | solution.py:267
  5.6 11.3 %collective-permute-start = (bf16[384,384]{1,0:T(8,128)(2,1)}, bf16[384,384]{1,0:T(8,128)(2,1)S(1)}, u32[]{:S(2)}, u32[]{:S(2)}) collective-permute-start(bf16[384,384]{1,0:T(8,128)(2,1)} %bitcast.11), channel_id=1, source_target_pairs={{0,0},{2,2},{1,12},{3,14},{4,4},{6,6},{5,8},{7,10},{8,5},{10,7},{9... | collective-permute-start | bytes 884744 | tf_op jit(solution)/shard_map/ppermute | solution.py:267
  7.6 2.6 %copy-start = (bf16[1,384,384]{2,1,0:T(8,128)(2,1)S(1)}, bf16[1,384,384]{2,1,0:T(8,128)(2,1)}, u32[]{:S(2)}) copy-start(bf16[1,384,384]{2,1,0:T(8,128)(2,1)} %param.9) | copy-start | bytes 884740
  10.1 10.2 %collective-permute-start.5 = (bf16[384,384]{1,0:T(8,128)(2,1)S(1)}, bf16[384,384]{1,0:T(8,128)(2,1)S(1)}, u32[]{:S(2)}, u32[]{:S(2)}) collective-permute-start(bf16[384,384]{1,0:T(8,128)(2,1)S(1)} %bitcast.9), channel_id=1, source_target_pairs={{2,0},{0,2},{3,1},{1,3},{6,4},{4,6},{7,5},{5,7},{10,8},{8,10},{11,... | collective-permute-start | bytes 884744 | tf_op jit(solution)/shard_map/ppermute | solution.py:273
  18.0 8.6 %collective-permute-start.3 = (bf16[384,512]{1,0:T(8,128)(2,1)S(1)}, bf16[384,512]{1,0:T(8,128)(2,1)S(1)}, u32[]{:S(2)}, u32[]{:S(2)}) collective-permute-start(bf16[384,512]{1,0:T(8,128)(2,1)S(1)} %get-tuple-element.42.refs_0_), channel_id=1, source_target_pairs={{4,0},{0,4},{12,8},{8,12},{5,1},{1,5},{13,9},{9,13},{6,2},{2,6},{1... | collective-permute-start | bytes 1179656 | tf_op jit(solution)/shard_map/ppermute | solution.py:281
  21.2 5.9 %collective-permute-start.6 = (bf16[192,768]{1,0:T(8,128)(2,1)S(1)}, bf16[192,768]{1,0:T(8,128)(2,1)S(1)}, u32[]{:S(2)}, u32[]{:S(2)}) collective-permute-start(bf16[192,768]{1,0:T(8,128)(2,1)S(1)} %get-tuple-element.49), channel_id=1, source_target_pairs={{2,0},{0,2},{3,1},{1,3},{6,4},{4,6},{7,5},{5,7},{10,8},{8,10},{11,... | collective-permute-start | bytes 884744 | tf_op jit(solution)/shard_map/ppermute | solution.py:273
  21.7 11.2 %collective-permute-start.8 = (bf16[384,512]{1,0:T(8,128)(2,1)S(1)}, bf16[384,512]{1,0:T(8,128)(2,1)S(1)}, u32[]{:S(2)}, u32[]{:S(2)}) collective-permute-start(bf16[384,512]{1,0:T(8,128)(2,1)S(1)} %project.3), channel_id=1, source_target_pairs={{0,0},{1,12},{4,4},{5,8},{8,5},{9,9},{12,1},{13,13},{2,2},{3,14},{... | collective-permute-start | bytes 1179656 | tf_op jit(solution)/shard_map/ppermute | solution.py:332
  26.5 6.4 %collective-permute-start.2 = (bf16[384,512]{1,0:T(8,128)(2,1)S(1)}, bf16[384,512]{1,0:T(8,128)(2,1)S(1)}, u32[]{:S(2)}, u32[]{:S(2)}) collective-permute-start(bf16[384,512]{1,0:T(8,128)(2,1)S(1)} %get-tuple-element.42.refs_0_), channel_id=1, source_target_pairs={{1,0},{0,1},{3,2},{2,3},{5,4},{4,5},{7,6},{6,7},{9,8},{8,9},{11,10... | collective-permute-start | bytes 1179656 | tf_op jit(solution)/shard_map/ppermute | solution.py:287
  26.6 6.3 %collective-permute-start.4 = (bf16[384,512]{1,0:T(8,128)(2,1)S(1)}, bf16[384,512]{1,0:T(8,128)(2,1)S(1)}, u32[]{:S(2)}, u32[]{:S(2)}) collective-permute-start(bf16[384,512]{1,0:T(8,128)(2,1)S(1)} %collective-permute-done.3.refs_1_), channel_id=1, source_target_pairs={{1,0},{0,1},{3,2},{2,3},{5,4},{4,5},{7,6},{6,7},{9,8},{8,9},{11,10... | collective-permute-start | bytes 1179656 | tf_op jit(solution)/shard_map/ppermute | solution.py:287
  27.1 2.3 %collective-permute-start.7 = (bf16[192,768]{1,0:T(8,128)(2,1)S(1)}, bf16[192,768]{1,0:T(8,128)(2,1)S(1)}, u32[]{:S(2)}, u32[]{:S(2)}) collective-permute-start(bf16[192,768]{1,0:T(8,128)(2,1)S(1)} %collective-permute-done.6.refs_0_), channel_id=1, source_target_pairs={{1,0},{0,1},{3,2},{2,3},{5,4},{4,5},{7,6},{6,7},{9,8},{8,9},{11,10... | collective-permute-start | bytes 884744 | tf_op jit(solution)/shard_map/ppermute | solution.py:287
  32.9 10.2 %collective-permute-start.10 = (bf16[384,512]{1,0:T(8,128)(2,1)S(1)}, bf16[384,512]{1,0:T(8,128)(2,1)S(1)}, u32[]{:S(2)}, u32[]{:S(2)}) collective-permute-start(bf16[384,512]{1,0:T(8,128)(2,1)S(1)} %collective-permute-done.8.refs_0_), channel_id=1, source_target_pairs={{4,0},{0,4},{12,8},{8,12},{5,1},{1,5},{13,9},{9,13},{6,2},{2,6},{1... | collective-permute-start | bytes 1179656 | tf_op jit(solution)/shard_map/ppermute | solution.py:281
  37.6 5.5 %collective-permute-start.9 = (bf16[384,256]{1,0:T(8,128)(2,1)S(1)}, bf16[384,256]{1,0:T(8,128)(2,1)S(1)}, u32[]{:S(2)}, u32[]{:S(2)}) collective-permute-start(bf16[384,256]{1,0:T(8,128)(2,1)S(1)} %end.1.refs_0_), channel_id=1, source_target_pairs={{2,0},{0,2},{3,1},{1,3},{6,4},{4,6},{7,5},{5,7},{10,8},{8,10},{11,... | collective-permute-start | bytes 589832 | tf_op jit(solution)/shard_map/ppermute | solution.py:273
  43.1 2.0 %collective-permute-start.11 = (bf16[384,512]{1,0:T(8,128)(2,1)S(1)}, bf16[384,512]{1,0:T(8,128)(2,1)S(1)}, u32[]{:S(2)}, u32[]{:S(2)}) collective-permute-start(bf16[384,512]{1,0:T(8,128)(2,1)S(1)} %collective-permute-done.8.refs_0_), channel_id=1, source_target_pairs={{1,0},{0,1},{3,2},{2,3},{5,4},{4,5},{7,6},{6,7},{9,8},{8,9},{11,10... | collective-permute-start | bytes 1179656 | tf_op jit(solution)/shard_map/ppermute | solution.py:287
  43.1 2.3 %collective-permute-start.12 = (bf16[384,512]{1,0:T(8,128)(2,1)S(1)}, bf16[384,512]{1,0:T(8,128)(2,1)S(1)}, u32[]{:S(2)}, u32[]{:S(2)}) collective-permute-start(bf16[384,512]{1,0:T(8,128)(2,1)S(1)} %collective-permute-done.10.refs_1_), channel_id=1, source_target_pairs={{1,0},{0,1},{3,2},{2,3},{5,4},{4,5},{7,6},{6,7},{9,8},{8,9},{11,10... | collective-permute-start | bytes 1179656 | tf_op jit(solution)/shard_map/ppermute | solution.py:287
  49.3 4.8 %collective-permute-start.13 = (bf16[3,80,256]{2,1,0:T(8,128)(2,1)S(1)}, bf16[3,80,256]{2,1,0:T(8,128)(2,1)S(1)}, u32[]{:S(2)}, u32[]{:S(2)}) collective-permute-start(bf16[3,80,256]{2,1,0:T(8,128)(2,1)S(1)} %get-tuple-element.68), channel_id=1, source_target_pairs={{2,0},{0,2},{3,1},{1,3},{6,4},{4,6},{7,5},{5,7},{10,8},{8,10},{11,... | collective-permute-start | bytes 368648 | tf_op jit(solution)/shard_map/ppermute | solution.py:273
  54.2 12.8 %collective-permute-start.14 = (bf16[3,80,256]{2,1,0:T(8,128)(2,1)S(1)}, bf16[3,80,256]{2,1,0:T(8,128)(2,1)S(1)}, u32[]{:S(2)}, u32[]{:S(2)}) collective-permute-start(bf16[3,80,256]{2,1,0:T(8,128)(2,1)S(1)} %add.1), channel_id=1, source_target_pairs={{0,0},{12,1},{4,4},{8,5},{5,8},{9,9},{1,12},{13,13},{2,2},{14,3},{... | collective-permute-start | bytes 368648 | tf_op jit(solution)/shard_map/ppermute | solution.py:387
  59.8 7.1 %collective-permute-start.16 = (bf16[2,80,256]{2,1,0:T(8,128)(2,1)S(1)}, bf16[2,80,256]{2,1,0:T(8,128)(2,1)S(1)}, u32[]{:S(2)}, u32[]{:S(2)}) collective-permute-start(bf16[2,80,256]{2,1,0:T(8,128)(2,1)S(1)} %slice.9), channel_id=1, source_target_pairs={{4,0},{8,1},{5,4},{9,5},{1,8},{13,9},{6,2},{10,3},{7,6},{11,7},{3,... | collective-permute-start | bytes 245768 | tf_op jit(solution)/shard_map/ppermute | solution.py:385
  61.7 0.7 collective-permute-start.15

commit v25 on v24

--- a/solution.py
+++ b/solution.py
@@ -137,7 +137,9 @@
 
 
 def add_kernel(*refs):
-    refs[-1][...] = sum(ref[...].astype(F32) for ref in refs[:-1]).astype(BF16)
+    total = sum(ref[...].astype(F32) for ref in refs[:-2]).astype(BF16)
+    refs[-2][...] = total
+    refs[-1][...] = jnp.concatenate([total, total[:1]], axis=0)
 
 
 def stage_kernel(*refs, cores):
@@ -381,8 +383,11 @@
         [pltpu.VMEM(board, F32)],
     )
     received = [from_tile(part, s) for s, part in enumerate(maps) if s > 0]
-    (features,) = run_kernel(add_kernel, "add", [(window, BF16)], [carried, maps[0], *received])
-    below = lax.ppermute(features[:2], both, up)
+    longer = (window[0] + 1, *window[1:])
+    features, raised = run_kernel(
+        add_kernel, "add", [(window, BF16), (longer, BF16)], [carried, maps[0], *received]
+    )
+    below = lax.ppermute(raised, both, up)
     above = lax.ppermute(features[-1:], both, down)
     features = lax.ppermute(features, both, back)
     (joined,) = run_kernel(

time: 68.2 us -> 67.6 us (level)
  starting transfers between devices: 29.1 us -> 27.9 us
  waiting for transfers between devices: 22.2 us -> 22.9 us
    ppermute x1, waiting for transfers between devices: 0.01 us -> 5.16 us  [body(): features = lax.ppermute(features, both, back)]
    ppermute x1, waiting for transfers between devices: 4.47 us -> 0.01 us  [body(): below = lax.ppermute(raised, both, up)]
    ppermute x1, starting transfers between devices: 5.63 us -> 2.13 us  [body(): features = lax.ppermute(features, both, back)]
    ppermute x1, starting transfers between devices: 1.92 us -> 4.17 us  [body(): below = lax.ppermute(raised, both, up)]
where the time goes in v25:
time: 67.6 us; the launch traced here: 67.4 us
  starting transfers between devices  27.9 us (41%)
  waiting for transfers between devices  22.9 us (34%)
  Pallas kernels  16.4 us (24%)
    pallas_call x12, Pallas kernels, run_kernel(): pl.pallas_call(kernel, out_shape=[jax.ShapeDtypeStruct(*s) for s in shape...  16.4 us
    ppermute x4, waiting for transfers between devices, from_tile(): lax.ppermute(value, 'tile', [((i + step) % tiles, i) for i in range(tiles)])  7.87 us
    ppermute x2, starting transfers between devices, fetched(): return lax.ppermute(value, ('blk', 'tile', 'pair'), pairs)  7.55 us
    ppermute x2, waiting for transfers between devices, fetched(): return lax.ppermute(value, ('blk', 'tile', 'pair'), pairs)  6.44 us
    ppermute x1, waiting for transfers between devices, body(): features = lax.ppermute(features, both, back)  5.16 us
    ppermute x1, starting transfers between devices, body(): right_pack = lax.ppermute(right_pack, both, there)  4.83 us
    ppermute x2, starting transfers between devices, neighbours(): lax.ppermute(pack, 'blk', [(g + (i + s) % span, g + i) for g, i in ring])  4.46 us
    ppermute x1, starting transfers between devices, body(): below = lax.ppermute(raised, both, up)  4.17 us
  transfers between devices with their start and end apart: 17, of which 6 were waited for; matrix products, arithmetic and copies ran while one was open for 0% of the time, Pallas kernels for 17%

profile of v25, /device:TPU:1, one launch (start us, length us, event | category | flops | bytes accessed | tf_op | source)
XLA Modules:
  0.0 67.4 jit_solution(12998038384523347037)
XLA Ops:
  0.0 5.6 %collective-permute-start.1 = (bf16[384,384]{1,0:T(8,128)(2,1)}, bf16[384,384]{1,0:T(8,128)(2,1)S(1)}, u32[]{:S(2)}, u32[]{:S(2)}) collective-permute-start(bf16[384,384]{1,0:T(8,128)(2,1)} %bitcast.10), channel_id=1, source_target_pairs={{2,0},{0,2},{3,12},{1,14},{6,4},{4,6},{7,8},{5,10},{10,5},{8,7},{1... | collective-permute-start | bytes 884744 | tf_op jit(solution)/shard_map/ppermute | solution.py:269
  5.6 1.9 %collective-permute-start = (bf16[384,384]{1,0:T(8,128)(2,1)}, bf16[384,384]{1,0:T(8,128)(2,1)S(1)}, u32[]{:S(2)}, u32[]{:S(2)}) collective-permute-start(bf16[384,384]{1,0:T(8,128)(2,1)} %bitcast.11), channel_id=1, source_target_pairs={{0,0},{2,2},{1,12},{3,14},{4,4},{6,6},{5,8},{7,10},{8,5},{10,7},{9... | collective-permute-start | bytes 884744 | tf_op jit(solution)/shard_map/ppermute | solution.py:269
  7.6 2.6 %stage.1 = (bf16[256,768]{1,0:T(8,128)(2,1)S(1)}, bf16[384,256]{1,0:T(8,128)(2,1)S(1)}, bf16[256,768]{1,0:T(8,128)(2,1)S(1)}, bf16[384,384]{1,0:T(8,128)(2,1)S(1...) custom-call(bf16[256,768]{1,0:T(8,128)(2,1)} %refs_0_.1, ...), custom_call_target="tpu_custom_call" | custom-call | tf_op jit(solution)/shard_map/stage/pallas_call | solution.py:22
  10.5 6.4 %collective-permute-done.refs_0_.refs_4_ = bf16[384,384]{1,0:T(8,128)(2,1)S(1)} collective-permute-done((bf16[384,384]{1,0:T(8,128)(2,1)}, bf16[384,384]{1,0:T(8,128)(2,1)S(1)}, u32[]{:S(2)}, u32[]{:S(2)}) %collective-permute-start) | collective-permute-done | bytes 294944 | tf_op jit(solution)/shard_map/ppermute | solution.py:269
  16.9 1.1 %project.2 = (bf16[384,256]{1,0:T(8,128)(2,1)S(1)}, bf16[384,512]{1,0:T(8,128)(2,1)S(1)}) custom-call(bf16[384,384]{1,0:T(8,128)(2,1)S(1)} %collective-permute-done.refs_0_.refs_4_, bf16[384,384]{1,0:T(8,128)(2,1)S(1)} %collective-permute-done.1.refs_1_.refs_5_, bf16[3,2,384,256]{3,2,1,0:T(8,128)(2,1)S(1)} %bitcast.7), custom_call_target="tpu_custom_call" | custom-call | tf_op jit(solution)/shard_map/project/pallas_call | solution.py:22
  18.0 2.4 %collective-permute-start.3 = (bf16[384,512]{1,0:T(8,128)(2,1)S(1)}, bf16[384,512]{1,0:T(8,128)(2,1)S(1)}, u32[]{:S(2)}, u32[]{:S(2)}) collective-permute-start(bf16[384,512]{1,0:T(8,128)(2,1)S(1)} %get-tuple-element.44.refs_0_), channel_id=1, source_target_pairs={{4,0},{0,4},{12,8},{8,12},{5,1},{1,5},{13,9},{9,13},{6,2},{2,6},{1... | collective-permute-start | bytes 1179656 | tf_op jit(solution)/shard_map/ppermute | solution.py:283
  20.4 0.8 %project.3 = bf16[384,512]{1,0:T(8,128)(2,1)S(1)} custom-call(bf16[384,384]{1,0:T(8,128)(2,1)S(1)} %get-tuple-element.48.refs_0_, bf16[384,384]{1,0:T(8,128)(2,1)S(1)} %collective-permute-done.5.refs_1_, bf16[3,2,384,256]{3,2,1,0:T(8,128)(2,1)S(1)} %bitcast.5), custom_call_target="tpu_custom_call" | custom-call | tf_op jit(solution)/shard_map/project/pallas_call | solution.py:22
  21.7 4.8 %collective-permute-start.8 = (bf16[384,512]{1,0:T(8,128)(2,1)S(1)}, bf16[384,512]{1,0:T(8,128)(2,1)S(1)}, u32[]{:S(2)}, u32[]{:S(2)}) collective-permute-start(bf16[384,512]{1,0:T(8,128)(2,1)S(1)} %project.3), channel_id=1, source_target_pairs={{0,0},{1,12},{4,4},{5,8},{8,5},{9,9},{12,1},{13,13},{2,2},{3,14},{... | collective-permute-start | bytes 1179656 | tf_op jit(solution)/shard_map/ppermute | solution.py:334
  27.2 2.2 %begin.1 = (f32[4,384,128]{2,1,0:T(8,128)S(1)}, f32[4,384,1]{2,1,0:T(8,128)S(1)}) custom-call(bf16[384,256]{1,0:T(8,128)(2,1)S(1)} %get-tuple-element.43.query, bf16[384,512]{1,0:T(8,128)(2,1)S(1)} %get-tuple-element.44.refs_0_, bf16[384,512]{1,0:T(8,128)(2,1)S(1)} %collective-permute-done.3.refs_1_), custom_call_target="tpu_custom_call" | custom-call | tf_op jit(solution)/shard_map/begin/pallas_call | solution.py:22
  29.8 3.1 %collective-permute-done.8.refs_0_ = bf16[384,512]{1,0:T(8,128)(2,1)S(1)} collective-permute-done((bf16[384,512]{1,0:T(8,128)(2,1)S(1)}, bf16[384,512]{1,0:T(8,128)(2,1)S(1)}, u32[]{:S(2)}, u32[]{:S(2)}) %collective-permute-start.8) | collective-permute-done | bytes 393248 | tf_op jit(solution)/shard_map/ppermute | solution.py:334
  32.9 2.1 %collective-permute-start.10 = (bf16[384,512]{1,0:T(8,128)(2,1)S(1)}, bf16[384,512]{1,0:T(8,128)(2,1)S(1)}, u32[]{:S(2)}, u32[]{:S(2)}) collective-permute-start(bf16[384,512]{1,0:T(8,128)(2,1)S(1)} %collective-permute-done.8.refs_0_), channel_id=1, source_target_pairs={{4,0},{0,4},{12,8},{8,12},{5,1},{1,5},{13,9},{9,13},{6,2},{2,6},{1... | collective-permute-start | bytes 1179656 | tf_op jit(solution)/shard_map/ppermute | solution.py:283
  35.0 2.6 %end.1.refs_0_ = bf16[384,256]{1,0:T(8,128)(2,1)S(1)} custom-call(bf16[384,256]{1,0:T(8,128)(2,1)S(1)} %get-tuple-element.43.query, bf16[384,512]{1,0:T(8,128)(2,1)S(1)} %collective-permute-done.2.refs_0_, bf16[384,512]{1,0:T(8,128)(2,1)S(1)} %collective-permute-done.4.refs_1_, f32[4,384,128]{2,1,0:T(8,128)S(1)} %get-tuple-element.56.refs_2_, ...), custom_call_target="tpu_custom_call" | custom-call | tf_op jit(solution)/shard_map/end/pallas_call | solution.py:22
  37.6 1.3 %collective-permute-start.9 = (bf16[384,256]{1,0:T(8,128)(2,1)S(1)}, bf16[384,256]{1,0:T(8,128)(2,1)S(1)}, u32[]{:S(2)}, u32[]{:S(2)}) collective-permute-start(bf16[384,256]{1,0:T(8,128)(2,1)S(1)} %end.1.refs_0_), channel_id=1, source_target_pairs={{2,0},{0,2},{3,1},{1,3},{6,4},{4,6},{7,5},{5,7},{10,8},{8,10},{11,... | collective-permute-start | bytes 589832 | tf_op jit(solution)/shard_map/ppermute | solution.py:275
  38.9 4.2 %collective-permute-done.9.refs_1_ = bf16[384,256]{1,0:T(8,128)(2,1)S(1)} collective-permute-done((bf16[384,256]{1,0:T(8,128)(2,1)S(1)}, bf16[384,256]{1,0:T(8,128)(2,1)S(1)}, u32[]{:S(2)}, u32[]{:S(2)}) %collective-permute-start.9) | collective-permute-done | bytes 196640 | tf_op jit(solution)/shard_map/ppermute | solution.py:275
  43.1 0.5 collective-permute-start.12
  43.7 1.5 %update.1 = (bf16[2,384,384]{2,1,0:T(8,128)(2,1)S(1)}, bf16[384,256]{1,0:T(8,128)(2,1)S(1)}) custom-call(bf16[384,256]{1,0:T(8,128)(2,1)S(1)} %end.1.refs_0_, bf16[384,256]{1,0:T(8,128)(2,1)S(1)} %collective-permute-done.9.refs_1_, bf16[256,768]{1,0:T(8,128)(2,1)S(1)} %get-tuple-element.61.refs_2_, bf16[256,768]{1,0:T(8,128)(2,1)S(1)} %get-tuple-element.62.refs_3_, ...), custom_call_target="tpu_custom_call" | custom-call | tf_op jit(solution)/shard_map/update/pallas_call | solution.py:22
  45.4 3.8 %end_map.1 = (bf16[3,80,256]{2,1,0:T(8,128)(2,1)S(1)}, bf16[3,80,256]{2,1,0:T(8,128)(2,1)S(1)}) custom-call(bf16[384,256]{1,0:T(8,128)(2,1)S(1)} %get-tuple-element.64.query, bf16[384,512]{1,0:T(8,128)(2,1)S(1)} %collective-permute-done.8.refs_0_, bf16[384,512]{1,0:T(8,128)(2,1)S(1)} %collective-permute-done.10.refs_1_, ...), custom_call_target="tpu_custom_call" | custom-call | tf_op jit(solution)/shard_map/end_map/pallas_call | solution.py:22
  49.3 0.8 %collective-permute-start.13 = (bf16[3,80,256]{2,1,0:T(8,128)(2,1)S(1)}, bf16[3,80,256]{2,1,0:T(8,128)(2,1)S(1)}, u32[]{:S(2)}, u32[]{:S(2)}) collective-permute-start(bf16[3,80,256]{2,1,0:T(8,128)(2,1)S(1)} %get-tuple-element.70), channel_id=1, source_target_pairs={{2,0},{0,2},{3,1},{1,3},{6,4},{4,6},{7,5},{5,7},{10,8},{8,10},{11,... | collective-permute-start | bytes 368648 | tf_op jit(solution)/shard_map/ppermute | solution.py:275
  50.5 3.6 %collective-permute-done.13.refs_2_ = bf16[3,80,256]{2,1,0:T(8,128)(2,1)S(1)} collective-permute-done((bf16[3,80,256]{2,1,0:T(8,128)(2,1)S(1)}, bf16[3,80,256]{2,1,0:T(8,128)(2,1)S(1)}, u32[]{:S(2)}, u32[]{:S(2)}) %collective-permute-start.13) | collective-permute-done | bytes 122912 | tf_op jit(solution)/shard_map/ppermute | solution.py:275
  54.1 4.2 %collective-permute-start.16 = (bf16[4,80,256]{2,1,0:T(8,128)(2,1)S(1)}, bf16[4,80,256]{2,1,0:T(8,128)(2,1)S(1)}, u32[]{:S(2)}, u32[]{:S(2)}) collective-permute-start(bf16[4,80,256]{2,1,0:T(8,128)(2,1)S(1)} %get-tuple-element.75), channel_id=1, source_target_pairs={{4,0},{8,1},{5,4},{9,5},{1,8},{13,9},{6,2},{10,3},{7,6},{11,7},{3,... | collective-permute-start | bytes 491528 | tf_op jit(solution)/shard_map/ppermute | solution.py:390
  58.3 2.1 %collective-permute-start.14 = (bf16[3,80,256]{2,1,0:T(8,128)(2,1)S(1)}, bf16[3,80,256]{2,1,0:T(8,128)(2,1)S(1)}, u32[]{:S(2)}, u32[]{:S(2)}) collective-permute-start(bf16[3,80,256]{2,1,0:T(8,128)(2,1)S(1)} %get-tuple-element.74), channel_id=1, source_target_pairs={{0,0},{12,1},{4,4},{8,5},{5,8},{9,9},{1,12},{13,13},{2,2},{14,3},{... | collective-permute-start | bytes 368648 | tf_op jit(solution)/shard_map/ppermute | solution.py:392
  60.5 0.7 collective-permute-start.15
  61.2 5.2 %collective-permute-done.14.window = bf16[3,80,256]{2,1,0:T(8,128)(2,1)S(1)} collective-permute-done((bf16[3,80,256]{2,1,0:T(8,128)(2,1)S(1)}, bf16[3,80,256]{2,1,0:T(8,128)(2,1)S(1)}, u32[]{:S(2)}, u32[]{:S(2)}) %collective-permute-start.14) | collective-permute-done | bytes 122912 | tf_op jit(solution)/shard_map/ppermute | solution.py:392
  66.3 1.0 %join.1 = bf16[3,64,256]{2,1,0:T(8,128)(2,1)} custom-call(bf16[3,80,256]{2,1,0:T(8,128)(2,1)S(1)} %collective-permute-done.14.window, bf16[1,80,256]{2,1,0:T(8,128)(2,1)S(1)} %collective-permute-done.15.above, bf16[4,80,256]{2,1,0:T(8,128)(2,1)S(1)} %collective-permute-done.16.below, bf16[3,3,256,256]{3,2,1,0:T(8,128)(2,1)S(1)} %get-tuple-element.76.weight), custom_call_target="tpu_custom_call" | custom-call | tf_op jit(solution)/shard_map/join/pallas_call | solution.py:22
  (25 shorter events, 2.6 us)
Async XLA Ops:
  0.0 10.5 %collective-permute-start.1 = (bf16[384,384]{1,0:T(8,128)(2,1)}, bf16[384,384]{1,0:T(8,128)(2,1)S(1)}, u32[]{:S(2)}, u32[]{:S(2)}) collective-permute-start(bf16[384,384]{1,0:T(8,128)(2,1)} %bitcast.10), channel_id=1, source_target_pairs={{2,0},{0,2},{3,12},{1,14},{6,4},{4,6},{7,8},{5,10},{10,5},{8,7},{1... | collective-permute-start | bytes 884744 | tf_op jit(solution)/shard_map/ppermute | solution.py:269
  5.6 11.3 %collective-permute-start = (bf16[384,384]{1,0:T(8,128)(2,1)}, bf16[384,384]{1,0:T(8,128)(2,1)S(1)}, u32[]{:S(2)}, u32[]{:S(2)}) collective-permute-start(bf16[384,384]{1,0:T(8,128)(2,1)} %bitcast.11), channel_id=1, source_target_pairs={{0,0},{2,2},{1,12},{3,14},{4,4},{6,6},{5,8},{7,10},{8,5},{10,7},{9... | collective-permute-start | bytes 884744 | tf_op jit(solution)/shard_map/ppermute | solution.py:269
  7.6 2.6 %copy-start = (bf16[1,384,384]{2,1,0:T(8,128)(2,1)S(1)}, bf16[1,384,384]{2,1,0:T(8,128)(2,1)}, u32[]{:S(2)}) copy-start(bf16[1,384,384]{2,1,0:T(8,128)(2,1)} %param.9) | copy-start | bytes 884740
  10.1 10.2 %collective-permute-start.5 = (bf16[384,384]{1,0:T(8,128)(2,1)S(1)}, bf16[384,384]{1,0:T(8,128)(2,1)S(1)}, u32[]{:S(2)}, u32[]{:S(2)}) collective-permute-start(bf16[384,384]{1,0:T(8,128)(2,1)S(1)} %bitcast.9), channel_id=1, source_target_pairs={{2,0},{0,2},{3,1},{1,3},{6,4},{4,6},{7,5},{5,7},{10,8},{8,10},{11,... | collective-permute-start | bytes 884744 | tf_op jit(solution)/shard_map/ppermute | solution.py:275
  18.0 8.6 %collective-permute-start.3 = (bf16[384,512]{1,0:T(8,128)(2,1)S(1)}, bf16[384,512]{1,0:T(8,128)(2,1)S(1)}, u32[]{:S(2)}, u32[]{:S(2)}) collective-permute-start(bf16[384,512]{1,0:T(8,128)(2,1)S(1)} %get-tuple-element.44.refs_0_), channel_id=1, source_target_pairs={{4,0},{0,4},{12,8},{8,12},{5,1},{1,5},{13,9},{9,13},{6,2},{2,6},{1... | collective-permute-start | bytes 1179656 | tf_op jit(solution)/shard_map/ppermute | solution.py:283
  21.2 5.9 %collective-permute-start.6 = (bf16[192,768]{1,0:T(8,128)(2,1)S(1)}, bf16[192,768]{1,0:T(8,128)(2,1)S(1)}, u32[]{:S(2)}, u32[]{:S(2)}) collective-permute-start(bf16[192,768]{1,0:T(8,128)(2,1)S(1)} %get-tuple-element.51), channel_id=1, source_target_pairs={{2,0},{0,2},{3,1},{1,3},{6,4},{4,6},{7,5},{5,7},{10,8},{8,10},{11,... | collective-permute-start | bytes 884744 | tf_op jit(solution)/shard_map/ppermute | solution.py:275
  21.7 11.2 %collective-permute-start.8 = (bf16[384,512]{1,0:T(8,128)(2,1)S(1)}, bf16[384,512]{1,0:T(8,128)(2,1)S(1)}, u32[]{:S(2)}, u32[]{:S(2)}) collective-permute-start(bf16[384,512]{1,0:T(8,128)(2,1)S(1)} %project.3), channel_id=1, source_target_pairs={{0,0},{1,12},{4,4},{5,8},{8,5},{9,9},{12,1},{13,13},{2,2},{3,14},{... | collective-permute-start | bytes 1179656 | tf_op jit(solution)/shard_map/ppermute | solution.py:334
  26.5 6.4 %collective-permute-start.2 = (bf16[384,512]{1,0:T(8,128)(2,1)S(1)}, bf16[384,512]{1,0:T(8,128)(2,1)S(1)}, u32[]{:S(2)}, u32[]{:S(2)}) collective-permute-start(bf16[384,512]{1,0:T(8,128)(2,1)S(1)} %get-tuple-element.44.refs_0_), channel_id=1, source_target_pairs={{1,0},{0,1},{3,2},{2,3},{5,4},{4,5},{7,6},{6,7},{9,8},{8,9},{11,10... | collective-permute-start | bytes 1179656 | tf_op jit(solution)/shard_map/ppermute | solution.py:289
  26.6 6.3 %collective-permute-start.4 = (bf16[384,512]{1,0:T(8,128)(2,1)S(1)}, bf16[384,512]{1,0:T(8,128)(2,1)S(1)}, u32[]{:S(2)}, u32[]{:S(2)}) collective-permute-start(bf16[384,512]{1,0:T(8,128)(2,1)S(1)} %collective-permute-done.3.refs_1_), channel_id=1, source_target_pairs={{1,0},{0,1},{3,2},{2,3},{5,4},{4,5},{7,6},{6,7},{9,8},{8,9},{11,10... | collective-permute-start | bytes 1179656 | tf_op jit(solution)/shard_map/ppermute | solution.py:289
  27.1 2.3 %collective-permute-start.7 = (bf16[192,768]{1,0:T(8,128)(2,1)S(1)}, bf16[192,768]{1,0:T(8,128)(2,1)S(1)}, u32[]{:S(2)}, u32[]{:S(2)}) collective-permute-start(bf16[192,768]{1,0:T(8,128)(2,1)S(1)} %collective-permute-done.6.refs_0_), channel_id=1, source_target_pairs={{1,0},{0,1},{3,2},{2,3},{5,4},{4,5},{7,6},{6,7},{9,8},{8,9},{11,10... | collective-permute-start | bytes 884744 | tf_op jit(solution)/shard_map/ppermute | solution.py:289
  32.9 10.2 %collective-permute-start.10 = (bf16[384,512]{1,0:T(8,128)(2,1)S(1)}, bf16[384,512]{1,0:T(8,128)(2,1)S(1)}, u32[]{:S(2)}, u32[]{:S(2)}) collective-permute-start(bf16[384,512]{1,0:T(8,128)(2,1)S(1)} %collective-permute-done.8.refs_0_), channel_id=1, source_target_pairs={{4,0},{0,4},{12,8},{8,12},{5,1},{1,5},{13,9},{9,13},{6,2},{2,6},{1... | collective-permute-start | bytes 1179656 | tf_op jit(solution)/shard_map/ppermute | solution.py:283
  37.6 5.5 %collective-permute-start.9 = (bf16[384,256]{1,0:T(8,128)(2,1)S(1)}, bf16[384,256]{1,0:T(8,128)(2,1)S(1)}, u32[]{:S(2)}, u32[]{:S(2)}) collective-permute-start(bf16[384,256]{1,0:T(8,128)(2,1)S(1)} %end.1.refs_0_), channel_id=1, source_target_pairs={{2,0},{0,2},{3,1},{1,3},{6,4},{4,6},{7,5},{5,7},{10,8},{8,10},{11,... | collective-permute-start | bytes 589832 | tf_op jit(solution)/shard_map/ppermute | solution.py:275
  43.1 2.0 %collective-permute-start.11 = (bf16[384,512]{1,0:T(8,128)(2,1)S(1)}, bf16[384,512]{1,0:T(8,128)(2,1)S(1)}, u32[]{:S(2)}, u32[]{:S(2)}) collective-permute-start(bf16[384,512]{1,0:T(8,128)(2,1)S(1)} %collective-permute-done.8.refs_0_), channel_id=1, source_target_pairs={{1,0},{0,1},{3,2},{2,3},{5,4},{4,5},{7,6},{6,7},{9,8},{8,9},{11,10... | collective-permute-start | bytes 1179656 | tf_op jit(solution)/shard_map/ppermute | solution.py:289
  43.1 2.3 %collective-permute-start.12 = (bf16[384,512]{1,0:T(8,128)(2,1)S(1)}, bf16[384,512]{1,0:T(8,128)(2,1)S(1)}, u32[]{:S(2)}, u32[]{:S(2)}) collective-permute-start(bf16[384,512]{1,0:T(8,128)(2,1)S(1)} %collective-permute-done.10.refs_1_), channel_id=1, source_target_pairs={{1,0},{0,1},{3,2},{2,3},{5,4},{4,5},{7,6},{6,7},{9,8},{8,9},{11,10... | collective-permute-start | bytes 1179656 | tf_op jit(solution)/shard_map/ppermute | solution.py:289
  49.3 4.8 %collective-permute-start.13 = (bf16[3,80,256]{2,1,0:T(8,128)(2,1)S(1)}, bf16[3,80,256]{2,1,0:T(8,128)(2,1)S(1)}, u32[]{:S(2)}, u32[]{:S(2)}) collective-permute-start(bf16[3,80,256]{2,1,0:T(8,128)(2,1)S(1)} %get-tuple-element.70), channel_id=1, source_target_pairs={{2,0},{0,2},{3,1},{1,3},{6,4},{4,6},{7,5},{5,7},{10,8},{8,10},{11,... | collective-permute-start | bytes 368648 | tf_op jit(solution)/shard_map/ppermute | solution.py:275
  54.1 12.2 %collective-permute-start.16 = (bf16[4,80,256]{2,1,0:T(8,128)(2,1)S(1)}, bf16[4,80,256]{2,1,0:T(8,128)(2,1)S(1)}, u32[]{:S(2)}, u32[]{:S(2)}) collective-permute-start(bf16[4,80,256]{2,1,0:T(8,128)(2,1)S(1)} %get-tuple-element.75), channel_id=1, source_target_pairs={{4,0},{8,1},{5,4},{9,5},{1,8},{13,9},{6,2},{10,3},{7,6},{11,7},{3,... | collective-permute-start | bytes 491528 | tf_op jit(solution)/shard_map/ppermute | solution.py:390
  58.3 8.0 %collective-permute-start.14 = (bf16[3,80,256]{2,1,0:T(8,128)(2,1)S(1)}, bf16[3,80,256]{2,1,0:T(8,128)(2,1)S(1)}, u32[]{:S(2)}, u32[]{:S(2)}) collective-permute-start(bf16[3,80,256]{2,1,0:T(8,128)(2,1)S(1)} %get-tuple-element.74), channel_id=1, source_target_pairs={{0,0},{12,1},{4,4},{8,5},{5,8},{9,9},{1,12},{13,13},{2,2},{14,3},{... | collective-permute-start | bytes 368648 | tf_op jit(solution)/shard_map/ppermute | solution.py:392
  60.5 0.7 %collective-permute-start.15 = (bf16[1,80,256]{2,1,0:T(8,128)(2,1)S(1)}, bf16[1,80,256]{2,1,0:T(8,128)(2,1)S(1)}, u32[]{:S(2)}, u32[]{:S(2)}) collective-permute-start(bf16[1,80,256]{2,1,0:T(8,128)(2,1)S(1)} %slice.3), channel_id=1, source_target_pairs={{0,4},{12,5},{4,8},{8,9},{5,12},{9,13},{2,6},{14,7},{6,10},{10,11}... | collective-permute-start | bytes 122888 | tf_op jit(solution)/shard_map/ppermute | solution.py:391

commit v26 on v25

--- a/solution.py
+++ b/solution.py
@@ -327,8 +327,8 @@
     query, pack = project(left, self_qkv, True, 0)
     (right_pack,) = project(tied(right, pack), cross_qkv, False, 1)
     beside = neighbours(pack)
-    near = [pack, *beside]
-    far = [q for p in near for q in across(p)]
+    near = [pack, *beside, *across(pack)]
+    far = [q for p in beside for q in across(p)]
     state = begin(query, near)
     halves = tile_pieces(tied(half, right_pack))[1:]
     right_pack = lax.ppermute(right_pack, both, there)

time: 67.6 us -> 67.3 us (level)
  starting transfers between devices: 27.9 us -> 27 us
    ppermute x4, waiting for transfers between devices: 7.87 us -> 8.64 us  [from_tile(): lax.ppermute(value, 'tile', [((i + step) % tiles, i) for i in range(tiles)])]
  transfers between devices with their start and end apart: 17 -> 17, of which waited for: 6 -> 7; matrix products, arithmetic and copies ran while one was open for 0% -> 0% of each run, Pallas kernels for 17% -> 17%
where the time goes in v26:
time: 67.3 us; the launch traced here: 67.1 us
  starting transfers between devices  27 us (40%)
  waiting for transfers between devices  23.3 us (35%)
  Pallas kernels  16.6 us (25%)
    pallas_call x12, Pallas kernels, run_kernel(): pl.pallas_call(kernel, out_shape=[jax.ShapeDtypeStruct(*s) for s in shape...  16.6 us
    ppermute x4, waiting for transfers between devices, from_tile(): lax.ppermute(value, 'tile', [((i + step) % tiles, i) for i in range(tiles)])  8.64 us
    ppermute x2, starting transfers between devices, fetched(): return lax.ppermute(value, ('blk', 'tile', 'pair'), pairs)  7.55 us
    ppermute x2, waiting for transfers between devices, fetched(): return lax.ppermute(value, ('blk', 'tile', 'pair'), pairs)  6.44 us
    ppermute x1, waiting for transfers between devices, body(): features = lax.ppermute(features, both, back)  5.27 us
    ppermute x1, starting transfers between devices, body(): right_pack = lax.ppermute(right_pack, both, there)  4.83 us
    ppermute x2, starting transfers between devices, neighbours(): lax.ppermute(pack, 'blk', [(g + (i + s) % span, g + i) for g, i in ring])  4.65 us
    ppermute x1, starting transfers between devices, body(): below = lax.ppermute(raised, both, up)  3.64 us
  transfers between devices with their start and end apart: 17, of which 7 were waited for; matrix products, arithmetic and copies ran while one was open for 0% of the time, Pallas kernels for 17%

profile of v26, /device:TPU:1, one launch (start us, length us, event | category | flops | bytes accessed | tf_op | source)
XLA Modules:
  0.0 67.1 jit_solution(1756140275300906838)
XLA Ops:
  0.0 5.6 %collective-permute-start.1 = (bf16[384,384]{1,0:T(8,128)(2,1)}, bf16[384,384]{1,0:T(8,128)(2,1)S(1)}, u32[]{:S(2)}, u32[]{:S(2)}) collective-permute-start(bf16[384,384]{1,0:T(8,128)(2,1)} %bitcast.10), channel_id=1, source_target_pairs={{2,0},{0,2},{3,12},{1,14},{6,4},{4,6},{7,8},{5,10},{10,5},{8,7},{1... | collective-permute-start | bytes 884744 | tf_op jit(solution)/shard_map/ppermute | solution.py:269
  5.6 1.9 %collective-permute-start = (bf16[384,384]{1,0:T(8,128)(2,1)}, bf16[384,384]{1,0:T(8,128)(2,1)S(1)}, u32[]{:S(2)}, u32[]{:S(2)}) collective-permute-start(bf16[384,384]{1,0:T(8,128)(2,1)} %bitcast.11), channel_id=1, source_target_pairs={{0,0},{2,2},{1,12},{3,14},{4,4},{6,6},{5,8},{7,10},{8,5},{10,7},{9... | collective-permute-start | bytes 884744 | tf_op jit(solution)/shard_map/ppermute | solution.py:269
  7.6 2.6 %stage.1 = (bf16[256,768]{1,0:T(8,128)(2,1)S(1)}, bf16[384,256]{1,0:T(8,128)(2,1)S(1)}, bf16[256,768]{1,0:T(8,128)(2,1)S(1)}, bf16[384,384]{1,0:T(8,128)(2,1)S(1...) custom-call(bf16[256,768]{1,0:T(8,128)(2,1)} %refs_0_.1, ...), custom_call_target="tpu_custom_call" | custom-call | tf_op jit(solution)/shard_map/stage/pallas_call | solution.py:22
  10.5 6.4 %collective-permute-done.refs_0_.refs_4_ = bf16[384,384]{1,0:T(8,128)(2,1)S(1)} collective-permute-done((bf16[384,384]{1,0:T(8,128)(2,1)}, bf16[384,384]{1,0:T(8,128)(2,1)S(1)}, u32[]{:S(2)}, u32[]{:S(2)}) %collective-permute-start) | collective-permute-done | bytes 294944 | tf_op jit(solution)/shard_map/ppermute | solution.py:269
  16.9 1.1 %project.2 = (bf16[384,256]{1,0:T(8,128)(2,1)S(1)}, bf16[384,512]{1,0:T(8,128)(2,1)S(1)}) custom-call(bf16[384,384]{1,0:T(8,128)(2,1)S(1)} %collective-permute-done.refs_0_.refs_4_, bf16[384,384]{1,0:T(8,128)(2,1)S(1)} %collective-permute-done.1.refs_1_.refs_5_, bf16[3,2,384,256]{3,2,1,0:T(8,128)(2,1)S(1)} %bitcast.7), custom_call_target="tpu_custom_call" | custom-call | tf_op jit(solution)/shard_map/project/pallas_call | solution.py:22
  18.0 2.4 %collective-permute-start.2 = (bf16[384,512]{1,0:T(8,128)(2,1)S(1)}, bf16[384,512]{1,0:T(8,128)(2,1)S(1)}, u32[]{:S(2)}, u32[]{:S(2)}) collective-permute-start(bf16[384,512]{1,0:T(8,128)(2,1)S(1)} %get-tuple-element.43.refs_0_), channel_id=1, source_target_pairs={{4,0},{0,4},{12,8},{8,12},{5,1},{1,5},{13,9},{9,13},{6,2},{2,6},{1... | collective-permute-start | bytes 1179656 | tf_op jit(solution)/shard_map/ppermute | solution.py:283
  20.4 0.8 %project.3 = bf16[384,512]{1,0:T(8,128)(2,1)S(1)} custom-call(bf16[384,384]{1,0:T(8,128)(2,1)S(1)} %get-tuple-element.47.refs_0_, bf16[384,384]{1,0:T(8,128)(2,1)S(1)} %collective-permute-done.4.refs_1_, bf16[3,2,384,256]{3,2,1,0:T(8,128)(2,1)S(1)} %bitcast.5), custom_call_target="tpu_custom_call" | custom-call | tf_op jit(solution)/shard_map/project/pallas_call | solution.py:22
  21.7 4.8 %collective-permute-start.7 = (bf16[384,512]{1,0:T(8,128)(2,1)S(1)}, bf16[384,512]{1,0:T(8,128)(2,1)S(1)}, u32[]{:S(2)}, u32[]{:S(2)}) collective-permute-start(bf16[384,512]{1,0:T(8,128)(2,1)S(1)} %project.3), channel_id=1, source_target_pairs={{0,0},{1,12},{4,4},{5,8},{8,5},{9,9},{12,1},{13,13},{2,2},{3,14},{... | collective-permute-start | bytes 1179656 | tf_op jit(solution)/shard_map/ppermute | solution.py:334
  27.1 2.8 %begin.1 = (f32[4,384,128]{2,1,0:T(8,128)S(1)}, f32[4,384,1]{2,1,0:T(8,128)S(1)}) custom-call(bf16[384,256]{1,0:T(8,128)(2,1)S(1)} %get-tuple-element.42.query, bf16[384,512]{1,0:T(8,128)(2,1)S(1)} %get-tuple-element.43.refs_0_, bf16[384,512]{1,0:T(8,128)(2,1)S(1)} %collective-permute-done.2.refs_1_, bf16[384,512]{1,0:T(8,128)(2,1)S(1)} %collective-permute-done.8.refs_2_), custom_call_target="tpu_custom_call" | custom-call | tf_op jit(solution)/shard_map/begin/pallas_call | solution.py:22
  30.3 2.7 %collective-permute-done.7.refs_0_ = bf16[384,512]{1,0:T(8,128)(2,1)S(1)} collective-permute-done((bf16[384,512]{1,0:T(8,128)(2,1)S(1)}, bf16[384,512]{1,0:T(8,128)(2,1)S(1)}, u32[]{:S(2)}, u32[]{:S(2)}) %collective-permute-start.7) | collective-permute-done | bytes 393248 | tf_op jit(solution)/shard_map/ppermute | solution.py:334
  32.9 2.3 %collective-permute-start.10 = (bf16[384,512]{1,0:T(8,128)(2,1)S(1)}, bf16[384,512]{1,0:T(8,128)(2,1)S(1)}, u32[]{:S(2)}, u32[]{:S(2)}) collective-permute-start(bf16[384,512]{1,0:T(8,128)(2,1)S(1)} %collective-permute-done.7.refs_0_), channel_id=1, source_target_pairs={{4,0},{0,4},{12,8},{8,12},{5,1},{1,5},{13,9},{9,13},{6,2},{2,6},{1... | collective-permute-start | bytes 1179656 | tf_op jit(solution)/shard_map/ppermute | solution.py:283
  35.2 2.2 %end.1.refs_0_ = bf16[384,256]{1,0:T(8,128)(2,1)S(1)} custom-call(bf16[384,256]{1,0:T(8,128)(2,1)S(1)} %get-tuple-element.42.query, bf16[384,512]{1,0:T(8,128)(2,1)S(1)} %collective-permute-done.3.refs_0_, f32[4,384,128]{2,1,0:T(8,128)S(1)} %get-tuple-element.55.refs_1_, f32[4,384,1]{2,1,0:T(8,128)S(1)} %get-tuple-element.56.refs_2_), custom_call_target="tpu_custom_call" | custom-call | tf_op jit(solution)/shard_map/end/pallas_call | solution.py:22
  37.5 1.1 %collective-permute-start.9 = (bf16[384,256]{1,0:T(8,128)(2,1)S(1)}, bf16[384,256]{1,0:T(8,128)(2,1)S(1)}, u32[]{:S(2)}, u32[]{:S(2)}) collective-permute-start(bf16[384,256]{1,0:T(8,128)(2,1)S(1)} %end.1.refs_0_), channel_id=1, source_target_pairs={{2,0},{0,2},{3,1},{1,3},{6,4},{4,6},{7,5},{5,7},{10,8},{8,10},{11,... | collective-permute-start | bytes 589832 | tf_op jit(solution)/shard_map/ppermute | solution.py:275
  38.5 4.7 %collective-permute-done.9.refs_1_ = bf16[384,256]{1,0:T(8,128)(2,1)S(1)} collective-permute-done((bf16[384,256]{1,0:T(8,128)(2,1)S(1)}, bf16[384,256]{1,0:T(8,128)(2,1)S(1)}, u32[]{:S(2)}, u32[]{:S(2)}) %collective-permute-start.9) | collective-permute-done | bytes 196640 | tf_op jit(solution)/shard_map/ppermute | solution.py:275
  43.3 0.5 collective-permute-start.12
  43.8 1.5 %update.1 = (bf16[2,384,384]{2,1,0:T(8,128)(2,1)S(1)}, bf16[384,256]{1,0:T(8,128)(2,1)S(1)}) custom-call(bf16[384,256]{1,0:T(8,128)(2,1)S(1)} %end.1.refs_0_, bf16[384,256]{1,0:T(8,128)(2,1)S(1)} %collective-permute-done.9.refs_1_, bf16[256,768]{1,0:T(8,128)(2,1)S(1)} %get-tuple-element.59.refs_2_, bf16[256,768]{1,0:T(8,128)(2,1)S(1)} %get-tuple-element.60.refs_3_, ...), custom_call_target="tpu_custom_call" | custom-call | tf_op jit(solution)/shard_map/update/pallas_call | solution.py:22
  45.6 3.8 %end_map.1 = (bf16[3,80,256]{2,1,0:T(8,128)(2,1)S(1)}, bf16[3,80,256]{2,1,0:T(8,128)(2,1)S(1)}) custom-call(bf16[384,256]{1,0:T(8,128)(2,1)S(1)} %get-tuple-element.62.query, bf16[384,512]{1,0:T(8,128)(2,1)S(1)} %collective-permute-done.7.refs_0_, bf16[384,512]{1,0:T(8,128)(2,1)S(1)} %collective-permute-done.10.refs_1_, ...), custom_call_target="tpu_custom_call" | custom-call | tf_op jit(solution)/shard_map/end_map/pallas_call | solution.py:22
  49.4 0.8 %collective-permute-start.13 = (bf16[3,80,256]{2,1,0:T(8,128)(2,1)S(1)}, bf16[3,80,256]{2,1,0:T(8,128)(2,1)S(1)}, u32[]{:S(2)}, u32[]{:S(2)}) collective-permute-start(bf16[3,80,256]{2,1,0:T(8,128)(2,1)S(1)} %get-tuple-element.68), channel_id=1, source_target_pairs={{2,0},{0,2},{3,1},{1,3},{6,4},{4,6},{7,5},{5,7},{10,8},{8,10},{11,... | collective-permute-start | bytes 368648 | tf_op jit(solution)/shard_map/ppermute | solution.py:275
  50.6 3.6 %collective-permute-done.13.refs_2_ = bf16[3,80,256]{2,1,0:T(8,128)(2,1)S(1)} collective-permute-done((bf16[3,80,256]{2,1,0:T(8,128)(2,1)S(1)}, bf16[3,80,256]{2,1,0:T(8,128)(2,1)S(1)}, u32[]{:S(2)}, u32[]{:S(2)}) %collective-permute-start.13) | collective-permute-done | bytes 122912 | tf_op jit(solution)/shard_map/ppermute | solution.py:275
  54.3 3.6 %collective-permute-start.16 = (bf16[4,80,256]{2,1,0:T(8,128)(2,1)S(1)}, bf16[4,80,256]{2,1,0:T(8,128)(2,1)S(1)}, u32[]{:S(2)}, u32[]{:S(2)}) collective-permute-start(bf16[4,80,256]{2,1,0:T(8,128)(2,1)S(1)} %get-tuple-element.73), channel_id=1, source_target_pairs={{4,0},{8,1},{5,4},{9,5},{1,8},{13,9},{6,2},{10,3},{7,6},{11,7},{3,... | collective-permute-start | bytes 491528 | tf_op jit(solution)/shard_map/ppermute | solution.py:390
  58.0 2.1 %collective-permute-start.14 = (bf16[3,80,256]{2,1,0:T(8,128)(2,1)S(1)}, bf16[3,80,256]{2,1,0:T(8,128)(2,1)S(1)}, u32[]{:S(2)}, u32[]{:S(2)}) collective-permute-start(bf16[3,80,256]{2,1,0:T(8,128)(2,1)S(1)} %get-tuple-element.72), channel_id=1, source_target_pairs={{0,0},{12,1},{4,4},{8,5},{5,8},{9,9},{1,12},{13,13},{2,2},{14,3},{... | collective-permute-start | bytes 368648 | tf_op jit(solution)/shard_map/ppermute | solution.py:392
  60.1 0.7 collective-permute-start.15
  60.8 5.3 %collective-permute-done.14.window = bf16[3,80,256]{2,1,0:T(8,128)(2,1)S(1)} collective-permute-done((bf16[3,80,256]{2,1,0:T(8,128)(2,1)S(1)}, bf16[3,80,256]{2,1,0:T(8,128)(2,1)S(1)}, u32[]{:S(2)}, u32[]{:S(2)}) %collective-permute-start.14) | collective-permute-done | bytes 122912 | tf_op jit(solution)/shard_map/ppermute | solution.py:392
  66.1 1.0 %join.1 = bf16[3,64,256]{2,1,0:T(8,128)(2,1)} custom-call(bf16[3,80,256]{2,1,0:T(8,128)(2,1)S(1)} %collective-permute-done.14.window, bf16[1,80,256]{2,1,0:T(8,128)(2,1)S(1)} %collective-permute-done.15.above, bf16[4,80,256]{2,1,0:T(8,128)(2,1)S(1)} %collective-permute-done.16.below, bf16[3,3,256,256]{3,2,1,0:T(8,128)(2,1)S(1)} %get-tuple-element.74.weight), custom_call_target="tpu_custom_call" | custom-call | tf_op jit(solution)/shard_map/join/pallas_call | solution.py:22
  (25 shorter events, 2.5 us)
Async XLA Ops:
  0.0 10.5 %collective-permute-start.1 = (bf16[384,384]{1,0:T(8,128)(2,1)}, bf16[384,384]{1,0:T(8,128)(2,1)S(1)}, u32[]{:S(2)}, u32[]{:S(2)}) collective-permute-start(bf16[384,384]{1,0:T(8,128)(2,1)} %bitcast.10), channel_id=1, source_target_pairs={{2,0},{0,2},{3,12},{1,14},{6,4},{4,6},{7,8},{5,10},{10,5},{8,7},{1... | collective-permute-start | bytes 884744 | tf_op jit(solution)/shard_map/ppermute | solution.py:269
  5.6 11.3 %collective-permute-start = (bf16[384,384]{1,0:T(8,128)(2,1)}, bf16[384,384]{1,0:T(8,128)(2,1)S(1)}, u32[]{:S(2)}, u32[]{:S(2)}) collective-permute-start(bf16[384,384]{1,0:T(8,128)(2,1)} %bitcast.11), channel_id=1, source_target_pairs={{0,0},{2,2},{1,12},{3,14},{4,4},{6,6},{5,8},{7,10},{8,5},{10,7},{9... | collective-permute-start | bytes 884744 | tf_op jit(solution)/shard_map/ppermute | solution.py:269
  7.6 2.6 %copy-start = (bf16[1,384,384]{2,1,0:T(8,128)(2,1)S(1)}, bf16[1,384,384]{2,1,0:T(8,128)(2,1)}, u32[]{:S(2)}) copy-start(bf16[1,384,384]{2,1,0:T(8,128)(2,1)} %param.9) | copy-start | bytes 884740
  10.1 10.2 %collective-permute-start.4 = (bf16[384,384]{1,0:T(8,128)(2,1)S(1)}, bf16[384,384]{1,0:T(8,128)(2,1)S(1)}, u32[]{:S(2)}, u32[]{:S(2)}) collective-permute-start(bf16[384,384]{1,0:T(8,128)(2,1)S(1)} %bitcast.9), channel_id=1, source_target_pairs={{2,0},{0,2},{3,1},{1,3},{6,4},{4,6},{7,5},{5,7},{10,8},{8,10},{11,... | collective-permute-start | bytes 884744 | tf_op jit(solution)/shard_map/ppermute | solution.py:275
  18.0 8.5 %collective-permute-start.2 = (bf16[384,512]{1,0:T(8,128)(2,1)S(1)}, bf16[384,512]{1,0:T(8,128)(2,1)S(1)}, u32[]{:S(2)}, u32[]{:S(2)}) collective-permute-start(bf16[384,512]{1,0:T(8,128)(2,1)S(1)} %get-tuple-element.43.refs_0_), channel_id=1, source_target_pairs={{4,0},{0,4},{12,8},{8,12},{5,1},{1,5},{13,9},{9,13},{6,2},{2,6},{1... | collective-permute-start | bytes 1179656 | tf_op jit(solution)/shard_map/ppermute | solution.py:283
  21.2 5.6 %collective-permute-start.5 = (bf16[192,768]{1,0:T(8,128)(2,1)S(1)}, bf16[192,768]{1,0:T(8,128)(2,1)S(1)}, u32[]{:S(2)}, u32[]{:S(2)}) collective-permute-start(bf16[192,768]{1,0:T(8,128)(2,1)S(1)} %get-tuple-element.50), channel_id=1, source_target_pairs={{2,0},{0,2},{3,1},{1,3},{6,4},{4,6},{7,5},{5,7},{10,8},{8,10},{11,... | collective-permute-start | bytes 884744 | tf_op jit(solution)/shard_map/ppermute | solution.py:275
  21.7 5.4 %collective-permute-start.8 = (bf16[384,512]{1,0:T(8,128)(2,1)S(1)}, bf16[384,512]{1,0:T(8,128)(2,1)S(1)}, u32[]{:S(2)}, u32[]{:S(2)}) collective-permute-start(bf16[384,512]{1,0:T(8,128)(2,1)S(1)} %get-tuple-element.43.refs_0_), channel_id=1, source_target_pairs={{1,0},{0,1},{3,2},{2,3},{5,4},{4,5},{7,6},{6,7},{9,8},{8,9},{11,10... | collective-permute-start | bytes 1179656 | tf_op jit(solution)/shard_map/ppermute | solution.py:289
  21.7 11.2 %collective-permute-start.7 = (bf16[384,512]{1,0:T(8,128)(2,1)S(1)}, bf16[384,512]{1,0:T(8,128)(2,1)S(1)}, u32[]{:S(2)}, u32[]{:S(2)}) collective-permute-start(bf16[384,512]{1,0:T(8,128)(2,1)S(1)} %project.3), channel_id=1, source_target_pairs={{0,0},{1,12},{4,4},{5,8},{8,5},{9,9},{12,1},{13,13},{2,2},{3,14},{... | collective-permute-start | bytes 1179656 | tf_op jit(solution)/shard_map/ppermute | solution.py:334
  26.5 6.4 %collective-permute-start.3 = (bf16[384,512]{1,0:T(8,128)(2,1)S(1)}, bf16[384,512]{1,0:T(8,128)(2,1)S(1)}, u32[]{:S(2)}, u32[]{:S(2)}) collective-permute-start(bf16[384,512]{1,0:T(8,128)(2,1)S(1)} %collective-permute-done.2.refs_1_), channel_id=1, source_target_pairs={{1,0},{0,1},{3,2},{2,3},{5,4},{4,5},{7,6},{6,7},{9,8},{8,9},{11,10... | collective-permute-start | bytes 1179656 | tf_op jit(solution)/shard_map/ppermute | solution.py:289
  26.9 3.0 %collective-permute-start.6 = (bf16[192,768]{1,0:T(8,128)(2,1)S(1)}, bf16[192,768]{1,0:T(8,128)(2,1)S(1)}, u32[]{:S(2)}, u32[]{:S(2)}) collective-permute-start(bf16[192,768]{1,0:T(8,128)(2,1)S(1)} %collective-permute-done.5.refs_0_), channel_id=1, source_target_pairs={{1,0},{0,1},{3,2},{2,3},{5,4},{4,5},{7,6},{6,7},{9,8},{8,9},{11,10... | collective-permute-start | bytes 884744 | tf_op jit(solution)/shard_map/ppermute | solution.py:289
  32.9 10.4 %collective-permute-start.10 = (bf16[384,512]{1,0:T(8,128)(2,1)S(1)}, bf16[384,512]{1,0:T(8,128)(2,1)S(1)}, u32[]{:S(2)}, u32[]{:S(2)}) collective-permute-start(bf16[384,512]{1,0:T(8,128)(2,1)S(1)} %collective-permute-done.7.refs_0_), channel_id=1, source_target_pairs={{4,0},{0,4},{12,8},{8,12},{5,1},{1,5},{13,9},{9,13},{6,2},{2,6},{1... | collective-permute-start | bytes 1179656 | tf_op jit(solution)/shard_map/ppermute | solution.py:283
  37.5 5.8 %collective-permute-start.9 = (bf16[384,256]{1,0:T(8,128)(2,1)S(1)}, bf16[384,256]{1,0:T(8,128)(2,1)S(1)}, u32[]{:S(2)}, u32[]{:S(2)}) collective-permute-start(bf16[384,256]{1,0:T(8,128)(2,1)S(1)} %end.1.refs_0_), channel_id=1, source_target_pairs={{2,0},{0,2},{3,1},{1,3},{6,4},{4,6},{7,5},{5,7},{10,8},{8,10},{11,... | collective-permute-start | bytes 589832 | tf_op jit(solution)/shard_map/ppermute | solution.py:275
  43.3 2.0 %collective-permute-start.11 = (bf16[384,512]{1,0:T(8,128)(2,1)S(1)}, bf16[384,512]{1,0:T(8,128)(2,1)S(1)}, u32[]{:S(2)}, u32[]{:S(2)}) collective-permute-start(bf16[384,512]{1,0:T(8,128)(2,1)S(1)} %collective-permute-done.7.refs_0_), channel_id=1, source_target_pairs={{1,0},{0,1},{3,2},{2,3},{5,4},{4,5},{7,6},{6,7},{9,8},{8,9},{11,10... | collective-permute-start | bytes 1179656 | tf_op jit(solution)/shard_map/ppermute | solution.py:289
  43.3 2.3 %collective-permute-start.12 = (bf16[384,512]{1,0:T(8,128)(2,1)S(1)}, bf16[384,512]{1,0:T(8,128)(2,1)S(1)}, u32[]{:S(2)}, u32[]{:S(2)}) collective-permute-start(bf16[384,512]{1,0:T(8,128)(2,1)S(1)} %collective-permute-done.10.refs_1_), channel_id=1, source_target_pairs={{1,0},{0,1},{3,2},{2,3},{5,4},{4,5},{7,6},{6,7},{9,8},{8,9},{11,10... | collective-permute-start | bytes 1179656 | tf_op jit(solution)/shard_map/ppermute | solution.py:289
  49.4 4.9 %collective-permute-start.13 = (bf16[3,80,256]{2,1,0:T(8,128)(2,1)S(1)}, bf16[3,80,256]{2,1,0:T(8,128)(2,1)S(1)}, u32[]{:S(2)}, u32[]{:S(2)}) collective-permute-start(bf16[3,80,256]{2,1,0:T(8,128)(2,1)S(1)} %get-tuple-element.68), channel_id=1, source_target_pairs={{2,0},{0,2},{3,1},{1,3},{6,4},{4,6},{7,5},{5,7},{10,8},{8,10},{11,... | collective-permute-start | bytes 368648 | tf_op jit(solution)/shard_map/ppermute | solution.py:275
  54.3 11.8 %collective-permute-start.16 = (bf16[4,80,256]{2,1,0:T(8,128)(2,1)S(1)}, bf16[4,80,256]{2,1,0:T(8,128)(2,1)S(1)}, u32[]{:S(2)}, u32[]{:S(2)}) collective-permute-start(bf16[4,80,256]{2,1,0:T(8,128)(2,1)S(1)} %get-tuple-element.73), channel_id=1, source_target_pairs={{4,0},{8,1},{5,4},{9,5},{1,8},{13,9},{6,2},{10,3},{7,6},{11,7},{3,... | collective-permute-start | bytes 491528 | tf_op jit(solution)/shard_map/ppermute | solution.py:390
  58.0 8.1 %collective-permute-start.14 = (bf16[3,80,256]{2,1,0:T(8,128)(2,1)S(1)}, bf16[3,80,256]{2,1,0:T(8,128)(2,1)S(1)}, u32[]{:S(2)}, u32[]{:S(2)}) collective-permute-start(bf16[3,80,256]{2,1,0:T(8,128)(2,1)S(1)} %get-tuple-element.72), channel_id=1, source_target_pairs={{0,0},{12,1},{4,4},{8,5},{5,8},{9,9},{1,12},{13,13},{2,2},{14,3},{... | collective-permute-start | bytes 368648 | tf_op jit(solution)/shard_map/ppermute | solution.py:392
  60.1 0.7 %collective-permute-start.15 = (bf16[1,80,256]{2,1,0:T(8,128)(2,1)S(1)}, bf16[1,80,256]{2,1,0:T(8,128)(2,1)S(1)}, u32[]{:S(2)}, u32[]{:S(2)}) collective-permute-start(bf16[1,80,256]{2,1,0:T(8,128)(2,1)S(1)} %slice.3), channel_id=1, source_target_pairs={{0,4},{12,5},{4,8},{8,9},{5,12},{9,13},{2,6},{14,7},{6,10},{10,11}... | collective-permute-start | bytes 122888 | tf_op jit(solution)/shard_map/ppermute | solution.py:391

commit v27 on v26

--- a/solution.py
+++ b/solution.py
@@ -220,7 +220,9 @@
 def conv_kernel(window, above, below, weight, out):
     width = out.shape[1]
     band_rows, channels = out.shape[0], out.shape[2]
-    grid = jnp.concatenate([above[...], window[...], below[:1]], axis=0).astype(F32)
+    grid = jnp.concatenate(
+        [above[band_rows - 1 : band_rows], window[...], below[:1]], axis=0
+    ).astype(F32)
     active = jnp.maximum(grid, 0.0)
     total = grid[1 : 1 + band_rows, EDGE : EDGE + width, :].reshape(band_rows * width, channels)
     for column in range(3):
@@ -388,7 +390,7 @@
         add_kernel, "add", [(window, BF16), (longer, BF16)], [carried, maps[0], *received]
     )
     below = lax.ppermute(raised, both, up)
-    above = lax.ppermute(features[-1:], both, down)
+    above = lax.ppermute(raised, both, down)
     features = lax.ppermute(features, both, back)
     (joined,) = run_kernel(
         conv_kernel,

time: 67.3 us -> 69.3 us (1.030)
  starting transfers between devices: 27 us -> 29 us
    ppermute x1, starting transfers between devices: 3.64 us -> 4.89 us  [body(): below = lax.ppermute(raised, both, up)]
    ppermute x1, starting transfers between devices: 2.13 us -> 2.92 us  [body(): features = lax.ppermute(features, both, back)]
where the time goes in v27:
time: 69.3 us; the launch traced here: 69 us
  starting transfers between devices  29 us (42%)
  waiting for transfers between devices  23.3 us (34%)
  Pallas kernels  16.6 us (24%)
    pallas_call x12, Pallas kernels, run_kernel(): pl.pallas_call(kernel, out_shape=[jax.ShapeDtypeStruct(*s) for s in shape...  16.6 us
    ppermute x4, waiting for transfers between devices, from_tile(): lax.ppermute(value, 'tile', [((i + step) % tiles, i) for i in range(tiles)])  8.64 us
    ppermute x2, starting transfers between devices, fetched(): return lax.ppermute(value, ('blk', 'tile', 'pair'), pairs)  7.55 us
    ppermute x2, waiting for transfers between devices, fetched(): return lax.ppermute(value, ('blk', 'tile', 'pair'), pairs)  6.44 us
    ppermute x1, waiting for transfers between devices, body(): features = lax.ppermute(features, both, back)  5.18 us
    ppermute x1, starting transfers between devices, body(): below = lax.ppermute(raised, both, up)  4.89 us
    ppermute x1, starting transfers between devices, body(): right_pack = lax.ppermute(right_pack, both, there)  4.83 us
    ppermute x2, starting transfers between devices, neighbours(): lax.ppermute(pack, 'blk', [(g + (i + s) % span, g + i) for g, i in ring])  4.65 us
  transfers between devices with their start and end apart: 17, of which 7 were waited for; matrix products, arithmetic and copies ran while one was open for 0% of the time, Pallas kernels for 17%

profile of v27, /device:TPU:1, one launch (start us, length us, event | category | flops | bytes accessed | tf_op | source)
XLA Modules:
  0.0 69.0 jit_solution(2904870236822366583)
XLA Ops:
  0.0 5.6 %collective-permute-start.1 = (bf16[384,384]{1,0:T(8,128)(2,1)}, bf16[384,384]{1,0:T(8,128)(2,1)S(1)}, u32[]{:S(2)}, u32[]{:S(2)}) collective-permute-start(bf16[384,384]{1,0:T(8,128)(2,1)} %bitcast.10), channel_id=1, source_target_pairs={{2,0},{0,2},{3,12},{1,14},{6,4},{4,6},{7,8},{5,10},{10,5},{8,7},{1... | collective-permute-start | bytes 884744 | tf_op jit(solution)/shard_map/ppermute | solution.py:271
  5.6 1.9 %collective-permute-start = (bf16[384,384]{1,0:T(8,128)(2,1)}, bf16[384,384]{1,0:T(8,128)(2,1)S(1)}, u32[]{:S(2)}, u32[]{:S(2)}) collective-permute-start(bf16[384,384]{1,0:T(8,128)(2,1)} %bitcast.11), channel_id=1, source_target_pairs={{0,0},{2,2},{1,12},{3,14},{4,4},{6,6},{5,8},{7,10},{8,5},{10,7},{9... | collective-permute-start | bytes 884744 | tf_op jit(solution)/shard_map/ppermute | solution.py:271
  7.6 2.6 %stage.1 = (bf16[256,768]{1,0:T(8,128)(2,1)S(1)}, bf16[384,256]{1,0:T(8,128)(2,1)S(1)}, bf16[256,768]{1,0:T(8,128)(2,1)S(1)}, bf16[384,384]{1,0:T(8,128)(2,1)S(1...) custom-call(bf16[256,768]{1,0:T(8,128)(2,1)} %refs_0_.1, ...), custom_call_target="tpu_custom_call" | custom-call | tf_op jit(solution)/shard_map/stage/pallas_call | solution.py:22
  10.5 6.4 %collective-permute-done.refs_0_.refs_4_ = bf16[384,384]{1,0:T(8,128)(2,1)S(1)} collective-permute-done((bf16[384,384]{1,0:T(8,128)(2,1)}, bf16[384,384]{1,0:T(8,128)(2,1)S(1)}, u32[]{:S(2)}, u32[]{:S(2)}) %collective-permute-start) | collective-permute-done | bytes 294944 | tf_op jit(solution)/shard_map/ppermute | solution.py:271
  16.9 1.1 %project.2 = (bf16[384,256]{1,0:T(8,128)(2,1)S(1)}, bf16[384,512]{1,0:T(8,128)(2,1)S(1)}) custom-call(bf16[384,384]{1,0:T(8,128)(2,1)S(1)} %collective-permute-done.refs_0_.refs_4_, bf16[384,384]{1,0:T(8,128)(2,1)S(1)} %collective-permute-done.1.refs_1_.refs_5_, bf16[3,2,384,256]{3,2,1,0:T(8,128)(2,1)S(1)} %bitcast.7), custom_call_target="tpu_custom_call" | custom-call | tf_op jit(solution)/shard_map/project/pallas_call | solution.py:22
  18.0 2.4 %collective-permute-start.2 = (bf16[384,512]{1,0:T(8,128)(2,1)S(1)}, bf16[384,512]{1,0:T(8,128)(2,1)S(1)}, u32[]{:S(2)}, u32[]{:S(2)}) collective-permute-start(bf16[384,512]{1,0:T(8,128)(2,1)S(1)} %get-tuple-element.43.refs_0_), channel_id=1, source_target_pairs={{4,0},{0,4},{12,8},{8,12},{5,1},{1,5},{13,9},{9,13},{6,2},{2,6},{1... | collective-permute-start | bytes 1179656 | tf_op jit(solution)/shard_map/ppermute | solution.py:285
  20.4 0.8 %project.3 = bf16[384,512]{1,0:T(8,128)(2,1)S(1)} custom-call(bf16[384,384]{1,0:T(8,128)(2,1)S(1)} %get-tuple-element.47.refs_0_, bf16[384,384]{1,0:T(8,128)(2,1)S(1)} %collective-permute-done.4.refs_1_, bf16[3,2,384,256]{3,2,1,0:T(8,128)(2,1)S(1)} %bitcast.5), custom_call_target="tpu_custom_call" | custom-call | tf_op jit(solution)/shard_map/project/pallas_call | solution.py:22
  21.7 4.8 %collective-permute-start.7 = (bf16[384,512]{1,0:T(8,128)(2,1)S(1)}, bf16[384,512]{1,0:T(8,128)(2,1)S(1)}, u32[]{:S(2)}, u32[]{:S(2)}) collective-permute-start(bf16[384,512]{1,0:T(8,128)(2,1)S(1)} %project.3), channel_id=1, source_target_pairs={{0,0},{1,12},{4,4},{5,8},{8,5},{9,9},{12,1},{13,13},{2,2},{3,14},{... | collective-permute-start | bytes 1179656 | tf_op jit(solution)/shard_map/ppermute | solution.py:336
  27.1 2.8 %begin.1 = (f32[4,384,128]{2,1,0:T(8,128)S(1)}, f32[4,384,1]{2,1,0:T(8,128)S(1)}) custom-call(bf16[384,256]{1,0:T(8,128)(2,1)S(1)} %get-tuple-element.42.query, bf16[384,512]{1,0:T(8,128)(2,1)S(1)} %get-tuple-element.43.refs_0_, bf16[384,512]{1,0:T(8,128)(2,1)S(1)} %collective-permute-done.2.refs_1_, bf16[384,512]{1,0:T(8,128)(2,1)S(1)} %collective-permute-done.8.refs_2_), custom_call_target="tpu_custom_call" | custom-call | tf_op jit(solution)/shard_map/begin/pallas_call | solution.py:22
  30.3 2.7 %collective-permute-done.7.refs_0_ = bf16[384,512]{1,0:T(8,128)(2,1)S(1)} collective-permute-done((bf16[384,512]{1,0:T(8,128)(2,1)S(1)}, bf16[384,512]{1,0:T(8,128)(2,1)S(1)}, u32[]{:S(2)}, u32[]{:S(2)}) %collective-permute-start.7) | collective-permute-done | bytes 393248 | tf_op jit(solution)/shard_map/ppermute | solution.py:336
  32.9 2.3 %collective-permute-start.10 = (bf16[384,512]{1,0:T(8,128)(2,1)S(1)}, bf16[384,512]{1,0:T(8,128)(2,1)S(1)}, u32[]{:S(2)}, u32[]{:S(2)}) collective-permute-start(bf16[384,512]{1,0:T(8,128)(2,1)S(1)} %collective-permute-done.7.refs_0_), channel_id=1, source_target_pairs={{4,0},{0,4},{12,8},{8,12},{5,1},{1,5},{13,9},{9,13},{6,2},{2,6},{1... | collective-permute-start | bytes 1179656 | tf_op jit(solution)/shard_map/ppermute | solution.py:285
  35.2 2.2 %end.1.refs_0_ = bf16[384,256]{1,0:T(8,128)(2,1)S(1)} custom-call(bf16[384,256]{1,0:T(8,128)(2,1)S(1)} %get-tuple-element.42.query, bf16[384,512]{1,0:T(8,128)(2,1)S(1)} %collective-permute-done.3.refs_0_, f32[4,384,128]{2,1,0:T(8,128)S(1)} %get-tuple-element.55.refs_1_, f32[4,384,1]{2,1,0:T(8,128)S(1)} %get-tuple-element.56.refs_2_), custom_call_target="tpu_custom_call" | custom-call | tf_op jit(solution)/shard_map/end/pallas_call | solution.py:22
  37.5 1.1 %collective-permute-start.9 = (bf16[384,256]{1,0:T(8,128)(2,1)S(1)}, bf16[384,256]{1,0:T(8,128)(2,1)S(1)}, u32[]{:S(2)}, u32[]{:S(2)}) collective-permute-start(bf16[384,256]{1,0:T(8,128)(2,1)S(1)} %end.1.refs_0_), channel_id=1, source_target_pairs={{2,0},{0,2},{3,1},{1,3},{6,4},{4,6},{7,5},{5,7},{10,8},{8,10},{11,... | collective-permute-start | bytes 589832 | tf_op jit(solution)/shard_map/ppermute | solution.py:277
  38.5 4.7 %collective-permute-done.9.refs_1_ = bf16[384,256]{1,0:T(8,128)(2,1)S(1)} collective-permute-done((bf16[384,256]{1,0:T(8,128)(2,1)S(1)}, bf16[384,256]{1,0:T(8,128)(2,1)S(1)}, u32[]{:S(2)}, u32[]{:S(2)}) %collective-permute-start.9) | collective-permute-done | bytes 196640 | tf_op jit(solution)/shard_map/ppermute | solution.py:277
  43.3 0.5 collective-permute-start.12
  43.8 1.5 %update.1 = (bf16[2,384,384]{2,1,0:T(8,128)(2,1)S(1)}, bf16[384,256]{1,0:T(8,128)(2,1)S(1)}) custom-call(bf16[384,256]{1,0:T(8,128)(2,1)S(1)} %end.1.refs_0_, bf16[384,256]{1,0:T(8,128)(2,1)S(1)} %collective-permute-done.9.refs_1_, bf16[256,768]{1,0:T(8,128)(2,1)S(1)} %get-tuple-element.59.refs_2_, bf16[256,768]{1,0:T(8,128)(2,1)S(1)} %get-tuple-element.60.refs_3_, ...), custom_call_target="tpu_custom_call" | custom-call | tf_op jit(solution)/shard_map/update/pallas_call | solution.py:22
  45.6 3.8 %end_map.1 = (bf16[3,80,256]{2,1,0:T(8,128)(2,1)S(1)}, bf16[3,80,256]{2,1,0:T(8,128)(2,1)S(1)}) custom-call(bf16[384,256]{1,0:T(8,128)(2,1)S(1)} %get-tuple-element.62.query, bf16[384,512]{1,0:T(8,128)(2,1)S(1)} %collective-permute-done.7.refs_0_, bf16[384,512]{1,0:T(8,128)(2,1)S(1)} %collective-permute-done.10.refs_1_, ...), custom_call_target="tpu_custom_call" | custom-call | tf_op jit(solution)/shard_map/end_map/pallas_call | solution.py:22
  49.4 0.8 %collective-permute-start.13 = (bf16[3,80,256]{2,1,0:T(8,128)(2,1)S(1)}, bf16[3,80,256]{2,1,0:T(8,128)(2,1)S(1)}, u32[]{:S(2)}, u32[]{:S(2)}) collective-permute-start(bf16[3,80,256]{2,1,0:T(8,128)(2,1)S(1)} %get-tuple-element.68), channel_id=1, source_target_pairs={{2,0},{0,2},{3,1},{1,3},{6,4},{4,6},{7,5},{5,7},{10,8},{8,10},{11,... | collective-permute-start | bytes 368648 | tf_op jit(solution)/shard_map/ppermute | solution.py:277
  50.6 3.6 %collective-permute-done.13.refs_2_ = bf16[3,80,256]{2,1,0:T(8,128)(2,1)S(1)} collective-permute-done((bf16[3,80,256]{2,1,0:T(8,128)(2,1)S(1)}, bf16[3,80,256]{2,1,0:T(8,128)(2,1)S(1)}, u32[]{:S(2)}, u32[]{:S(2)}) %collective-permute-start.13) | collective-permute-done | bytes 122912 | tf_op jit(solution)/shard_map/ppermute | solution.py:277
  54.3 0.7 collective-permute-start.15
  55.0 4.9 %collective-permute-start.16 = (bf16[4,80,256]{2,1,0:T(8,128)(2,1)S(1)}, bf16[4,80,256]{2,1,0:T(8,128)(2,1)S(1)}, u32[]{:S(2)}, u32[]{:S(2)}) collective-permute-start(bf16[4,80,256]{2,1,0:T(8,128)(2,1)S(1)} %get-tuple-element.73), channel_id=1, source_target_pairs={{4,0},{8,1},{5,4},{9,5},{1,8},{13,9},{6,2},{10,3},{7,6},{11,7},{3,... | collective-permute-start | bytes 491528 | tf_op jit(solution)/shard_map/ppermute | solution.py:392
  59.9 2.9 %collective-permute-start.14 = (bf16[3,80,256]{2,1,0:T(8,128)(2,1)S(1)}, bf16[3,80,256]{2,1,0:T(8,128)(2,1)S(1)}, u32[]{:S(2)}, u32[]{:S(2)}) collective-permute-start(bf16[3,80,256]{2,1,0:T(8,128)(2,1)S(1)} %get-tuple-element.72), channel_id=1, source_target_pairs={{0,0},{12,1},{4,4},{8,5},{5,8},{9,9},{1,12},{13,13},{2,2},{14,3},{... | collective-permute-start | bytes 368648 | tf_op jit(solution)/shard_map/ppermute | solution.py:394
  62.8 5.2 %collective-permute-done.14.window = bf16[3,80,256]{2,1,0:T(8,128)(2,1)S(1)} collective-permute-done((bf16[3,80,256]{2,1,0:T(8,128)(2,1)S(1)}, bf16[3,80,256]{2,1,0:T(8,128)(2,1)S(1)}, u32[]{:S(2)}, u32[]{:S(2)}) %collective-permute-start.14) | collective-permute-done | bytes 122912 | tf_op jit(solution)/shard_map/ppermute | solution.py:394
  68.0 1.1 %join.1 = bf16[3,64,256]{2,1,0:T(8,128)(2,1)} custom-call(bf16[3,80,256]{2,1,0:T(8,128)(2,1)S(1)} %collective-permute-done.14.window, bf16[4,80,256]{2,1,0:T(8,128)(2,1)S(1)} %collective-permute-done.15.above, bf16[4,80,256]{2,1,0:T(8,128)(2,1)S(1)} %collective-permute-done.16.below, bf16[3,3,256,256]{3,2,1,0:T(8,128)(2,1)S(1)} %get-tuple-element.74.weight), custom_call_target="tpu_custom_call" | custom-call | tf_op jit(solution)/shard_map/join/pallas_call | solution.py:22
  (24 shorter events, 2.5 us)
Async XLA Ops:
  0.0 10.5 %collective-permute-start.1 = (bf16[384,384]{1,0:T(8,128)(2,1)}, bf16[384,384]{1,0:T(8,128)(2,1)S(1)}, u32[]{:S(2)}, u32[]{:S(2)}) collective-permute-start(bf16[384,384]{1,0:T(8,128)(2,1)} %bitcast.10), channel_id=1, source_target_pairs={{2,0},{0,2},{3,12},{1,14},{6,4},{4,6},{7,8},{5,10},{10,5},{8,7},{1... | collective-permute-start | bytes 884744 | tf_op jit(solution)/shard_map/ppermute | solution.py:271
  5.6 11.3 %collective-permute-start = (bf16[384,384]{1,0:T(8,128)(2,1)}, bf16[384,384]{1,0:T(8,128)(2,1)S(1)}, u32[]{:S(2)}, u32[]{:S(2)}) collective-permute-start(bf16[384,384]{1,0:T(8,128)(2,1)} %bitcast.11), channel_id=1, source_target_pairs={{0,0},{2,2},{1,12},{3,14},{4,4},{6,6},{5,8},{7,10},{8,5},{10,7},{9... | collective-permute-start | bytes 884744 | tf_op jit(solution)/shard_map/ppermute | solution.py:271
  7.6 2.6 %copy-start = (bf16[1,384,384]{2,1,0:T(8,128)(2,1)S(1)}, bf16[1,384,384]{2,1,0:T(8,128)(2,1)}, u32[]{:S(2)}) copy-start(bf16[1,384,384]{2,1,0:T(8,128)(2,1)} %param.9) | copy-start | bytes 884740
  10.1 10.2 %collective-permute-start.4 = (bf16[384,384]{1,0:T(8,128)(2,1)S(1)}, bf16[384,384]{1,0:T(8,128)(2,1)S(1)}, u32[]{:S(2)}, u32[]{:S(2)}) collective-permute-start(bf16[384,384]{1,0:T(8,128)(2,1)S(1)} %bitcast.9), channel_id=1, source_target_pairs={{2,0},{0,2},{3,1},{1,3},{6,4},{4,6},{7,5},{5,7},{10,8},{8,10},{11,... | collective-permute-start | bytes 884744 | tf_op jit(solution)/shard_map/ppermute | solution.py:277
  18.0 8.5 %collective-permute-start.2 = (bf16[384,512]{1,0:T(8,128)(2,1)S(1)}, bf16[384,512]{1,0:T(8,128)(2,1)S(1)}, u32[]{:S(2)}, u32[]{:S(2)}) collective-permute-start(bf16[384,512]{1,0:T(8,128)(2,1)S(1)} %get-tuple-element.43.refs_0_), channel_id=1, source_target_pairs={{4,0},{0,4},{12,8},{8,12},{5,1},{1,5},{13,9},{9,13},{6,2},{2,6},{1... | collective-permute-start | bytes 1179656 | tf_op jit(solution)/shard_map/ppermute | solution.py:285
  21.2 5.6 %collective-permute-start.5 = (bf16[192,768]{1,0:T(8,128)(2,1)S(1)}, bf16[192,768]{1,0:T(8,128)(2,1)S(1)}, u32[]{:S(2)}, u32[]{:S(2)}) collective-permute-start(bf16[192,768]{1,0:T(8,128)(2,1)S(1)} %get-tuple-element.50), channel_id=1, source_target_pairs={{2,0},{0,2},{3,1},{1,3},{6,4},{4,6},{7,5},{5,7},{10,8},{8,10},{11,... | collective-permute-start | bytes 884744 | tf_op jit(solution)/shard_map/ppermute | solution.py:277
  21.7 5.4 %collective-permute-start.8 = (bf16[384,512]{1,0:T(8,128)(2,1)S(1)}, bf16[384,512]{1,0:T(8,128)(2,1)S(1)}, u32[]{:S(2)}, u32[]{:S(2)}) collective-permute-start(bf16[384,512]{1,0:T(8,128)(2,1)S(1)} %get-tuple-element.43.refs_0_), channel_id=1, source_target_pairs={{1,0},{0,1},{3,2},{2,3},{5,4},{4,5},{7,6},{6,7},{9,8},{8,9},{11,10... | collective-permute-start | bytes 1179656 | tf_op jit(solution)/shard_map/ppermute | solution.py:291
  21.7 11.2 %collective-permute-start.7 = (bf16[384,512]{1,0:T(8,128)(2,1)S(1)}, bf16[384,512]{1,0:T(8,128)(2,1)S(1)}, u32[]{:S(2)}, u32[]{:S(2)}) collective-permute-start(bf16[384,512]{1,0:T(8,128)(2,1)S(1)} %project.3), channel_id=1, source_target_pairs={{0,0},{1,12},{4,4},{5,8},{8,5},{9,9},{12,1},{13,13},{2,2},{3,14},{... | collective-permute-start | bytes 1179656 | tf_op jit(solution)/shard_map/ppermute | solution.py:336
  26.5 6.4 %collective-permute-start.3 = (bf16[384,512]{1,0:T(8,128)(2,1)S(1)}, bf16[384,512]{1,0:T(8,128)(2,1)S(1)}, u32[]{:S(2)}, u32[]{:S(2)}) collective-permute-start(bf16[384,512]{1,0:T(8,128)(2,1)S(1)} %collective-permute-done.2.refs_1_), channel_id=1, source_target_pairs={{1,0},{0,1},{3,2},{2,3},{5,4},{4,5},{7,6},{6,7},{9,8},{8,9},{11,10... | collective-permute-start | bytes 1179656 | tf_op jit(solution)/shard_map/ppermute | solution.py:291
  26.9 3.0 %collective-permute-start.6 = (bf16[192,768]{1,0:T(8,128)(2,1)S(1)}, bf16[192,768]{1,0:T(8,128)(2,1)S(1)}, u32[]{:S(2)}, u32[]{:S(2)}) collective-permute-start(bf16[192,768]{1,0:T(8,128)(2,1)S(1)} %collective-permute-done.5.refs_0_), channel_id=1, source_target_pairs={{1,0},{0,1},{3,2},{2,3},{5,4},{4,5},{7,6},{6,7},{9,8},{8,9},{11,10... | collective-permute-start | bytes 884744 | tf_op jit(solution)/shard_map/ppermute | solution.py:291
  32.9 10.4 %collective-permute-start.10 = (bf16[384,512]{1,0:T(8,128)(2,1)S(1)}, bf16[384,512]{1,0:T(8,128)(2,1)S(1)}, u32[]{:S(2)}, u32[]{:S(2)}) collective-permute-start(bf16[384,512]{1,0:T(8,128)(2,1)S(1)} %collective-permute-done.7.refs_0_), channel_id=1, source_target_pairs={{4,0},{0,4},{12,8},{8,12},{5,1},{1,5},{13,9},{9,13},{6,2},{2,6},{1... | collective-permute-start | bytes 1179656 | tf_op jit(solution)/shard_map/ppermute | solution.py:285
  37.5 5.8 %collective-permute-start.9 = (bf16[384,256]{1,0:T(8,128)(2,1)S(1)}, bf16[384,256]{1,0:T(8,128)(2,1)S(1)}, u32[]{:S(2)}, u32[]{:S(2)}) collective-permute-start(bf16[384,256]{1,0:T(8,128)(2,1)S(1)} %end.1.refs_0_), channel_id=1, source_target_pairs={{2,0},{0,2},{3,1},{1,3},{6,4},{4,6},{7,5},{5,7},{10,8},{8,10},{11,... | collective-permute-start | bytes 589832 | tf_op jit(solution)/shard_map/ppermute | solution.py:277
  43.3 2.0 %collective-permute-start.11 = (bf16[384,512]{1,0:T(8,128)(2,1)S(1)}, bf16[384,512]{1,0:T(8,128)(2,1)S(1)}, u32[]{:S(2)}, u32[]{:S(2)}) collective-permute-start(bf16[384,512]{1,0:T(8,128)(2,1)S(1)} %collective-permute-done.7.refs_0_), channel_id=1, source_target_pairs={{1,0},{0,1},{3,2},{2,3},{5,4},{4,5},{7,6},{6,7},{9,8},{8,9},{11,10... | collective-permute-start | bytes 1179656 | tf_op jit(solution)/shard_map/ppermute | solution.py:291
  43.3 2.3 %collective-permute-start.12 = (bf16[384,512]{1,0:T(8,128)(2,1)S(1)}, bf16[384,512]{1,0:T(8,128)(2,1)S(1)}, u32[]{:S(2)}, u32[]{:S(2)}) collective-permute-start(bf16[384,512]{1,0:T(8,128)(2,1)S(1)} %collective-permute-done.10.refs_1_), channel_id=1, source_target_pairs={{1,0},{0,1},{3,2},{2,3},{5,4},{4,5},{7,6},{6,7},{9,8},{8,9},{11,10... | collective-permute-start | bytes 1179656 | tf_op jit(solution)/shard_map/ppermute | solution.py:291
  49.4 4.9 %collective-permute-start.13 = (bf16[3,80,256]{2,1,0:T(8,128)(2,1)S(1)}, bf16[3,80,256]{2,1,0:T(8,128)(2,1)S(1)}, u32[]{:S(2)}, u32[]{:S(2)}) collective-permute-start(bf16[3,80,256]{2,1,0:T(8,128)(2,1)S(1)} %get-tuple-element.68), channel_id=1, source_target_pairs={{2,0},{0,2},{3,1},{1,3},{6,4},{4,6},{7,5},{5,7},{10,8},{8,10},{11,... | collective-permute-start | bytes 368648 | tf_op jit(solution)/shard_map/ppermute | solution.py:277
  54.3 13.7 %collective-permute-start.15 = (bf16[4,80,256]{2,1,0:T(8,128)(2,1)S(1)}, bf16[4,80,256]{2,1,0:T(8,128)(2,1)S(1)}, u32[]{:S(2)}, u32[]{:S(2)}) collective-permute-start(bf16[4,80,256]{2,1,0:T(8,128)(2,1)S(1)} %get-tuple-element.73), channel_id=1, source_target_pairs={{0,4},{12,5},{4,8},{8,9},{5,12},{9,13},{2,6},{14,7},{6,10},{10,11}... | collective-permute-start | bytes 491528 | tf_op jit(solution)/shard_map/ppermute | solution.py:393
  55.0 13.0 %collective-permute-start.16 = (bf16[4,80,256]{2,1,0:T(8,128)(2,1)S(1)}, bf16[4,80,256]{2,1,0:T(8,128)(2,1)S(1)}, u32[]{:S(2)}, u32[]{:S(2)}) collective-permute-start(bf16[4,80,256]{2,1,0:T(8,128)(2,1)S(1)} %get-tuple-element.73), channel_id=1, source_target_pairs={{4,0},{8,1},{5,4},{9,5},{1,8},{13,9},{6,2},{10,3},{7,6},{11,7},{3,... | collective-permute-start | bytes 491528 | tf_op jit(solution)/shard_map/ppermute | solution.py:392
  59.9 8.1 %collective-permute-start.14 = (bf16[3,80,256]{2,1,0:T(8,128)(2,1)S(1)}, bf16[3,80,256]{2,1,0:T(8,128)(2,1)S(1)}, u32[]{:S(2)}, u32[]{:S(2)}) collective-permute-start(bf16[3,80,256]{2,1,0:T(8,128)(2,1)S(1)} %get-tuple-element.72), channel_id=1, source_target_pairs={{0,0},{12,1},{4,4},{8,5},{5,8},{9,9},{1,12},{13,13},{2,2},{14,3},{... | collective-permute-start | bytes 368648 | tf_op jit(solution)/shard_map/ppermute | solution.py:394
